TPU v7x, 32 devices: a whole 2x2x4 slice. The times are simulated.
32 devices in a mesh: groups: 1, expert: 32 (over z, y, x, core), dp: 1, tensor: 1.
Axes of the slice: x: 2, y: 2, z: 4, core: 2. Of those that a mesh axis runs over, the one named last changes fastest.
Arguments:
- tokens: bfloat16 [4096, 2048], P(('groups', 'expert', 'dp'), 'tensor'), may hold values from -6 to 6
- out_grad: bfloat16 [4096, 2048], P(('groups', 'expert', 'dp'), 'tensor'), may hold values from -6 to 6
- routes: int32 [4096, 8], P(('groups', 'expert', 'dp')), may hold values from 0 to 63, all different within a row; in each aligned block of 128 rows (0 to 127, 128 to 255, ...) at most 24 rows name the same one
- combine_fixed: int32 [4096, 8], P(('groups', 'expert', 'dp')), may hold values from 16 to 255
- down_proj: bfloat16 [512, 2048], P(('expert', 'dp'), 'tensor'), may hold values from -0.125 to 0.125
- up_proj: bfloat16 [512, 2048], P(('expert', 'dp'), 'tensor'), may hold values from -0.25 to 0.25
- expert_gate: bfloat16 [64, 512, 1024], P('expert', None, 'tensor'), may hold values from -0.25 to 0.25
- expert_up: bfloat16 [64, 512, 1024], P('expert', None, 'tensor'), may hold values from -0.25 to 0.25
- expert_down: bfloat16 [64, 1024, 512], P('expert', 'tensor'), may hold values from -0.1875 to 0.1875
Outputs:
- layer_out: bfloat16 [4096, 2048], P(('groups', 'expert', 'dp'), 'tensor')
- token_grad: bfloat16 [4096, 2048], P(('groups', 'expert', 'dp'), 'tensor')
- down_grad: float32 [512, 2048], P(('groups', 'expert', 'dp'), 'tensor')
- up_grad: float32 [512, 2048], P(('groups', 'expert', 'dp'), 'tensor')
Inputs may be any that keep to these rules, and one draw needn't show every extreme that they name: `routes`: each row names 8 different experts; among the rows of one data shard (128 aligned rows) no expert is named by more than 24 rows, and in every draw some expert is named by exactly 24 rows of some shard.
All inputs are finite; a program needn't handle non-finite values.
Results may differ from a plain program's by a relative error of at most 0.011.
Values may be sent and summed in bfloat16 or wider, within the bound.
No kernel may reach another device: no remote copies, remote signals or barrier semaphores. Data moves between devices by JAX's collectives and lax.ppermute only.
A program may use at most 64 MiB of HBM per device.

v0:
```python
import jax
import jax.numpy as jnp
from jax import lax
from jax.sharding import PartitionSpec as P


def move_rows(blocks):
    return lax.all_to_all(blocks, "expert", split_axis=0, concat_axis=0, tiled=True)


def tensor_total(partial_sum):
    return lax.psum(partial_sum, "tensor")


def dispatch_rows(blocks):
    return move_rows(blocks)


def local(
    tokens, out_grad, routes, combine_fixed, down_proj, up_proj, expert_gate, expert_up, expert_down
):
    down_full, up_full = (
        lax.all_gather(down_proj, ("expert", "dp"), axis=0, tiled=True),
        lax.all_gather(up_proj, ("expert", "dp"), axis=0, tiled=True),
    )
    row_count = tokens.shape[0]
    top_count = routes.shape[1]
    latent_width = down_full.shape[0]
    local_experts = expert_gate.shape[0]
    groups = lax.axis_size("expert")
    experts = local_experts * groups
    capacity = 3 * row_count * top_count // (2 * experts)
    chosen = routes[:, :, None] == jnp.arange(experts, dtype=jnp.int32)[None, None, :]
    member = jnp.any(chosen, axis=1)
    ranking = jnp.cumsum(member.astype(jnp.int32), axis=0) - 1
    fixed_scale = combine_fixed[:, :, None].astype(jnp.float32) / 256.0
    scales = jnp.sum(jnp.where(chosen, fixed_scale, 0.0), axis=1)
    placed = (
        ranking.T[:, None, :] == jnp.arange(capacity, dtype=jnp.int32)[None, :, None]
    ) & member.T[:, None, :]
    dispatch = placed.astype(jnp.bfloat16)
    combining = jnp.where(placed, scales.T[:, None, :], 0.0).astype(jnp.bfloat16)
    latent_part = jnp.einsum("td,ld->tl", tokens, down_full, preferred_element_type=jnp.float32)
    latent = tensor_total(latent_part).astype(jnp.bfloat16)
    outgoing = jnp.einsum(
        "ect,tl->ecl", dispatch, latent, preferred_element_type=jnp.float32
    ).astype(jnp.bfloat16)
    arrived = dispatch_rows(outgoing).reshape(groups, local_experts, capacity, latent_width)
    gate_act = jnp.einsum(
        "sjcl,jlf->sjcf", arrived, expert_gate, preferred_element_type=jnp.float32
    )
    up_act = jnp.einsum("sjcl,jlf->sjcf", arrived, expert_up, preferred_element_type=jnp.float32)
    sigmoid_gate = jax.nn.sigmoid(gate_act)
    hidden = (gate_act * sigmoid_gate * up_act).astype(jnp.bfloat16)
    half_out = jnp.einsum(
        "sjcf,jfl->sjcl", hidden, expert_down, preferred_element_type=jnp.float32
    ).astype(jnp.bfloat16)
    returned = move_rows(half_out.reshape(experts, capacity, latent_width))
    mixed_part = jnp.einsum("ect,ecl->tl", combining, returned, preferred_element_type=jnp.float32)
    mixed_rows = tensor_total(mixed_part).astype(jnp.bfloat16)
    layer_out = jnp.dot(mixed_rows, up_full, preferred_element_type=jnp.float32).astype(
        jnp.bfloat16
    )
    mix_part = jnp.einsum("td,ld->tl", out_grad, up_full, preferred_element_type=jnp.float32)
    mix_grad = tensor_total(mix_part).astype(jnp.bfloat16)
    grad_rows = jnp.einsum(
        "ect,tl->ecl", combining, mix_grad, preferred_element_type=jnp.float32
    ).astype(jnp.bfloat16)
    grad_arrived = dispatch_rows(grad_rows).reshape(groups, local_experts, capacity, latent_width)
    hidden_grad = jnp.einsum(
        "sjcl,jfl->sjcf", grad_arrived, expert_down, preferred_element_type=jnp.float32
    )
    gate_grad = (
        hidden_grad * up_act * sigmoid_gate * (1.0 + gate_act * (1.0 - sigmoid_gate))
    ).astype(jnp.bfloat16)
    value_grad = (hidden_grad * gate_act * sigmoid_gate).astype(jnp.bfloat16)
    back_sum = jnp.einsum(
        "sjcf,jlf->sjcl", gate_grad, expert_gate, preferred_element_type=jnp.float32
    )
    back_sum = back_sum + jnp.einsum(
        "sjcf,jlf->sjcl", value_grad, expert_up, preferred_element_type=jnp.float32
    )
    back_rows = move_rows(back_sum.astype(jnp.bfloat16).reshape(experts, capacity, latent_width))
    latent_part_grad = jnp.einsum(
        "ect,ecl->tl", dispatch, back_rows, preferred_element_type=jnp.float32
    )
    latent_grad = tensor_total(latent_part_grad).astype(jnp.bfloat16)
    token_grad = jnp.dot(latent_grad, down_full, preferred_element_type=jnp.float32).astype(
        jnp.bfloat16
    )
    down_term = jnp.einsum("tl,td->ld", latent_grad, tokens, preferred_element_type=jnp.float32)
    up_term = jnp.einsum("tl,td->ld", mixed_rows, out_grad, preferred_element_type=jnp.float32)
    down_grad, up_grad = (
        lax.psum_scatter(down_term, ("expert", "dp"), scatter_dimension=0, tiled=True),
        lax.psum_scatter(up_term, ("expert", "dp"), scatter_dimension=0, tiled=True),
    )
    return (layer_out, token_grad, down_grad, up_grad)


def solution(mesh):
    in_specs = (
        P(("groups", "expert", "dp"), "tensor"),
        P(("groups", "expert", "dp"), "tensor"),
        P(("groups", "expert", "dp"), None),
        P(("groups", "expert", "dp"), None),
        P(("expert", "dp"), "tensor"),
        P(("expert", "dp"), "tensor"),
        P("expert", None, "tensor"),
        P("expert", None, "tensor"),
        P("expert", "tensor", None),
    )
    out_specs = (
        P(("groups", "expert", "dp"), "tensor"),
        P(("groups", "expert", "dp"), "tensor"),
        P(("groups", "expert", "dp"), "tensor"),
        P(("groups", "expert", "dp"), "tensor"),
    )
    return jax.shard_map(local, mesh=mesh, in_specs=in_specs, out_specs=out_specs, check_vma=False)
```

profile of v0, /device:TPU:0, one launch (start us, length us, event | category | flops | bytes accessed | tf_op | source)
XLA Modules:
  0.0 538.0 jit_solution(6120593625740556284)
XLA Ops:
  7.2 0.0 copy-start
  7.2 0.0 all-gather.3.cloned.1.call-start
  7.2 0.7 all-gather.3.cloned.1.call-update
  7.9 0.0 all-gather.5.cloned.1.call-start
  8.0 0.7 all-gather.5.cloned.1.call-update
  8.7 0.7 fusion.68
  9.4 0.1 copy.48
  9.5 0.2 reduce_window_sum.11
  9.7 0.1 copy.49
  9.7 0.2 fusion.65
  9.9 60.1 %all-gather.3.cloned.1.call-done = bf16[512,2048]{1,0:T(8,128)(2,1)} async-done(((bf16[16,2048]{1,0:T(8,128)(2,1)}), bf16[512,2048]{1,0:T(8,128)(2,1)}) %all-gather.3.cloned.1.call-update) | async-done | bytes 2097168 | tf_op jit(solution)/shard_map/all_gather | solution.py:23
  70.0 4.3 convolution_convert_fusion.2
  74.3 3.6 all-to-all-start
  77.9 0.0 copy-done.8
  77.9 0.2 select_convert_fusion
  78.1 54.9 %all-gather.5.cloned.1.call-done = bf16[512,2048]{1,0:T(8,128)(2,1)} async-done(((bf16[16,2048]{1,0:T(8,128)(2,1)}), bf16[512,2048]{1,0:T(8,128)(2,1)}) %all-gather.5.cloned.1.call-update) | async-done | bytes 2097168 | tf_op jit(solution)/shard_map/all_gather | solution.py:24
  133.0 4.1 convolution_convert_fusion.3
  137.1 0.0 all-to-all-done
  137.1 3.6 all-to-all-start.2
  140.7 0.2 reduce-scatter.3.cloned.1.call-start
  140.9 0.0 copy-start.4
  140.9 6.0 %fusion.17 = f32[2,32,24,1024]{3,2,1,0:T(8,128)} fusion(bf16[2,512,1024]{2,1,0:T(8,128)(2,1)S(1)} %copy-done, bf16[32,2,24,512]{3,2,1,0:T(8,128)(2,1)} %bitcast.4), kind=kOutput, calls=%fused_computation.23 | convolution fusion | flops 1610612736 | bytes 9961472 | tf_op jit(solution)/shard_map/sjcl,jlf->sjcf/dot_general | solution.py:52
  147.0 5.9 %fusion.20 = f32[2,32,24,1024]{3,2,1,0:T(8,128)} fusion(bf16[2,512,1024]{2,1,0:T(8,128)(2,1)S(1)} %copy-done.4, bf16[32,2,24,512]{3,2,1,0:T(8,128)(2,1)} %bitcast.4), kind=kOutput, calls=%fused_computation.26 | convolution fusion | flops 1610612736 | bytes 9961472 | tf_op jit(solution)/shard_map/sjcl,jlf->sjcf/dot_general | solution.py:49
  152.8 25.6 %all-to-all-done.2 = bf16[64,24,512]{2,1,0:T(8,128)(2,1)} async-done(((bf16[64,24,512]{2,1,0:T(8,128)(2,1)}), bf16[64,24,512]{2,1,0:T(8,128)(2,1)}, u32[]{:S(2)}, u32[]{:S(2)}) %all-to-all-start.2) | async-done | bytes 1572896 | tf_op jit(solution)/shard_map/all_to_all | solution.py:8
  178.4 4.0 fusion.22
  182.4 0.0 copy-start.3
  182.5 2.6 copy-done.3
  185.0 0.0 copy-done.2
  185.0 3.6 fusion.12
  188.7 12.6 %fusion.39 = bf16[32,2,24,512]{3,2,0,1:T(8,128)(2,1)} fusion(f32[2,32,24,512]{3,2,1,0:T(8,128)} %fusion.12, bf16[2,512,1024]{2,1,0:T(8,128)(2,1)} %param.15, f32[2,32,24,1024]{3,2,1,0:T(8,128)} %copy-done.3, f32[2,32,24,1024]{3,2,1,0:T(8,128)} %fusion.17, f32[2,32,24,1024]{3,2,1,0:T(8,128)} %fusion.20), kind=kOutput, calls=%fused_computation.39 | convolution fusion | flops 1627914240 | bytes 25690112 | tf_op jit(solution)/shard_map/sjcf,jlf->sjcl/dot_general | solution.py:77
  201.3 1.6 copy.57
  202.9 0.0 copy-start.5
  202.9 41.6 %all_to_all.20 = bf16[64,24,512]{2,1,0:T(8,128)(2,1)S(1)} all-to-all(bf16[64,24,512]{2,1,0:T(8,128)(2,1)S(1)} %bitcast.137), channel_id=1, replica_groups=mesh['groups'=1,'expert'=32,'dp'=1,'tensor'=1] {'expert'}, dimensions={0} | all-to-all | bytes 3145728 | tf_op jit(solution)/shard_map/all_to_all | solution.py:8
  244.5 0.7 fusion.57
  245.2 2.7 fusion.75
  247.9 0.0 reduce-scatter.3.cloned.1.call-update
  247.9 0.3 reduce-scatter.5.cloned.1.call-start
  248.2 7.6 %fusion.44 = bf16[32,2,24,512]{3,2,0,1:T(8,128)(2,1)S(1)} fusion(bf16[2,1024,512]{2,1,0:T(8,128)(2,1)} %param.17, f32[2,32,24,1024]{3,2,1,0:T(8,128)} %fusion.17, f32[2,32,24,1024]{3,2,1,0:T(8,128)} %fusion.20), kind=kOutput, calls=%fused_computation.40 | convolution fusion | flops 1620836352 | bytes 16252928 | tf_op jit(solution)/shard_map/sjcf,jfl->sjcl/dot_general | solution.py:55
  255.8 0.2 copy.53
  256.0 46.4 %all_to_all.21 = bf16[64,24,512]{2,1,0:T(8,128)(2,1)S(1)} all-to-all(bf16[64,24,512]{2,1,0:T(8,128)(2,1)S(1)} %bitcast.138), channel_id=1, replica_groups=mesh['groups'=1,'expert'=32,'dp'=1,'tensor'=1] {'expert'}, dimensions={0} | all-to-all | bytes 3145728 | tf_op jit(solution)/shard_map/all_to_all | solution.py:8
  302.4 0.8 fusion.60
  303.2 2.7 fusion.76
  305.9 0.0 reduce-scatter.5.cloned.1.call-update
  305.9 0.0 copy-start.1
  305.9 3.0 convolution_convert_fusion.1
  308.9 1.2 convolution_convert_fusion
  310.1 81.6 %reduce-scatter.3.cloned.1.call-done = f32[16,2048]{1,0:T(8,128)} async-done(((f32[512,2048]{1,0:T(8,128)}), f32[16,2048]{1,0:T(8,128)}) %reduce-scatter.3.cloned.1.call-update) | async-done | bytes 131088 | tf_op jit(solution)/shard_map/reduce_scatter | solution.py:94
  391.8 139.6 %reduce-scatter.5.cloned.1.call-done = f32[16,2048]{1,0:T(8,128)} async-done(((f32[512,2048]{1,0:T(8,128)}), f32[16,2048]{1,0:T(8,128)}) %reduce-scatter.5.cloned.1.call-update) | async-done | bytes 131088 | tf_op jit(solution)/shard_map/reduce_scatter | solution.py:95
  (14 shorter events, 0.1 us)
Async XLA Ops:
  7.2 133.7 %copy-start = (bf16[2,512,1024]{2,1,0:T(8,128)(2,1)S(1)}, bf16[2,512,1024]{2,1,0:T(8,128)(2,1)}, u32[]{:S(2)}) copy-start(bf16[2,512,1024]{2,1,0:T(8,128)(2,1)} %param.16) | copy-start | bytes 6291460
  7.2 62.8 %all-gather.3.cloned.1.call-start = ((), (), s32[]{:S(2)}) async-start(), calls=%async_computation.6 | async-start | bytes 2162688 | tf_op jit(solution)/shard_map/all_gather | solution.py:23
  7.9 125.1 %all-gather.5.cloned.1.call-start = ((), (), s32[]{:S(2)}) async-start(), calls=%async_computation.7 | async-start | bytes 2162688 | tf_op jit(solution)/shard_map/all_gather | solution.py:24
  74.3 3.6 copy-start.8
  74.3 3.6 copy-start.7
  74.3 58.7 %copy-start.6 = (bf16[128,2048]{1,0:T(8,128)(2,1)S(1)}, bf16[128,2048]{1,0:T(8,128)(2,1)}, u32[]{:S(2)}) copy-start(bf16[128,2048]{1,0:T(8,128)(2,1)} %param.10) | copy-start | bytes 1572868
  74.3 62.8 %all-to-all-start = ((bf16[64,24,512]{2,1,0:T(8,128)(2,1)}), bf16[64,24,512]{2,1,0:T(8,128)(2,1)}, u32[]{:S(2)}, u32[]{:S(2)}) async-start(bf16[64,24,512]{2,1,0:T(8,128)(2,1)} %convolution_convert_fusion.2), calls=%async_computation | async-start | bytes 3145728 | tf_op jit(solution)/shard_map/all_to_all | solution.py:8
  137.1 41.3 %all-to-all-start.2 = ((bf16[64,24,512]{2,1,0:T(8,128)(2,1)}), bf16[64,24,512]{2,1,0:T(8,128)(2,1)}, u32[]{:S(2)}, u32[]{:S(2)}) async-start(bf16[64,24,512]{2,1,0:T(8,128)(2,1)} %convolution_convert_fusion.3), calls=%async_computation.2 | async-start | bytes 3145728 | tf_op jit(solution)/shard_map/all_to_all | solution.py:8
  140.7 251.1 %reduce-scatter.3.cloned.1.call-start = ((), (), s32[]{:S(2)}) async-start(), calls=%async_computation.8 | async-start | bytes 4325376 | tf_op jit(solution)/shard_map/reduce_scatter | solution.py:94
  140.9 6.0 %copy-start.4 = (bf16[2,512,1024]{2,1,0:T(8,128)(2,1)S(1)}, bf16[2,512,1024]{2,1,0:T(8,128)(2,1)}, u32[]{:S(2)}) copy-start(bf16[2,512,1024]{2,1,0:T(8,128)(2,1)} %param.15) | copy-start | bytes 6291460
  178.4 6.7 %copy-start.2 = (f32[2,32,24,1024]{3,2,1,0:T(8,128)S(1)}, f32[2,32,24,1024]{3,2,1,0:T(8,128)}, u32[]{:S(2)}) copy-start(f32[2,32,24,1024]{3,2,1,0:T(8,128)} %fusion.20) | copy-start | bytes 18874372
  182.4 2.6 copy-start.3
  202.9 42.3 %copy-start.5 = (bf16[128,2048]{1,0:T(8,128)(2,1)S(1)}, bf16[128,2048]{1,0:T(8,128)(2,1)}, u32[]{:S(2)}) copy-start(bf16[128,2048]{1,0:T(8,128)(2,1)} %param.9) | copy-start | bytes 1572868
  247.9 283.5 %reduce-scatter.5.cloned.1.call-start = ((), (), s32[]{:S(2)}) async-start(), calls=%async_computation.9 | async-start | bytes 4325376 | tf_op jit(solution)/shard_map/reduce_scatter | solution.py:95
  305.9 3.0 copy-start.1
Sparse Core Ops, SparseCore 0:
  10.9 59.0 all-gather.2
  72.8 60.1 all-gather.4
  248.0 143.7 reduce-scatter.2
  394.5 136.8 reduce-scatter.4
where the time goes:
time: 538 us
  waiting for transfers between devices  363 us (67%)
  blocking collectives  88 us (16%)
  matrix products  59.3 us (11%)
  between operations  14 us (3%)
  starting transfers between devices  7.69 us (1%)
    reduce_scatter x1, waiting for transfers between devices, local(): lax.psum_scatter(up_term, ('expert', 'dp'), scatter_dimension=0, tiled=True)  140 us
    all_to_all x2, blocking collectives, move_rows(): lax.all_to_all(blocks, 'expert', split_axis=0, concat_axis=0, tiled=True)  88 us
    reduce_scatter x1, waiting for transfers between devices, local(): lax.psum_scatter(down_term, ('expert', 'dp'), scatter_dimension=0, tiled=...  81.6 us
    all_gather x1, waiting for transfers between devices, local(): lax.all_gather(down_proj, ('expert', 'dp'), axis=0, tiled=True)  60.1 us
    all_gather x1, waiting for transfers between devices, local(): lax.all_gather(up_proj, ('expert', 'dp'), axis=0, tiled=True)  54.9 us
    all_to_all x2, waiting for transfers between devices, move_rows(): lax.all_to_all(blocks, 'expert', split_axis=0, concat_axis=0, tiled=True)  25.6 us
    dot_general x1, matrix products, local(): jnp.einsum('sjcf,jlf->sjcl', gate_grad, expert_gate, preferred_element_ty...  12.6 us
  transfers between devices with their start and end apart: 6, of which 5 were waited for; matrix products, arithmetic and copies ran while one was open for 7% of the time, Pallas kernels for 0%

commit v1 on v0

--- a/solution.py
+++ b/solution.py
@@ -1,3 +1,5 @@
+import math
+
 import jax
 import jax.numpy as jnp
 from jax import lax
@@ -16,13 +18,99 @@
     return move_rows(blocks)
 
 
+OWNERS = ("expert", "dp")
+
+
+def radices(count):
+    return (count // 8, 2, 2, 2) if count % 8 == 0 else (count, 1, 1, 1)
+
+
+def digit_of(count, place):
+    sizes = radices(count)
+    stride = math.prod(sizes[place + 1 :])
+    return lax.rem(lax.axis_index(OWNERS) // stride, sizes[place])
+
+
+def shifted(block, count, place, step):
+    sizes = radices(count)
+    stride = math.prod(sizes[place + 1 :])
+    pairs = []
+    for here in range(count):
+        digit = here // stride % sizes[place]
+        pairs.append((here, here + ((digit + step) % sizes[place] - digit) * stride))
+    return lax.ppermute(block, OWNERS, pairs)
+
+
+def gather_rows(shard, count, order):
+    sizes = radices(count)
+    block = shard.reshape((1, 1, 1, 1) + shard.shape)
+    for place in order:
+        size = sizes[place]
+        if size == 1:
+            continue
+        digit = digit_of(count, place)
+        if size == 2:
+            other = shifted(block, count, place, 1)
+            block = jnp.where(
+                digit == 0,
+                lax.concatenate([block, other], place),
+                lax.concatenate([other, block], place),
+            )
+            continue
+        pieces = [block] + [shifted(block, count, place, step) for step in range(1, size)]
+        whole = jnp.zeros(block.shape[:place] + (size,) + block.shape[place + 1 :], block.dtype)
+        for step, piece in enumerate(pieces):
+            owner = lax.rem(digit + size - step, size)
+            whole = lax.dynamic_update_slice_in_dim(whole, piece, owner, place)
+        block = whole
+    return block.reshape((count * shard.shape[0],) + shard.shape[1:])
+
+
+def scatter_total(left, right, count, order):
+    sizes = radices(count)
+    width = left.shape[1]
+    columns = left.reshape((left.shape[0],) + sizes + (width // count,))
+
+    def product(part):
+        out = jnp.einsum(
+            "tl,td->ld", part.reshape(left.shape[0], -1), right, preferred_element_type=jnp.float32
+        )
+        return out.reshape(part.shape[1:] + right.shape[1:])
+
+    def own(array, place, step, offset):
+        size = sizes[place]
+        where = lax.rem(digit_of(count, place) + step, size)
+        return lax.dynamic_slice_in_dim(array, where, 1, place + offset)
+
+    first, rest = order[0], order[1:]
+    received = [
+        shifted(product(own(columns, first, step, 1)).astype(jnp.bfloat16), count, first, step)
+        for step in range(1, sizes[first])
+    ]
+    kept = product(own(columns, first, 0, 1))
+    for place in rest:
+        size = sizes[place]
+        arriving = []
+        for step in range(1, size):
+            part = own(kept, place, step, 0)
+            for block in received:
+                part = part + own(block, place, step, 0).astype(jnp.float32)
+            arriving.append(shifted(part.astype(jnp.bfloat16), count, place, step))
+        kept = own(kept, place, 0, 0)
+        for block in received:
+            kept = kept + own(block, place, 0, 0).astype(jnp.float32)
+        received = arriving
+    for block in received:
+        kept = kept + block.astype(jnp.float32)
+    return kept.reshape(width // count, right.shape[1])
+
+
 def local(
     tokens, out_grad, routes, combine_fixed, down_proj, up_proj, expert_gate, expert_up, expert_down
 ):
-    down_full, up_full = (
-        lax.all_gather(down_proj, ("expert", "dp"), axis=0, tiled=True),
-        lax.all_gather(up_proj, ("expert", "dp"), axis=0, tiled=True),
-    )
+    count = lax.axis_size("expert") * lax.axis_size("dp")
+    down_full = gather_rows(down_proj, count, (0, 1, 2, 3))
+    up_full = gather_rows(up_proj, count, (0, 2, 1, 3))
     row_count = tokens.shape[0]
     top_count = routes.shape[1]
     latent_width = down_full.shape[0]
@@ -88,12 +176,8 @@
     token_grad = jnp.dot(latent_grad, down_full, preferred_element_type=jnp.float32).astype(
         jnp.bfloat16
     )
-    down_term = jnp.einsum("tl,td->ld", latent_grad, tokens, preferred_element_type=jnp.float32)
-    up_term = jnp.einsum("tl,td->ld", mixed_rows, out_grad, preferred_element_type=jnp.float32)
-    down_grad, up_grad = (
-        lax.psum_scatter(down_term, ("expert", "dp"), scatter_dimension=0, tiled=True),
-        lax.psum_scatter(up_term, ("expert", "dp"), scatter_dimension=0, tiled=True),
-    )
+    down_grad = scatter_total(latent_grad, tokens, count, (3, 2, 1, 0))
+    up_grad = scatter_total(mixed_rows, out_grad, count, (3, 1, 2, 0))
     return (layer_out, token_grad, down_grad, up_grad)
 
 

time: 538 us -> 288 us (0.54)
  waiting for transfers between devices: 363 us -> 163 us
  blocking collectives: 88 us -> 0 us
  starting transfers between devices: 7.69 us -> 47.1 us
  between operations: 14 us -> 1.13 us
  other arithmetic: 1.27 us -> 12.9 us
    reduce_scatter x2 -> x0, waiting for transfers between devices: 221 us -> none  [the longest x1 140 us: local(): lax.psum_scatter(up_term, ('expert', 'dp'), scatter_dimension=0, tiled=True)]
    all_gather x2 -> x0, waiting for transfers between devices: 115 us -> none  [the longest x1 60.1 us: local(): lax.all_gather(down_proj, ('expert', 'dp'), axis=0, tiled=True)]
    all_to_all x2 -> x0, blocking collectives: 88 us -> none  [move_rows(): lax.all_to_all(blocks, 'expert', split_axis=0, concat_axis=0, tiled=True)]
    ppermute x0 -> x24, waiting for transfers between devices: none -> 73.8 us  [shifted(): return lax.ppermute(block, OWNERS, pairs)]
    all_to_all x2 -> x4, waiting for transfers between devices: 25.6 us -> 88.9 us  [move_rows(): lax.all_to_all(blocks, 'expert', split_axis=0, concat_axis=0, tiled=True)]
    ppermute x0 -> x24, starting transfers between devices: none -> 29.6 us  [shifted(): return lax.ppermute(block, OWNERS, pairs)]
    all_to_all x2 -> x4, starting transfers between devices: 7.12 us -> 17.5 us  [move_rows(): lax.all_to_all(blocks, 'expert', split_axis=0, concat_axis=0, tiled=True)]
    select_n x0 -> x6, other arithmetic: none -> 6.88 us  [gather_rows(): jnp.where(digit == 0, lax.concatenate([block, other], place), lax.concate...]
  transfers between devices with their start and end apart: 6 -> 28, of which waited for: 5 -> 14; matrix products, arithmetic and copies ran while one was open for 7% -> 18% of each run, Pallas kernels for 0% -> 0%
where the time goes in v1:
time: 288 us
  waiting for transfers between devices  163 us (57%)
  matrix products  56.5 us (20%)
  starting transfers between devices  47.1 us (16%)
  other arithmetic  12.9 us (4%)
  local copies, waits for them, and re-layouts  7.4 us (3%)
    all_to_all x4, waiting for transfers between devices, move_rows(): lax.all_to_all(blocks, 'expert', split_axis=0, concat_axis=0, tiled=True)  88.9 us
    ppermute x24, waiting for transfers between devices, shifted(): return lax.ppermute(block, OWNERS, pairs)  73.8 us
    ppermute x24, starting transfers between devices, shifted(): return lax.ppermute(block, OWNERS, pairs)  29.6 us
    all_to_all x4, starting transfers between devices, move_rows(): lax.all_to_all(blocks, 'expert', split_axis=0, concat_axis=0, tiled=True)  17.5 us
    dot_general x1, matrix products, local(): jnp.einsum('sjcf,jlf->sjcl', gate_grad, expert_gate, preferred_element_ty...  11.5 us
    dot_general x1, matrix products, local(): jnp.einsum('sjcf,jfl->sjcl', hidden, expert_down, preferred_element_type=...  6.9 us
    select_n x6, other arithmetic, gather_rows(): jnp.where(digit == 0, lax.concatenate([block, other], place), lax.concate...  6.88 us
    dot_general x1, matrix products, local(): jnp.einsum('sjcl,jlf->sjcf', arrived, expert_up, preferred_element_type=j...  6.04 us
  transfers between devices with their start and end apart: 28, of which 14 were waited for; matrix products, arithmetic and copies ran while one was open for 18% of the time, Pallas kernels for 0%

profile of v1, /device:TPU:0, one launch (start us, length us, event | category | flops | bytes accessed | tf_op | source)
XLA Modules:
  0.0 287.7 jit_solution(13119446306124996753)
XLA Ops:
  0.7 3.1 %collective-permute-start = (bf16[1,1,1,1,16,2048]{5,4,3,2,1,0:T(8,128)(2,1)}, bf16[1,1,1,1,16,2048]{5,4,3,2,1,0:T(8,128)(2,1)S(1)}, u32[]{:S(2)}, u32[]{:S(2)}) collective-permute-start(bf16[1,1,1,1,16,2048]{5,4,3,2,1,0:T(8,128)(2,1)} %bitcast.243), channel_id=1, source_target_pairs={{0,8},{1,9},{2,10},{3,11},{4,12},{5,13},{6,14},{7,15},{8,16},{9,17... | collective-permute-start | bytes 196616 | tf_op jit(solution)/shard_map/ppermute | solution.py:41
  3.7 2.6 collective-permute-start.1
  6.3 1.3 collective-permute-start.2
  10.6 2.9 collective-permute-start.8
  13.5 1.6 collective-permute-start.3
  15.2 5.0 %collective-permute-done.3 = bf16[4,1,1,1,16,2048]{5,4,3,2,1,0:T(8,128)(2,1)S(1)} collective-permute-done((bf16[4,1,1,1,16,2048]{5,4,3,2,1,0:T(8,128)(2,1)S(1)}, bf16[4,1,1,1,16,2048]{5,4,3,2,1,0:T(8,128)(2,1)S(1)}, u32[]{:S(2)}, u32[]{:S(2)}) %collective-permute-start.3) | collective-permute-done | bytes 262176 | tf_op jit(solution)/shard_map/ppermute | solution.py:41
  20.3 1.6 collective-permute-start.4
  22.0 9.7 %collective-permute-done.4 = bf16[4,2,1,1,16,2048]{5,4,3,2,1,0:T(8,128)(2,1)S(1)} collective-permute-done((bf16[4,2,1,1,16,2048]{5,4,3,2,1,0:T(8,128)(2,1)S(1)}, bf16[4,2,1,1,16,2048]{5,4,3,2,1,0:T(8,128)(2,1)S(1)}, u32[]{:S(2)}, u32[]{:S(2)}) %collective-permute-start.4) | collective-permute-done | bytes 524320 | tf_op jit(solution)/shard_map/ppermute | solution.py:41
  33.0 2.8 collective-permute-done.5
  35.8 3.9 %maximum_select_fusion = bf16[4,2,2,2,16,2048]{5,4,3,2,1,0:T(8,128)(2,1)} fusion(bf16[4,2,2,1,16,2048]{5,4,3,2,1,0:T(8,128)(2,1)} %collective-permute-done.5, bf16[4,2,2,1,16,2048]{5,4,3,2,1,0:T(8,128)(2,1)} %maximum_select_fusion.2, pred[]{:T(512)S(6)} %eq.44), kind=kLoop, calls=%fused_computation.26 | loop fusion | flops 3145728 | bytes 4194305 | tf_op jit(solution)/shard_map/jit(_where)/select_n | solution.py:54
  39.7 4.7 %convolution_convert_fusion.4 = bf16[64,24,512]{2,1,0:T(8,128)(2,1)} fusion(bf16[512,2048]{1,0:T(8,128)(2,1)} %bitcast.223, bf16[128,2048]{1,0:T(8,128)(2,1)S(1)} %copy-done.6, pred[64,24,128]{2,0,1:T(32,128)(4,1)S(1)} %fusion.69), kind=kOutput, calls=%fused_computation.38 | convolution fusion | flops 470614016 | bytes 4390912 | tf_op jit(solution)/shard_map/ect,tl->ecl/dot_general | solution.py:133
  44.4 4.7 %all-to-all-start = ((bf16[64,24,512]{2,1,0:T(8,128)(2,1)}), bf16[64,24,512]{2,1,0:T(8,128)(2,1)}, u32[]{:S(2)}, u32[]{:S(2)}) async-start(bf16[64,24,512]{2,1,0:T(8,128)(2,1)} %convolution_convert_fusion.4), calls=%async_computation | async-start | bytes 3145728 | tf_op jit(solution)/shard_map/all_to_all | solution.py:10
  49.2 1.8 collective-permute-start.9
  51.0 20.3 %collective-permute-done.9 = bf16[4,1,1,1,16,2048]{5,4,0,3,2,1:T(8,128)(2,1)S(1)} collective-permute-done((bf16[4,1,1,1,16,2048]{5,4,0,3,2,1:T(8,128)(2,1)S(1)}, bf16[4,1,1,1,16,2048]{5,4,0,3,2,1:T(8,128)(2,1)S(1)}, u32[]{:S(2)}, u32[]{:S(2)}) %collective-permute-start.9) | collective-permute-done | bytes 262176 | tf_op jit(solution)/shard_map/ppermute | solution.py:41
  71.4 1.5 collective-permute-start.10
  72.9 15.0 %collective-permute-done.10 = bf16[4,1,2,1,16,2048]{5,4,3,2,1,0:T(8,128)(2,1)S(1)} collective-permute-done((bf16[4,1,2,1,16,2048]{5,4,3,2,1,0:T(8,128)(2,1)S(1)}, bf16[4,1,2,1,16,2048]{5,4,3,2,1,0:T(8,128)(2,1)S(1)}, u32[]{:S(2)}, u32[]{:S(2)}) %collective-permute-start.10) | collective-permute-done | bytes 524320 | tf_op jit(solution)/shard_map/ppermute | solution.py:41
  89.0 1.8 collective-permute-done.11
  90.7 1.6 maximum_select_fusion.1
  92.3 4.7 %convolution_convert_fusion.5 = bf16[64,24,512]{2,1,0:T(8,128)(2,1)} fusion(bf16[512,2048]{1,0:T(8,128)(2,1)} %bitcast.225, bf16[128,2048]{1,0:T(8,128)(2,1)S(1)} %copy-done.7, bf16[64,24,128]{2,0,1:T(8,128)(2,1)S(1)} %select_convert_fusion), kind=kOutput, calls=%fused_computation.39 | convolution fusion | flops 470614016 | bytes 4587520 | tf_op jit(solution)/shard_map/ect,tl->ecl/dot_general | solution.py:154
  97.1 5.0 %all-to-all-start.2 = ((bf16[64,24,512]{2,1,0:T(8,128)(2,1)}), bf16[64,24,512]{2,1,0:T(8,128)(2,1)}, u32[]{:S(2)}, u32[]{:S(2)}) async-start(bf16[64,24,512]{2,1,0:T(8,128)(2,1)} %convolution_convert_fusion.5), calls=%async_computation.2 | async-start | bytes 3145728 | tf_op jit(solution)/shard_map/all_to_all | solution.py:10
  102.1 6.0 %fusion.19 = f32[2,32,24,1024]{3,2,1,0:T(8,128)} fusion(bf16[2,512,1024]{2,1,0:T(8,128)(2,1)S(1)} %copy-done, bf16[32,2,24,512]{3,2,1,0:T(8,128)(2,1)} %bitcast.9), kind=kOutput, calls=%fused_computation.29 | convolution fusion | flops 1610612736 | bytes 9961472 | tf_op jit(solution)/shard_map/sjcl,jlf->sjcf/dot_general | solution.py:140
  108.1 5.9 %fusion.22 = f32[2,32,24,1024]{3,2,1,0:T(8,128)} fusion(bf16[2,512,1024]{2,1,0:T(8,128)(2,1)S(1)} %copy-done.8, bf16[32,2,24,512]{3,2,1,0:T(8,128)(2,1)} %bitcast.9), kind=kOutput, calls=%fused_computation.32 | convolution fusion | flops 1610612736 | bytes 9961472 | tf_op jit(solution)/shard_map/sjcl,jlf->sjcf/dot_general | solution.py:137
  114.0 25.6 %all-to-all-done.2 = bf16[64,24,512]{2,1,0:T(8,128)(2,1)} async-done(((bf16[64,24,512]{2,1,0:T(8,128)(2,1)}), bf16[64,24,512]{2,1,0:T(8,128)(2,1)}, u32[]{:S(2)}, u32[]{:S(2)}) %all-to-all-start.2) | async-done | bytes 1572896 | tf_op jit(solution)/shard_map/all_to_all | solution.py:10
  139.6 4.0 %fusion.24 = f32[2,32,24,1024]{3,2,1,0:T(8,128)S(1)} fusion(bf16[2,1024,512]{2,1,0:T(8,128)(2,1)} %param.17, bf16[32,2,24,512]{3,2,1,0:T(8,128)(2,1)} %bitcast.34), kind=kOutput, calls=%fused_computation.34 | convolution fusion | flops 1610612736 | bytes 9961472 | tf_op jit(solution)/shard_map/sjcl,jfl->sjcf/dot_general | solution.py:158
  143.7 2.6 copy-done.5
  146.3 3.7 %fusion.12 = f32[2,32,24,512]{3,2,1,0:T(8,128)} fusion(f32[2,32,24,1024]{3,2,1,0:T(8,128)S(1)} %fusion.24, f32[2,32,24,1024]{3,2,1,0:T(8,128)S(1)} %copy-done.4, bf16[2,512,1024]{2,1,0:T(8,128)(2,1)S(1)} %copy-done), kind=kOutput, calls=%fused_computation.18 | convolution fusion | flops 1620049920 | bytes 17825792 | tf_op jit(solution)/shard_map/sjcf,jlf->sjcl/dot_general | solution.py:168
  150.0 11.5 %fusion.41 = bf16[32,2,24,512]{3,2,0,1:T(8,128)(2,1)S(1)} fusion(f32[2,32,24,512]{3,2,1,0:T(8,128)} %fusion.12, bf16[2,512,1024]{2,1,0:T(8,128)(2,1)} %param.15, f32[2,32,24,1024]{3,2,1,0:T(8,128)} %copy-done.5, f32[2,32,24,1024]{3,2,1,0:T(8,128)} %fusion.19, f32[2,32,24,1024]{3,2,1,0:T(8,128)} %fusion.22), kind=kOutput, calls=%fused_computation.45 | convolution fusion | flops 1627914240 | bytes 25690112 | tf_op jit(solution)/shard_map/sjcf,jlf->sjcl/dot_general | solution.py:165
  161.4 1.4 copy.97
  162.8 3.8 %all-to-all-start.3 = ((bf16[64,24,512]{2,1,0:T(8,128)(2,1)}), bf16[64,24,512]{2,1,0:T(8,128)(2,1)}, u32[]{:S(2)}, u32[]{:S(2)}) async-start(bf16[64,24,512]{2,1,0:T(8,128)(2,1)} %bitcast.40), calls=%async_computation.3 | async-start | bytes 3145728 | tf_op jit(solution)/shard_map/all_to_all | solution.py:10
  166.7 6.9 %fusion.46 = bf16[32,2,24,512]{3,2,0,1:T(8,128)(2,1)S(1)} fusion(bf16[2,1024,512]{2,1,0:T(8,128)(2,1)S(1)} %copy-done.9, f32[2,32,24,1024]{3,2,1,0:T(8,128)} %fusion.19, f32[2,32,24,1024]{3,2,1,0:T(8,128)} %fusion.22), kind=kOutput, calls=%fused_computation.46 | convolution fusion | flops 1620836352 | bytes 16252928 | tf_op jit(solution)/shard_map/sjcf,jfl->sjcl/dot_general | solution.py:143
  173.6 1.4 copy.85
  175.0 29.4 %all-to-all-done.3 = bf16[64,24,512]{2,1,0:T(8,128)(2,1)} async-done(((bf16[64,24,512]{2,1,0:T(8,128)(2,1)}), bf16[64,24,512]{2,1,0:T(8,128)(2,1)}, u32[]{:S(2)}, u32[]{:S(2)}) %all-to-all-start.3) | async-done | bytes 1572896 | tf_op jit(solution)/shard_map/all_to_all | solution.py:10
  204.4 4.0 %all-to-all-start.1 = ((bf16[64,24,512]{2,1,0:T(8,128)(2,1)}), bf16[64,24,512]{2,1,0:T(8,128)(2,1)S(1)}, u32[]{:S(2)}, u32[]{:S(2)}) async-start(bf16[64,24,512]{2,1,0:T(8,128)(2,1)} %bitcast.19), calls=%async_computation.1 | async-start | bytes 3145728 | tf_op jit(solution)/shard_map/all_to_all | solution.py:10
  208.4 2.1 fusion.59
  210.7 1.4 fusion.16
  212.1 33.9 %all-to-all-done.1 = bf16[64,24,512]{2,1,0:T(8,128)(2,1)S(1)} async-done(((bf16[64,24,512]{2,1,0:T(8,128)(2,1)}), bf16[64,24,512]{2,1,0:T(8,128)(2,1)S(1)}, u32[]{:S(2)}, u32[]{:S(2)}) %all-to-all-start.1) | async-done | bytes 1572896 | tf_op jit(solution)/shard_map/all_to_all | solution.py:10
  246.9 1.4 fusion.17
  249.1 1.5 fusion.68
  251.9 1.4 fusion.67
  253.4 1.6 collective-permute-start.19
  255.0 1.3 convolution_convert_fusion.3
  256.2 8.8 %collective-permute-done.13 = bf16[4,2,1,1,16,2048]{5,4,2,1,0,3:T(8,128)(2,1)S(1)} collective-permute-done((bf16[4,2,1,1,16,2048]{5,4,2,1,0,3:T(8,128)(2,1)S(1)}, bf16[4,2,1,1,16,2048]{5,4,2,1,0,3:T(8,128)(2,1)S(1)}, u32[]{:S(2)}, u32[]{:S(2)}) %collective-permute-start.13) | collective-permute-done | bytes 524320 | tf_op jit(solution)/shard_map/ppermute | solution.py:41
  265.2 1.3 collective-permute-start.14
  269.8 3.4 %collective-permute-done.14 = bf16[4,1,1,1,16,2048]{5,4,2,1,0,3:T(8,128)(2,1)S(1)} collective-permute-done((bf16[4,1,1,1,16,2048]{5,4,2,1,0,3:T(8,128)(2,1)S(1)}, bf16[4,1,1,1,16,2048]{5,4,2,1,0,3:T(8,128)(2,1)S(1)}, u32[]{:S(2)}, u32[]{:S(2)}) %collective-permute-start.14) | collective-permute-done | bytes 262176 | tf_op jit(solution)/shard_map/ppermute | solution.py:41
  273.2 1.6 collective-permute-start.17
  276.0 2.8 collective-permute-start.23
  280.4 3.9 %collective-permute-done.16 = bf16[1,1,1,1,16,2048]{5,4,2,1,0,3:T(8,128)(2,1)S(1)} collective-permute-done((bf16[1,1,1,1,16,2048]{5,4,2,1,0,3:T(8,128)(2,1)S(1)}, bf16[1,1,1,1,16,2048]{5,4,2,1,0,3:T(8,128)(2,1)S(1)}, u32[]{:S(2)}, u32[]{:S(2)}) %collective-permute-start.16) | collective-permute-done | bytes 65568 | tf_op jit(solution)/shard_map/ppermute | solution.py:41
  284.9 2.1 collective-permute-done.22
  (98 shorter events, 16.4 us)
Async XLA Ops:
  0.6 101.4 %copy-start = (bf16[2,512,1024]{2,1,0:T(8,128)(2,1)S(1)}, bf16[2,512,1024]{2,1,0:T(8,128)(2,1)}, u32[]{:S(2)}) copy-start(bf16[2,512,1024]{2,1,0:T(8,128)(2,1)} %param.16) | copy-start | bytes 6291460
  0.6 21.2 %copy-start.14 = (bf16[16,2048]{1,0:T(8,128)(2,1)S(1)}, bf16[16,2048]{1,0:T(8,128)(2,1)}, u32[]{:S(2)}) copy-start(bf16[16,2048]{1,0:T(8,128)(2,1)} %param.14) | copy-start | bytes 196612
  0.7 9.9 %collective-permute-start = (bf16[1,1,1,1,16,2048]{5,4,3,2,1,0:T(8,128)(2,1)}, bf16[1,1,1,1,16,2048]{5,4,3,2,1,0:T(8,128)(2,1)S(1)}, u32[]{:S(2)}, u32[]{:S(2)}) collective-permute-start(bf16[1,1,1,1,16,2048]{5,4,3,2,1,0:T(8,128)(2,1)} %bitcast.243), channel_id=1, source_target_pairs={{0,8},{1,9},{2,10},{3,11},{4,12},{5,13},{6,14},{7,15},{8,16},{9,17... | collective-permute-start | bytes 196616 | tf_op jit(solution)/shard_map/ppermute | solution.py:41
  3.7 9.7 %collective-permute-start.1 = (bf16[1,1,1,1,16,2048]{5,4,3,2,1,0:T(8,128)(2,1)}, bf16[1,1,1,1,16,2048]{5,4,3,2,1,0:T(8,128)(2,1)S(1)}, u32[]{:S(2)}, u32[]{:S(2)}) collective-permute-start(bf16[1,1,1,1,16,2048]{5,4,3,2,1,0:T(8,128)(2,1)} %bitcast.244), channel_id=1, source_target_pairs={{0,16},{1,17},{2,18},{3,19},{4,20},{5,21},{6,22},{7,23},{8,24},{9,... | collective-permute-start | bytes 196616 | tf_op jit(solution)/shard_map/ppermute | solution.py:41
  6.3 7.2 %collective-permute-start.2 = (bf16[1,1,1,1,16,2048]{5,4,3,2,1,0:T(8,128)(2,1)}, bf16[1,1,1,1,16,2048]{5,4,3,2,1,0:T(8,128)(2,1)S(1)}, u32[]{:S(2)}, u32[]{:S(2)}) collective-permute-start(bf16[1,1,1,1,16,2048]{5,4,3,2,1,0:T(8,128)(2,1)} %bitcast.245), channel_id=1, source_target_pairs={{0,24},{1,25},{2,26},{3,27},{4,28},{5,29},{6,30},{7,31},{8,0},{9,1... | collective-permute-start | bytes 196616 | tf_op jit(solution)/shard_map/ppermute | solution.py:41
  7.7 25.3 %collective-permute-start.6 = (bf16[1,1,1,1,16,2048]{5,4,3,2,1,0:T(8,128)(2,1)}, bf16[1,1,1,1,16,2048]{5,4,3,2,1,0:T(8,128)(2,1)S(1)}, u32[]{:S(2)}, u32[]{:S(2)}) collective-permute-start(bf16[1,1,1,1,16,2048]{5,4,3,2,1,0:T(8,128)(2,1)} %bitcast.246), channel_id=1, source_target_pairs={{0,8},{1,9},{2,10},{3,11},{4,12},{5,13},{6,14},{7,15},{8,16},{9,17... | collective-permute-start | bytes 196616 | tf_op jit(solution)/shard_map/ppermute | solution.py:41
  8.4 24.6 %collective-permute-start.7 = (bf16[1,1,1,1,16,2048]{5,4,3,2,1,0:T(8,128)(2,1)}, bf16[1,1,1,1,16,2048]{5,4,3,2,1,0:T(8,128)(2,1)S(1)}, u32[]{:S(2)}, u32[]{:S(2)}) collective-permute-start(bf16[1,1,1,1,16,2048]{5,4,3,2,1,0:T(8,128)(2,1)} %bitcast.247), channel_id=1, source_target_pairs={{0,16},{1,17},{2,18},{3,19},{4,20},{5,21},{6,22},{7,23},{8,24},{9,... | collective-permute-start | bytes 196616 | tf_op jit(solution)/shard_map/ppermute | solution.py:41
  10.6 38.6 %collective-permute-start.8 = (bf16[1,1,1,1,16,2048]{5,4,3,2,1,0:T(8,128)(2,1)}, bf16[1,1,1,1,16,2048]{5,4,3,2,1,0:T(8,128)(2,1)S(1)}, u32[]{:S(2)}, u32[]{:S(2)}) collective-permute-start(bf16[1,1,1,1,16,2048]{5,4,3,2,1,0:T(8,128)(2,1)} %bitcast.248), channel_id=1, source_target_pairs={{0,24},{1,25},{2,26},{3,27},{4,28},{5,29},{6,30},{7,31},{8,0},{9,1... | collective-permute-start | bytes 196616 | tf_op jit(solution)/shard_map/ppermute | solution.py:41
  13.5 6.7 %collective-permute-start.3 = (bf16[4,1,1,1,16,2048]{5,4,3,2,1,0:T(8,128)(2,1)S(1)}, bf16[4,1,1,1,16,2048]{5,4,3,2,1,0:T(8,128)(2,1)S(1)}, u32[]{:S(2)}, u32[]{:S(2)}) collective-permute-start(bf16[4,1,1,1,16,2048]{5,4,3,2,1,0:T(8,128)(2,1)S(1)} %constant_dynamic-update-slice_fusion), channel_id=1, source_target_pairs={{0,4},{1,5},{2,6},{3,7},{4,0},{5,1},{6,2},{7,3},{8,12},{9,13},{10,... | collective-permute-start | bytes 786440 | tf_op jit(solution)/shard_map/ppermute | solution.py:41
  15.2 73.0 %copy-start.10 = (s32[64,128]{1,0:T(8,128)}, s32[64,128]{1,0:T(8,128)S(1)}, u32[]{:S(2)}) copy-start(s32[64,128]{1,0:T(8,128)S(1)} %copy.80) | copy-start | bytes 98308
  20.3 11.4 %collective-permute-start.4 = (bf16[4,2,1,1,16,2048]{5,4,3,2,1,0:T(8,128)(2,1)S(1)}, bf16[4,2,1,1,16,2048]{5,4,3,2,1,0:T(8,128)(2,1)S(1)}, u32[]{:S(2)}, u32[]{:S(2)}) collective-permute-start(bf16[4,2,1,1,16,2048]{5,4,3,2,1,0:T(8,128)(2,1)S(1)} %maximum_select_fusion.5), channel_id=1, source_target_pairs={{0,2},{1,3},{2,0},{3,1},{4,6},{5,7},{6,4},{7,5},{8,10},{9,11},{10,... | collective-permute-start | bytes 1572872 | tf_op jit(solution)/shard_map/ppermute | solution.py:41
  32.8 3.0 %collective-permute-start.5 = (bf16[4,2,2,1,16,2048]{5,4,3,2,1,0:T(8,128)(2,1)}, bf16[4,2,2,1,16,2048]{5,4,3,2,1,0:T(8,128)(2,1)}, u32[]{:S(2)}, u32[]{:S(2)}) collective-permute-start(bf16[4,2,2,1,16,2048]{5,4,3,2,1,0:T(8,128)(2,1)} %maximum_select_fusion.2), channel_id=1, source_target_pairs={{0,1},{1,0},{2,3},{3,2},{4,5},{5,4},{6,7},{7,6},{8,9},{9,8},{10,11... | collective-permute-start | bytes 3145736 | tf_op jit(solution)/shard_map/ppermute | solution.py:41
  33.0 6.7 %copy-start.6 = (bf16[128,2048]{1,0:T(8,128)(2,1)S(1)}, bf16[128,2048]{1,0:T(8,128)(2,1)}, u32[]{:S(2)}) copy-start(bf16[128,2048]{1,0:T(8,128)(2,1)} %param.9) | copy-start | bytes 1572868
  44.4 52.6 %all-to-all-start = ((bf16[64,24,512]{2,1,0:T(8,128)(2,1)}), bf16[64,24,512]{2,1,0:T(8,128)(2,1)}, u32[]{:S(2)}, u32[]{:S(2)}) async-start(bf16[64,24,512]{2,1,0:T(8,128)(2,1)} %convolution_convert_fusion.4), calls=%async_computation | async-start | bytes 3145728 | tf_op jit(solution)/shard_map/all_to_all | solution.py:10
  49.2 22.0 %collective-permute-start.9 = (bf16[4,1,1,1,16,2048]{5,4,0,3,2,1:T(8,128)(2,1)S(1)}, bf16[4,1,1,1,16,2048]{5,4,0,3,2,1:T(8,128)(2,1)S(1)}, u32[]{:S(2)}, u32[]{:S(2)}) collective-permute-start(bf16[4,1,1,1,16,2048]{5,4,0,3,2,1:T(8,128)(2,1)S(1)} %bitcast_dynamic-update-slice_fusion.1), channel_id=1, source_target_pairs={{0,2},{1,3},{2,0},{3,1},{4,6},{5,7},{6,4},{7,5},{8,10},{9,11},{10,... | collective-permute-start | bytes 786440 | tf_op jit(solution)/shard_map/ppermute | solution.py:41
  71.2 16.9 %copy-start.16 = (s32[128,8]{0,1:T(8,128)S(1)}, s32[128,8]{0,1:T(8,128)}, u32[]{:S(2)}) copy-start(s32[128,8]{0,1:T(8,128)} %param.12) | copy-start | bytes 12292
  71.2 16.9 %copy-start.15 = (s32[128,8]{0,1:T(8,128)S(1)}, s32[128,8]{0,1:T(8,128)}, u32[]{:S(2)}) copy-start(s32[128,8]{0,1:T(8,128)} %param.11) | copy-start | bytes 12292
  71.4 16.6 %collective-permute-start.10 = (bf16[4,1,2,1,16,2048]{5,4,3,2,1,0:T(8,128)(2,1)S(1)}, bf16[4,1,2,1,16,2048]{5,4,3,2,1,0:T(8,128)(2,1)S(1)}, u32[]{:S(2)}, u32[]{:S(2)}) collective-permute-start(bf16[4,1,2,1,16,2048]{5,4,3,2,1,0:T(8,128)(2,1)S(1)} %maximum_select_fusion.7), channel_id=1, source_target_pairs={{0,4},{1,5},{2,6},{3,7},{4,0},{5,1},{6,2},{7,3},{8,12},{9,13},{10,... | collective-permute-start | bytes 1572872 | tf_op jit(solution)/shard_map/ppermute | solution.py:41
  88.0 2.7 collective-permute-start.11
  88.2 0.6 copy-start.12
  88.9 3.4 %copy-start.7 = (bf16[128,2048]{1,0:T(8,128)(2,1)S(1)}, bf16[128,2048]{1,0:T(8,128)(2,1)}, u32[]{:S(2)}) copy-start(bf16[128,2048]{1,0:T(8,128)(2,1)} %param.10) | copy-start | bytes 1572868
  97.1 42.6 %all-to-all-start.2 = ((bf16[64,24,512]{2,1,0:T(8,128)(2,1)}), bf16[64,24,512]{2,1,0:T(8,128)(2,1)}, u32[]{:S(2)}, u32[]{:S(2)}) async-start(bf16[64,24,512]{2,1,0:T(8,128)(2,1)} %convolution_convert_fusion.5), calls=%async_computation.2 | async-start | bytes 3145728 | tf_op jit(solution)/shard_map/all_to_all | solution.py:10
  102.1 6.1 %copy-start.8 = (bf16[2,512,1024]{2,1,0:T(8,128)(2,1)S(1)}, bf16[2,512,1024]{2,1,0:T(8,128)(2,1)}, u32[]{:S(2)}) copy-start(bf16[2,512,1024]{2,1,0:T(8,128)(2,1)} %param.15) | copy-start | bytes 6291460
  139.6 6.7 %copy-start.4 = (f32[2,32,24,1024]{3,2,1,0:T(8,128)S(1)}, f32[2,32,24,1024]{3,2,1,0:T(8,128)}, u32[]{:S(2)}) copy-start(f32[2,32,24,1024]{3,2,1,0:T(8,128)} %fusion.22) | copy-start | bytes 18874372
  143.7 2.6 copy-start.5
  162.8 3.9 %copy-start.9 = (bf16[2,1024,512]{2,1,0:T(8,128)(2,1)S(1)}, bf16[2,1024,512]{2,1,0:T(8,128)(2,1)}, u32[]{:S(2)}) copy-start(bf16[2,1024,512]{2,1,0:T(8,128)(2,1)} %param.17) | copy-start | bytes 6291460
  162.8 41.6 %all-to-all-start.3 = ((bf16[64,24,512]{2,1,0:T(8,128)(2,1)}), bf16[64,24,512]{2,1,0:T(8,128)(2,1)}, u32[]{:S(2)}, u32[]{:S(2)}) async-start(bf16[64,24,512]{2,1,0:T(8,128)(2,1)} %bitcast.40), calls=%async_computation.3 | async-start | bytes 3145728 | tf_op jit(solution)/shard_map/all_to_all | solution.py:10
  175.0 33.4 %copy-start.11 = (s32[64,128]{1,0:T(8,128)S(1)}, s32[64,128]{1,0:T(8,128)}, u32[]{:S(2)}) copy-start(s32[64,128]{1,0:T(8,128)} %copy-done.10) | copy-start | bytes 98308
  204.4 41.6 %all-to-all-start.1 = ((bf16[64,24,512]{2,1,0:T(8,128)(2,1)}), bf16[64,24,512]{2,1,0:T(8,128)(2,1)S(1)}, u32[]{:S(2)}, u32[]{:S(2)}) async-start(bf16[64,24,512]{2,1,0:T(8,128)(2,1)} %bitcast.19), calls=%async_computation.1 | async-start | bytes 3145728 | tf_op jit(solution)/shard_map/all_to_all | solution.py:10
  208.4 37.5 %copy-start.13 = (bf16[128,64]{0,1:T(8,128)(2,1)S(1)}, bf16[128,64]{0,1:T(8,128)(2,1)}, u32[]{:S(2)}) copy-start(bf16[128,64]{0,1:T(8,128)(2,1)} %copy-done.12) | copy-start | bytes 49156
  212.0 37.1 %collective-permute-start.12 = (bf16[4,2,2,1,16,2048]{5,4,2,1,0,3:T(8,128)(2,1)}, bf16[4,2,2,1,16,2048]{5,4,2,1,0,3:T(8,128)(2,1)}, u32[]{:S(2)}, u32[]{:S(2)}) collective-permute-start(bf16[4,2,2,1,16,2048]{5,4,2,1,0,3:T(8,128)(2,1)} %fusion.16), channel_id=1, source_target_pairs={{0,1},{1,0},{2,3},{3,2},{4,5},{5,4},{6,7},{7,6},{8,9},{9,8},{10,11... | collective-permute-start | bytes 3145736 | tf_op jit(solution)/shard_map/ppermute | solution.py:41
  248.3 3.6 %collective-permute-start.18 = (bf16[4,2,2,1,16,2048]{5,4,2,1,0,3:T(8,128)(2,1)}, bf16[4,2,2,1,16,2048]{5,4,2,1,0,3:T(8,128)(2,1)}, u32[]{:S(2)}, u32[]{:S(2)}) collective-permute-start(bf16[4,2,2,1,16,2048]{5,4,2,1,0,3:T(8,128)(2,1)} %fusion.17), channel_id=1, source_target_pairs={{0,1},{1,0},{2,3},{3,2},{4,5},{5,4},{6,7},{7,6},{8,9},{9,8},{10,11... | collective-permute-start | bytes 3145736 | tf_op jit(solution)/shard_map/ppermute | solution.py:41
  250.7 4.3 %copy-start.3 = (bf16[4,2,2,2,16,2048]{5,4,3,2,1,0:T(8,128)(2,1)S(1)}, bf16[4,2,2,2,16,2048]{5,4,3,2,1,0:T(8,128)(2,1)}, u32[]{:S(2)}) copy-start(bf16[4,2,2,2,16,2048]{5,4,3,2,1,0:T(8,128)(2,1)} %maximum_select_fusion.1) | copy-start | bytes 6291460
  250.7 14.4 %collective-permute-start.13 = (bf16[4,2,1,1,16,2048]{5,4,2,1,0,3:T(8,128)(2,1)S(1)}, bf16[4,2,1,1,16,2048]{5,4,2,1,0,3:T(8,128)(2,1)S(1)}, u32[]{:S(2)}, u32[]{:S(2)}) collective-permute-start(bf16[4,2,1,1,16,2048]{5,4,2,1,0,3:T(8,128)(2,1)S(1)} %get-tuple-element.6), channel_id=1, source_target_pairs={{0,2},{1,3},{2,0},{3,1},{4,6},{5,7},{6,4},{7,5},{8,10},{9,11},{10,... | collective-permute-start | bytes 1572872 | tf_op jit(solution)/shard_map/ppermute | solution.py:41
  253.4 14.1 %collective-permute-start.19 = (bf16[4,1,2,1,16,2048]{5,4,2,1,0,3:T(8,128)(2,1)S(1)}, bf16[4,1,2,1,16,2048]{5,4,2,1,0,3:T(8,128)(2,1)S(1)}, u32[]{:S(2)}, u32[]{:S(2)}) collective-permute-start(bf16[4,1,2,1,16,2048]{5,4,2,1,0,3:T(8,128)(2,1)S(1)} %get-tuple-element.4), channel_id=1, source_target_pairs={{0,4},{1,5},{2,6},{3,7},{4,0},{5,1},{6,2},{7,3},{8,12},{9,13},{10,... | collective-permute-start | bytes 1572872 | tf_op jit(solution)/shard_map/ppermute | solution.py:41
  265.1 3.5 %copy-start.2 = (bf16[4,2,2,2,16,2048]{5,4,3,2,1,0:T(8,128)(2,1)S(1)}, bf16[4,2,2,2,16,2048]{5,4,3,2,1,0:T(8,128)(2,1)}, u32[]{:S(2)}) copy-start(bf16[4,2,2,2,16,2048]{5,4,3,2,1,0:T(8,128)(2,1)} %maximum_select_fusion) | copy-start | bytes 6291460
  265.2 8.0 %collective-permute-start.14 = (bf16[4,1,1,1,16,2048]{5,4,2,1,0,3:T(8,128)(2,1)S(1)}, bf16[4,1,1,1,16,2048]{5,4,2,1,0,3:T(8,128)(2,1)S(1)}, u32[]{:S(2)}, u32[]{:S(2)}) collective-permute-start(bf16[4,1,1,1,16,2048]{5,4,2,1,0,3:T(8,128)(2,1)S(1)} %get-tuple-element.10), channel_id=1, source_target_pairs={{0,4},{1,5},{2,6},{3,7},{4,0},{5,1},{6,2},{7,3},{8,12},{9,13},{10,... | collective-permute-start | bytes 786440 | tf_op jit(solution)/shard_map/ppermute | solution.py:41
  267.6 20.1 %copy-start.1 = (bf16[2,512,1024]{2,1,0:T(8,128)(2,1)S(1)}, bf16[2,512,1024]{2,1,0:T(8,128)(2,1)}, u32[]{:S(2)}) copy-start(bf16[2,512,1024]{2,1,0:T(8,128)(2,1)} %param.16) | copy-start | bytes 6291460
  267.6 8.4 %collective-permute-start.20 = (bf16[4,1,1,1,16,2048]{5,4,2,1,0,3:T(8,128)(2,1)S(1)}, bf16[4,1,1,1,16,2048]{5,4,2,1,0,3:T(8,128)(2,1)S(1)}, u32[]{:S(2)}, u32[]{:S(2)}) collective-permute-start(bf16[4,1,1,1,16,2048]{5,4,2,1,0,3:T(8,128)(2,1)S(1)} %get-tuple-element.8), channel_id=1, source_target_pairs={{0,2},{1,3},{2,0},{3,1},{4,6},{5,7},{6,4},{7,5},{8,10},{9,11},{10,... | collective-permute-start | bytes 786440 | tf_op jit(solution)/shard_map/ppermute | solution.py:41
  273.2 6.6 %collective-permute-start.17 = (bf16[1,1,1,1,16,2048]{5,4,2,1,0,3:T(8,128)(2,1)S(1)}, bf16[1,1,1,1,16,2048]{5,4,2,1,0,3:T(8,128)(2,1)S(1)}, u32[]{:S(2)}, u32[]{:S(2)}) collective-permute-start(bf16[1,1,1,1,16,2048]{5,4,2,1,0,3:T(8,128)(2,1)S(1)} %get-tuple-element.16), channel_id=1, source_target_pairs={{0,24},{1,25},{2,26},{3,27},{4,28},{5,29},{6,30},{7,31},{8,0},{9,1... | collective-permute-start | bytes 196616 | tf_op jit(solution)/shard_map/ppermute | solution.py:41
  274.8 9.4 %collective-permute-start.16 = (bf16[1,1,1,1,16,2048]{5,4,2,1,0,3:T(8,128)(2,1)S(1)}, bf16[1,1,1,1,16,2048]{5,4,2,1,0,3:T(8,128)(2,1)S(1)}, u32[]{:S(2)}, u32[]{:S(2)}) collective-permute-start(bf16[1,1,1,1,16,2048]{5,4,2,1,0,3:T(8,128)(2,1)S(1)} %get-tuple-element.17), channel_id=1, source_target_pairs={{0,16},{1,17},{2,18},{3,19},{4,20},{5,21},{6,22},{7,23},{8,24},{9,... | collective-permute-start | bytes 196616 | tf_op jit(solution)/shard_map/ppermute | solution.py:41
  274.9 9.3 %collective-permute-start.15 = (bf16[1,1,1,1,16,2048]{5,4,2,1,0,3:T(8,128)(2,1)S(1)}, bf16[1,1,1,1,16,2048]{5,4,2,1,0,3:T(8,128)(2,1)S(1)}, u32[]{:S(2)}, u32[]{:S(2)}) collective-permute-start(bf16[1,1,1,1,16,2048]{5,4,2,1,0,3:T(8,128)(2,1)S(1)} %get-tuple-element.15), channel_id=1, source_target_pairs={{0,8},{1,9},{2,10},{3,11},{4,12},{5,13},{6,14},{7,15},{8,16},{9,17... | collective-permute-start | bytes 196616 | tf_op jit(solution)/shard_map/ppermute | solution.py:41
  276.0 8.9 %collective-permute-start.23 = (bf16[1,1,1,1,16,2048]{5,4,2,1,0,3:T(8,128)(2,1)S(1)}, bf16[1,1,1,1,16,2048]{5,4,2,1,0,3:T(8,128)(2,1)S(1)}, u32[]{:S(2)}, u32[]{:S(2)}) collective-permute-start(bf16[1,1,1,1,16,2048]{5,4,2,1,0,3:T(8,128)(2,1)S(1)} %get-tuple-element.13), channel_id=1, source_target_pairs={{0,24},{1,25},{2,26},{3,27},{4,28},{5,29},{6,30},{7,31},{8,0},{9,1... | collective-permute-start | bytes 196616 | tf_op jit(solution)/shard_map/ppermute | solution.py:41
  278.9 8.1 %collective-permute-start.22 = (bf16[1,1,1,1,16,2048]{5,4,2,1,0,3:T(8,128)(2,1)S(1)}, bf16[1,1,1,1,16,2048]{5,4,2,1,0,3:T(8,128)(2,1)S(1)}, u32[]{:S(2)}, u32[]{:S(2)}) collective-permute-start(bf16[1,1,1,1,16,2048]{5,4,2,1,0,3:T(8,128)(2,1)S(1)} %get-tuple-element.14), channel_id=1, source_target_pairs={{0,16},{1,17},{2,18},{3,19},{4,20},{5,21},{6,22},{7,23},{8,24},{9,... | collective-permute-start | bytes 196616 | tf_op jit(solution)/shard_map/ppermute | solution.py:41
  279.8 7.2 %collective-permute-start.21 = (bf16[1,1,1,1,16,2048]{5,4,2,1,0,3:T(8,128)(2,1)S(1)}, bf16[1,1,1,1,16,2048]{5,4,2,1,0,3:T(8,128)(2,1)S(1)}, u32[]{:S(2)}, u32[]{:S(2)}) collective-permute-start(bf16[1,1,1,1,16,2048]{5,4,2,1,0,3:T(8,128)(2,1)S(1)} %get-tuple-element.12), channel_id=1, source_target_pairs={{0,8},{1,9},{2,10},{3,11},{4,12},{5,13},{6,14},{7,15},{8,16},{9,17... | collective-permute-start | bytes 196616 | tf_op jit(solution)/shard_map/ppermute | solution.py:41

commit v2 on v1

v2 whole, which is shorter than its diff:
```python
import math

import jax
import jax.numpy as jnp
from jax import lax
from jax.experimental import pallas as pl
from jax.experimental.pallas import tpu as pltpu
from jax.sharding import PartitionSpec as P

OWNERS = ("expert", "dp")
EXPERT = ("expert",)
Z, Y, X, CORE = 0, 1, 2, 3
FAR_AWAY = -128.0


def tensor_total(partial_sum):
    return lax.psum(partial_sum, "tensor")


def radices(count):
    return (count // 8, 2, 2, 2)


def digit_of(axes, place):
    sizes = radices(math.prod(lax.axis_size(axis) for axis in axes))
    stride = math.prod(sizes[place + 1 :])
    return lax.rem(lax.axis_index(axes) // stride, sizes[place])


def shifted(block, axes, place, step=1):
    count = math.prod(lax.axis_size(axis) for axis in axes)
    sizes = radices(count)
    stride = math.prod(sizes[place + 1 :])
    pairs = []
    for here in range(count):
        digit = here // stride % sizes[place]
        pairs.append((here, here + ((digit + step) % sizes[place] - digit) * stride))
    return lax.ppermute(block, axes, pairs)


def gather_rows(shard, count, order):
    sizes = radices(count)
    block = shard.reshape((1, 1, 1, 1) + shard.shape)
    for place in order:
        size = sizes[place]
        digit = digit_of(OWNERS, place)
        if size == 2:
            other = shifted(block, OWNERS, place)
            block = jnp.where(
                digit == 0,
                lax.concatenate([block, other], place),
                lax.concatenate([other, block], place),
            )
            continue
        pieces = [block] + [shifted(block, OWNERS, place, step) for step in range(1, size)]
        whole = jnp.zeros(block.shape[:place] + (size,) + block.shape[place + 1 :], block.dtype)
        for step, piece in enumerate(pieces):
            owner = lax.rem(digit + size - step, size)
            whole = lax.dynamic_update_slice_in_dim(whole, piece, owner, place)
        block = whole
    return block.reshape((count * shard.shape[0],) + shard.shape[1:])


def scatter_total(left, right, count, order):
    sizes = radices(count)
    width = left.shape[1]
    columns = left.reshape((left.shape[0],) + sizes + (width // count,))

    def product(part):
        out = jnp.einsum(
            "tl,td->ld", part.reshape(left.shape[0], -1), right, preferred_element_type=jnp.float32
        )
        return out.reshape(part.shape[1:] + right.shape[1:])

    def own(array, place, step, offset):
        size = sizes[place]
        where = lax.rem(digit_of(OWNERS, place) + step, size)
        return lax.dynamic_slice_in_dim(array, where, 1, place + offset)

    first, rest = order[0], order[1:]
    received = [
        shifted(product(own(columns, first, step, 1)).astype(jnp.bfloat16), OWNERS, first, step)
        for step in range(1, sizes[first])
    ]
    kept = product(own(columns, first, 0, 1))
    for place in rest:
        size = sizes[place]
        arriving = []
        for step in range(1, size):
            part = own(kept, place, step, 0)
            for block in received:
                part = part + own(block, place, step, 0).astype(jnp.float32)
            arriving.append(shifted(part.astype(jnp.bfloat16), OWNERS, place, step))
        kept = own(kept, place, 0, 0)
        for block in received:
            kept = kept + own(block, place, 0, 0).astype(jnp.float32)
        received = arriving
    for block in received:
        kept = kept + block.astype(jnp.float32)
    return kept.reshape(width // count, right.shape[1])


def relative_owner(core_step, y_step, x_step, z_step):
    depth = radices(lax.axis_size("expert"))[Z]
    z = lax.rem(digit_of(EXPERT, Z) + depth - z_step, depth)
    y = lax.rem(digit_of(EXPERT, Y) + y_step, 2)
    x = lax.rem(digit_of(EXPERT, X) + x_step, 2)
    core = lax.rem(digit_of(EXPERT, CORE) + core_step, 2)
    return ((z * 2 + y) * 2 + x) * 2 + core


def relative_owners():
    depth = radices(lax.axis_size("expert"))[Z]
    return jnp.stack(
        [
            relative_owner(core_step, y_step, x_step, z_step)
            for core_step in (0, 1)
            for y_step, x_step in ((0, 0), (1, 0), (0, 1), (1, 1))
            for z_step in range(depth)
        ]
    )


def gather_tokens(rows):
    depth = radices(lax.axis_size("expert"))[Z]
    half = rows.shape[1] // 2
    own = lax.concatenate([rows] + [shifted(rows, EXPERT, Z, step) for step in range(1, depth)], 0)
    along_y = shifted(own, EXPERT, Y)
    along_x = shifted(own, EXPERT, X)
    across = lax.concatenate(
        [shifted(along_y[:, :half], EXPERT, X), shifted(along_x[:, half:], EXPERT, Y)], 1
    )
    near = lax.concatenate([own, along_y, along_x, across], 0)
    return near, shifted(near, EXPERT, CORE)


def total_tokens(near, far):
    depth = radices(lax.axis_size("expert"))[Z]
    half = near.shape[1] // 2
    terms = near.astype(jnp.float32) + shifted(far, EXPERT, CORE).astype(jnp.float32)
    own, along_y, along_x, across = jnp.split(terms, 4, axis=0)
    across = across.astype(jnp.bfloat16)
    left = shifted(across[:, :half], EXPERT, X).astype(jnp.float32)
    right = shifted(across[:, half:], EXPERT, Y).astype(jnp.float32)
    along_y = lax.concatenate([along_y[:, :half] + left, along_y[:, half:]], 1)
    along_x = lax.concatenate([along_x[:, :half], along_x[:, half:] + right], 1)
    own = own + shifted(along_y.astype(jnp.bfloat16), EXPERT, Y).astype(jnp.float32)
    own = own + shifted(along_x.astype(jnp.bfloat16), EXPERT, X).astype(jnp.float32)
    pieces = jnp.split(own, depth, axis=0)
    total = pieces[0]
    for step in range(1, depth):
        piece = shifted(pieces[step].astype(jnp.bfloat16), EXPERT, Z, depth - step)
        total = total + piece.astype(jnp.float32)
    return total


def matmul(left, right, contract=((1,), (0,))):
    return lax.dot_general(left, right, (contract, ((), ())), preferred_element_type=jnp.float32)


def selected(slot_ref, group, expert, slots, values=None):
    slot = slot_ref[group, expert]
    here = lax.broadcasted_iota(jnp.int32, (slots, slot.shape[1]), 0) == slot
    return jnp.where(here, 1.0 if values is None else values, 0.0).astype(jnp.bfloat16)


def forward_kernel(
    slot_ref,
    scale_ref,
    near_ref,
    far_ref,
    gate_ref,
    up_ref,
    down_ref,
    near_out,
    far_out,
    rows,
    hidden,
    results,
):
    experts, groups, slots, _ = results.shape
    span = near_ref.shape[0] // groups
    width = hidden.shape[1]
    chunk = 256
    for side, (source, target) in enumerate(((near_ref, near_out), (far_ref, far_out))):

        @pl.loop(0, experts)
        def _(expert):
            for group in range(groups):
                pick = selected(slot_ref, side * groups + group, expert, slots)
                picked = matmul(pick, source[group * span : (group + 1) * span, :])
                rows[group * slots : (group + 1) * slots, :] = picked.astype(jnp.bfloat16)
            for start in range(0, width, chunk):
                columns = slice(start, start + chunk)
                gate_act = matmul(rows[...], gate_ref[expert, :, columns])
                up_act = matmul(rows[...], up_ref[expert, :, columns])
                act = gate_act * jax.nn.sigmoid(gate_act) * up_act
                hidden[:, columns] = act.astype(jnp.bfloat16)
            result = matmul(hidden[...], down_ref[expert]).astype(jnp.bfloat16)
            for group in range(groups):
                results[expert, group] = result[group * slots : (group + 1) * slots, :]

        for group in range(groups):
            place = side * groups + group
            weights = jnp.concatenate(
                [
                    selected(slot_ref, place, expert, slots, scale_ref[place, expert])
                    for expert in range(experts)
                ],
                0,
            )
            values = jnp.concatenate([results[expert, group] for expert in range(experts)], 0)
            mixed = matmul(weights, values, ((0,), (0,)))
            target[group * span : (group + 1) * span, :] = mixed.astype(jnp.bfloat16)


def backward_kernel(
    slot_ref,
    scale_ref,
    near_ref,
    far_ref,
    near_grad,
    far_grad,
    gate_ref,
    up_ref,
    down_ref,
    near_out,
    far_out,
    rows,
    grads,
    gate_grads,
    value_grads,
    results,
):
    experts, groups, slots, _ = results.shape
    span = near_ref.shape[0] // groups
    width = gate_grads.shape[1]
    chunk = 256
    for side, (source, source_grad, target) in enumerate(
        ((near_ref, near_grad, near_out), (far_ref, far_grad, far_out))
    ):

        @pl.loop(0, experts)
        def _(expert):
            for group in range(groups):
                place = side * groups + group
                tokens = slice(group * span, (group + 1) * span)
                held = slice(group * slots, (group + 1) * slots)
                pick = selected(slot_ref, place, expert, slots)
                rows[held, :] = matmul(pick, source[tokens, :]).astype(jnp.bfloat16)
                weighed = selected(slot_ref, place, expert, slots, scale_ref[place, expert])
                grads[held, :] = matmul(weighed, source_grad[tokens, :]).astype(jnp.bfloat16)
            for start in range(0, width, chunk):
                columns = slice(start, start + chunk)
                gate_act = matmul(rows[...], gate_ref[expert, :, columns])
                up_act = matmul(rows[...], up_ref[expert, :, columns])
                hidden_grad = matmul(grads[...], down_ref[expert, columns, :], ((1,), (1,)))
                sigmoid = jax.nn.sigmoid(gate_act)
                scaled = hidden_grad * sigmoid
                gate_grad = scaled * up_act * (1.0 + gate_act * (1.0 - sigmoid))
                gate_grads[:, columns] = gate_grad.astype(jnp.bfloat16)
                value_grads[:, columns] = (scaled * gate_act).astype(jnp.bfloat16)
            result = matmul(gate_grads[...], gate_ref[expert], ((1,), (1,)))
            result = result + matmul(value_grads[...], up_ref[expert], ((1,), (1,)))
            result = result.astype(jnp.bfloat16)
            for group in range(groups):
                results[expert, group] = result[group * slots : (group + 1) * slots, :]

        for group in range(groups):
            place = side * groups + group
            picks = jnp.concatenate(
                [selected(slot_ref, place, expert, slots) for expert in range(experts)], 0
            )
            values = jnp.concatenate([results[expert, group] for expert in range(experts)], 0)
            total = matmul(picks, values, ((0,), (0,)))
            target[group * span : (group + 1) * span, :] = total.astype(jnp.bfloat16)


def expert_call(kernel, products, scratch, slots, scales, arrays, weights):
    near = arrays[0]
    experts, latent_width, width = weights[0].shape
    operands = (slots, scales) + tuple(arrays) + tuple(weights)
    whole = pl.BlockSpec(memory_space=pltpu.VMEM)
    row_count = scratch[0].shape[0] * 2
    return pl.pallas_call(
        kernel,
        out_shape=(jax.ShapeDtypeStruct(near.shape, jnp.bfloat16),) * 2,
        in_specs=[whole] * len(operands),
        out_specs=(whole,) * 2,
        scratch_shapes=scratch,
        compiler_params=pltpu.CompilerParams(vmem_limit_bytes=44 << 20),
        cost_estimate=pl.CostEstimate(
            flops=2 * products * experts * row_count * latent_width * width,
            bytes_accessed=sum(array.size * 2 for array in operands) + near.size * 4,
            transcendentals=experts * row_count * width,
        ),
    )(*operands)


def local(
    tokens, out_grad, routes, combine_fixed, down_proj, up_proj, expert_gate, expert_up, expert_down
):
    count = lax.axis_size("expert") * lax.axis_size("dp")
    down_full = gather_rows(down_proj, count, (Z, Y, X, CORE))
    up_full = gather_rows(up_proj, count, (Z, X, Y, CORE))
    row_count = tokens.shape[0]
    top_count = routes.shape[1]
    latent_width = down_full.shape[0]
    local_experts, _, width = expert_gate.shape
    shards = lax.axis_size("expert")
    depth = radices(shards)[Z]
    experts = local_experts * shards
    capacity = 3 * row_count * top_count // (2 * experts)

    chosen = routes[:, :, None] == jnp.arange(experts, dtype=jnp.int32)[None, None, :]
    member = jnp.any(chosen, axis=1)
    ranking = jnp.cumsum(member.astype(jnp.int32), axis=0) - 1
    slot = jnp.where(member, ranking.astype(jnp.float32), FAR_AWAY)
    fixed = jnp.sum(jnp.where(chosen, combine_fixed[:, :, None], 0), axis=1).astype(jnp.float32)
    plan = jnp.stack(
        [
            slot.T.reshape(shards, local_experts, row_count),
            fixed.T.reshape(shards, local_experts, row_count),
        ],
        1,
    )
    plan = plan.reshape(shards, 2 * local_experts * row_count).astype(jnp.bfloat16)
    plan = lax.all_to_all(plan, "expert", split_axis=0, concat_axis=0, tiled=True)
    order = relative_owners()[:, None] == jnp.arange(shards, dtype=jnp.int32)[None, :]
    plan = jnp.dot(order.astype(jnp.bfloat16), plan, preferred_element_type=jnp.float32)
    plan = plan.reshape(shards // depth, depth, 2, local_experts, row_count)
    plan = plan.transpose(2, 0, 3, 1, 4)
    offsets = (jnp.arange(depth, dtype=jnp.float32) * capacity)[:, None]
    slots = (plan[0] + offsets).astype(jnp.int32)
    slots = slots.reshape(shards // depth, local_experts, 1, depth * row_count)
    scales = (plan[1] / 256.0).reshape(slots.shape)

    latent_part = jnp.einsum("td,ld->tl", tokens, down_full, preferred_element_type=jnp.float32)
    latent = tensor_total(latent_part).astype(jnp.bfloat16)
    mix_part = jnp.einsum("td,ld->tl", out_grad, up_full, preferred_element_type=jnp.float32)
    mix_grad = tensor_total(mix_part).astype(jnp.bfloat16)
    latents = gather_tokens(latent)
    mix_grads = gather_tokens(mix_grad)

    half = shards // depth // 2 * depth * capacity
    narrow = pltpu.VMEM((half, latent_width), jnp.bfloat16)
    wide = pltpu.VMEM((half, width), jnp.bfloat16)
    held = pltpu.VMEM(
        (local_experts, shards // depth // 2, depth * capacity, latent_width), jnp.bfloat16
    )
    weights = (expert_gate, expert_up, expert_down)
    mixed_terms = expert_call(
        forward_kernel, 3, (narrow, wide, held), slots, scales, latents, weights
    )
    grad_terms = expert_call(
        backward_kernel,
        5,
        (narrow, narrow, wide, wide, held),
        slots,
        scales,
        latents + mix_grads,
        weights,
    )
    mixed_rows = tensor_total(total_tokens(*mixed_terms)).astype(jnp.bfloat16)
    latent_grad = tensor_total(total_tokens(*grad_terms)).astype(jnp.bfloat16)

    layer_out = jnp.dot(mixed_rows, up_full, preferred_element_type=jnp.float32).astype(
        jnp.bfloat16
    )
    token_grad = jnp.dot(latent_grad, down_full, preferred_element_type=jnp.float32).astype(
        jnp.bfloat16
    )
    up_grad = scatter_total(mixed_rows, out_grad, count, (CORE, Y, X, Z))
    down_grad = scatter_total(latent_grad, tokens, count, (CORE, X, Y, Z))
    return (layer_out, token_grad, down_grad, up_grad)


def solution(mesh):
    in_specs = (
        P(("groups", "expert", "dp"), "tensor"),
        P(("groups", "expert", "dp"), "tensor"),
        P(("groups", "expert", "dp"), None),
        P(("groups", "expert", "dp"), None),
        P(("expert", "dp"), "tensor"),
        P(("expert", "dp"), "tensor"),
        P("expert", None, "tensor"),
        P("expert", None, "tensor"),
        P("expert", "tensor", None),
    )
    out_specs = (
        P(("groups", "expert", "dp"), "tensor"),
        P(("groups", "expert", "dp"), "tensor"),
        P(("groups", "expert", "dp"), "tensor"),
        P(("groups", "expert", "dp"), "tensor"),
    )
    return jax.shard_map(local, mesh=mesh, in_specs=in_specs, out_specs=out_specs, check_vma=False)
```

time: 288 us -> 239 us (0.83)
  waiting for transfers between devices: 163 us -> 95.8 us
  matrix products: 56.5 us -> 8.7 us
  Pallas kernels: 0 us -> 30.2 us
  starting transfers between devices: 47.1 us -> 73.4 us
  other arithmetic: 12.9 us -> 20.2 us
    all_to_all x4 -> x1, waiting for transfers between devices: 88.9 us -> 6.66 us  [local(): lax.all_to_all(plan, 'expert', split_axis=0, concat_axis=0, tiled=True)]
    dot_general x10 -> x3, matrix products: 50.3 us -> 2.5 us  [the longest x1 1.48 us: local(): jnp.einsum('td,ld->tl', out_grad, up_full, preferred_element_type=jnp.flo...]
    ppermute x24 -> x56, starting transfers between devices: 29.6 us -> 63.4 us  [shifted(): return lax.ppermute(block, axes, pairs)]
    pallas_call x0 -> x2, Pallas kernels: none -> 30.2 us  [expert_call(): pl.pallas_call(kernel, out_shape=(jax.ShapeDtypeStruct(near.shape, jnp.bf...]
    ppermute x24 -> x56, waiting for transfers between devices: 73.8 us -> 89.2 us  [shifted(): return lax.ppermute(block, axes, pairs)]
    another operation x0 -> x8, other arithmetic: none -> 8.4 us
    all_to_all x4 -> x1, starting transfers between devices: 17.5 us -> 10 us  [local(): lax.all_to_all(plan, 'expert', split_axis=0, concat_axis=0, tiled=True)]
  transfers between devices with their start and end apart: 28 -> 57, of which waited for: 14 -> 31; matrix products, arithmetic and copies ran while one was open for 18% -> 15% of each run, Pallas kernels for 0% -> 5%
where the time goes in v2:
time: 239 us; the launch traced here: 238 us
  waiting for transfers between devices  95.8 us (40%)
  starting transfers between devices  73.4 us (31%)
  Pallas kernels  30.2 us (13%)
  other arithmetic  20.2 us (8%)
  local copies, waits for them, and re-layouts  8.73 us (4%)
  matrix products  8.7 us (4%)
    ppermute x56, waiting for transfers between devices, shifted(): return lax.ppermute(block, axes, pairs)  89.2 us
    ppermute x56, starting transfers between devices, shifted(): return lax.ppermute(block, axes, pairs)  63.4 us
    pallas_call x2, Pallas kernels, expert_call(): pl.pallas_call(kernel, out_shape=(jax.ShapeDtypeStruct(near.shape, jnp.bf...  30.2 us
    all_to_all x1, starting transfers between devices, local(): lax.all_to_all(plan, 'expert', split_axis=0, concat_axis=0, tiled=True)  10 us
    another operation x7, other arithmetic  8.35 us
    all_to_all x1, waiting for transfers between devices, local(): lax.all_to_all(plan, 'expert', split_axis=0, concat_axis=0, tiled=True)  6.66 us
  transfers between devices with their start and end apart: 57, of which 31 were waited for; matrix products, arithmetic and copies ran while one was open for 15% of the time, Pallas kernels for 5%

profile of v2, /device:TPU:0, one launch (start us, length us, event | category | flops | bytes accessed | tf_op | source)
XLA Modules:
  0.0 238.4 jit_solution(11991748608697683144)
XLA Ops:
  0.6 3.1 %collective-permute-start = (bf16[1,1,1,1,16,2048]{5,4,3,2,1,0:T(8,128)(2,1)}, bf16[1,1,1,1,16,2048]{5,4,3,2,1,0:T(8,128)(2,1)S(1)}, u32[]{:S(2)}, u32[]{:S(2)}) collective-permute-start(bf16[1,1,1,1,16,2048]{5,4,3,2,1,0:T(8,128)(2,1)} %bitcast.181), channel_id=1, source_target_pairs={{0,8},{1,9},{2,10},{3,11},{4,12},{5,13},{6,14},{7,15},{8,16},{9,17... | collective-permute-start | bytes 196616 | tf_op jit(solution)/shard_map/ppermute | solution.py:38
  3.7 2.6 %collective-permute-start.1 = (bf16[1,1,1,1,16,2048]{5,4,3,2,1,0:T(8,128)(2,1)}, bf16[1,1,1,1,16,2048]{5,4,3,2,1,0:T(8,128)(2,1)S(1)}, u32[]{:S(2)}, u32[]{:S(2)}) collective-permute-start(bf16[1,1,1,1,16,2048]{5,4,3,2,1,0:T(8,128)(2,1)} %bitcast.182), channel_id=1, source_target_pairs={{0,16},{1,17},{2,18},{3,19},{4,20},{5,21},{6,22},{7,23},{8,24},{9,... | collective-permute-start | bytes 196616 | tf_op jit(solution)/shard_map/ppermute | solution.py:38
  10.4 2.9 %collective-permute-start.24 = (bf16[1,1,1,1,16,2048]{5,4,3,2,1,0:T(8,128)(2,1)}, bf16[1,1,1,1,16,2048]{5,4,3,2,1,0:T(8,128)(2,1)S(1)}, u32[]{:S(2)}, u32[]{:S(2)}) collective-permute-start(bf16[1,1,1,1,16,2048]{5,4,3,2,1,0:T(8,128)(2,1)} %bitcast.186), channel_id=1, source_target_pairs={{0,24},{1,25},{2,26},{3,27},{4,28},{5,29},{6,30},{7,31},{8,0},{9,1... | collective-permute-start | bytes 196616 | tf_op jit(solution)/shard_map/ppermute | solution.py:38
  13.4 1.6 collective-permute-start.3
  15.0 1.7 collective-permute-done.23
  17.2 1.6 collective-permute-start.25
  20.1 1.6 collective-permute-start.4
  21.7 4.8 %collective-permute-done.25 = bf16[4,1,1,1,16,2048]{5,4,0,3,2,1:T(8,128)(2,1)S(1)} collective-permute-done((bf16[4,1,1,1,16,2048]{5,4,0,3,2,1:T(8,128)(2,1)S(1)}, bf16[4,1,1,1,16,2048]{5,4,0,3,2,1:T(8,128)(2,1)S(1)}, u32[]{:S(2)}, u32[]{:S(2)}) %collective-permute-start.25) | collective-permute-done | bytes 262176 | tf_op jit(solution)/shard_map/ppermute | solution.py:38
  26.6 1.6 collective-permute-start.26
  28.3 7.7 %collective-permute-done.4 = bf16[4,2,1,1,16,2048]{5,4,3,2,1,0:T(8,128)(2,1)S(1)} collective-permute-done((bf16[4,2,1,1,16,2048]{5,4,3,2,1,0:T(8,128)(2,1)S(1)}, bf16[4,2,1,1,16,2048]{5,4,3,2,1,0:T(8,128)(2,1)S(1)}, u32[]{:S(2)}, u32[]{:S(2)}) %collective-permute-start.4) | collective-permute-done | bytes 524320 | tf_op jit(solution)/shard_map/ppermute | solution.py:38
  39.9 1.5 collective-permute-start.6
  42.4 1.5 collective-permute-start.8
  43.8 2.6 %maximum_select_fusion.1 = bf16[4,2,2,2,16,2048]{5,4,3,2,1,0:T(8,128)(2,1)S(1)} fusion(bf16[4,2,2,1,16,2048]{5,4,3,2,1,0:T(8,128)(2,1)} %collective-permute-done.27, bf16[4,2,2,1,16,2048]{5,4,3,2,1,0:T(8,128)(2,1)} %maximum_select_fusion.3, pred[]{:T(512)S(6)} %eq.64), kind=kLoop, calls=%fused_computation.9 | loop fusion | flops 3145728 | bytes 4194305 | tf_op jit(solution)/shard_map/jit(_where)/select_n | solution.py:49
  46.5 1.5 constant_dynamic-update-slice_fusion.11
  48.5 2.0 collective-permute-start.29
  50.5 2.4 %collective-permute-start.30 = (bf16[128,512]{1,0:T(8,128)(2,1)S(1)}, bf16[128,512]{1,0:T(8,128)(2,1)S(1)}, u32[]{:S(2)}, u32[]{:S(2)}) collective-permute-start(bf16[128,512]{1,0:T(8,128)(2,1)S(1)} %get-tuple-element.57), channel_id=1, source_target_pairs={{0,24},{1,25},{2,26},{3,27},{4,28},{5,29},{6,30},{7,31},{8,0},{9,1... | collective-permute-start | bytes 393224 | tf_op jit(solution)/shard_map/ppermute | solution.py:38
  55.1 1.5 collective-permute-start.10
  56.7 7.6 %collective-permute-done.29 = bf16[128,512]{1,0:T(8,128)(2,1)S(1)} collective-permute-done((bf16[128,512]{1,0:T(8,128)(2,1)S(1)}, bf16[128,512]{1,0:T(8,128)(2,1)S(1)}, u32[]{:S(2)}, u32[]{:S(2)}) %collective-permute-start.29) | collective-permute-done | bytes 131104 | tf_op jit(solution)/shard_map/ppermute | solution.py:38
  65.6 1.5 collective-permute-start.32
  71.1 9.4 %collective-permute-done.32 = bf16[512,512]{1,0:T(8,128)(2,1)S(1)} collective-permute-done((bf16[512,512]{1,0:T(8,128)(2,1)S(1)}, bf16[512,512]{1,0:T(8,128)(2,1)S(1)}, u32[]{:S(2)}, u32[]{:S(2)}) %collective-permute-start.32) | collective-permute-done | bytes 524320 | tf_op jit(solution)/shard_map/ppermute | solution.py:38
  86.2 3.8 %collective-permute-done.34 = bf16[512,256]{1,0:T(8,128)(2,1)S(1)} collective-permute-done((bf16[512,256]{1,0:T(8,128)(2,1)S(1)}, bf16[512,256]{1,0:T(8,128)(2,1)S(1)}, u32[]{:S(2)}, u32[]{:S(2)}) %collective-permute-start.34) | collective-permute-done | bytes 262176 | tf_op jit(solution)/shard_map/ppermute | solution.py:38
  94.4 10.0 %all-to-all-start = ((bf16[32,2,256]{2,1,0:T(2,128)(2,1)}), bf16[32,2,256]{2,1,0:T(2,128)(2,1)S(1)}, u32[]{:S(2)}, u32[]{:S(2)}) async-start(bf16[32,2,256]{2,1,0:T(2,128)(2,1)} %reshape.602), calls=%async_computation | async-start | bytes 65536 | tf_op jit(solution)/shard_map/all_to_all | solution.py:328
  104.9 6.7 %all-to-all-done = bf16[32,2,256]{2,1,0:T(2,128)(2,1)S(1)} async-done(((bf16[32,2,256]{2,1,0:T(2,128)(2,1)}), bf16[32,2,256]{2,1,0:T(2,128)(2,1)S(1)}, u32[]{:S(2)}, u32[]{:S(2)}) %all-to-all-start) | async-done | bytes 32800 | tf_op jit(solution)/shard_map/all_to_all | solution.py:328
  111.9 18.2 %shard_map.121 = (bf16[2048,512]{1,0:T(8,128)(2,1)S(1)}, bf16[2048,512]{1,0:T(8,128)(2,1)S(1)}) custom-call(s32[8,2,1,512]{3,2,1,0:T(1,128)S(1)} %add_convert_fusion.8.slot_ref, f32[8,2,1,512]{3,2,1,0:T(1,128)S(1)} %bitcast.163, bf16[2048,512]{1,0:T(8,128)(2,1)S(1)} %maximum_dynamic-update-slice_fusion.near_ref, ...), custom_call_target="tpu_custom_call" | custom-call | flops 8053063680 | bytes 18907136 | tf_op jit(solution)/shard_map/pallas_call | solution.py:285
  130.3 12.0 %shard_map.120 = (bf16[2048,512]{1,0:T(8,128)(2,1)S(1)}, bf16[2048,512]{1,0:T(8,128)(2,1)S(1)}) custom-call(s32[8,2,1,512]{3,2,1,0:T(1,128)S(1)} %add_convert_fusion.8.slot_ref, f32[8,2,1,512]{3,2,1,0:T(1,128)S(1)} %bitcast.164, bf16[2048,512]{1,0:T(8,128)(2,1)S(1)} %maximum_dynamic-update-slice_fusion.near_ref, ...), custom_call_target="tpu_custom_call" | custom-call | flops 4831838208 | bytes 14712832 | tf_op jit(solution)/shard_map/pallas_call | solution.py:285
  145.0 1.6 collective-permute-done.14
  146.5 2.8 %fusion.44 = (bf16[2048,512]{1,0:T(8,128)(2,1)S(1)}, f32[2048,512]{1,0:T(8,128)}) fusion(bf16[2048,512]{1,0:T(8,128)(2,1)S(1)} %collective-permute-done.14, bf16[2048,512]{1,0:T(8,128)(2,1)S(1)} %get-tuple-element.8), kind=kLoop, calls=%fused_computation.126 | loop fusion | flops 4194304 | bytes 10485760 | tf_op jit(solution)/shard_map/convert.19
  153.3 1.5 collective-permute-start.40
  156.2 3.3 %collective-permute-done.15 = bf16[512,256]{1,0:T(8,128)(2,1)S(1)} collective-permute-done((bf16[512,256]{1,0:T(8,128)(2,1)}, bf16[512,256]{1,0:T(8,128)(2,1)S(1)}, u32[]{:S(2)}, u32[]{:S(2)}) %collective-permute-start.15) | collective-permute-done | bytes 262176 | tf_op jit(solution)/shard_map/ppermute | solution.py:38
  159.9 1.4 fusion.11
  161.3 1.6 collective-permute-start.18
  163.6 7.1 %collective-permute-done.40 = bf16[512,512]{1,0:T(8,128)(2,1)S(1)} collective-permute-done((bf16[512,512]{1,0:T(8,128)(2,1)}, bf16[512,512]{1,0:T(8,128)(2,1)S(1)}, u32[]{:S(2)}, u32[]{:S(2)}) %collective-permute-start.40) | collective-permute-done | bytes 524320 | tf_op jit(solution)/shard_map/ppermute | solution.py:38
  171.1 1.6 fusion.46
  174.0 2.7 %collective-permute-start.41 = (bf16[128,512]{1,0:T(8,128)(2,1)S(1)}, bf16[128,512]{1,0:T(8,128)(2,1)S(1)}, u32[]{:S(2)}, u32[]{:S(2)}) collective-permute-start(bf16[128,512]{1,0:T(8,128)(2,1)S(1)} %get-tuple-element.46), channel_id=1, source_target_pairs={{0,24},{1,25},{2,26},{3,27},{4,28},{5,29},{6,30},{7,31},{8,0},{9,1... | collective-permute-start | bytes 393224 | tf_op jit(solution)/shard_map/ppermute | solution.py:38
  176.7 4.7 %collective-permute-done.18 = bf16[512,512]{1,0:T(8,128)(2,1)S(1)} collective-permute-done((bf16[512,512]{1,0:T(8,128)(2,1)S(1)}, bf16[512,512]{1,0:T(8,128)(2,1)S(1)}, u32[]{:S(2)}, u32[]{:S(2)}) %collective-permute-start.18) | collective-permute-done | bytes 524320 | tf_op jit(solution)/shard_map/ppermute | solution.py:38
  181.4 1.5 fusion.48
  184.2 2.7 %collective-permute-start.19 = (bf16[128,512]{1,0:T(8,128)(2,1)S(1)}, bf16[128,512]{1,0:T(8,128)(2,1)S(1)}, u32[]{:S(2)}, u32[]{:S(2)}) collective-permute-start(bf16[128,512]{1,0:T(8,128)(2,1)S(1)} %get-tuple-element.49), channel_id=1, source_target_pairs={{0,24},{1,25},{2,26},{3,27},{4,28},{5,29},{6,30},{7,31},{8,0},{9,1... | collective-permute-start | bytes 393224 | tf_op jit(solution)/shard_map/ppermute | solution.py:38
  187.0 1.4 fusion
  188.5 2.8 %collective-permute-done.21 = bf16[128,512]{1,0:T(8,128)(2,1)S(1)} collective-permute-done((bf16[128,512]{1,0:T(8,128)(2,1)S(1)}, bf16[128,512]{1,0:T(8,128)(2,1)S(1)}, u32[]{:S(2)}, u32[]{:S(2)}) %collective-permute-start.21) | collective-permute-done | bytes 131104 | tf_op jit(solution)/shard_map/ppermute | solution.py:38
  191.3 4.3 %collective-permute-done.20 = bf16[128,512]{1,0:T(8,128)(2,1)S(1)} collective-permute-done((bf16[128,512]{1,0:T(8,128)(2,1)S(1)}, bf16[128,512]{1,0:T(8,128)(2,1)S(1)}, u32[]{:S(2)}, u32[]{:S(2)}) %collective-permute-start.20) | collective-permute-done | bytes 131104 | tf_op jit(solution)/shard_map/ppermute | solution.py:38
  195.7 1.4 fusion.1
  198.0 1.5 fusion.7
  203.0 10.9 %collective-permute-done.45 = bf16[4,2,1,1,16,2048]{5,4,2,1,0,3:T(8,128)(2,1)S(1)} collective-permute-done((bf16[4,2,1,1,16,2048]{5,4,2,1,0,3:T(8,128)(2,1)S(1)}, bf16[4,2,1,1,16,2048]{5,4,2,1,0,3:T(8,128)(2,1)S(1)}, u32[]{:S(2)}, u32[]{:S(2)}) %collective-permute-start.45) | collective-permute-done | bytes 524320 | tf_op jit(solution)/shard_map/ppermute | solution.py:38
  217.5 4.5 %collective-permute-done.46 = bf16[4,1,1,1,16,2048]{5,4,2,1,0,3:T(8,128)(2,1)S(1)} collective-permute-done((bf16[4,1,1,1,16,2048]{5,4,2,1,0,3:T(8,128)(2,1)S(1)}, bf16[4,1,1,1,16,2048]{5,4,2,1,0,3:T(8,128)(2,1)S(1)}, u32[]{:S(2)}, u32[]{:S(2)}) %collective-permute-start.46) | collective-permute-done | bytes 262176 | tf_op jit(solution)/shard_map/ppermute | solution.py:38
  222.1 3.5 %collective-permute-start.49 = (bf16[1,1,1,1,16,2048]{5,4,2,1,0,3:T(8,128)(2,1)S(1)}, bf16[1,1,1,1,16,2048]{5,4,2,1,0,3:T(8,128)(2,1)S(1)}, u32[]{:S(2)}, u32[]{:S(2)}) collective-permute-start(bf16[1,1,1,1,16,2048]{5,4,2,1,0,3:T(8,128)(2,1)S(1)} %get-tuple-element.44), channel_id=1, source_target_pairs={{0,24},{1,25},{2,26},{3,27},{4,28},{5,29},{6,30},{7,31},{8,0},{9,1... | collective-permute-start | bytes 196616 | tf_op jit(solution)/shard_map/ppermute | solution.py:38
  226.6 3.9 %collective-permute-start.55 = (bf16[1,1,1,1,16,2048]{5,4,2,1,0,3:T(8,128)(2,1)S(1)}, bf16[1,1,1,1,16,2048]{5,4,2,1,0,3:T(8,128)(2,1)S(1)}, u32[]{:S(2)}, u32[]{:S(2)}) collective-permute-start(bf16[1,1,1,1,16,2048]{5,4,2,1,0,3:T(8,128)(2,1)S(1)} %get-tuple-element.41), channel_id=1, source_target_pairs={{0,24},{1,25},{2,26},{3,27},{4,28},{5,29},{6,30},{7,31},{8,0},{9,1... | collective-permute-start | bytes 196616 | tf_op jit(solution)/shard_map/ppermute | solution.py:38
  231.3 3.6 %collective-permute-done.48 = bf16[1,1,1,1,16,2048]{5,4,2,1,0,3:T(8,128)(2,1)S(1)} collective-permute-done((bf16[1,1,1,1,16,2048]{5,4,2,1,0,3:T(8,128)(2,1)S(1)}, bf16[1,1,1,1,16,2048]{5,4,2,1,0,3:T(8,128)(2,1)S(1)}, u32[]{:S(2)}, u32[]{:S(2)}) %collective-permute-start.48) | collective-permute-done | bytes 65568 | tf_op jit(solution)/shard_map/ppermute | solution.py:38
  235.7 2.0 collective-permute-done.54
  (184 shorter events, 53.5 us)
Async XLA Ops:
  0.6 9.8 %collective-permute-start = (bf16[1,1,1,1,16,2048]{5,4,3,2,1,0:T(8,128)(2,1)}, bf16[1,1,1,1,16,2048]{5,4,3,2,1,0:T(8,128)(2,1)S(1)}, u32[]{:S(2)}, u32[]{:S(2)}) collective-permute-start(bf16[1,1,1,1,16,2048]{5,4,3,2,1,0:T(8,128)(2,1)} %bitcast.181), channel_id=1, source_target_pairs={{0,8},{1,9},{2,10},{3,11},{4,12},{5,13},{6,14},{7,15},{8,16},{9,17... | collective-permute-start | bytes 196616 | tf_op jit(solution)/shard_map/ppermute | solution.py:38
  3.7 9.6 %collective-permute-start.1 = (bf16[1,1,1,1,16,2048]{5,4,3,2,1,0:T(8,128)(2,1)}, bf16[1,1,1,1,16,2048]{5,4,3,2,1,0:T(8,128)(2,1)S(1)}, u32[]{:S(2)}, u32[]{:S(2)}) collective-permute-start(bf16[1,1,1,1,16,2048]{5,4,3,2,1,0:T(8,128)(2,1)} %bitcast.182), channel_id=1, source_target_pairs={{0,16},{1,17},{2,18},{3,19},{4,20},{5,21},{6,22},{7,23},{8,24},{9,... | collective-permute-start | bytes 196616 | tf_op jit(solution)/shard_map/ppermute | solution.py:38
  7.7 7.3 %collective-permute-start.22 = (bf16[1,1,1,1,16,2048]{5,4,3,2,1,0:T(8,128)(2,1)}, bf16[1,1,1,1,16,2048]{5,4,3,2,1,0:T(8,128)(2,1)S(1)}, u32[]{:S(2)}, u32[]{:S(2)}) collective-permute-start(bf16[1,1,1,1,16,2048]{5,4,3,2,1,0:T(8,128)(2,1)} %bitcast.184), channel_id=1, source_target_pairs={{0,8},{1,9},{2,10},{3,11},{4,12},{5,13},{6,14},{7,15},{8,16},{9,17... | collective-permute-start | bytes 196616 | tf_op jit(solution)/shard_map/ppermute | solution.py:38
  8.3 8.3 %collective-permute-start.23 = (bf16[1,1,1,1,16,2048]{5,4,3,2,1,0:T(8,128)(2,1)}, bf16[1,1,1,1,16,2048]{5,4,3,2,1,0:T(8,128)(2,1)S(1)}, u32[]{:S(2)}, u32[]{:S(2)}) collective-permute-start(bf16[1,1,1,1,16,2048]{5,4,3,2,1,0:T(8,128)(2,1)} %bitcast.185), channel_id=1, source_target_pairs={{0,16},{1,17},{2,18},{3,19},{4,20},{5,21},{6,22},{7,23},{8,24},{9,... | collective-permute-start | bytes 196616 | tf_op jit(solution)/shard_map/ppermute | solution.py:38
  17.2 9.3 %collective-permute-start.25 = (bf16[4,1,1,1,16,2048]{5,4,0,3,2,1:T(8,128)(2,1)S(1)}, bf16[4,1,1,1,16,2048]{5,4,0,3,2,1:T(8,128)(2,1)S(1)}, u32[]{:S(2)}, u32[]{:S(2)}) collective-permute-start(bf16[4,1,1,1,16,2048]{5,4,0,3,2,1:T(8,128)(2,1)S(1)} %bitcast_dynamic-update-slice_fusion.1), channel_id=1, source_target_pairs={{0,2},{1,3},{2,0},{3,1},{4,6},{5,7},{6,4},{7,5},{8,10},{9,11},{10,... | collective-permute-start | bytes 786440 | tf_op jit(solution)/shard_map/ppermute | solution.py:38
  20.1 15.9 %collective-permute-start.4 = (bf16[4,2,1,1,16,2048]{5,4,3,2,1,0:T(8,128)(2,1)S(1)}, bf16[4,2,1,1,16,2048]{5,4,3,2,1,0:T(8,128)(2,1)S(1)}, u32[]{:S(2)}, u32[]{:S(2)}) collective-permute-start(bf16[4,2,1,1,16,2048]{5,4,3,2,1,0:T(8,128)(2,1)S(1)} %maximum_select_fusion.5), channel_id=1, source_target_pairs={{0,2},{1,3},{2,0},{3,1},{4,6},{5,7},{6,4},{7,5},{8,10},{9,11},{10,... | collective-permute-start | bytes 1572872 | tf_op jit(solution)/shard_map/ppermute | solution.py:38
  26.6 10.5 %collective-permute-start.26 = (bf16[4,1,2,1,16,2048]{5,4,3,2,1,0:T(8,128)(2,1)S(1)}, bf16[4,1,2,1,16,2048]{5,4,3,2,1,0:T(8,128)(2,1)S(1)}, u32[]{:S(2)}, u32[]{:S(2)}) collective-permute-start(bf16[4,1,2,1,16,2048]{5,4,3,2,1,0:T(8,128)(2,1)S(1)} %maximum_select_fusion.7), channel_id=1, source_target_pairs={{0,4},{1,5},{2,6},{3,7},{4,0},{5,1},{6,2},{7,3},{8,12},{9,13},{10,... | collective-permute-start | bytes 1572872 | tf_op jit(solution)/shard_map/ppermute | solution.py:38
  39.9 10.6 %collective-permute-start.6 = (bf16[128,512]{1,0:T(8,128)(2,1)S(1)}, bf16[128,512]{1,0:T(8,128)(2,1)S(1)}, u32[]{:S(2)}, u32[]{:S(2)}) collective-permute-start(bf16[128,512]{1,0:T(8,128)(2,1)S(1)} %get-tuple-element.55), channel_id=1, source_target_pairs={{0,8},{1,9},{2,10},{3,11},{4,12},{5,13},{6,14},{7,15},{8,16},{9,17... | collective-permute-start | bytes 393224 | tf_op jit(solution)/shard_map/ppermute | solution.py:38
  41.4 12.5 %collective-permute-start.7 = (bf16[128,512]{1,0:T(8,128)(2,1)S(1)}, bf16[128,512]{1,0:T(8,128)(2,1)S(1)}, u32[]{:S(2)}, u32[]{:S(2)}) collective-permute-start(bf16[128,512]{1,0:T(8,128)(2,1)S(1)} %get-tuple-element.55), channel_id=1, source_target_pairs={{0,16},{1,17},{2,18},{3,19},{4,20},{5,21},{6,22},{7,23},{8,24},{9,... | collective-permute-start | bytes 393224 | tf_op jit(solution)/shard_map/ppermute | solution.py:38
  42.4 11.5 %collective-permute-start.8 = (bf16[128,512]{1,0:T(8,128)(2,1)S(1)}, bf16[128,512]{1,0:T(8,128)(2,1)S(1)}, u32[]{:S(2)}, u32[]{:S(2)}) collective-permute-start(bf16[128,512]{1,0:T(8,128)(2,1)S(1)} %get-tuple-element.55), channel_id=1, source_target_pairs={{0,24},{1,25},{2,26},{3,27},{4,28},{5,29},{6,30},{7,31},{8,0},{9,1... | collective-permute-start | bytes 393224 | tf_op jit(solution)/shard_map/ppermute | solution.py:38
  48.0 8.7 %collective-permute-start.28 = (bf16[128,512]{1,0:T(8,128)(2,1)S(1)}, bf16[128,512]{1,0:T(8,128)(2,1)S(1)}, u32[]{:S(2)}, u32[]{:S(2)}) collective-permute-start(bf16[128,512]{1,0:T(8,128)(2,1)S(1)} %get-tuple-element.57), channel_id=1, source_target_pairs={{0,8},{1,9},{2,10},{3,11},{4,12},{5,13},{6,14},{7,15},{8,16},{9,17... | collective-permute-start | bytes 393224 | tf_op jit(solution)/shard_map/ppermute | solution.py:38
  48.5 15.8 %collective-permute-start.29 = (bf16[128,512]{1,0:T(8,128)(2,1)S(1)}, bf16[128,512]{1,0:T(8,128)(2,1)S(1)}, u32[]{:S(2)}, u32[]{:S(2)}) collective-permute-start(bf16[128,512]{1,0:T(8,128)(2,1)S(1)} %get-tuple-element.57), channel_id=1, source_target_pairs={{0,16},{1,17},{2,18},{3,19},{4,20},{5,21},{6,22},{7,23},{8,24},{9,... | collective-permute-start | bytes 393224 | tf_op jit(solution)/shard_map/ppermute | solution.py:38
  50.5 13.8 %collective-permute-start.30 = (bf16[128,512]{1,0:T(8,128)(2,1)S(1)}, bf16[128,512]{1,0:T(8,128)(2,1)S(1)}, u32[]{:S(2)}, u32[]{:S(2)}) collective-permute-start(bf16[128,512]{1,0:T(8,128)(2,1)S(1)} %get-tuple-element.57), channel_id=1, source_target_pairs={{0,24},{1,25},{2,26},{3,27},{4,28},{5,29},{6,30},{7,31},{8,0},{9,1... | collective-permute-start | bytes 393224 | tf_op jit(solution)/shard_map/ppermute | solution.py:38
  53.9 16.1 %collective-permute-start.9 = (bf16[512,512]{1,0:T(8,128)(2,1)S(1)}, bf16[512,512]{1,0:T(8,128)(2,1)S(1)}, u32[]{:S(2)}, u32[]{:S(2)}) collective-permute-start(bf16[512,512]{1,0:T(8,128)(2,1)S(1)} %pad_maximum_fusion), channel_id=1, source_target_pairs={{0,4},{1,5},{2,6},{3,7},{4,0},{5,1},{6,2},{7,3},{8,12},{9,13},{10,... | collective-permute-start | bytes 1572872 | tf_op jit(solution)/shard_map/ppermute | solution.py:38
  55.1 14.1 %collective-permute-start.10 = (bf16[512,512]{1,0:T(8,128)(2,1)S(1)}, bf16[512,512]{1,0:T(8,128)(2,1)S(1)}, u32[]{:S(2)}, u32[]{:S(2)}) collective-permute-start(bf16[512,512]{1,0:T(8,128)(2,1)S(1)} %pad_maximum_fusion), channel_id=1, source_target_pairs={{0,2},{1,3},{2,0},{3,1},{4,6},{5,7},{6,4},{7,5},{8,10},{9,11},{10,... | collective-permute-start | bytes 1572872 | tf_op jit(solution)/shard_map/ppermute | solution.py:38
  64.3 17.0 %collective-permute-start.31 = (bf16[512,512]{1,0:T(8,128)(2,1)S(1)}, bf16[512,512]{1,0:T(8,128)(2,1)S(1)}, u32[]{:S(2)}, u32[]{:S(2)}) collective-permute-start(bf16[512,512]{1,0:T(8,128)(2,1)S(1)} %pad_maximum_fusion.4), channel_id=1, source_target_pairs={{0,4},{1,5},{2,6},{3,7},{4,0},{5,1},{6,2},{7,3},{8,12},{9,13},{10,... | collective-permute-start | bytes 1572872 | tf_op jit(solution)/shard_map/ppermute | solution.py:38
  65.6 14.8 %collective-permute-start.32 = (bf16[512,512]{1,0:T(8,128)(2,1)S(1)}, bf16[512,512]{1,0:T(8,128)(2,1)S(1)}, u32[]{:S(2)}, u32[]{:S(2)}) collective-permute-start(bf16[512,512]{1,0:T(8,128)(2,1)S(1)} %pad_maximum_fusion.4), channel_id=1, source_target_pairs={{0,2},{1,3},{2,0},{3,1},{4,6},{5,7},{6,4},{7,5},{8,10},{9,11},{10,... | collective-permute-start | bytes 1572872 | tf_op jit(solution)/shard_map/ppermute | solution.py:38
  69.2 15.8 %collective-permute-start.12 = (bf16[512,256]{1,0:T(8,128)(2,1)S(1)}, bf16[512,256]{1,0:T(8,128)(2,1)S(1)}, u32[]{:S(2)}, u32[]{:S(2)}) collective-permute-start(bf16[512,256]{1,0:T(8,128)(2,1)S(1)} %slice.91), channel_id=1, source_target_pairs={{0,4},{1,5},{2,6},{3,7},{4,0},{5,1},{6,2},{7,3},{8,12},{9,13},{10,... | collective-permute-start | bytes 786440 | tf_op jit(solution)/shard_map/ppermute | solution.py:38
  70.0 16.1 %collective-permute-start.11 = (bf16[512,256]{1,0:T(8,128)(2,1)S(1)}, bf16[512,256]{1,0:T(8,128)(2,1)S(1)}, u32[]{:S(2)}, u32[]{:S(2)}) collective-permute-start(bf16[512,256]{1,0:T(8,128)(2,1)S(1)} %slice.90), channel_id=1, source_target_pairs={{0,2},{1,3},{2,0},{3,1},{4,6},{5,7},{6,4},{7,5},{8,10},{9,11},{10,... | collective-permute-start | bytes 786440 | tf_op jit(solution)/shard_map/ppermute | solution.py:38
  80.5 9.5 %collective-permute-start.34 = (bf16[512,256]{1,0:T(8,128)(2,1)S(1)}, bf16[512,256]{1,0:T(8,128)(2,1)S(1)}, u32[]{:S(2)}, u32[]{:S(2)}) collective-permute-start(bf16[512,256]{1,0:T(8,128)(2,1)S(1)} %slice.99), channel_id=1, source_target_pairs={{0,4},{1,5},{2,6},{3,7},{4,0},{5,1},{6,2},{7,3},{8,12},{9,13},{10,... | collective-permute-start | bytes 786440 | tf_op jit(solution)/shard_map/ppermute | solution.py:38
  81.4 9.5 %collective-permute-start.33 = (bf16[512,256]{1,0:T(8,128)(2,1)S(1)}, bf16[512,256]{1,0:T(8,128)(2,1)S(1)}, u32[]{:S(2)}, u32[]{:S(2)}) collective-permute-start(bf16[512,256]{1,0:T(8,128)(2,1)S(1)} %slice.98), channel_id=1, source_target_pairs={{0,2},{1,3},{2,0},{3,1},{4,6},{5,7},{6,4},{7,5},{8,10},{9,11},{10,... | collective-permute-start | bytes 786440 | tf_op jit(solution)/shard_map/ppermute | solution.py:38
  86.1 25.7 %collective-permute-start.13 = (bf16[2048,512]{1,0:T(8,128)(2,1)S(1)}, bf16[2048,512]{1,0:T(8,128)(2,1)}, u32[]{:S(2)}, u32[]{:S(2)}) collective-permute-start(bf16[2048,512]{1,0:T(8,128)(2,1)S(1)} %maximum_dynamic-update-slice_fusion.near_ref), channel_id=1, source_target_pairs={{0,1},{1,0},{2,3},{3,2},{4,5},{5,4},{6,7},{7,6},{8,9},{9,8},{10,11... | collective-permute-start | bytes 6291464 | tf_op jit(solution)/shard_map/ppermute | solution.py:38
  91.7 20.2 %collective-permute-start.35 = (bf16[2048,512]{1,0:T(8,128)(2,1)}, bf16[2048,512]{1,0:T(8,128)(2,1)}, u32[]{:S(2)}, u32[]{:S(2)}) collective-permute-start(bf16[2048,512]{1,0:T(8,128)(2,1)} %maximum_dynamic-update-slice_fusion.1.near_grad), channel_id=1, source_target_pairs={{0,1},{1,0},{2,3},{3,2},{4,5},{5,4},{6,7},{7,6},{8,9},{9,8},{10,11... | collective-permute-start | bytes 6291464 | tf_op jit(solution)/shard_map/ppermute | solution.py:38
  94.4 17.1 %all-to-all-start = ((bf16[32,2,256]{2,1,0:T(2,128)(2,1)}), bf16[32,2,256]{2,1,0:T(2,128)(2,1)S(1)}, u32[]{:S(2)}, u32[]{:S(2)}) async-start(bf16[32,2,256]{2,1,0:T(2,128)(2,1)} %reshape.602), calls=%async_computation | async-start | bytes 65536 | tf_op jit(solution)/shard_map/all_to_all | solution.py:328
  130.1 12.7 %collective-permute-start.36 = (bf16[2048,512]{1,0:T(8,128)(2,1)S(1)}, bf16[2048,512]{1,0:T(8,128)(2,1)S(1)}, u32[]{:S(2)}, u32[]{:S(2)}) collective-permute-start(bf16[2048,512]{1,0:T(8,128)(2,1)S(1)} %get-tuple-element.11), channel_id=1, source_target_pairs={{0,1},{1,0},{2,3},{3,2},{4,5},{5,4},{6,7},{7,6},{8,9},{9,8},{10,11... | collective-permute-start | bytes 6291464 | tf_op jit(solution)/shard_map/ppermute | solution.py:38
  143.7 8.4 %collective-permute-start.37 = (bf16[512,256]{1,0:T(8,128)(2,1)S(1)}, bf16[512,256]{1,0:T(8,128)(2,1)S(1)}, u32[]{:S(2)}, u32[]{:S(2)}) collective-permute-start(bf16[512,256]{1,0:T(8,128)(2,1)S(1)} %get-tuple-element.28), channel_id=1, source_target_pairs={{0,2},{1,3},{2,0},{3,1},{4,6},{5,7},{6,4},{7,5},{8,10},{9,11},{10,... | collective-permute-start | bytes 786440 | tf_op jit(solution)/shard_map/ppermute | solution.py:38
  144.2 8.1 %collective-permute-start.39 = (bf16[512,256]{1,0:T(8,128)(2,1)S(1)}, bf16[512,256]{1,0:T(8,128)(2,1)S(1)}, u32[]{:S(2)}, u32[]{:S(2)}) collective-permute-start(bf16[512,256]{1,0:T(8,128)(2,1)S(1)} %get-tuple-element.29), channel_id=1, source_target_pairs={{0,4},{1,5},{2,6},{3,7},{4,0},{5,1},{6,2},{7,3},{8,12},{9,13},{10,... | collective-permute-start | bytes 786440 | tf_op jit(solution)/shard_map/ppermute | solution.py:38
  150.1 9.3 %collective-permute-start.15 = (bf16[512,256]{1,0:T(8,128)(2,1)}, bf16[512,256]{1,0:T(8,128)(2,1)S(1)}, u32[]{:S(2)}, u32[]{:S(2)}) collective-permute-start(bf16[512,256]{1,0:T(8,128)(2,1)} %get-tuple-element.32), channel_id=1, source_target_pairs={{0,2},{1,3},{2,0},{3,1},{4,6},{5,7},{6,4},{7,5},{8,10},{9,11},{10,... | collective-permute-start | bytes 786440 | tf_op jit(solution)/shard_map/ppermute | solution.py:38
  150.6 9.3 %collective-permute-start.17 = (bf16[512,256]{1,0:T(8,128)(2,1)S(1)}, bf16[512,256]{1,0:T(8,128)(2,1)}, u32[]{:S(2)}, u32[]{:S(2)}) collective-permute-start(bf16[512,256]{1,0:T(8,128)(2,1)S(1)} %get-tuple-element.33), channel_id=1, source_target_pairs={{0,4},{1,5},{2,6},{3,7},{4,0},{5,1},{6,2},{7,3},{8,12},{9,13},{10,... | collective-permute-start | bytes 786440 | tf_op jit(solution)/shard_map/ppermute | solution.py:38
  153.3 17.4 %collective-permute-start.40 = (bf16[512,512]{1,0:T(8,128)(2,1)}, bf16[512,512]{1,0:T(8,128)(2,1)S(1)}, u32[]{:S(2)}, u32[]{:S(2)}) collective-permute-start(bf16[512,512]{1,0:T(8,128)(2,1)} %pad_maximum_fusion.6), channel_id=1, source_target_pairs={{0,2},{1,3},{2,0},{3,1},{4,6},{5,7},{6,4},{7,5},{8,10},{9,11},{10,... | collective-permute-start | bytes 1572872 | tf_op jit(solution)/shard_map/ppermute | solution.py:38
  155.7 15.5 %collective-permute-start.38 = (bf16[512,512]{1,0:T(8,128)(2,1)}, bf16[512,512]{1,0:T(8,128)(2,1)}, u32[]{:S(2)}, u32[]{:S(2)}) collective-permute-start(bf16[512,512]{1,0:T(8,128)(2,1)} %pad_maximum_fusion.5), channel_id=1, source_target_pairs={{0,4},{1,5},{2,6},{3,7},{4,0},{5,1},{6,2},{7,3},{8,12},{9,13},{10,... | collective-permute-start | bytes 1572872 | tf_op jit(solution)/shard_map/ppermute | solution.py:38
  161.3 20.1 %collective-permute-start.18 = (bf16[512,512]{1,0:T(8,128)(2,1)S(1)}, bf16[512,512]{1,0:T(8,128)(2,1)S(1)}, u32[]{:S(2)}, u32[]{:S(2)}) collective-permute-start(bf16[512,512]{1,0:T(8,128)(2,1)S(1)} %pad_maximum_fusion.2), channel_id=1, source_target_pairs={{0,2},{1,3},{2,0},{3,1},{4,6},{5,7},{6,4},{7,5},{8,10},{9,11},{10,... | collective-permute-start | bytes 1572872 | tf_op jit(solution)/shard_map/ppermute | solution.py:38
  163.0 18.4 %collective-permute-start.16 = (bf16[512,512]{1,0:T(8,128)(2,1)S(1)}, bf16[512,512]{1,0:T(8,128)(2,1)S(1)}, u32[]{:S(2)}, u32[]{:S(2)}) collective-permute-start(bf16[512,512]{1,0:T(8,128)(2,1)S(1)} %pad_maximum_fusion.1), channel_id=1, source_target_pairs={{0,4},{1,5},{2,6},{3,7},{4,0},{5,1},{6,2},{7,3},{8,12},{9,13},{10,... | collective-permute-start | bytes 1572872 | tf_op jit(solution)/shard_map/ppermute | solution.py:38
  172.8 11.4 %collective-permute-start.43 = (bf16[128,512]{1,0:T(8,128)(2,1)S(1)}, bf16[128,512]{1,0:T(8,128)(2,1)S(1)}, u32[]{:S(2)}, u32[]{:S(2)}) collective-permute-start(bf16[128,512]{1,0:T(8,128)(2,1)S(1)} %get-tuple-element.47), channel_id=1, source_target_pairs={{0,8},{1,9},{2,10},{3,11},{4,12},{5,13},{6,14},{7,15},{8,16},{9,17... | collective-permute-start | bytes 393224 | tf_op jit(solution)/shard_map/ppermute | solution.py:38
  173.5 13.4 %collective-permute-start.42 = (bf16[128,512]{1,0:T(8,128)(2,1)S(1)}, bf16[128,512]{1,0:T(8,128)(2,1)S(1)}, u32[]{:S(2)}, u32[]{:S(2)}) collective-permute-start(bf16[128,512]{1,0:T(8,128)(2,1)S(1)} %get-tuple-element.48), channel_id=1, source_target_pairs={{0,16},{1,17},{2,18},{3,19},{4,20},{5,21},{6,22},{7,23},{8,24},{9,... | collective-permute-start | bytes 393224 | tf_op jit(solution)/shard_map/ppermute | solution.py:38
  174.0 12.8 %collective-permute-start.41 = (bf16[128,512]{1,0:T(8,128)(2,1)S(1)}, bf16[128,512]{1,0:T(8,128)(2,1)S(1)}, u32[]{:S(2)}, u32[]{:S(2)}) collective-permute-start(bf16[128,512]{1,0:T(8,128)(2,1)S(1)} %get-tuple-element.46), channel_id=1, source_target_pairs={{0,24},{1,25},{2,26},{3,27},{4,28},{5,29},{6,30},{7,31},{8,0},{9,1... | collective-permute-start | bytes 393224 | tf_op jit(solution)/shard_map/ppermute | solution.py:38
  183.0 8.3 %collective-permute-start.21 = (bf16[128,512]{1,0:T(8,128)(2,1)S(1)}, bf16[128,512]{1,0:T(8,128)(2,1)S(1)}, u32[]{:S(2)}, u32[]{:S(2)}) collective-permute-start(bf16[128,512]{1,0:T(8,128)(2,1)S(1)} %get-tuple-element.50), channel_id=1, source_target_pairs={{0,8},{1,9},{2,10},{3,11},{4,12},{5,13},{6,14},{7,15},{8,16},{9,17... | collective-permute-start | bytes 393224 | tf_op jit(solution)/shard_map/ppermute | solution.py:38
  183.6 12.0 %collective-permute-start.20 = (bf16[128,512]{1,0:T(8,128)(2,1)S(1)}, bf16[128,512]{1,0:T(8,128)(2,1)S(1)}, u32[]{:S(2)}, u32[]{:S(2)}) collective-permute-start(bf16[128,512]{1,0:T(8,128)(2,1)S(1)} %get-tuple-element.51), channel_id=1, source_target_pairs={{0,16},{1,17},{2,18},{3,19},{4,20},{5,21},{6,22},{7,23},{8,24},{9,... | collective-permute-start | bytes 393224 | tf_op jit(solution)/shard_map/ppermute | solution.py:38
  184.2 11.4 %collective-permute-start.19 = (bf16[128,512]{1,0:T(8,128)(2,1)S(1)}, bf16[128,512]{1,0:T(8,128)(2,1)S(1)}, u32[]{:S(2)}, u32[]{:S(2)}) collective-permute-start(bf16[128,512]{1,0:T(8,128)(2,1)S(1)} %get-tuple-element.49), channel_id=1, source_target_pairs={{0,24},{1,25},{2,26},{3,27},{4,28},{5,29},{6,30},{7,31},{8,0},{9,1... | collective-permute-start | bytes 393224 | tf_op jit(solution)/shard_map/ppermute | solution.py:38
  188.5 9.6 %collective-permute-start.44 = (bf16[4,2,2,1,16,2048]{5,4,2,1,0,3:T(8,128)(2,1)}, bf16[4,2,2,1,16,2048]{5,4,2,1,0,3:T(8,128)(2,1)}, u32[]{:S(2)}, u32[]{:S(2)}) collective-permute-start(bf16[4,2,2,1,16,2048]{5,4,2,1,0,3:T(8,128)(2,1)} %fusion), channel_id=1, source_target_pairs={{0,1},{1,0},{2,3},{3,2},{4,5},{5,4},{6,7},{7,6},{8,9},{9,8},{10,11... | collective-permute-start | bytes 3145736 | tf_op jit(solution)/shard_map/ppermute | solution.py:38
  199.6 14.4 %collective-permute-start.45 = (bf16[4,2,1,1,16,2048]{5,4,2,1,0,3:T(8,128)(2,1)S(1)}, bf16[4,2,1,1,16,2048]{5,4,2,1,0,3:T(8,128)(2,1)S(1)}, u32[]{:S(2)}, u32[]{:S(2)}) collective-permute-start(bf16[4,2,1,1,16,2048]{5,4,2,1,0,3:T(8,128)(2,1)S(1)} %get-tuple-element.26), channel_id=1, source_target_pairs={{0,2},{1,3},{2,0},{3,1},{4,6},{5,7},{6,4},{7,5},{8,10},{9,11},{10,... | collective-permute-start | bytes 1572872 | tf_op jit(solution)/shard_map/ppermute | solution.py:38
  201.1 14.1 %collective-permute-start.51 = (bf16[4,1,2,1,16,2048]{5,4,2,1,0,3:T(8,128)(2,1)S(1)}, bf16[4,1,2,1,16,2048]{5,4,2,1,0,3:T(8,128)(2,1)S(1)}, u32[]{:S(2)}, u32[]{:S(2)}) collective-permute-start(bf16[4,1,2,1,16,2048]{5,4,2,1,0,3:T(8,128)(2,1)S(1)} %get-tuple-element.24), channel_id=1, source_target_pairs={{0,4},{1,5},{2,6},{3,7},{4,0},{5,1},{6,2},{7,3},{8,12},{9,13},{10,... | collective-permute-start | bytes 1572872 | tf_op jit(solution)/shard_map/ppermute | solution.py:38
  214.1 8.0 %collective-permute-start.46 = (bf16[4,1,1,1,16,2048]{5,4,2,1,0,3:T(8,128)(2,1)S(1)}, bf16[4,1,1,1,16,2048]{5,4,2,1,0,3:T(8,128)(2,1)S(1)}, u32[]{:S(2)}, u32[]{:S(2)}) collective-permute-start(bf16[4,1,1,1,16,2048]{5,4,2,1,0,3:T(8,128)(2,1)S(1)} %get-tuple-element.38), channel_id=1, source_target_pairs={{0,4},{1,5},{2,6},{3,7},{4,0},{5,1},{6,2},{7,3},{8,12},{9,13},{10,... | collective-permute-start | bytes 786440 | tf_op jit(solution)/shard_map/ppermute | solution.py:38
  215.4 11.1 %collective-permute-start.52 = (bf16[4,1,1,1,16,2048]{5,4,2,1,0,3:T(8,128)(2,1)S(1)}, bf16[4,1,1,1,16,2048]{5,4,2,1,0,3:T(8,128)(2,1)S(1)}, u32[]{:S(2)}, u32[]{:S(2)}) collective-permute-start(bf16[4,1,1,1,16,2048]{5,4,2,1,0,3:T(8,128)(2,1)S(1)} %get-tuple-element.36), channel_id=1, source_target_pairs={{0,2},{1,3},{2,0},{3,1},{4,6},{5,7},{6,4},{7,5},{8,10},{9,11},{10,... | collective-permute-start | bytes 786440 | tf_op jit(solution)/shard_map/ppermute | solution.py:38
  222.1 8.6 %collective-permute-start.49 = (bf16[1,1,1,1,16,2048]{5,4,2,1,0,3:T(8,128)(2,1)S(1)}, bf16[1,1,1,1,16,2048]{5,4,2,1,0,3:T(8,128)(2,1)S(1)}, u32[]{:S(2)}, u32[]{:S(2)}) collective-permute-start(bf16[1,1,1,1,16,2048]{5,4,2,1,0,3:T(8,128)(2,1)S(1)} %get-tuple-element.44), channel_id=1, source_target_pairs={{0,24},{1,25},{2,26},{3,27},{4,28},{5,29},{6,30},{7,31},{8,0},{9,1... | collective-permute-start | bytes 196616 | tf_op jit(solution)/shard_map/ppermute | solution.py:38
  225.6 9.4 %collective-permute-start.48 = (bf16[1,1,1,1,16,2048]{5,4,2,1,0,3:T(8,128)(2,1)S(1)}, bf16[1,1,1,1,16,2048]{5,4,2,1,0,3:T(8,128)(2,1)S(1)}, u32[]{:S(2)}, u32[]{:S(2)}) collective-permute-start(bf16[1,1,1,1,16,2048]{5,4,2,1,0,3:T(8,128)(2,1)S(1)} %get-tuple-element.45), channel_id=1, source_target_pairs={{0,16},{1,17},{2,18},{3,19},{4,20},{5,21},{6,22},{7,23},{8,24},{9,... | collective-permute-start | bytes 196616 | tf_op jit(solution)/shard_map/ppermute | solution.py:38
  226.5 8.5 %collective-permute-start.47 = (bf16[1,1,1,1,16,2048]{5,4,2,1,0,3:T(8,128)(2,1)S(1)}, bf16[1,1,1,1,16,2048]{5,4,2,1,0,3:T(8,128)(2,1)S(1)}, u32[]{:S(2)}, u32[]{:S(2)}) collective-permute-start(bf16[1,1,1,1,16,2048]{5,4,2,1,0,3:T(8,128)(2,1)S(1)} %get-tuple-element.43), channel_id=1, source_target_pairs={{0,8},{1,9},{2,10},{3,11},{4,12},{5,13},{6,14},{7,15},{8,16},{9,17... | collective-permute-start | bytes 196616 | tf_op jit(solution)/shard_map/ppermute | solution.py:38
  226.6 9.1 %collective-permute-start.55 = (bf16[1,1,1,1,16,2048]{5,4,2,1,0,3:T(8,128)(2,1)S(1)}, bf16[1,1,1,1,16,2048]{5,4,2,1,0,3:T(8,128)(2,1)S(1)}, u32[]{:S(2)}, u32[]{:S(2)}) collective-permute-start(bf16[1,1,1,1,16,2048]{5,4,2,1,0,3:T(8,128)(2,1)S(1)} %get-tuple-element.41), channel_id=1, source_target_pairs={{0,24},{1,25},{2,26},{3,27},{4,28},{5,29},{6,30},{7,31},{8,0},{9,1... | collective-permute-start | bytes 196616 | tf_op jit(solution)/shard_map/ppermute | solution.py:38
  (18 other events, 153.0 us)

commit v3 on v0

v3 whole, which is shorter than its diff:
```python
import math

import jax
import jax.numpy as jnp
from jax import lax
from jax.experimental import pallas as pl
from jax.experimental.pallas import tpu as pltpu
from jax.sharding import PartitionSpec as P

OWNERS = ("expert", "dp")
EXPERT = ("expert",)
Z, Y, X, CORE = 0, 1, 2, 3


def tensor_total(partial_sum):
    return lax.psum(partial_sum, "tensor")


def radices(count):
    return (count // 8, 2, 2, 2)


def digit_of(axes, place):
    sizes = radices(math.prod(lax.axis_size(axis) for axis in axes))
    stride = math.prod(sizes[place + 1 :])
    return lax.rem(lax.axis_index(axes) // stride, sizes[place])


def shifted(block, axes, place, step=1):
    count = math.prod(lax.axis_size(axis) for axis in axes)
    sizes = radices(count)
    stride = math.prod(sizes[place + 1 :])
    pairs = []
    for here in range(count):
        digit = here // stride % sizes[place]
        pairs.append((here, here + ((digit + step) % sizes[place] - digit) * stride))
    return lax.ppermute(block, axes, pairs)


SIDES = ((0, 0), (1, 0), (0, 1), (1, 1))


def device_count(axes):
    return math.prod(lax.axis_size(axis) for axis in axes)


def relative_owners(axes, first, second):
    depth = radices(device_count(axes))[Z]
    owners = []
    for core_step in (0, 1):
        for first_step, second_step in SIDES:
            for z_step in range(depth):
                steps = {Z: depth - z_step, first: first_step, second: second_step, CORE: core_step}
                owner = 0
                for place, size in enumerate(radices(device_count(axes))):
                    digit = lax.rem(digit_of(axes, place) + steps[place], size)
                    owner = owner * size + digit
                owners.append(owner)
    return jnp.stack(owners)


def gather_quarters(rows, axes, first, second):
    depth = radices(device_count(axes))[Z]
    half = rows.shape[1] // 2
    own = lax.concatenate([rows] + [shifted(rows, axes, Z, step) for step in range(1, depth)], 0)
    along_first = shifted(own, axes, first)
    along_second = shifted(own, axes, second)
    across = (
        shifted(along_first[:, :half], axes, second),
        shifted(along_second[:, half:], axes, first),
    )
    return (own, along_first, along_second) + across


def joined(quarters):
    return lax.concatenate(list(quarters[:3]) + [lax.concatenate(list(quarters[3:]), 1)], 0)


def total_tokens(near, far):
    depth = radices(device_count(EXPERT))[Z]

    def both_cores(index):
        other = shifted(far[index], EXPERT, CORE)
        return near[index].astype(jnp.float32) + other.astype(jnp.float32)

    across = both_cores(3).astype(jnp.bfloat16)
    half = across.shape[1] // 2
    left = shifted(across[:, :half], EXPERT, X).astype(jnp.float32)
    right = shifted(across[:, half:], EXPERT, Y).astype(jnp.float32)
    along_y, along_x = both_cores(1), both_cores(2)
    along_y = lax.concatenate([along_y[:, :half] + left, along_y[:, half:]], 1)
    along_x = lax.concatenate([along_x[:, :half], along_x[:, half:] + right], 1)
    own = both_cores(0)
    own = own + shifted(along_y.astype(jnp.bfloat16), EXPERT, Y).astype(jnp.float32)
    own = own + shifted(along_x.astype(jnp.bfloat16), EXPERT, X).astype(jnp.float32)
    pieces = jnp.split(own, depth, axis=0)
    total = pieces[0]
    for step in range(1, depth):
        piece = shifted(pieces[step].astype(jnp.bfloat16), EXPERT, Z, depth - step)
        total = total + piece.astype(jnp.float32)
    return total


def placement(rows, first, second):
    owners = relative_owners(OWNERS, first, second)
    targets = (owners[:, None] * rows + jnp.arange(rows, dtype=jnp.int32)[None, :]).reshape(-1)
    columns = jnp.arange(targets.shape[0], dtype=jnp.int32)
    return (targets[:, None] == columns[None, :]).astype(jnp.bfloat16)


def projected(pair_inputs, near_rows, place):
    part = tensor_total(matmul(pair_inputs, near_rows, ((1,), (1,)))).astype(jnp.bfloat16)
    count = part.shape[0] // 2
    other = shifted(part[count:], OWNERS, CORE)
    relative = lax.concatenate([part[:count], other], 1)
    return matmul(relative, place).astype(jnp.bfloat16)


def projection_grad(relative, quad_inputs, first, second):
    depth = radices(device_count(OWNERS))[Z]
    half = relative.shape[1] // 2
    pair = lax.concatenate([relative[:, :half], shifted(relative[:, half:], OWNERS, CORE)], 0)
    half = half // 2
    quad = lax.concatenate([pair[:, :half], shifted(pair[:, half:], OWNERS, second)], 0)
    half = half // 2
    sent = matmul(quad[:, half:], quad_inputs, ((0,), (0,))).astype(jnp.bfloat16)
    sent = shifted(sent, OWNERS, first)
    kept = matmul(quad[:, :half], quad_inputs, ((0,), (0,))) + sent.astype(jnp.float32)
    pieces = jnp.split(kept, depth, axis=0)
    total = pieces[0]
    for step in range(1, depth):
        piece = shifted(pieces[step].astype(jnp.bfloat16), OWNERS, Z, depth - step)
        total = total + piece.astype(jnp.float32)
    return total


def matmul(left, right, contract=((1,), (0,))):
    return lax.dot_general(left, right, (contract, ((), ())), preferred_element_type=jnp.float32)


def selected(slot_ref, group, expert, slots, values=None):
    slot = slot_ref[group, expert]
    here = lax.broadcasted_iota(jnp.int32, (slots, slot.shape[1]), 0) == slot
    return jnp.where(here, 1.0 if values is None else values, 0.0).astype(jnp.bfloat16)


def weight_copies(sources, targets, arrived, expert):
    return [
        pltpu.make_async_copy(source.at[expert], target.at[expert], arrived.at[place, expert])
        for place, (source, target) in enumerate(zip(sources, targets))
    ]


def pick_rows(pick, quarters, group, target, held):
    if group < 3:
        target[held, :] = matmul(pick, quarters[group][...]).astype(jnp.bfloat16)
        return
    half = target.shape[1] // 2
    for part in (0, 1):
        columns = slice(part * half, (part + 1) * half)
        target[held, columns] = matmul(pick, quarters[3 + part][...]).astype(jnp.bfloat16)


def spread_rows(slot_ref, scale_ref, results, targets):
    experts, groups, slots, _ = results.shape
    for group in range(groups):
        weights = jnp.concatenate(
            [
                selected(
                    slot_ref,
                    group,
                    expert,
                    slots,
                    None if scale_ref is None else scale_ref[group, expert],
                )
                for expert in range(experts)
            ],
            0,
        )
        values = jnp.concatenate([results[expert, group] for expert in range(experts)], 0)
        targets[group][...] = matmul(weights, values, ((0,), (0,))).astype(jnp.bfloat16)


def forward_kernel(*refs):
    slot_ref, scale_ref, *quarters = refs[:7]
    hbm_weights = refs[7:10]
    targets = refs[10:14]
    rows, hidden, results, gate_ref, up_ref, down_ref, arrived = refs[14:]
    experts, groups, slots, _ = results.shape
    width = hidden.shape[1]
    chunk = 256
    for expert in range(experts):
        for copy in weight_copies(hbm_weights, (gate_ref, up_ref, down_ref), arrived, expert):
            copy.start()

    @pl.loop(0, experts)
    def _(expert):
        copies = weight_copies(hbm_weights, (gate_ref, up_ref, down_ref), arrived, expert)
        for group in range(groups):
            held = slice(group * slots, (group + 1) * slots)
            pick_rows(selected(slot_ref, group, expert, slots), quarters, group, rows, held)
        copies[0].wait()
        copies[1].wait()
        for start in range(0, width, chunk):
            columns = slice(start, start + chunk)
            gate_act = matmul(rows[...], gate_ref[expert, :, columns])
            up_act = matmul(rows[...], up_ref[expert, :, columns])
            act = gate_act * jax.nn.sigmoid(gate_act) * up_act
            hidden[:, columns] = act.astype(jnp.bfloat16)
        copies[2].wait()
        result = matmul(hidden[...], down_ref[expert]).astype(jnp.bfloat16)
        for group in range(groups):
            results[expert, group] = result[group * slots : (group + 1) * slots, :]

    spread_rows(slot_ref, scale_ref, results, targets)


def backward_kernel(*refs):
    slot_ref, scale_ref, *quarters = refs[:7]
    quarter_grads = refs[7:12]
    hbm_weights = refs[12:15]
    targets = refs[15:19]
    rows, grads, gate_grads, value_grads, results, gate_ref, up_ref, down_ref, arrived = refs[19:]
    experts, groups, slots, _ = results.shape
    width = gate_grads.shape[1]
    chunk = 256
    for expert in range(experts):
        for copy in weight_copies(hbm_weights, (gate_ref, up_ref, down_ref), arrived, expert):
            copy.start()

    @pl.loop(0, experts)
    def _(expert):
        for group in range(groups):
            held = slice(group * slots, (group + 1) * slots)
            pick_rows(selected(slot_ref, group, expert, slots), quarters, group, rows, held)
            weighed = selected(slot_ref, group, expert, slots, scale_ref[group, expert])
            pick_rows(weighed, quarter_grads, group, grads, held)
        for copy in weight_copies(hbm_weights, (gate_ref, up_ref, down_ref), arrived, expert):
            copy.wait()
        for start in range(0, width, chunk):
            columns = slice(start, start + chunk)
            gate_act = matmul(rows[...], gate_ref[expert, :, columns])
            up_act = matmul(rows[...], up_ref[expert, :, columns])
            hidden_grad = matmul(grads[...], down_ref[expert, columns, :], ((1,), (1,)))
            sigmoid = jax.nn.sigmoid(gate_act)
            scaled = hidden_grad * sigmoid
            gate_grad = scaled * up_act * (1.0 + gate_act * (1.0 - sigmoid))
            gate_grads[:, columns] = gate_grad.astype(jnp.bfloat16)
            value_grads[:, columns] = (scaled * gate_act).astype(jnp.bfloat16)
        result = matmul(gate_grads[...], gate_ref[expert], ((1,), (1,)))
        result = result + matmul(value_grads[...], up_ref[expert], ((1,), (1,)))
        result = result.astype(jnp.bfloat16)
        for group in range(groups):
            results[expert, group] = result[group * slots : (group + 1) * slots, :]

    spread_rows(slot_ref, None, results, targets)


def expert_call(kernel, products, buffers, plan, quarters, weights):
    slots, scales = plan
    experts, latent_width, width = weights[0].shape
    groups, _, _, span = slots.shape
    operands = (slots, scales) + tuple(quarters) + tuple(weights)
    whole = pl.BlockSpec(memory_space=pltpu.VMEM)
    picked = buffers[0].shape[0]
    scratch = list(buffers) + [
        pltpu.VMEM((experts, groups, picked // groups, latent_width), jnp.bfloat16),
        *[pltpu.VMEM(weight.shape, jnp.bfloat16) for weight in weights],
        pltpu.SemaphoreType.DMA((3, experts)),
    ]
    return pl.pallas_call(
        kernel,
        out_shape=(jax.ShapeDtypeStruct((span, latent_width), jnp.bfloat16),) * groups,
        in_specs=[whole] * (len(operands) - 3) + [pl.BlockSpec(memory_space=pl.ANY)] * 3,
        out_specs=(whole,) * groups,
        scratch_shapes=scratch,
        compiler_params=pltpu.CompilerParams(vmem_limit_bytes=36 << 20),
        cost_estimate=pl.CostEstimate(
            flops=2 * products * experts * picked * latent_width * width,
            bytes_accessed=2 * sum(array.size for array in operands),
            transcendentals=experts * picked * width,
        ),
    )(*operands)


def expert_plans(routes, combine_fixed, local_experts):
    shards = lax.axis_size("expert")
    depth = radices(shards)[Z]
    row_count, top_count = routes.shape
    capacity = 3 * row_count * top_count // (2 * local_experts * shards)
    told = lax.concatenate([routes.T, combine_fixed.T], 0).astype(jnp.bfloat16)
    told = lax.all_gather(told.reshape(1, -1), "expert", axis=0, tiled=True)
    owners = relative_owners(EXPERT, Y, X)
    order = owners[:, None] == jnp.arange(shards, dtype=jnp.int32)[None, :]
    told = matmul(order.astype(jnp.bfloat16), told)
    told = told.astype(jnp.int32).reshape(shards, 2, top_count, row_count)
    mine = lax.axis_index("expert") * local_experts + jnp.arange(local_experts, dtype=jnp.int32)
    chosen = told[:, 0][:, None] == mine[None, :, None, None]
    fixed = jnp.sum(jnp.where(chosen, told[:, 1][:, None], 0), axis=2)
    member = jnp.any(chosen, axis=2)
    earlier = jnp.arange(row_count)[:, None] < jnp.arange(row_count)[None, :]
    ranking = jnp.einsum(
        "set,tu->seu",
        member.astype(jnp.bfloat16),
        earlier.astype(jnp.bfloat16),
        preferred_element_type=jnp.float32,
    ).astype(jnp.int32)
    offset = (jnp.arange(shards, dtype=jnp.int32) % depth * capacity)[:, None, None]
    slots = jnp.where(member, ranking + offset, -1)
    scales = fixed.astype(jnp.float32) / 256.0

    def by_quarter(values):
        values = values.reshape(2, 4, depth, local_experts, row_count).transpose(0, 1, 3, 2, 4)
        return values.reshape(2, 4, local_experts, 1, depth * row_count)

    slots, scales = by_quarter(slots), by_quarter(scales)
    return [(slots[core], scales[core]) for core in (0, 1)], depth * capacity


def local(
    tokens, out_grad, routes, combine_fixed, down_proj, up_proj, expert_gate, expert_up, expert_down
):
    local_experts, latent_width, width = expert_gate.shape
    rows = down_proj.shape[0]
    plans, slot_count = expert_plans(routes, combine_fixed, local_experts)

    pair_tokens = lax.concatenate([tokens, shifted(tokens, OWNERS, CORE)], 0)
    down_parts = gather_quarters(down_proj, OWNERS, Y, X)
    pair_grads = lax.concatenate([out_grad, shifted(out_grad, OWNERS, CORE)], 0)
    up_parts = gather_quarters(up_proj, OWNERS, X, Y)
    down_near, up_near = joined(down_parts), joined(up_parts)

    down_place = placement(rows, Y, X)
    up_place = placement(rows, X, Y)
    latent = projected(pair_tokens, down_near, down_place)
    near = gather_quarters(latent, EXPERT, Y, X)
    far = tuple(shifted(part, EXPERT, CORE) for part in near)
    mix_grad = projected(pair_grads, up_near, up_place)
    near_grad = gather_quarters(mix_grad, EXPERT, Y, X)
    far_grad = tuple(shifted(part, EXPERT, CORE) for part in near_grad)

    narrow = pltpu.VMEM((4 * slot_count, latent_width), jnp.bfloat16)
    wide = pltpu.VMEM((4 * slot_count, width), jnp.bfloat16)
    weights = (expert_gate, expert_up, expert_down)
    forward = [
        expert_call(forward_kernel, 3, (narrow, wide), plan, quarters, weights)
        for plan, quarters in zip(plans, (near, far))
    ]
    far_grad, forward = lax.optimization_barrier((far_grad, forward))
    backward = [
        expert_call(backward_kernel, 5, (narrow, narrow, wide, wide), plan, quarters, weights)
        for plan, quarters in zip(plans, (near + near_grad, far + far_grad))
    ]
    down_far = shifted(down_near, OWNERS, CORE)
    up_far = shifted(up_near, OWNERS, CORE)
    quad_tokens = lax.concatenate([pair_tokens, shifted(pair_tokens, OWNERS, X)], 0)
    quad_grads = lax.concatenate([pair_grads, shifted(pair_grads, OWNERS, Y)], 0)

    mixed_rows = tensor_total(total_tokens(*forward)).astype(jnp.bfloat16)
    mixed_relative = matmul(mixed_rows, up_place, ((1,), (1,))).astype(jnp.bfloat16)
    up_grad = projection_grad(mixed_relative, quad_grads, X, Y)
    layer_out = matmul(mixed_relative, lax.concatenate([up_near, up_far], 0)).astype(jnp.bfloat16)

    latent_grad = tensor_total(total_tokens(*backward)).astype(jnp.bfloat16)
    grad_relative = matmul(latent_grad, down_place, ((1,), (1,))).astype(jnp.bfloat16)
    down_grad = projection_grad(grad_relative, quad_tokens, Y, X)
    token_grad = matmul(grad_relative, lax.concatenate([down_near, down_far], 0)).astype(
        jnp.bfloat16
    )
    return (layer_out, token_grad, down_grad, up_grad)


def solution(mesh):
    in_specs = (
        P(("groups", "expert", "dp"), "tensor"),
        P(("groups", "expert", "dp"), "tensor"),
        P(("groups", "expert", "dp"), None),
        P(("groups", "expert", "dp"), None),
        P(("expert", "dp"), "tensor"),
        P(("expert", "dp"), "tensor"),
        P("expert", None, "tensor"),
        P("expert", None, "tensor"),
        P("expert", "tensor", None),
    )
    out_specs = (
        P(("groups", "expert", "dp"), "tensor"),
        P(("groups", "expert", "dp"), "tensor"),
        P(("groups", "expert", "dp"), "tensor"),
        P(("groups", "expert", "dp"), "tensor"),
    )
    return jax.shard_map(local, mesh=mesh, in_specs=in_specs, out_specs=out_specs, check_vma=False)
```

time: 538 us -> 298 us (0.55)
  waiting for transfers between devices: 363 us -> 107 us
  starting transfers between devices: 7.69 us -> 69 us
  matrix products: 59.3 us -> 13.3 us
  blocking collectives: 88 us -> 42.3 us
  Pallas kernels: 0 us -> 26.1 us
  local copies, waits for them, and re-layouts: 4.54 us -> 30.4 us
  between operations: 14 us -> 1.48 us
  other arithmetic: 1.27 us -> 7.3 us
    reduce_scatter x2 -> x0, waiting for transfers between devices: 221 us -> none  [the longest x1 140 us: local(): lax.psum_scatter(up_term, ('expert', 'dp'), scatter_dimension=0, tiled=True)]
    all_gather x2 -> x0, waiting for transfers between devices: 115 us -> none  [the longest x1 60.1 us: local(): lax.all_gather(down_proj, ('expert', 'dp'), axis=0, tiled=True)]
    ppermute x0 -> x80, waiting for transfers between devices: none -> 107 us  [shifted(): return lax.ppermute(block, axes, pairs)]
    all_to_all x2 -> x0, blocking collectives: 88 us -> none  [move_rows(): lax.all_to_all(blocks, 'expert', split_axis=0, concat_axis=0, tiled=True)]
    ppermute x0 -> x80, starting transfers between devices: none -> 69 us  [shifted(): return lax.ppermute(block, axes, pairs)]
    dot_general x14, matrix products: 59.3 us -> 13.3 us  [the longest x13 13.2 us: matmul(): lax.dot_general(left, right, (contract, ((), ())), preferred_element_type...]
    all_gather x0 -> x1, blocking collectives: none -> 42.3 us  [expert_plans(): told = lax.all_gather(told.reshape(1, -1), 'expert', axis=0, tiled=True)]
    pallas_call x0 -> x4, Pallas kernels: none -> 26.1 us  [expert_call(): pl.pallas_call(kernel, out_shape=(jax.ShapeDtypeStruct((span, latent_widt...]
  transfers between devices with their start and end apart: 6 -> 80, of which waited for: 5 -> 32; matrix products, arithmetic and copies ran while one was open for 7% -> 17% of each run, Pallas kernels for 0% -> 9%
where the time goes in v3:
time: 298 us; the launch traced here: 297 us
  waiting for transfers between devices  107 us (36%)
  starting transfers between devices  69 us (23%)
  blocking collectives  42.3 us (14%)
  local copies, waits for them, and re-layouts  30.4 us (10%)
  Pallas kernels  26.1 us (9%)
  matrix products  13.3 us (4%)
  other arithmetic  7.3 us (2%)
    ppermute x80, waiting for transfers between devices, shifted(): return lax.ppermute(block, axes, pairs)  107 us
    ppermute x80, starting transfers between devices, shifted(): return lax.ppermute(block, axes, pairs)  69 us
    all_gather x1, blocking collectives, expert_plans(): told = lax.all_gather(told.reshape(1, -1), 'expert', axis=0, tiled=True)  42.3 us
    pallas_call x4, Pallas kernels, expert_call(): pl.pallas_call(kernel, out_shape=(jax.ShapeDtypeStruct((span, latent_widt...  26.1 us
    unnamed x46, local copies, waits for them, and re-layouts  23.3 us
    dot_general x13, matrix products, matmul(): lax.dot_general(left, right, (contract, ((), ())), preferred_element_type...  13.2 us
  transfers between devices with their start and end apart: 80, of which 32 were waited for; matrix products, arithmetic and copies ran while one was open for 17% of the time, Pallas kernels for 9%

profile of v3, /device:TPU:0, one launch (start us, length us, event | category | flops | bytes accessed | tf_op | source)
XLA Modules:
  0.0 296.8 jit_solution(1929114718166065767)
XLA Ops:
  0.6 4.1 %collective-permute-start.23 = (bf16[16,2048]{1,0:T(8,128)(2,1)}, bf16[16,2048]{1,0:T(8,128)(2,1)S(1)}, u32[]{:S(2)}, u32[]{:S(2)}) collective-permute-start(bf16[16,2048]{1,0:T(8,128)(2,1)} %param.13), channel_id=1, source_target_pairs={{0,16},{1,17},{2,18},{3,19},{4,20},{5,21},{6,22},{7,23},{8,24},{9,... | collective-permute-start | bytes 196616 | tf_op jit(solution)/shard_map/ppermute | solution.py:37
  6.3 2.2 collective-permute-start.24
  13.8 42.3 %all-gather = bf16[32,1,2048]{2,1,0:T(2,128)(2,1)S(1)} all-gather(bf16[1,1,2048]{2,1,0:T(2,128)(2,1)S(1)} %reshape.602), channel_id=1, replica_groups=mesh['groups'=1,'expert'=32,'dp'=1,'tensor'=1] {'expert'}, dimensions={0}, use_global_device_ids=true | all-gather | bytes 135168 | tf_op jit(solution)/shard_map/all_gather | solution.py:292
  57.2 2.2 constant_dynamic-update-slice_fusion.42
  75.2 1.8 constant_dynamic-update-slice_fusion.35
  78.1 2.3 collective-permute-done.5
  80.5 2.1 collective-permute-start.27
  85.2 1.8 constant_dynamic-update-slice_fusion.26
  89.3 2.8 collective-permute-done.6
  97.0 1.7 convolution_convert_fusion.10
  99.7 3.5 %collective-permute-start.31 = (bf16[128,512]{1,0:T(8,128)(2,1)S(1)}, bf16[128,512]{1,0:T(8,128)(2,1)S(1)}, u32[]{:S(2)}, u32[]{:S(2)}) collective-permute-start(bf16[128,512]{1,0:T(8,128)(2,1)S(1)} %convolution_convert_fusion.7), channel_id=1, source_target_pairs={{0,16},{1,17},{2,18},{3,19},{4,20},{5,21},{6,22},{7,23},{8,24},{9,... | collective-permute-start | bytes 393224 | tf_op jit(solution)/shard_map/ppermute | solution.py:37
  103.7 3.9 %collective-permute-start.11 = (bf16[128,512]{1,0:T(8,128)(2,1)S(1)}, bf16[128,512]{1,0:T(8,128)(2,1)S(1)}, u32[]{:S(2)}, u32[]{:S(2)}) collective-permute-start(bf16[128,512]{1,0:T(8,128)(2,1)S(1)} %convolution_convert_fusion.8), channel_id=1, source_target_pairs={{0,24},{1,25},{2,26},{3,27},{4,28},{5,29},{6,30},{7,31},{8,0},{9,1... | collective-permute-start | bytes 393224 | tf_op jit(solution)/shard_map/ppermute | solution.py:37
  107.5 7.1 %collective-permute-start.9 = (bf16[128,512]{1,0:T(8,128)(2,1)S(1)}, bf16[128,512]{1,0:T(8,128)(2,1)S(1)}, u32[]{:S(2)}, u32[]{:S(2)}) collective-permute-start(bf16[128,512]{1,0:T(8,128)(2,1)S(1)} %convolution_convert_fusion.8), channel_id=1, source_target_pairs={{0,8},{1,9},{2,10},{3,11},{4,12},{5,13},{6,14},{7,15},{8,16},{9,17... | collective-permute-start | bytes 393224 | tf_op jit(solution)/shard_map/ppermute | solution.py:37
  114.8 6.8 %collective-permute-done.31 = bf16[128,512]{1,0:T(8,128)(2,1)S(1)} collective-permute-done((bf16[128,512]{1,0:T(8,128)(2,1)S(1)}, bf16[128,512]{1,0:T(8,128)(2,1)S(1)}, u32[]{:S(2)}, u32[]{:S(2)}) %collective-permute-start.31) | collective-permute-done | bytes 131104 | tf_op jit(solution)/shard_map/ppermute | solution.py:37
  121.8 2.1 collective-permute-start.34
  123.9 2.5 collective-permute-done.10
  126.3 2.1 collective-permute-start.15
  128.6 8.0 %collective-permute-done.34.refs_4_ = bf16[512,512]{1,0:T(8,128)(2,1)S(1)} collective-permute-done((bf16[512,512]{1,0:T(8,128)(2,1)S(1)}, bf16[512,512]{1,0:T(8,128)(2,1)S(1)}, u32[]{:S(2)}, u32[]{:S(2)}) %collective-permute-start.34) | collective-permute-done | bytes 524320 | tf_op jit(solution)/shard_map/ppermute | solution.py:37
  136.6 2.0 collective-permute-done.33.refs_3_
  138.6 9.0 %collective-permute-done.15.refs_9_ = bf16[512,512]{1,0:T(8,128)(2,1)S(1)} collective-permute-done((bf16[512,512]{1,0:T(8,128)(2,1)S(1)}, bf16[512,512]{1,0:T(8,128)(2,1)S(1)}, u32[]{:S(2)}, u32[]{:S(2)}) %collective-permute-start.15) | collective-permute-done | bytes 524320 | tf_op jit(solution)/shard_map/ppermute | solution.py:37
  147.6 1.8 collective-permute-start.35
  150.5 4.9 %collective-permute-done.36.refs_6_ = bf16[512,256]{1,0:T(8,128)(2,1)S(1)} collective-permute-done((bf16[512,256]{1,0:T(8,128)(2,1)S(1)}, bf16[512,256]{1,0:T(8,128)(2,1)S(1)}, u32[]{:S(2)}, u32[]{:S(2)}) %collective-permute-start.36) | collective-permute-done | bytes 262176 | tf_op jit(solution)/shard_map/ppermute | solution.py:37
  156.2 2.0 collective-permute-start.68
  158.2 2.1 collective-permute-done.19.refs_11_
  161.6 3.1 %collective-permute-done.17.refs_10_ = bf16[512,256]{1,0:T(8,128)(2,1)S(1)} collective-permute-done((bf16[512,256]{1,0:T(8,128)(2,1)S(1)}, bf16[512,256]{1,0:T(8,128)(2,1)S(1)}, u32[]{:S(2)}, u32[]{:S(2)}) %collective-permute-start.17) | collective-permute-done | bytes 262176 | tf_op jit(solution)/shard_map/ppermute | solution.py:37
  164.7 7.7 %shard_map.122 = (bf16[512,512]{1,0:T(8,128)(2,1)S(1)}, bf16[512,512]{1,0:T(8,128)(2,1)S(1)}, bf16[512,512]{1,0:T(8,128)(2,1)S(1)}, bf16[512,512]{1,0:T(8,128)(2,1)S(1)}) custom-call(s32[4,2,1,512]{3,2,1,0:T(1,128)S(1)} %bitcast.79, f32[4,2,1,512]{3,2,1,0:T(1,128)S(1)} %bitcast.75, bf16[512,512]{1,0:T(8,128)(2,1)S(1)} %pad_maximum_fusion.1.refs_2_, ...), custom_call_target="tpu_custom_call" | custom-call | flops 4026531840 | bytes 10502144 | tf_op jit(solution)/shard_map/pallas_call | solution.py:271
  175.7 9.0 %collective-permute-done.68 = bf16[256,2048]{1,0:T(8,128)(2,1)S(1)} collective-permute-done((bf16[256,2048]{1,0:T(8,128)(2,1)S(1)}, bf16[256,2048]{1,0:T(8,128)(2,1)S(1)}, u32[]{:S(2)}, u32[]{:S(2)}) %collective-permute-start.68) | collective-permute-done | bytes 1048608 | tf_op jit(solution)/shard_map/ppermute | solution.py:37
  185.8 5.3 %shard_map.120 = (bf16[512,512]{1,0:T(8,128)(2,1)S(1)}, bf16[512,512]{1,0:T(8,128)(2,1)S(1)}, bf16[512,512]{1,0:T(8,128)(2,1)S(1)}, bf16[512,512]{1,0:T(8,128)(2,1)S(1)}) custom-call(s32[4,2,1,512]{3,2,1,0:T(1,128)S(1)} %bitcast.80, f32[4,2,1,512]{3,2,1,0:T(1,128)S(1)} %bitcast.76, bf16[512,512]{1,0:T(8,128)(2,1)S(1)} %pad_maximum_fusion.1.refs_2_, ...), custom_call_target="tpu_custom_call" | custom-call | flops 2415919104 | bytes 8404992 | tf_op jit(solution)/shard_map/pallas_call | solution.py:271
  191.9 5.3 %shard_map.121 = (bf16[512,512]{1,0:T(8,128)(2,1)S(1)}, bf16[512,512]{1,0:T(8,128)(2,1)S(1)}, bf16[512,512]{1,0:T(8,128)(2,1)S(1)}, bf16[512,512]{1,0:T(8,128)(2,1)S(1)}) custom-call(s32[4,2,1,512]{3,2,1,0:T(1,128)S(1)} %bitcast.77, f32[4,2,1,512]{3,2,1,0:T(1,128)S(1)} %bitcast.73, bf16[512,512]{1,0:T(8,128)(2,1)S(1)} %collective-permute-done.37.refs_2_, ...), custom_call_target="tpu_custom_call" | custom-call | flops 2415919104 | bytes 8404992 | tf_op jit(solution)/shard_map/pallas_call | solution.py:271
  197.4 7.8 %shard_map.123 = (bf16[512,512]{1,0:T(8,128)(2,1)S(1)}, bf16[512,512]{1,0:T(8,128)(2,1)S(1)}, bf16[512,512]{1,0:T(8,128)(2,1)S(1)}, bf16[512,512]{1,0:T(8,128)(2,1)S(1)}) custom-call(s32[4,2,1,512]{3,2,1,0:T(1,128)S(1)} %bitcast.78, f32[4,2,1,512]{3,2,1,0:T(1,128)S(1)} %bitcast.74, bf16[512,512]{1,0:T(8,128)(2,1)S(1)} %collective-permute-done.37.refs_2_, ...), custom_call_target="tpu_custom_call" | custom-call | flops 4026531840 | bytes 10502144 | tf_op jit(solution)/shard_map/pallas_call | solution.py:271
  205.6 1.8 collective-permute-done.75
  215.0 5.1 %collective-permute-done.45 = bf16[512,256]{1,0:T(8,128)(2,1)S(1)} collective-permute-done((bf16[512,256]{1,0:T(8,128)(2,1)S(1)}, bf16[512,256]{1,0:T(8,128)(2,1)S(1)}, u32[]{:S(2)}, u32[]{:S(2)}) %collective-permute-start.45) | collective-permute-done | bytes 262176 | tf_op jit(solution)/shard_map/ppermute | solution.py:37
  222.5 2.4 collective-permute-done.57
  226.2 3.2 %collective-permute-done.60 = bf16[512,256]{1,0:T(8,128)(2,1)S(1)} collective-permute-done((bf16[512,256]{1,0:T(8,128)(2,1)S(1)}, bf16[512,256]{1,0:T(8,128)(2,1)S(1)}, u32[]{:S(2)}, u32[]{:S(2)}) %collective-permute-start.60) | collective-permute-done | bytes 262176 | tf_op jit(solution)/shard_map/ppermute | solution.py:37
  231.4 9.2 %collective-permute-done.46 = bf16[512,512]{1,0:T(8,128)(2,1)S(1)} collective-permute-done((bf16[512,512]{1,0:T(8,128)(2,1)S(1)}, bf16[512,512]{1,0:T(8,128)(2,1)S(1)}, u32[]{:S(2)}, u32[]{:S(2)}) %collective-permute-start.46) | collective-permute-done | bytes 524320 | tf_op jit(solution)/shard_map/ppermute | solution.py:37
  241.0 2.0 collective-permute-start.52
  243.0 6.3 %collective-permute-done.58 = bf16[512,512]{1,0:T(8,128)(2,1)S(1)} collective-permute-done((bf16[512,512]{1,0:T(8,128)(2,1)S(1)}, bf16[512,512]{1,0:T(8,128)(2,1)S(1)}, u32[]{:S(2)}, u32[]{:S(2)}) %collective-permute-start.58) | collective-permute-done | bytes 524320 | tf_op jit(solution)/shard_map/ppermute | solution.py:37
  249.7 2.0 collective-permute-start.64
  252.6 4.4 %collective-permute-done.62 = bf16[128,512]{1,0:T(8,128)(2,1)S(1)} collective-permute-done((bf16[128,512]{1,0:T(8,128)(2,1)S(1)}, bf16[128,512]{1,0:T(8,128)(2,1)S(1)}, u32[]{:S(2)}, u32[]{:S(2)}) %collective-permute-start.62) | collective-permute-done | bytes 131104 | tf_op jit(solution)/shard_map/ppermute | solution.py:37
  257.0 4.9 %collective-permute-done.63 = bf16[128,512]{1,0:T(8,128)(2,1)S(1)} collective-permute-done((bf16[128,512]{1,0:T(8,128)(2,1)S(1)}, bf16[128,512]{1,0:T(8,128)(2,1)S(1)}, u32[]{:S(2)}, u32[]{:S(2)}) %collective-permute-start.63) | collective-permute-done | bytes 131104 | tf_op jit(solution)/shard_map/ppermute | solution.py:37
  262.3 2.8 convolution_convert_fusion
  265.2 2.8 convolution_convert_fusion.1
  268.0 1.7 collective-permute-start.74
  270.5 2.1 collective-permute-done.74
  276.3 4.9 %collective-permute-done.76 = bf16[64,2048]{1,0:T(8,128)(2,1)S(1)} collective-permute-done((bf16[64,2048]{1,0:T(8,128)(2,1)S(1)}, bf16[64,2048]{1,0:T(8,128)(2,1)S(1)}, u32[]{:S(2)}, u32[]{:S(2)}) %collective-permute-start.76) | collective-permute-done | bytes 262176 | tf_op jit(solution)/shard_map/ppermute | solution.py:37
  281.7 2.2 collective-permute-start.77
  285.1 3.3 %collective-permute-start.70 = (bf16[16,2048]{1,0:T(8,128)(2,1)S(1)}, bf16[16,2048]{1,0:T(8,128)(2,1)S(1)}, u32[]{:S(2)}, u32[]{:S(2)}) collective-permute-start(bf16[16,2048]{1,0:T(8,128)(2,1)S(1)} %get-tuple-element.87), channel_id=1, source_target_pairs={{0,24},{1,25},{2,26},{3,27},{4,28},{5,29},{6,30},{7,31},{8,0},{9,1... | collective-permute-start | bytes 196616 | tf_op jit(solution)/shard_map/ppermute | solution.py:37
  291.5 3.0 %collective-permute-done.72 = bf16[16,2048]{1,0:T(8,128)(2,1)S(1)} collective-permute-done((bf16[16,2048]{1,0:T(8,128)(2,1)S(1)}, bf16[16,2048]{1,0:T(8,128)(2,1)S(1)}, u32[]{:S(2)}, u32[]{:S(2)}) %collective-permute-start.72) | collective-permute-done | bytes 65568 | tf_op jit(solution)/shard_map/ppermute | solution.py:37
  (248 shorter events, 72.2 us)
Async XLA Ops:
  0.6 60.7 %collective-permute-start.23 = (bf16[16,2048]{1,0:T(8,128)(2,1)}, bf16[16,2048]{1,0:T(8,128)(2,1)S(1)}, u32[]{:S(2)}, u32[]{:S(2)}) collective-permute-start(bf16[16,2048]{1,0:T(8,128)(2,1)} %param.13), channel_id=1, source_target_pairs={{0,16},{1,17},{2,18},{3,19},{4,20},{5,21},{6,22},{7,23},{8,24},{9,... | collective-permute-start | bytes 196616 | tf_op jit(solution)/shard_map/ppermute | solution.py:37
  4.7 55.8 %collective-permute-start.22 = (bf16[16,2048]{1,0:T(8,128)(2,1)}, bf16[16,2048]{1,0:T(8,128)(2,1)S(1)}, u32[]{:S(2)}, u32[]{:S(2)}) collective-permute-start(bf16[16,2048]{1,0:T(8,128)(2,1)} %param.13), channel_id=1, source_target_pairs={{0,8},{1,9},{2,10},{3,11},{4,12},{5,13},{6,14},{7,15},{8,16},{9,17... | collective-permute-start | bytes 196616 | tf_op jit(solution)/shard_map/ppermute | solution.py:37
  6.3 56.1 %collective-permute-start.24 = (bf16[16,2048]{1,0:T(8,128)(2,1)}, bf16[16,2048]{1,0:T(8,128)(2,1)S(1)}, u32[]{:S(2)}, u32[]{:S(2)}) collective-permute-start(bf16[16,2048]{1,0:T(8,128)(2,1)} %param.13), channel_id=1, source_target_pairs={{0,24},{1,25},{2,26},{3,27},{4,28},{5,29},{6,30},{7,31},{8,0},{9,1... | collective-permute-start | bytes 196616 | tf_op jit(solution)/shard_map/ppermute | solution.py:37
  8.6 56.8 %collective-permute-start.2 = (bf16[16,2048]{1,0:T(8,128)(2,1)}, bf16[16,2048]{1,0:T(8,128)(2,1)}, u32[]{:S(2)}, u32[]{:S(2)}) collective-permute-start(bf16[16,2048]{1,0:T(8,128)(2,1)} %param.14), channel_id=1, source_target_pairs={{0,16},{1,17},{2,18},{3,19},{4,20},{5,21},{6,22},{7,23},{8,24},{9,... | collective-permute-start | bytes 196616 | tf_op jit(solution)/shard_map/ppermute | solution.py:37
  8.6 54.7 %collective-permute-start.1 = (bf16[16,2048]{1,0:T(8,128)(2,1)}, bf16[16,2048]{1,0:T(8,128)(2,1)S(1)}, u32[]{:S(2)}, u32[]{:S(2)}) collective-permute-start(bf16[16,2048]{1,0:T(8,128)(2,1)} %param.14), channel_id=1, source_target_pairs={{0,8},{1,9},{2,10},{3,11},{4,12},{5,13},{6,14},{7,15},{8,16},{9,17... | collective-permute-start | bytes 196616 | tf_op jit(solution)/shard_map/ppermute | solution.py:37
  61.3 31.4 %collective-permute-start.21 = (bf16[128,2048]{1,0:T(8,128)(2,1)}, bf16[128,2048]{1,0:T(8,128)(2,1)}, u32[]{:S(2)}, u32[]{:S(2)}) collective-permute-start(bf16[128,2048]{1,0:T(8,128)(2,1)} %param.9), channel_id=1, source_target_pairs={{0,1},{1,0},{2,3},{3,2},{4,5},{5,4},{6,7},{7,6},{8,9},{9,8},{10,11... | collective-permute-start | bytes 1572872 | tf_op jit(solution)/shard_map/ppermute | solution.py:37
  62.4 33.4 %collective-permute-start = (bf16[128,2048]{1,0:T(8,128)(2,1)}, bf16[128,2048]{1,0:T(8,128)(2,1)}, u32[]{:S(2)}, u32[]{:S(2)}) collective-permute-start(bf16[128,2048]{1,0:T(8,128)(2,1)} %param.10), channel_id=1, source_target_pairs={{0,1},{1,0},{2,3},{3,2},{4,5},{5,4},{6,7},{7,6},{8,9},{9,8},{10,11... | collective-permute-start | bytes 1572872 | tf_op jit(solution)/shard_map/ppermute | solution.py:37
  65.4 9.4 %collective-permute-start.25 = (bf16[64,2048]{1,0:T(8,128)(2,1)}, bf16[64,2048]{1,0:T(8,128)(2,1)}, u32[]{:S(2)}, u32[]{:S(2)}) collective-permute-start(bf16[64,2048]{1,0:T(8,128)(2,1)} %get-tuple-element.114), channel_id=1, source_target_pairs={{0,4},{1,5},{2,6},{3,7},{4,0},{5,1},{6,2},{7,3},{8,12},{9,13},{10,... | collective-permute-start | bytes 786440 | tf_op jit(solution)/shard_map/ppermute | solution.py:37
  68.0 12.5 %collective-permute-start.5 = (bf16[64,2048]{1,0:T(8,128)(2,1)}, bf16[64,2048]{1,0:T(8,128)(2,1)}, u32[]{:S(2)}, u32[]{:S(2)}) collective-permute-start(bf16[64,2048]{1,0:T(8,128)(2,1)} %get-tuple-element.126), channel_id=1, source_target_pairs={{0,4},{1,5},{2,6},{3,7},{4,0},{5,1},{6,2},{7,3},{8,12},{9,13},{10,... | collective-permute-start | bytes 786440 | tf_op jit(solution)/shard_map/ppermute | solution.py:37
  72.6 11.7 %collective-permute-start.4 = (bf16[64,2048]{1,0:T(8,128)(2,1)}, bf16[64,2048]{1,0:T(8,128)(2,1)S(1)}, u32[]{:S(2)}, u32[]{:S(2)}) collective-permute-start(bf16[64,2048]{1,0:T(8,128)(2,1)} %get-tuple-element.126), channel_id=1, source_target_pairs={{0,2},{1,3},{2,0},{3,1},{4,6},{5,7},{6,4},{7,5},{8,10},{9,11},{10,... | collective-permute-start | bytes 786440 | tf_op jit(solution)/shard_map/ppermute | solution.py:37
  74.8 12.2 %collective-permute-start.28 = (bf16[64,1024]{1,0:T(8,128)(2,1)S(1)}, bf16[64,1024]{1,0:T(8,128)(2,1)S(1)}, u32[]{:S(2)}, u32[]{:S(2)}) collective-permute-start(bf16[64,1024]{1,0:T(8,128)(2,1)S(1)} %slice.187), channel_id=1, source_target_pairs={{0,4},{1,5},{2,6},{3,7},{4,0},{5,1},{6,2},{7,3},{8,12},{9,13},{10,... | collective-permute-start | bytes 393224 | tf_op jit(solution)/shard_map/ppermute | solution.py:37
  99.7 21.9 %collective-permute-start.31 = (bf16[128,512]{1,0:T(8,128)(2,1)S(1)}, bf16[128,512]{1,0:T(8,128)(2,1)S(1)}, u32[]{:S(2)}, u32[]{:S(2)}) collective-permute-start(bf16[128,512]{1,0:T(8,128)(2,1)S(1)} %convolution_convert_fusion.7), channel_id=1, source_target_pairs={{0,16},{1,17},{2,18},{3,19},{4,20},{5,21},{6,22},{7,23},{8,24},{9,... | collective-permute-start | bytes 393224 | tf_op jit(solution)/shard_map/ppermute | solution.py:37
  103.2 18.4 %collective-permute-start.30 = (bf16[128,512]{1,0:T(8,128)(2,1)S(1)}, bf16[128,512]{1,0:T(8,128)(2,1)S(1)}, u32[]{:S(2)}, u32[]{:S(2)}) collective-permute-start(bf16[128,512]{1,0:T(8,128)(2,1)S(1)} %convolution_convert_fusion.7), channel_id=1, source_target_pairs={{0,8},{1,9},{2,10},{3,11},{4,12},{5,13},{6,14},{7,15},{8,16},{9,17... | collective-permute-start | bytes 393224 | tf_op jit(solution)/shard_map/ppermute | solution.py:37
  103.7 20.2 %collective-permute-start.11 = (bf16[128,512]{1,0:T(8,128)(2,1)S(1)}, bf16[128,512]{1,0:T(8,128)(2,1)S(1)}, u32[]{:S(2)}, u32[]{:S(2)}) collective-permute-start(bf16[128,512]{1,0:T(8,128)(2,1)S(1)} %convolution_convert_fusion.8), channel_id=1, source_target_pairs={{0,24},{1,25},{2,26},{3,27},{4,28},{5,29},{6,30},{7,31},{8,0},{9,1... | collective-permute-start | bytes 393224 | tf_op jit(solution)/shard_map/ppermute | solution.py:37
  107.5 18.8 %collective-permute-start.10 = (bf16[128,512]{1,0:T(8,128)(2,1)S(1)}, bf16[128,512]{1,0:T(8,128)(2,1)S(1)}, u32[]{:S(2)}, u32[]{:S(2)}) collective-permute-start(bf16[128,512]{1,0:T(8,128)(2,1)S(1)} %convolution_convert_fusion.8), channel_id=1, source_target_pairs={{0,16},{1,17},{2,18},{3,19},{4,20},{5,21},{6,22},{7,23},{8,24},{9,... | collective-permute-start | bytes 393224 | tf_op jit(solution)/shard_map/ppermute | solution.py:37
  107.5 18.8 %collective-permute-start.9 = (bf16[128,512]{1,0:T(8,128)(2,1)S(1)}, bf16[128,512]{1,0:T(8,128)(2,1)S(1)}, u32[]{:S(2)}, u32[]{:S(2)}) collective-permute-start(bf16[128,512]{1,0:T(8,128)(2,1)S(1)} %convolution_convert_fusion.8), channel_id=1, source_target_pairs={{0,8},{1,9},{2,10},{3,11},{4,12},{5,13},{6,14},{7,15},{8,16},{9,17... | collective-permute-start | bytes 393224 | tf_op jit(solution)/shard_map/ppermute | solution.py:37
  121.7 27.7 %collective-permute-start.37 = (bf16[512,512]{1,0:T(8,128)(2,1)S(1)}, bf16[512,512]{1,0:T(8,128)(2,1)S(1)}, u32[]{:S(2)}, u32[]{:S(2)}) collective-permute-start(bf16[512,512]{1,0:T(8,128)(2,1)S(1)} %pad_maximum_fusion.1.refs_2_), channel_id=1, source_target_pairs={{0,1},{1,0},{2,3},{3,2},{4,5},{5,4},{6,7},{7,6},{8,9},{9,8},{10,11... | collective-permute-start | bytes 1572872 | tf_op jit(solution)/shard_map/ppermute | solution.py:37
  121.8 14.9 %collective-permute-start.34 = (bf16[512,512]{1,0:T(8,128)(2,1)S(1)}, bf16[512,512]{1,0:T(8,128)(2,1)S(1)}, u32[]{:S(2)}, u32[]{:S(2)}) collective-permute-start(bf16[512,512]{1,0:T(8,128)(2,1)S(1)} %pad_maximum_fusion.1.refs_2_), channel_id=1, source_target_pairs={{0,2},{1,3},{2,0},{3,1},{4,6},{5,7},{6,4},{7,5},{8,10},{9,11},{10,... | collective-permute-start | bytes 1572872 | tf_op jit(solution)/shard_map/ppermute | solution.py:37
  123.8 14.8 %collective-permute-start.33 = (bf16[512,512]{1,0:T(8,128)(2,1)S(1)}, bf16[512,512]{1,0:T(8,128)(2,1)S(1)}, u32[]{:S(2)}, u32[]{:S(2)}) collective-permute-start(bf16[512,512]{1,0:T(8,128)(2,1)S(1)} %pad_maximum_fusion.1.refs_2_), channel_id=1, source_target_pairs={{0,4},{1,5},{2,6},{3,7},{4,0},{5,1},{6,2},{7,3},{8,12},{9,13},{10,... | collective-permute-start | bytes 1572872 | tf_op jit(solution)/shard_map/ppermute | solution.py:37
  126.3 21.2 %collective-permute-start.15 = (bf16[512,512]{1,0:T(8,128)(2,1)S(1)}, bf16[512,512]{1,0:T(8,128)(2,1)S(1)}, u32[]{:S(2)}, u32[]{:S(2)}) collective-permute-start(bf16[512,512]{1,0:T(8,128)(2,1)S(1)} %pad_maximum_fusion.refs_7_), channel_id=1, source_target_pairs={{0,2},{1,3},{2,0},{3,1},{4,6},{5,7},{6,4},{7,5},{8,10},{9,11},{10,... | collective-permute-start | bytes 1572872 | tf_op jit(solution)/shard_map/ppermute | solution.py:37
  128.4 21.4 %collective-permute-start.13 = (bf16[512,512]{1,0:T(8,128)(2,1)S(1)}, bf16[512,512]{1,0:T(8,128)(2,1)S(1)}, u32[]{:S(2)}, u32[]{:S(2)}) collective-permute-start(bf16[512,512]{1,0:T(8,128)(2,1)S(1)} %pad_maximum_fusion.refs_7_), channel_id=1, source_target_pairs={{0,4},{1,5},{2,6},{3,7},{4,0},{5,1},{6,2},{7,3},{8,12},{9,13},{10,... | collective-permute-start | bytes 1572872 | tf_op jit(solution)/shard_map/ppermute | solution.py:37
  136.6 36.4 %collective-permute-start.65 = (bf16[256,2048]{1,0:T(8,128)(2,1)}, bf16[256,2048]{1,0:T(8,128)(2,1)S(1)}, u32[]{:S(2)}, u32[]{:S(2)}) collective-permute-start(bf16[256,2048]{1,0:T(8,128)(2,1)} %maximum_dynamic-update-slice_fusion.1), channel_id=1, source_target_pairs={{0,1},{1,0},{2,3},{3,2},{4,5},{5,4},{6,7},{7,6},{8,9},{9,8},{10,11... | collective-permute-start | bytes 3145736 | tf_op jit(solution)/shard_map/ppermute | solution.py:37
  138.6 16.9 %collective-permute-start.36 = (bf16[512,256]{1,0:T(8,128)(2,1)S(1)}, bf16[512,256]{1,0:T(8,128)(2,1)S(1)}, u32[]{:S(2)}, u32[]{:S(2)}) collective-permute-start(bf16[512,256]{1,0:T(8,128)(2,1)S(1)} %slice.191), channel_id=1, source_target_pairs={{0,4},{1,5},{2,6},{3,7},{4,0},{5,1},{6,2},{7,3},{8,12},{9,13},{10,... | collective-permute-start | bytes 786440 | tf_op jit(solution)/shard_map/ppermute | solution.py:37
  149.4 10.9 %collective-permute-start.19 = (bf16[512,256]{1,0:T(8,128)(2,1)S(1)}, bf16[512,256]{1,0:T(8,128)(2,1)S(1)}, u32[]{:S(2)}, u32[]{:S(2)}) collective-permute-start(bf16[512,256]{1,0:T(8,128)(2,1)S(1)} %slice.181), channel_id=1, source_target_pairs={{0,4},{1,5},{2,6},{3,7},{4,0},{5,1},{6,2},{7,3},{8,12},{9,13},{10,... | collective-permute-start | bytes 786440 | tf_op jit(solution)/shard_map/ppermute | solution.py:37
  149.9 24.3 %collective-permute-start.53 = (bf16[256,2048]{1,0:T(8,128)(2,1)}, bf16[256,2048]{1,0:T(8,128)(2,1)S(1)}, u32[]{:S(2)}, u32[]{:S(2)}) collective-permute-start(bf16[256,2048]{1,0:T(8,128)(2,1)} %maximum_dynamic-update-slice_fusion), channel_id=1, source_target_pairs={{0,1},{1,0},{2,3},{3,2},{4,5},{5,4},{6,7},{7,6},{8,9},{9,8},{10,11... | collective-permute-start | bytes 3145736 | tf_op jit(solution)/shard_map/ppermute | solution.py:37
  155.5 9.2 %collective-permute-start.17 = (bf16[512,256]{1,0:T(8,128)(2,1)S(1)}, bf16[512,256]{1,0:T(8,128)(2,1)S(1)}, u32[]{:S(2)}, u32[]{:S(2)}) collective-permute-start(bf16[512,256]{1,0:T(8,128)(2,1)S(1)} %slice.180), channel_id=1, source_target_pairs={{0,2},{1,3},{2,0},{3,1},{4,6},{5,7},{6,4},{7,5},{8,10},{9,11},{10,... | collective-permute-start | bytes 786440 | tf_op jit(solution)/shard_map/ppermute | solution.py:37
  156.2 28.5 %collective-permute-start.68 = (bf16[256,2048]{1,0:T(8,128)(2,1)S(1)}, bf16[256,2048]{1,0:T(8,128)(2,1)S(1)}, u32[]{:S(2)}, u32[]{:S(2)}) collective-permute-start(bf16[256,2048]{1,0:T(8,128)(2,1)S(1)} %get-tuple-element.71), channel_id=1, source_target_pairs={{0,2},{1,3},{2,0},{3,1},{4,6},{5,7},{6,4},{7,5},{8,10},{9,11},{10,... | collective-permute-start | bytes 3145736 | tf_op jit(solution)/shard_map/ppermute | solution.py:37
  160.3 12.1 %collective-permute-start.12 = (bf16[512,512]{1,0:T(8,128)(2,1)S(1)}, bf16[512,512]{1,0:T(8,128)(2,1)S(1)}, u32[]{:S(2)}, u32[]{:S(2)}) collective-permute-start(bf16[512,512]{1,0:T(8,128)(2,1)S(1)} %pad_maximum_fusion.refs_7_), channel_id=1, source_target_pairs={{0,1},{1,0},{2,3},{3,2},{4,5},{5,4},{6,7},{7,6},{8,9},{9,8},{10,11... | collective-permute-start | bytes 1572872 | tf_op jit(solution)/shard_map/ppermute | solution.py:37
  164.7 20.6 %collective-permute-start.39 = (bf16[512,512]{1,0:T(8,128)(2,1)S(1)}, bf16[512,512]{1,0:T(8,128)(2,1)S(1)}, u32[]{:S(2)}, u32[]{:S(2)}) collective-permute-start(bf16[512,512]{1,0:T(8,128)(2,1)S(1)} %collective-permute-done.34.refs_4_), channel_id=1, source_target_pairs={{0,1},{1,0},{2,3},{3,2},{4,5},{5,4},{6,7},{7,6},{8,9},{9,8},{10,11... | collective-permute-start | bytes 1572872 | tf_op jit(solution)/shard_map/ppermute | solution.py:37
  172.5 18.9 %collective-permute-start.38 = (bf16[512,512]{1,0:T(8,128)(2,1)S(1)}, bf16[512,512]{1,0:T(8,128)(2,1)S(1)}, u32[]{:S(2)}, u32[]{:S(2)}) collective-permute-start(bf16[512,512]{1,0:T(8,128)(2,1)S(1)} %collective-permute-done.33.refs_3_), channel_id=1, source_target_pairs={{0,1},{1,0},{2,3},{3,2},{4,5},{5,4},{6,7},{7,6},{8,9},{9,8},{10,11... | collective-permute-start | bytes 1572872 | tf_op jit(solution)/shard_map/ppermute | solution.py:37
  173.0 12.3 %collective-permute-start.41 = (bf16[512,256]{1,0:T(8,128)(2,1)S(1)}, bf16[512,256]{1,0:T(8,128)(2,1)S(1)}, u32[]{:S(2)}, u32[]{:S(2)}) collective-permute-start(bf16[512,256]{1,0:T(8,128)(2,1)S(1)} %collective-permute-done.36.refs_6_), channel_id=1, source_target_pairs={{0,1},{1,0},{2,3},{3,2},{4,5},{5,4},{6,7},{7,6},{8,9},{9,8},{10,11... | collective-permute-start | bytes 786440 | tf_op jit(solution)/shard_map/ppermute | solution.py:37
  174.2 17.0 %collective-permute-start.40 = (bf16[512,256]{1,0:T(8,128)(2,1)S(1)}, bf16[512,256]{1,0:T(8,128)(2,1)S(1)}, u32[]{:S(2)}, u32[]{:S(2)}) collective-permute-start(bf16[512,256]{1,0:T(8,128)(2,1)S(1)} %collective-permute-done.35.refs_5_), channel_id=1, source_target_pairs={{0,1},{1,0},{2,3},{3,2},{4,5},{5,4},{6,7},{7,6},{8,9},{9,8},{10,11... | collective-permute-start | bytes 786440 | tf_op jit(solution)/shard_map/ppermute | solution.py:37
  184.7 22.7 %collective-permute-start.75 = (bf16[256,2048]{1,0:T(8,128)(2,1)S(1)}, bf16[256,2048]{1,0:T(8,128)(2,1)S(1)}, u32[]{:S(2)}, u32[]{:S(2)}) collective-permute-start(bf16[256,2048]{1,0:T(8,128)(2,1)S(1)} %get-tuple-element.67), channel_id=1, source_target_pairs={{0,4},{1,5},{2,6},{3,7},{4,0},{5,1},{6,2},{7,3},{8,12},{9,13},{10,... | collective-permute-start | bytes 3145736 | tf_op jit(solution)/shard_map/ppermute | solution.py:37
  185.3 11.9 %collective-permute-start.16 = (bf16[512,512]{1,0:T(8,128)(2,1)S(1)}, bf16[512,512]{1,0:T(8,128)(2,1)S(1)}, u32[]{:S(2)}, u32[]{:S(2)}) collective-permute-start(bf16[512,512]{1,0:T(8,128)(2,1)S(1)} %collective-permute-done.15.refs_9_), channel_id=1, source_target_pairs={{0,1},{1,0},{2,3},{3,2},{4,5},{5,4},{6,7},{7,6},{8,9},{9,8},{10,11... | collective-permute-start | bytes 1572872 | tf_op jit(solution)/shard_map/ppermute | solution.py:37
  185.3 11.9 %collective-permute-start.14 = (bf16[512,512]{1,0:T(8,128)(2,1)S(1)}, bf16[512,512]{1,0:T(8,128)(2,1)S(1)}, u32[]{:S(2)}, u32[]{:S(2)}) collective-permute-start(bf16[512,512]{1,0:T(8,128)(2,1)S(1)} %collective-permute-done.13.refs_8_), channel_id=1, source_target_pairs={{0,1},{1,0},{2,3},{3,2},{4,5},{5,4},{6,7},{7,6},{8,9},{9,8},{10,11... | collective-permute-start | bytes 1572872 | tf_op jit(solution)/shard_map/ppermute | solution.py:37
  197.2 10.9 %collective-permute-start.43 = (bf16[512,512]{1,0:T(8,128)(2,1)S(1)}, bf16[512,512]{1,0:T(8,128)(2,1)S(1)}, u32[]{:S(2)}, u32[]{:S(2)}) collective-permute-start(bf16[512,512]{1,0:T(8,128)(2,1)S(1)} %get-tuple-element.44), channel_id=1, source_target_pairs={{0,1},{1,0},{2,3},{3,2},{4,5},{5,4},{6,7},{7,6},{8,9},{9,8},{10,11... | collective-permute-start | bytes 1572872 | tf_op jit(solution)/shard_map/ppermute | solution.py:37
  207.5 23.3 %collective-permute-start.42 = (bf16[512,512]{1,0:T(8,128)(2,1)S(1)}, bf16[512,512]{1,0:T(8,128)(2,1)S(1)}, u32[]{:S(2)}, u32[]{:S(2)}) collective-permute-start(bf16[512,512]{1,0:T(8,128)(2,1)S(1)} %get-tuple-element.42), channel_id=1, source_target_pairs={{0,1},{1,0},{2,3},{3,2},{4,5},{5,4},{6,7},{7,6},{8,9},{9,8},{10,11... | collective-permute-start | bytes 1572872 | tf_op jit(solution)/shard_map/ppermute | solution.py:37
  208.1 34.9 %collective-permute-start.54 = (bf16[512,512]{1,0:T(8,128)(2,1)S(1)}, bf16[512,512]{1,0:T(8,128)(2,1)S(1)}, u32[]{:S(2)}, u32[]{:S(2)}) collective-permute-start(bf16[512,512]{1,0:T(8,128)(2,1)S(1)} %get-tuple-element.55), channel_id=1, source_target_pairs={{0,1},{1,0},{2,3},{3,2},{4,5},{5,4},{6,7},{7,6},{8,9},{9,8},{10,11... | collective-permute-start | bytes 1572872 | tf_op jit(solution)/shard_map/ppermute | solution.py:37
  213.9 11.0 %collective-permute-start.57 = (bf16[512,256]{1,0:T(8,128)(2,1)S(1)}, bf16[512,256]{1,0:T(8,128)(2,1)S(1)}, u32[]{:S(2)}, u32[]{:S(2)}) collective-permute-start(bf16[512,256]{1,0:T(8,128)(2,1)S(1)} %get-tuple-element.77), channel_id=1, source_target_pairs={{0,2},{1,3},{2,0},{3,1},{4,6},{5,7},{6,4},{7,5},{8,10},{9,11},{10,... | collective-permute-start | bytes 786440 | tf_op jit(solution)/shard_map/ppermute | solution.py:37
  221.5 19.1 %collective-permute-start.46 = (bf16[512,512]{1,0:T(8,128)(2,1)S(1)}, bf16[512,512]{1,0:T(8,128)(2,1)S(1)}, u32[]{:S(2)}, u32[]{:S(2)}) collective-permute-start(bf16[512,512]{1,0:T(8,128)(2,1)S(1)} %pad_maximum_fusion.2), channel_id=1, source_target_pairs={{0,4},{1,5},{2,6},{3,7},{4,0},{5,1},{6,2},{7,3},{8,12},{9,13},{10,... | collective-permute-start | bytes 1572872 | tf_op jit(solution)/shard_map/ppermute | solution.py:37
  224.9 15.7 %collective-permute-start.49 = (bf16[512,512]{1,0:T(8,128)(2,1)S(1)}, bf16[512,512]{1,0:T(8,128)(2,1)S(1)}, u32[]{:S(2)}, u32[]{:S(2)}) collective-permute-start(bf16[512,512]{1,0:T(8,128)(2,1)S(1)} %pad_maximum_fusion.3), channel_id=1, source_target_pairs={{0,2},{1,3},{2,0},{3,1},{4,6},{5,7},{6,4},{7,5},{8,10},{9,11},{10,... | collective-permute-start | bytes 1572872 | tf_op jit(solution)/shard_map/ppermute | solution.py:37
  229.4 19.9 %collective-permute-start.58 = (bf16[512,512]{1,0:T(8,128)(2,1)S(1)}, bf16[512,512]{1,0:T(8,128)(2,1)S(1)}, u32[]{:S(2)}, u32[]{:S(2)}) collective-permute-start(bf16[512,512]{1,0:T(8,128)(2,1)S(1)} %pad_maximum_fusion.4), channel_id=1, source_target_pairs={{0,4},{1,5},{2,6},{3,7},{4,0},{5,1},{6,2},{7,3},{8,12},{9,13},{10,... | collective-permute-start | bytes 1572872 | tf_op jit(solution)/shard_map/ppermute | solution.py:37
  230.8 18.6 %collective-permute-start.61 = (bf16[512,512]{1,0:T(8,128)(2,1)S(1)}, bf16[512,512]{1,0:T(8,128)(2,1)S(1)}, u32[]{:S(2)}, u32[]{:S(2)}) collective-permute-start(bf16[512,512]{1,0:T(8,128)(2,1)S(1)} %pad_maximum_fusion.5), channel_id=1, source_target_pairs={{0,2},{1,3},{2,0},{3,1},{4,6},{5,7},{6,4},{7,5},{8,10},{9,11},{10,... | collective-permute-start | bytes 1572872 | tf_op jit(solution)/shard_map/ppermute | solution.py:37
  240.9 10.8 %collective-permute-start.50 = (bf16[128,512]{1,0:T(8,128)(2,1)S(1)}, bf16[128,512]{1,0:T(8,128)(2,1)S(1)}, u32[]{:S(2)}, u32[]{:S(2)}) collective-permute-start(bf16[128,512]{1,0:T(8,128)(2,1)S(1)} %get-tuple-element.79), channel_id=1, source_target_pairs={{0,24},{1,25},{2,26},{3,27},{4,28},{5,29},{6,30},{7,31},{8,0},{9,1... | collective-permute-start | bytes 393224 | tf_op jit(solution)/shard_map/ppermute | solution.py:37
  241.0 10.7 %collective-permute-start.52 = (bf16[128,512]{1,0:T(8,128)(2,1)S(1)}, bf16[128,512]{1,0:T(8,128)(2,1)S(1)}, u32[]{:S(2)}, u32[]{:S(2)}) collective-permute-start(bf16[128,512]{1,0:T(8,128)(2,1)S(1)} %get-tuple-element.80), channel_id=1, source_target_pairs={{0,8},{1,9},{2,10},{3,11},{4,12},{5,13},{6,14},{7,15},{8,16},{9,17... | collective-permute-start | bytes 393224 | tf_op jit(solution)/shard_map/ppermute | solution.py:37
  251.7 10.1 %collective-permute-start.63 = (bf16[128,512]{1,0:T(8,128)(2,1)S(1)}, bf16[128,512]{1,0:T(8,128)(2,1)S(1)}, u32[]{:S(2)}, u32[]{:S(2)}) collective-permute-start(bf16[128,512]{1,0:T(8,128)(2,1)S(1)} %get-tuple-element.76), channel_id=1, source_target_pairs={{0,16},{1,17},{2,18},{3,19},{4,20},{5,21},{6,22},{7,23},{8,24},{9,... | collective-permute-start | bytes 393224 | tf_op jit(solution)/shard_map/ppermute | solution.py:37
  252.5 15.5 %collective-permute-start.73 = (bf16[128,256]{1,0:T(8,128)(2,1)S(1)}, bf16[128,256]{1,0:T(8,128)(2,1)S(1)}, u32[]{:S(2)}, u32[]{:S(2)}) collective-permute-start(bf16[128,256]{1,0:T(8,128)(2,1)S(1)} %get-tuple-element.103), channel_id=1, source_target_pairs={{0,1},{1,0},{2,3},{3,2},{4,5},{5,4},{6,7},{7,6},{8,9},{9,8},{10,11... | collective-permute-start | bytes 196616 | tf_op jit(solution)/shard_map/ppermute | solution.py:37
  275.3 9.3 %collective-permute-start.69 = (bf16[64,2048]{1,0:T(8,128)(2,1)S(1)}, bf16[64,2048]{1,0:T(8,128)(2,1)S(1)}, u32[]{:S(2)}, u32[]{:S(2)}) collective-permute-start(bf16[64,2048]{1,0:T(8,128)(2,1)S(1)} %convolution_convert_fusion.3), channel_id=1, source_target_pairs={{0,4},{1,5},{2,6},{3,7},{4,0},{5,1},{6,2},{7,3},{8,12},{9,13},{10,... | collective-permute-start | bytes 786440 | tf_op jit(solution)/shard_map/ppermute | solution.py:37
  (44 other events, 482.0 us)

commit v4 on v3

--- a/solution.py
+++ b/solution.py
@@ -60,9 +60,16 @@
 
 
 def gather_quarters(rows, axes, first, second):
+    return gather_chips(gather_depth(rows, axes), axes, first, second)
+
+
+def gather_depth(rows, axes):
     depth = radices(device_count(axes))[Z]
-    half = rows.shape[1] // 2
-    own = lax.concatenate([rows] + [shifted(rows, axes, Z, step) for step in range(1, depth)], 0)
+    return lax.concatenate([rows] + [shifted(rows, axes, Z, step) for step in range(1, depth)], 0)
+
+
+def gather_chips(own, axes, first, second):
+    half = own.shape[1] // 256 * 128 or own.shape[1] // 2
     along_first = shifted(own, axes, first)
     along_second = shifted(own, axes, second)
     across = (
@@ -76,21 +83,21 @@
     return lax.concatenate(list(quarters[:3]) + [lax.concatenate(list(quarters[3:]), 1)], 0)
 
 
-def total_tokens(near, far):
+def core_totals(near, far):
+    return [
+        near[index].astype(jnp.float32) + shifted(far[index], EXPERT, CORE).astype(jnp.float32)
+        for index in (3, 1, 2, 0)
+    ]
+
+
+def total_tokens(across, along_y, along_x, own):
     depth = radices(device_count(EXPERT))[Z]
-
-    def both_cores(index):
-        other = shifted(far[index], EXPERT, CORE)
-        return near[index].astype(jnp.float32) + other.astype(jnp.float32)
-
-    across = both_cores(3).astype(jnp.bfloat16)
+    across = across.astype(jnp.bfloat16)
     half = across.shape[1] // 2
     left = shifted(across[:, :half], EXPERT, X).astype(jnp.float32)
     right = shifted(across[:, half:], EXPERT, Y).astype(jnp.float32)
-    along_y, along_x = both_cores(1), both_cores(2)
     along_y = lax.concatenate([along_y[:, :half] + left, along_y[:, half:]], 1)
     along_x = lax.concatenate([along_x[:, :half], along_x[:, half:] + right], 1)
-    own = both_cores(0)
     own = own + shifted(along_y.astype(jnp.bfloat16), EXPERT, Y).astype(jnp.float32)
     own = own + shifted(along_x.astype(jnp.bfloat16), EXPERT, X).astype(jnp.float32)
     pieces = jnp.split(own, depth, axis=0)
@@ -108,12 +115,74 @@
     return (targets[:, None] == columns[None, :]).astype(jnp.bfloat16)
 
 
-def projected(pair_inputs, near_rows, place):
-    part = tensor_total(matmul(pair_inputs, near_rows, ((1,), (1,)))).astype(jnp.bfloat16)
-    count = part.shape[0] // 2
-    other = shifted(part[count:], OWNERS, CORE)
-    relative = lax.concatenate([part[:count], other], 1)
-    return matmul(relative, place).astype(jnp.bfloat16)
+def vmem_call(kernel, out_shape, operands, products):
+    whole = pl.BlockSpec(memory_space=pltpu.VMEM)
+    return pl.pallas_call(
+        kernel,
+        out_shape=out_shape,
+        in_specs=[whole] * len(operands),
+        out_specs=(whole,) * len(out_shape),
+        compiler_params=pltpu.CompilerParams(vmem_limit_bytes=20 << 20),
+        cost_estimate=pl.CostEstimate(
+            flops=2 * products,
+            bytes_accessed=2 * sum(array.size for array in operands),
+            transcendentals=0,
+        ),
+    )(*operands)
+
+
+def projection_kernel(inputs, others, own, first, second, left, right, near, told, part, other):
+    width = near.shape[1]
+    count = own.shape[0]
+    half = left.shape[1]
+    for index, quarter in enumerate((own, first, second)):
+        held = slice(index * count, (index + 1) * count)
+        near[held, :] = quarter[:, :width]
+        if quarter.shape[1] > width:
+            told[held, :] = quarter[:, width:]
+    near[3 * count :, :half] = left[...]
+    near[3 * count :, half:] = right[:, : width - half]
+    if half + right.shape[1] > width:
+        told[3 * count :, :] = right[:, width - half :]
+    else:
+        told[...] = jnp.zeros_like(told)
+    part[...] = matmul(inputs[...], near[...], ((1,), (1,))).astype(part.dtype)
+    other[...] = matmul(others[...], near[...], ((1,), (1,))).astype(other.dtype)
+
+
+def projected(inputs, others, quarters, place):
+    width = inputs.shape[1]
+    count = 4 * quarters[0].shape[0]
+    extra = max(quarters[0].shape[1] - width, 128)
+    dtype = jnp.bfloat16 if lax.axis_size("tensor") == 1 else jnp.float32
+    result = jax.ShapeDtypeStruct((inputs.shape[0], count), dtype)
+    near, told, part, other = vmem_call(
+        projection_kernel,
+        (
+            jax.ShapeDtypeStruct((count, width), jnp.bfloat16),
+            jax.ShapeDtypeStruct((count, extra), jnp.bfloat16),
+            result,
+            result,
+        ),
+        (inputs, others) + tuple(quarters),
+        2 * inputs.shape[0] * width * count,
+    )
+    other = shifted(tensor_total(other).astype(jnp.bfloat16), OWNERS, CORE)
+    relative = lax.concatenate([tensor_total(part).astype(jnp.bfloat16), other], 1)
+    return matmul(relative, place).astype(jnp.bfloat16), near, told
+
+
+def grad_kernel(quad, *refs):
+    inputs, (sent, kept) = refs[:4], refs[4:]
+    count = inputs[0].shape[0]
+    half = quad.shape[1] // 2
+    for target, columns in ((sent, slice(half, None)), (kept, slice(0, half))):
+        total = None
+        for index, block in enumerate(inputs):
+            part = quad[index * count : (index + 1) * count, columns]
+            term = matmul(part, block[...], ((0,), (0,)))
+            total = term if total is None else total + term
+        target[...] = total.astype(target.dtype)
 
 
 def projection_grad(relative, quad_inputs, first, second):
@@ -123,9 +192,14 @@
     half = half // 2
     quad = lax.concatenate([pair[:, :half], shifted(pair[:, half:], OWNERS, second)], 0)
     half = half // 2
-    sent = matmul(quad[:, half:], quad_inputs, ((0,), (0,))).astype(jnp.bfloat16)
-    sent = shifted(sent, OWNERS, first)
-    kept = matmul(quad[:, :half], quad_inputs, ((0,), (0,))) + sent.astype(jnp.float32)
+    shape = (half, quad_inputs[0].shape[1])
+    sent, kept = vmem_call(
+        grad_kernel,
+        (jax.ShapeDtypeStruct(shape, jnp.bfloat16), jax.ShapeDtypeStruct(shape, jnp.float32)),
+        (quad,) + tuple(quad_inputs),
+        quad.size * shape[1],
+    )
+    kept = kept + shifted(sent, OWNERS, first).astype(jnp.float32)
     pieces = jnp.split(kept, depth, axis=0)
     total = pieces[0]
     for step in range(1, depth):
@@ -283,17 +357,11 @@
     )(*operands)
 
 
-def expert_plans(routes, combine_fixed, local_experts):
+def expert_plans(told, local_experts, row_count):
     shards = lax.axis_size("expert")
     depth = radices(shards)[Z]
-    row_count, top_count = routes.shape
-    capacity = 3 * row_count * top_count // (2 * local_experts * shards)
-    told = lax.concatenate([routes.T, combine_fixed.T], 0).astype(jnp.bfloat16)
-    told = lax.all_gather(told.reshape(1, -1), "expert", axis=0, tiled=True)
-    owners = relative_owners(EXPERT, Y, X)
-    order = owners[:, None] == jnp.arange(shards, dtype=jnp.int32)[None, :]
-    told = matmul(order.astype(jnp.bfloat16), told)
-    told = told.astype(jnp.int32).reshape(shards, 2, top_count, row_count)
+    told = told.astype(jnp.int32).reshape(shards, 2, -1, row_count)
+    capacity = 3 * row_count * told.shape[2] // (2 * local_experts * shards)
     mine = lax.axis_index("expert") * local_experts + jnp.arange(local_experts, dtype=jnp.int32)
     chosen = told[:, 0][:, None] == mine[None, :, None, None]
     fixed = jnp.sum(jnp.where(chosen, told[:, 1][:, None], 0), axis=2)
@@ -317,56 +385,83 @@
     return [(slots[core], scales[core]) for core in (0, 1)], depth * capacity
 
 
+def after(value, *earlier):
+    return lax.optimization_barrier((value, earlier))[0]
+
+
 def local(
     tokens, out_grad, routes, combine_fixed, down_proj, up_proj, expert_gate, expert_up, expert_down
 ):
     local_experts, latent_width, width = expert_gate.shape
+    row_count = tokens.shape[0]
     rows = down_proj.shape[0]
-    plans, slot_count = expert_plans(routes, combine_fixed, local_experts)
-
-    pair_tokens = lax.concatenate([tokens, shifted(tokens, OWNERS, CORE)], 0)
-    down_parts = gather_quarters(down_proj, OWNERS, Y, X)
-    pair_grads = lax.concatenate([out_grad, shifted(out_grad, OWNERS, CORE)], 0)
-    up_parts = gather_quarters(up_proj, OWNERS, X, Y)
-    down_near, up_near = joined(down_parts), joined(up_parts)
+    told = lax.concatenate([routes.T, combine_fixed.T], 0).astype(jnp.bfloat16)
+    ride = lax.axis_size("dp") == 1
+    down_sent = down_proj
+    if ride:
+        down_sent = lax.concatenate([down_proj, told.reshape(rows, -1)], 1)
+    down_own = gather_depth(down_sent, OWNERS)
+    other_tokens = shifted(tokens, OWNERS, CORE)
+    down_parts = gather_chips(down_own, OWNERS, Y, X)
+    up_own = gather_depth(after(up_proj, down_own), OWNERS)
+    other_grads = shifted(after(out_grad, down_own), OWNERS, CORE)
+    up_parts = gather_chips(up_own, OWNERS, X, Y)
 
     down_place = placement(rows, Y, X)
     up_place = placement(rows, X, Y)
-    latent = projected(pair_tokens, down_near, down_place)
-    near = gather_quarters(latent, EXPERT, Y, X)
+    latent, down_near, told_near = projected(tokens, other_tokens, down_parts, down_place)
+    if not ride:
+        told_near = joined(gather_quarters(told, EXPERT, Y, X))
+    told_far = shifted(told_near, EXPERT, CORE)
+    plans, slot_count = expert_plans(
+        lax.concatenate([told_near, told_far], 0), local_experts, row_count
+    )
+    latent_own = gather_depth(latent, EXPERT)
+    near = gather_chips(latent_own, EXPERT, Y, X)
     far = tuple(shifted(part, EXPERT, CORE) for part in near)
-    mix_grad = projected(pair_grads, up_near, up_place)
-    near_grad = gather_quarters(mix_grad, EXPERT, Y, X)
+    mix_grad, up_near, _ = projected(out_grad, other_grads, up_parts, up_place)
+    near_grad = gather_quarters(after(mix_grad, latent_own), EXPERT, Y, X)
     far_grad = tuple(shifted(part, EXPERT, CORE) for part in near_grad)
 
     narrow = pltpu.VMEM((4 * slot_count, latent_width), jnp.bfloat16)
     wide = pltpu.VMEM((4 * slot_count, width), jnp.bfloat16)
     weights = (expert_gate, expert_up, expert_down)
-    forward = [
-        expert_call(forward_kernel, 3, (narrow, wide), plan, quarters, weights)
-        for plan, quarters in zip(plans, (near, far))
-    ]
-    far_grad, forward = lax.optimization_barrier((far_grad, forward))
-    backward = [
-        expert_call(backward_kernel, 5, (narrow, narrow, wide, wide), plan, quarters, weights)
-        for plan, quarters in zip(plans, (near + near_grad, far + far_grad))
-    ]
-    down_far = shifted(down_near, OWNERS, CORE)
-    up_far = shifted(up_near, OWNERS, CORE)
-    quad_tokens = lax.concatenate([pair_tokens, shifted(pair_tokens, OWNERS, X)], 0)
-    quad_grads = lax.concatenate([pair_grads, shifted(pair_grads, OWNERS, Y)], 0)
-
-    mixed_rows = tensor_total(total_tokens(*forward)).astype(jnp.bfloat16)
+    scratch = (narrow, narrow, wide, wide)
+    forward_near = expert_call(forward_kernel, 3, (narrow, wide), plans[0], near, weights)
+    forward_far = expert_call(
+        forward_kernel, 3, (narrow, wide), plans[1], after(far, forward_near), weights
+    )
+    backward_far = expert_call(
+        backward_kernel, 5, scratch, plans[1], far + after(far_grad, forward_far), weights
+    )
+    forward_sums = core_totals(forward_near, forward_far)
+    near_grad = after(near_grad, backward_far, forward_sums)
+    backward_near = expert_call(
+        backward_kernel, 5, scratch, plans[0], near + near_grad, weights
+    )
+
+    tokens, out_grad, down_far, up_far = after(
+        (tokens, out_grad, down_near, up_near), forward_far
+    )
+    down_far = shifted(down_far, OWNERS, CORE)
+    up_far = shifted(up_far, OWNERS, CORE)
+    next_tokens, next_grads = shifted(tokens, OWNERS, X), shifted(out_grad, OWNERS, Y)
+    quad_tokens = (tokens, other_tokens, next_tokens, shifted(next_tokens, OWNERS, CORE))
+    quad_grads = (out_grad, other_grads, next_grads, shifted(next_grads, OWNERS, CORE))
+
+    mixed_rows = tensor_total(total_tokens(*forward_sums)).astype(jnp.bfloat16)
     mixed_relative = matmul(mixed_rows, up_place, ((1,), (1,))).astype(jnp.bfloat16)
     up_grad = projection_grad(mixed_relative, quad_grads, X, Y)
-    layer_out = matmul(mixed_relative, lax.concatenate([up_near, up_far], 0)).astype(jnp.bfloat16)
-
-    latent_grad = tensor_total(total_tokens(*backward)).astype(jnp.bfloat16)
+    half = latent_width // 2
+    layer_out = matmul(mixed_relative[:, :half], up_near)
+    layer_out = (layer_out + matmul(mixed_relative[:, half:], up_far)).astype(jnp.bfloat16)
+
+    backward_sums = core_totals(backward_near, backward_far)
+    latent_grad = tensor_total(total_tokens(*backward_sums)).astype(jnp.bfloat16)
     grad_relative = matmul(latent_grad, down_place, ((1,), (1,))).astype(jnp.bfloat16)
     down_grad = projection_grad(grad_relative, quad_tokens, Y, X)
-    token_grad = matmul(grad_relative, lax.concatenate([down_near, down_far], 0)).astype(
-        jnp.bfloat16
-    )
+    token_grad = matmul(grad_relative[:, :half], down_near)
+    token_grad = (token_grad + matmul(grad_relative[:, half:], down_far)).astype(jnp.bfloat16)
     return (layer_out, token_grad, down_grad, up_grad)
 
 

time: 298 us -> 234 us (0.79)
  blocking collectives: 42.3 us -> 0 us
  local copies, waits for them, and re-layouts: 30.4 us -> 12.2 us
  matrix products: 13.3 us -> 4.6 us
  Pallas kernels: 26.1 us -> 32.4 us
    all_gather x1 -> x0, blocking collectives: 42.3 us -> none  [expert_plans(): told = lax.all_gather(told.reshape(1, -1), 'expert', axis=0, tiled=True)]
    unnamed x46 -> x34, local copies, waits for them, and re-layouts: 23.3 us -> 6.63 us
    dot_general x13 -> x8, matrix products: 13.2 us -> 4.51 us  [matmul(): lax.dot_general(left, right, (contract, ((), ())), preferred_element_type...]
    pallas_call x0 -> x4, Pallas kernels: none -> 6.37 us  [vmem_call(): pl.pallas_call(kernel, out_shape=out_shape, in_specs=[whole] * len(operan...]
    ppermute x80 -> x83, waiting for transfers between devices: 107 us -> 106 us  [shifted(): return lax.ppermute(block, axes, pairs)]
    ppermute x80 -> x83, starting transfers between devices: 69 us -> 68.6 us  [shifted(): return lax.ppermute(block, axes, pairs)]
  transfers between devices with their start and end apart: 80 -> 83, of which waited for: 32 -> 34; matrix products, arithmetic and copies ran while one was open for 17% -> 8% of each run, Pallas kernels for 9% -> 14%
where the time goes in v4:
time: 234 us
  waiting for transfers between devices  106 us (45%)
  starting transfers between devices  68.6 us (29%)
  Pallas kernels  32.4 us (14%)
  local copies, waits for them, and re-layouts  12.2 us (5%)
  other arithmetic  8.31 us (4%)
  matrix products  4.6 us (2%)
    ppermute x83, waiting for transfers between devices, shifted(): return lax.ppermute(block, axes, pairs)  106 us
    ppermute x83, starting transfers between devices, shifted(): return lax.ppermute(block, axes, pairs)  68.6 us
    pallas_call x4, Pallas kernels, expert_call(): pl.pallas_call(kernel, out_shape=(jax.ShapeDtypeStruct((span, latent_widt...  26.1 us
    unnamed x34, local copies, waits for them, and re-layouts  6.63 us
    pallas_call x4, Pallas kernels, vmem_call(): pl.pallas_call(kernel, out_shape=out_shape, in_specs=[whole] * len(operan...  6.37 us
  transfers between devices with their start and end apart: 83, of which 34 were waited for; matrix products, arithmetic and copies ran while one was open for 8% of the time, Pallas kernels for 14%

profile of v4, /device:TPU:0, one launch (start us, length us, event | category | flops | bytes accessed | tf_op | source)
XLA Modules:
  0.0 233.6 jit_solution(2936909736189649295)
XLA Ops:
  2.3 3.0 %collective-permute-start.1 = (bf16[16,2176]{1,0:T(8,128)(2,1)S(1)}, bf16[16,2176]{1,0:T(8,128)(2,1)S(1)}, u32[]{:S(2)}, u32[]{:S(2)}) collective-permute-start(bf16[16,2176]{1,0:T(8,128)(2,1)S(1)} %maximum_maximum_fusion), channel_id=1, source_target_pairs={{0,8},{1,9},{2,10},{3,11},{4,12},{5,13},{6,14},{7,15},{8,16},{9,17... | collective-permute-start | bytes 208904 | tf_op jit(solution)/shard_map/ppermute | solution.py:37
  5.3 2.6 %collective-permute-start.2 = (bf16[16,2176]{1,0:T(8,128)(2,1)S(1)}, bf16[16,2176]{1,0:T(8,128)(2,1)S(1)}, u32[]{:S(2)}, u32[]{:S(2)}) collective-permute-start(bf16[16,2176]{1,0:T(8,128)(2,1)S(1)} %maximum_maximum_fusion), channel_id=1, source_target_pairs={{0,16},{1,17},{2,18},{3,19},{4,20},{5,21},{6,22},{7,23},{8,24},{9,... | collective-permute-start | bytes 208904 | tf_op jit(solution)/shard_map/ppermute | solution.py:37
  9.9 2.7 %collective-permute-done.2 = bf16[16,2176]{1,0:T(8,128)(2,1)S(1)} collective-permute-done((bf16[16,2176]{1,0:T(8,128)(2,1)S(1)}, bf16[16,2176]{1,0:T(8,128)(2,1)S(1)}, u32[]{:S(2)}, u32[]{:S(2)}) %collective-permute-start.2) | collective-permute-done | bytes 69664 | tf_op jit(solution)/shard_map/ppermute | solution.py:37
  13.6 1.6 collective-permute-start.5
  15.2 1.5 collective-permute-start.4
  16.7 1.7 collective-permute-start.34
  20.0 2.0 collective-permute-start.35
  21.9 1.9 collective-permute-done.34
  25.0 1.5 collective-permute-done.35
  31.2 1.9 collective-permute-start.7
  33.8 1.7 collective-permute-done.37.first
  37.9 1.8 collective-permute-done.38.second
  40.8 1.6 collective-permute-start.40
  44.9 2.4 %shard_map.120 = (bf16[256,2048]{1,0:T(8,128)(2,1)S(1)}, bf16[256,128]{1,0:T(8,128)(2,1)S(1)}, bf16[128,256]{1,0:T(8,128)(2,1)S(1)}, bf16[128,256]{1,0:T(8,128)(2,1)}) custom-call(bf16[128,2048]{1,0:T(8,128)(2,1)S(1)} %copy-done.1, bf16[128,2048]{1,0:T(8,128)(2,1)S(1)} %collective-permute-done.others.refs_1_, bf16[64,2176]{1,0:T(8,128)(2,1)S(1)} %pad_maximum_fusion.5.own, ...), custom_call_target="tpu_custom_call" | custom-call | flops 268435456 | bytes 2162688 | tf_op jit(solution)/shard_map/pallas_call | solution.py:120
  51.4 2.3 shard_map.123
  54.3 2.9 %collective-permute-start.11 = (bf16[128,512]{1,0:T(8,128)(2,1)S(1)}, bf16[128,512]{1,0:T(8,128)(2,1)S(1)}, u32[]{:S(2)}, u32[]{:S(2)}) collective-permute-start(bf16[128,512]{1,0:T(8,128)(2,1)S(1)} %convolution_convert_fusion.3), channel_id=1, source_target_pairs={{0,16},{1,17},{2,18},{3,19},{4,20},{5,21},{6,22},{7,23},{8,24},{9,... | collective-permute-start | bytes 393224 | tf_op jit(solution)/shard_map/ppermute | solution.py:37
  58.5 4.0 %collective-permute-done.10 = bf16[128,512]{1,0:T(8,128)(2,1)S(1)} collective-permute-done((bf16[128,512]{1,0:T(8,128)(2,1)S(1)}, bf16[128,512]{1,0:T(8,128)(2,1)S(1)}, u32[]{:S(2)}, u32[]{:S(2)}) %collective-permute-start.10) | collective-permute-done | bytes 131104 | tf_op jit(solution)/shard_map/ppermute | solution.py:37
  62.5 4.7 %collective-permute-done.11 = bf16[128,512]{1,0:T(8,128)(2,1)S(1)} collective-permute-done((bf16[128,512]{1,0:T(8,128)(2,1)S(1)}, bf16[128,512]{1,0:T(8,128)(2,1)S(1)}, u32[]{:S(2)}, u32[]{:S(2)}) %collective-permute-start.11) | collective-permute-done | bytes 131104 | tf_op jit(solution)/shard_map/ppermute | solution.py:37
  67.2 3.0 %collective-permute-start.43 = (bf16[128,512]{1,0:T(8,128)(2,1)S(1)}, bf16[128,512]{1,0:T(8,128)(2,1)S(1)}, u32[]{:S(2)}, u32[]{:S(2)}) collective-permute-start(bf16[128,512]{1,0:T(8,128)(2,1)S(1)} %convolution_convert_fusion.1), channel_id=1, source_target_pairs={{0,8},{1,9},{2,10},{3,11},{4,12},{5,13},{6,14},{7,15},{8,16},{9,17... | collective-permute-start | bytes 393224 | tf_op jit(solution)/shard_map/ppermute | solution.py:37
  73.0 1.8 collective-permute-start.45
  74.8 6.0 %collective-permute-done.44 = bf16[128,512]{1,0:T(8,128)(2,1)S(1)} collective-permute-done((bf16[128,512]{1,0:T(8,128)(2,1)S(1)}, bf16[128,512]{1,0:T(8,128)(2,1)S(1)}, u32[]{:S(2)}, u32[]{:S(2)}) %collective-permute-start.44) | collective-permute-done | bytes 131104 | tf_op jit(solution)/shard_map/ppermute | solution.py:37
  80.9 1.6 collective-permute-start.46
  83.3 1.7 collective-permute-done.13.refs_3_
  85.0 1.8 collective-permute-start.15
  87.1 9.1 %collective-permute-done.46.refs_8_ = bf16[512,512]{1,0:T(8,128)(2,1)S(1)} collective-permute-done((bf16[512,512]{1,0:T(8,128)(2,1)S(1)}, bf16[512,512]{1,0:T(8,128)(2,1)S(1)}, u32[]{:S(2)}, u32[]{:S(2)}) %collective-permute-start.46) | collective-permute-done | bytes 524320 | tf_op jit(solution)/shard_map/ppermute | solution.py:37
  96.3 1.8 collective-permute-start.48
  98.6 4.4 %collective-permute-done.15.refs_5_ = bf16[512,256]{1,0:T(8,128)(2,1)S(1)} collective-permute-done((bf16[512,256]{1,0:T(8,128)(2,1)S(1)}, bf16[512,256]{1,0:T(8,128)(2,1)S(1)}, u32[]{:S(2)}, u32[]{:S(2)}) %collective-permute-start.15) | collective-permute-done | bytes 262176 | tf_op jit(solution)/shard_map/ppermute | solution.py:37
  103.5 3.2 %collective-permute-done.48.refs_10_ = bf16[512,256]{1,0:T(8,128)(2,1)S(1)} collective-permute-done((bf16[512,256]{1,0:T(8,128)(2,1)S(1)}, bf16[512,256]{1,0:T(8,128)(2,1)S(1)}, u32[]{:S(2)}, u32[]{:S(2)}) %collective-permute-start.48) | collective-permute-done | bytes 262176 | tf_op jit(solution)/shard_map/ppermute | solution.py:37
  108.4 5.5 %shard_map.121 = (bf16[512,512]{1,0:T(8,128)(2,1)S(1)}, bf16[512,512]{1,0:T(8,128)(2,1)S(1)}, bf16[512,512]{1,0:T(8,128)(2,1)S(1)}, bf16[512,512]{1,0:T(8,128)(2,1)S(1)}) custom-call(s32[4,2,1,512]{3,2,1,0:T(1,128)S(1)} %bitcast.64, f32[4,2,1,512]{3,2,1,0:T(1,128)S(1)} %bitcast.60, bf16[512,512]{1,0:T(8,128)(2,1)S(1)} %pad_maximum_fusion.refs_2_, ...), custom_call_target="tpu_custom_call" | custom-call | flops 2415919104 | bytes 8404992 | tf_op jit(solution)/shard_map/pallas_call | solution.py:345
  114.5 5.3 %shard_map.122 = (bf16[512,512]{1,0:T(8,128)(2,1)S(1)}, bf16[512,512]{1,0:T(8,128)(2,1)S(1)}, bf16[512,512]{1,0:T(8,128)(2,1)S(1)}, bf16[512,512]{1,0:T(8,128)(2,1)S(1)}) custom-call(s32[4,2,1,512]{3,2,1,0:T(1,128)S(1)} %bitcast.66, f32[4,2,1,512]{3,2,1,0:T(1,128)S(1)} %bitcast.62, bf16[512,512]{1,0:T(8,128)(2,1)S(1)} %collective-permute-done.17.refs_2_, ...), custom_call_target="tpu_custom_call" | custom-call | flops 2415919104 | bytes 8404992 | tf_op jit(solution)/shard_map/pallas_call | solution.py:345
  120.9 7.5 %shard_map.124 = (bf16[512,512]{1,0:T(8,128)(2,1)S(1)}, bf16[512,512]{1,0:T(8,128)(2,1)S(1)}, bf16[512,512]{1,0:T(8,128)(2,1)S(1)}, bf16[512,512]{1,0:T(8,128)(2,1)S(1)}) custom-call(s32[4,2,1,512]{3,2,1,0:T(1,128)S(1)} %bitcast.67, f32[4,2,1,512]{3,2,1,0:T(1,128)S(1)} %bitcast.63, bf16[512,512]{1,0:T(8,128)(2,1)S(1)} %collective-permute-done.17.refs_2_, ...), custom_call_target="tpu_custom_call" | custom-call | flops 4026531840 | bytes 10502144 | tf_op jit(solution)/shard_map/pallas_call | solution.py:345
  131.1 7.7 %shard_map.125 = (bf16[512,512]{1,0:T(8,128)(2,1)S(1)}, bf16[512,512]{1,0:T(8,128)(2,1)S(1)}, bf16[512,512]{1,0:T(8,128)(2,1)S(1)}, bf16[512,512]{1,0:T(8,128)(2,1)S(1)}) custom-call(s32[4,2,1,512]{3,2,1,0:T(1,128)S(1)} %bitcast.65, f32[4,2,1,512]{3,2,1,0:T(1,128)S(1)} %bitcast.61, bf16[512,512]{1,0:T(8,128)(2,1)S(1)} %pad_maximum_fusion.refs_2_, ...), custom_call_target="tpu_custom_call" | custom-call | flops 4026531840 | bytes 10502144 | tf_op jit(solution)/shard_map/pallas_call | solution.py:345
  138.9 1.6 collective-permute-start.28
  142.6 5.6 %collective-permute-done.28 = bf16[512,256]{1,0:T(8,128)(2,1)S(1)} collective-permute-done((bf16[512,256]{1,0:T(8,128)(2,1)S(1)}, bf16[512,256]{1,0:T(8,128)(2,1)S(1)}, u32[]{:S(2)}, u32[]{:S(2)}) %collective-permute-start.28) | collective-permute-done | bytes 262176 | tf_op jit(solution)/shard_map/ppermute | solution.py:37
  151.8 2.0 collective-permute-done.61
  153.9 11.1 %collective-permute-done.26 = bf16[512,512]{1,0:T(8,128)(2,1)S(1)} collective-permute-done((bf16[512,512]{1,0:T(8,128)(2,1)S(1)}, bf16[512,512]{1,0:T(8,128)(2,1)S(1)}, u32[]{:S(2)}, u32[]{:S(2)}) %collective-permute-start.26) | collective-permute-done | bytes 524320 | tf_op jit(solution)/shard_map/ppermute | solution.py:37
  165.4 2.7 %collective-permute-start.30 = (bf16[128,512]{1,0:T(8,128)(2,1)S(1)}, bf16[128,512]{1,0:T(8,128)(2,1)S(1)}, u32[]{:S(2)}, u32[]{:S(2)}) collective-permute-start(bf16[128,512]{1,0:T(8,128)(2,1)S(1)} %get-tuple-element.115), channel_id=1, source_target_pairs={{0,24},{1,25},{2,26},{3,27},{4,28},{5,29},{6,30},{7,31},{8,0},{9,1... | collective-permute-start | bytes 393224 | tf_op jit(solution)/shard_map/ppermute | solution.py:37
  169.1 2.7 %collective-permute-done.30 = bf16[128,512]{1,0:T(8,128)(2,1)S(1)} collective-permute-done((bf16[128,512]{1,0:T(8,128)(2,1)S(1)}, bf16[128,512]{1,0:T(8,128)(2,1)S(1)}, u32[]{:S(2)}, u32[]{:S(2)}) %collective-permute-start.30) | collective-permute-done | bytes 131104 | tf_op jit(solution)/shard_map/ppermute | solution.py:37
  171.8 1.8 collective-permute-start.59
  173.6 5.1 %collective-permute-done.31 = bf16[128,512]{1,0:T(8,128)(2,1)S(1)} collective-permute-done((bf16[128,512]{1,0:T(8,128)(2,1)S(1)}, bf16[128,512]{1,0:T(8,128)(2,1)S(1)}, u32[]{:S(2)}, u32[]{:S(2)}) %collective-permute-start.31) | collective-permute-done | bytes 131104 | tf_op jit(solution)/shard_map/ppermute | solution.py:37
  181.5 5.0 %collective-permute-done.59 = bf16[512,512]{1,0:T(8,128)(2,1)S(1)} collective-permute-done((bf16[512,512]{1,0:T(8,128)(2,1)S(1)}, bf16[512,512]{1,0:T(8,128)(2,1)S(1)}, u32[]{:S(2)}, u32[]{:S(2)}) %collective-permute-start.59) | collective-permute-done | bytes 524320 | tf_op jit(solution)/shard_map/ppermute | solution.py:37
  186.4 7.1 %collective-permute-done.62 = bf16[512,512]{1,0:T(8,128)(2,1)S(1)} collective-permute-done((bf16[512,512]{1,0:T(8,128)(2,1)S(1)}, bf16[512,512]{1,0:T(8,128)(2,1)S(1)}, u32[]{:S(2)}, u32[]{:S(2)}) %collective-permute-start.62) | collective-permute-done | bytes 524320 | tf_op jit(solution)/shard_map/ppermute | solution.py:37
  197.4 4.5 %collective-permute-done.69.refs_2_ = bf16[128,2048]{1,0:T(8,128)(2,1)S(1)} collective-permute-done((bf16[128,2048]{1,0:T(8,128)(2,1)S(1)}, bf16[128,2048]{1,0:T(8,128)(2,1)S(1)}, u32[]{:S(2)}, u32[]{:S(2)}) %collective-permute-start.69) | collective-permute-done | bytes 524320 | tf_op jit(solution)/shard_map/ppermute | solution.py:37
  203.2 1.8 collective-permute-start.79
  205.0 4.9 %collective-permute-done.64 = bf16[128,512]{1,0:T(8,128)(2,1)S(1)} collective-permute-done((bf16[128,512]{1,0:T(8,128)(2,1)S(1)}, bf16[128,512]{1,0:T(8,128)(2,1)S(1)}, u32[]{:S(2)}, u32[]{:S(2)}) %collective-permute-start.64) | collective-permute-done | bytes 131104 | tf_op jit(solution)/shard_map/ppermute | solution.py:37
  214.0 2.1 collective-permute-done.68
  220.3 3.9 %collective-permute-done.71 = bf16[64,2048]{1,0:T(8,128)(2,1)S(1)} collective-permute-done((bf16[64,2048]{1,0:T(8,128)(2,1)S(1)}, bf16[64,2048]{1,0:T(8,128)(2,1)S(1)}, u32[]{:S(2)}, u32[]{:S(2)}) %collective-permute-start.71) | collective-permute-done | bytes 262176 | tf_op jit(solution)/shard_map/ppermute | solution.py:37
  229.3 2.3 collective-permute-done.73
  (240 shorter events, 65.8 us)
Async XLA Ops:
  9.2 33.8 %collective-permute-start = (bf16[128,2048]{1,0:T(8,128)(2,1)}, bf16[128,2048]{1,0:T(8,128)(2,1)S(1)}, u32[]{:S(2)}, u32[]{:S(2)}) collective-permute-start(bf16[128,2048]{1,0:T(8,128)(2,1)} %refs_0_), channel_id=1, source_target_pairs={{0,1},{1,0},{2,3},{3,2},{4,5},{5,4},{6,7},{7,6},{8,9},{9,8},{10,11... | collective-permute-start | bytes 1572872 | tf_op jit(solution)/shard_map/ppermute | solution.py:37
  13.6 16.7 %collective-permute-start.5 = (bf16[64,2176]{1,0:T(8,128)(2,1)S(1)}, bf16[64,2176]{1,0:T(8,128)(2,1)S(1)}, u32[]{:S(2)}, u32[]{:S(2)}) collective-permute-start(bf16[64,2176]{1,0:T(8,128)(2,1)S(1)} %pad_maximum_fusion.5.own), channel_id=1, source_target_pairs={{0,2},{1,3},{2,0},{3,1},{4,6},{5,7},{6,4},{7,5},{8,10},{9,11},{10,... | collective-permute-start | bytes 835592 | tf_op jit(solution)/shard_map/ppermute | solution.py:37
  15.2 16.0 %collective-permute-start.4 = (bf16[64,2176]{1,0:T(8,128)(2,1)S(1)}, bf16[64,2176]{1,0:T(8,128)(2,1)S(1)}, u32[]{:S(2)}, u32[]{:S(2)}) collective-permute-start(bf16[64,2176]{1,0:T(8,128)(2,1)S(1)} %pad_maximum_fusion.5.own), channel_id=1, source_target_pairs={{0,4},{1,5},{2,6},{3,7},{4,0},{5,1},{6,2},{7,3},{8,12},{9,13},{10,... | collective-permute-start | bytes 835592 | tf_op jit(solution)/shard_map/ppermute | solution.py:37
  30.2 19.3 %collective-permute-start.33 = (bf16[128,2048]{1,0:T(8,128)(2,1)}, bf16[128,2048]{1,0:T(8,128)(2,1)S(1)}, u32[]{:S(2)}, u32[]{:S(2)}) collective-permute-start(bf16[128,2048]{1,0:T(8,128)(2,1)} %refs_0_.1), channel_id=1, source_target_pairs={{0,1},{1,0},{2,3},{3,2},{4,5},{5,4},{6,7},{7,6},{8,9},{9,8},{10,11... | collective-permute-start | bytes 1572872 | tf_op jit(solution)/shard_map/ppermute | solution.py:37
  30.3 9.4 %collective-permute-start.38 = (bf16[64,2048]{1,0:T(8,128)(2,1)}, bf16[64,2048]{1,0:T(8,128)(2,1)S(1)}, u32[]{:S(2)}, u32[]{:S(2)}) collective-permute-start(bf16[64,2048]{1,0:T(8,128)(2,1)} %constant_dynamic-update-slice_fusion.own), channel_id=1, source_target_pairs={{0,4},{1,5},{2,6},{3,7},{4,0},{5,1},{6,2},{7,3},{8,12},{9,13},{10,... | collective-permute-start | bytes 786440 | tf_op jit(solution)/shard_map/ppermute | solution.py:37
  31.2 11.8 %collective-permute-start.7 = (bf16[64,1152]{1,0:T(8,128)(2,1)}, bf16[64,1152]{1,0:T(8,128)(2,1)}, u32[]{:S(2)}, u32[]{:S(2)}) collective-permute-start(bf16[64,1152]{1,0:T(8,128)(2,1)} %slice.149), channel_id=1, source_target_pairs={{0,4},{1,5},{2,6},{3,7},{4,0},{5,1},{6,2},{7,3},{8,12},{9,13},{10,... | collective-permute-start | bytes 442376 | tf_op jit(solution)/shard_map/ppermute | solution.py:37
  39.7 9.8 %collective-permute-start.39 = (bf16[64,1024]{1,0:T(8,128)(2,1)}, bf16[64,1024]{1,0:T(8,128)(2,1)}, u32[]{:S(2)}, u32[]{:S(2)}) collective-permute-start(bf16[64,1024]{1,0:T(8,128)(2,1)} %slice.165), channel_id=1, source_target_pairs={{0,4},{1,5},{2,6},{3,7},{4,0},{5,1},{6,2},{7,3},{8,12},{9,13},{10,... | collective-permute-start | bytes 393224 | tf_op jit(solution)/shard_map/ppermute | solution.py:37
  49.0 21.2 %collective-permute-start.8 = (bf16[256,128]{1,0:T(8,128)(2,1)S(1)}, bf16[256,128]{1,0:T(8,128)(2,1)S(1)}, u32[]{:S(2)}, u32[]{:S(2)}) collective-permute-start(bf16[256,128]{1,0:T(8,128)(2,1)S(1)} %get-tuple-element.53), channel_id=1, source_target_pairs={{0,1},{1,0},{2,3},{3,2},{4,5},{5,4},{6,7},{7,6},{8,9},{9,8},{10,11... | collective-permute-start | bytes 196616 | tf_op jit(solution)/shard_map/ppermute | solution.py:37
  54.3 12.9 %collective-permute-start.11 = (bf16[128,512]{1,0:T(8,128)(2,1)S(1)}, bf16[128,512]{1,0:T(8,128)(2,1)S(1)}, u32[]{:S(2)}, u32[]{:S(2)}) collective-permute-start(bf16[128,512]{1,0:T(8,128)(2,1)S(1)} %convolution_convert_fusion.3), channel_id=1, source_target_pairs={{0,16},{1,17},{2,18},{3,19},{4,20},{5,21},{6,22},{7,23},{8,24},{9,... | collective-permute-start | bytes 393224 | tf_op jit(solution)/shard_map/ppermute | solution.py:37
  57.1 10.0 %collective-permute-start.12 = (bf16[128,512]{1,0:T(8,128)(2,1)S(1)}, bf16[128,512]{1,0:T(8,128)(2,1)S(1)}, u32[]{:S(2)}, u32[]{:S(2)}) collective-permute-start(bf16[128,512]{1,0:T(8,128)(2,1)S(1)} %convolution_convert_fusion.3), channel_id=1, source_target_pairs={{0,24},{1,25},{2,26},{3,27},{4,28},{5,29},{6,30},{7,31},{8,0},{9,1... | collective-permute-start | bytes 393224 | tf_op jit(solution)/shard_map/ppermute | solution.py:37
  70.3 14.7 %collective-permute-start.13 = (bf16[512,512]{1,0:T(8,128)(2,1)S(1)}, bf16[512,512]{1,0:T(8,128)(2,1)S(1)}, u32[]{:S(2)}, u32[]{:S(2)}) collective-permute-start(bf16[512,512]{1,0:T(8,128)(2,1)S(1)} %pad_maximum_fusion.refs_2_), channel_id=1, source_target_pairs={{0,4},{1,5},{2,6},{3,7},{4,0},{5,1},{6,2},{7,3},{8,12},{9,13},{10,... | collective-permute-start | bytes 1572872 | tf_op jit(solution)/shard_map/ppermute | solution.py:37
  71.3 15.5 %collective-permute-start.14 = (bf16[512,512]{1,0:T(8,128)(2,1)S(1)}, bf16[512,512]{1,0:T(8,128)(2,1)S(1)}, u32[]{:S(2)}, u32[]{:S(2)}) collective-permute-start(bf16[512,512]{1,0:T(8,128)(2,1)S(1)} %pad_maximum_fusion.refs_2_), channel_id=1, source_target_pairs={{0,2},{1,3},{2,0},{3,1},{4,6},{5,7},{6,4},{7,5},{8,10},{9,11},{10,... | collective-permute-start | bytes 1572872 | tf_op jit(solution)/shard_map/ppermute | solution.py:37
  80.9 15.4 %collective-permute-start.46 = (bf16[512,512]{1,0:T(8,128)(2,1)S(1)}, bf16[512,512]{1,0:T(8,128)(2,1)S(1)}, u32[]{:S(2)}, u32[]{:S(2)}) collective-permute-start(bf16[512,512]{1,0:T(8,128)(2,1)S(1)} %constant_dynamic-update-slice_fusion.4.refs_7_), channel_id=1, source_target_pairs={{0,4},{1,5},{2,6},{3,7},{4,0},{5,1},{6,2},{7,3},{8,12},{9,13},{10,... | collective-permute-start | bytes 1572872 | tf_op jit(solution)/shard_map/ppermute | solution.py:37
  82.5 15.6 %collective-permute-start.47 = (bf16[512,512]{1,0:T(8,128)(2,1)S(1)}, bf16[512,512]{1,0:T(8,128)(2,1)S(1)}, u32[]{:S(2)}, u32[]{:S(2)}) collective-permute-start(bf16[512,512]{1,0:T(8,128)(2,1)S(1)} %constant_dynamic-update-slice_fusion.4.refs_7_), channel_id=1, source_target_pairs={{0,2},{1,3},{2,0},{3,1},{4,6},{5,7},{6,4},{7,5},{8,10},{9,11},{10,... | collective-permute-start | bytes 1572872 | tf_op jit(solution)/shard_map/ppermute | solution.py:37
  83.2 15.3 %collective-permute-start.17 = (bf16[512,512]{1,0:T(8,128)(2,1)S(1)}, bf16[512,512]{1,0:T(8,128)(2,1)S(1)}, u32[]{:S(2)}, u32[]{:S(2)}) collective-permute-start(bf16[512,512]{1,0:T(8,128)(2,1)S(1)} %pad_maximum_fusion.refs_2_), channel_id=1, source_target_pairs={{0,1},{1,0},{2,3},{3,2},{4,5},{5,4},{6,7},{7,6},{8,9},{9,8},{10,11... | collective-permute-start | bytes 1572872 | tf_op jit(solution)/shard_map/ppermute | solution.py:37
  85.0 18.0 %collective-permute-start.15 = (bf16[512,256]{1,0:T(8,128)(2,1)S(1)}, bf16[512,256]{1,0:T(8,128)(2,1)S(1)}, u32[]{:S(2)}, u32[]{:S(2)}) collective-permute-start(bf16[512,256]{1,0:T(8,128)(2,1)S(1)} %slice.154), channel_id=1, source_target_pairs={{0,2},{1,3},{2,0},{3,1},{4,6},{5,7},{6,4},{7,5},{8,10},{9,11},{10,... | collective-permute-start | bytes 786440 | tf_op jit(solution)/shard_map/ppermute | solution.py:37
  86.8 16.2 %collective-permute-start.16 = (bf16[512,256]{1,0:T(8,128)(2,1)S(1)}, bf16[512,256]{1,0:T(8,128)(2,1)S(1)}, u32[]{:S(2)}, u32[]{:S(2)}) collective-permute-start(bf16[512,256]{1,0:T(8,128)(2,1)S(1)} %slice.155), channel_id=1, source_target_pairs={{0,4},{1,5},{2,6},{3,7},{4,0},{5,1},{6,2},{7,3},{8,12},{9,13},{10,... | collective-permute-start | bytes 786440 | tf_op jit(solution)/shard_map/ppermute | solution.py:37
  96.3 10.4 %collective-permute-start.48 = (bf16[512,256]{1,0:T(8,128)(2,1)S(1)}, bf16[512,256]{1,0:T(8,128)(2,1)S(1)}, u32[]{:S(2)}, u32[]{:S(2)}) collective-permute-start(bf16[512,256]{1,0:T(8,128)(2,1)S(1)} %slice.168), channel_id=1, source_target_pairs={{0,2},{1,3},{2,0},{3,1},{4,6},{5,7},{6,4},{7,5},{8,10},{9,11},{10,... | collective-permute-start | bytes 786440 | tf_op jit(solution)/shard_map/ppermute | solution.py:37
  98.5 15.4 %collective-permute-start.18 = (bf16[512,512]{1,0:T(8,128)(2,1)S(1)}, bf16[512,512]{1,0:T(8,128)(2,1)S(1)}, u32[]{:S(2)}, u32[]{:S(2)}) collective-permute-start(bf16[512,512]{1,0:T(8,128)(2,1)S(1)} %collective-permute-done.13.refs_3_), channel_id=1, source_target_pairs={{0,1},{1,0},{2,3},{3,2},{4,5},{5,4},{6,7},{7,6},{8,9},{9,8},{10,11... | collective-permute-start | bytes 1572872 | tf_op jit(solution)/shard_map/ppermute | solution.py:37
  103.0 11.3 %collective-permute-start.19 = (bf16[512,512]{1,0:T(8,128)(2,1)S(1)}, bf16[512,512]{1,0:T(8,128)(2,1)S(1)}, u32[]{:S(2)}, u32[]{:S(2)}) collective-permute-start(bf16[512,512]{1,0:T(8,128)(2,1)S(1)} %collective-permute-done.14.refs_4_), channel_id=1, source_target_pairs={{0,1},{1,0},{2,3},{3,2},{4,5},{5,4},{6,7},{7,6},{8,9},{9,8},{10,11... | collective-permute-start | bytes 1572872 | tf_op jit(solution)/shard_map/ppermute | solution.py:37
  106.9 12.9 %collective-permute-start.50 = (bf16[512,512]{1,0:T(8,128)(2,1)S(1)}, bf16[512,512]{1,0:T(8,128)(2,1)S(1)}, u32[]{:S(2)}, u32[]{:S(2)}) collective-permute-start(bf16[512,512]{1,0:T(8,128)(2,1)S(1)} %constant_dynamic-update-slice_fusion.4.refs_7_), channel_id=1, source_target_pairs={{0,1},{1,0},{2,3},{3,2},{4,5},{5,4},{6,7},{7,6},{8,9},{9,8},{10,11... | collective-permute-start | bytes 1572872 | tf_op jit(solution)/shard_map/ppermute | solution.py:37
  107.5 13.3 %collective-permute-start.51 = (bf16[512,512]{1,0:T(8,128)(2,1)S(1)}, bf16[512,512]{1,0:T(8,128)(2,1)S(1)}, u32[]{:S(2)}, u32[]{:S(2)}) collective-permute-start(bf16[512,512]{1,0:T(8,128)(2,1)S(1)} %collective-permute-done.46.refs_8_), channel_id=1, source_target_pairs={{0,1},{1,0},{2,3},{3,2},{4,5},{5,4},{6,7},{7,6},{8,9},{9,8},{10,11... | collective-permute-start | bytes 1572872 | tf_op jit(solution)/shard_map/ppermute | solution.py:37
  108.2 12.7 %collective-permute-start.52 = (bf16[512,512]{1,0:T(8,128)(2,1)S(1)}, bf16[512,512]{1,0:T(8,128)(2,1)S(1)}, u32[]{:S(2)}, u32[]{:S(2)}) collective-permute-start(bf16[512,512]{1,0:T(8,128)(2,1)S(1)} %collective-permute-done.47.refs_9_), channel_id=1, source_target_pairs={{0,1},{1,0},{2,3},{3,2},{4,5},{5,4},{6,7},{7,6},{8,9},{9,8},{10,11... | collective-permute-start | bytes 1572872 | tf_op jit(solution)/shard_map/ppermute | solution.py:37
  119.8 9.1 %collective-permute-start.24 = (bf16[512,512]{1,0:T(8,128)(2,1)S(1)}, bf16[512,512]{1,0:T(8,128)(2,1)S(1)}, u32[]{:S(2)}, u32[]{:S(2)}) collective-permute-start(bf16[512,512]{1,0:T(8,128)(2,1)S(1)} %get-tuple-element.67), channel_id=1, source_target_pairs={{0,1},{1,0},{2,3},{3,2},{4,5},{5,4},{6,7},{7,6},{8,9},{9,8},{10,11... | collective-permute-start | bytes 1572872 | tf_op jit(solution)/shard_map/ppermute | solution.py:37
  120.4 9.4 %collective-permute-start.27 = (bf16[512,512]{1,0:T(8,128)(2,1)S(1)}, bf16[512,512]{1,0:T(8,128)(2,1)S(1)}, u32[]{:S(2)}, u32[]{:S(2)}) collective-permute-start(bf16[512,512]{1,0:T(8,128)(2,1)S(1)} %get-tuple-element.68), channel_id=1, source_target_pairs={{0,1},{1,0},{2,3},{3,2},{4,5},{5,4},{6,7},{7,6},{8,9},{9,8},{10,11... | collective-permute-start | bytes 1572872 | tf_op jit(solution)/shard_map/ppermute | solution.py:37
  120.8 33.1 %collective-permute-start.22 = (bf16[512,512]{1,0:T(8,128)(2,1)S(1)}, bf16[512,512]{1,0:T(8,128)(2,1)S(1)}, u32[]{:S(2)}, u32[]{:S(2)}) collective-permute-start(bf16[512,512]{1,0:T(8,128)(2,1)S(1)} %get-tuple-element.65), channel_id=1, source_target_pairs={{0,1},{1,0},{2,3},{3,2},{4,5},{5,4},{6,7},{7,6},{8,9},{9,8},{10,11... | collective-permute-start | bytes 1572872 | tf_op jit(solution)/shard_map/ppermute | solution.py:37
  128.5 12.3 %collective-permute-start.56 = (bf16[512,512]{1,0:T(8,128)(2,1)S(1)}, bf16[512,512]{1,0:T(8,128)(2,1)S(1)}, u32[]{:S(2)}, u32[]{:S(2)}) collective-permute-start(bf16[512,512]{1,0:T(8,128)(2,1)S(1)} %get-tuple-element.83), channel_id=1, source_target_pairs={{0,1},{1,0},{2,3},{3,2},{4,5},{5,4},{6,7},{7,6},{8,9},{9,8},{10,11... | collective-permute-start | bytes 1572872 | tf_op jit(solution)/shard_map/ppermute | solution.py:37
  128.9 10.0 %collective-permute-start.57 = (bf16[512,512]{1,0:T(8,128)(2,1)S(1)}, bf16[512,512]{1,0:T(8,128)(2,1)S(1)}, u32[]{:S(2)}, u32[]{:S(2)}) collective-permute-start(bf16[512,512]{1,0:T(8,128)(2,1)S(1)} %get-tuple-element.85), channel_id=1, source_target_pairs={{0,1},{1,0},{2,3},{3,2},{4,5},{5,4},{6,7},{7,6},{8,9},{9,8},{10,11... | collective-permute-start | bytes 1572872 | tf_op jit(solution)/shard_map/ppermute | solution.py:37
  129.2 20.6 %collective-permute-start.60 = (bf16[512,512]{1,0:T(8,128)(2,1)S(1)}, bf16[512,512]{1,0:T(8,128)(2,1)S(1)}, u32[]{:S(2)}, u32[]{:S(2)}) collective-permute-start(bf16[512,512]{1,0:T(8,128)(2,1)S(1)} %get-tuple-element.84), channel_id=1, source_target_pairs={{0,1},{1,0},{2,3},{3,2},{4,5},{5,4},{6,7},{7,6},{8,9},{9,8},{10,11... | collective-permute-start | bytes 1572872 | tf_op jit(solution)/shard_map/ppermute | solution.py:37
  129.8 11.7 %collective-permute-start.25 = (bf16[512,256]{1,0:T(8,128)(2,1)S(1)}, bf16[512,256]{1,0:T(8,128)(2,1)S(1)}, u32[]{:S(2)}, u32[]{:S(2)}) collective-permute-start(bf16[512,256]{1,0:T(8,128)(2,1)S(1)} %get-tuple-element.118), channel_id=1, source_target_pairs={{0,2},{1,3},{2,0},{3,1},{4,6},{5,7},{6,4},{7,5},{8,10},{9,11},{10,... | collective-permute-start | bytes 786440 | tf_op jit(solution)/shard_map/ppermute | solution.py:37
  138.9 9.3 %collective-permute-start.28 = (bf16[512,256]{1,0:T(8,128)(2,1)S(1)}, bf16[512,256]{1,0:T(8,128)(2,1)S(1)}, u32[]{:S(2)}, u32[]{:S(2)}) collective-permute-start(bf16[512,256]{1,0:T(8,128)(2,1)S(1)} %get-tuple-element.119), channel_id=1, source_target_pairs={{0,4},{1,5},{2,6},{3,7},{4,0},{5,1},{6,2},{7,3},{8,12},{9,13},{10,... | collective-permute-start | bytes 786440 | tf_op jit(solution)/shard_map/ppermute | solution.py:37
  140.7 10.0 %collective-permute-start.58 = (bf16[512,256]{1,0:T(8,128)(2,1)S(1)}, bf16[512,256]{1,0:T(8,128)(2,1)S(1)}, u32[]{:S(2)}, u32[]{:S(2)}) collective-permute-start(bf16[512,256]{1,0:T(8,128)(2,1)S(1)} %get-tuple-element.113), channel_id=1, source_target_pairs={{0,2},{1,3},{2,0},{3,1},{4,6},{5,7},{6,4},{7,5},{8,10},{9,11},{10,... | collective-permute-start | bytes 786440 | tf_op jit(solution)/shard_map/ppermute | solution.py:37
  141.5 12.3 %collective-permute-start.61 = (bf16[512,256]{1,0:T(8,128)(2,1)S(1)}, bf16[512,256]{1,0:T(8,128)(2,1)S(1)}, u32[]{:S(2)}, u32[]{:S(2)}) collective-permute-start(bf16[512,256]{1,0:T(8,128)(2,1)S(1)} %get-tuple-element.114), channel_id=1, source_target_pairs={{0,4},{1,5},{2,6},{3,7},{4,0},{5,1},{6,2},{7,3},{8,12},{9,13},{10,... | collective-permute-start | bytes 786440 | tf_op jit(solution)/shard_map/ppermute | solution.py:37
  148.2 16.9 %collective-permute-start.26 = (bf16[512,512]{1,0:T(8,128)(2,1)S(1)}, bf16[512,512]{1,0:T(8,128)(2,1)S(1)}, u32[]{:S(2)}, u32[]{:S(2)}) collective-permute-start(bf16[512,512]{1,0:T(8,128)(2,1)S(1)} %pad_maximum_fusion.1), channel_id=1, source_target_pairs={{0,4},{1,5},{2,6},{3,7},{4,0},{5,1},{6,2},{7,3},{8,12},{9,13},{10,... | collective-permute-start | bytes 1572872 | tf_op jit(solution)/shard_map/ppermute | solution.py:37
  149.9 15.2 %collective-permute-start.29 = (bf16[512,512]{1,0:T(8,128)(2,1)S(1)}, bf16[512,512]{1,0:T(8,128)(2,1)S(1)}, u32[]{:S(2)}, u32[]{:S(2)}) collective-permute-start(bf16[512,512]{1,0:T(8,128)(2,1)S(1)} %pad_maximum_fusion.2), channel_id=1, source_target_pairs={{0,2},{1,3},{2,0},{3,1},{4,6},{5,7},{6,4},{7,5},{8,10},{9,11},{10,... | collective-permute-start | bytes 1572872 | tf_op jit(solution)/shard_map/ppermute | solution.py:37
  150.7 29.9 %collective-permute-start.77 = (bf16[128,2048]{1,0:T(8,128)(2,1)S(1)}, bf16[128,2048]{1,0:T(8,128)(2,1)S(1)}, u32[]{:S(2)}, u32[]{:S(2)}) collective-permute-start(bf16[128,2048]{1,0:T(8,128)(2,1)S(1)} %copy-done), channel_id=1, source_target_pairs={{0,4},{1,5},{2,6},{3,7},{4,0},{5,1},{6,2},{7,3},{8,12},{9,13},{10,... | collective-permute-start | bytes 1572872 | tf_op jit(solution)/shard_map/ppermute | solution.py:37
  153.8 27.4 %collective-permute-start.55 = (bf16[512,512]{1,0:T(8,128)(2,1)S(1)}, bf16[512,512]{1,0:T(8,128)(2,1)S(1)}, u32[]{:S(2)}, u32[]{:S(2)}) collective-permute-start(bf16[512,512]{1,0:T(8,128)(2,1)S(1)} %get-tuple-element.82), channel_id=1, source_target_pairs={{0,1},{1,0},{2,3},{3,2},{4,5},{5,4},{6,7},{7,6},{8,9},{9,8},{10,11... | collective-permute-start | bytes 1572872 | tf_op jit(solution)/shard_map/ppermute | solution.py:37
  168.1 10.6 %collective-permute-start.31 = (bf16[128,512]{1,0:T(8,128)(2,1)S(1)}, bf16[128,512]{1,0:T(8,128)(2,1)S(1)}, u32[]{:S(2)}, u32[]{:S(2)}) collective-permute-start(bf16[128,512]{1,0:T(8,128)(2,1)S(1)} %get-tuple-element.117), channel_id=1, source_target_pairs={{0,16},{1,17},{2,18},{3,19},{4,20},{5,21},{6,22},{7,23},{8,24},{9,... | collective-permute-start | bytes 393224 | tf_op jit(solution)/shard_map/ppermute | solution.py:37
  169.0 11.2 %collective-permute-start.32 = (bf16[128,512]{1,0:T(8,128)(2,1)S(1)}, bf16[128,512]{1,0:T(8,128)(2,1)S(1)}, u32[]{:S(2)}, u32[]{:S(2)}) collective-permute-start(bf16[128,512]{1,0:T(8,128)(2,1)S(1)} %get-tuple-element.116), channel_id=1, source_target_pairs={{0,8},{1,9},{2,10},{3,11},{4,12},{5,13},{6,14},{7,15},{8,16},{9,17... | collective-permute-start | bytes 393224 | tf_op jit(solution)/shard_map/ppermute | solution.py:37
  171.8 14.6 %collective-permute-start.59 = (bf16[512,512]{1,0:T(8,128)(2,1)S(1)}, bf16[512,512]{1,0:T(8,128)(2,1)S(1)}, u32[]{:S(2)}, u32[]{:S(2)}) collective-permute-start(bf16[512,512]{1,0:T(8,128)(2,1)S(1)} %pad_maximum_fusion.3), channel_id=1, source_target_pairs={{0,4},{1,5},{2,6},{3,7},{4,0},{5,1},{6,2},{7,3},{8,12},{9,13},{10,... | collective-permute-start | bytes 1572872 | tf_op jit(solution)/shard_map/ppermute | solution.py:37
  178.7 14.9 %collective-permute-start.62 = (bf16[512,512]{1,0:T(8,128)(2,1)S(1)}, bf16[512,512]{1,0:T(8,128)(2,1)S(1)}, u32[]{:S(2)}, u32[]{:S(2)}) collective-permute-start(bf16[512,512]{1,0:T(8,128)(2,1)S(1)} %pad_maximum_fusion.4), channel_id=1, source_target_pairs={{0,2},{1,3},{2,0},{3,1},{4,6},{5,7},{6,4},{7,5},{8,10},{9,11},{10,... | collective-permute-start | bytes 1572872 | tf_op jit(solution)/shard_map/ppermute | solution.py:37
  180.1 13.7 %collective-permute-start.41 = (bf16[256,2048]{1,0:T(8,128)(2,1)S(1)}, bf16[256,2048]{1,0:T(8,128)(2,1)S(1)}, u32[]{:S(2)}, u32[]{:S(2)}) collective-permute-start(bf16[256,2048]{1,0:T(8,128)(2,1)S(1)} %get-tuple-element.73), channel_id=1, source_target_pairs={{0,1},{1,0},{2,3},{3,2},{4,5},{5,4},{6,7},{7,6},{8,9},{9,8},{10,11... | collective-permute-start | bytes 3145736 | tf_op jit(solution)/shard_map/ppermute | solution.py:37
  180.6 21.2 %collective-permute-start.69 = (bf16[128,2048]{1,0:T(8,128)(2,1)S(1)}, bf16[128,2048]{1,0:T(8,128)(2,1)S(1)}, u32[]{:S(2)}, u32[]{:S(2)}) collective-permute-start(bf16[128,2048]{1,0:T(8,128)(2,1)S(1)} %copy-done.1), channel_id=1, source_target_pairs={{0,2},{1,3},{2,0},{3,1},{4,6},{5,7},{6,4},{7,5},{8,10},{9,11},{10,... | collective-permute-start | bytes 1572872 | tf_op jit(solution)/shard_map/ppermute | solution.py:37
  181.2 29.3 %collective-permute-start.66 = (bf16[256,2048]{1,0:T(8,128)(2,1)S(1)}, bf16[256,2048]{1,0:T(8,128)(2,1)S(1)}, u32[]{:S(2)}, u32[]{:S(2)}) collective-permute-start(bf16[256,2048]{1,0:T(8,128)(2,1)S(1)} %get-tuple-element.95), channel_id=1, source_target_pairs={{0,1},{1,0},{2,3},{3,2},{4,5},{5,4},{6,7},{7,6},{8,9},{9,8},{10,11... | collective-permute-start | bytes 3145736 | tf_op jit(solution)/shard_map/ppermute | solution.py:37
  186.4 15.9 %collective-permute-start.78 = (bf16[128,2048]{1,0:T(8,128)(2,1)S(1)}, bf16[128,2048]{1,0:T(8,128)(2,1)S(1)}, u32[]{:S(2)}, u32[]{:S(2)}) collective-permute-start(bf16[128,2048]{1,0:T(8,128)(2,1)S(1)} %collective-permute-done.77.refs_2_), channel_id=1, source_target_pairs={{0,1},{1,0},{2,3},{3,2},{4,5},{5,4},{6,7},{7,6},{8,9},{9,8},{10,11... | collective-permute-start | bytes 1572872 | tf_op jit(solution)/shard_map/ppermute | solution.py:37
  193.9 9.3 %collective-permute-start.63 = (bf16[128,512]{1,0:T(8,128)(2,1)S(1)}, bf16[128,512]{1,0:T(8,128)(2,1)S(1)}, u32[]{:S(2)}, u32[]{:S(2)}) collective-permute-start(bf16[128,512]{1,0:T(8,128)(2,1)S(1)} %get-tuple-element.110), channel_id=1, source_target_pairs={{0,24},{1,25},{2,26},{3,27},{4,28},{5,29},{6,30},{7,31},{8,0},{9,1... | collective-permute-start | bytes 393224 | tf_op jit(solution)/shard_map/ppermute | solution.py:37
  202.3 13.8 %collective-permute-start.70 = (bf16[128,2048]{1,0:T(8,128)(2,1)S(1)}, bf16[128,2048]{1,0:T(8,128)(2,1)S(1)}, u32[]{:S(2)}, u32[]{:S(2)}) collective-permute-start(bf16[128,2048]{1,0:T(8,128)(2,1)S(1)} %collective-permute-done.69.refs_2_), channel_id=1, source_target_pairs={{0,1},{1,0},{2,3},{3,2},{4,5},{5,4},{6,7},{7,6},{8,9},{9,8},{10,11... | collective-permute-start | bytes 1572872 | tf_op jit(solution)/shard_map/ppermute | solution.py:37
  203.2 14.6 %collective-permute-start.79 = (bf16[64,2048]{1,0:T(8,128)(2,1)S(1)}, bf16[64,2048]{1,0:T(8,128)(2,1)S(1)}, u32[]{:S(2)}, u32[]{:S(2)}) collective-permute-start(bf16[64,2048]{1,0:T(8,128)(2,1)S(1)} %get-tuple-element.101), channel_id=1, source_target_pairs={{0,2},{1,3},{2,0},{3,1},{4,6},{5,7},{6,4},{7,5},{8,10},{9,11},{10,... | collective-permute-start | bytes 786440 | tf_op jit(solution)/shard_map/ppermute | solution.py:37
  (49 other events, 502.4 us)

commit v5 on v4

--- a/solution.py
+++ b/solution.py
@@ -26,14 +26,17 @@
     return lax.rem(lax.axis_index(axes) // stride, sizes[place])
 
 
-def shifted(block, axes, place, step=1):
+def shifted(block, axes, *places, step=1):
     count = math.prod(lax.axis_size(axis) for axis in axes)
     sizes = radices(count)
-    stride = math.prod(sizes[place + 1 :])
     pairs = []
     for here in range(count):
-        digit = here // stride % sizes[place]
-        pairs.append((here, here + ((digit + step) % sizes[place] - digit) * stride))
+        there = here
+        for place in places:
+            stride = math.prod(sizes[place + 1 :])
+            digit = here // stride % sizes[place]
+            there += ((digit + step) % sizes[place] - digit) * stride
+        pairs.append((here, there))
     return lax.ppermute(block, axes, pairs)
 
 
@@ -59,28 +62,28 @@
     return jnp.stack(owners)
 
 
-def gather_quarters(rows, axes, first, second):
-    return gather_chips(gather_depth(rows, axes), axes, first, second)
-
-
 def gather_depth(rows, axes):
     depth = radices(device_count(axes))[Z]
-    return lax.concatenate([rows] + [shifted(rows, axes, Z, step) for step in range(1, depth)], 0)
+    return lax.concatenate(
+        [rows] + [shifted(rows, axes, Z, step=step) for step in range(1, depth)], 0
+    )
 
 
 def gather_chips(own, axes, first, second):
-    half = own.shape[1] // 256 * 128 or own.shape[1] // 2
-    along_first = shifted(own, axes, first)
-    along_second = shifted(own, axes, second)
-    across = (
-        shifted(along_first[:, :half], axes, second),
-        shifted(along_second[:, half:], axes, first),
-    )
-    return (own, along_first, along_second) + across
-
-
-def joined(quarters):
-    return lax.concatenate(list(quarters[:3]) + [lax.concatenate(list(quarters[3:]), 1)], 0)
+    return (
+        own,
+        shifted(own, axes, first),
+        shifted(own, axes, second),
+        shifted(own, axes, first, second),
+    )
+
+
+def gather_chips_by_turns(alongs, axes, first, second):
+    own, along_first, along_second = alongs
+    half = own.shape[1] // 2
+    left = shifted(along_first[:, :half], axes, second)
+    right = shifted(along_second[:, half:], axes, first)
+    return (own, along_first, along_second, lax.concatenate([left, right], 1))
 
 
 def core_totals(near, far):
@@ -90,8 +93,25 @@
     ]
 
 
-def total_tokens(across, along_y, along_x, own):
-    depth = radices(device_count(EXPERT))[Z]
+def depth_total(terms, axes):
+    depth = radices(device_count(axes))[Z]
+    pieces = jnp.split(terms, depth, axis=0)
+    total = pieces[0]
+    for step in range(1, depth):
+        piece = shifted(pieces[step].astype(jnp.bfloat16), axes, Z, step=depth - step)
+        total = total + piece.astype(jnp.float32)
+    return total
+
+
+def chip_totals(across, along_y, along_x, own):
+    across = shifted(across.astype(jnp.bfloat16), EXPERT, X, Y)
+    along_y = shifted(along_y.astype(jnp.bfloat16), EXPERT, Y)
+    along_x = shifted(along_x.astype(jnp.bfloat16), EXPERT, X)
+    total = own + across.astype(jnp.float32)
+    return total + along_y.astype(jnp.float32) + along_x.astype(jnp.float32)
+
+
+def chip_totals_by_turns(across, along_y, along_x, own):
     across = across.astype(jnp.bfloat16)
     half = across.shape[1] // 2
     left = shifted(across[:, :half], EXPERT, X).astype(jnp.float32)
@@ -99,13 +119,7 @@
     along_y = lax.concatenate([along_y[:, :half] + left, along_y[:, half:]], 1)
     along_x = lax.concatenate([along_x[:, :half], along_x[:, half:] + right], 1)
     own = own + shifted(along_y.astype(jnp.bfloat16), EXPERT, Y).astype(jnp.float32)
-    own = own + shifted(along_x.astype(jnp.bfloat16), EXPERT, X).astype(jnp.float32)
-    pieces = jnp.split(own, depth, axis=0)
-    total = pieces[0]
-    for step in range(1, depth):
-        piece = shifted(pieces[step].astype(jnp.bfloat16), EXPERT, Z, depth - step)
-        total = total + piece.astype(jnp.float32)
-    return total
+    return own + shifted(along_x.astype(jnp.bfloat16), EXPERT, X).astype(jnp.float32)
 
 
 def placement(rows, first, second):
@@ -131,21 +145,17 @@
     )(*operands)
 
 
-def projection_kernel(inputs, others, own, first, second, left, right, near, told, part, other):
+def projection_kernel(inputs, others, *refs):
+    quarters, (near, told, part, other) = refs[:4], refs[4:]
     width = near.shape[1]
-    count = own.shape[0]
-    half = left.shape[1]
-    for index, quarter in enumerate((own, first, second)):
+    count = quarters[0].shape[0]
+    for index, quarter in enumerate(quarters):
         held = slice(index * count, (index + 1) * count)
         near[held, :] = quarter[:, :width]
         if quarter.shape[1] > width:
             told[held, :] = quarter[:, width:]
-    near[3 * count :, :half] = left[...]
-    near[3 * count :, half:] = right[:, : width - half]
-    if half + right.shape[1] > width:
-        told[3 * count :, :] = right[:, width - half :]
-    else:
-        told[...] = jnp.zeros_like(told)
+        else:
+            told[held, :] = jnp.zeros((count, told.shape[1]), told.dtype)
     part[...] = matmul(inputs[...], near[...], ((1,), (1,))).astype(part.dtype)
     other[...] = matmul(others[...], near[...], ((1,), (1,))).astype(other.dtype)
 
@@ -172,40 +182,35 @@
     return matmul(relative, place).astype(jnp.bfloat16), near, told
 
 
-def grad_kernel(quad, *refs):
-    inputs, (sent, kept) = refs[:4], refs[4:]
-    count = inputs[0].shape[0]
-    half = quad.shape[1] // 2
+def grad_kernel(*refs):
+    quad, inputs, (sent, kept) = refs[:4], refs[4:8], refs[8:]
+    half = quad[0].shape[1] // 2
     for target, columns in ((sent, slice(half, None)), (kept, slice(0, half))):
         total = None
-        for index, block in enumerate(inputs):
-            part = quad[index * count : (index + 1) * count, columns]
-            term = matmul(part, block[...], ((0,), (0,)))
+        for part, block in zip(quad, inputs):
+            term = matmul(part[:, columns], block[...], ((0,), (0,)))
             total = term if total is None else total + term
         target[...] = total.astype(target.dtype)
 
 
 def projection_grad(relative, quad_inputs, first, second):
-    depth = radices(device_count(OWNERS))[Z]
-    half = relative.shape[1] // 2
-    pair = lax.concatenate([relative[:, :half], shifted(relative[:, half:], OWNERS, CORE)], 0)
-    half = half // 2
-    quad = lax.concatenate([pair[:, :half], shifted(pair[:, half:], OWNERS, second)], 0)
-    half = half // 2
+    mine, along_second, along_core, across = jnp.split(relative, 4, axis=1)
+    quad = (
+        mine,
+        shifted(along_core, OWNERS, CORE),
+        shifted(along_second, OWNERS, second),
+        shifted(across, OWNERS, second, CORE),
+    )
+    half = mine.shape[1] // 2
     shape = (half, quad_inputs[0].shape[1])
     sent, kept = vmem_call(
         grad_kernel,
         (jax.ShapeDtypeStruct(shape, jnp.bfloat16), jax.ShapeDtypeStruct(shape, jnp.float32)),
-        (quad,) + tuple(quad_inputs),
-        quad.size * shape[1],
+        quad + tuple(quad_inputs),
+        4 * mine.size * shape[1],
     )
     kept = kept + shifted(sent, OWNERS, first).astype(jnp.float32)
-    pieces = jnp.split(kept, depth, axis=0)
-    total = pieces[0]
-    for step in range(1, depth):
-        piece = shifted(pieces[step].astype(jnp.bfloat16), OWNERS, Z, depth - step)
-        total = total + piece.astype(jnp.float32)
-    return total
+    return depth_total(kept, OWNERS)
 
 
 def matmul(left, right, contract=((1,), (0,))):
@@ -225,14 +230,8 @@
     ]
 
 
-def pick_rows(pick, quarters, group, target, held):
-    if group < 3:
-        target[held, :] = matmul(pick, quarters[group][...]).astype(jnp.bfloat16)
-        return
-    half = target.shape[1] // 2
-    for part in (0, 1):
-        columns = slice(part * half, (part + 1) * half)
-        target[held, columns] = matmul(pick, quarters[3 + part][...]).astype(jnp.bfloat16)
+def pick_rows(pick, quarter, target, held):
+    target[held, :] = matmul(pick, quarter[...]).astype(jnp.bfloat16)
 
 
 def spread_rows(slot_ref, scale_ref, results, targets):
@@ -256,10 +255,10 @@
 
 
 def forward_kernel(*refs):
-    slot_ref, scale_ref, *quarters = refs[:7]
-    hbm_weights = refs[7:10]
-    targets = refs[10:14]
-    rows, hidden, results, gate_ref, up_ref, down_ref, arrived = refs[14:]
+    slot_ref, scale_ref, *quarters = refs[:6]
+    hbm_weights = refs[6:9]
+    targets = refs[9:13]
+    rows, hidden, results, gate_ref, up_ref, down_ref, arrived = refs[13:]
     experts, groups, slots, _ = results.shape
     width = hidden.shape[1]
     chunk = 256
@@ -272,7 +271,7 @@
         copies = weight_copies(hbm_weights, (gate_ref, up_ref, down_ref), arrived, expert)
         for group in range(groups):
             held = slice(group * slots, (group + 1) * slots)
-            pick_rows(selected(slot_ref, group, expert, slots), quarters, group, rows, held)
+            pick_rows(selected(slot_ref, group, expert, slots), quarters[group], rows, held)
         copies[0].wait()
         copies[1].wait()
         for start in range(0, width, chunk):
@@ -290,11 +289,11 @@
 
 
 def backward_kernel(*refs):
-    slot_ref, scale_ref, *quarters = refs[:7]
-    quarter_grads = refs[7:12]
-    hbm_weights = refs[12:15]
-    targets = refs[15:19]
-    rows, grads, gate_grads, value_grads, results, gate_ref, up_ref, down_ref, arrived = refs[19:]
+    slot_ref, scale_ref, *quarters = refs[:6]
+    quarter_grads = refs[6:10]
+    hbm_weights = refs[10:13]
+    targets = refs[13:17]
+    rows, grads, gate_grads, value_grads, results, gate_ref, up_ref, down_ref, arrived = refs[17:]
     experts, groups, slots, _ = results.shape
     width = gate_grads.shape[1]
     chunk = 256
@@ -306,9 +305,9 @@
     def _(expert):
         for group in range(groups):
             held = slice(group * slots, (group + 1) * slots)
-            pick_rows(selected(slot_ref, group, expert, slots), quarters, group, rows, held)
+            pick_rows(selected(slot_ref, group, expert, slots), quarters[group], rows, held)
             weighed = selected(slot_ref, group, expert, slots, scale_ref[group, expert])
-            pick_rows(weighed, quarter_grads, group, grads, held)
+            pick_rows(weighed, quarter_grads[group], grads, held)
         for copy in weight_copies(hbm_weights, (gate_ref, up_ref, down_ref), arrived, expert):
             copy.wait()
         for start in range(0, width, chunk):
@@ -402,54 +401,69 @@
         down_sent = lax.concatenate([down_proj, told.reshape(rows, -1)], 1)
     down_own = gather_depth(down_sent, OWNERS)
     other_tokens = shifted(tokens, OWNERS, CORE)
+    next_tokens = shifted(tokens, OWNERS, X)
     down_parts = gather_chips(down_own, OWNERS, Y, X)
+    next_grads = shifted(out_grad, OWNERS, Y)
     up_own = gather_depth(after(up_proj, down_own), OWNERS)
     other_grads = shifted(after(out_grad, down_own), OWNERS, CORE)
     up_parts = gather_chips(up_own, OWNERS, X, Y)
 
     down_place = placement(rows, Y, X)
     up_place = placement(rows, X, Y)
-    latent, down_near, told_near = projected(tokens, other_tokens, down_parts, down_place)
+    latent, down_near, told_near = projected(
+        after(tokens, next_tokens), other_tokens, down_parts, down_place
+    )
     if not ride:
-        told_near = joined(gather_quarters(told, EXPERT, Y, X))
-    told_far = shifted(told_near, EXPERT, CORE)
+        told_near = lax.concatenate(
+            list(gather_chips(gather_depth(told, EXPERT), EXPERT, Y, X)), 0
+        )
+    latent_own = gather_depth(latent, EXPERT)
+    told_far = shifted(after(told_near, latent), EXPERT, CORE)
     plans, slot_count = expert_plans(
         lax.concatenate([told_near, told_far], 0), local_experts, row_count
     )
-    latent_own = gather_depth(latent, EXPERT)
-    near = gather_chips(latent_own, EXPERT, Y, X)
+    near = (latent_own, shifted(latent_own, EXPERT, Y), shifted(latent_own, EXPERT, X))
+    mix_grad, up_near, _ = projected(
+        after(out_grad, next_grads), other_grads, after(up_parts, latent), up_place
+    )
+    mix_own = gather_depth(after(mix_grad, latent_own), EXPERT)
+    mix_own, near = lax.optimization_barrier((mix_own, near))
+    near = gather_chips_by_turns(near, EXPERT, Y, X)
     far = tuple(shifted(part, EXPERT, CORE) for part in near)
-    mix_grad, up_near, _ = projected(out_grad, other_grads, up_parts, up_place)
-    near_grad = gather_quarters(after(mix_grad, latent_own), EXPERT, Y, X)
-    far_grad = tuple(shifted(part, EXPERT, CORE) for part in near_grad)
+    near_grad = (mix_own, shifted(mix_own, EXPERT, Y), shifted(mix_own, EXPERT, X))
 
     narrow = pltpu.VMEM((4 * slot_count, latent_width), jnp.bfloat16)
     wide = pltpu.VMEM((4 * slot_count, width), jnp.bfloat16)
     weights = (expert_gate, expert_up, expert_down)
     scratch = (narrow, narrow, wide, wide)
     forward_near = expert_call(forward_kernel, 3, (narrow, wide), plans[0], near, weights)
+    near_grad = gather_chips_by_turns(after(near_grad, forward_near), EXPERT, Y, X)
     forward_far = expert_call(
         forward_kernel, 3, (narrow, wide), plans[1], after(far, forward_near), weights
     )
+    far_grad = tuple(shifted(part, EXPERT, CORE) for part in near_grad)
+    forward_sums = core_totals(forward_near, forward_far)
+    far_grad = after(far_grad, forward_sums)
     backward_far = expert_call(
-        backward_kernel, 5, scratch, plans[1], far + after(far_grad, forward_far), weights
-    )
-    forward_sums = core_totals(forward_near, forward_far)
-    near_grad = after(near_grad, backward_far, forward_sums)
+        backward_kernel, 5, scratch, plans[1], far + far_grad, weights
+    )
+    near_grad = after(near_grad, backward_far)
     backward_near = expert_call(
         backward_kernel, 5, scratch, plans[0], near + near_grad, weights
     )
 
-    tokens, out_grad, down_far, up_far = after(
-        (tokens, out_grad, down_near, up_near), forward_far
+    down_far, up_far, last_tokens, last_grads = after(
+        (down_near, up_near, next_tokens, next_grads), forward_far
     )
     down_far = shifted(down_far, OWNERS, CORE)
     up_far = shifted(up_far, OWNERS, CORE)
-    next_tokens, next_grads = shifted(tokens, OWNERS, X), shifted(out_grad, OWNERS, Y)
-    quad_tokens = (tokens, other_tokens, next_tokens, shifted(next_tokens, OWNERS, CORE))
-    quad_grads = (out_grad, other_grads, next_grads, shifted(next_grads, OWNERS, CORE))
-
-    mixed_rows = tensor_total(total_tokens(*forward_sums)).astype(jnp.bfloat16)
+    last_tokens = shifted(last_tokens, OWNERS, CORE)
+    last_grads = shifted(last_grads, OWNERS, CORE)
+    quad_tokens = (tokens, other_tokens, next_tokens, last_tokens)
+    quad_grads = (out_grad, other_grads, next_grads, last_grads)
+
+    mixed_rows = depth_total(chip_totals(*forward_sums), EXPERT)
+    mixed_rows = tensor_total(mixed_rows).astype(jnp.bfloat16)
     mixed_relative = matmul(mixed_rows, up_place, ((1,), (1,))).astype(jnp.bfloat16)
     up_grad = projection_grad(mixed_relative, quad_grads, X, Y)
     half = latent_width // 2
@@ -457,7 +471,8 @@
     layer_out = (layer_out + matmul(mixed_relative[:, half:], up_far)).astype(jnp.bfloat16)
 
     backward_sums = core_totals(backward_near, backward_far)
-    latent_grad = tensor_total(total_tokens(*backward_sums)).astype(jnp.bfloat16)
+    latent_grad = depth_total(chip_totals_by_turns(*backward_sums), EXPERT)
+    latent_grad = tensor_total(latent_grad).astype(jnp.bfloat16)
     grad_relative = matmul(latent_grad, down_place, ((1,), (1,))).astype(jnp.bfloat16)
     down_grad = projection_grad(grad_relative, quad_tokens, Y, X)
     token_grad = matmul(grad_relative[:, :half], down_near)

time: 234 us -> 234 us (level)
  starting transfers between devices: 68.6 us -> 80 us
  local copies, waits for them, and re-layouts: 12.2 us -> 3.42 us
    ppermute x83 -> x80, starting transfers between devices: 68.6 us -> 80 us  [shifted(): return lax.ppermute(block, axes, pairs)]
    unnamed x34 -> x29, local copies, waits for them, and re-layouts: 6.63 us -> 2.01 us
    slice x16 -> x7, local copies, waits for them, and re-layouts: 2.97 us -> 0.18 us  [the longest x2 0.04 us: gather_chips_by_turns(): left = shifted(along_first[:, :half], axes, second)]
    ppermute x83 -> x80, waiting for transfers between devices: 106 us -> 104 us  [shifted(): return lax.ppermute(block, axes, pairs)]
  transfers between devices with their start and end apart: 83 -> 80, of which waited for: 34 -> 37; matrix products, arithmetic and copies ran while one was open for 8% -> 6% of each run, Pallas kernels for 14% -> 14%
where the time goes in v5:
time: 234 us; the launch traced here: 233 us
  waiting for transfers between devices  104 us (44%)
  starting transfers between devices  80 us (34%)
  Pallas kernels  31.8 us (14%)
  other arithmetic  7.39 us (3%)
  matrix products  5.27 us (2%)
  local copies, waits for them, and re-layouts  3.42 us (1%)
    ppermute x80, waiting for transfers between devices, shifted(): return lax.ppermute(block, axes, pairs)  104 us
    ppermute x80, starting transfers between devices, shifted(): return lax.ppermute(block, axes, pairs)  80 us
    pallas_call x4, Pallas kernels, expert_call(): pl.pallas_call(kernel, out_shape=(jax.ShapeDtypeStruct((span, latent_widt...  25.9 us
    pallas_call x4, Pallas kernels, vmem_call(): pl.pallas_call(kernel, out_shape=out_shape, in_specs=[whole] * len(operan...  5.86 us
    dot_general x8, matrix products, matmul(): lax.dot_general(left, right, (contract, ((), ())), preferred_element_type...  5.17 us
  transfers between devices with their start and end apart: 80, of which 37 were waited for; matrix products, arithmetic and copies ran while one was open for 6% of the time, Pallas kernels for 14%

profile of v5, /device:TPU:0, one launch (start us, length us, event | category | flops | bytes accessed | tf_op | source)
XLA Modules:
  0.0 233.2 jit_solution(12813572744737948198)
XLA Ops:
  0.6 3.0 %collective-permute-start = (bf16[128,2048]{1,0:T(8,128)(2,1)}, bf16[128,2048]{1,0:T(8,128)(2,1)S(1)}, u32[]{:S(2)}, u32[]{:S(2)}) collective-permute-start(bf16[128,2048]{1,0:T(8,128)(2,1)} %refs_4_.2), channel_id=1, source_target_pairs={{0,2},{1,3},{2,0},{3,1},{4,6},{5,7},{6,4},{7,5},{8,10},{9,11},{10,... | collective-permute-start | bytes 1572872 | tf_op jit(solution)/shard_map/ppermute | solution.py:40
  5.2 3.6 %collective-permute-start.4 = (bf16[16,2176]{1,0:T(8,128)(2,1)S(1)}, bf16[16,2176]{1,0:T(8,128)(2,1)S(1)}, u32[]{:S(2)}, u32[]{:S(2)}) collective-permute-start(bf16[16,2176]{1,0:T(8,128)(2,1)S(1)} %maximum_maximum_fusion), channel_id=1, source_target_pairs={{0,24},{1,25},{2,26},{3,27},{4,28},{5,29},{6,30},{7,31},{8,0},{9,1... | collective-permute-start | bytes 208904 | tf_op jit(solution)/shard_map/ppermute | solution.py:40
  11.3 5.0 %collective-permute-done.3 = bf16[16,2176]{1,0:T(8,128)(2,1)S(1)} collective-permute-done((bf16[16,2176]{1,0:T(8,128)(2,1)S(1)}, bf16[16,2176]{1,0:T(8,128)(2,1)S(1)}, u32[]{:S(2)}, u32[]{:S(2)}) %collective-permute-start.3) | collective-permute-done | bytes 69664 | tf_op jit(solution)/shard_map/ppermute | solution.py:40
  18.9 2.3 collective-permute-start.13
  22.0 3.3 %collective-permute-done.12 = bf16[16,2048]{1,0:T(8,128)(2,1)S(1)} collective-permute-done((bf16[16,2048]{1,0:T(8,128)(2,1)}, bf16[16,2048]{1,0:T(8,128)(2,1)S(1)}, u32[]{:S(2)}, u32[]{:S(2)}) %collective-permute-start.12) | collective-permute-done | bytes 65568 | tf_op jit(solution)/shard_map/ppermute | solution.py:40
  27.3 1.6 collective-permute-start.10
  30.2 4.7 %collective-permute-done.6.refs_2_ = bf16[64,2176]{1,0:T(8,128)(2,1)S(1)} collective-permute-done((bf16[64,2176]{1,0:T(8,128)(2,1)S(1)}, bf16[64,2176]{1,0:T(8,128)(2,1)S(1)}, u32[]{:S(2)}, u32[]{:S(2)}) %collective-permute-start.6) | collective-permute-done | bytes 278560 | tf_op jit(solution)/shard_map/ppermute | solution.py:40
  34.9 3.3 %collective-permute-done.7.refs_3_ = bf16[64,2176]{1,0:T(8,128)(2,1)S(1)} collective-permute-done((bf16[64,2176]{1,0:T(8,128)(2,1)S(1)}, bf16[64,2176]{1,0:T(8,128)(2,1)S(1)}, u32[]{:S(2)}, u32[]{:S(2)}) %collective-permute-start.7) | collective-permute-done | bytes 278560 | tf_op jit(solution)/shard_map/ppermute | solution.py:40
  44.8 1.9 collective-permute-done.10.refs_6_
  49.9 6.6 %collective-permute-done.16.refs_2_ = bf16[64,2048]{1,0:T(8,128)(2,1)} collective-permute-done((bf16[64,2048]{1,0:T(8,128)(2,1)S(1)}, bf16[64,2048]{1,0:T(8,128)(2,1)}, u32[]{:S(2)}, u32[]{:S(2)}) %collective-permute-start.16) | collective-permute-done | bytes 262176 | tf_op jit(solution)/shard_map/ppermute | solution.py:40
  56.8 1.9 collective-permute-start.19
  58.7 2.4 %shard_map.121 = (bf16[256,2048]{1,0:T(8,128)(2,1)S(1)}, bf16[256,128]{1,0:T(8,128)(2,1)}, bf16[128,256]{1,0:T(8,128)(2,1)S(1)}, bf16[128,256]{1,0:T(8,128)(2,1)S(1)}) custom-call(bf16[128,2048]{1,0:T(8,128)(2,1)S(1)} %copy-done, bf16[128,2048]{1,0:T(8,128)(2,1)S(1)} %collective-permute-done.11.others.refs_5_, ...), custom_call_target="tpu_custom_call" | custom-call | flops 268435456 | bytes 2097152 | tf_op jit(solution)/shard_map/pallas_call | solution.py:134
  61.4 4.2 %collective-permute-done.20 = bf16[128,512]{1,0:T(8,128)(2,1)S(1)} collective-permute-done((bf16[128,512]{1,0:T(8,128)(2,1)}, bf16[128,512]{1,0:T(8,128)(2,1)S(1)}, u32[]{:S(2)}, u32[]{:S(2)}) %collective-permute-start.20) | collective-permute-done | bytes 131104 | tf_op jit(solution)/shard_map/ppermute | solution.py:40
  65.7 2.2 collective-permute-start.25
  67.9 2.0 collective-permute-start.26
  71.2 1.9 collective-permute-start.22
  73.2 3.6 %collective-permute-done.24 = bf16[128,512]{1,0:T(8,128)(2,1)S(1)} collective-permute-done((bf16[128,512]{1,0:T(8,128)(2,1)S(1)}, bf16[128,512]{1,0:T(8,128)(2,1)S(1)}, u32[]{:S(2)}, u32[]{:S(2)}) %collective-permute-start.24) | collective-permute-done | bytes 131104 | tf_op jit(solution)/shard_map/ppermute | solution.py:40
  76.7 5.8 %collective-permute-done.23 = bf16[128,512]{1,0:T(8,128)(2,1)S(1)} collective-permute-done((bf16[128,512]{1,0:T(8,128)(2,1)S(1)}, bf16[128,512]{1,0:T(8,128)(2,1)S(1)}, u32[]{:S(2)}, u32[]{:S(2)}) %collective-permute-start.23) | collective-permute-done | bytes 131104 | tf_op jit(solution)/shard_map/ppermute | solution.py:40
  85.1 5.1 %collective-permute-done.27 = bf16[512,256]{1,0:T(8,128)(2,1)S(1)} collective-permute-done((bf16[512,256]{1,0:T(8,128)(2,1)S(1)}, bf16[512,256]{1,0:T(8,128)(2,1)S(1)}, u32[]{:S(2)}, u32[]{:S(2)}) %collective-permute-start.27) | collective-permute-done | bytes 262176 | tf_op jit(solution)/shard_map/ppermute | solution.py:40
  90.2 2.3 collective-permute-done.28
  94.5 5.3 %shard_map.122 = (bf16[512,512]{1,0:T(8,128)(2,1)S(1)}, bf16[512,512]{1,0:T(8,128)(2,1)S(1)}, bf16[512,512]{1,0:T(8,128)(2,1)S(1)}, bf16[512,512]{1,0:T(8,128)(2,1)S(1)}) custom-call(s32[4,2,1,512]{3,2,1,0:T(1,128)S(1)} %bitcast.64, f32[4,2,1,512]{3,2,1,0:T(1,128)S(1)} %bitcast.60, bf16[512,512]{1,0:T(8,128)(2,1)S(1)} %pad_maximum_fusion.refs_2_, ...), custom_call_target="tpu_custom_call" | custom-call | flops 2415919104 | bytes 8404992 | tf_op jit(solution)/shard_map/pallas_call | solution.py:344
  99.8 5.3 %shard_map.123 = (bf16[512,512]{1,0:T(8,128)(2,1)S(1)}, bf16[512,512]{1,0:T(8,128)(2,1)S(1)}, bf16[512,512]{1,0:T(8,128)(2,1)S(1)}, bf16[512,512]{1,0:T(8,128)(2,1)S(1)}) custom-call(s32[4,2,1,512]{3,2,1,0:T(1,128)S(1)} %bitcast.66, f32[4,2,1,512]{3,2,1,0:T(1,128)S(1)} %bitcast.62, bf16[512,512]{1,0:T(8,128)(2,1)S(1)} %collective-permute-done.29.refs_2_, ...), custom_call_target="tpu_custom_call" | custom-call | flops 2415919104 | bytes 8404992 | tf_op jit(solution)/shard_map/pallas_call | solution.py:344
  105.2 1.8 collective-permute-done.44.refs_7_
  110.6 4.3 %collective-permute-done.46 = bf16[512,256]{1,0:T(8,128)(2,1)S(1)} collective-permute-done((bf16[512,256]{1,0:T(8,128)(2,1)S(1)}, bf16[512,256]{1,0:T(8,128)(2,1)S(1)}, u32[]{:S(2)}, u32[]{:S(2)}) %collective-permute-start.46) | collective-permute-done | bytes 262176 | tf_op jit(solution)/shard_map/ppermute | solution.py:40
  116.9 1.7 collective-permute-done.34
  122.8 7.5 %shard_map.124 = (bf16[512,512]{1,0:T(8,128)(2,1)S(1)}, bf16[512,512]{1,0:T(8,128)(2,1)S(1)}, bf16[512,512]{1,0:T(8,128)(2,1)S(1)}, bf16[512,512]{1,0:T(8,128)(2,1)S(1)}) custom-call(s32[4,2,1,512]{3,2,1,0:T(1,128)S(1)} %bitcast.67, f32[4,2,1,512]{3,2,1,0:T(1,128)S(1)} %bitcast.63, bf16[512,512]{1,0:T(8,128)(2,1)S(1)} %collective-permute-done.29.refs_2_, ...), custom_call_target="tpu_custom_call" | custom-call | flops 4026531840 | bytes 10502144 | tf_op jit(solution)/shard_map/pallas_call | solution.py:344
  130.4 7.8 %shard_map.125 = (bf16[512,512]{1,0:T(8,128)(2,1)S(1)}, bf16[512,512]{1,0:T(8,128)(2,1)S(1)}, bf16[512,512]{1,0:T(8,128)(2,1)S(1)}, bf16[512,512]{1,0:T(8,128)(2,1)S(1)}) custom-call(s32[4,2,1,512]{3,2,1,0:T(1,128)S(1)} %bitcast.65, f32[4,2,1,512]{3,2,1,0:T(1,128)S(1)} %bitcast.61, bf16[512,512]{1,0:T(8,128)(2,1)S(1)} %pad_maximum_fusion.refs_2_, ...), custom_call_target="tpu_custom_call" | custom-call | flops 4026531840 | bytes 10502144 | tf_op jit(solution)/shard_map/pallas_call | solution.py:344
  138.7 5.4 %collective-permute-done.37 = bf16[512,512]{1,0:T(8,128)(2,1)S(1)} collective-permute-done((bf16[512,512]{1,0:T(8,128)(2,1)S(1)}, bf16[512,512]{1,0:T(8,128)(2,1)S(1)}, u32[]{:S(2)}, u32[]{:S(2)}) %collective-permute-start.37) | collective-permute-done | bytes 524320 | tf_op jit(solution)/shard_map/ppermute | solution.py:40
  147.3 2.3 collective-permute-start.41
  149.8 1.8 collective-permute-start.40
  151.8 2.3 collective-permute-done.42
  154.0 1.8 collective-permute-start.58
  155.9 3.4 %collective-permute-done.41 = bf16[128,512]{1,0:T(8,128)(2,1)S(1)} collective-permute-done((bf16[128,512]{1,0:T(8,128)(2,1)S(1)}, bf16[128,512]{1,0:T(8,128)(2,1)S(1)}, u32[]{:S(2)}, u32[]{:S(2)}) %collective-permute-start.41) | collective-permute-done | bytes 131104 | tf_op jit(solution)/shard_map/ppermute | solution.py:40
  164.8 1.8 shard_map.127
  168.9 4.2 %collective-permute-done.55 = bf16[512,256]{1,0:T(8,128)(2,1)S(1)} collective-permute-done((bf16[512,256]{1,0:T(8,128)(2,1)S(1)}, bf16[512,256]{1,0:T(8,128)(2,1)S(1)}, u32[]{:S(2)}, u32[]{:S(2)}) %collective-permute-start.55) | collective-permute-done | bytes 262176 | tf_op jit(solution)/shard_map/ppermute | solution.py:40
  173.2 1.6 collective-permute-start.56
  175.9 2.7 %collective-permute-done.76 = bf16[64,2048]{1,0:T(8,128)(2,1)S(1)} collective-permute-done((bf16[64,2048]{1,0:T(8,128)(2,1)S(1)}, bf16[64,2048]{1,0:T(8,128)(2,1)S(1)}, u32[]{:S(2)}, u32[]{:S(2)}) %collective-permute-start.76) | collective-permute-done | bytes 262176 | tf_op jit(solution)/shard_map/ppermute | solution.py:40
  178.8 9.4 %collective-permute-done.59 = bf16[512,512]{1,0:T(8,128)(2,1)S(1)} collective-permute-done((bf16[512,512]{1,0:T(8,128)(2,1)S(1)}, bf16[512,512]{1,0:T(8,128)(2,1)S(1)}, u32[]{:S(2)}, u32[]{:S(2)}) %collective-permute-start.59) | collective-permute-done | bytes 524320 | tf_op jit(solution)/shard_map/ppermute | solution.py:40
  188.6 3.3 %collective-permute-start.62 = (bf16[128,512]{1,0:T(8,128)(2,1)S(1)}, bf16[128,512]{1,0:T(8,128)(2,1)S(1)}, u32[]{:S(2)}, u32[]{:S(2)}) collective-permute-start(bf16[128,512]{1,0:T(8,128)(2,1)S(1)} %get-tuple-element.133), channel_id=1, source_target_pairs={{0,8},{1,9},{2,10},{3,11},{4,12},{5,13},{6,14},{7,15},{8,16},{9,17... | collective-permute-start | bytes 393224 | tf_op jit(solution)/shard_map/ppermute | solution.py:40
  193.3 2.0 collective-permute-start.60
  195.3 1.9 collective-permute-done.62
  197.1 4.5 %collective-permute-start.79 = (bf16[16,2048]{1,0:T(8,128)(2,1)S(1)}, bf16[16,2048]{1,0:T(8,128)(2,1)S(1)}, u32[]{:S(2)}, u32[]{:S(2)}) collective-permute-start(bf16[16,2048]{1,0:T(8,128)(2,1)S(1)} %get-tuple-element.141), channel_id=1, source_target_pairs={{0,8},{1,9},{2,10},{3,11},{4,12},{5,13},{6,14},{7,15},{8,16},{9,17... | collective-permute-start | bytes 196616 | tf_op jit(solution)/shard_map/ppermute | solution.py:40
  201.9 1.9 collective-permute-start.78
  203.8 4.6 %collective-permute-start.77 = (bf16[16,2048]{1,0:T(8,128)(2,1)S(1)}, bf16[16,2048]{1,0:T(8,128)(2,1)S(1)}, u32[]{:S(2)}, u32[]{:S(2)}) collective-permute-start(bf16[16,2048]{1,0:T(8,128)(2,1)S(1)} %get-tuple-element.140), channel_id=1, source_target_pairs={{0,24},{1,25},{2,26},{3,27},{4,28},{5,29},{6,30},{7,31},{8,0},{9,1... | collective-permute-start | bytes 196616 | tf_op jit(solution)/shard_map/ppermute | solution.py:40
  216.4 6.6 %collective-permute-done.68 = bf16[64,2048]{1,0:T(8,128)(2,1)S(1)} collective-permute-done((bf16[64,2048]{1,0:T(8,128)(2,1)S(1)}, bf16[64,2048]{1,0:T(8,128)(2,1)S(1)}, u32[]{:S(2)}, u32[]{:S(2)}) %collective-permute-start.68) | collective-permute-done | bytes 262176 | tf_op jit(solution)/shard_map/ppermute | solution.py:40
  223.1 2.1 collective-permute-start.71
  225.1 2.9 %collective-permute-start.70 = (bf16[16,2048]{1,0:T(8,128)(2,1)S(1)}, bf16[16,2048]{1,0:T(8,128)(2,1)S(1)}, u32[]{:S(2)}, u32[]{:S(2)}) collective-permute-start(bf16[16,2048]{1,0:T(8,128)(2,1)S(1)} %get-tuple-element.145), channel_id=1, source_target_pairs={{0,16},{1,17},{2,18},{3,19},{4,20},{5,21},{6,22},{7,23},{8,24},{9,... | collective-permute-start | bytes 196616 | tf_op jit(solution)/shard_map/ppermute | solution.py:40
  230.4 1.6 collective-permute-done.70
  (216 shorter events, 63.3 us)
Async XLA Ops:
  0.6 28.3 %collective-permute-start = (bf16[128,2048]{1,0:T(8,128)(2,1)}, bf16[128,2048]{1,0:T(8,128)(2,1)S(1)}, u32[]{:S(2)}, u32[]{:S(2)}) collective-permute-start(bf16[128,2048]{1,0:T(8,128)(2,1)} %refs_4_.2), channel_id=1, source_target_pairs={{0,2},{1,3},{2,0},{3,1},{4,6},{5,7},{6,4},{7,5},{8,10},{9,11},{10,... | collective-permute-start | bytes 1572872 | tf_op jit(solution)/shard_map/ppermute | solution.py:40
  3.6 34.6 %collective-permute-start.1 = (bf16[128,2048]{1,0:T(8,128)(2,1)}, bf16[128,2048]{1,0:T(8,128)(2,1)S(1)}, u32[]{:S(2)}, u32[]{:S(2)}) collective-permute-start(bf16[128,2048]{1,0:T(8,128)(2,1)} %refs_4_.2), channel_id=1, source_target_pairs={{0,1},{1,0},{2,3},{3,2},{4,5},{5,4},{6,7},{7,6},{8,9},{9,8},{10,11... | collective-permute-start | bytes 1572872 | tf_op jit(solution)/shard_map/ppermute | solution.py:40
  17.2 10.1 %collective-permute-start.5 = (bf16[64,2176]{1,0:T(8,128)(2,1)S(1)}, bf16[64,2176]{1,0:T(8,128)(2,1)S(1)}, u32[]{:S(2)}, u32[]{:S(2)}) collective-permute-start(bf16[64,2176]{1,0:T(8,128)(2,1)S(1)} %pad_maximum_fusion.4.refs_0_), channel_id=1, source_target_pairs={{0,4},{1,5},{2,6},{3,7},{4,0},{5,1},{6,2},{7,3},{8,12},{9,13},{10,... | collective-permute-start | bytes 835592 | tf_op jit(solution)/shard_map/ppermute | solution.py:40
  25.3 9.6 %collective-permute-start.6 = (bf16[64,2176]{1,0:T(8,128)(2,1)S(1)}, bf16[64,2176]{1,0:T(8,128)(2,1)S(1)}, u32[]{:S(2)}, u32[]{:S(2)}) collective-permute-start(bf16[64,2176]{1,0:T(8,128)(2,1)S(1)} %pad_maximum_fusion.4.refs_0_), channel_id=1, source_target_pairs={{0,2},{1,3},{2,0},{3,1},{4,6},{5,7},{6,4},{7,5},{8,10},{9,11},{10,... | collective-permute-start | bytes 835592 | tf_op jit(solution)/shard_map/ppermute | solution.py:40
  26.6 11.6 %collective-permute-start.7 = (bf16[64,2176]{1,0:T(8,128)(2,1)S(1)}, bf16[64,2176]{1,0:T(8,128)(2,1)S(1)}, u32[]{:S(2)}, u32[]{:S(2)}) collective-permute-start(bf16[64,2176]{1,0:T(8,128)(2,1)S(1)} %pad_maximum_fusion.4.refs_0_), channel_id=1, source_target_pairs={{0,6},{1,7},{2,4},{3,5},{4,2},{5,3},{6,0},{7,1},{8,14},{9,15},{10,... | collective-permute-start | bytes 835592 | tf_op jit(solution)/shard_map/ppermute | solution.py:40
  27.3 19.4 %collective-permute-start.10 = (bf16[128,2048]{1,0:T(8,128)(2,1)}, bf16[128,2048]{1,0:T(8,128)(2,1)}, u32[]{:S(2)}, u32[]{:S(2)}) collective-permute-start(bf16[128,2048]{1,0:T(8,128)(2,1)} %refs_4_.3), channel_id=1, source_target_pairs={{0,4},{1,5},{2,6},{3,7},{4,0},{5,1},{6,2},{7,3},{8,12},{9,13},{10,... | collective-permute-start | bytes 1572872 | tf_op jit(solution)/shard_map/ppermute | solution.py:40
  28.9 11.3 %collective-permute-start.14 = (bf16[16,2048]{1,0:T(8,128)(2,1)}, bf16[16,2048]{1,0:T(8,128)(2,1)S(1)}, u32[]{:S(2)}, u32[]{:S(2)}) collective-permute-start(bf16[16,2048]{1,0:T(8,128)(2,1)} %param.14), channel_id=1, source_target_pairs={{0,24},{1,25},{2,26},{3,27},{4,28},{5,29},{6,30},{7,31},{8,0},{9,1... | collective-permute-start | bytes 196616 | tf_op jit(solution)/shard_map/ppermute | solution.py:40
  34.9 23.8 %collective-permute-start.11 = (bf16[128,2048]{1,0:T(8,128)(2,1)}, bf16[128,2048]{1,0:T(8,128)(2,1)S(1)}, u32[]{:S(2)}, u32[]{:S(2)}) collective-permute-start(bf16[128,2048]{1,0:T(8,128)(2,1)} %refs_4_.3), channel_id=1, source_target_pairs={{0,1},{1,0},{2,3},{3,2},{4,5},{5,4},{6,7},{7,6},{8,9},{9,8},{10,11... | collective-permute-start | bytes 1572872 | tf_op jit(solution)/shard_map/ppermute | solution.py:40
  40.2 9.3 %collective-permute-start.15 = (bf16[64,2048]{1,0:T(8,128)(2,1)S(1)}, bf16[64,2048]{1,0:T(8,128)(2,1)}, u32[]{:S(2)}, u32[]{:S(2)}) collective-permute-start(bf16[64,2048]{1,0:T(8,128)(2,1)S(1)} %constant_dynamic-update-slice_fusion.refs_0_), channel_id=1, source_target_pairs={{0,2},{1,3},{2,0},{3,1},{4,6},{5,7},{6,4},{7,5},{8,10},{9,11},{10,... | collective-permute-start | bytes 786440 | tf_op jit(solution)/shard_map/ppermute | solution.py:40
  40.8 15.7 %collective-permute-start.16 = (bf16[64,2048]{1,0:T(8,128)(2,1)S(1)}, bf16[64,2048]{1,0:T(8,128)(2,1)}, u32[]{:S(2)}, u32[]{:S(2)}) collective-permute-start(bf16[64,2048]{1,0:T(8,128)(2,1)S(1)} %constant_dynamic-update-slice_fusion.refs_0_), channel_id=1, source_target_pairs={{0,4},{1,5},{2,6},{3,7},{4,0},{5,1},{6,2},{7,3},{8,12},{9,13},{10,... | collective-permute-start | bytes 786440 | tf_op jit(solution)/shard_map/ppermute | solution.py:40
  42.3 14.5 %collective-permute-start.17 = (bf16[64,2048]{1,0:T(8,128)(2,1)S(1)}, bf16[64,2048]{1,0:T(8,128)(2,1)}, u32[]{:S(2)}, u32[]{:S(2)}) collective-permute-start(bf16[64,2048]{1,0:T(8,128)(2,1)S(1)} %constant_dynamic-update-slice_fusion.refs_0_), channel_id=1, source_target_pairs={{0,6},{1,7},{2,4},{3,5},{4,2},{5,3},{6,0},{7,1},{8,14},{9,15},{10,... | collective-permute-start | bytes 786440 | tf_op jit(solution)/shard_map/ppermute | solution.py:40
  46.7 14.4 %collective-permute-start.9 = (bf16[256,128]{1,0:T(8,128)(2,1)S(1)}, bf16[256,128]{1,0:T(8,128)(2,1)S(1)}, u32[]{:S(2)}, u32[]{:S(2)}) collective-permute-start(bf16[256,128]{1,0:T(8,128)(2,1)S(1)} %get-tuple-element.68), channel_id=1, source_target_pairs={{0,1},{1,0},{2,3},{3,2},{4,5},{5,4},{6,7},{7,6},{8,9},{9,8},{10,11... | collective-permute-start | bytes 196616 | tf_op jit(solution)/shard_map/ppermute | solution.py:40
  49.5 12.0 %collective-permute-start.21 = (bf16[128,512]{1,0:T(8,128)(2,1)}, bf16[128,512]{1,0:T(8,128)(2,1)S(1)}, u32[]{:S(2)}, u32[]{:S(2)}) collective-permute-start(bf16[128,512]{1,0:T(8,128)(2,1)} %convolution_convert_fusion.3), channel_id=1, source_target_pairs={{0,24},{1,25},{2,26},{3,27},{4,28},{5,29},{6,30},{7,31},{8,0},{9,1... | collective-permute-start | bytes 393224 | tf_op jit(solution)/shard_map/ppermute | solution.py:40
  56.5 9.1 %collective-permute-start.20 = (bf16[128,512]{1,0:T(8,128)(2,1)}, bf16[128,512]{1,0:T(8,128)(2,1)S(1)}, u32[]{:S(2)}, u32[]{:S(2)}) collective-permute-start(bf16[128,512]{1,0:T(8,128)(2,1)} %convolution_convert_fusion.3), channel_id=1, source_target_pairs={{0,16},{1,17},{2,18},{3,19},{4,20},{5,21},{6,22},{7,23},{8,24},{9,... | collective-permute-start | bytes 393224 | tf_op jit(solution)/shard_map/ppermute | solution.py:40
  56.8 8.8 %collective-permute-start.19 = (bf16[128,512]{1,0:T(8,128)(2,1)}, bf16[128,512]{1,0:T(8,128)(2,1)S(1)}, u32[]{:S(2)}, u32[]{:S(2)}) collective-permute-start(bf16[128,512]{1,0:T(8,128)(2,1)} %convolution_convert_fusion.3), channel_id=1, source_target_pairs={{0,8},{1,9},{2,10},{3,11},{4,12},{5,13},{6,14},{7,15},{8,16},{9,17... | collective-permute-start | bytes 393224 | tf_op jit(solution)/shard_map/ppermute | solution.py:40
  61.2 8.7 %collective-permute-start.18 = (bf16[128,256]{1,0:T(8,128)(2,1)S(1)}, bf16[128,256]{1,0:T(8,128)(2,1)S(1)}, u32[]{:S(2)}, u32[]{:S(2)}) collective-permute-start(bf16[128,256]{1,0:T(8,128)(2,1)S(1)} %get-tuple-element.77), channel_id=1, source_target_pairs={{0,1},{1,0},{2,3},{3,2},{4,5},{5,4},{6,7},{7,6},{8,9},{9,8},{10,11... | collective-permute-start | bytes 196616 | tf_op jit(solution)/shard_map/ppermute | solution.py:40
  65.7 16.9 %collective-permute-start.25 = (bf16[512,512]{1,0:T(8,128)(2,1)S(1)}, bf16[512,512]{1,0:T(8,128)(2,1)S(1)}, u32[]{:S(2)}, u32[]{:S(2)}) collective-permute-start(bf16[512,512]{1,0:T(8,128)(2,1)S(1)} %pad_maximum_fusion.refs_2_), channel_id=1, source_target_pairs={{0,4},{1,5},{2,6},{3,7},{4,0},{5,1},{6,2},{7,3},{8,12},{9,13},{10,... | collective-permute-start | bytes 1572872 | tf_op jit(solution)/shard_map/ppermute | solution.py:40
  67.9 14.7 %collective-permute-start.26 = (bf16[512,512]{1,0:T(8,128)(2,1)S(1)}, bf16[512,512]{1,0:T(8,128)(2,1)S(1)}, u32[]{:S(2)}, u32[]{:S(2)}) collective-permute-start(bf16[512,512]{1,0:T(8,128)(2,1)S(1)} %pad_maximum_fusion.refs_2_), channel_id=1, source_target_pairs={{0,2},{1,3},{2,0},{3,1},{4,6},{5,7},{6,4},{7,5},{8,10},{9,11},{10,... | collective-permute-start | bytes 1572872 | tf_op jit(solution)/shard_map/ppermute | solution.py:40
  70.3 12.2 %collective-permute-start.23 = (bf16[128,512]{1,0:T(8,128)(2,1)S(1)}, bf16[128,512]{1,0:T(8,128)(2,1)S(1)}, u32[]{:S(2)}, u32[]{:S(2)}) collective-permute-start(bf16[128,512]{1,0:T(8,128)(2,1)S(1)} %convolution_convert_fusion.2), channel_id=1, source_target_pairs={{0,16},{1,17},{2,18},{3,19},{4,20},{5,21},{6,22},{7,23},{8,24},{9,... | collective-permute-start | bytes 393224 | tf_op jit(solution)/shard_map/ppermute | solution.py:40
  71.2 11.3 %collective-permute-start.22 = (bf16[128,512]{1,0:T(8,128)(2,1)S(1)}, bf16[128,512]{1,0:T(8,128)(2,1)S(1)}, u32[]{:S(2)}, u32[]{:S(2)}) collective-permute-start(bf16[128,512]{1,0:T(8,128)(2,1)S(1)} %convolution_convert_fusion.2), channel_id=1, source_target_pairs={{0,8},{1,9},{2,10},{3,11},{4,12},{5,13},{6,14},{7,15},{8,16},{9,17... | collective-permute-start | bytes 393224 | tf_op jit(solution)/shard_map/ppermute | solution.py:40
  83.7 9.6 %collective-permute-start.29 = (bf16[512,512]{1,0:T(8,128)(2,1)S(1)}, bf16[512,512]{1,0:T(8,128)(2,1)S(1)}, u32[]{:S(2)}, u32[]{:S(2)}) collective-permute-start(bf16[512,512]{1,0:T(8,128)(2,1)S(1)} %pad_maximum_fusion.refs_2_), channel_id=1, source_target_pairs={{0,1},{1,0},{2,3},{3,2},{4,5},{5,4},{6,7},{7,6},{8,9},{9,8},{10,11... | collective-permute-start | bytes 1572872 | tf_op jit(solution)/shard_map/ppermute | solution.py:40
  83.8 8.8 %collective-permute-start.28 = (bf16[512,256]{1,0:T(8,128)(2,1)S(1)}, bf16[512,256]{1,0:T(8,128)(2,1)S(1)}, u32[]{:S(2)}, u32[]{:S(2)}) collective-permute-start(bf16[512,256]{1,0:T(8,128)(2,1)S(1)} %slice.71), channel_id=1, source_target_pairs={{0,4},{1,5},{2,6},{3,7},{4,0},{5,1},{6,2},{7,3},{8,12},{9,13},{10,... | collective-permute-start | bytes 786440 | tf_op jit(solution)/shard_map/ppermute | solution.py:40
  84.5 15.3 %collective-permute-start.30 = (bf16[512,512]{1,0:T(8,128)(2,1)S(1)}, bf16[512,512]{1,0:T(8,128)(2,1)S(1)}, u32[]{:S(2)}, u32[]{:S(2)}) collective-permute-start(bf16[512,512]{1,0:T(8,128)(2,1)S(1)} %collective-permute-done.25.refs_3_), channel_id=1, source_target_pairs={{0,1},{1,0},{2,3},{3,2},{4,5},{5,4},{6,7},{7,6},{8,9},{9,8},{10,11... | collective-permute-start | bytes 1572872 | tf_op jit(solution)/shard_map/ppermute | solution.py:40
  84.8 15.0 %collective-permute-start.31 = (bf16[512,512]{1,0:T(8,128)(2,1)S(1)}, bf16[512,512]{1,0:T(8,128)(2,1)S(1)}, u32[]{:S(2)}, u32[]{:S(2)}) collective-permute-start(bf16[512,512]{1,0:T(8,128)(2,1)S(1)} %collective-permute-done.26.refs_4_), channel_id=1, source_target_pairs={{0,1},{1,0},{2,3},{3,2},{4,5},{5,4},{6,7},{7,6},{8,9},{9,8},{10,11... | collective-permute-start | bytes 1572872 | tf_op jit(solution)/shard_map/ppermute | solution.py:40
  92.6 14.3 %collective-permute-start.44 = (bf16[512,512]{1,0:T(8,128)(2,1)S(1)}, bf16[512,512]{1,0:T(8,128)(2,1)S(1)}, u32[]{:S(2)}, u32[]{:S(2)}) collective-permute-start(bf16[512,512]{1,0:T(8,128)(2,1)S(1)} %pad_maximum_fusion.1.refs_6_), channel_id=1, source_target_pairs={{0,4},{1,5},{2,6},{3,7},{4,0},{5,1},{6,2},{7,3},{8,12},{9,13},{10,... | collective-permute-start | bytes 1572872 | tf_op jit(solution)/shard_map/ppermute | solution.py:40
  93.2 14.0 %collective-permute-start.45 = (bf16[512,512]{1,0:T(8,128)(2,1)S(1)}, bf16[512,512]{1,0:T(8,128)(2,1)S(1)}, u32[]{:S(2)}, u32[]{:S(2)}) collective-permute-start(bf16[512,512]{1,0:T(8,128)(2,1)S(1)} %pad_maximum_fusion.1.refs_6_), channel_id=1, source_target_pairs={{0,2},{1,3},{2,0},{3,1},{4,6},{5,7},{6,4},{7,5},{8,10},{9,11},{10,... | collective-permute-start | bytes 1572872 | tf_op jit(solution)/shard_map/ppermute | solution.py:40
  105.1 10.8 %collective-permute-start.38 = (bf16[512,512]{1,0:T(8,128)(2,1)S(1)}, bf16[512,512]{1,0:T(8,128)(2,1)S(1)}, u32[]{:S(2)}, u32[]{:S(2)}) collective-permute-start(bf16[512,512]{1,0:T(8,128)(2,1)S(1)} %get-tuple-element.93), channel_id=1, source_target_pairs={{0,1},{1,0},{2,3},{3,2},{4,5},{5,4},{6,7},{7,6},{8,9},{9,8},{10,11... | collective-permute-start | bytes 1572872 | tf_op jit(solution)/shard_map/ppermute | solution.py:40
  110.1 9.2 %collective-permute-start.49 = (bf16[512,512]{1,0:T(8,128)(2,1)S(1)}, bf16[512,512]{1,0:T(8,128)(2,1)S(1)}, u32[]{:S(2)}, u32[]{:S(2)}) collective-permute-start(bf16[512,512]{1,0:T(8,128)(2,1)S(1)} %collective-permute-done.44.refs_7_), channel_id=1, source_target_pairs={{0,1},{1,0},{2,3},{3,2},{4,5},{5,4},{6,7},{7,6},{8,9},{9,8},{10,11... | collective-permute-start | bytes 1572872 | tf_op jit(solution)/shard_map/ppermute | solution.py:40
  118.6 19.5 %collective-permute-start.33 = (bf16[512,512]{1,0:T(8,128)(2,1)S(1)}, bf16[512,512]{1,0:T(8,128)(2,1)S(1)}, u32[]{:S(2)}, u32[]{:S(2)}) collective-permute-start(bf16[512,512]{1,0:T(8,128)(2,1)S(1)} %get-tuple-element.90), channel_id=1, source_target_pairs={{0,1},{1,0},{2,3},{3,2},{4,5},{5,4},{6,7},{7,6},{8,9},{9,8},{10,11... | collective-permute-start | bytes 1572872 | tf_op jit(solution)/shard_map/ppermute | solution.py:40
  118.9 42.4 %collective-permute-start.43 = (bf16[256,2048]{1,0:T(8,128)(2,1)S(1)}, bf16[256,2048]{1,0:T(8,128)(2,1)S(1)}, u32[]{:S(2)}, u32[]{:S(2)}) collective-permute-start(bf16[256,2048]{1,0:T(8,128)(2,1)S(1)} %get-tuple-element.96), channel_id=1, source_target_pairs={{0,1},{1,0},{2,3},{3,2},{4,5},{5,4},{6,7},{7,6},{8,9},{9,8},{10,11... | collective-permute-start | bytes 3145736 | tf_op jit(solution)/shard_map/ppermute | solution.py:40
  119.3 18.9 %collective-permute-start.39 = (bf16[512,512]{1,0:T(8,128)(2,1)S(1)}, bf16[512,512]{1,0:T(8,128)(2,1)S(1)}, u32[]{:S(2)}, u32[]{:S(2)}) collective-permute-start(bf16[512,512]{1,0:T(8,128)(2,1)S(1)} %fusion.44), channel_id=1, source_target_pairs={{0,2},{1,3},{2,0},{3,1},{4,6},{5,7},{6,4},{7,5},{8,10},{9,11},{10,... | collective-permute-start | bytes 1572872 | tf_op jit(solution)/shard_map/ppermute | solution.py:40
  120.3 23.9 %collective-permute-start.37 = (bf16[512,512]{1,0:T(8,128)(2,1)S(1)}, bf16[512,512]{1,0:T(8,128)(2,1)S(1)}, u32[]{:S(2)}, u32[]{:S(2)}) collective-permute-start(bf16[512,512]{1,0:T(8,128)(2,1)S(1)} %fusion.43), channel_id=1, source_target_pairs={{0,4},{1,5},{2,6},{3,7},{4,0},{5,1},{6,2},{7,3},{8,12},{9,13},{10,... | collective-permute-start | bytes 1572872 | tf_op jit(solution)/shard_map/ppermute | solution.py:40
  121.7 23.7 %collective-permute-start.35 = (bf16[512,512]{1,0:T(8,128)(2,1)S(1)}, bf16[512,512]{1,0:T(8,128)(2,1)S(1)}, u32[]{:S(2)}, u32[]{:S(2)}) collective-permute-start(bf16[512,512]{1,0:T(8,128)(2,1)S(1)} %fusion.42), channel_id=1, source_target_pairs={{0,6},{1,7},{2,4},{3,5},{4,2},{5,3},{6,0},{7,1},{8,14},{9,15},{10,... | collective-permute-start | bytes 1572872 | tf_op jit(solution)/shard_map/ppermute | solution.py:40
  138.1 23.9 %collective-permute-start.75 = (bf16[128,2048]{1,0:T(8,128)(2,1)}, bf16[128,2048]{1,0:T(8,128)(2,1)S(1)}, u32[]{:S(2)}, u32[]{:S(2)}) collective-permute-start(bf16[128,2048]{1,0:T(8,128)(2,1)} %collective-permute-done.10.refs_6_), channel_id=1, source_target_pairs={{0,1},{1,0},{2,3},{3,2},{4,5},{5,4},{6,7},{7,6},{8,9},{9,8},{10,11... | collective-permute-start | bytes 1572872 | tf_op jit(solution)/shard_map/ppermute | solution.py:40
  147.3 12.0 %collective-permute-start.41 = (bf16[128,512]{1,0:T(8,128)(2,1)S(1)}, bf16[128,512]{1,0:T(8,128)(2,1)S(1)}, u32[]{:S(2)}, u32[]{:S(2)}) collective-permute-start(bf16[128,512]{1,0:T(8,128)(2,1)S(1)} %get-tuple-element.139), channel_id=1, source_target_pairs={{0,16},{1,17},{2,18},{3,19},{4,20},{5,21},{6,22},{7,23},{8,24},{9,... | collective-permute-start | bytes 393224 | tf_op jit(solution)/shard_map/ppermute | solution.py:40
  149.8 9.4 %collective-permute-start.40 = (bf16[128,512]{1,0:T(8,128)(2,1)S(1)}, bf16[128,512]{1,0:T(8,128)(2,1)S(1)}, u32[]{:S(2)}, u32[]{:S(2)}) collective-permute-start(bf16[128,512]{1,0:T(8,128)(2,1)S(1)} %get-tuple-element.137), channel_id=1, source_target_pairs={{0,24},{1,25},{2,26},{3,27},{4,28},{5,29},{6,30},{7,31},{8,0},{9,1... | collective-permute-start | bytes 393224 | tf_op jit(solution)/shard_map/ppermute | solution.py:40
  154.0 13.7 %collective-permute-start.58 = (bf16[512,256]{1,0:T(8,128)(2,1)S(1)}, bf16[512,256]{1,0:T(8,128)(2,1)S(1)}, u32[]{:S(2)}, u32[]{:S(2)}) collective-permute-start(bf16[512,256]{1,0:T(8,128)(2,1)S(1)} %get-tuple-element.136), channel_id=1, source_target_pairs={{0,4},{1,5},{2,6},{3,7},{4,0},{5,1},{6,2},{7,3},{8,12},{9,13},{10,... | collective-permute-start | bytes 786440 | tf_op jit(solution)/shard_map/ppermute | solution.py:40
  162.0 54.1 %collective-permute-start.63 = (bf16[256,2048]{1,0:T(8,128)(2,1)S(1)}, bf16[256,2048]{1,0:T(8,128)(2,1)S(1)}, u32[]{:S(2)}, u32[]{:S(2)}) collective-permute-start(bf16[256,2048]{1,0:T(8,128)(2,1)S(1)} %get-tuple-element.117), channel_id=1, source_target_pairs={{0,1},{1,0},{2,3},{3,2},{4,5},{5,4},{6,7},{7,6},{8,9},{9,8},{10,11... | collective-permute-start | bytes 3145736 | tf_op jit(solution)/shard_map/ppermute | solution.py:40
  162.4 16.3 %collective-permute-start.52 = (bf16[512,512]{1,0:T(8,128)(2,1)S(1)}, bf16[512,512]{1,0:T(8,128)(2,1)S(1)}, u32[]{:S(2)}, u32[]{:S(2)}) collective-permute-start(bf16[512,512]{1,0:T(8,128)(2,1)S(1)} %get-tuple-element.105), channel_id=1, source_target_pairs={{0,1},{1,0},{2,3},{3,2},{4,5},{5,4},{6,7},{7,6},{8,9},{9,8},{10,11... | collective-permute-start | bytes 1572872 | tf_op jit(solution)/shard_map/ppermute | solution.py:40
  163.8 9.2 %collective-permute-start.55 = (bf16[512,256]{1,0:T(8,128)(2,1)S(1)}, bf16[512,256]{1,0:T(8,128)(2,1)S(1)}, u32[]{:S(2)}, u32[]{:S(2)}) collective-permute-start(bf16[512,256]{1,0:T(8,128)(2,1)S(1)} %get-tuple-element.135), channel_id=1, source_target_pairs={{0,2},{1,3},{2,0},{3,1},{4,6},{5,7},{6,4},{7,5},{8,10},{9,11},{10,... | collective-permute-start | bytes 786440 | tf_op jit(solution)/shard_map/ppermute | solution.py:40
  166.6 12.1 %collective-permute-start.76 = (bf16[64,2048]{1,0:T(8,128)(2,1)S(1)}, bf16[64,2048]{1,0:T(8,128)(2,1)S(1)}, u32[]{:S(2)}, u32[]{:S(2)}) collective-permute-start(bf16[64,2048]{1,0:T(8,128)(2,1)S(1)} %get-tuple-element.123), channel_id=1, source_target_pairs={{0,2},{1,3},{2,0},{3,1},{4,6},{5,7},{6,4},{7,5},{8,10},{9,11},{10,... | collective-permute-start | bytes 786440 | tf_op jit(solution)/shard_map/ppermute | solution.py:40
  167.9 20.3 %collective-permute-start.59 = (bf16[512,512]{1,0:T(8,128)(2,1)S(1)}, bf16[512,512]{1,0:T(8,128)(2,1)S(1)}, u32[]{:S(2)}, u32[]{:S(2)}) collective-permute-start(bf16[512,512]{1,0:T(8,128)(2,1)S(1)} %pad_maximum_fusion.3), channel_id=1, source_target_pairs={{0,2},{1,3},{2,0},{3,1},{4,6},{5,7},{6,4},{7,5},{8,10},{9,11},{10,... | collective-permute-start | bytes 1572872 | tf_op jit(solution)/shard_map/ppermute | solution.py:40
  173.2 15.0 %collective-permute-start.56 = (bf16[512,512]{1,0:T(8,128)(2,1)S(1)}, bf16[512,512]{1,0:T(8,128)(2,1)S(1)}, u32[]{:S(2)}, u32[]{:S(2)}) collective-permute-start(bf16[512,512]{1,0:T(8,128)(2,1)S(1)} %pad_maximum_fusion.2), channel_id=1, source_target_pairs={{0,4},{1,5},{2,6},{3,7},{4,0},{5,1},{6,2},{7,3},{8,12},{9,13},{10,... | collective-permute-start | bytes 1572872 | tf_op jit(solution)/shard_map/ppermute | solution.py:40
  178.7 33.2 %collective-permute-start.67 = (bf16[128,2048]{1,0:T(8,128)(2,1)S(1)}, bf16[128,2048]{1,0:T(8,128)(2,1)S(1)}, u32[]{:S(2)}, u32[]{:S(2)}) collective-permute-start(bf16[128,2048]{1,0:T(8,128)(2,1)S(1)} %collective-permute-done.refs_6_), channel_id=1, source_target_pairs={{0,1},{1,0},{2,3},{3,2},{4,5},{5,4},{6,7},{7,6},{8,9},{9,8},{10,11... | collective-permute-start | bytes 1572872 | tf_op jit(solution)/shard_map/ppermute | solution.py:40
  188.6 8.6 %collective-permute-start.62 = (bf16[128,512]{1,0:T(8,128)(2,1)S(1)}, bf16[128,512]{1,0:T(8,128)(2,1)S(1)}, u32[]{:S(2)}, u32[]{:S(2)}) collective-permute-start(bf16[128,512]{1,0:T(8,128)(2,1)S(1)} %get-tuple-element.133), channel_id=1, source_target_pairs={{0,8},{1,9},{2,10},{3,11},{4,12},{5,13},{6,14},{7,15},{8,16},{9,17... | collective-permute-start | bytes 393224 | tf_op jit(solution)/shard_map/ppermute | solution.py:40
  191.9 10.0 %collective-permute-start.61 = (bf16[128,512]{1,0:T(8,128)(2,1)S(1)}, bf16[128,512]{1,0:T(8,128)(2,1)S(1)}, u32[]{:S(2)}, u32[]{:S(2)}) collective-permute-start(bf16[128,512]{1,0:T(8,128)(2,1)S(1)} %get-tuple-element.134), channel_id=1, source_target_pairs={{0,16},{1,17},{2,18},{3,19},{4,20},{5,21},{6,22},{7,23},{8,24},{9,... | collective-permute-start | bytes 393224 | tf_op jit(solution)/shard_map/ppermute | solution.py:40
  193.3 10.5 %collective-permute-start.60 = (bf16[128,512]{1,0:T(8,128)(2,1)S(1)}, bf16[128,512]{1,0:T(8,128)(2,1)S(1)}, u32[]{:S(2)}, u32[]{:S(2)}) collective-permute-start(bf16[128,512]{1,0:T(8,128)(2,1)S(1)} %get-tuple-element.132), channel_id=1, source_target_pairs={{0,24},{1,25},{2,26},{3,27},{4,28},{5,29},{6,30},{7,31},{8,0},{9,1... | collective-permute-start | bytes 393224 | tf_op jit(solution)/shard_map/ppermute | solution.py:40
  197.1 11.8 %collective-permute-start.79 = (bf16[16,2048]{1,0:T(8,128)(2,1)S(1)}, bf16[16,2048]{1,0:T(8,128)(2,1)S(1)}, u32[]{:S(2)}, u32[]{:S(2)}) collective-permute-start(bf16[16,2048]{1,0:T(8,128)(2,1)S(1)} %get-tuple-element.141), channel_id=1, source_target_pairs={{0,8},{1,9},{2,10},{3,11},{4,12},{5,13},{6,14},{7,15},{8,16},{9,17... | collective-permute-start | bytes 196616 | tf_op jit(solution)/shard_map/ppermute | solution.py:40
  (44 other events, 470.7 us)

commit v6 on v5

--- a/solution.py
+++ b/solution.py
@@ -111,11 +111,15 @@
     return total + along_y.astype(jnp.float32) + along_x.astype(jnp.float32)
 
 
-def chip_totals_by_turns(across, along_y, along_x, own):
+def across_by_turns(across):
     across = across.astype(jnp.bfloat16)
     half = across.shape[1] // 2
-    left = shifted(across[:, :half], EXPERT, X).astype(jnp.float32)
-    right = shifted(across[:, half:], EXPERT, Y).astype(jnp.float32)
+    return shifted(across[:, :half], EXPERT, X), shifted(across[:, half:], EXPERT, Y)
+
+
+def chip_totals_by_turns(left, right, along_y, along_x, own):
+    half = left.shape[1]
+    left, right = left.astype(jnp.float32), right.astype(jnp.float32)
     along_y = lax.concatenate([along_y[:, :half] + left, along_y[:, half:]], 1)
     along_x = lax.concatenate([along_x[:, :half], along_x[:, half:] + right], 1)
     own = own + shifted(along_y.astype(jnp.bfloat16), EXPERT, Y).astype(jnp.float32)
@@ -193,24 +197,24 @@
         target[...] = total.astype(target.dtype)
 
 
-def projection_grad(relative, quad_inputs, first, second):
+def quad_columns(relative, second):
     mine, along_second, along_core, across = jnp.split(relative, 4, axis=1)
-    quad = (
+    return (
         mine,
         shifted(along_core, OWNERS, CORE),
         shifted(along_second, OWNERS, second),
         shifted(across, OWNERS, second, CORE),
     )
-    half = mine.shape[1] // 2
-    shape = (half, quad_inputs[0].shape[1])
-    sent, kept = vmem_call(
+
+
+def quad_grads_of(quad, quad_inputs):
+    shape = (quad[0].shape[1] // 2, quad_inputs[0].shape[1])
+    return vmem_call(
         grad_kernel,
         (jax.ShapeDtypeStruct(shape, jnp.bfloat16), jax.ShapeDtypeStruct(shape, jnp.float32)),
         quad + tuple(quad_inputs),
-        4 * mine.size * shape[1],
-    )
-    kept = kept + shifted(sent, OWNERS, first).astype(jnp.float32)
-    return depth_total(kept, OWNERS)
+        4 * quad[0].size * shape[1],
+    )
 
 
 def matmul(left, right, contract=((1,), (0,))):
@@ -384,8 +388,8 @@
     return [(slots[core], scales[core]) for core in (0, 1)], depth * capacity
 
 
-def after(value, *earlier):
-    return lax.optimization_barrier((value, earlier))[0]
+def tied(*values):
+    return lax.optimization_barrier(values)
 
 
 def local(
@@ -399,36 +403,43 @@
     down_sent = down_proj
     if ride:
         down_sent = lax.concatenate([down_proj, told.reshape(rows, -1)], 1)
-    down_own = gather_depth(down_sent, OWNERS)
-    other_tokens = shifted(tokens, OWNERS, CORE)
-    next_tokens = shifted(tokens, OWNERS, X)
+    next_tokens, next_grads = shifted(tokens, OWNERS, X), shifted(out_grad, OWNERS, Y)
+    down_own, later_tokens, later_up = tied(
+        gather_depth(down_sent, OWNERS), tokens, up_proj
+    )
     down_parts = gather_chips(down_own, OWNERS, Y, X)
-    next_grads = shifted(out_grad, OWNERS, Y)
-    up_own = gather_depth(after(up_proj, down_own), OWNERS)
-    other_grads = shifted(after(out_grad, down_own), OWNERS, CORE)
-    up_parts = gather_chips(up_own, OWNERS, X, Y)
+    other_tokens = shifted(later_tokens, OWNERS, CORE)
+    up_own = gather_depth(later_up, OWNERS)
+    down_parts, next_tokens, next_grads = tied(down_parts, next_tokens, next_grads)
 
     down_place = placement(rows, Y, X)
     up_place = placement(rows, X, Y)
-    latent, down_near, told_near = projected(
-        after(tokens, next_tokens), other_tokens, down_parts, down_place
-    )
+    latent, down_near, told_near = projected(tokens, other_tokens, down_parts, down_place)
     if not ride:
         told_near = lax.concatenate(
             list(gather_chips(gather_depth(told, EXPERT), EXPERT, Y, X)), 0
         )
+    latent, up_own, later_grads, next_tokens, next_grads = tied(
+        latent, up_own, out_grad, next_tokens, next_grads
+    )
     latent_own = gather_depth(latent, EXPERT)
-    told_far = shifted(after(told_near, latent), EXPERT, CORE)
+    up_parts = gather_chips(up_own, OWNERS, X, Y)
+    other_grads = shifted(later_grads, OWNERS, CORE)
+    last_tokens = shifted(next_tokens, OWNERS, CORE)
+    last_grads = shifted(next_grads, OWNERS, CORE)
+    latent_own, told_near = tied(latent_own, told_near)
+    near = (latent_own, shifted(latent_own, EXPERT, Y), shifted(latent_own, EXPERT, X))
+    up_parts, latent_own, last_tokens, last_grads = tied(
+        up_parts, latent_own, last_tokens, last_grads
+    )
+    near = (latent_own,) + near[1:]
+    mix_grad, up_near, _ = projected(out_grad, other_grads, up_parts, up_place)
+    mix_own = gather_depth(mix_grad, EXPERT)
+    told_far = shifted(told_near, EXPERT, CORE)
     plans, slot_count = expert_plans(
         lax.concatenate([told_near, told_far], 0), local_experts, row_count
     )
-    near = (latent_own, shifted(latent_own, EXPERT, Y), shifted(latent_own, EXPERT, X))
-    mix_grad, up_near, _ = projected(
-        after(out_grad, next_grads), other_grads, after(up_parts, latent), up_place
-    )
-    mix_own = gather_depth(after(mix_grad, latent_own), EXPERT)
-    mix_own, near = lax.optimization_barrier((mix_own, near))
-    near = gather_chips_by_turns(near, EXPERT, Y, X)
+    mix_own, near = tied(mix_own, gather_chips_by_turns(near, EXPERT, Y, X))
     far = tuple(shifted(part, EXPERT, CORE) for part in near)
     near_grad = (mix_own, shifted(mix_own, EXPERT, Y), shifted(mix_own, EXPERT, X))
 
@@ -437,46 +448,50 @@
     weights = (expert_gate, expert_up, expert_down)
     scratch = (narrow, narrow, wide, wide)
     forward_near = expert_call(forward_kernel, 3, (narrow, wide), plans[0], near, weights)
-    near_grad = gather_chips_by_turns(after(near_grad, forward_near), EXPERT, Y, X)
-    forward_far = expert_call(
-        forward_kernel, 3, (narrow, wide), plans[1], after(far, forward_near), weights
-    )
+    forward_near, far, down_near, up_near = tied(forward_near, far, down_near, up_near)
+    near_grad = gather_chips_by_turns(near_grad, EXPERT, Y, X)
+    forward_far = expert_call(forward_kernel, 3, (narrow, wide), plans[1], far, weights)
     far_grad = tuple(shifted(part, EXPERT, CORE) for part in near_grad)
-    forward_sums = core_totals(forward_near, forward_far)
-    far_grad = after(far_grad, forward_sums)
+    down_far = shifted(down_near, OWNERS, CORE)
+    up_far = shifted(up_near, OWNERS, CORE)
+    across, along_y, along_x, own = core_totals(forward_near, forward_far)
+    forward_sums = [part.astype(jnp.bfloat16) for part in (across, along_y, along_x)] + [own]
+    far_grad, forward_sums = tied(far_grad, forward_sums)
     backward_far = expert_call(
-        backward_kernel, 5, scratch, plans[1], far + far_grad, weights
-    )
-    near_grad = after(near_grad, backward_far)
+        backward_kernel, 5, scratch, plans[1], far + tuple(far_grad), weights
+    )
+    near_grad, backward_far, down_far, up_far = tied(near_grad, backward_far, down_far, up_far)
     backward_near = expert_call(
-        backward_kernel, 5, scratch, plans[0], near + near_grad, weights
-    )
-
-    down_far, up_far, last_tokens, last_grads = after(
-        (down_near, up_near, next_tokens, next_grads), forward_far
-    )
-    down_far = shifted(down_far, OWNERS, CORE)
-    up_far = shifted(up_far, OWNERS, CORE)
-    last_tokens = shifted(last_tokens, OWNERS, CORE)
-    last_grads = shifted(last_grads, OWNERS, CORE)
+        backward_kernel, 5, scratch, plans[0], near + tuple(near_grad), weights
+    )
     quad_tokens = (tokens, other_tokens, next_tokens, last_tokens)
     quad_grads = (out_grad, other_grads, next_grads, last_grads)
 
-    mixed_rows = depth_total(chip_totals(*forward_sums), EXPERT)
-    mixed_rows = tensor_total(mixed_rows).astype(jnp.bfloat16)
+    mixed_sums = chip_totals(*forward_sums)
+    backward_across, *backward_sums = core_totals(backward_near, backward_far)
+    backward_across = across_by_turns(backward_across)
+    mixed_sums, backward_sums = tied(mixed_sums, backward_sums)
+    mixed_rows = tensor_total(depth_total(mixed_sums, EXPERT)).astype(jnp.bfloat16)
     mixed_relative = matmul(mixed_rows, up_place, ((1,), (1,))).astype(jnp.bfloat16)
-    up_grad = projection_grad(mixed_relative, quad_grads, X, Y)
+    mixed_relative, backward_across = tied(mixed_relative, backward_across)
+    latent_sums = chip_totals_by_turns(*backward_across, *backward_sums)
+    quad = quad_columns(mixed_relative, Y)
+    quad, latent_sums = tied(quad, latent_sums)
+    latent_grad = tensor_total(depth_total(latent_sums, EXPERT)).astype(jnp.bfloat16)
+    up_sent, up_kept = quad_grads_of(quad, quad_grads)
+    up_sums = up_kept + shifted(up_sent, OWNERS, X).astype(jnp.float32)
+    grad_relative = matmul(latent_grad, down_place, ((1,), (1,))).astype(jnp.bfloat16)
+    up_sums, mixed_relative, grad_relative = tied(up_sums, mixed_relative, grad_relative)
+    quad = quad_columns(grad_relative, X)
+    up_grad = depth_total(up_sums, OWNERS)
+    down_sent, down_kept = quad_grads_of(quad, quad_tokens)
+    down_sums = down_kept + shifted(down_sent, OWNERS, Y).astype(jnp.float32)
     half = latent_width // 2
     layer_out = matmul(mixed_relative[:, :half], up_near)
     layer_out = (layer_out + matmul(mixed_relative[:, half:], up_far)).astype(jnp.bfloat16)
-
-    backward_sums = core_totals(backward_near, backward_far)
-    latent_grad = depth_total(chip_totals_by_turns(*backward_sums), EXPERT)
-    latent_grad = tensor_total(latent_grad).astype(jnp.bfloat16)
-    grad_relative = matmul(latent_grad, down_place, ((1,), (1,))).astype(jnp.bfloat16)
-    down_grad = projection_grad(grad_relative, quad_tokens, Y, X)
     token_grad = matmul(grad_relative[:, :half], down_near)
     token_grad = (token_grad + matmul(grad_relative[:, half:], down_far)).astype(jnp.bfloat16)
+    down_grad = depth_total(down_sums, OWNERS)
     return (layer_out, token_grad, down_grad, up_grad)
 
 

time: 234 us -> 236 us (level)
  starting transfers between devices: 80 us -> 73.4 us
  waiting for transfers between devices: 104 us -> 109 us
  other arithmetic: 7.39 us -> 10.2 us
    ppermute x80, starting transfers between devices: 80 us -> 73.4 us  [shifted(): return lax.ppermute(block, axes, pairs)]
    ppermute x80, waiting for transfers between devices: 104 us -> 109 us  [shifted(): return lax.ppermute(block, axes, pairs)]
    concatenate x3 -> x4, other arithmetic: 0.93 us -> 3.75 us  [gather_depth(): lax.concatenate([rows] + [shifted(rows, axes, Z, step=step) for step in r...]
  transfers between devices with their start and end apart: 80 -> 80, of which waited for: 37 -> 34; matrix products, arithmetic and copies ran while one was open for 6% -> 5% of each run, Pallas kernels for 14% -> 14%
where the time goes in v6:
time: 236 us; the launch traced here: 235 us
  waiting for transfers between devices  109 us (46%)
  starting transfers between devices  73.4 us (31%)
  Pallas kernels  32.9 us (14%)
  other arithmetic  10.2 us (4%)
  matrix products  5.27 us (2%)
  local copies, waits for them, and re-layouts  3.54 us (2%)
    ppermute x80, waiting for transfers between devices, shifted(): return lax.ppermute(block, axes, pairs)  109 us
    ppermute x80, starting transfers between devices, shifted(): return lax.ppermute(block, axes, pairs)  73.4 us
    pallas_call x4, Pallas kernels, expert_call(): pl.pallas_call(kernel, out_shape=(jax.ShapeDtypeStruct((span, latent_widt...  25.9 us
    pallas_call x4, Pallas kernels, vmem_call(): pl.pallas_call(kernel, out_shape=out_shape, in_specs=[whole] * len(operan...  7.05 us
    dot_general x8, matrix products, matmul(): lax.dot_general(left, right, (contract, ((), ())), preferred_element_type...  5.17 us
  transfers between devices with their start and end apart: 80, of which 34 were waited for; matrix products, arithmetic and copies ran while one was open for 5% of the time, Pallas kernels for 14%

profile of v6, /device:TPU:0, one launch (start us, length us, event | category | flops | bytes accessed | tf_op | source)
XLA Modules:
  0.0 235.4 jit_solution(15172079997944971766)
XLA Ops:
  2.2 3.0 %collective-permute-start = (bf16[16,2176]{1,0:T(8,128)(2,1)S(1)}, bf16[16,2176]{1,0:T(8,128)(2,1)S(1)}, u32[]{:S(2)}, u32[]{:S(2)}) collective-permute-start(bf16[16,2176]{1,0:T(8,128)(2,1)S(1)} %maximum_maximum_fusion), channel_id=1, source_target_pairs={{0,8},{1,9},{2,10},{3,11},{4,12},{5,13},{6,14},{7,15},{8,16},{9,17... | collective-permute-start | bytes 208904 | tf_op jit(solution)/shard_map/ppermute | solution.py:40
  5.2 2.6 %collective-permute-start.1 = (bf16[16,2176]{1,0:T(8,128)(2,1)S(1)}, bf16[16,2176]{1,0:T(8,128)(2,1)S(1)}, u32[]{:S(2)}, u32[]{:S(2)}) collective-permute-start(bf16[16,2176]{1,0:T(8,128)(2,1)S(1)} %maximum_maximum_fusion), channel_id=1, source_target_pairs={{0,16},{1,17},{2,18},{3,19},{4,20},{5,21},{6,22},{7,23},{8,24},{9,... | collective-permute-start | bytes 208904 | tf_op jit(solution)/shard_map/ppermute | solution.py:40
  7.8 1.3 collective-permute-start.2
  9.8 2.7 %collective-permute-done.1 = bf16[16,2176]{1,0:T(8,128)(2,1)S(1)} collective-permute-done((bf16[16,2176]{1,0:T(8,128)(2,1)S(1)}, bf16[16,2176]{1,0:T(8,128)(2,1)S(1)}, u32[]{:S(2)}, u32[]{:S(2)}) %collective-permute-start.1) | collective-permute-done | bytes 69664 | tf_op jit(solution)/shard_map/ppermute | solution.py:40
  13.6 1.6 collective-permute-start.4
  15.2 1.5 collective-permute-start.7
  17.9 2.5 %collective-permute-start.6 = (bf16[64,2176]{1,0:T(8,128)(2,1)S(1)}, bf16[64,2176]{1,0:T(8,128)(2,1)S(1)}, u32[]{:S(2)}, u32[]{:S(2)}) collective-permute-start(bf16[64,2176]{1,0:T(8,128)(2,1)S(1)} %pad_maximum_fusion.5.refs_0_), channel_id=1, source_target_pairs={{0,6},{1,7},{2,4},{3,5},{4,2},{5,3},{6,0},{7,1},{8,14},{9,15},{10,... | collective-permute-start | bytes 835592 | tf_op jit(solution)/shard_map/ppermute | solution.py:40
  20.4 2.8 %collective-permute-done.4.refs_1_ = bf16[64,2176]{1,0:T(8,128)(2,1)S(1)} collective-permute-done((bf16[64,2176]{1,0:T(8,128)(2,1)S(1)}, bf16[64,2176]{1,0:T(8,128)(2,1)S(1)}, u32[]{:S(2)}, u32[]{:S(2)}) %collective-permute-start.4) | collective-permute-done | bytes 278560 | tf_op jit(solution)/shard_map/ppermute | solution.py:40
  23.4 12.8 %collective-permute-done.5.refs_2_ = bf16[64,2176]{1,0:T(8,128)(2,1)S(1)} collective-permute-done((bf16[64,2176]{1,0:T(8,128)(2,1)S(1)}, bf16[64,2176]{1,0:T(8,128)(2,1)S(1)}, u32[]{:S(2)}, u32[]{:S(2)}) %collective-permute-start.5) | collective-permute-done | bytes 278560 | tf_op jit(solution)/shard_map/ppermute | solution.py:40
  36.2 1.7 collective-permute-start.10
  38.0 2.6 %collective-permute-done.6.refs_3_ = bf16[64,2176]{1,0:T(8,128)(2,1)S(1)} collective-permute-done((bf16[64,2176]{1,0:T(8,128)(2,1)S(1)}, bf16[64,2176]{1,0:T(8,128)(2,1)S(1)}, u32[]{:S(2)}, u32[]{:S(2)}) %collective-permute-start.6) | collective-permute-done | bytes 278560 | tf_op jit(solution)/shard_map/ppermute | solution.py:40
  42.3 3.4 %collective-permute-start.12 = (bf16[16,2048]{1,0:T(8,128)(2,1)}, bf16[16,2048]{1,0:T(8,128)(2,1)}, u32[]{:S(2)}, u32[]{:S(2)}) collective-permute-start(bf16[16,2048]{1,0:T(8,128)(2,1)} %param.14), channel_id=1, source_target_pairs={{0,24},{1,25},{2,26},{3,27},{4,28},{5,29},{6,30},{7,31},{8,0},{9,1... | collective-permute-start | bytes 196616 | tf_op jit(solution)/shard_map/ppermute | solution.py:40
  50.9 3.6 %collective-permute-start.18 = (bf16[128,512]{1,0:T(8,128)(2,1)}, bf16[128,512]{1,0:T(8,128)(2,1)}, u32[]{:S(2)}, u32[]{:S(2)}) collective-permute-start(bf16[128,512]{1,0:T(8,128)(2,1)} %convolution_convert_fusion.3), channel_id=1, source_target_pairs={{0,16},{1,17},{2,18},{3,19},{4,20},{5,21},{6,22},{7,23},{8,24},{9,... | collective-permute-start | bytes 393224 | tf_op jit(solution)/shard_map/ppermute | solution.py:40
  56.1 3.4 %collective-permute-done.17 = bf16[128,512]{1,0:T(8,128)(2,1)} collective-permute-done((bf16[128,512]{1,0:T(8,128)(2,1)}, bf16[128,512]{1,0:T(8,128)(2,1)}, u32[]{:S(2)}, u32[]{:S(2)}) %collective-permute-start.17) | collective-permute-done | bytes 131104 | tf_op jit(solution)/shard_map/ppermute | solution.py:40
  59.5 5.0 %collective-permute-done.18 = bf16[128,512]{1,0:T(8,128)(2,1)} collective-permute-done((bf16[128,512]{1,0:T(8,128)(2,1)}, bf16[128,512]{1,0:T(8,128)(2,1)}, u32[]{:S(2)}, u32[]{:S(2)}) %collective-permute-start.18) | collective-permute-done | bytes 131104 | tf_op jit(solution)/shard_map/ppermute | solution.py:40
  64.5 1.9 pad_maximum_fusion.refs_2_
  68.0 1.3 collective-permute-start.15
  69.3 1.4 collective-permute-start.16
  71.6 10.5 %collective-permute-done.15.refs_2_ = bf16[64,2048]{1,0:T(8,128)(2,1)S(1)} collective-permute-done((bf16[64,2048]{1,0:T(8,128)(2,1)S(1)}, bf16[64,2048]{1,0:T(8,128)(2,1)S(1)}, u32[]{:S(2)}, u32[]{:S(2)}) %collective-permute-start.15) | collective-permute-done | bytes 262176 | tf_op jit(solution)/shard_map/ppermute | solution.py:40
  82.1 1.3 collective-permute-start.26
  83.4 1.5 collective-permute-start.27
  85.1 2.4 %shard_map.121 = (bf16[256,2048]{1,0:T(8,128)(2,1)S(1)}, bf16[256,128]{1,0:T(8,128)(2,1)}, bf16[128,256]{1,0:T(8,128)(2,1)S(1)}, bf16[128,256]{1,0:T(8,128)(2,1)S(1)}) custom-call(bf16[128,2048]{1,0:T(8,128)(2,1)S(1)} %copy-done, bf16[128,2048]{1,0:T(8,128)(2,1)S(1)} %collective-permute-done.13.others.refs_5_, ...), custom_call_target="tpu_custom_call" | custom-call | flops 268435456 | bytes 2097152 | tf_op jit(solution)/shard_map/pallas_call | solution.py:138
  89.2 2.0 collective-permute-start.23
  92.3 1.4 collective-permute-start.25
  93.7 2.1 collective-permute-done.26.refs_3_
  95.8 1.3 collective-permute-start.28
  97.1 1.6 collective-permute-start.29
  98.7 3.6 %collective-permute-done.24 = bf16[128,512]{1,0:T(8,128)(2,1)S(1)} collective-permute-done((bf16[128,512]{1,0:T(8,128)(2,1)S(1)}, bf16[128,512]{1,0:T(8,128)(2,1)S(1)}, u32[]{:S(2)}, u32[]{:S(2)}) %collective-permute-start.24) | collective-permute-done | bytes 131104 | tf_op jit(solution)/shard_map/ppermute | solution.py:40
  105.3 1.6 collective-permute-start.31
  107.5 5.3 %shard_map.122 = (bf16[512,512]{1,0:T(8,128)(2,1)S(1)}, bf16[512,512]{1,0:T(8,128)(2,1)S(1)}, bf16[512,512]{1,0:T(8,128)(2,1)S(1)}, bf16[512,512]{1,0:T(8,128)(2,1)S(1)}) custom-call(s32[4,2,1,512]{3,2,1,0:T(1,128)S(1)} %bitcast.64, f32[4,2,1,512]{3,2,1,0:T(1,128)S(1)} %bitcast.60, bf16[512,512]{1,0:T(8,128)(2,1)S(1)} %copy-done.3, ...), custom_call_target="tpu_custom_call" | custom-call | flops 2415919104 | bytes 8404992 | tf_op jit(solution)/shard_map/pallas_call | solution.py:348
  112.8 5.3 %shard_map.123 = (bf16[512,512]{1,0:T(8,128)(2,1)S(1)}, bf16[512,512]{1,0:T(8,128)(2,1)S(1)}, bf16[512,512]{1,0:T(8,128)(2,1)S(1)}, bf16[512,512]{1,0:T(8,128)(2,1)S(1)}) custom-call(s32[4,2,1,512]{3,2,1,0:T(1,128)S(1)} %bitcast.66, f32[4,2,1,512]{3,2,1,0:T(1,128)S(1)} %bitcast.62, bf16[512,512]{1,0:T(8,128)(2,1)S(1)} %collective-permute-done.39.refs_2_, ...), custom_call_target="tpu_custom_call" | custom-call | flops 2415919104 | bytes 8404992 | tf_op jit(solution)/shard_map/pallas_call | solution.py:348
  122.0 5.1 %collective-permute-done.35 = bf16[512,256]{1,0:T(8,128)(2,1)S(1)} collective-permute-done((bf16[512,256]{1,0:T(8,128)(2,1)S(1)}, bf16[512,256]{1,0:T(8,128)(2,1)S(1)}, u32[]{:S(2)}, u32[]{:S(2)}) %collective-permute-start.35) | collective-permute-done | bytes 262176 | tf_op jit(solution)/shard_map/ppermute | solution.py:40
  130.7 3.3 %collective-permute-done.32.refs_7_ = bf16[512,512]{1,0:T(8,128)(2,1)S(1)} collective-permute-done((bf16[512,512]{1,0:T(8,128)(2,1)S(1)}, bf16[512,512]{1,0:T(8,128)(2,1)S(1)}, u32[]{:S(2)}, u32[]{:S(2)}) %collective-permute-start.32) | collective-permute-done | bytes 524320 | tf_op jit(solution)/shard_map/ppermute | solution.py:40
  139.0 7.5 %shard_map.124 = (bf16[512,512]{1,0:T(8,128)(2,1)S(1)}, bf16[512,512]{1,0:T(8,128)(2,1)S(1)}, bf16[512,512]{1,0:T(8,128)(2,1)S(1)}, bf16[512,512]{1,0:T(8,128)(2,1)S(1)}) custom-call(s32[4,2,1,512]{3,2,1,0:T(1,128)S(1)} %bitcast.67, f32[4,2,1,512]{3,2,1,0:T(1,128)S(1)} %bitcast.63, bf16[512,512]{1,0:T(8,128)(2,1)S(1)} %collective-permute-done.39.refs_2_, ...), custom_call_target="tpu_custom_call" | custom-call | flops 4026531840 | bytes 10502144 | tf_op jit(solution)/shard_map/pallas_call | solution.py:348
  147.1 7.7 %shard_map.125 = (bf16[512,512]{1,0:T(8,128)(2,1)S(1)}, bf16[512,512]{1,0:T(8,128)(2,1)S(1)}, bf16[512,512]{1,0:T(8,128)(2,1)S(1)}, bf16[512,512]{1,0:T(8,128)(2,1)S(1)}) custom-call(s32[4,2,1,512]{3,2,1,0:T(1,128)S(1)} %bitcast.65, f32[4,2,1,512]{3,2,1,0:T(1,128)S(1)} %bitcast.61, bf16[512,512]{1,0:T(8,128)(2,1)S(1)} %copy-done.3, ...), custom_call_target="tpu_custom_call" | custom-call | flops 4026531840 | bytes 10502144 | tf_op jit(solution)/shard_map/pallas_call | solution.py:348
  155.0 6.6 %collective-permute-done.48 = bf16[512,512]{1,0:T(8,128)(2,1)S(1)} collective-permute-done((bf16[512,512]{1,0:T(8,128)(2,1)S(1)}, bf16[512,512]{1,0:T(8,128)(2,1)S(1)}, u32[]{:S(2)}, u32[]{:S(2)}) %collective-permute-start.48) | collective-permute-done | bytes 524320 | tf_op jit(solution)/shard_map/ppermute | solution.py:40
  163.8 2.5 %collective-permute-start.55 = (bf16[128,512]{1,0:T(8,128)(2,1)S(1)}, bf16[128,512]{1,0:T(8,128)(2,1)S(1)}, u32[]{:S(2)}, u32[]{:S(2)}) collective-permute-start(bf16[128,512]{1,0:T(8,128)(2,1)S(1)} %get-tuple-element.207), channel_id=1, source_target_pairs={{0,24},{1,25},{2,26},{3,27},{4,28},{5,29},{6,30},{7,31},{8,0},{9,1... | collective-permute-start | bytes 393224 | tf_op jit(solution)/shard_map/ppermute | solution.py:40
  170.2 8.5 %collective-permute-done.56 = bf16[128,512]{1,0:T(8,128)(2,1)S(1)} collective-permute-done((bf16[128,512]{1,0:T(8,128)(2,1)S(1)}, bf16[128,512]{1,0:T(8,128)(2,1)S(1)}, u32[]{:S(2)}, u32[]{:S(2)}) %collective-permute-start.56) | collective-permute-done | bytes 131104 | tf_op jit(solution)/shard_map/ppermute | solution.py:40
  183.5 9.9 %collective-permute-done.64 = bf16[512,512]{1,0:T(8,128)(2,1)S(1)} collective-permute-done((bf16[512,512]{1,0:T(8,128)(2,1)S(1)}, bf16[512,512]{1,0:T(8,128)(2,1)S(1)}, u32[]{:S(2)}, u32[]{:S(2)}) %collective-permute-start.64) | collective-permute-done | bytes 524320 | tf_op jit(solution)/shard_map/ppermute | solution.py:40
  193.9 1.6 collective-permute-start.68
  195.5 1.9 collective-permute-start.69
  197.4 2.0 shard_map.126
  200.5 7.2 %collective-permute-done.68 = bf16[128,512]{1,0:T(8,128)(2,1)S(1)} collective-permute-done((bf16[128,512]{1,0:T(8,128)(2,1)S(1)}, bf16[128,512]{1,0:T(8,128)(2,1)S(1)}, u32[]{:S(2)}, u32[]{:S(2)}) %collective-permute-start.68) | collective-permute-done | bytes 131104 | tf_op jit(solution)/shard_map/ppermute | solution.py:40
  213.5 2.0 collective-permute-start.79
  215.5 1.8 shard_map.127
  219.4 6.3 %collective-permute-done.73 = bf16[64,2048]{1,0:T(8,128)(2,1)S(1)} collective-permute-done((bf16[64,2048]{1,0:T(8,128)(2,1)S(1)}, bf16[64,2048]{1,0:T(8,128)(2,1)S(1)}, u32[]{:S(2)}, u32[]{:S(2)}) %collective-permute-start.73) | collective-permute-done | bytes 262176 | tf_op jit(solution)/shard_map/ppermute | solution.py:40
  225.8 2.1 collective-permute-start.74
  230.2 4.5 %collective-permute-done.75 = bf16[16,2048]{1,0:T(8,128)(2,1)S(1)} collective-permute-done((bf16[16,2048]{1,0:T(8,128)(2,1)S(1)}, bf16[16,2048]{1,0:T(8,128)(2,1)S(1)}, u32[]{:S(2)}, u32[]{:S(2)}) %collective-permute-start.75) | collective-permute-done | bytes 65568 | tf_op jit(solution)/shard_map/ppermute | solution.py:40
  (213 shorter events, 58.2 us)
Async XLA Ops:
  13.6 9.6 %collective-permute-start.4 = (bf16[64,2176]{1,0:T(8,128)(2,1)S(1)}, bf16[64,2176]{1,0:T(8,128)(2,1)S(1)}, u32[]{:S(2)}, u32[]{:S(2)}) collective-permute-start(bf16[64,2176]{1,0:T(8,128)(2,1)S(1)} %pad_maximum_fusion.5.refs_0_), channel_id=1, source_target_pairs={{0,4},{1,5},{2,6},{3,7},{4,0},{5,1},{6,2},{7,3},{8,12},{9,13},{10,... | collective-permute-start | bytes 835592 | tf_op jit(solution)/shard_map/ppermute | solution.py:40
  15.2 27.1 %collective-permute-start.7 = (bf16[128,2048]{1,0:T(8,128)(2,1)}, bf16[128,2048]{1,0:T(8,128)(2,1)S(1)}, u32[]{:S(2)}, u32[]{:S(2)}) collective-permute-start(bf16[128,2048]{1,0:T(8,128)(2,1)} %refs_4_.3), channel_id=1, source_target_pairs={{0,2},{1,3},{2,0},{3,1},{4,6},{5,7},{6,4},{7,5},{8,10},{9,11},{10,... | collective-permute-start | bytes 1572872 | tf_op jit(solution)/shard_map/ppermute | solution.py:40
  16.7 29.0 %collective-permute-start.8 = (bf16[128,2048]{1,0:T(8,128)(2,1)}, bf16[128,2048]{1,0:T(8,128)(2,1)}, u32[]{:S(2)}, u32[]{:S(2)}) collective-permute-start(bf16[128,2048]{1,0:T(8,128)(2,1)} %refs_4_.2), channel_id=1, source_target_pairs={{0,4},{1,5},{2,6},{3,7},{4,0},{5,1},{6,2},{7,3},{8,12},{9,13},{10,... | collective-permute-start | bytes 1572872 | tf_op jit(solution)/shard_map/ppermute | solution.py:40
  17.3 18.9 %collective-permute-start.5 = (bf16[64,2176]{1,0:T(8,128)(2,1)S(1)}, bf16[64,2176]{1,0:T(8,128)(2,1)S(1)}, u32[]{:S(2)}, u32[]{:S(2)}) collective-permute-start(bf16[64,2176]{1,0:T(8,128)(2,1)S(1)} %pad_maximum_fusion.5.refs_0_), channel_id=1, source_target_pairs={{0,2},{1,3},{2,0},{3,1},{4,6},{5,7},{6,4},{7,5},{8,10},{9,11},{10,... | collective-permute-start | bytes 835592 | tf_op jit(solution)/shard_map/ppermute | solution.py:40
  17.9 22.7 %collective-permute-start.6 = (bf16[64,2176]{1,0:T(8,128)(2,1)S(1)}, bf16[64,2176]{1,0:T(8,128)(2,1)S(1)}, u32[]{:S(2)}, u32[]{:S(2)}) collective-permute-start(bf16[64,2176]{1,0:T(8,128)(2,1)S(1)} %pad_maximum_fusion.5.refs_0_), channel_id=1, source_target_pairs={{0,6},{1,7},{2,4},{3,5},{4,2},{5,3},{6,0},{7,1},{8,14},{9,15},{10,... | collective-permute-start | bytes 835592 | tf_op jit(solution)/shard_map/ppermute | solution.py:40
  23.2 22.5 %collective-permute-start.3 = (bf16[128,2048]{1,0:T(8,128)(2,1)}, bf16[128,2048]{1,0:T(8,128)(2,1)S(1)}, u32[]{:S(2)}, u32[]{:S(2)}) collective-permute-start(bf16[128,2048]{1,0:T(8,128)(2,1)} %refs_4_.3), channel_id=1, source_target_pairs={{0,1},{1,0},{2,3},{3,2},{4,5},{5,4},{6,7},{7,6},{8,9},{9,8},{10,11... | collective-permute-start | bytes 1572872 | tf_op jit(solution)/shard_map/ppermute | solution.py:40
  36.2 12.4 %collective-permute-start.10 = (bf16[16,2048]{1,0:T(8,128)(2,1)}, bf16[16,2048]{1,0:T(8,128)(2,1)}, u32[]{:S(2)}, u32[]{:S(2)}) collective-permute-start(bf16[16,2048]{1,0:T(8,128)(2,1)} %param.14), channel_id=1, source_target_pairs={{0,8},{1,9},{2,10},{3,11},{4,12},{5,13},{6,14},{7,15},{8,16},{9,17... | collective-permute-start | bytes 196616 | tf_op jit(solution)/shard_map/ppermute | solution.py:40
  50.9 8.6 %collective-permute-start.17 = (bf16[128,512]{1,0:T(8,128)(2,1)}, bf16[128,512]{1,0:T(8,128)(2,1)}, u32[]{:S(2)}, u32[]{:S(2)}) collective-permute-start(bf16[128,512]{1,0:T(8,128)(2,1)} %convolution_convert_fusion.3), channel_id=1, source_target_pairs={{0,8},{1,9},{2,10},{3,11},{4,12},{5,13},{6,14},{7,15},{8,16},{9,17... | collective-permute-start | bytes 393224 | tf_op jit(solution)/shard_map/ppermute | solution.py:40
  50.9 13.6 %collective-permute-start.18 = (bf16[128,512]{1,0:T(8,128)(2,1)}, bf16[128,512]{1,0:T(8,128)(2,1)}, u32[]{:S(2)}, u32[]{:S(2)}) collective-permute-start(bf16[128,512]{1,0:T(8,128)(2,1)} %convolution_convert_fusion.3), channel_id=1, source_target_pairs={{0,16},{1,17},{2,18},{3,19},{4,20},{5,21},{6,22},{7,23},{8,24},{9,... | collective-permute-start | bytes 393224 | tf_op jit(solution)/shard_map/ppermute | solution.py:40
  54.6 9.9 %collective-permute-start.19 = (bf16[128,512]{1,0:T(8,128)(2,1)}, bf16[128,512]{1,0:T(8,128)(2,1)}, u32[]{:S(2)}, u32[]{:S(2)}) collective-permute-start(bf16[128,512]{1,0:T(8,128)(2,1)} %convolution_convert_fusion.3), channel_id=1, source_target_pairs={{0,24},{1,25},{2,26},{3,27},{4,28},{5,29},{6,30},{7,31},{8,0},{9,1... | collective-permute-start | bytes 393224 | tf_op jit(solution)/shard_map/ppermute | solution.py:40
  54.8 14.4 %collective-permute-start.14 = (bf16[64,2048]{1,0:T(8,128)(2,1)S(1)}, bf16[64,2048]{1,0:T(8,128)(2,1)}, u32[]{:S(2)}, u32[]{:S(2)}) collective-permute-start(bf16[64,2048]{1,0:T(8,128)(2,1)S(1)} %pad_maximum_fusion.6.refs_0_), channel_id=1, source_target_pairs={{0,2},{1,3},{2,0},{3,1},{4,6},{5,7},{6,4},{7,5},{8,10},{9,11},{10,... | collective-permute-start | bytes 786440 | tf_op jit(solution)/shard_map/ppermute | solution.py:40
  56.1 29.0 %collective-permute-start.20 = (bf16[128,2048]{1,0:T(8,128)(2,1)S(1)}, bf16[128,2048]{1,0:T(8,128)(2,1)}, u32[]{:S(2)}, u32[]{:S(2)}) collective-permute-start(bf16[128,2048]{1,0:T(8,128)(2,1)S(1)} %collective-permute-done.7.refs_6_), channel_id=1, source_target_pairs={{0,1},{1,0},{2,3},{3,2},{4,5},{5,4},{6,7},{7,6},{8,9},{9,8},{10,11... | collective-permute-start | bytes 1572872 | tf_op jit(solution)/shard_map/ppermute | solution.py:40
  59.5 25.6 %collective-permute-start.21 = (bf16[128,2048]{1,0:T(8,128)(2,1)}, bf16[128,2048]{1,0:T(8,128)(2,1)}, u32[]{:S(2)}, u32[]{:S(2)}) collective-permute-start(bf16[128,2048]{1,0:T(8,128)(2,1)} %collective-permute-done.8.refs_6_), channel_id=1, source_target_pairs={{0,1},{1,0},{2,3},{3,2},{4,5},{5,4},{6,7},{7,6},{8,9},{9,8},{10,11... | collective-permute-start | bytes 1572872 | tf_op jit(solution)/shard_map/ppermute | solution.py:40
  64.5 20.6 %collective-permute-start.13 = (bf16[128,2048]{1,0:T(8,128)(2,1)S(1)}, bf16[128,2048]{1,0:T(8,128)(2,1)S(1)}, u32[]{:S(2)}, u32[]{:S(2)}) collective-permute-start(bf16[128,2048]{1,0:T(8,128)(2,1)S(1)} %copy-done), channel_id=1, source_target_pairs={{0,1},{1,0},{2,3},{3,2},{4,5},{5,4},{6,7},{7,6},{8,9},{9,8},{10,11... | collective-permute-start | bytes 1572872 | tf_op jit(solution)/shard_map/ppermute | solution.py:40
  68.0 14.2 %collective-permute-start.15 = (bf16[64,2048]{1,0:T(8,128)(2,1)S(1)}, bf16[64,2048]{1,0:T(8,128)(2,1)S(1)}, u32[]{:S(2)}, u32[]{:S(2)}) collective-permute-start(bf16[64,2048]{1,0:T(8,128)(2,1)S(1)} %pad_maximum_fusion.6.refs_0_), channel_id=1, source_target_pairs={{0,4},{1,5},{2,6},{3,7},{4,0},{5,1},{6,2},{7,3},{8,12},{9,13},{10,... | collective-permute-start | bytes 786440 | tf_op jit(solution)/shard_map/ppermute | solution.py:40
  69.3 14.2 %collective-permute-start.16 = (bf16[64,2048]{1,0:T(8,128)(2,1)S(1)}, bf16[64,2048]{1,0:T(8,128)(2,1)S(1)}, u32[]{:S(2)}, u32[]{:S(2)}) collective-permute-start(bf16[64,2048]{1,0:T(8,128)(2,1)S(1)} %pad_maximum_fusion.6.refs_0_), channel_id=1, source_target_pairs={{0,6},{1,7},{2,4},{3,5},{4,2},{5,3},{6,0},{7,1},{8,14},{9,15},{10,... | collective-permute-start | bytes 786440 | tf_op jit(solution)/shard_map/ppermute | solution.py:40
  82.1 13.6 %collective-permute-start.26 = (bf16[512,512]{1,0:T(8,128)(2,1)}, bf16[512,512]{1,0:T(8,128)(2,1)S(1)}, u32[]{:S(2)}, u32[]{:S(2)}) collective-permute-start(bf16[512,512]{1,0:T(8,128)(2,1)} %pad_maximum_fusion.refs_2_), channel_id=1, source_target_pairs={{0,4},{1,5},{2,6},{3,7},{4,0},{5,1},{6,2},{7,3},{8,12},{9,13},{10,... | collective-permute-start | bytes 1572872 | tf_op jit(solution)/shard_map/ppermute | solution.py:40
  83.4 13.6 %collective-permute-start.27 = (bf16[512,512]{1,0:T(8,128)(2,1)}, bf16[512,512]{1,0:T(8,128)(2,1)S(1)}, u32[]{:S(2)}, u32[]{:S(2)}) collective-permute-start(bf16[512,512]{1,0:T(8,128)(2,1)} %pad_maximum_fusion.refs_2_), channel_id=1, source_target_pairs={{0,2},{1,3},{2,0},{3,1},{4,6},{5,7},{6,4},{7,5},{8,10},{9,11},{10,... | collective-permute-start | bytes 1572872 | tf_op jit(solution)/shard_map/ppermute | solution.py:40
  89.2 9.5 %collective-permute-start.23 = (bf16[128,512]{1,0:T(8,128)(2,1)S(1)}, bf16[128,512]{1,0:T(8,128)(2,1)S(1)}, u32[]{:S(2)}, u32[]{:S(2)}) collective-permute-start(bf16[128,512]{1,0:T(8,128)(2,1)S(1)} %convolution_convert_fusion.2), channel_id=1, source_target_pairs={{0,8},{1,9},{2,10},{3,11},{4,12},{5,13},{6,14},{7,15},{8,16},{9,17... | collective-permute-start | bytes 393224 | tf_op jit(solution)/shard_map/ppermute | solution.py:40
  91.2 11.1 %collective-permute-start.24 = (bf16[128,512]{1,0:T(8,128)(2,1)S(1)}, bf16[128,512]{1,0:T(8,128)(2,1)S(1)}, u32[]{:S(2)}, u32[]{:S(2)}) collective-permute-start(bf16[128,512]{1,0:T(8,128)(2,1)S(1)} %convolution_convert_fusion.2), channel_id=1, source_target_pairs={{0,16},{1,17},{2,18},{3,19},{4,20},{5,21},{6,22},{7,23},{8,24},{9,... | collective-permute-start | bytes 393224 | tf_op jit(solution)/shard_map/ppermute | solution.py:40
  92.3 10.1 %collective-permute-start.25 = (bf16[128,512]{1,0:T(8,128)(2,1)S(1)}, bf16[128,512]{1,0:T(8,128)(2,1)S(1)}, u32[]{:S(2)}, u32[]{:S(2)}) collective-permute-start(bf16[128,512]{1,0:T(8,128)(2,1)S(1)} %convolution_convert_fusion.2), channel_id=1, source_target_pairs={{0,24},{1,25},{2,26},{3,27},{4,28},{5,29},{6,30},{7,31},{8,0},{9,1... | collective-permute-start | bytes 393224 | tf_op jit(solution)/shard_map/ppermute | solution.py:40
  104.0 8.8 %collective-permute-start.40 = (bf16[512,512]{1,0:T(8,128)(2,1)S(1)}, bf16[512,512]{1,0:T(8,128)(2,1)S(1)}, u32[]{:S(2)}, u32[]{:S(2)}) collective-permute-start(bf16[512,512]{1,0:T(8,128)(2,1)S(1)} %collective-permute-done.26.refs_3_), channel_id=1, source_target_pairs={{0,1},{1,0},{2,3},{3,2},{4,5},{5,4},{6,7},{7,6},{8,9},{9,8},{10,11... | collective-permute-start | bytes 1572872 | tf_op jit(solution)/shard_map/ppermute | solution.py:40
  105.3 14.0 %collective-permute-start.31 = (bf16[512,512]{1,0:T(8,128)(2,1)S(1)}, bf16[512,512]{1,0:T(8,128)(2,1)S(1)}, u32[]{:S(2)}, u32[]{:S(2)}) collective-permute-start(bf16[512,512]{1,0:T(8,128)(2,1)S(1)} %pad_maximum_fusion.1.refs_6_), channel_id=1, source_target_pairs={{0,4},{1,5},{2,6},{3,7},{4,0},{5,1},{6,2},{7,3},{8,12},{9,13},{10,... | collective-permute-start | bytes 1572872 | tf_op jit(solution)/shard_map/ppermute | solution.py:40
  106.9 13.7 %collective-permute-start.33 = (bf16[512,512]{1,0:T(8,128)(2,1)S(1)}, bf16[512,512]{1,0:T(8,128)(2,1)S(1)}, u32[]{:S(2)}, u32[]{:S(2)}) collective-permute-start(bf16[512,512]{1,0:T(8,128)(2,1)S(1)} %pad_maximum_fusion.1.refs_6_), channel_id=1, source_target_pairs={{0,2},{1,3},{2,0},{3,1},{4,6},{5,7},{6,4},{7,5},{8,10},{9,11},{10,... | collective-permute-start | bytes 1572872 | tf_op jit(solution)/shard_map/ppermute | solution.py:40
  118.2 10.2 %collective-permute-start.45 = (bf16[512,512]{1,0:T(8,128)(2,1)S(1)}, bf16[512,512]{1,0:T(8,128)(2,1)S(1)}, u32[]{:S(2)}, u32[]{:S(2)}) collective-permute-start(bf16[512,512]{1,0:T(8,128)(2,1)S(1)} %get-tuple-element.148), channel_id=1, source_target_pairs={{0,1},{1,0},{2,3},{3,2},{4,5},{5,4},{6,7},{7,6},{8,9},{9,8},{10,11... | collective-permute-start | bytes 1572872 | tf_op jit(solution)/shard_map/ppermute | solution.py:40
  128.4 18.1 %collective-permute-start.50 = (bf16[256,2048]{1,0:T(8,128)(2,1)S(1)}, bf16[256,2048]{1,0:T(8,128)(2,1)S(1)}, u32[]{:S(2)}, u32[]{:S(2)}) collective-permute-start(bf16[256,2048]{1,0:T(8,128)(2,1)S(1)} %get-tuple-element.163), channel_id=1, source_target_pairs={{0,1},{1,0},{2,3},{3,2},{4,5},{5,4},{6,7},{7,6},{8,9},{9,8},{10,11... | collective-permute-start | bytes 3145736 | tf_op jit(solution)/shard_map/ppermute | solution.py:40
  129.1 17.4 %collective-permute-start.51 = (bf16[256,2048]{1,0:T(8,128)(2,1)S(1)}, bf16[256,2048]{1,0:T(8,128)(2,1)S(1)}, u32[]{:S(2)}, u32[]{:S(2)}) collective-permute-start(bf16[256,2048]{1,0:T(8,128)(2,1)S(1)} %get-tuple-element.164), channel_id=1, source_target_pairs={{0,1},{1,0},{2,3},{3,2},{4,5},{5,4},{6,7},{7,6},{8,9},{9,8},{10,11... | collective-permute-start | bytes 3145736 | tf_op jit(solution)/shard_map/ppermute | solution.py:40
  135.5 19.4 %collective-permute-start.47 = (bf16[512,512]{1,0:T(8,128)(2,1)S(1)}, bf16[512,512]{1,0:T(8,128)(2,1)S(1)}, u32[]{:S(2)}, u32[]{:S(2)}) collective-permute-start(bf16[512,512]{1,0:T(8,128)(2,1)S(1)} %add_convert_fusion.3), channel_id=1, source_target_pairs={{0,6},{1,7},{2,4},{3,5},{4,2},{5,3},{6,0},{7,1},{8,14},{9,15},{10,... | collective-permute-start | bytes 1572872 | tf_op jit(solution)/shard_map/ppermute | solution.py:40
  136.7 24.9 %collective-permute-start.48 = (bf16[512,512]{1,0:T(8,128)(2,1)S(1)}, bf16[512,512]{1,0:T(8,128)(2,1)S(1)}, u32[]{:S(2)}, u32[]{:S(2)}) collective-permute-start(bf16[512,512]{1,0:T(8,128)(2,1)S(1)} %add_convert_fusion.2), channel_id=1, source_target_pairs={{0,4},{1,5},{2,6},{3,7},{4,0},{5,1},{6,2},{7,3},{8,12},{9,13},{10,... | collective-permute-start | bytes 1572872 | tf_op jit(solution)/shard_map/ppermute | solution.py:40
  137.9 23.7 %collective-permute-start.49 = (bf16[512,512]{1,0:T(8,128)(2,1)S(1)}, bf16[512,512]{1,0:T(8,128)(2,1)S(1)}, u32[]{:S(2)}, u32[]{:S(2)}) collective-permute-start(bf16[512,512]{1,0:T(8,128)(2,1)S(1)} %add_convert_fusion.1), channel_id=1, source_target_pairs={{0,2},{1,3},{2,0},{3,1},{4,6},{5,7},{6,4},{7,5},{8,10},{9,11},{10,... | collective-permute-start | bytes 1572872 | tf_op jit(solution)/shard_map/ppermute | solution.py:40
  146.6 20.4 %collective-permute-start.58 = (bf16[512,512]{1,0:T(8,128)(2,1)S(1)}, bf16[512,512]{1,0:T(8,128)(2,1)S(1)}, u32[]{:S(2)}, u32[]{:S(2)}) collective-permute-start(bf16[512,512]{1,0:T(8,128)(2,1)S(1)} %get-tuple-element.177), channel_id=1, source_target_pairs={{0,1},{1,0},{2,3},{3,2},{4,5},{5,4},{6,7},{7,6},{8,9},{9,8},{10,11... | collective-permute-start | bytes 1572872 | tf_op jit(solution)/shard_map/ppermute | solution.py:40
  146.6 15.3 %collective-permute-start.54 = (bf16[512,512]{1,0:T(8,128)(2,1)S(1)}, bf16[512,512]{1,0:T(8,128)(2,1)S(1)}, u32[]{:S(2)}, u32[]{:S(2)}) collective-permute-start(bf16[512,512]{1,0:T(8,128)(2,1)S(1)} %get-tuple-element.174), channel_id=1, source_target_pairs={{0,1},{1,0},{2,3},{3,2},{4,5},{5,4},{6,7},{7,6},{8,9},{9,8},{10,11... | collective-permute-start | bytes 1572872 | tf_op jit(solution)/shard_map/ppermute | solution.py:40
  166.3 12.5 %collective-permute-start.56 = (bf16[128,512]{1,0:T(8,128)(2,1)S(1)}, bf16[128,512]{1,0:T(8,128)(2,1)S(1)}, u32[]{:S(2)}, u32[]{:S(2)}) collective-permute-start(bf16[128,512]{1,0:T(8,128)(2,1)S(1)} %get-tuple-element.209), channel_id=1, source_target_pairs={{0,16},{1,17},{2,18},{3,19},{4,20},{5,21},{6,22},{7,23},{8,24},{9,... | collective-permute-start | bytes 393224 | tf_op jit(solution)/shard_map/ppermute | solution.py:40
  166.8 11.9 %collective-permute-start.57 = (bf16[128,512]{1,0:T(8,128)(2,1)S(1)}, bf16[128,512]{1,0:T(8,128)(2,1)S(1)}, u32[]{:S(2)}, u32[]{:S(2)}) collective-permute-start(bf16[128,512]{1,0:T(8,128)(2,1)S(1)} %get-tuple-element.208), channel_id=1, source_target_pairs={{0,8},{1,9},{2,10},{3,11},{4,12},{5,13},{6,14},{7,15},{8,16},{9,17... | collective-permute-start | bytes 393224 | tf_op jit(solution)/shard_map/ppermute | solution.py:40
  167.1 12.1 %collective-permute-start.59 = (bf16[512,256]{1,0:T(8,128)(2,1)S(1)}, bf16[512,256]{1,0:T(8,128)(2,1)S(1)}, u32[]{:S(2)}, u32[]{:S(2)}) collective-permute-start(bf16[512,256]{1,0:T(8,128)(2,1)S(1)} %get-tuple-element.206), channel_id=1, source_target_pairs={{0,2},{1,3},{2,0},{3,1},{4,6},{5,7},{6,4},{7,5},{8,10},{9,11},{10,... | collective-permute-start | bytes 786440 | tf_op jit(solution)/shard_map/ppermute | solution.py:40
  168.1 11.1 %collective-permute-start.60 = (bf16[512,256]{1,0:T(8,128)(2,1)S(1)}, bf16[512,256]{1,0:T(8,128)(2,1)S(1)}, u32[]{:S(2)}, u32[]{:S(2)}) collective-permute-start(bf16[512,256]{1,0:T(8,128)(2,1)S(1)} %get-tuple-element.205), channel_id=1, source_target_pairs={{0,4},{1,5},{2,6},{3,7},{4,0},{5,1},{6,2},{7,3},{8,12},{9,13},{10,... | collective-permute-start | bytes 786440 | tf_op jit(solution)/shard_map/ppermute | solution.py:40
  179.4 14.0 %collective-permute-start.64 = (bf16[512,512]{1,0:T(8,128)(2,1)S(1)}, bf16[512,512]{1,0:T(8,128)(2,1)S(1)}, u32[]{:S(2)}, u32[]{:S(2)}) collective-permute-start(bf16[512,512]{1,0:T(8,128)(2,1)S(1)} %pad_maximum_fusion.3), channel_id=1, source_target_pairs={{0,4},{1,5},{2,6},{3,7},{4,0},{5,1},{6,2},{7,3},{8,12},{9,13},{10,... | collective-permute-start | bytes 1572872 | tf_op jit(solution)/shard_map/ppermute | solution.py:40
  180.5 12.9 %collective-permute-start.65 = (bf16[512,512]{1,0:T(8,128)(2,1)S(1)}, bf16[512,512]{1,0:T(8,128)(2,1)S(1)}, u32[]{:S(2)}, u32[]{:S(2)}) collective-permute-start(bf16[512,512]{1,0:T(8,128)(2,1)S(1)} %pad_maximum_fusion.4), channel_id=1, source_target_pairs={{0,2},{1,3},{2,0},{3,1},{4,6},{5,7},{6,4},{7,5},{8,10},{9,11},{10,... | collective-permute-start | bytes 1572872 | tf_op jit(solution)/shard_map/ppermute | solution.py:40
  181.5 12.1 %collective-permute-start.61 = (bf16[128,128]{1,0:T(8,128)(2,1)S(1)}, bf16[128,128]{1,0:T(8,128)(2,1)S(1)}, u32[]{:S(2)}, u32[]{:S(2)}) collective-permute-start(bf16[128,128]{1,0:T(8,128)(2,1)S(1)} %get-tuple-element.224), channel_id=1, source_target_pairs={{0,1},{1,0},{2,3},{3,2},{4,5},{5,4},{6,7},{7,6},{8,9},{9,8},{10,11... | collective-permute-start | bytes 98312 | tf_op jit(solution)/shard_map/ppermute | solution.py:40
  181.6 12.2 %collective-permute-start.62 = (bf16[128,128]{1,0:T(8,128)(2,1)S(1)}, bf16[128,128]{1,0:T(8,128)(2,1)S(1)}, u32[]{:S(2)}, u32[]{:S(2)}) collective-permute-start(bf16[128,128]{1,0:T(8,128)(2,1)S(1)} %get-tuple-element.223), channel_id=1, source_target_pairs={{0,4},{1,5},{2,6},{3,7},{4,0},{5,1},{6,2},{7,3},{8,12},{9,13},{10,... | collective-permute-start | bytes 98312 | tf_op jit(solution)/shard_map/ppermute | solution.py:40
  182.8 11.0 %collective-permute-start.63 = (bf16[128,128]{1,0:T(8,128)(2,1)S(1)}, bf16[128,128]{1,0:T(8,128)(2,1)S(1)}, u32[]{:S(2)}, u32[]{:S(2)}) collective-permute-start(bf16[128,128]{1,0:T(8,128)(2,1)S(1)} %get-tuple-element.222), channel_id=1, source_target_pairs={{0,5},{1,4},{2,7},{3,6},{4,1},{5,0},{6,3},{7,2},{8,13},{9,12},{10,... | collective-permute-start | bytes 98312 | tf_op jit(solution)/shard_map/ppermute | solution.py:40
  193.9 13.7 %collective-permute-start.68 = (bf16[128,512]{1,0:T(8,128)(2,1)S(1)}, bf16[128,512]{1,0:T(8,128)(2,1)S(1)}, u32[]{:S(2)}, u32[]{:S(2)}) collective-permute-start(bf16[128,512]{1,0:T(8,128)(2,1)S(1)} %get-tuple-element.204), channel_id=1, source_target_pairs={{0,16},{1,17},{2,18},{3,19},{4,20},{5,21},{6,22},{7,23},{8,24},{9,... | collective-permute-start | bytes 393224 | tf_op jit(solution)/shard_map/ppermute | solution.py:40
  195.5 12.2 %collective-permute-start.69 = (bf16[128,512]{1,0:T(8,128)(2,1)S(1)}, bf16[128,512]{1,0:T(8,128)(2,1)S(1)}, u32[]{:S(2)}, u32[]{:S(2)}) collective-permute-start(bf16[128,512]{1,0:T(8,128)(2,1)S(1)} %get-tuple-element.203), channel_id=1, source_target_pairs={{0,8},{1,9},{2,10},{3,11},{4,12},{5,13},{6,14},{7,15},{8,16},{9,17... | collective-permute-start | bytes 393224 | tf_op jit(solution)/shard_map/ppermute | solution.py:40
  199.4 8.7 %collective-permute-start.66 = (bf16[64,2048]{1,0:T(8,128)(2,1)S(1)}, bf16[64,2048]{1,0:T(8,128)(2,1)S(1)}, u32[]{:S(2)}, u32[]{:S(2)}) collective-permute-start(bf16[64,2048]{1,0:T(8,128)(2,1)S(1)} %get-tuple-element.190), channel_id=1, source_target_pairs={{0,2},{1,3},{2,0},{3,1},{4,6},{5,7},{6,4},{7,5},{8,10},{9,11},{10,... | collective-permute-start | bytes 786440 | tf_op jit(solution)/shard_map/ppermute | solution.py:40
  208.3 20.2 %collective-permute-start.77 = (bf16[16,2048]{1,0:T(8,128)(2,1)S(1)}, bf16[16,2048]{1,0:T(8,128)(2,1)S(1)}, u32[]{:S(2)}, u32[]{:S(2)}) collective-permute-start(bf16[16,2048]{1,0:T(8,128)(2,1)S(1)} %get-tuple-element.210), channel_id=1, source_target_pairs={{0,24},{1,25},{2,26},{3,27},{4,28},{5,29},{6,30},{7,31},{8,0},{9,1... | collective-permute-start | bytes 196616 | tf_op jit(solution)/shard_map/ppermute | solution.py:40
  209.4 20.0 %collective-permute-start.78 = (bf16[16,2048]{1,0:T(8,128)(2,1)S(1)}, bf16[16,2048]{1,0:T(8,128)(2,1)S(1)}, u32[]{:S(2)}, u32[]{:S(2)}) collective-permute-start(bf16[16,2048]{1,0:T(8,128)(2,1)S(1)} %get-tuple-element.212), channel_id=1, source_target_pairs={{0,16},{1,17},{2,18},{3,19},{4,20},{5,21},{6,22},{7,23},{8,24},{9,... | collective-permute-start | bytes 196616 | tf_op jit(solution)/shard_map/ppermute | solution.py:40
  213.5 15.9 %collective-permute-start.79 = (bf16[16,2048]{1,0:T(8,128)(2,1)S(1)}, bf16[16,2048]{1,0:T(8,128)(2,1)S(1)}, u32[]{:S(2)}, u32[]{:S(2)}) collective-permute-start(bf16[16,2048]{1,0:T(8,128)(2,1)S(1)} %get-tuple-element.211), channel_id=1, source_target_pairs={{0,8},{1,9},{2,10},{3,11},{4,12},{5,13},{6,14},{7,15},{8,16},{9,17... | collective-permute-start | bytes 196616 | tf_op jit(solution)/shard_map/ppermute | solution.py:40
  217.4 8.3 %collective-permute-start.73 = (bf16[64,2048]{1,0:T(8,128)(2,1)S(1)}, bf16[64,2048]{1,0:T(8,128)(2,1)S(1)}, u32[]{:S(2)}, u32[]{:S(2)}) collective-permute-start(bf16[64,2048]{1,0:T(8,128)(2,1)S(1)} %get-tuple-element.198), channel_id=1, source_target_pairs={{0,4},{1,5},{2,6},{3,7},{4,0},{5,1},{6,2},{7,3},{8,12},{9,13},{10,... | collective-permute-start | bytes 786440 | tf_op jit(solution)/shard_map/ppermute | solution.py:40
  (42 other events, 312.7 us)

commit v7 on v6

--- a/solution.py
+++ b/solution.py
@@ -149,41 +149,50 @@
     )(*operands)
 
 
-def projection_kernel(inputs, others, *refs):
-    quarters, (near, told, part, other) = refs[:4], refs[4:]
-    width = near.shape[1]
+def projection_kernel(*refs):
+    tokens, other_tokens, grads, other_grads, *quarters = refs[:8]
+    nears, (told, part, other) = refs[8:10], refs[10:]
+    width = nears[0].shape[1]
     count = quarters[0].shape[0]
+    for near, start, order in zip(nears, (0, width), ((0, 1, 2, 3), (0, 2, 1, 3))):
+        for index, quarter in enumerate(order):
+            held = slice(index * count, (index + 1) * count)
+            near[held, :] = quarters[quarter][:, start : start + width]
     for index, quarter in enumerate(quarters):
         held = slice(index * count, (index + 1) * count)
-        near[held, :] = quarter[:, :width]
-        if quarter.shape[1] > width:
-            told[held, :] = quarter[:, width:]
+        if quarter.shape[1] > 2 * width:
+            told[held, :] = quarter[:, 2 * width :]
         else:
             told[held, :] = jnp.zeros((count, told.shape[1]), told.dtype)
-    part[...] = matmul(inputs[...], near[...], ((1,), (1,))).astype(part.dtype)
-    other[...] = matmul(others[...], near[...], ((1,), (1,))).astype(other.dtype)
-
-
-def projected(inputs, others, quarters, place):
-    width = inputs.shape[1]
+    half = nears[0].shape[0]
+    for target, down, up in ((part, tokens, grads), (other, other_tokens, other_grads)):
+        for source, near, start in ((down, nears[0], 0), (up, nears[1], half)):
+            product = matmul(source[...], near[...], ((1,), (1,)))
+            target[:, start : start + half] = product.astype(target.dtype)
+
+
+def projected(inputs, quarters):
+    row_count, width = inputs[0].shape
     count = 4 * quarters[0].shape[0]
-    extra = max(quarters[0].shape[1] - width, 128)
+    extra = max(quarters[0].shape[1] - 2 * width, 128)
     dtype = jnp.bfloat16 if lax.axis_size("tensor") == 1 else jnp.float32
-    result = jax.ShapeDtypeStruct((inputs.shape[0], count), dtype)
-    near, told, part, other = vmem_call(
+    near = jax.ShapeDtypeStruct((count, width), jnp.bfloat16)
+    result = jax.ShapeDtypeStruct((row_count, 2 * count), dtype)
+    down_near, up_near, told, part, other = vmem_call(
         projection_kernel,
-        (
-            jax.ShapeDtypeStruct((count, width), jnp.bfloat16),
-            jax.ShapeDtypeStruct((count, extra), jnp.bfloat16),
-            result,
-            result,
-        ),
-        (inputs, others) + tuple(quarters),
-        2 * inputs.shape[0] * width * count,
+        (near, near, jax.ShapeDtypeStruct((count, extra), jnp.bfloat16), result, result),
+        tuple(inputs) + tuple(quarters),
+        4 * row_count * width * count,
     )
     other = shifted(tensor_total(other).astype(jnp.bfloat16), OWNERS, CORE)
-    relative = lax.concatenate([tensor_total(part).astype(jnp.bfloat16), other], 1)
-    return matmul(relative, place).astype(jnp.bfloat16), near, told
+    part = tensor_total(part).astype(jnp.bfloat16)
+    results = []
+    for start, (first, second) in ((0, (Y, X)), (count, (X, Y))):
+        place = placement(count // 4 // radices(device_count(OWNERS))[Z], first, second)
+        columns = slice(start, start + count)
+        relative = lax.concatenate([part[:, columns], other[:, columns]], 1)
+        results.append(matmul(relative, place).astype(jnp.bfloat16))
+    return results, (down_near, up_near), told
 
 
 def grad_kernel(*refs):
@@ -400,40 +409,34 @@
     rows = down_proj.shape[0]
     told = lax.concatenate([routes.T, combine_fixed.T], 0).astype(jnp.bfloat16)
     ride = lax.axis_size("dp") == 1
-    down_sent = down_proj
+    sent = [down_proj, up_proj]
     if ride:
-        down_sent = lax.concatenate([down_proj, told.reshape(rows, -1)], 1)
+        sent.append(told.reshape(rows, -1))
     next_tokens, next_grads = shifted(tokens, OWNERS, X), shifted(out_grad, OWNERS, Y)
-    down_own, later_tokens, later_up = tied(
-        gather_depth(down_sent, OWNERS), tokens, up_proj
-    )
-    down_parts = gather_chips(down_own, OWNERS, Y, X)
+    own = gather_depth(lax.concatenate(sent, 1), OWNERS)
+    own, next_tokens, next_grads, later_tokens, later_grads = tied(
+        own, next_tokens, next_grads, tokens, out_grad
+    )
+    quarters = gather_chips(own, OWNERS, Y, X)
     other_tokens = shifted(later_tokens, OWNERS, CORE)
-    up_own = gather_depth(later_up, OWNERS)
-    down_parts, next_tokens, next_grads = tied(down_parts, next_tokens, next_grads)
-
+    other_grads = shifted(later_grads, OWNERS, CORE)
     down_place = placement(rows, Y, X)
     up_place = placement(rows, X, Y)
-    latent, down_near, told_near = projected(tokens, other_tokens, down_parts, down_place)
+    (latent, mix_grad), (down_near, up_near), told_near = projected(
+        (tokens, other_tokens, out_grad, other_grads), quarters
+    )
     if not ride:
         told_near = lax.concatenate(
             list(gather_chips(gather_depth(told, EXPERT), EXPERT, Y, X)), 0
         )
-    latent, up_own, later_grads, next_tokens, next_grads = tied(
-        latent, up_own, out_grad, next_tokens, next_grads
-    )
+    latent, next_tokens, next_grads, told_near = tied(latent, next_tokens, next_grads, told_near)
     latent_own = gather_depth(latent, EXPERT)
-    up_parts = gather_chips(up_own, OWNERS, X, Y)
-    other_grads = shifted(later_grads, OWNERS, CORE)
     last_tokens = shifted(next_tokens, OWNERS, CORE)
     last_grads = shifted(next_grads, OWNERS, CORE)
-    latent_own, told_near = tied(latent_own, told_near)
+    latent_own, last_tokens, last_grads, mix_grad = tied(
+        latent_own, last_tokens, last_grads, mix_grad
+    )
     near = (latent_own, shifted(latent_own, EXPERT, Y), shifted(latent_own, EXPERT, X))
-    up_parts, latent_own, last_tokens, last_grads = tied(
-        up_parts, latent_own, last_tokens, last_grads
-    )
-    near = (latent_own,) + near[1:]
-    mix_grad, up_near, _ = projected(out_grad, other_grads, up_parts, up_place)
     mix_own = gather_depth(mix_grad, EXPERT)
     told_far = shifted(told_near, EXPERT, CORE)
     plans, slot_count = expert_plans(

time: 236 us -> 222 us (0.941)
  starting transfers between devices: 73.4 us -> 64.5 us
  other arithmetic: 10.2 us -> 7.75 us
    ppermute x80 -> x73, starting transfers between devices: 73.4 us -> 64.5 us  [shifted(): return lax.ppermute(block, axes, pairs)]
    concatenate x4 -> x3, other arithmetic: 3.75 us -> 1 us  [gather_depth(): lax.concatenate([rows] + [shifted(rows, axes, Z, step=step) for step in r...]
    pallas_call x4 -> x3, Pallas kernels: 7.05 us -> 5.53 us  [vmem_call(): pl.pallas_call(kernel, out_shape=out_shape, in_specs=[whole] * len(operan...]
    ppermute x80 -> x73, waiting for transfers between devices: 109 us -> 109 us  [shifted(): return lax.ppermute(block, axes, pairs)]
  transfers between devices with their start and end apart: 80 -> 73, of which waited for: 34 -> 33; matrix products, arithmetic and copies ran while one was open for 5% -> 5% of each run, Pallas kernels for 14% -> 13%
where the time goes in v7:
time: 222 us
  waiting for transfers between devices  109 us (49%)
  starting transfers between devices  64.5 us (29%)
  Pallas kernels  31.4 us (14%)
  other arithmetic  7.75 us (3%)
  matrix products  5.44 us (2%)
  local copies, waits for them, and re-layouts  2.4 us (1%)
    ppermute x73, waiting for transfers between devices, shifted(): return lax.ppermute(block, axes, pairs)  109 us
    ppermute x73, starting transfers between devices, shifted(): return lax.ppermute(block, axes, pairs)  64.5 us
    pallas_call x4, Pallas kernels, expert_call(): pl.pallas_call(kernel, out_shape=(jax.ShapeDtypeStruct((span, latent_widt...  25.9 us
    pallas_call x3, Pallas kernels, vmem_call(): pl.pallas_call(kernel, out_shape=out_shape, in_specs=[whole] * len(operan...  5.53 us
    dot_general x8, matrix products, matmul(): lax.dot_general(left, right, (contract, ((), ())), preferred_element_type...  5.35 us
  transfers between devices with their start and end apart: 73, of which 33 were waited for; matrix products, arithmetic and copies ran while one was open for 5% of the time, Pallas kernels for 13%

profile of v7, /device:TPU:0, one launch (start us, length us, event | category | flops | bytes accessed | tf_op | source)
XLA Modules:
  0.0 222.0 jit_solution(764441097774755902)
XLA Ops:
  2.3 3.1 %collective-permute-start = (bf16[16,4224]{1,0:T(8,128)(2,1)S(1)}, bf16[16,4224]{1,0:T(8,128)(2,1)S(1)}, u32[]{:S(2)}, u32[]{:S(2)}) collective-permute-start(bf16[16,4224]{1,0:T(8,128)(2,1)S(1)} %maximum_maximum_fusion), channel_id=1, source_target_pairs={{0,8},{1,9},{2,10},{3,11},{4,12},{5,13},{6,14},{7,15},{8,16},{9,17... | collective-permute-start | bytes 405512 | tf_op jit(solution)/shard_map/ppermute | solution.py:40
  5.4 2.6 %collective-permute-start.1 = (bf16[16,4224]{1,0:T(8,128)(2,1)S(1)}, bf16[16,4224]{1,0:T(8,128)(2,1)S(1)}, u32[]{:S(2)}, u32[]{:S(2)}) collective-permute-start(bf16[16,4224]{1,0:T(8,128)(2,1)S(1)} %maximum_maximum_fusion), channel_id=1, source_target_pairs={{0,16},{1,17},{2,18},{3,19},{4,20},{5,21},{6,22},{7,23},{8,24},{9,... | collective-permute-start | bytes 405512 | tf_op jit(solution)/shard_map/ppermute | solution.py:40
  8.0 1.3 collective-permute-start.2
  9.3 1.5 collective-permute-start.3
  10.8 1.5 collective-permute-start.4
  12.8 4.1 %collective-permute-done.1 = bf16[16,4224]{1,0:T(8,128)(2,1)S(1)} collective-permute-done((bf16[16,4224]{1,0:T(8,128)(2,1)S(1)}, bf16[16,4224]{1,0:T(8,128)(2,1)S(1)}, u32[]{:S(2)}, u32[]{:S(2)}) %collective-permute-start.1) | collective-permute-done | bytes 135200 | tf_op jit(solution)/shard_map/ppermute | solution.py:40
  17.8 4.7 %collective-permute-done.3.refs_6_ = bf16[128,2048]{1,0:T(8,128)(2,1)} collective-permute-done((bf16[128,2048]{1,0:T(8,128)(2,1)}, bf16[128,2048]{1,0:T(8,128)(2,1)}, u32[]{:S(2)}, u32[]{:S(2)}) %collective-permute-start.3) | collective-permute-done | bytes 524320 | tf_op jit(solution)/shard_map/ppermute | solution.py:40
  22.5 1.2 collective-permute-done.4.refs_6_
  23.7 1.5 collective-permute-start.7
  25.8 1.4 collective-permute-start.9
  29.9 8.2 %collective-permute-done.7.refs_5_ = bf16[64,4224]{1,0:T(8,128)(2,1)S(1)} collective-permute-done((bf16[64,4224]{1,0:T(8,128)(2,1)S(1)}, bf16[64,4224]{1,0:T(8,128)(2,1)S(1)}, u32[]{:S(2)}, u32[]{:S(2)}) %collective-permute-start.7) | collective-permute-done | bytes 540704 | tf_op jit(solution)/shard_map/ppermute | solution.py:40
  38.0 2.4 %collective-permute-done.8.refs_6_ = bf16[64,4224]{1,0:T(8,128)(2,1)S(1)} collective-permute-done((bf16[64,4224]{1,0:T(8,128)(2,1)S(1)}, bf16[64,4224]{1,0:T(8,128)(2,1)S(1)}, u32[]{:S(2)}, u32[]{:S(2)}) %collective-permute-start.8) | collective-permute-done | bytes 540704 | tf_op jit(solution)/shard_map/ppermute | solution.py:40
  40.4 8.0 %collective-permute-done.9.refs_7_ = bf16[64,4224]{1,0:T(8,128)(2,1)S(1)} collective-permute-done((bf16[64,4224]{1,0:T(8,128)(2,1)S(1)}, bf16[64,4224]{1,0:T(8,128)(2,1)S(1)}, u32[]{:S(2)}, u32[]{:S(2)}) %collective-permute-start.9) | collective-permute-done | bytes 540704 | tf_op jit(solution)/shard_map/ppermute | solution.py:40
  48.4 1.5 shard_map.120
  50.9 1.3 collective-permute-done.10
  55.6 2.8 %collective-permute-start.13 = (bf16[128,512]{1,0:T(8,128)(2,1)S(1)}, bf16[128,512]{1,0:T(8,128)(2,1)S(1)}, u32[]{:S(2)}, u32[]{:S(2)}) collective-permute-start(bf16[128,512]{1,0:T(8,128)(2,1)S(1)} %convolution_convert_fusion.3), channel_id=1, source_target_pairs={{0,24},{1,25},{2,26},{3,27},{4,28},{5,29},{6,30},{7,31},{8,0},{9,1... | collective-permute-start | bytes 393224 | tf_op jit(solution)/shard_map/ppermute | solution.py:40
  58.4 1.2 convolution_convert_fusion.2
  59.8 3.1 %collective-permute-done.11 = bf16[128,512]{1,0:T(8,128)(2,1)S(1)} collective-permute-done((bf16[128,512]{1,0:T(8,128)(2,1)S(1)}, bf16[128,512]{1,0:T(8,128)(2,1)S(1)}, u32[]{:S(2)}, u32[]{:S(2)}) %collective-permute-start.11) | collective-permute-done | bytes 131104 | tf_op jit(solution)/shard_map/ppermute | solution.py:40
  62.9 5.0 %collective-permute-done.12 = bf16[128,512]{1,0:T(8,128)(2,1)S(1)} collective-permute-done((bf16[128,512]{1,0:T(8,128)(2,1)S(1)}, bf16[128,512]{1,0:T(8,128)(2,1)S(1)}, u32[]{:S(2)}, u32[]{:S(2)}) %collective-permute-start.12) | collective-permute-done | bytes 131104 | tf_op jit(solution)/shard_map/ppermute | solution.py:40
  68.0 1.6 collective-permute-start.19
  70.3 3.0 %collective-permute-start.16 = (bf16[128,512]{1,0:T(8,128)(2,1)S(1)}, bf16[128,512]{1,0:T(8,128)(2,1)S(1)}, u32[]{:S(2)}, u32[]{:S(2)}) collective-permute-start(bf16[128,512]{1,0:T(8,128)(2,1)S(1)} %convolution_convert_fusion.2), channel_id=1, source_target_pairs={{0,8},{1,9},{2,10},{3,11},{4,12},{5,13},{6,14},{7,15},{8,16},{9,17... | collective-permute-start | bytes 393224 | tf_op jit(solution)/shard_map/ppermute | solution.py:40
  73.5 2.3 %collective-permute-start.18 = (bf16[128,512]{1,0:T(8,128)(2,1)S(1)}, bf16[128,512]{1,0:T(8,128)(2,1)S(1)}, u32[]{:S(2)}, u32[]{:S(2)}) collective-permute-start(bf16[128,512]{1,0:T(8,128)(2,1)S(1)} %convolution_convert_fusion.2), channel_id=1, source_target_pairs={{0,24},{1,25},{2,26},{3,27},{4,28},{5,29},{6,30},{7,31},{8,0},{9,1... | collective-permute-start | bytes 393224 | tf_op jit(solution)/shard_map/ppermute | solution.py:40
  75.8 5.0 %collective-permute-done.19.refs_3_ = bf16[512,512]{1,0:T(8,128)(2,1)S(1)} collective-permute-done((bf16[512,512]{1,0:T(8,128)(2,1)S(1)}, bf16[512,512]{1,0:T(8,128)(2,1)S(1)}, u32[]{:S(2)}, u32[]{:S(2)}) %collective-permute-start.19) | collective-permute-done | bytes 524320 | tf_op jit(solution)/shard_map/ppermute | solution.py:40
  83.5 4.2 %collective-permute-done.21 = bf16[512,256]{1,0:T(8,128)(2,1)S(1)} collective-permute-done((bf16[512,256]{1,0:T(8,128)(2,1)S(1)}, bf16[512,256]{1,0:T(8,128)(2,1)S(1)}, u32[]{:S(2)}, u32[]{:S(2)}) %collective-permute-start.21) | collective-permute-done | bytes 262176 | tf_op jit(solution)/shard_map/ppermute | solution.py:40
  87.7 1.3 collective-permute-done.22
  92.6 5.3 %shard_map.121 = (bf16[512,512]{1,0:T(8,128)(2,1)S(1)}, bf16[512,512]{1,0:T(8,128)(2,1)S(1)}, bf16[512,512]{1,0:T(8,128)(2,1)S(1)}, bf16[512,512]{1,0:T(8,128)(2,1)S(1)}) custom-call(s32[4,2,1,512]{3,2,1,0:T(1,128)S(1)} %bitcast.64, f32[4,2,1,512]{3,2,1,0:T(1,128)S(1)} %bitcast.60, bf16[512,512]{1,0:T(8,128)(2,1)S(1)} %pad_maximum_fusion.1.refs_2_, ...), custom_call_target="tpu_custom_call" | custom-call | flops 2415919104 | bytes 8404992 | tf_op jit(solution)/shard_map/pallas_call | solution.py:357
  97.9 5.3 %shard_map.122 = (bf16[512,512]{1,0:T(8,128)(2,1)S(1)}, bf16[512,512]{1,0:T(8,128)(2,1)S(1)}, bf16[512,512]{1,0:T(8,128)(2,1)S(1)}, bf16[512,512]{1,0:T(8,128)(2,1)S(1)}) custom-call(s32[4,2,1,512]{3,2,1,0:T(1,128)S(1)} %bitcast.66, f32[4,2,1,512]{3,2,1,0:T(1,128)S(1)} %bitcast.62, bf16[512,512]{1,0:T(8,128)(2,1)S(1)} %collective-permute-done.32.refs_2_, ...), custom_call_target="tpu_custom_call" | custom-call | flops 2415919104 | bytes 8404992 | tf_op jit(solution)/shard_map/pallas_call | solution.py:357
  105.1 1.4 collective-permute-start.29
  107.1 5.1 %collective-permute-done.28 = bf16[512,256]{1,0:T(8,128)(2,1)S(1)} collective-permute-done((bf16[512,256]{1,0:T(8,128)(2,1)S(1)}, bf16[512,256]{1,0:T(8,128)(2,1)S(1)}, u32[]{:S(2)}, u32[]{:S(2)}) %collective-permute-start.28) | collective-permute-done | bytes 262176 | tf_op jit(solution)/shard_map/ppermute | solution.py:40
  115.2 3.3 %collective-permute-done.25.refs_7_ = bf16[512,512]{1,0:T(8,128)(2,1)S(1)} collective-permute-done((bf16[512,512]{1,0:T(8,128)(2,1)S(1)}, bf16[512,512]{1,0:T(8,128)(2,1)S(1)}, u32[]{:S(2)}, u32[]{:S(2)}) %collective-permute-start.25) | collective-permute-done | bytes 524320 | tf_op jit(solution)/shard_map/ppermute | solution.py:40
  120.1 1.6 collective-permute-start.40
  123.6 7.5 %shard_map.123 = (bf16[512,512]{1,0:T(8,128)(2,1)S(1)}, bf16[512,512]{1,0:T(8,128)(2,1)S(1)}, bf16[512,512]{1,0:T(8,128)(2,1)S(1)}, bf16[512,512]{1,0:T(8,128)(2,1)S(1)}) custom-call(s32[4,2,1,512]{3,2,1,0:T(1,128)S(1)} %bitcast.67, f32[4,2,1,512]{3,2,1,0:T(1,128)S(1)} %bitcast.63, bf16[512,512]{1,0:T(8,128)(2,1)S(1)} %collective-permute-done.32.refs_2_, ...), custom_call_target="tpu_custom_call" | custom-call | flops 4026531840 | bytes 10502144 | tf_op jit(solution)/shard_map/pallas_call | solution.py:357
  131.7 7.7 %shard_map.124 = (bf16[512,512]{1,0:T(8,128)(2,1)S(1)}, bf16[512,512]{1,0:T(8,128)(2,1)S(1)}, bf16[512,512]{1,0:T(8,128)(2,1)S(1)}, bf16[512,512]{1,0:T(8,128)(2,1)S(1)}) custom-call(s32[4,2,1,512]{3,2,1,0:T(1,128)S(1)} %bitcast.65, f32[4,2,1,512]{3,2,1,0:T(1,128)S(1)} %bitcast.61, bf16[512,512]{1,0:T(8,128)(2,1)S(1)} %pad_maximum_fusion.1.refs_2_, ...), custom_call_target="tpu_custom_call" | custom-call | flops 4026531840 | bytes 10502144 | tf_op jit(solution)/shard_map/pallas_call | solution.py:357
  139.6 6.6 %collective-permute-done.41 = bf16[512,512]{1,0:T(8,128)(2,1)S(1)} collective-permute-done((bf16[512,512]{1,0:T(8,128)(2,1)S(1)}, bf16[512,512]{1,0:T(8,128)(2,1)S(1)}, u32[]{:S(2)}, u32[]{:S(2)}) %collective-permute-start.41) | collective-permute-done | bytes 524320 | tf_op jit(solution)/shard_map/ppermute | solution.py:40
  146.8 1.3 collective-permute-done.45
  148.3 3.4 %collective-permute-start.48 = (bf16[128,512]{1,0:T(8,128)(2,1)S(1)}, bf16[128,512]{1,0:T(8,128)(2,1)S(1)}, u32[]{:S(2)}, u32[]{:S(2)}) collective-permute-start(bf16[128,512]{1,0:T(8,128)(2,1)S(1)} %get-tuple-element.183), channel_id=1, source_target_pairs={{0,24},{1,25},{2,26},{3,27},{4,28},{5,29},{6,30},{7,31},{8,0},{9,1... | collective-permute-start | bytes 393224 | tf_op jit(solution)/shard_map/ppermute | solution.py:40
  151.7 1.9 collective-permute-start.49
  155.9 9.6 %collective-permute-done.49 = bf16[128,512]{1,0:T(8,128)(2,1)S(1)} collective-permute-done((bf16[128,512]{1,0:T(8,128)(2,1)S(1)}, bf16[128,512]{1,0:T(8,128)(2,1)S(1)}, u32[]{:S(2)}, u32[]{:S(2)}) %collective-permute-start.49) | collective-permute-done | bytes 131104 | tf_op jit(solution)/shard_map/ppermute | solution.py:40
  168.3 1.3 collective-permute-start.55
  170.1 9.9 %collective-permute-done.57 = bf16[512,512]{1,0:T(8,128)(2,1)S(1)} collective-permute-done((bf16[512,512]{1,0:T(8,128)(2,1)S(1)}, bf16[512,512]{1,0:T(8,128)(2,1)S(1)}, u32[]{:S(2)}, u32[]{:S(2)}) %collective-permute-start.57) | collective-permute-done | bytes 524320 | tf_op jit(solution)/shard_map/ppermute | solution.py:40
  181.7 1.9 collective-permute-start.62
  183.6 2.0 shard_map.125
  187.2 6.7 %collective-permute-done.61 = bf16[128,512]{1,0:T(8,128)(2,1)S(1)} collective-permute-done((bf16[128,512]{1,0:T(8,128)(2,1)S(1)}, bf16[128,512]{1,0:T(8,128)(2,1)S(1)}, u32[]{:S(2)}, u32[]{:S(2)}) %collective-permute-start.61) | collective-permute-done | bytes 131104 | tf_op jit(solution)/shard_map/ppermute | solution.py:40
  200.1 2.0 collective-permute-start.72
  202.1 2.0 shard_map.126
  206.2 6.3 %collective-permute-done.66 = bf16[64,2048]{1,0:T(8,128)(2,1)S(1)} collective-permute-done((bf16[64,2048]{1,0:T(8,128)(2,1)S(1)}, bf16[64,2048]{1,0:T(8,128)(2,1)S(1)}, u32[]{:S(2)}, u32[]{:S(2)}) %collective-permute-start.66) | collective-permute-done | bytes 262176 | tf_op jit(solution)/shard_map/ppermute | solution.py:40
  212.6 1.9 collective-permute-start.67
  216.9 4.4 %collective-permute-done.68 = bf16[16,2048]{1,0:T(8,128)(2,1)S(1)} collective-permute-done((bf16[16,2048]{1,0:T(8,128)(2,1)S(1)}, bf16[16,2048]{1,0:T(8,128)(2,1)S(1)}, u32[]{:S(2)}, u32[]{:S(2)}) %collective-permute-start.68) | collective-permute-done | bytes 65568 | tf_op jit(solution)/shard_map/ppermute | solution.py:40
  (203 shorter events, 48.2 us)
Async XLA Ops:
  2.3 10.4 %collective-permute-start = (bf16[16,4224]{1,0:T(8,128)(2,1)S(1)}, bf16[16,4224]{1,0:T(8,128)(2,1)S(1)}, u32[]{:S(2)}, u32[]{:S(2)}) collective-permute-start(bf16[16,4224]{1,0:T(8,128)(2,1)S(1)} %maximum_maximum_fusion), channel_id=1, source_target_pairs={{0,8},{1,9},{2,10},{3,11},{4,12},{5,13},{6,14},{7,15},{8,16},{9,17... | collective-permute-start | bytes 405512 | tf_op jit(solution)/shard_map/ppermute | solution.py:40
  5.4 11.5 %collective-permute-start.1 = (bf16[16,4224]{1,0:T(8,128)(2,1)S(1)}, bf16[16,4224]{1,0:T(8,128)(2,1)S(1)}, u32[]{:S(2)}, u32[]{:S(2)}) collective-permute-start(bf16[16,4224]{1,0:T(8,128)(2,1)S(1)} %maximum_maximum_fusion), channel_id=1, source_target_pairs={{0,16},{1,17},{2,18},{3,19},{4,20},{5,21},{6,22},{7,23},{8,24},{9,... | collective-permute-start | bytes 405512 | tf_op jit(solution)/shard_map/ppermute | solution.py:40
  8.0 8.9 %collective-permute-start.2 = (bf16[16,4224]{1,0:T(8,128)(2,1)S(1)}, bf16[16,4224]{1,0:T(8,128)(2,1)S(1)}, u32[]{:S(2)}, u32[]{:S(2)}) collective-permute-start(bf16[16,4224]{1,0:T(8,128)(2,1)S(1)} %maximum_maximum_fusion), channel_id=1, source_target_pairs={{0,24},{1,25},{2,26},{3,27},{4,28},{5,29},{6,30},{7,31},{8,0},{9,1... | collective-permute-start | bytes 405512 | tf_op jit(solution)/shard_map/ppermute | solution.py:40
  9.3 13.1 %collective-permute-start.3 = (bf16[128,2048]{1,0:T(8,128)(2,1)}, bf16[128,2048]{1,0:T(8,128)(2,1)}, u32[]{:S(2)}, u32[]{:S(2)}) collective-permute-start(bf16[128,2048]{1,0:T(8,128)(2,1)} %refs_4_.3), channel_id=1, source_target_pairs={{0,2},{1,3},{2,0},{3,1},{4,6},{5,7},{6,4},{7,5},{8,10},{9,11},{10,... | collective-permute-start | bytes 1572872 | tf_op jit(solution)/shard_map/ppermute | solution.py:40
  10.8 12.9 %collective-permute-start.4 = (bf16[128,2048]{1,0:T(8,128)(2,1)}, bf16[128,2048]{1,0:T(8,128)(2,1)}, u32[]{:S(2)}, u32[]{:S(2)}) collective-permute-start(bf16[128,2048]{1,0:T(8,128)(2,1)} %refs_4_.2), channel_id=1, source_target_pairs={{0,4},{1,5},{2,6},{3,7},{4,0},{5,1},{6,2},{7,3},{8,12},{9,13},{10,... | collective-permute-start | bytes 1572872 | tf_op jit(solution)/shard_map/ppermute | solution.py:40
  23.7 14.3 %collective-permute-start.7 = (bf16[64,4224]{1,0:T(8,128)(2,1)S(1)}, bf16[64,4224]{1,0:T(8,128)(2,1)S(1)}, u32[]{:S(2)}, u32[]{:S(2)}) collective-permute-start(bf16[64,4224]{1,0:T(8,128)(2,1)S(1)} %pad_maximum_fusion.refs_4_), channel_id=1, source_target_pairs={{0,4},{1,5},{2,6},{3,7},{4,0},{5,1},{6,2},{7,3},{8,12},{9,13},{10,... | collective-permute-start | bytes 1622024 | tf_op jit(solution)/shard_map/ppermute | solution.py:40
  25.2 15.2 %collective-permute-start.8 = (bf16[64,4224]{1,0:T(8,128)(2,1)S(1)}, bf16[64,4224]{1,0:T(8,128)(2,1)S(1)}, u32[]{:S(2)}, u32[]{:S(2)}) collective-permute-start(bf16[64,4224]{1,0:T(8,128)(2,1)S(1)} %pad_maximum_fusion.refs_4_), channel_id=1, source_target_pairs={{0,2},{1,3},{2,0},{3,1},{4,6},{5,7},{6,4},{7,5},{8,10},{9,11},{10,... | collective-permute-start | bytes 1622024 | tf_op jit(solution)/shard_map/ppermute | solution.py:40
  25.8 22.7 %collective-permute-start.9 = (bf16[64,4224]{1,0:T(8,128)(2,1)S(1)}, bf16[64,4224]{1,0:T(8,128)(2,1)S(1)}, u32[]{:S(2)}, u32[]{:S(2)}) collective-permute-start(bf16[64,4224]{1,0:T(8,128)(2,1)S(1)} %pad_maximum_fusion.refs_4_), channel_id=1, source_target_pairs={{0,6},{1,7},{2,4},{3,5},{4,2},{5,3},{6,0},{7,1},{8,14},{9,15},{10,... | collective-permute-start | bytes 1622024 | tf_op jit(solution)/shard_map/ppermute | solution.py:40
  52.9 15.0 %collective-permute-start.14 = (bf16[128,2048]{1,0:T(8,128)(2,1)}, bf16[128,2048]{1,0:T(8,128)(2,1)}, u32[]{:S(2)}, u32[]{:S(2)}) collective-permute-start(bf16[128,2048]{1,0:T(8,128)(2,1)} %collective-permute-done.3.refs_6_), channel_id=1, source_target_pairs={{0,1},{1,0},{2,3},{3,2},{4,5},{5,4},{6,7},{7,6},{8,9},{9,8},{10,11... | collective-permute-start | bytes 1572872 | tf_op jit(solution)/shard_map/ppermute | solution.py:40
  53.3 14.7 %collective-permute-start.15 = (bf16[128,2048]{1,0:T(8,128)(2,1)}, bf16[128,2048]{1,0:T(8,128)(2,1)}, u32[]{:S(2)}, u32[]{:S(2)}) collective-permute-start(bf16[128,2048]{1,0:T(8,128)(2,1)} %collective-permute-done.4.refs_6_), channel_id=1, source_target_pairs={{0,1},{1,0},{2,3},{3,2},{4,5},{5,4},{6,7},{7,6},{8,9},{9,8},{10,11... | collective-permute-start | bytes 1572872 | tf_op jit(solution)/shard_map/ppermute | solution.py:40
  54.6 8.3 %collective-permute-start.11 = (bf16[128,512]{1,0:T(8,128)(2,1)S(1)}, bf16[128,512]{1,0:T(8,128)(2,1)S(1)}, u32[]{:S(2)}, u32[]{:S(2)}) collective-permute-start(bf16[128,512]{1,0:T(8,128)(2,1)S(1)} %convolution_convert_fusion.3), channel_id=1, source_target_pairs={{0,8},{1,9},{2,10},{3,11},{4,12},{5,13},{6,14},{7,15},{8,16},{9,17... | collective-permute-start | bytes 393224 | tf_op jit(solution)/shard_map/ppermute | solution.py:40
  55.3 12.6 %collective-permute-start.12 = (bf16[128,512]{1,0:T(8,128)(2,1)S(1)}, bf16[128,512]{1,0:T(8,128)(2,1)S(1)}, u32[]{:S(2)}, u32[]{:S(2)}) collective-permute-start(bf16[128,512]{1,0:T(8,128)(2,1)S(1)} %convolution_convert_fusion.3), channel_id=1, source_target_pairs={{0,16},{1,17},{2,18},{3,19},{4,20},{5,21},{6,22},{7,23},{8,24},{9,... | collective-permute-start | bytes 393224 | tf_op jit(solution)/shard_map/ppermute | solution.py:40
  55.6 12.3 %collective-permute-start.13 = (bf16[128,512]{1,0:T(8,128)(2,1)S(1)}, bf16[128,512]{1,0:T(8,128)(2,1)S(1)}, u32[]{:S(2)}, u32[]{:S(2)}) collective-permute-start(bf16[128,512]{1,0:T(8,128)(2,1)S(1)} %convolution_convert_fusion.3), channel_id=1, source_target_pairs={{0,24},{1,25},{2,26},{3,27},{4,28},{5,29},{6,30},{7,31},{8,0},{9,1... | collective-permute-start | bytes 393224 | tf_op jit(solution)/shard_map/ppermute | solution.py:40
  68.0 12.8 %collective-permute-start.19 = (bf16[512,512]{1,0:T(8,128)(2,1)S(1)}, bf16[512,512]{1,0:T(8,128)(2,1)S(1)}, u32[]{:S(2)}, u32[]{:S(2)}) collective-permute-start(bf16[512,512]{1,0:T(8,128)(2,1)S(1)} %pad_maximum_fusion.1.refs_2_), channel_id=1, source_target_pairs={{0,4},{1,5},{2,6},{3,7},{4,0},{5,1},{6,2},{7,3},{8,12},{9,13},{10,... | collective-permute-start | bytes 1572872 | tf_op jit(solution)/shard_map/ppermute | solution.py:40
  69.6 13.0 %collective-permute-start.20 = (bf16[512,512]{1,0:T(8,128)(2,1)S(1)}, bf16[512,512]{1,0:T(8,128)(2,1)S(1)}, u32[]{:S(2)}, u32[]{:S(2)}) collective-permute-start(bf16[512,512]{1,0:T(8,128)(2,1)S(1)} %pad_maximum_fusion.1.refs_2_), channel_id=1, source_target_pairs={{0,2},{1,3},{2,0},{3,1},{4,6},{5,7},{6,4},{7,5},{8,10},{9,11},{10,... | collective-permute-start | bytes 1572872 | tf_op jit(solution)/shard_map/ppermute | solution.py:40
  70.3 13.1 %collective-permute-start.16 = (bf16[128,512]{1,0:T(8,128)(2,1)S(1)}, bf16[128,512]{1,0:T(8,128)(2,1)S(1)}, u32[]{:S(2)}, u32[]{:S(2)}) collective-permute-start(bf16[128,512]{1,0:T(8,128)(2,1)S(1)} %convolution_convert_fusion.2), channel_id=1, source_target_pairs={{0,8},{1,9},{2,10},{3,11},{4,12},{5,13},{6,14},{7,15},{8,16},{9,17... | collective-permute-start | bytes 393224 | tf_op jit(solution)/shard_map/ppermute | solution.py:40
  73.3 10.1 %collective-permute-start.17 = (bf16[128,512]{1,0:T(8,128)(2,1)S(1)}, bf16[128,512]{1,0:T(8,128)(2,1)S(1)}, u32[]{:S(2)}, u32[]{:S(2)}) collective-permute-start(bf16[128,512]{1,0:T(8,128)(2,1)S(1)} %convolution_convert_fusion.2), channel_id=1, source_target_pairs={{0,16},{1,17},{2,18},{3,19},{4,20},{5,21},{6,22},{7,23},{8,24},{9,... | collective-permute-start | bytes 393224 | tf_op jit(solution)/shard_map/ppermute | solution.py:40
  73.5 10.0 %collective-permute-start.18 = (bf16[128,512]{1,0:T(8,128)(2,1)S(1)}, bf16[128,512]{1,0:T(8,128)(2,1)S(1)}, u32[]{:S(2)}, u32[]{:S(2)}) collective-permute-start(bf16[128,512]{1,0:T(8,128)(2,1)S(1)} %convolution_convert_fusion.2), channel_id=1, source_target_pairs={{0,24},{1,25},{2,26},{3,27},{4,28},{5,29},{6,30},{7,31},{8,0},{9,1... | collective-permute-start | bytes 393224 | tf_op jit(solution)/shard_map/ppermute | solution.py:40
  89.3 8.7 %collective-permute-start.33 = (bf16[512,512]{1,0:T(8,128)(2,1)S(1)}, bf16[512,512]{1,0:T(8,128)(2,1)S(1)}, u32[]{:S(2)}, u32[]{:S(2)}) collective-permute-start(bf16[512,512]{1,0:T(8,128)(2,1)S(1)} %collective-permute-done.19.refs_3_), channel_id=1, source_target_pairs={{0,1},{1,0},{2,3},{3,2},{4,5},{5,4},{6,7},{7,6},{8,9},{9,8},{10,11... | collective-permute-start | bytes 1572872 | tf_op jit(solution)/shard_map/ppermute | solution.py:40
  89.8 8.1 %collective-permute-start.34 = (bf16[512,512]{1,0:T(8,128)(2,1)S(1)}, bf16[512,512]{1,0:T(8,128)(2,1)S(1)}, u32[]{:S(2)}, u32[]{:S(2)}) collective-permute-start(bf16[512,512]{1,0:T(8,128)(2,1)S(1)} %collective-permute-done.20.refs_4_), channel_id=1, source_target_pairs={{0,1},{1,0},{2,3},{3,2},{4,5},{5,4},{6,7},{7,6},{8,9},{9,8},{10,11... | collective-permute-start | bytes 1572872 | tf_op jit(solution)/shard_map/ppermute | solution.py:40
  89.9 8.0 %collective-permute-start.35 = (bf16[512,512]{1,0:T(8,128)(2,1)S(1)}, bf16[512,512]{1,0:T(8,128)(2,1)S(1)}, u32[]{:S(2)}, u32[]{:S(2)}) collective-permute-start(bf16[512,512]{1,0:T(8,128)(2,1)S(1)} %pad_maximum_fusion.3.refs_5_), channel_id=1, source_target_pairs={{0,1},{1,0},{2,3},{3,2},{4,5},{5,4},{6,7},{7,6},{8,9},{9,8},{10,11... | collective-permute-start | bytes 1572872 | tf_op jit(solution)/shard_map/ppermute | solution.py:40
  90.5 14.0 %collective-permute-start.24 = (bf16[512,512]{1,0:T(8,128)(2,1)S(1)}, bf16[512,512]{1,0:T(8,128)(2,1)S(1)}, u32[]{:S(2)}, u32[]{:S(2)}) collective-permute-start(bf16[512,512]{1,0:T(8,128)(2,1)S(1)} %pad_maximum_fusion.2.refs_6_), channel_id=1, source_target_pairs={{0,4},{1,5},{2,6},{3,7},{4,0},{5,1},{6,2},{7,3},{8,12},{9,13},{10,... | collective-permute-start | bytes 1572872 | tf_op jit(solution)/shard_map/ppermute | solution.py:40
  91.4 13.7 %collective-permute-start.26 = (bf16[512,512]{1,0:T(8,128)(2,1)S(1)}, bf16[512,512]{1,0:T(8,128)(2,1)S(1)}, u32[]{:S(2)}, u32[]{:S(2)}) collective-permute-start(bf16[512,512]{1,0:T(8,128)(2,1)S(1)} %pad_maximum_fusion.2.refs_6_), channel_id=1, source_target_pairs={{0,2},{1,3},{2,0},{3,1},{4,6},{5,7},{6,4},{7,5},{8,10},{9,11},{10,... | collective-permute-start | bytes 1572872 | tf_op jit(solution)/shard_map/ppermute | solution.py:40
  103.3 9.6 %collective-permute-start.38 = (bf16[512,512]{1,0:T(8,128)(2,1)S(1)}, bf16[512,512]{1,0:T(8,128)(2,1)S(1)}, u32[]{:S(2)}, u32[]{:S(2)}) collective-permute-start(bf16[512,512]{1,0:T(8,128)(2,1)S(1)} %get-tuple-element.124), channel_id=1, source_target_pairs={{0,1},{1,0},{2,3},{3,2},{4,5},{5,4},{6,7},{7,6},{8,9},{9,8},{10,11... | collective-permute-start | bytes 1572872 | tf_op jit(solution)/shard_map/ppermute | solution.py:40
  105.1 7.7 %collective-permute-start.29 = (bf16[512,256]{1,0:T(8,128)(2,1)S(1)}, bf16[512,256]{1,0:T(8,128)(2,1)S(1)}, u32[]{:S(2)}, u32[]{:S(2)}) collective-permute-start(bf16[512,256]{1,0:T(8,128)(2,1)S(1)} %slice.107), channel_id=1, source_target_pairs={{0,4},{1,5},{2,6},{3,7},{4,0},{5,1},{6,2},{7,3},{8,12},{9,13},{10,... | collective-permute-start | bytes 786440 | tf_op jit(solution)/shard_map/ppermute | solution.py:40
  112.9 18.2 %collective-permute-start.43 = (bf16[256,2048]{1,0:T(8,128)(2,1)S(1)}, bf16[256,2048]{1,0:T(8,128)(2,1)S(1)}, u32[]{:S(2)}, u32[]{:S(2)}) collective-permute-start(bf16[256,2048]{1,0:T(8,128)(2,1)S(1)} %copy-done.3), channel_id=1, source_target_pairs={{0,1},{1,0},{2,3},{3,2},{4,5},{5,4},{6,7},{7,6},{8,9},{9,8},{10,11... | collective-permute-start | bytes 3145736 | tf_op jit(solution)/shard_map/ppermute | solution.py:40
  113.6 17.5 %collective-permute-start.44 = (bf16[256,2048]{1,0:T(8,128)(2,1)S(1)}, bf16[256,2048]{1,0:T(8,128)(2,1)S(1)}, u32[]{:S(2)}, u32[]{:S(2)}) collective-permute-start(bf16[256,2048]{1,0:T(8,128)(2,1)S(1)} %get-tuple-element.140), channel_id=1, source_target_pairs={{0,1},{1,0},{2,3},{3,2},{4,5},{5,4},{6,7},{7,6},{8,9},{9,8},{10,11... | collective-permute-start | bytes 3145736 | tf_op jit(solution)/shard_map/ppermute | solution.py:40
  120.1 19.4 %collective-permute-start.40 = (bf16[512,512]{1,0:T(8,128)(2,1)S(1)}, bf16[512,512]{1,0:T(8,128)(2,1)S(1)}, u32[]{:S(2)}, u32[]{:S(2)}) collective-permute-start(bf16[512,512]{1,0:T(8,128)(2,1)S(1)} %add_convert_fusion.3), channel_id=1, source_target_pairs={{0,6},{1,7},{2,4},{3,5},{4,2},{5,3},{6,0},{7,1},{8,14},{9,15},{10,... | collective-permute-start | bytes 1572872 | tf_op jit(solution)/shard_map/ppermute | solution.py:40
  121.6 24.5 %collective-permute-start.41 = (bf16[512,512]{1,0:T(8,128)(2,1)S(1)}, bf16[512,512]{1,0:T(8,128)(2,1)S(1)}, u32[]{:S(2)}, u32[]{:S(2)}) collective-permute-start(bf16[512,512]{1,0:T(8,128)(2,1)S(1)} %add_convert_fusion.2), channel_id=1, source_target_pairs={{0,4},{1,5},{2,6},{3,7},{4,0},{5,1},{6,2},{7,3},{8,12},{9,13},{10,... | collective-permute-start | bytes 1572872 | tf_op jit(solution)/shard_map/ppermute | solution.py:40
  122.6 23.6 %collective-permute-start.42 = (bf16[512,512]{1,0:T(8,128)(2,1)S(1)}, bf16[512,512]{1,0:T(8,128)(2,1)S(1)}, u32[]{:S(2)}, u32[]{:S(2)}) collective-permute-start(bf16[512,512]{1,0:T(8,128)(2,1)S(1)} %add_convert_fusion.1), channel_id=1, source_target_pairs={{0,2},{1,3},{2,0},{3,1},{4,6},{5,7},{6,4},{7,5},{8,10},{9,11},{10,... | collective-permute-start | bytes 1572872 | tf_op jit(solution)/shard_map/ppermute | solution.py:40
  131.1 22.4 %collective-permute-start.51 = (bf16[512,512]{1,0:T(8,128)(2,1)S(1)}, bf16[512,512]{1,0:T(8,128)(2,1)S(1)}, u32[]{:S(2)}, u32[]{:S(2)}) collective-permute-start(bf16[512,512]{1,0:T(8,128)(2,1)S(1)} %get-tuple-element.153), channel_id=1, source_target_pairs={{0,1},{1,0},{2,3},{3,2},{4,5},{5,4},{6,7},{7,6},{8,9},{9,8},{10,11... | collective-permute-start | bytes 1572872 | tf_op jit(solution)/shard_map/ppermute | solution.py:40
  131.2 15.3 %collective-permute-start.47 = (bf16[512,512]{1,0:T(8,128)(2,1)S(1)}, bf16[512,512]{1,0:T(8,128)(2,1)S(1)}, u32[]{:S(2)}, u32[]{:S(2)}) collective-permute-start(bf16[512,512]{1,0:T(8,128)(2,1)S(1)} %get-tuple-element.150), channel_id=1, source_target_pairs={{0,1},{1,0},{2,3},{3,2},{4,5},{5,4},{6,7},{7,6},{8,9},{9,8},{10,11... | collective-permute-start | bytes 1572872 | tf_op jit(solution)/shard_map/ppermute | solution.py:40
  151.7 13.8 %collective-permute-start.49 = (bf16[128,512]{1,0:T(8,128)(2,1)S(1)}, bf16[128,512]{1,0:T(8,128)(2,1)S(1)}, u32[]{:S(2)}, u32[]{:S(2)}) collective-permute-start(bf16[128,512]{1,0:T(8,128)(2,1)S(1)} %get-tuple-element.185), channel_id=1, source_target_pairs={{0,16},{1,17},{2,18},{3,19},{4,20},{5,21},{6,22},{7,23},{8,24},{9,... | collective-permute-start | bytes 393224 | tf_op jit(solution)/shard_map/ppermute | solution.py:40
  153.5 11.9 %collective-permute-start.50 = (bf16[128,512]{1,0:T(8,128)(2,1)S(1)}, bf16[128,512]{1,0:T(8,128)(2,1)S(1)}, u32[]{:S(2)}, u32[]{:S(2)}) collective-permute-start(bf16[128,512]{1,0:T(8,128)(2,1)S(1)} %get-tuple-element.184), channel_id=1, source_target_pairs={{0,8},{1,9},{2,10},{3,11},{4,12},{5,13},{6,14},{7,15},{8,16},{9,17... | collective-permute-start | bytes 393224 | tf_op jit(solution)/shard_map/ppermute | solution.py:40
  153.7 12.2 %collective-permute-start.52 = (bf16[512,256]{1,0:T(8,128)(2,1)S(1)}, bf16[512,256]{1,0:T(8,128)(2,1)S(1)}, u32[]{:S(2)}, u32[]{:S(2)}) collective-permute-start(bf16[512,256]{1,0:T(8,128)(2,1)S(1)} %get-tuple-element.182), channel_id=1, source_target_pairs={{0,2},{1,3},{2,0},{3,1},{4,6},{5,7},{6,4},{7,5},{8,10},{9,11},{10,... | collective-permute-start | bytes 786440 | tf_op jit(solution)/shard_map/ppermute | solution.py:40
  154.8 11.2 %collective-permute-start.53 = (bf16[512,256]{1,0:T(8,128)(2,1)S(1)}, bf16[512,256]{1,0:T(8,128)(2,1)S(1)}, u32[]{:S(2)}, u32[]{:S(2)}) collective-permute-start(bf16[512,256]{1,0:T(8,128)(2,1)S(1)} %get-tuple-element.181), channel_id=1, source_target_pairs={{0,4},{1,5},{2,6},{3,7},{4,0},{5,1},{6,2},{7,3},{8,12},{9,13},{10,... | collective-permute-start | bytes 786440 | tf_op jit(solution)/shard_map/ppermute | solution.py:40
  166.1 13.9 %collective-permute-start.57 = (bf16[512,512]{1,0:T(8,128)(2,1)S(1)}, bf16[512,512]{1,0:T(8,128)(2,1)S(1)}, u32[]{:S(2)}, u32[]{:S(2)}) collective-permute-start(bf16[512,512]{1,0:T(8,128)(2,1)S(1)} %pad_maximum_fusion.4), channel_id=1, source_target_pairs={{0,4},{1,5},{2,6},{3,7},{4,0},{5,1},{6,2},{7,3},{8,12},{9,13},{10,... | collective-permute-start | bytes 1572872 | tf_op jit(solution)/shard_map/ppermute | solution.py:40
  167.0 13.0 %collective-permute-start.58 = (bf16[512,512]{1,0:T(8,128)(2,1)S(1)}, bf16[512,512]{1,0:T(8,128)(2,1)S(1)}, u32[]{:S(2)}, u32[]{:S(2)}) collective-permute-start(bf16[512,512]{1,0:T(8,128)(2,1)S(1)} %pad_maximum_fusion.5), channel_id=1, source_target_pairs={{0,2},{1,3},{2,0},{3,1},{4,6},{5,7},{6,4},{7,5},{8,10},{9,11},{10,... | collective-permute-start | bytes 1572872 | tf_op jit(solution)/shard_map/ppermute | solution.py:40
  168.2 12.1 %collective-permute-start.54 = (bf16[128,128]{1,0:T(8,128)(2,1)S(1)}, bf16[128,128]{1,0:T(8,128)(2,1)S(1)}, u32[]{:S(2)}, u32[]{:S(2)}) collective-permute-start(bf16[128,128]{1,0:T(8,128)(2,1)S(1)} %get-tuple-element.200), channel_id=1, source_target_pairs={{0,1},{1,0},{2,3},{3,2},{4,5},{5,4},{6,7},{7,6},{8,9},{9,8},{10,11... | collective-permute-start | bytes 98312 | tf_op jit(solution)/shard_map/ppermute | solution.py:40
  168.3 12.1 %collective-permute-start.55 = (bf16[128,128]{1,0:T(8,128)(2,1)S(1)}, bf16[128,128]{1,0:T(8,128)(2,1)S(1)}, u32[]{:S(2)}, u32[]{:S(2)}) collective-permute-start(bf16[128,128]{1,0:T(8,128)(2,1)S(1)} %get-tuple-element.199), channel_id=1, source_target_pairs={{0,4},{1,5},{2,6},{3,7},{4,0},{5,1},{6,2},{7,3},{8,12},{9,13},{10,... | collective-permute-start | bytes 98312 | tf_op jit(solution)/shard_map/ppermute | solution.py:40
  169.5 10.9 %collective-permute-start.56 = (bf16[128,128]{1,0:T(8,128)(2,1)S(1)}, bf16[128,128]{1,0:T(8,128)(2,1)S(1)}, u32[]{:S(2)}, u32[]{:S(2)}) collective-permute-start(bf16[128,128]{1,0:T(8,128)(2,1)S(1)} %get-tuple-element.198), channel_id=1, source_target_pairs={{0,5},{1,4},{2,7},{3,6},{4,1},{5,0},{6,3},{7,2},{8,13},{9,12},{10,... | collective-permute-start | bytes 98312 | tf_op jit(solution)/shard_map/ppermute | solution.py:40
  180.5 13.3 %collective-permute-start.61 = (bf16[128,512]{1,0:T(8,128)(2,1)S(1)}, bf16[128,512]{1,0:T(8,128)(2,1)S(1)}, u32[]{:S(2)}, u32[]{:S(2)}) collective-permute-start(bf16[128,512]{1,0:T(8,128)(2,1)S(1)} %get-tuple-element.180), channel_id=1, source_target_pairs={{0,16},{1,17},{2,18},{3,19},{4,20},{5,21},{6,22},{7,23},{8,24},{9,... | collective-permute-start | bytes 393224 | tf_op jit(solution)/shard_map/ppermute | solution.py:40
  181.7 12.2 %collective-permute-start.62 = (bf16[128,512]{1,0:T(8,128)(2,1)S(1)}, bf16[128,512]{1,0:T(8,128)(2,1)S(1)}, u32[]{:S(2)}, u32[]{:S(2)}) collective-permute-start(bf16[128,512]{1,0:T(8,128)(2,1)S(1)} %get-tuple-element.179), channel_id=1, source_target_pairs={{0,8},{1,9},{2,10},{3,11},{4,12},{5,13},{6,14},{7,15},{8,16},{9,17... | collective-permute-start | bytes 393224 | tf_op jit(solution)/shard_map/ppermute | solution.py:40
  185.6 8.7 %collective-permute-start.59 = (bf16[64,2048]{1,0:T(8,128)(2,1)S(1)}, bf16[64,2048]{1,0:T(8,128)(2,1)S(1)}, u32[]{:S(2)}, u32[]{:S(2)}) collective-permute-start(bf16[64,2048]{1,0:T(8,128)(2,1)S(1)} %get-tuple-element.166), channel_id=1, source_target_pairs={{0,2},{1,3},{2,0},{3,1},{4,6},{5,7},{6,4},{7,5},{8,10},{9,11},{10,... | collective-permute-start | bytes 786440 | tf_op jit(solution)/shard_map/ppermute | solution.py:40
  194.4 20.5 %collective-permute-start.70 = (bf16[16,2048]{1,0:T(8,128)(2,1)S(1)}, bf16[16,2048]{1,0:T(8,128)(2,1)S(1)}, u32[]{:S(2)}, u32[]{:S(2)}) collective-permute-start(bf16[16,2048]{1,0:T(8,128)(2,1)S(1)} %get-tuple-element.186), channel_id=1, source_target_pairs={{0,24},{1,25},{2,26},{3,27},{4,28},{5,29},{6,30},{7,31},{8,0},{9,1... | collective-permute-start | bytes 196616 | tf_op jit(solution)/shard_map/ppermute | solution.py:40
  195.5 20.2 %collective-permute-start.71 = (bf16[16,2048]{1,0:T(8,128)(2,1)S(1)}, bf16[16,2048]{1,0:T(8,128)(2,1)S(1)}, u32[]{:S(2)}, u32[]{:S(2)}) collective-permute-start(bf16[16,2048]{1,0:T(8,128)(2,1)S(1)} %get-tuple-element.188), channel_id=1, source_target_pairs={{0,16},{1,17},{2,18},{3,19},{4,20},{5,21},{6,22},{7,23},{8,24},{9,... | collective-permute-start | bytes 196616 | tf_op jit(solution)/shard_map/ppermute | solution.py:40
  200.1 15.6 %collective-permute-start.72 = (bf16[16,2048]{1,0:T(8,128)(2,1)S(1)}, bf16[16,2048]{1,0:T(8,128)(2,1)S(1)}, u32[]{:S(2)}, u32[]{:S(2)}) collective-permute-start(bf16[16,2048]{1,0:T(8,128)(2,1)S(1)} %get-tuple-element.187), channel_id=1, source_target_pairs={{0,8},{1,9},{2,10},{3,11},{4,12},{5,13},{6,14},{7,15},{8,16},{9,17... | collective-permute-start | bytes 196616 | tf_op jit(solution)/shard_map/ppermute | solution.py:40
  204.2 8.3 %collective-permute-start.66 = (bf16[64,2048]{1,0:T(8,128)(2,1)S(1)}, bf16[64,2048]{1,0:T(8,128)(2,1)S(1)}, u32[]{:S(2)}, u32[]{:S(2)}) collective-permute-start(bf16[64,2048]{1,0:T(8,128)(2,1)S(1)} %get-tuple-element.174), channel_id=1, source_target_pairs={{0,4},{1,5},{2,6},{3,7},{4,0},{5,1},{6,2},{7,3},{8,12},{9,13},{10,... | collective-permute-start | bytes 786440 | tf_op jit(solution)/shard_map/ppermute | solution.py:40
  (37 other events, 330.7 us)

commit v8 on v7

--- a/solution.py
+++ b/solution.py
@@ -268,11 +268,10 @@
 
 
 def forward_kernel(*refs):
-    slot_ref, scale_ref, *quarters = refs[:6]
-    hbm_weights = refs[6:9]
-    targets = refs[9:13]
-    rows, hidden, results, gate_ref, up_ref, down_ref, arrived = refs[13:]
+    slot_ref, scale_ref, *refs = refs
+    rows, hidden, results, gate_ref, up_ref, down_ref, arrived = refs[-7:]
     experts, groups, slots, _ = results.shape
+    quarters, hbm_weights, targets = refs[:groups], refs[groups : groups + 3], refs[groups + 3 : -7]
     width = hidden.shape[1]
     chunk = 256
     for expert in range(experts):
@@ -302,12 +301,11 @@
 
 
 def backward_kernel(*refs):
-    slot_ref, scale_ref, *quarters = refs[:6]
-    quarter_grads = refs[6:10]
-    hbm_weights = refs[10:13]
-    targets = refs[13:17]
-    rows, grads, gate_grads, value_grads, results, gate_ref, up_ref, down_ref, arrived = refs[17:]
+    slot_ref, scale_ref, *refs = refs
+    rows, grads, gate_grads, value_grads, results, gate_ref, up_ref, down_ref, arrived = refs[-9:]
     experts, groups, slots, _ = results.shape
+    quarters, quarter_grads = refs[:groups], refs[groups : 2 * groups]
+    hbm_weights, targets = refs[2 * groups : 2 * groups + 3], refs[2 * groups + 3 : -9]
     width = gate_grads.shape[1]
     chunk = 256
     for expert in range(experts):
@@ -342,31 +340,68 @@
     spread_rows(slot_ref, None, results, targets)
 
 
-def expert_call(kernel, products, buffers, plan, quarters, weights):
+def expert_call(kernel, plan, quarters, weights, slot_count, grads=None):
     slots, scales = plan
     experts, latent_width, width = weights[0].shape
     groups, _, _, span = slots.shape
-    operands = (slots, scales) + tuple(quarters) + tuple(weights)
-    whole = pl.BlockSpec(memory_space=pltpu.VMEM)
-    picked = buffers[0].shape[0]
-    scratch = list(buffers) + [
-        pltpu.VMEM((experts, groups, picked // groups, latent_width), jnp.bfloat16),
+    picked = groups * slot_count
+    narrow = pltpu.VMEM((picked, latent_width), jnp.bfloat16)
+    wide = pltpu.VMEM((picked, width), jnp.bfloat16)
+    products = 3
+    scratch = [narrow, wide]
+    operands = (slots, scales) + tuple(quarters)
+    if grads is not None:
+        products = 5
+        scratch = [narrow, narrow, wide, wide]
+        operands = operands + tuple(grads)
+    operands = operands + tuple(weights)
+    scratch = scratch + [
+        pltpu.VMEM((experts, groups, slot_count, latent_width), jnp.bfloat16),
         *[pltpu.VMEM(weight.shape, jnp.bfloat16) for weight in weights],
         pltpu.SemaphoreType.DMA((3, experts)),
     ]
+    whole = pl.BlockSpec(memory_space=pltpu.VMEM)
     return pl.pallas_call(
         kernel,
         out_shape=(jax.ShapeDtypeStruct((span, latent_width), jnp.bfloat16),) * groups,
         in_specs=[whole] * (len(operands) - 3) + [pl.BlockSpec(memory_space=pl.ANY)] * 3,
         out_specs=(whole,) * groups,
         scratch_shapes=scratch,
-        compiler_params=pltpu.CompilerParams(vmem_limit_bytes=36 << 20),
+        compiler_params=pltpu.CompilerParams(vmem_limit_bytes=32 << 20),
         cost_estimate=pl.CostEstimate(
             flops=2 * products * experts * picked * latent_width * width,
             bytes_accessed=2 * sum(array.size for array in operands),
             transcendentals=experts * picked * width,
         ),
     )(*operands)
+
+
+STAGES = ((0,), (1, 2), (3,))
+
+
+def stage_sums(kernel, plans, near, far, weights, slot_count, stage, grads=None):
+    plan = [
+        lax.concatenate(
+            [plans[side][part][index : index + 1] for side in (0, 1) for index in stage], 0
+        )
+        for part in (0, 1)
+    ]
+    return expert_call(
+        kernel,
+        plan,
+        [side[index] for side in (near, far) for index in stage],
+        weights,
+        slot_count,
+        None if grads is None else [side[index] for side in grads for index in stage],
+    )
+
+
+def by_quarter(stages):
+    near, far = [], []
+    for sums in stages:
+        near.extend(sums[: len(sums) // 2])
+        far.extend(sums[len(sums) // 2 :])
+    return near, far
 
 
 def expert_plans(told, local_experts, row_count):
@@ -389,11 +424,11 @@
     slots = jnp.where(member, ranking + offset, -1)
     scales = fixed.astype(jnp.float32) / 256.0
 
-    def by_quarter(values):
+    def in_quarters(values):
         values = values.reshape(2, 4, depth, local_experts, row_count).transpose(0, 1, 3, 2, 4)
         return values.reshape(2, 4, local_experts, 1, depth * row_count)
 
-    slots, scales = by_quarter(slots), by_quarter(scales)
+    slots, scales = in_quarters(slots), in_quarters(scales)
     return [(slots[core], scales[core]) for core in (0, 1)], depth * capacity
 
 
@@ -412,10 +447,8 @@
     sent = [down_proj, up_proj]
     if ride:
         sent.append(told.reshape(rows, -1))
-    next_tokens, next_grads = shifted(tokens, OWNERS, X), shifted(out_grad, OWNERS, Y)
-    own = gather_depth(lax.concatenate(sent, 1), OWNERS)
-    own, next_tokens, next_grads, later_tokens, later_grads = tied(
-        own, next_tokens, next_grads, tokens, out_grad
+    own, later_tokens, later_grads = tied(
+        gather_depth(lax.concatenate(sent, 1), OWNERS), tokens, out_grad
     )
     quarters = gather_chips(own, OWNERS, Y, X)
     other_tokens = shifted(later_tokens, OWNERS, CORE)
@@ -429,12 +462,11 @@
         told_near = lax.concatenate(
             list(gather_chips(gather_depth(told, EXPERT), EXPERT, Y, X)), 0
         )
-    latent, next_tokens, next_grads, told_near = tied(latent, next_tokens, next_grads, told_near)
+    latent, later_tokens, later_grads, told_near = tied(latent, tokens, out_grad, told_near)
     latent_own = gather_depth(latent, EXPERT)
-    last_tokens = shifted(next_tokens, OWNERS, CORE)
-    last_grads = shifted(next_grads, OWNERS, CORE)
-    latent_own, last_tokens, last_grads, mix_grad = tied(
-        latent_own, last_tokens, last_grads, mix_grad
+    next_tokens, next_grads = shifted(later_tokens, OWNERS, X), shifted(later_grads, OWNERS, Y)
+    latent_own, next_tokens, next_grads, mix_grad = tied(
+        latent_own, next_tokens, next_grads, mix_grad
     )
     near = (latent_own, shifted(latent_own, EXPERT, Y), shifted(latent_own, EXPERT, X))
     mix_own = gather_depth(mix_grad, EXPERT)
@@ -442,30 +474,38 @@
     plans, slot_count = expert_plans(
         lax.concatenate([told_near, told_far], 0), local_experts, row_count
     )
-    mix_own, near = tied(mix_own, gather_chips_by_turns(near, EXPERT, Y, X))
-    far = tuple(shifted(part, EXPERT, CORE) for part in near)
+    mix_own, near = tied(mix_own, near)
+    near = gather_chips_by_turns(near, EXPERT, Y, X)
+    far = tuple(shifted(part, EXPERT, CORE) for part in near[:3])
     near_grad = (mix_own, shifted(mix_own, EXPERT, Y), shifted(mix_own, EXPERT, X))
-
-    narrow = pltpu.VMEM((4 * slot_count, latent_width), jnp.bfloat16)
-    wide = pltpu.VMEM((4 * slot_count, width), jnp.bfloat16)
+    near_grad = gather_chips_by_turns(near_grad, EXPERT, Y, X)
+
     weights = (expert_gate, expert_up, expert_down)
-    scratch = (narrow, narrow, wide, wide)
-    forward_near = expert_call(forward_kernel, 3, (narrow, wide), plans[0], near, weights)
-    forward_near, far, down_near, up_near = tied(forward_near, far, down_near, up_near)
-    near_grad = gather_chips_by_turns(near_grad, EXPERT, Y, X)
-    forward_far = expert_call(forward_kernel, 3, (narrow, wide), plans[1], far, weights)
+    shared = (weights, slot_count)
+    first_sums = stage_sums(forward_kernel, plans, near, far, *shared, STAGES[0])
+    last_near, first_sums = tied(near[3], first_sums)
+    far = far + (shifted(last_near, EXPERT, CORE),)
+    forward = [first_sums] + [
+        stage_sums(forward_kernel, plans, near, far, *shared, stage) for stage in STAGES[1:]
+    ]
+    forward_near, forward_far = by_quarter(forward)
+    forward_far, near_grad, later_near, next_tokens, next_grads = tied(
+        forward_far, near_grad, (down_near, up_near), next_tokens, next_grads
+    )
     far_grad = tuple(shifted(part, EXPERT, CORE) for part in near_grad)
-    down_far = shifted(down_near, OWNERS, CORE)
-    up_far = shifted(up_near, OWNERS, CORE)
+    down_far = shifted(later_near[0], OWNERS, CORE)
+    up_far = shifted(later_near[1], OWNERS, CORE)
+    last_tokens = shifted(next_tokens, OWNERS, CORE)
+    last_grads = shifted(next_grads, OWNERS, CORE)
     across, along_y, along_x, own = core_totals(forward_near, forward_far)
     forward_sums = [part.astype(jnp.bfloat16) for part in (across, along_y, along_x)] + [own]
-    far_grad, forward_sums = tied(far_grad, forward_sums)
-    backward_far = expert_call(
-        backward_kernel, 5, scratch, plans[1], far + tuple(far_grad), weights
-    )
-    near_grad, backward_far, down_far, up_far = tied(near_grad, backward_far, down_far, up_far)
-    backward_near = expert_call(
-        backward_kernel, 5, scratch, plans[0], near + tuple(near_grad), weights
+    backward_near, backward_far = by_quarter(
+        [
+            stage_sums(
+                backward_kernel, plans, near, far, *shared, stage, (near_grad, far_grad)
+            )
+            for stage in STAGES
+        ]
     )
     quad_tokens = (tokens, other_tokens, next_tokens, last_tokens)
     quad_grads = (out_grad, other_grads, next_grads, last_grads)
@@ -473,13 +513,14 @@
     mixed_sums = chip_totals(*forward_sums)
     backward_across, *backward_sums = core_totals(backward_near, backward_far)
     backward_across = across_by_turns(backward_across)
-    mixed_sums, backward_sums = tied(mixed_sums, backward_sums)
+    mixed_sums, backward_across, backward_sums = tied(
+        mixed_sums, backward_across, backward_sums
+    )
     mixed_rows = tensor_total(depth_total(mixed_sums, EXPERT)).astype(jnp.bfloat16)
     mixed_relative = matmul(mixed_rows, up_place, ((1,), (1,))).astype(jnp.bfloat16)
-    mixed_relative, backward_across = tied(mixed_relative, backward_across)
     latent_sums = chip_totals_by_turns(*backward_across, *backward_sums)
+    mixed_relative, latent_sums = tied(mixed_relative, latent_sums)
     quad = quad_columns(mixed_relative, Y)
-    quad, latent_sums = tied(quad, latent_sums)
     latent_grad = tensor_total(depth_total(latent_sums, EXPERT)).astype(jnp.bfloat16)
     up_sent, up_kept = quad_grads_of(quad, quad_grads)
     up_sums = up_kept + shifted(up_sent, OWNERS, X).astype(jnp.float32)

time: 222 us -> 226 us (1.018)
  waiting for transfers between devices: 109 us -> 115 us
  Pallas kernels: 31.4 us -> 35.1 us
  starting transfers between devices: 64.5 us -> 61.9 us
    ppermute x73, waiting for transfers between devices: 109 us -> 115 us  [shifted(): return lax.ppermute(block, axes, pairs)]
    pallas_call x4 -> x6, Pallas kernels: 25.9 us -> 30.8 us  [expert_call(): pl.pallas_call(kernel, out_shape=(jax.ShapeDtypeStruct((span, latent_widt...]
    ppermute x73, starting transfers between devices: 64.5 us -> 61.9 us  [shifted(): return lax.ppermute(block, axes, pairs)]
  transfers between devices with their start and end apart: 73 -> 73, of which waited for: 33 -> 33; matrix products, arithmetic and copies ran while one was open for 5% -> 4% of each run, Pallas kernels for 13% -> 13%
where the time goes in v8:
time: 226 us; the launch traced here: 225 us
  waiting for transfers between devices  115 us (51%)
  starting transfers between devices  61.9 us (27%)
  Pallas kernels  35.1 us (16%)
  other arithmetic  6.67 us (3%)
  matrix products  4.61 us (2%)
    ppermute x73, waiting for transfers between devices, shifted(): return lax.ppermute(block, axes, pairs)  115 us
    ppermute x73, starting transfers between devices, shifted(): return lax.ppermute(block, axes, pairs)  61.9 us
    pallas_call x6, Pallas kernels, expert_call(): pl.pallas_call(kernel, out_shape=(jax.ShapeDtypeStruct((span, latent_widt...  30.8 us
  transfers between devices with their start and end apart: 73, of which 33 were waited for; matrix products, arithmetic and copies ran while one was open for 4% of the time, Pallas kernels for 13%

profile of v8, /device:TPU:0, one launch (start us, length us, event | category | flops | bytes accessed | tf_op | source)
XLA Modules:
  0.0 225.4 jit_solution(13486965050599315015)
XLA Ops:
  2.3 5.1 %collective-permute-start.2 = (bf16[16,4224]{1,0:T(8,128)(2,1)S(1)}, bf16[16,4224]{1,0:T(8,128)(2,1)S(1)}, u32[]{:S(2)}, u32[]{:S(2)}) collective-permute-start(bf16[16,4224]{1,0:T(8,128)(2,1)S(1)} %maximum_maximum_fusion), channel_id=1, source_target_pairs={{0,24},{1,25},{2,26},{3,27},{4,28},{5,29},{6,30},{7,31},{8,0},{9,1... | collective-permute-start | bytes 405512 | tf_op jit(solution)/shard_map/ppermute | solution.py:40
  8.8 2.7 %collective-permute-done.2 = bf16[16,4224]{1,0:T(8,128)(2,1)S(1)} collective-permute-done((bf16[16,4224]{1,0:T(8,128)(2,1)S(1)}, bf16[16,4224]{1,0:T(8,128)(2,1)S(1)}, u32[]{:S(2)}, u32[]{:S(2)}) %collective-permute-start.2) | collective-permute-done | bytes 135200 | tf_op jit(solution)/shard_map/ppermute | solution.py:40
  11.4 7.5 %collective-permute-done.1 = bf16[16,4224]{1,0:T(8,128)(2,1)S(1)} collective-permute-done((bf16[16,4224]{1,0:T(8,128)(2,1)S(1)}, bf16[16,4224]{1,0:T(8,128)(2,1)S(1)}, u32[]{:S(2)}, u32[]{:S(2)}) %collective-permute-start.1) | collective-permute-done | bytes 135200 | tf_op jit(solution)/shard_map/ppermute | solution.py:40
  19.9 2.5 %collective-permute-start.7 = (bf16[64,4224]{1,0:T(8,128)(2,1)S(1)}, bf16[64,4224]{1,0:T(8,128)(2,1)S(1)}, u32[]{:S(2)}, u32[]{:S(2)}) collective-permute-start(bf16[64,4224]{1,0:T(8,128)(2,1)S(1)} %pad_maximum_fusion.refs_4_), channel_id=1, source_target_pairs={{0,6},{1,7},{2,4},{3,5},{4,2},{5,3},{6,0},{7,1},{8,14},{9,15},{10,... | collective-permute-start | bytes 1622024 | tf_op jit(solution)/shard_map/ppermute | solution.py:40
  26.1 10.0 %collective-permute-done.7.refs_7_ = bf16[64,4224]{1,0:T(8,128)(2,1)S(1)} collective-permute-done((bf16[64,4224]{1,0:T(8,128)(2,1)S(1)}, bf16[64,4224]{1,0:T(8,128)(2,1)S(1)}, u32[]{:S(2)}, u32[]{:S(2)}) %collective-permute-start.7) | collective-permute-done | bytes 540704 | tf_op jit(solution)/shard_map/ppermute | solution.py:40
  36.1 10.1 %collective-permute-done.6.refs_6_ = bf16[64,4224]{1,0:T(8,128)(2,1)} collective-permute-done((bf16[64,4224]{1,0:T(8,128)(2,1)S(1)}, bf16[64,4224]{1,0:T(8,128)(2,1)}, u32[]{:S(2)}, u32[]{:S(2)}) %collective-permute-start.6) | collective-permute-done | bytes 540704 | tf_op jit(solution)/shard_map/ppermute | solution.py:40
  46.2 2.8 %shard_map.120 = (bf16[256,2048]{1,0:T(8,128)(2,1)S(1)}, bf16[256,2048]{1,0:T(8,128)(2,1)S(1)}, bf16[256,128]{1,0:T(8,128)(2,1)S(1)}, bf16[128,512]{1,0:T(8,128)(2,1)S(1)}, bf16[128,512]{1,0:T(8,128)(2,1)S(1)}) custom-call(bf16[128,2048]{1,0:T(8,128)(2,1)S(1)} %copy-done.4, bf16[128,2048]{1,0:T(8,128)(2,1)S(1)} %collective-permute-done.3.refs_1_.refs_5_, ...), custom_call_target="tpu_custom_call" | custom-call | flops 536870912 | bytes 4259840 | tf_op jit(solution)/shard_map/pallas_call | solution.py:138
  51.4 2.1 collective-permute-start.10
  53.5 1.9 collective-permute-start.9
  55.4 1.5 collective-permute-start.12
  57.3 1.5 collective-permute-start.13
  59.4 6.2 %collective-permute-done.10 = bf16[128,512]{1,0:T(8,128)(2,1)S(1)} collective-permute-done((bf16[128,512]{1,0:T(8,128)(2,1)S(1)}, bf16[128,512]{1,0:T(8,128)(2,1)S(1)}, u32[]{:S(2)}, u32[]{:S(2)}) %collective-permute-start.10) | collective-permute-done | bytes 131104 | tf_op jit(solution)/shard_map/ppermute | solution.py:40
  65.7 4.1 %collective-permute-done.12.refs_6_ = bf16[128,2048]{1,0:T(8,128)(2,1)S(1)} collective-permute-done((bf16[128,2048]{1,0:T(8,128)(2,1)S(1)}, bf16[128,2048]{1,0:T(8,128)(2,1)S(1)}, u32[]{:S(2)}, u32[]{:S(2)}) %collective-permute-start.12) | collective-permute-done | bytes 524320 | tf_op jit(solution)/shard_map/ppermute | solution.py:40
  69.7 1.7 collective-permute-done.13.refs_6_
  72.1 1.4 collective-permute-start.17
  73.6 1.9 collective-permute-start.16
  76.1 3.3 %collective-permute-done.16 = bf16[128,512]{1,0:T(8,128)(2,1)S(1)} collective-permute-done((bf16[128,512]{1,0:T(8,128)(2,1)S(1)}, bf16[128,512]{1,0:T(8,128)(2,1)S(1)}, u32[]{:S(2)}, u32[]{:S(2)}) %collective-permute-start.16) | collective-permute-done | bytes 131104 | tf_op jit(solution)/shard_map/ppermute | solution.py:40
  79.4 7.0 %collective-permute-done.15 = bf16[128,512]{1,0:T(8,128)(2,1)S(1)} collective-permute-done((bf16[128,512]{1,0:T(8,128)(2,1)S(1)}, bf16[128,512]{1,0:T(8,128)(2,1)S(1)}, u32[]{:S(2)}, u32[]{:S(2)}) %collective-permute-start.15) | collective-permute-done | bytes 131104 | tf_op jit(solution)/shard_map/ppermute | solution.py:40
  90.8 5.1 %collective-permute-done.20 = bf16[512,256]{1,0:T(8,128)(2,1)S(1)} collective-permute-done((bf16[512,256]{1,0:T(8,128)(2,1)S(1)}, bf16[512,256]{1,0:T(8,128)(2,1)S(1)}, u32[]{:S(2)}, u32[]{:S(2)}) %collective-permute-start.20) | collective-permute-done | bytes 262176 | tf_op jit(solution)/shard_map/ppermute | solution.py:40
  96.6 3.7 %shard_map.121 = (bf16[512,512]{1,0:T(8,128)(2,1)S(1)}, bf16[512,512]{1,0:T(8,128)(2,1)S(1)}) custom-call(s32[2,2,1,512]{3,2,1,0:T(1,128)S(1)} %pad_add_fusion.1.refs_0_, f32[2,2,1,512]{3,2,1,0:T(1,128)S(1)} %pad_maximum_fusion.8.refs_1_, bf16[512,512]{1,0:T(8,128)(2,1)S(1)} %pad_maximum_fusion.1.refs_2_, ...), custom_call_target="tpu_custom_call" | custom-call | flops 1207959552 | bytes 7348224 | tf_op jit(solution)/shard_map/pallas_call | solution.py:364
  100.9 4.9 %collective-permute-done.27.refs_7_ = bf16[512,512]{1,0:T(8,128)(2,1)S(1)} collective-permute-done((bf16[512,512]{1,0:T(8,128)(2,1)S(1)}, bf16[512,512]{1,0:T(8,128)(2,1)S(1)}, u32[]{:S(2)}, u32[]{:S(2)}) %collective-permute-start.27) | collective-permute-done | bytes 524320 | tf_op jit(solution)/shard_map/ppermute | solution.py:40
  105.8 1.5 collective-permute-start.29
  107.3 1.5 collective-permute-start.28
  108.8 5.3 %shard_map.122 = (bf16[512,512]{1,0:T(8,128)(2,1)S(1)}, bf16[512,512]{1,0:T(8,128)(2,1)S(1)}, bf16[512,512]{1,0:T(8,128)(2,1)S(1)}, bf16[512,512]{1,0:T(8,128)(2,1)S(1)}) custom-call(s32[4,2,1,512]{3,2,1,0:T(1,128)S(1)} %pad_add_fusion.refs_0_, f32[4,2,1,512]{3,2,1,0:T(1,128)S(1)} %pad_maximum_fusion.7.refs_1_, ...), custom_call_target="tpu_custom_call" | custom-call | flops 2415919104 | bytes 8404992 | tf_op jit(solution)/shard_map/pallas_call | solution.py:364
  114.2 3.5 %shard_map.123 = (bf16[512,512]{1,0:T(8,128)(2,1)S(1)}, bf16[512,512]{1,0:T(8,128)(2,1)S(1)}) custom-call(s32[2,2,1,512]{3,2,1,0:T(1,128)S(1)} %pad_add_fusion.2.refs_0_, f32[2,2,1,512]{3,2,1,0:T(1,128)S(1)} %pad_maximum_fusion.9.refs_1_, bf16[512,512]{1,0:T(8,128)(2,1)S(1)} %constant_dynamic-update-slice_fusion.refs_2_, ...), custom_call_target="tpu_custom_call" | custom-call | flops 1207959552 | bytes 7348224 | tf_op jit(solution)/shard_map/pallas_call | solution.py:364
  120.6 7.5 %shard_map.125 = (bf16[512,512]{1,0:T(8,128)(2,1)S(1)}, bf16[512,512]{1,0:T(8,128)(2,1)S(1)}, bf16[512,512]{1,0:T(8,128)(2,1)S(1)}, bf16[512,512]{1,0:T(8,128)(2,1)S(1)}) custom-call(s32[4,2,1,512]{3,2,1,0:T(1,128)S(1)} %pad_add_fusion.refs_0_, f32[4,2,1,512]{3,2,1,0:T(1,128)S(1)} %pad_maximum_fusion.7.refs_1_, ...), custom_call_target="tpu_custom_call" | custom-call | flops 4026531840 | bytes 10502144 | tf_op jit(solution)/shard_map/pallas_call | solution.py:364
  130.0 5.2 %shard_map.124 = (bf16[512,512]{1,0:T(8,128)(2,1)S(1)}, bf16[512,512]{1,0:T(8,128)(2,1)S(1)}) custom-call(s32[2,2,1,512]{3,2,1,0:T(1,128)S(1)} %pad_add_fusion.2.refs_0_, f32[2,2,1,512]{3,2,1,0:T(1,128)S(1)} %pad_maximum_fusion.9.refs_1_, bf16[512,512]{1,0:T(8,128)(2,1)S(1)} %constant_dynamic-update-slice_fusion.refs_2_, ...), custom_call_target="tpu_custom_call" | custom-call | flops 2013265920 | bytes 8396800 | tf_op jit(solution)/shard_map/pallas_call | solution.py:364
  135.3 1.5 collective-permute-start.34
  136.8 5.5 %shard_map.126 = (bf16[512,512]{1,0:T(8,128)(2,1)S(1)}, bf16[512,512]{1,0:T(8,128)(2,1)S(1)}) custom-call(s32[2,2,1,512]{3,2,1,0:T(1,128)S(1)} %pad_add_fusion.1.refs_0_, f32[2,2,1,512]{3,2,1,0:T(1,128)S(1)} %pad_maximum_fusion.8.refs_1_, bf16[512,512]{1,0:T(8,128)(2,1)S(1)} %pad_maximum_fusion.1.refs_2_, ...), custom_call_target="tpu_custom_call" | custom-call | flops 2013265920 | bytes 8396800 | tf_op jit(solution)/shard_map/pallas_call | solution.py:364
  147.4 7.5 %collective-permute-done.34 = bf16[512,512]{1,0:T(8,128)(2,1)S(1)} collective-permute-done((bf16[512,512]{1,0:T(8,128)(2,1)S(1)}, bf16[512,512]{1,0:T(8,128)(2,1)S(1)}, u32[]{:S(2)}, u32[]{:S(2)}) %collective-permute-start.34) | collective-permute-done | bytes 524320 | tf_op jit(solution)/shard_map/ppermute | solution.py:40
  154.9 4.1 %collective-permute-done.36 = bf16[512,512]{1,0:T(8,128)(2,1)S(1)} collective-permute-done((bf16[512,512]{1,0:T(8,128)(2,1)S(1)}, bf16[512,512]{1,0:T(8,128)(2,1)S(1)}, u32[]{:S(2)}, u32[]{:S(2)}) %collective-permute-start.36) | collective-permute-done | bytes 524320 | tf_op jit(solution)/shard_map/ppermute | solution.py:40
  160.5 3.4 %collective-permute-done.39 = bf16[512,256]{1,0:T(8,128)(2,1)S(1)} collective-permute-done((bf16[512,256]{1,0:T(8,128)(2,1)S(1)}, bf16[512,256]{1,0:T(8,128)(2,1)S(1)}, u32[]{:S(2)}, u32[]{:S(2)}) %collective-permute-start.39) | collective-permute-done | bytes 262176 | tf_op jit(solution)/shard_map/ppermute | solution.py:40
  166.4 1.8 collective-permute-start.49
  168.2 1.5 collective-permute-start.48
  169.7 3.4 %collective-permute-done.47 = bf16[128,512]{1,0:T(8,128)(2,1)S(1)} collective-permute-done((bf16[128,512]{1,0:T(8,128)(2,1)S(1)}, bf16[128,512]{1,0:T(8,128)(2,1)S(1)}, u32[]{:S(2)}, u32[]{:S(2)}) %collective-permute-start.47) | collective-permute-done | bytes 131104 | tf_op jit(solution)/shard_map/ppermute | solution.py:40
  173.2 2.4 %collective-permute-done.49 = bf16[128,512]{1,0:T(8,128)(2,1)S(1)} collective-permute-done((bf16[128,512]{1,0:T(8,128)(2,1)S(1)}, bf16[128,512]{1,0:T(8,128)(2,1)S(1)}, u32[]{:S(2)}, u32[]{:S(2)}) %collective-permute-start.49) | collective-permute-done | bytes 131104 | tf_op jit(solution)/shard_map/ppermute | solution.py:40
  175.6 3.5 %collective-permute-done.48 = bf16[128,512]{1,0:T(8,128)(2,1)S(1)} collective-permute-done((bf16[128,512]{1,0:T(8,128)(2,1)S(1)}, bf16[128,512]{1,0:T(8,128)(2,1)S(1)}, u32[]{:S(2)}, u32[]{:S(2)}) %collective-permute-start.48) | collective-permute-done | bytes 131104 | tf_op jit(solution)/shard_map/ppermute | solution.py:40
  179.9 1.9 collective-permute-start.57
  182.5 1.5 collective-permute-start.53
  184.0 2.2 collective-permute-done.54.refs_3_
  187.1 1.8 collective-permute-done.52.refs_1_
  191.3 1.5 collective-permute-done.58
  193.2 4.9 %collective-permute-done.56 = bf16[64,2048]{1,0:T(8,128)(2,1)S(1)} collective-permute-done((bf16[64,2048]{1,0:T(8,128)(2,1)S(1)}, bf16[64,2048]{1,0:T(8,128)(2,1)S(1)}, u32[]{:S(2)}, u32[]{:S(2)}) %collective-permute-start.56) | collective-permute-done | bytes 262176 | tf_op jit(solution)/shard_map/ppermute | solution.py:40
  201.7 3.2 %collective-permute-start.70 = (bf16[16,2048]{1,0:T(8,128)(2,1)S(1)}, bf16[16,2048]{1,0:T(8,128)(2,1)S(1)}, u32[]{:S(2)}, u32[]{:S(2)}) collective-permute-start(bf16[16,2048]{1,0:T(8,128)(2,1)S(1)} %get-tuple-element.146), channel_id=1, source_target_pairs={{0,24},{1,25},{2,26},{3,27},{4,28},{5,29},{6,30},{7,31},{8,0},{9,1... | collective-permute-start | bytes 196616 | tf_op jit(solution)/shard_map/ppermute | solution.py:40
  205.8 1.5 collective-permute-start.71
  210.4 5.5 %collective-permute-done.66 = bf16[64,2048]{1,0:T(8,128)(2,1)S(1)} collective-permute-done((bf16[64,2048]{1,0:T(8,128)(2,1)S(1)}, bf16[64,2048]{1,0:T(8,128)(2,1)S(1)}, u32[]{:S(2)}, u32[]{:S(2)}) %collective-permute-start.66) | collective-permute-done | bytes 262176 | tf_op jit(solution)/shard_map/ppermute | solution.py:40
  216.0 2.6 %collective-permute-start.67 = (bf16[16,2048]{1,0:T(8,128)(2,1)S(1)}, bf16[16,2048]{1,0:T(8,128)(2,1)S(1)}, u32[]{:S(2)}, u32[]{:S(2)}) collective-permute-start(bf16[16,2048]{1,0:T(8,128)(2,1)S(1)} %get-tuple-element.149), channel_id=1, source_target_pairs={{0,24},{1,25},{2,26},{3,27},{4,28},{5,29},{6,30},{7,31},{8,0},{9,1... | collective-permute-start | bytes 196616 | tf_op jit(solution)/shard_map/ppermute | solution.py:40
  221.1 3.6 %collective-permute-done.69 = bf16[16,2048]{1,0:T(8,128)(2,1)S(1)} collective-permute-done((bf16[16,2048]{1,0:T(8,128)(2,1)S(1)}, bf16[16,2048]{1,0:T(8,128)(2,1)S(1)}, u32[]{:S(2)}, u32[]{:S(2)}) %collective-permute-start.69) | collective-permute-done | bytes 65568 | tf_op jit(solution)/shard_map/ppermute | solution.py:40
  (194 shorter events, 47.7 us)
Async XLA Ops:
  2.3 9.1 %collective-permute-start.2 = (bf16[16,4224]{1,0:T(8,128)(2,1)S(1)}, bf16[16,4224]{1,0:T(8,128)(2,1)S(1)}, u32[]{:S(2)}, u32[]{:S(2)}) collective-permute-start(bf16[16,4224]{1,0:T(8,128)(2,1)S(1)} %maximum_maximum_fusion), channel_id=1, source_target_pairs={{0,24},{1,25},{2,26},{3,27},{4,28},{5,29},{6,30},{7,31},{8,0},{9,1... | collective-permute-start | bytes 405512 | tf_op jit(solution)/shard_map/ppermute | solution.py:40
  7.4 11.5 %collective-permute-start.1 = (bf16[16,4224]{1,0:T(8,128)(2,1)S(1)}, bf16[16,4224]{1,0:T(8,128)(2,1)S(1)}, u32[]{:S(2)}, u32[]{:S(2)}) collective-permute-start(bf16[16,4224]{1,0:T(8,128)(2,1)S(1)} %maximum_maximum_fusion), channel_id=1, source_target_pairs={{0,16},{1,17},{2,18},{3,19},{4,20},{5,21},{6,22},{7,23},{8,24},{9,... | collective-permute-start | bytes 405512 | tf_op jit(solution)/shard_map/ppermute | solution.py:40
  7.4 11.5 %collective-permute-start = (bf16[16,4224]{1,0:T(8,128)(2,1)S(1)}, bf16[16,4224]{1,0:T(8,128)(2,1)S(1)}, u32[]{:S(2)}, u32[]{:S(2)}) collective-permute-start(bf16[16,4224]{1,0:T(8,128)(2,1)S(1)} %maximum_maximum_fusion), channel_id=1, source_target_pairs={{0,8},{1,9},{2,10},{3,11},{4,12},{5,13},{6,14},{7,15},{8,16},{9,17... | collective-permute-start | bytes 405512 | tf_op jit(solution)/shard_map/ppermute | solution.py:40
  19.9 16.2 %collective-permute-start.7 = (bf16[64,4224]{1,0:T(8,128)(2,1)S(1)}, bf16[64,4224]{1,0:T(8,128)(2,1)S(1)}, u32[]{:S(2)}, u32[]{:S(2)}) collective-permute-start(bf16[64,4224]{1,0:T(8,128)(2,1)S(1)} %pad_maximum_fusion.refs_4_), channel_id=1, source_target_pairs={{0,6},{1,7},{2,4},{3,5},{4,2},{5,3},{6,0},{7,1},{8,14},{9,15},{10,... | collective-permute-start | bytes 1622024 | tf_op jit(solution)/shard_map/ppermute | solution.py:40
  22.4 23.8 %collective-permute-start.6 = (bf16[64,4224]{1,0:T(8,128)(2,1)S(1)}, bf16[64,4224]{1,0:T(8,128)(2,1)}, u32[]{:S(2)}, u32[]{:S(2)}) collective-permute-start(bf16[64,4224]{1,0:T(8,128)(2,1)S(1)} %pad_maximum_fusion.refs_4_), channel_id=1, source_target_pairs={{0,2},{1,3},{2,0},{3,1},{4,6},{5,7},{6,4},{7,5},{8,10},{9,11},{10,... | collective-permute-start | bytes 1622024 | tf_op jit(solution)/shard_map/ppermute | solution.py:40
  22.9 23.2 %collective-permute-start.5 = (bf16[64,4224]{1,0:T(8,128)(2,1)S(1)}, bf16[64,4224]{1,0:T(8,128)(2,1)}, u32[]{:S(2)}, u32[]{:S(2)}) collective-permute-start(bf16[64,4224]{1,0:T(8,128)(2,1)S(1)} %pad_maximum_fusion.refs_4_), channel_id=1, source_target_pairs={{0,4},{1,5},{2,6},{3,7},{4,0},{5,1},{6,2},{7,3},{8,12},{9,13},{10,... | collective-permute-start | bytes 1622024 | tf_op jit(solution)/shard_map/ppermute | solution.py:40
  51.4 14.2 %collective-permute-start.10 = (bf16[128,512]{1,0:T(8,128)(2,1)S(1)}, bf16[128,512]{1,0:T(8,128)(2,1)S(1)}, u32[]{:S(2)}, u32[]{:S(2)}) collective-permute-start(bf16[128,512]{1,0:T(8,128)(2,1)S(1)} %convolution_convert_fusion.3), channel_id=1, source_target_pairs={{0,16},{1,17},{2,18},{3,19},{4,20},{5,21},{6,22},{7,23},{8,24},{9,... | collective-permute-start | bytes 393224 | tf_op jit(solution)/shard_map/ppermute | solution.py:40
  53.5 12.2 %collective-permute-start.9 = (bf16[128,512]{1,0:T(8,128)(2,1)S(1)}, bf16[128,512]{1,0:T(8,128)(2,1)S(1)}, u32[]{:S(2)}, u32[]{:S(2)}) collective-permute-start(bf16[128,512]{1,0:T(8,128)(2,1)S(1)} %convolution_convert_fusion.3), channel_id=1, source_target_pairs={{0,8},{1,9},{2,10},{3,11},{4,12},{5,13},{6,14},{7,15},{8,16},{9,17... | collective-permute-start | bytes 393224 | tf_op jit(solution)/shard_map/ppermute | solution.py:40
  55.4 14.3 %collective-permute-start.12 = (bf16[128,2048]{1,0:T(8,128)(2,1)S(1)}, bf16[128,2048]{1,0:T(8,128)(2,1)S(1)}, u32[]{:S(2)}, u32[]{:S(2)}) collective-permute-start(bf16[128,2048]{1,0:T(8,128)(2,1)S(1)} %copy-done.4), channel_id=1, source_target_pairs={{0,2},{1,3},{2,0},{3,1},{4,6},{5,7},{6,4},{7,5},{8,10},{9,11},{10,... | collective-permute-start | bytes 1572872 | tf_op jit(solution)/shard_map/ppermute | solution.py:40
  57.3 14.1 %collective-permute-start.13 = (bf16[128,2048]{1,0:T(8,128)(2,1)S(1)}, bf16[128,2048]{1,0:T(8,128)(2,1)S(1)}, u32[]{:S(2)}, u32[]{:S(2)}) collective-permute-start(bf16[128,2048]{1,0:T(8,128)(2,1)S(1)} %copy-done.3), channel_id=1, source_target_pairs={{0,4},{1,5},{2,6},{3,7},{4,0},{5,1},{6,2},{7,3},{8,12},{9,13},{10,... | collective-permute-start | bytes 1572872 | tf_op jit(solution)/shard_map/ppermute | solution.py:40
  71.4 15.1 %collective-permute-start.18 = (bf16[512,512]{1,0:T(8,128)(2,1)S(1)}, bf16[512,512]{1,0:T(8,128)(2,1)S(1)}, u32[]{:S(2)}, u32[]{:S(2)}) collective-permute-start(bf16[512,512]{1,0:T(8,128)(2,1)S(1)} %pad_maximum_fusion.1.refs_2_), channel_id=1, source_target_pairs={{0,2},{1,3},{2,0},{3,1},{4,6},{5,7},{6,4},{7,5},{8,10},{9,11},{10,... | collective-permute-start | bytes 1572872 | tf_op jit(solution)/shard_map/ppermute | solution.py:40
  72.1 14.4 %collective-permute-start.17 = (bf16[512,512]{1,0:T(8,128)(2,1)S(1)}, bf16[512,512]{1,0:T(8,128)(2,1)S(1)}, u32[]{:S(2)}, u32[]{:S(2)}) collective-permute-start(bf16[512,512]{1,0:T(8,128)(2,1)S(1)} %pad_maximum_fusion.1.refs_2_), channel_id=1, source_target_pairs={{0,4},{1,5},{2,6},{3,7},{4,0},{5,1},{6,2},{7,3},{8,12},{9,13},{10,... | collective-permute-start | bytes 1572872 | tf_op jit(solution)/shard_map/ppermute | solution.py:40
  75.5 11.0 %collective-permute-start.15 = (bf16[128,512]{1,0:T(8,128)(2,1)S(1)}, bf16[128,512]{1,0:T(8,128)(2,1)S(1)}, u32[]{:S(2)}, u32[]{:S(2)}) collective-permute-start(bf16[128,512]{1,0:T(8,128)(2,1)S(1)} %convolution_convert_fusion.2), channel_id=1, source_target_pairs={{0,16},{1,17},{2,18},{3,19},{4,20},{5,21},{6,22},{7,23},{8,24},{9,... | collective-permute-start | bytes 393224 | tf_op jit(solution)/shard_map/ppermute | solution.py:40
  75.5 11.0 %collective-permute-start.14 = (bf16[128,512]{1,0:T(8,128)(2,1)S(1)}, bf16[128,512]{1,0:T(8,128)(2,1)S(1)}, u32[]{:S(2)}, u32[]{:S(2)}) collective-permute-start(bf16[128,512]{1,0:T(8,128)(2,1)S(1)} %convolution_convert_fusion.2), channel_id=1, source_target_pairs={{0,8},{1,9},{2,10},{3,11},{4,12},{5,13},{6,14},{7,15},{8,16},{9,17... | collective-permute-start | bytes 393224 | tf_op jit(solution)/shard_map/ppermute | solution.py:40
  86.6 9.3 %collective-permute-start.20 = (bf16[512,256]{1,0:T(8,128)(2,1)S(1)}, bf16[512,256]{1,0:T(8,128)(2,1)S(1)}, u32[]{:S(2)}, u32[]{:S(2)}) collective-permute-start(bf16[512,256]{1,0:T(8,128)(2,1)S(1)} %slice.203), channel_id=1, source_target_pairs={{0,4},{1,5},{2,6},{3,7},{4,0},{5,1},{6,2},{7,3},{8,12},{9,13},{10,... | collective-permute-start | bytes 786440 | tf_op jit(solution)/shard_map/ppermute | solution.py:40
  87.3 9.2 %collective-permute-start.19 = (bf16[512,256]{1,0:T(8,128)(2,1)S(1)}, bf16[512,256]{1,0:T(8,128)(2,1)S(1)}, u32[]{:S(2)}, u32[]{:S(2)}) collective-permute-start(bf16[512,256]{1,0:T(8,128)(2,1)S(1)} %slice.202), channel_id=1, source_target_pairs={{0,2},{1,3},{2,0},{3,1},{4,6},{5,7},{6,4},{7,5},{8,10},{9,11},{10,... | collective-permute-start | bytes 786440 | tf_op jit(solution)/shard_map/ppermute | solution.py:40
  88.6 17.1 %collective-permute-start.27 = (bf16[512,512]{1,0:T(8,128)(2,1)S(1)}, bf16[512,512]{1,0:T(8,128)(2,1)S(1)}, u32[]{:S(2)}, u32[]{:S(2)}) collective-permute-start(bf16[512,512]{1,0:T(8,128)(2,1)S(1)} %pad_maximum_fusion.2.refs_4_), channel_id=1, source_target_pairs={{0,2},{1,3},{2,0},{3,1},{4,6},{5,7},{6,4},{7,5},{8,10},{9,11},{10,... | collective-permute-start | bytes 1572872 | tf_op jit(solution)/shard_map/ppermute | solution.py:40
  89.4 17.9 %collective-permute-start.26 = (bf16[512,512]{1,0:T(8,128)(2,1)S(1)}, bf16[512,512]{1,0:T(8,128)(2,1)S(1)}, u32[]{:S(2)}, u32[]{:S(2)}) collective-permute-start(bf16[512,512]{1,0:T(8,128)(2,1)S(1)} %pad_maximum_fusion.2.refs_4_), channel_id=1, source_target_pairs={{0,4},{1,5},{2,6},{3,7},{4,0},{5,1},{6,2},{7,3},{8,12},{9,13},{10,... | collective-permute-start | bytes 1572872 | tf_op jit(solution)/shard_map/ppermute | solution.py:40
  95.9 12.9 %collective-permute-start.23 = (bf16[512,512]{1,0:T(8,128)(2,1)S(1)}, bf16[512,512]{1,0:T(8,128)(2,1)S(1)}, u32[]{:S(2)}, u32[]{:S(2)}) collective-permute-start(bf16[512,512]{1,0:T(8,128)(2,1)S(1)} %collective-permute-done.17.refs_2_), channel_id=1, source_target_pairs={{0,1},{1,0},{2,3},{3,2},{4,5},{5,4},{6,7},{7,6},{8,9},{9,8},{10,11... | collective-permute-start | bytes 1572872 | tf_op jit(solution)/shard_map/ppermute | solution.py:40
  96.5 12.3 %collective-permute-start.24 = (bf16[512,512]{1,0:T(8,128)(2,1)S(1)}, bf16[512,512]{1,0:T(8,128)(2,1)S(1)}, u32[]{:S(2)}, u32[]{:S(2)}) collective-permute-start(bf16[512,512]{1,0:T(8,128)(2,1)S(1)} %collective-permute-done.18.refs_3_), channel_id=1, source_target_pairs={{0,1},{1,0},{2,3},{3,2},{4,5},{5,4},{6,7},{7,6},{8,9},{9,8},{10,11... | collective-permute-start | bytes 1572872 | tf_op jit(solution)/shard_map/ppermute | solution.py:40
  100.3 13.9 %collective-permute-start.25 = (bf16[512,512]{1,0:T(8,128)(2,1)S(1)}, bf16[512,512]{1,0:T(8,128)(2,1)S(1)}, u32[]{:S(2)}, u32[]{:S(2)}) collective-permute-start(bf16[512,512]{1,0:T(8,128)(2,1)S(1)} %constant_dynamic-update-slice_fusion.refs_2_), channel_id=1, source_target_pairs={{0,1},{1,0},{2,3},{3,2},{4,5},{5,4},{6,7},{7,6},{8,9},{9,8},{10,11... | collective-permute-start | bytes 1572872 | tf_op jit(solution)/shard_map/ppermute | solution.py:40
  118.3 9.8 %collective-permute-start.31 = (bf16[512,512]{1,0:T(8,128)(2,1)S(1)}, bf16[512,512]{1,0:T(8,128)(2,1)S(1)}, u32[]{:S(2)}, u32[]{:S(2)}) collective-permute-start(bf16[512,512]{1,0:T(8,128)(2,1)S(1)} %get-tuple-element.100), channel_id=1, source_target_pairs={{0,1},{1,0},{2,3},{3,2},{4,5},{5,4},{6,7},{7,6},{8,9},{9,8},{10,11... | collective-permute-start | bytes 1572872 | tf_op jit(solution)/shard_map/ppermute | solution.py:40
  118.4 27.3 %collective-permute-start.30 = (bf16[512,512]{1,0:T(8,128)(2,1)S(1)}, bf16[512,512]{1,0:T(8,128)(2,1)S(1)}, u32[]{:S(2)}, u32[]{:S(2)}) collective-permute-start(bf16[512,512]{1,0:T(8,128)(2,1)S(1)} %get-tuple-element.98), channel_id=1, source_target_pairs={{0,1},{1,0},{2,3},{3,2},{4,5},{5,4},{6,7},{7,6},{8,9},{9,8},{10,11... | collective-permute-start | bytes 1572872 | tf_op jit(solution)/shard_map/ppermute | solution.py:40
  118.8 9.9 %collective-permute-start.33 = (bf16[512,512]{1,0:T(8,128)(2,1)S(1)}, bf16[512,512]{1,0:T(8,128)(2,1)S(1)}, u32[]{:S(2)}, u32[]{:S(2)}) collective-permute-start(bf16[512,512]{1,0:T(8,128)(2,1)S(1)} %get-tuple-element.102), channel_id=1, source_target_pairs={{0,1},{1,0},{2,3},{3,2},{4,5},{5,4},{6,7},{7,6},{8,9},{9,8},{10,11... | collective-permute-start | bytes 1572872 | tf_op jit(solution)/shard_map/ppermute | solution.py:40
  119.7 22.6 %collective-permute-start.35 = (bf16[512,512]{1,0:T(8,128)(2,1)S(1)}, bf16[512,512]{1,0:T(8,128)(2,1)S(1)}, u32[]{:S(2)}, u32[]{:S(2)}) collective-permute-start(bf16[512,512]{1,0:T(8,128)(2,1)S(1)} %get-tuple-element.104), channel_id=1, source_target_pairs={{0,1},{1,0},{2,3},{3,2},{4,5},{5,4},{6,7},{7,6},{8,9},{9,8},{10,11... | collective-permute-start | bytes 1572872 | tf_op jit(solution)/shard_map/ppermute | solution.py:40
  120.4 9.5 %collective-permute-start.37 = (bf16[512,512]{1,0:T(8,128)(2,1)S(1)}, bf16[512,512]{1,0:T(8,128)(2,1)S(1)}, u32[]{:S(2)}, u32[]{:S(2)}) collective-permute-start(bf16[512,512]{1,0:T(8,128)(2,1)S(1)} %pad_maximum_fusion.3.refs_4_), channel_id=1, source_target_pairs={{0,1},{1,0},{2,3},{3,2},{4,5},{5,4},{6,7},{7,6},{8,9},{9,8},{10,11... | collective-permute-start | bytes 1572872 | tf_op jit(solution)/shard_map/ppermute | solution.py:40
  128.7 17.7 %collective-permute-start.32 = (bf16[512,512]{1,0:T(8,128)(2,1)S(1)}, bf16[512,512]{1,0:T(8,128)(2,1)S(1)}, u32[]{:S(2)}, u32[]{:S(2)}) collective-permute-start(bf16[512,512]{1,0:T(8,128)(2,1)S(1)} %add_convert_fusion.3), channel_id=1, source_target_pairs={{0,6},{1,7},{2,4},{3,5},{4,2},{5,3},{6,0},{7,1},{8,14},{9,15},{10,... | collective-permute-start | bytes 1572872 | tf_op jit(solution)/shard_map/ppermute | solution.py:40
  130.0 12.7 %collective-permute-start.43 = (bf16[512,512]{1,0:T(8,128)(2,1)S(1)}, bf16[512,512]{1,0:T(8,128)(2,1)S(1)}, u32[]{:S(2)}, u32[]{:S(2)}) collective-permute-start(bf16[512,512]{1,0:T(8,128)(2,1)S(1)} %get-tuple-element.111), channel_id=1, source_target_pairs={{0,1},{1,0},{2,3},{3,2},{4,5},{5,4},{6,7},{7,6},{8,9},{9,8},{10,11... | collective-permute-start | bytes 1572872 | tf_op jit(solution)/shard_map/ppermute | solution.py:40
  135.3 19.6 %collective-permute-start.34 = (bf16[512,512]{1,0:T(8,128)(2,1)S(1)}, bf16[512,512]{1,0:T(8,128)(2,1)S(1)}, u32[]{:S(2)}, u32[]{:S(2)}) collective-permute-start(bf16[512,512]{1,0:T(8,128)(2,1)S(1)} %add_convert_fusion.2), channel_id=1, source_target_pairs={{0,4},{1,5},{2,6},{3,7},{4,0},{5,1},{6,2},{7,3},{8,12},{9,13},{10,... | collective-permute-start | bytes 1572872 | tf_op jit(solution)/shard_map/ppermute | solution.py:40
  144.3 14.8 %collective-permute-start.36 = (bf16[512,512]{1,0:T(8,128)(2,1)S(1)}, bf16[512,512]{1,0:T(8,128)(2,1)S(1)}, u32[]{:S(2)}, u32[]{:S(2)}) collective-permute-start(bf16[512,512]{1,0:T(8,128)(2,1)S(1)} %add_convert_fusion.1), channel_id=1, source_target_pairs={{0,2},{1,3},{2,0},{3,1},{4,6},{5,7},{6,4},{7,5},{8,10},{9,11},{10,... | collective-permute-start | bytes 1572872 | tf_op jit(solution)/shard_map/ppermute | solution.py:40
  145.4 13.9 %collective-permute-start.46 = (bf16[512,512]{1,0:T(8,128)(2,1)S(1)}, bf16[512,512]{1,0:T(8,128)(2,1)S(1)}, u32[]{:S(2)}, u32[]{:S(2)}) collective-permute-start(bf16[512,512]{1,0:T(8,128)(2,1)S(1)} %get-tuple-element.116), channel_id=1, source_target_pairs={{0,1},{1,0},{2,3},{3,2},{4,5},{5,4},{6,7},{7,6},{8,9},{9,8},{10,11... | collective-permute-start | bytes 1572872 | tf_op jit(solution)/shard_map/ppermute | solution.py:40
  145.7 14.8 %collective-permute-start.40 = (bf16[512,256]{1,0:T(8,128)(2,1)S(1)}, bf16[512,256]{1,0:T(8,128)(2,1)S(1)}, u32[]{:S(2)}, u32[]{:S(2)}) collective-permute-start(bf16[512,256]{1,0:T(8,128)(2,1)S(1)} %get-tuple-element.144), channel_id=1, source_target_pairs={{0,4},{1,5},{2,6},{3,7},{4,0},{5,1},{6,2},{7,3},{8,12},{9,13},{10,... | collective-permute-start | bytes 786440 | tf_op jit(solution)/shard_map/ppermute | solution.py:40
  146.4 17.5 %collective-permute-start.39 = (bf16[512,256]{1,0:T(8,128)(2,1)S(1)}, bf16[512,256]{1,0:T(8,128)(2,1)S(1)}, u32[]{:S(2)}, u32[]{:S(2)}) collective-permute-start(bf16[512,256]{1,0:T(8,128)(2,1)S(1)} %get-tuple-element.145), channel_id=1, source_target_pairs={{0,2},{1,3},{2,0},{3,1},{4,6},{5,7},{6,4},{7,5},{8,10},{9,11},{10,... | collective-permute-start | bytes 786440 | tf_op jit(solution)/shard_map/ppermute | solution.py:40
  164.3 15.2 %collective-permute-start.51 = (bf16[512,512]{1,0:T(8,128)(2,1)S(1)}, bf16[512,512]{1,0:T(8,128)(2,1)S(1)}, u32[]{:S(2)}, u32[]{:S(2)}) collective-permute-start(bf16[512,512]{1,0:T(8,128)(2,1)S(1)} %pad_maximum_fusion.5), channel_id=1, source_target_pairs={{0,2},{1,3},{2,0},{3,1},{4,6},{5,7},{6,4},{7,5},{8,10},{9,11},{10,... | collective-permute-start | bytes 1572872 | tf_op jit(solution)/shard_map/ppermute | solution.py:40
  165.4 14.1 %collective-permute-start.50 = (bf16[512,512]{1,0:T(8,128)(2,1)S(1)}, bf16[512,512]{1,0:T(8,128)(2,1)S(1)}, u32[]{:S(2)}, u32[]{:S(2)}) collective-permute-start(bf16[512,512]{1,0:T(8,128)(2,1)S(1)} %pad_maximum_fusion.4), channel_id=1, source_target_pairs={{0,4},{1,5},{2,6},{3,7},{4,0},{5,1},{6,2},{7,3},{8,12},{9,13},{10,... | collective-permute-start | bytes 1572872 | tf_op jit(solution)/shard_map/ppermute | solution.py:40
  166.4 9.1 %collective-permute-start.49 = (bf16[128,512]{1,0:T(8,128)(2,1)S(1)}, bf16[128,512]{1,0:T(8,128)(2,1)S(1)}, u32[]{:S(2)}, u32[]{:S(2)}) collective-permute-start(bf16[128,512]{1,0:T(8,128)(2,1)S(1)} %get-tuple-element.142), channel_id=1, source_target_pairs={{0,8},{1,9},{2,10},{3,11},{4,12},{5,13},{6,14},{7,15},{8,16},{9,17... | collective-permute-start | bytes 393224 | tf_op jit(solution)/shard_map/ppermute | solution.py:40
  168.2 10.9 %collective-permute-start.48 = (bf16[128,512]{1,0:T(8,128)(2,1)S(1)}, bf16[128,512]{1,0:T(8,128)(2,1)S(1)}, u32[]{:S(2)}, u32[]{:S(2)}) collective-permute-start(bf16[128,512]{1,0:T(8,128)(2,1)S(1)} %get-tuple-element.143), channel_id=1, source_target_pairs={{0,16},{1,17},{2,18},{3,19},{4,20},{5,21},{6,22},{7,23},{8,24},{9,... | collective-permute-start | bytes 393224 | tf_op jit(solution)/shard_map/ppermute | solution.py:40
  173.2 9.3 %collective-permute-start.55 = (bf16[128,2048]{1,0:T(8,128)(2,1)S(1)}, bf16[128,2048]{1,0:T(8,128)(2,1)S(1)}, u32[]{:S(2)}, u32[]{:S(2)}) collective-permute-start(bf16[128,2048]{1,0:T(8,128)(2,1)S(1)} %collective-permute-done.13.refs_6_), channel_id=1, source_target_pairs={{0,1},{1,0},{2,3},{3,2},{4,5},{5,4},{6,7},{7,6},{8,9},{9,8},{10,11... | collective-permute-start | bytes 1572872 | tf_op jit(solution)/shard_map/ppermute | solution.py:40
  179.9 10.9 %collective-permute-start.57 = (bf16[128,512]{1,0:T(8,128)(2,1)S(1)}, bf16[128,512]{1,0:T(8,128)(2,1)S(1)}, u32[]{:S(2)}, u32[]{:S(2)}) collective-permute-start(bf16[128,512]{1,0:T(8,128)(2,1)S(1)} %get-tuple-element.138), channel_id=1, source_target_pairs={{0,24},{1,25},{2,26},{3,27},{4,28},{5,29},{6,30},{7,31},{8,0},{9,1... | collective-permute-start | bytes 393224 | tf_op jit(solution)/shard_map/ppermute | solution.py:40
  181.8 9.0 %collective-permute-start.59 = (bf16[128,512]{1,0:T(8,128)(2,1)S(1)}, bf16[128,512]{1,0:T(8,128)(2,1)S(1)}, u32[]{:S(2)}, u32[]{:S(2)}) collective-permute-start(bf16[128,512]{1,0:T(8,128)(2,1)S(1)} %get-tuple-element.139), channel_id=1, source_target_pairs={{0,8},{1,9},{2,10},{3,11},{4,12},{5,13},{6,14},{7,15},{8,16},{9,17... | collective-permute-start | bytes 393224 | tf_op jit(solution)/shard_map/ppermute | solution.py:40
  182.0 10.8 %collective-permute-start.58 = (bf16[128,512]{1,0:T(8,128)(2,1)S(1)}, bf16[128,512]{1,0:T(8,128)(2,1)S(1)}, u32[]{:S(2)}, u32[]{:S(2)}) collective-permute-start(bf16[128,512]{1,0:T(8,128)(2,1)S(1)} %get-tuple-element.140), channel_id=1, source_target_pairs={{0,16},{1,17},{2,18},{3,19},{4,20},{5,21},{6,22},{7,23},{8,24},{9,... | collective-permute-start | bytes 393224 | tf_op jit(solution)/shard_map/ppermute | solution.py:40
  186.2 13.2 %collective-permute-start.60 = (bf16[256,2048]{1,0:T(8,128)(2,1)S(1)}, bf16[256,2048]{1,0:T(8,128)(2,1)S(1)}, u32[]{:S(2)}, u32[]{:S(2)}) collective-permute-start(bf16[256,2048]{1,0:T(8,128)(2,1)S(1)} %get-tuple-element.129), channel_id=1, source_target_pairs={{0,1},{1,0},{2,3},{3,2},{4,5},{5,4},{6,7},{7,6},{8,9},{9,8},{10,11... | collective-permute-start | bytes 3145736 | tf_op jit(solution)/shard_map/ppermute | solution.py:40
  190.8 14.4 %collective-permute-start.65 = (bf16[128,2048]{1,0:T(8,128)(2,1)S(1)}, bf16[128,2048]{1,0:T(8,128)(2,1)S(1)}, u32[]{:S(2)}, u32[]{:S(2)}) collective-permute-start(bf16[128,2048]{1,0:T(8,128)(2,1)S(1)} %collective-permute-done.12.refs_6_), channel_id=1, source_target_pairs={{0,1},{1,0},{2,3},{3,2},{4,5},{5,4},{6,7},{7,6},{8,9},{9,8},{10,11... | collective-permute-start | bytes 1572872 | tf_op jit(solution)/shard_map/ppermute | solution.py:40
  190.8 10.9 %collective-permute-start.61 = (bf16[256,2048]{1,0:T(8,128)(2,1)S(1)}, bf16[256,2048]{1,0:T(8,128)(2,1)S(1)}, u32[]{:S(2)}, u32[]{:S(2)}) collective-permute-start(bf16[256,2048]{1,0:T(8,128)(2,1)S(1)} %get-tuple-element.131), channel_id=1, source_target_pairs={{0,1},{1,0},{2,3},{3,2},{4,5},{5,4},{6,7},{7,6},{8,9},{9,8},{10,11... | collective-permute-start | bytes 3145736 | tf_op jit(solution)/shard_map/ppermute | solution.py:40
  198.3 9.1 %collective-permute-start.63 = (bf16[128,128]{1,0:T(8,128)(2,1)S(1)}, bf16[128,128]{1,0:T(8,128)(2,1)S(1)}, u32[]{:S(2)}, u32[]{:S(2)}) collective-permute-start(bf16[128,128]{1,0:T(8,128)(2,1)S(1)} %get-tuple-element.155), channel_id=1, source_target_pairs={{0,2},{1,3},{2,0},{3,1},{4,6},{5,7},{6,4},{7,5},{8,10},{9,11},{10,... | collective-permute-start | bytes 98312 | tf_op jit(solution)/shard_map/ppermute | solution.py:40
  201.7 16.9 %collective-permute-start.70 = (bf16[16,2048]{1,0:T(8,128)(2,1)S(1)}, bf16[16,2048]{1,0:T(8,128)(2,1)S(1)}, u32[]{:S(2)}, u32[]{:S(2)}) collective-permute-start(bf16[16,2048]{1,0:T(8,128)(2,1)S(1)} %get-tuple-element.146), channel_id=1, source_target_pairs={{0,24},{1,25},{2,26},{3,27},{4,28},{5,29},{6,30},{7,31},{8,0},{9,1... | collective-permute-start | bytes 196616 | tf_op jit(solution)/shard_map/ppermute | solution.py:40
  205.2 14.3 %collective-permute-start.72 = (bf16[16,2048]{1,0:T(8,128)(2,1)S(1)}, bf16[16,2048]{1,0:T(8,128)(2,1)S(1)}, u32[]{:S(2)}, u32[]{:S(2)}) collective-permute-start(bf16[16,2048]{1,0:T(8,128)(2,1)S(1)} %get-tuple-element.147), channel_id=1, source_target_pairs={{0,8},{1,9},{2,10},{3,11},{4,12},{5,13},{6,14},{7,15},{8,16},{9,17... | collective-permute-start | bytes 196616 | tf_op jit(solution)/shard_map/ppermute | solution.py:40
  205.8 13.7 %collective-permute-start.71 = (bf16[16,2048]{1,0:T(8,128)(2,1)S(1)}, bf16[16,2048]{1,0:T(8,128)(2,1)S(1)}, u32[]{:S(2)}, u32[]{:S(2)}) collective-permute-start(bf16[16,2048]{1,0:T(8,128)(2,1)S(1)} %get-tuple-element.148), channel_id=1, source_target_pairs={{0,16},{1,17},{2,18},{3,19},{4,20},{5,21},{6,22},{7,23},{8,24},{9,... | collective-permute-start | bytes 196616 | tf_op jit(solution)/shard_map/ppermute | solution.py:40
  (30 other events, 252.5 us)

commit v9 on v8

--- a/solution.py
+++ b/solution.py
@@ -150,20 +150,22 @@
 
 
 def projection_kernel(*refs):
-    tokens, other_tokens, grads, other_grads, *quarters = refs[:8]
-    nears, (told, part, other) = refs[8:10], refs[10:]
+    tokens, other_tokens, grads, other_grads, *quarters, left, right = refs[:9]
+    nears, (told, part, other) = refs[9:11], refs[11:]
     width = nears[0].shape[1]
-    count = quarters[0].shape[0]
-    for near, start, order in zip(nears, (0, width), ((0, 1, 2, 3), (0, 2, 1, 3))):
+    count = left.shape[0]
+    for near, start, order in zip(nears, (0, width), ((0, 1, 2), (0, 2, 1))):
         for index, quarter in enumerate(order):
             held = slice(index * count, (index + 1) * count)
             near[held, :] = quarters[quarter][:, start : start + width]
-    for index, quarter in enumerate(quarters):
-        held = slice(index * count, (index + 1) * count)
-        if quarter.shape[1] > 2 * width:
-            told[held, :] = quarter[:, 2 * width :]
-        else:
-            told[held, :] = jnp.zeros((count, told.shape[1]), told.dtype)
+    nears[0][3 * count :, :] = left[...]
+    nears[1][3 * count :, :] = right[:, :width]
+    if right.shape[1] > width:
+        for index, quarter in enumerate(quarters):
+            told[index * count : (index + 1) * count, :] = quarter[:, 2 * width :]
+        told[3 * count :, :] = right[:, width:]
+    else:
+        told[...] = jnp.zeros_like(told)
     half = nears[0].shape[0]
     for target, down, up in ((part, tokens, grads), (other, other_tokens, other_grads)):
         for source, near, start in ((down, nears[0], 0), (up, nears[1], half)):
@@ -450,7 +452,14 @@
     own, later_tokens, later_grads = tied(
         gather_depth(lax.concatenate(sent, 1), OWNERS), tokens, out_grad
     )
-    quarters = gather_chips(own, OWNERS, Y, X)
+    along_y, along_x = shifted(own, OWNERS, Y), shifted(own, OWNERS, X)
+    quarters = (
+        own,
+        along_y,
+        along_x,
+        shifted(along_y[:, : tokens.shape[1]], OWNERS, X),
+        shifted(along_x[:, tokens.shape[1] :], OWNERS, Y),
+    )
     other_tokens = shifted(later_tokens, OWNERS, CORE)
     other_grads = shifted(later_grads, OWNERS, CORE)
     down_place = placement(rows, Y, X)
@@ -465,16 +474,14 @@
     latent, later_tokens, later_grads, told_near = tied(latent, tokens, out_grad, told_near)
     latent_own = gather_depth(latent, EXPERT)
     next_tokens, next_grads = shifted(later_tokens, OWNERS, X), shifted(later_grads, OWNERS, Y)
-    latent_own, next_tokens, next_grads, mix_grad = tied(
-        latent_own, next_tokens, next_grads, mix_grad
-    )
+    latent_own, mix_grad = tied(latent_own, mix_grad)
     near = (latent_own, shifted(latent_own, EXPERT, Y), shifted(latent_own, EXPERT, X))
     mix_own = gather_depth(mix_grad, EXPERT)
     told_far = shifted(told_near, EXPERT, CORE)
     plans, slot_count = expert_plans(
         lax.concatenate([told_near, told_far], 0), local_experts, row_count
     )
-    mix_own, near = tied(mix_own, near)
+    mix_own, near, next_tokens, next_grads = tied(mix_own, near, next_tokens, next_grads)
     near = gather_chips_by_turns(near, EXPERT, Y, X)
     far = tuple(shifted(part, EXPERT, CORE) for part in near[:3])
     near_grad = (mix_own, shifted(mix_own, EXPERT, Y), shifted(mix_own, EXPERT, X))
@@ -489,24 +496,30 @@
         stage_sums(forward_kernel, plans, near, far, *shared, stage) for stage in STAGES[1:]
     ]
     forward_near, forward_far = by_quarter(forward)
-    forward_far, near_grad, later_near, next_tokens, next_grads = tied(
-        forward_far, near_grad, (down_near, up_near), next_tokens, next_grads
-    )
     far_grad = tuple(shifted(part, EXPERT, CORE) for part in near_grad)
-    down_far = shifted(later_near[0], OWNERS, CORE)
-    up_far = shifted(later_near[1], OWNERS, CORE)
-    last_tokens = shifted(next_tokens, OWNERS, CORE)
-    last_grads = shifted(next_grads, OWNERS, CORE)
     across, along_y, along_x, own = core_totals(forward_near, forward_far)
     forward_sums = [part.astype(jnp.bfloat16) for part in (across, along_y, along_x)] + [own]
-    backward_near, backward_far = by_quarter(
-        [
-            stage_sums(
-                backward_kernel, plans, near, far, *shared, stage, (near_grad, far_grad)
-            )
-            for stage in STAGES
-        ]
-    )
+    mix_own, *forward_alongs = tied(near_grad[0], *forward_sums[1:])
+    near_grad = (mix_own,) + tuple(near_grad[1:])
+    backward = [
+        stage_sums(
+            backward_kernel, plans, near, far, *shared, STAGES[0], (near_grad, far_grad)
+        )
+    ]
+    along_grads, forward_across = tied(near_grad[1:], forward_sums[0])
+    forward_sums = [forward_across] + forward_alongs
+    near_grad = near_grad[:1] + tuple(along_grads)
+    backward += [
+        stage_sums(backward_kernel, plans, near, far, *shared, stage, (near_grad, far_grad))
+        for stage in STAGES[1:]
+    ]
+    backward[0], next_tokens, next_grads, down_near, up_near = tied(
+        backward[0], next_tokens, next_grads, down_near, up_near
+    )
+    backward_near, backward_far = by_quarter(backward)
+    last_tokens, last_grads, down_far, up_far = [
+        shifted(array, OWNERS, CORE) for array in (next_tokens, next_grads, down_near, up_near)
+    ]
     quad_tokens = (tokens, other_tokens, next_tokens, last_tokens)
     quad_grads = (out_grad, other_grads, next_grads, last_grads)
 
@@ -525,10 +538,12 @@
     up_sent, up_kept = quad_grads_of(quad, quad_grads)
     up_sums = up_kept + shifted(up_sent, OWNERS, X).astype(jnp.float32)
     grad_relative = matmul(latent_grad, down_place, ((1,), (1,))).astype(jnp.bfloat16)
-    up_sums, mixed_relative, grad_relative = tied(up_sums, mixed_relative, grad_relative)
     quad = quad_columns(grad_relative, X)
+    down_sent, down_kept = quad_grads_of(quad, quad_tokens)
+    up_sums, mixed_relative, grad_relative, down_sent = tied(
+        up_sums, mixed_relative, grad_relative, down_sent
+    )
     up_grad = depth_total(up_sums, OWNERS)
-    down_sent, down_kept = quad_grads_of(quad, quad_tokens)
     down_sums = down_kept + shifted(down_sent, OWNERS, Y).astype(jnp.float32)
     half = latent_width // 2
     layer_out = matmul(mixed_relative[:, :half], up_near)

time: 226 us -> 211 us (0.934)
  waiting for transfers between devices: 115 us -> 92.7 us
  starting transfers between devices: 61.9 us -> 66.7 us
  local copies, waits for them, and re-layouts: 0.81 us -> 3.28 us
    ppermute x73 -> x74, waiting for transfers between devices: 115 us -> 92.7 us  [shifted(): return lax.ppermute(block, axes, pairs)]
    ppermute x73 -> x74, starting transfers between devices: 61.9 us -> 66.7 us  [shifted(): return lax.ppermute(block, axes, pairs)]
    slice x0 -> x2, local copies, waits for them, and re-layouts: none -> 2.4 us  [the longest x1 1.67 us: local(): along_y[:, :tokens.shape[1]]]
  transfers between devices with their start and end apart: 73 -> 74, of which waited for: 33 -> 33; matrix products, arithmetic and copies ran while one was open for 4% -> 5% of each run, Pallas kernels for 13% -> 15%
where the time goes in v9:
time: 211 us; the launch traced here: 210 us
  waiting for transfers between devices  92.7 us (44%)
  starting transfers between devices  66.7 us (32%)
  Pallas kernels  35.1 us (17%)
  other arithmetic  6.72 us (3%)
  matrix products  4.61 us (2%)
  local copies, waits for them, and re-layouts  3.28 us (2%)
    ppermute x74, waiting for transfers between devices, shifted(): return lax.ppermute(block, axes, pairs)  92.7 us
    ppermute x74, starting transfers between devices, shifted(): return lax.ppermute(block, axes, pairs)  66.7 us
    pallas_call x6, Pallas kernels, expert_call(): pl.pallas_call(kernel, out_shape=(jax.ShapeDtypeStruct((span, latent_widt...  30.8 us
    dot_general x8, matrix products, matmul(): lax.dot_general(left, right, (contract, ((), ())), preferred_element_type...  4.52 us
    pallas_call x3, Pallas kernels, vmem_call(): pl.pallas_call(kernel, out_shape=out_shape, in_specs=[whole] * len(operan...  4.29 us
  transfers between devices with their start and end apart: 74, of which 33 were waited for; matrix products, arithmetic and copies ran while one was open for 5% of the time, Pallas kernels for 15%

profile of v9, /device:TPU:0, one launch (start us, length us, event | category | flops | bytes accessed | tf_op | source)
XLA Modules:
  0.0 210.5 jit_solution(11672246363412838336)
XLA Ops:
  2.3 5.1 %collective-permute-start.2 = (bf16[16,4224]{1,0:T(8,128)(2,1)S(1)}, bf16[16,4224]{1,0:T(8,128)(2,1)S(1)}, u32[]{:S(2)}, u32[]{:S(2)}) collective-permute-start(bf16[16,4224]{1,0:T(8,128)(2,1)S(1)} %maximum_maximum_fusion), channel_id=1, source_target_pairs={{0,24},{1,25},{2,26},{3,27},{4,28},{5,29},{6,30},{7,31},{8,0},{9,1... | collective-permute-start | bytes 405512 | tf_op jit(solution)/shard_map/ppermute | solution.py:40
  8.6 2.9 %collective-permute-done.2 = bf16[16,4224]{1,0:T(8,128)(2,1)S(1)} collective-permute-done((bf16[16,4224]{1,0:T(8,128)(2,1)S(1)}, bf16[16,4224]{1,0:T(8,128)(2,1)S(1)}, u32[]{:S(2)}, u32[]{:S(2)}) %collective-permute-start.2) | collective-permute-done | bytes 135200 | tf_op jit(solution)/shard_map/ppermute | solution.py:40
  11.4 7.5 %collective-permute-done.1 = bf16[16,4224]{1,0:T(8,128)(2,1)S(1)} collective-permute-done((bf16[16,4224]{1,0:T(8,128)(2,1)S(1)}, bf16[16,4224]{1,0:T(8,128)(2,1)S(1)}, u32[]{:S(2)}, u32[]{:S(2)}) %collective-permute-start.1) | collective-permute-done | bytes 135200 | tf_op jit(solution)/shard_map/ppermute | solution.py:40
  19.9 1.6 collective-permute-start.5
  21.4 1.5 collective-permute-start.6
  23.7 9.9 %collective-permute-done.5.refs_5_ = bf16[64,4224]{1,0:T(8,128)(2,1)} collective-permute-done((bf16[64,4224]{1,0:T(8,128)(2,1)S(1)}, bf16[64,4224]{1,0:T(8,128)(2,1)}, u32[]{:S(2)}, u32[]{:S(2)}) %collective-permute-start.5) | collective-permute-done | bytes 540704 | tf_op jit(solution)/shard_map/ppermute | solution.py:40
  33.6 1.7 slice.258
  35.2 1.5 collective-permute-start.7
  37.5 1.5 collective-permute-start.8
  39.2 2.9 %collective-permute-done.7.refs_7_ = bf16[64,2048]{1,0:T(8,128)(2,1)} collective-permute-done((bf16[64,2048]{1,0:T(8,128)(2,1)}, bf16[64,2048]{1,0:T(8,128)(2,1)}, u32[]{:S(2)}, u32[]{:S(2)}) %collective-permute-start.7) | collective-permute-done | bytes 262176 | tf_op jit(solution)/shard_map/ppermute | solution.py:40
  42.2 2.2 %collective-permute-done.8.refs_8_ = bf16[64,2176]{1,0:T(8,128)(2,1)S(1)} collective-permute-done((bf16[64,2176]{1,0:T(8,128)(2,1)}, bf16[64,2176]{1,0:T(8,128)(2,1)S(1)}, u32[]{:S(2)}, u32[]{:S(2)}) %collective-permute-start.8) | collective-permute-done | bytes 278560 | tf_op jit(solution)/shard_map/ppermute | solution.py:40
  44.4 2.7 %shard_map.120 = (bf16[256,2048]{1,0:T(8,128)(2,1)S(1)}, bf16[256,2048]{1,0:T(8,128)(2,1)S(1)}, bf16[256,128]{1,0:T(8,128)(2,1)S(1)}, bf16[128,512]{1,0:T(8,128)(2,1)S(1)}, bf16[128,512]{1,0:T(8,128)(2,1)S(1)}) custom-call(bf16[128,2048]{1,0:T(8,128)(2,1)S(1)} %copy-done.4, bf16[128,2048]{1,0:T(8,128)(2,1)S(1)} %collective-permute-done.3.refs_1_.refs_5_, ...), custom_call_target="tpu_custom_call" | custom-call | flops 536870912 | bytes 4259840 | tf_op jit(solution)/shard_map/pallas_call | solution.py:138
  49.4 2.1 %collective-permute-start.11 = (bf16[128,512]{1,0:T(8,128)(2,1)S(1)}, bf16[128,512]{1,0:T(8,128)(2,1)S(1)}, u32[]{:S(2)}, u32[]{:S(2)}) collective-permute-start(bf16[128,512]{1,0:T(8,128)(2,1)S(1)} %convolution_convert_fusion.3), channel_id=1, source_target_pairs={{0,16},{1,17},{2,18},{3,19},{4,20},{5,21},{6,22},{7,23},{8,24},{9,... | collective-permute-start | bytes 393224 | tf_op jit(solution)/shard_map/ppermute | solution.py:40
  51.5 1.9 collective-permute-start.10
  54.7 1.5 collective-permute-start.19
  56.8 6.9 %collective-permute-done.11 = bf16[128,512]{1,0:T(8,128)(2,1)S(1)} collective-permute-done((bf16[128,512]{1,0:T(8,128)(2,1)S(1)}, bf16[128,512]{1,0:T(8,128)(2,1)S(1)}, u32[]{:S(2)}, u32[]{:S(2)}) %collective-permute-start.11) | collective-permute-done | bytes 131104 | tf_op jit(solution)/shard_map/ppermute | solution.py:40
  64.4 1.5 collective-permute-start.16
  65.9 3.8 %collective-permute-done.15 = bf16[128,512]{1,0:T(8,128)(2,1)S(1)} collective-permute-done((bf16[128,512]{1,0:T(8,128)(2,1)S(1)}, bf16[128,512]{1,0:T(8,128)(2,1)S(1)}, u32[]{:S(2)}, u32[]{:S(2)}) %collective-permute-start.15) | collective-permute-done | bytes 131104 | tf_op jit(solution)/shard_map/ppermute | solution.py:40
  70.3 3.3 %collective-permute-done.14 = bf16[128,512]{1,0:T(8,128)(2,1)S(1)} collective-permute-done((bf16[128,512]{1,0:T(8,128)(2,1)S(1)}, bf16[128,512]{1,0:T(8,128)(2,1)S(1)}, u32[]{:S(2)}, u32[]{:S(2)}) %collective-permute-start.14) | collective-permute-done | bytes 131104 | tf_op jit(solution)/shard_map/ppermute | solution.py:40
  73.7 6.7 %collective-permute-done.13 = bf16[128,512]{1,0:T(8,128)(2,1)S(1)} collective-permute-done((bf16[128,512]{1,0:T(8,128)(2,1)S(1)}, bf16[128,512]{1,0:T(8,128)(2,1)S(1)}, u32[]{:S(2)}, u32[]{:S(2)}) %collective-permute-start.13) | collective-permute-done | bytes 131104 | tf_op jit(solution)/shard_map/ppermute | solution.py:40
  82.0 1.6 collective-permute-start.26
  84.5 3.3 %collective-permute-done.25 = bf16[512,256]{1,0:T(8,128)(2,1)S(1)} collective-permute-done((bf16[512,256]{1,0:T(8,128)(2,1)S(1)}, bf16[512,256]{1,0:T(8,128)(2,1)S(1)}, u32[]{:S(2)}, u32[]{:S(2)}) %collective-permute-start.25) | collective-permute-done | bytes 262176 | tf_op jit(solution)/shard_map/ppermute | solution.py:40
  87.8 2.9 %collective-permute-done.26 = bf16[512,256]{1,0:T(8,128)(2,1)S(1)} collective-permute-done((bf16[512,256]{1,0:T(8,128)(2,1)S(1)}, bf16[512,256]{1,0:T(8,128)(2,1)S(1)}, u32[]{:S(2)}, u32[]{:S(2)}) %collective-permute-start.26) | collective-permute-done | bytes 262176 | tf_op jit(solution)/shard_map/ppermute | solution.py:40
  91.7 3.7 %shard_map.122 = (bf16[512,512]{1,0:T(8,128)(2,1)S(1)}, bf16[512,512]{1,0:T(8,128)(2,1)S(1)}) custom-call(s32[2,2,1,512]{3,2,1,0:T(1,128)S(1)} %pad_add_fusion.1.refs_0_, f32[2,2,1,512]{3,2,1,0:T(1,128)S(1)} %pad_maximum_fusion.7.refs_1_, bf16[512,512]{1,0:T(8,128)(2,1)S(1)} %pad_maximum_fusion.1.refs_2_, ...), custom_call_target="tpu_custom_call" | custom-call | flops 1207959552 | bytes 7348224 | tf_op jit(solution)/shard_map/pallas_call | solution.py:366
  95.4 4.6 %collective-permute-done.29.refs_6_ = bf16[512,512]{1,0:T(8,128)(2,1)S(1)} collective-permute-done((bf16[512,512]{1,0:T(8,128)(2,1)S(1)}, bf16[512,512]{1,0:T(8,128)(2,1)S(1)}, u32[]{:S(2)}, u32[]{:S(2)}) %collective-permute-start.29) | collective-permute-done | bytes 524320 | tf_op jit(solution)/shard_map/ppermute | solution.py:40
  101.2 2.1 %collective-permute-done.30.refs_7_ = bf16[512,512]{1,0:T(8,128)(2,1)S(1)} collective-permute-done((bf16[512,512]{1,0:T(8,128)(2,1)S(1)}, bf16[512,512]{1,0:T(8,128)(2,1)S(1)}, u32[]{:S(2)}, u32[]{:S(2)}) %collective-permute-start.30) | collective-permute-done | bytes 524320 | tf_op jit(solution)/shard_map/ppermute | solution.py:40
  104.0 2.1 %collective-permute-start.32 = (bf16[512,256]{1,0:T(8,128)(2,1)S(1)}, bf16[512,256]{1,0:T(8,128)(2,1)S(1)}, u32[]{:S(2)}, u32[]{:S(2)}) collective-permute-start(bf16[512,256]{1,0:T(8,128)(2,1)S(1)} %slice.277), channel_id=1, source_target_pairs={{0,4},{1,5},{2,6},{3,7},{4,0},{5,1},{6,2},{7,3},{8,12},{9,13},{10,... | collective-permute-start | bytes 786440 | tf_op jit(solution)/shard_map/ppermute | solution.py:40
  106.1 5.3 %shard_map.121 = (bf16[512,512]{1,0:T(8,128)(2,1)S(1)}, bf16[512,512]{1,0:T(8,128)(2,1)S(1)}, bf16[512,512]{1,0:T(8,128)(2,1)S(1)}, bf16[512,512]{1,0:T(8,128)(2,1)S(1)}) custom-call(s32[4,2,1,512]{3,2,1,0:T(1,128)S(1)} %pad_add_fusion.refs_0_, f32[4,2,1,512]{3,2,1,0:T(1,128)S(1)} %pad_maximum_fusion.6.refs_1_, ...), custom_call_target="tpu_custom_call" | custom-call | flops 2415919104 | bytes 8404992 | tf_op jit(solution)/shard_map/pallas_call | solution.py:366
  113.3 3.5 %shard_map.123 = (bf16[512,512]{1,0:T(8,128)(2,1)S(1)}, bf16[512,512]{1,0:T(8,128)(2,1)S(1)}) custom-call(s32[2,2,1,512]{3,2,1,0:T(1,128)S(1)} %pad_add_fusion.2.refs_0_, f32[2,2,1,512]{3,2,1,0:T(1,128)S(1)} %pad_maximum_fusion.8.refs_1_, bf16[512,512]{1,0:T(8,128)(2,1)S(1)} %constant_dynamic-update-slice_fusion.refs_2_, ...), custom_call_target="tpu_custom_call" | custom-call | flops 1207959552 | bytes 7348224 | tf_op jit(solution)/shard_map/pallas_call | solution.py:366
  118.0 5.2 %shard_map.126 = (bf16[512,512]{1,0:T(8,128)(2,1)S(1)}, bf16[512,512]{1,0:T(8,128)(2,1)S(1)}) custom-call(s32[2,2,1,512]{3,2,1,0:T(1,128)S(1)} %pad_add_fusion.1.refs_0_, f32[2,2,1,512]{3,2,1,0:T(1,128)S(1)} %pad_maximum_fusion.7.refs_1_, bf16[512,512]{1,0:T(8,128)(2,1)S(1)} %pad_maximum_fusion.1.refs_2_, ...), custom_call_target="tpu_custom_call" | custom-call | flops 2013265920 | bytes 8396800 | tf_op jit(solution)/shard_map/pallas_call | solution.py:366
  124.5 1.8 collective-permute-start.36
  126.5 5.2 %shard_map.124 = (bf16[512,512]{1,0:T(8,128)(2,1)S(1)}, bf16[512,512]{1,0:T(8,128)(2,1)S(1)}) custom-call(s32[2,2,1,512]{3,2,1,0:T(1,128)S(1)} %pad_add_fusion.2.refs_0_, f32[2,2,1,512]{3,2,1,0:T(1,128)S(1)} %pad_maximum_fusion.8.refs_1_, bf16[512,512]{1,0:T(8,128)(2,1)S(1)} %constant_dynamic-update-slice_fusion.refs_2_, ...), custom_call_target="tpu_custom_call" | custom-call | flops 2013265920 | bytes 8396800 | tf_op jit(solution)/shard_map/pallas_call | solution.py:366
  132.6 7.7 %shard_map.125 = (bf16[512,512]{1,0:T(8,128)(2,1)S(1)}, bf16[512,512]{1,0:T(8,128)(2,1)S(1)}, bf16[512,512]{1,0:T(8,128)(2,1)S(1)}, bf16[512,512]{1,0:T(8,128)(2,1)S(1)}) custom-call(s32[4,2,1,512]{3,2,1,0:T(1,128)S(1)} %pad_add_fusion.refs_0_, f32[4,2,1,512]{3,2,1,0:T(1,128)S(1)} %pad_maximum_fusion.6.refs_1_, ...), custom_call_target="tpu_custom_call" | custom-call | flops 4026531840 | bytes 10502144 | tf_op jit(solution)/shard_map/pallas_call | solution.py:366
  143.7 1.8 collective-permute-start.41
  145.5 4.3 %collective-permute-done.36 = bf16[512,512]{1,0:T(8,128)(2,1)S(1)} collective-permute-done((bf16[512,512]{1,0:T(8,128)(2,1)S(1)}, bf16[512,512]{1,0:T(8,128)(2,1)S(1)}, u32[]{:S(2)}, u32[]{:S(2)}) %collective-permute-start.36) | collective-permute-done | bytes 524320 | tf_op jit(solution)/shard_map/ppermute | solution.py:40
  151.0 3.6 %collective-permute-done.40 = bf16[512,256]{1,0:T(8,128)(2,1)S(1)} collective-permute-done((bf16[512,256]{1,0:T(8,128)(2,1)S(1)}, bf16[512,256]{1,0:T(8,128)(2,1)S(1)}, u32[]{:S(2)}, u32[]{:S(2)}) %collective-permute-start.40) | collective-permute-done | bytes 262176 | tf_op jit(solution)/shard_map/ppermute | solution.py:40
  159.6 2.4 %collective-permute-start.49 = (bf16[128,512]{1,0:T(8,128)(2,1)S(1)}, bf16[128,512]{1,0:T(8,128)(2,1)S(1)}, u32[]{:S(2)}, u32[]{:S(2)}) collective-permute-start(bf16[128,512]{1,0:T(8,128)(2,1)S(1)} %get-tuple-element.149), channel_id=1, source_target_pairs={{0,16},{1,17},{2,18},{3,19},{4,20},{5,21},{6,22},{7,23},{8,24},{9,... | collective-permute-start | bytes 393224 | tf_op jit(solution)/shard_map/ppermute | solution.py:40
  163.4 3.6 %collective-permute-done.50 = bf16[128,512]{1,0:T(8,128)(2,1)S(1)} collective-permute-done((bf16[128,512]{1,0:T(8,128)(2,1)S(1)}, bf16[128,512]{1,0:T(8,128)(2,1)S(1)}, u32[]{:S(2)}, u32[]{:S(2)}) %collective-permute-start.50) | collective-permute-done | bytes 131104 | tf_op jit(solution)/shard_map/ppermute | solution.py:40
  167.0 3.4 %collective-permute-done.49 = bf16[128,512]{1,0:T(8,128)(2,1)S(1)} collective-permute-done((bf16[128,512]{1,0:T(8,128)(2,1)S(1)}, bf16[128,512]{1,0:T(8,128)(2,1)S(1)}, u32[]{:S(2)}, u32[]{:S(2)}) %collective-permute-start.49) | collective-permute-done | bytes 131104 | tf_op jit(solution)/shard_map/ppermute | solution.py:40
  171.4 3.0 %collective-permute-start.60 = (bf16[128,512]{1,0:T(8,128)(2,1)S(1)}, bf16[128,512]{1,0:T(8,128)(2,1)S(1)}, u32[]{:S(2)}, u32[]{:S(2)}) collective-permute-start(bf16[128,512]{1,0:T(8,128)(2,1)S(1)} %get-tuple-element.145), channel_id=1, source_target_pairs={{0,8},{1,9},{2,10},{3,11},{4,12},{5,13},{6,14},{7,15},{8,16},{9,17... | collective-permute-start | bytes 393224 | tf_op jit(solution)/shard_map/ppermute | solution.py:40
  178.8 2.1 collective-permute-done.54.refs_2_
  186.8 5.2 %collective-permute-done.62.refs_2_ = bf16[128,128]{1,0:T(8,128)(2,1)S(1)} collective-permute-done((bf16[128,128]{1,0:T(8,128)(2,1)S(1)}, bf16[128,128]{1,0:T(8,128)(2,1)S(1)}, u32[]{:S(2)}, u32[]{:S(2)}) %collective-permute-start.62) | collective-permute-done | bytes 32800 | tf_op jit(solution)/shard_map/ppermute | solution.py:40
  195.0 1.5 collective-permute-start.72
  197.1 1.5 collective-permute-start.71
  202.5 1.5 collective-permute-start.69
  204.0 1.8 collective-permute-start.68
  206.5 1.6 collective-permute-done.70
  208.1 1.7 collective-permute-done.69
  (200 shorter events, 52.2 us)
Async XLA Ops:
  2.3 9.1 %collective-permute-start.2 = (bf16[16,4224]{1,0:T(8,128)(2,1)S(1)}, bf16[16,4224]{1,0:T(8,128)(2,1)S(1)}, u32[]{:S(2)}, u32[]{:S(2)}) collective-permute-start(bf16[16,4224]{1,0:T(8,128)(2,1)S(1)} %maximum_maximum_fusion), channel_id=1, source_target_pairs={{0,24},{1,25},{2,26},{3,27},{4,28},{5,29},{6,30},{7,31},{8,0},{9,1... | collective-permute-start | bytes 405512 | tf_op jit(solution)/shard_map/ppermute | solution.py:40
  7.4 11.5 %collective-permute-start.1 = (bf16[16,4224]{1,0:T(8,128)(2,1)S(1)}, bf16[16,4224]{1,0:T(8,128)(2,1)S(1)}, u32[]{:S(2)}, u32[]{:S(2)}) collective-permute-start(bf16[16,4224]{1,0:T(8,128)(2,1)S(1)} %maximum_maximum_fusion), channel_id=1, source_target_pairs={{0,16},{1,17},{2,18},{3,19},{4,20},{5,21},{6,22},{7,23},{8,24},{9,... | collective-permute-start | bytes 405512 | tf_op jit(solution)/shard_map/ppermute | solution.py:40
  7.4 11.5 %collective-permute-start = (bf16[16,4224]{1,0:T(8,128)(2,1)S(1)}, bf16[16,4224]{1,0:T(8,128)(2,1)S(1)}, u32[]{:S(2)}, u32[]{:S(2)}) collective-permute-start(bf16[16,4224]{1,0:T(8,128)(2,1)S(1)} %maximum_maximum_fusion), channel_id=1, source_target_pairs={{0,8},{1,9},{2,10},{3,11},{4,12},{5,13},{6,14},{7,15},{8,16},{9,17... | collective-permute-start | bytes 405512 | tf_op jit(solution)/shard_map/ppermute | solution.py:40
  19.9 13.7 %collective-permute-start.5 = (bf16[64,4224]{1,0:T(8,128)(2,1)S(1)}, bf16[64,4224]{1,0:T(8,128)(2,1)}, u32[]{:S(2)}, u32[]{:S(2)}) collective-permute-start(bf16[64,4224]{1,0:T(8,128)(2,1)S(1)} %pad_maximum_fusion.refs_4_), channel_id=1, source_target_pairs={{0,4},{1,5},{2,6},{3,7},{4,0},{5,1},{6,2},{7,3},{8,12},{9,13},{10,... | collective-permute-start | bytes 1622024 | tf_op jit(solution)/shard_map/ppermute | solution.py:40
  21.4 15.3 %collective-permute-start.6 = (bf16[64,4224]{1,0:T(8,128)(2,1)S(1)}, bf16[64,4224]{1,0:T(8,128)(2,1)S(1)}, u32[]{:S(2)}, u32[]{:S(2)}) collective-permute-start(bf16[64,4224]{1,0:T(8,128)(2,1)S(1)} %pad_maximum_fusion.refs_4_), channel_id=1, source_target_pairs={{0,2},{1,3},{2,0},{3,1},{4,6},{5,7},{6,4},{7,5},{8,10},{9,11},{10,... | collective-permute-start | bytes 1622024 | tf_op jit(solution)/shard_map/ppermute | solution.py:40
  23.1 16.1 %collective-permute-start.3 = (bf16[128,2048]{1,0:T(8,128)(2,1)S(1)}, bf16[128,2048]{1,0:T(8,128)(2,1)S(1)}, u32[]{:S(2)}, u32[]{:S(2)}) collective-permute-start(bf16[128,2048]{1,0:T(8,128)(2,1)S(1)} %copy-done.4), channel_id=1, source_target_pairs={{0,1},{1,0},{2,3},{3,2},{4,5},{5,4},{6,7},{7,6},{8,9},{9,8},{10,11... | collective-permute-start | bytes 1572872 | tf_op jit(solution)/shard_map/ppermute | solution.py:40
  23.2 16.1 %collective-permute-start.4 = (bf16[128,2048]{1,0:T(8,128)(2,1)S(1)}, bf16[128,2048]{1,0:T(8,128)(2,1)S(1)}, u32[]{:S(2)}, u32[]{:S(2)}) collective-permute-start(bf16[128,2048]{1,0:T(8,128)(2,1)S(1)} %copy-done.3), channel_id=1, source_target_pairs={{0,1},{1,0},{2,3},{3,2},{4,5},{5,4},{6,7},{7,6},{8,9},{9,8},{10,11... | collective-permute-start | bytes 1572872 | tf_op jit(solution)/shard_map/ppermute | solution.py:40
  49.4 14.3 %collective-permute-start.11 = (bf16[128,512]{1,0:T(8,128)(2,1)S(1)}, bf16[128,512]{1,0:T(8,128)(2,1)S(1)}, u32[]{:S(2)}, u32[]{:S(2)}) collective-permute-start(bf16[128,512]{1,0:T(8,128)(2,1)S(1)} %convolution_convert_fusion.3), channel_id=1, source_target_pairs={{0,16},{1,17},{2,18},{3,19},{4,20},{5,21},{6,22},{7,23},{8,24},{9,... | collective-permute-start | bytes 393224 | tf_op jit(solution)/shard_map/ppermute | solution.py:40
  51.5 12.2 %collective-permute-start.10 = (bf16[128,512]{1,0:T(8,128)(2,1)S(1)}, bf16[128,512]{1,0:T(8,128)(2,1)S(1)}, u32[]{:S(2)}, u32[]{:S(2)}) collective-permute-start(bf16[128,512]{1,0:T(8,128)(2,1)S(1)} %convolution_convert_fusion.3), channel_id=1, source_target_pairs={{0,8},{1,9},{2,10},{3,11},{4,12},{5,13},{6,14},{7,15},{8,16},{9,17... | collective-permute-start | bytes 393224 | tf_op jit(solution)/shard_map/ppermute | solution.py:40
  53.4 27.0 %collective-permute-start.18 = (bf16[128,2048]{1,0:T(8,128)(2,1)S(1)}, bf16[128,2048]{1,0:T(8,128)(2,1)S(1)}, u32[]{:S(2)}, u32[]{:S(2)}) collective-permute-start(bf16[128,2048]{1,0:T(8,128)(2,1)S(1)} %copy-done.4), channel_id=1, source_target_pairs={{0,2},{1,3},{2,0},{3,1},{4,6},{5,7},{6,4},{7,5},{8,10},{9,11},{10,... | collective-permute-start | bytes 1572872 | tf_op jit(solution)/shard_map/ppermute | solution.py:40
  54.7 25.8 %collective-permute-start.19 = (bf16[128,2048]{1,0:T(8,128)(2,1)S(1)}, bf16[128,2048]{1,0:T(8,128)(2,1)S(1)}, u32[]{:S(2)}, u32[]{:S(2)}) collective-permute-start(bf16[128,2048]{1,0:T(8,128)(2,1)S(1)} %copy-done.3), channel_id=1, source_target_pairs={{0,4},{1,5},{2,6},{3,7},{4,0},{5,1},{6,2},{7,3},{8,12},{9,13},{10,... | collective-permute-start | bytes 1572872 | tf_op jit(solution)/shard_map/ppermute | solution.py:40
  63.8 9.9 %collective-permute-start.14 = (bf16[128,512]{1,0:T(8,128)(2,1)S(1)}, bf16[128,512]{1,0:T(8,128)(2,1)S(1)}, u32[]{:S(2)}, u32[]{:S(2)}) collective-permute-start(bf16[128,512]{1,0:T(8,128)(2,1)S(1)} %convolution_convert_fusion.2), channel_id=1, source_target_pairs={{0,16},{1,17},{2,18},{3,19},{4,20},{5,21},{6,22},{7,23},{8,24},{9,... | collective-permute-start | bytes 393224 | tf_op jit(solution)/shard_map/ppermute | solution.py:40
  64.4 16.0 %collective-permute-start.16 = (bf16[512,512]{1,0:T(8,128)(2,1)S(1)}, bf16[512,512]{1,0:T(8,128)(2,1)S(1)}, u32[]{:S(2)}, u32[]{:S(2)}) collective-permute-start(bf16[512,512]{1,0:T(8,128)(2,1)S(1)} %pad_maximum_fusion.1.refs_2_), channel_id=1, source_target_pairs={{0,4},{1,5},{2,6},{3,7},{4,0},{5,1},{6,2},{7,3},{8,12},{9,13},{10,... | collective-permute-start | bytes 1572872 | tf_op jit(solution)/shard_map/ppermute | solution.py:40
  69.8 11.6 %collective-permute-start.17 = (bf16[512,512]{1,0:T(8,128)(2,1)S(1)}, bf16[512,512]{1,0:T(8,128)(2,1)S(1)}, u32[]{:S(2)}, u32[]{:S(2)}) collective-permute-start(bf16[512,512]{1,0:T(8,128)(2,1)S(1)} %pad_maximum_fusion.1.refs_2_), channel_id=1, source_target_pairs={{0,2},{1,3},{2,0},{3,1},{4,6},{5,7},{6,4},{7,5},{8,10},{9,11},{10,... | collective-permute-start | bytes 1572872 | tf_op jit(solution)/shard_map/ppermute | solution.py:40
  82.0 8.7 %collective-permute-start.26 = (bf16[512,256]{1,0:T(8,128)(2,1)S(1)}, bf16[512,256]{1,0:T(8,128)(2,1)S(1)}, u32[]{:S(2)}, u32[]{:S(2)}) collective-permute-start(bf16[512,256]{1,0:T(8,128)(2,1)S(1)} %slice.229), channel_id=1, source_target_pairs={{0,4},{1,5},{2,6},{3,7},{4,0},{5,1},{6,2},{7,3},{8,12},{9,13},{10,... | collective-permute-start | bytes 786440 | tf_op jit(solution)/shard_map/ppermute | solution.py:40
  83.7 16.3 %collective-permute-start.29 = (bf16[512,512]{1,0:T(8,128)(2,1)S(1)}, bf16[512,512]{1,0:T(8,128)(2,1)S(1)}, u32[]{:S(2)}, u32[]{:S(2)}) collective-permute-start(bf16[512,512]{1,0:T(8,128)(2,1)S(1)} %pad_maximum_fusion.2.refs_4_), channel_id=1, source_target_pairs={{0,4},{1,5},{2,6},{3,7},{4,0},{5,1},{6,2},{7,3},{8,12},{9,13},{10,... | collective-permute-start | bytes 1572872 | tf_op jit(solution)/shard_map/ppermute | solution.py:40
  84.3 19.2 %collective-permute-start.21 = (bf16[512,512]{1,0:T(8,128)(2,1)S(1)}, bf16[512,512]{1,0:T(8,128)(2,1)S(1)}, u32[]{:S(2)}, u32[]{:S(2)}) collective-permute-start(bf16[512,512]{1,0:T(8,128)(2,1)S(1)} %collective-permute-done.16.refs_2_), channel_id=1, source_target_pairs={{0,1},{1,0},{2,3},{3,2},{4,5},{5,4},{6,7},{7,6},{8,9},{9,8},{10,11... | collective-permute-start | bytes 1572872 | tf_op jit(solution)/shard_map/ppermute | solution.py:40
  87.8 16.2 %collective-permute-start.22 = (bf16[512,512]{1,0:T(8,128)(2,1)S(1)}, bf16[512,512]{1,0:T(8,128)(2,1)S(1)}, u32[]{:S(2)}, u32[]{:S(2)}) collective-permute-start(bf16[512,512]{1,0:T(8,128)(2,1)S(1)} %collective-permute-done.17.refs_3_), channel_id=1, source_target_pairs={{0,1},{1,0},{2,3},{3,2},{4,5},{5,4},{6,7},{7,6},{8,9},{9,8},{10,11... | collective-permute-start | bytes 1572872 | tf_op jit(solution)/shard_map/ppermute | solution.py:40
  90.7 12.7 %collective-permute-start.30 = (bf16[512,512]{1,0:T(8,128)(2,1)S(1)}, bf16[512,512]{1,0:T(8,128)(2,1)S(1)}, u32[]{:S(2)}, u32[]{:S(2)}) collective-permute-start(bf16[512,512]{1,0:T(8,128)(2,1)S(1)} %pad_maximum_fusion.2.refs_4_), channel_id=1, source_target_pairs={{0,2},{1,3},{2,0},{3,1},{4,6},{5,7},{6,4},{7,5},{8,10},{9,11},{10,... | collective-permute-start | bytes 1572872 | tf_op jit(solution)/shard_map/ppermute | solution.py:40
  100.0 11.5 %collective-permute-start.31 = (bf16[512,256]{1,0:T(8,128)(2,1)S(1)}, bf16[512,256]{1,0:T(8,128)(2,1)S(1)}, u32[]{:S(2)}, u32[]{:S(2)}) collective-permute-start(bf16[512,256]{1,0:T(8,128)(2,1)S(1)} %slice.276), channel_id=1, source_target_pairs={{0,2},{1,3},{2,0},{3,1},{4,6},{5,7},{6,4},{7,5},{8,10},{9,11},{10,... | collective-permute-start | bytes 786440 | tf_op jit(solution)/shard_map/ppermute | solution.py:40
  101.2 11.5 %collective-permute-start.33 = (bf16[512,512]{1,0:T(8,128)(2,1)S(1)}, bf16[512,512]{1,0:T(8,128)(2,1)S(1)}, u32[]{:S(2)}, u32[]{:S(2)}) collective-permute-start(bf16[512,512]{1,0:T(8,128)(2,1)S(1)} %constant_dynamic-update-slice_fusion.refs_2_), channel_id=1, source_target_pairs={{0,1},{1,0},{2,3},{3,2},{4,5},{5,4},{6,7},{7,6},{8,9},{9,8},{10,11... | collective-permute-start | bytes 1572872 | tf_op jit(solution)/shard_map/ppermute | solution.py:40
  103.4 14.6 %collective-permute-start.46 = (bf16[512,512]{1,0:T(8,128)(2,1)S(1)}, bf16[512,512]{1,0:T(8,128)(2,1)S(1)}, u32[]{:S(2)}, u32[]{:S(2)}) collective-permute-start(bf16[512,512]{1,0:T(8,128)(2,1)S(1)} %pad_maximum_fusion.2.refs_4_), channel_id=1, source_target_pairs={{0,1},{1,0},{2,3},{3,2},{4,5},{5,4},{6,7},{7,6},{8,9},{9,8},{10,11... | collective-permute-start | bytes 1572872 | tf_op jit(solution)/shard_map/ppermute | solution.py:40
  103.4 13.4 %collective-permute-start.28 = (bf16[512,512]{1,0:T(8,128)(2,1)S(1)}, bf16[512,512]{1,0:T(8,128)(2,1)S(1)}, u32[]{:S(2)}, u32[]{:S(2)}) collective-permute-start(bf16[512,512]{1,0:T(8,128)(2,1)S(1)} %get-tuple-element.96), channel_id=1, source_target_pairs={{0,1},{1,0},{2,3},{3,2},{4,5},{5,4},{6,7},{7,6},{8,9},{9,8},{10,11... | collective-permute-start | bytes 1572872 | tf_op jit(solution)/shard_map/ppermute | solution.py:40
  104.0 8.7 %collective-permute-start.32 = (bf16[512,256]{1,0:T(8,128)(2,1)S(1)}, bf16[512,256]{1,0:T(8,128)(2,1)S(1)}, u32[]{:S(2)}, u32[]{:S(2)}) collective-permute-start(bf16[512,256]{1,0:T(8,128)(2,1)S(1)} %slice.277), channel_id=1, source_target_pairs={{0,4},{1,5},{2,6},{3,7},{4,0},{5,1},{6,2},{7,3},{8,12},{9,13},{10,... | collective-permute-start | bytes 786440 | tf_op jit(solution)/shard_map/ppermute | solution.py:40
  112.7 19.1 %collective-permute-start.42 = (bf16[512,512]{1,0:T(8,128)(2,1)S(1)}, bf16[512,512]{1,0:T(8,128)(2,1)S(1)}, u32[]{:S(2)}, u32[]{:S(2)}) collective-permute-start(bf16[512,512]{1,0:T(8,128)(2,1)S(1)} %collective-permute-done.29.refs_6_), channel_id=1, source_target_pairs={{0,1},{1,0},{2,3},{3,2},{4,5},{5,4},{6,7},{7,6},{8,9},{9,8},{10,11... | collective-permute-start | bytes 1572872 | tf_op jit(solution)/shard_map/ppermute | solution.py:40
  116.8 15.6 %collective-permute-start.43 = (bf16[512,512]{1,0:T(8,128)(2,1)S(1)}, bf16[512,512]{1,0:T(8,128)(2,1)S(1)}, u32[]{:S(2)}, u32[]{:S(2)}) collective-permute-start(bf16[512,512]{1,0:T(8,128)(2,1)S(1)} %collective-permute-done.30.refs_7_), channel_id=1, source_target_pairs={{0,1},{1,0},{2,3},{3,2},{4,5},{5,4},{6,7},{7,6},{8,9},{9,8},{10,11... | collective-permute-start | bytes 1572872 | tf_op jit(solution)/shard_map/ppermute | solution.py:40
  117.8 8.7 %collective-permute-start.38 = (bf16[512,512]{1,0:T(8,128)(2,1)S(1)}, bf16[512,512]{1,0:T(8,128)(2,1)S(1)}, u32[]{:S(2)}, u32[]{:S(2)}) collective-permute-start(bf16[512,512]{1,0:T(8,128)(2,1)S(1)} %constant_dynamic-update-slice_fusion.2.refs_4_), channel_id=1, source_target_pairs={{0,1},{1,0},{2,3},{3,2},{4,5},{5,4},{6,7},{7,6},{8,9},{9,8},{10,11... | collective-permute-start | bytes 1572872 | tf_op jit(solution)/shard_map/ppermute | solution.py:40
  123.3 20.4 %collective-permute-start.37 = (bf16[512,512]{1,0:T(8,128)(2,1)S(1)}, bf16[512,512]{1,0:T(8,128)(2,1)S(1)}, u32[]{:S(2)}, u32[]{:S(2)}) collective-permute-start(bf16[512,512]{1,0:T(8,128)(2,1)S(1)} %add_convert_fusion.2), channel_id=1, source_target_pairs={{0,2},{1,3},{2,0},{3,1},{4,6},{5,7},{6,4},{7,5},{8,10},{9,11},{10,... | collective-permute-start | bytes 1572872 | tf_op jit(solution)/shard_map/ppermute | solution.py:40
  124.5 25.3 %collective-permute-start.36 = (bf16[512,512]{1,0:T(8,128)(2,1)S(1)}, bf16[512,512]{1,0:T(8,128)(2,1)S(1)}, u32[]{:S(2)}, u32[]{:S(2)}) collective-permute-start(bf16[512,512]{1,0:T(8,128)(2,1)S(1)} %add_convert_fusion.3), channel_id=1, source_target_pairs={{0,4},{1,5},{2,6},{3,7},{4,0},{5,1},{6,2},{7,3},{8,12},{9,13},{10,... | collective-permute-start | bytes 1572872 | tf_op jit(solution)/shard_map/ppermute | solution.py:40
  126.4 13.9 %collective-permute-start.47 = (bf16[512,512]{1,0:T(8,128)(2,1)S(1)}, bf16[512,512]{1,0:T(8,128)(2,1)S(1)}, u32[]{:S(2)}, u32[]{:S(2)}) collective-permute-start(bf16[512,512]{1,0:T(8,128)(2,1)S(1)} %get-tuple-element.121), channel_id=1, source_target_pairs={{0,1},{1,0},{2,3},{3,2},{4,5},{5,4},{6,7},{7,6},{8,9},{9,8},{10,11... | collective-permute-start | bytes 1572872 | tf_op jit(solution)/shard_map/ppermute | solution.py:40
  131.8 18.7 %collective-permute-start.35 = (bf16[512,512]{1,0:T(8,128)(2,1)S(1)}, bf16[512,512]{1,0:T(8,128)(2,1)S(1)}, u32[]{:S(2)}, u32[]{:S(2)}) collective-permute-start(bf16[512,512]{1,0:T(8,128)(2,1)S(1)} %add_convert_fusion.1), channel_id=1, source_target_pairs={{0,6},{1,7},{2,4},{3,5},{4,2},{5,3},{6,0},{7,1},{8,14},{9,15},{10,... | collective-permute-start | bytes 1572872 | tf_op jit(solution)/shard_map/ppermute | solution.py:40
  132.4 8.5 %collective-permute-start.39 = (bf16[512,512]{1,0:T(8,128)(2,1)S(1)}, bf16[512,512]{1,0:T(8,128)(2,1)S(1)}, u32[]{:S(2)}, u32[]{:S(2)}) collective-permute-start(bf16[512,512]{1,0:T(8,128)(2,1)S(1)} %get-tuple-element.106), channel_id=1, source_target_pairs={{0,1},{1,0},{2,3},{3,2},{4,5},{5,4},{6,7},{7,6},{8,9},{9,8},{10,11... | collective-permute-start | bytes 1572872 | tf_op jit(solution)/shard_map/ppermute | solution.py:40
  140.9 9.9 %collective-permute-start.45 = (bf16[512,512]{1,0:T(8,128)(2,1)S(1)}, bf16[512,512]{1,0:T(8,128)(2,1)S(1)}, u32[]{:S(2)}, u32[]{:S(2)}) collective-permute-start(bf16[512,512]{1,0:T(8,128)(2,1)S(1)} %get-tuple-element.112), channel_id=1, source_target_pairs={{0,1},{1,0},{2,3},{3,2},{4,5},{5,4},{6,7},{7,6},{8,9},{9,8},{10,11... | collective-permute-start | bytes 1572872 | tf_op jit(solution)/shard_map/ppermute | solution.py:40
  142.4 12.2 %collective-permute-start.40 = (bf16[512,256]{1,0:T(8,128)(2,1)S(1)}, bf16[512,256]{1,0:T(8,128)(2,1)S(1)}, u32[]{:S(2)}, u32[]{:S(2)}) collective-permute-start(bf16[512,256]{1,0:T(8,128)(2,1)S(1)} %get-tuple-element.151), channel_id=1, source_target_pairs={{0,2},{1,3},{2,0},{3,1},{4,6},{5,7},{6,4},{7,5},{8,10},{9,11},{10,... | collective-permute-start | bytes 786440 | tf_op jit(solution)/shard_map/ppermute | solution.py:40
  143.7 12.0 %collective-permute-start.41 = (bf16[512,256]{1,0:T(8,128)(2,1)S(1)}, bf16[512,256]{1,0:T(8,128)(2,1)S(1)}, u32[]{:S(2)}, u32[]{:S(2)}) collective-permute-start(bf16[512,256]{1,0:T(8,128)(2,1)S(1)} %get-tuple-element.150), channel_id=1, source_target_pairs={{0,4},{1,5},{2,6},{3,7},{4,0},{5,1},{6,2},{7,3},{8,12},{9,13},{10,... | collective-permute-start | bytes 786440 | tf_op jit(solution)/shard_map/ppermute | solution.py:40
  155.9 14.9 %collective-permute-start.52 = (bf16[512,512]{1,0:T(8,128)(2,1)S(1)}, bf16[512,512]{1,0:T(8,128)(2,1)S(1)}, u32[]{:S(2)}, u32[]{:S(2)}) collective-permute-start(bf16[512,512]{1,0:T(8,128)(2,1)S(1)} %pad_maximum_fusion.4), channel_id=1, source_target_pairs={{0,2},{1,3},{2,0},{3,1},{4,6},{5,7},{6,4},{7,5},{8,10},{9,11},{10,... | collective-permute-start | bytes 1572872 | tf_op jit(solution)/shard_map/ppermute | solution.py:40
  157.4 13.6 %collective-permute-start.51 = (bf16[512,512]{1,0:T(8,128)(2,1)S(1)}, bf16[512,512]{1,0:T(8,128)(2,1)S(1)}, u32[]{:S(2)}, u32[]{:S(2)}) collective-permute-start(bf16[512,512]{1,0:T(8,128)(2,1)S(1)} %pad_maximum_fusion.3), channel_id=1, source_target_pairs={{0,4},{1,5},{2,6},{3,7},{4,0},{5,1},{6,2},{7,3},{8,12},{9,13},{10,... | collective-permute-start | bytes 1572872 | tf_op jit(solution)/shard_map/ppermute | solution.py:40
  159.6 10.8 %collective-permute-start.49 = (bf16[128,512]{1,0:T(8,128)(2,1)S(1)}, bf16[128,512]{1,0:T(8,128)(2,1)S(1)}, u32[]{:S(2)}, u32[]{:S(2)}) collective-permute-start(bf16[128,512]{1,0:T(8,128)(2,1)S(1)} %get-tuple-element.149), channel_id=1, source_target_pairs={{0,16},{1,17},{2,18},{3,19},{4,20},{5,21},{6,22},{7,23},{8,24},{9,... | collective-permute-start | bytes 393224 | tf_op jit(solution)/shard_map/ppermute | solution.py:40
  167.0 9.9 %collective-permute-start.56 = (bf16[128,2048]{1,0:T(8,128)(2,1)S(1)}, bf16[128,2048]{1,0:T(8,128)(2,1)S(1)}, u32[]{:S(2)}, u32[]{:S(2)}) collective-permute-start(bf16[128,2048]{1,0:T(8,128)(2,1)S(1)} %collective-permute-done.19.refs_6_), channel_id=1, source_target_pairs={{0,1},{1,0},{2,3},{3,2},{4,5},{5,4},{6,7},{7,6},{8,9},{9,8},{10,11... | collective-permute-start | bytes 1572872 | tf_op jit(solution)/shard_map/ppermute | solution.py:40
  171.4 12.2 %collective-permute-start.60 = (bf16[128,512]{1,0:T(8,128)(2,1)S(1)}, bf16[128,512]{1,0:T(8,128)(2,1)S(1)}, u32[]{:S(2)}, u32[]{:S(2)}) collective-permute-start(bf16[128,512]{1,0:T(8,128)(2,1)S(1)} %get-tuple-element.145), channel_id=1, source_target_pairs={{0,8},{1,9},{2,10},{3,11},{4,12},{5,13},{6,14},{7,15},{8,16},{9,17... | collective-permute-start | bytes 393224 | tf_op jit(solution)/shard_map/ppermute | solution.py:40
  174.3 9.6 %collective-permute-start.59 = (bf16[128,512]{1,0:T(8,128)(2,1)S(1)}, bf16[128,512]{1,0:T(8,128)(2,1)S(1)}, u32[]{:S(2)}, u32[]{:S(2)}) collective-permute-start(bf16[128,512]{1,0:T(8,128)(2,1)S(1)} %get-tuple-element.146), channel_id=1, source_target_pairs={{0,16},{1,17},{2,18},{3,19},{4,20},{5,21},{6,22},{7,23},{8,24},{9,... | collective-permute-start | bytes 393224 | tf_op jit(solution)/shard_map/ppermute | solution.py:40
  182.2 10.6 %collective-permute-start.57 = (bf16[64,2048]{1,0:T(8,128)(2,1)S(1)}, bf16[64,2048]{1,0:T(8,128)(2,1)S(1)}, u32[]{:S(2)}, u32[]{:S(2)}) collective-permute-start(bf16[64,2048]{1,0:T(8,128)(2,1)S(1)} %get-tuple-element.131), channel_id=1, source_target_pairs={{0,2},{1,3},{2,0},{3,1},{4,6},{5,7},{6,4},{7,5},{8,10},{9,11},{10,... | collective-permute-start | bytes 786440 | tf_op jit(solution)/shard_map/ppermute | solution.py:40
  186.3 10.8 %collective-permute-start.65 = (bf16[256,2048]{1,0:T(8,128)(2,1)S(1)}, bf16[256,2048]{1,0:T(8,128)(2,1)S(1)}, u32[]{:S(2)}, u32[]{:S(2)}) collective-permute-start(bf16[256,2048]{1,0:T(8,128)(2,1)S(1)} %get-tuple-element.136), channel_id=1, source_target_pairs={{0,1},{1,0},{2,3},{3,2},{4,5},{5,4},{6,7},{7,6},{8,9},{9,8},{10,11... | collective-permute-start | bytes 3145736 | tf_op jit(solution)/shard_map/ppermute | solution.py:40
  186.7 13.1 %collective-permute-start.66 = (bf16[256,2048]{1,0:T(8,128)(2,1)S(1)}, bf16[256,2048]{1,0:T(8,128)(2,1)S(1)}, u32[]{:S(2)}, u32[]{:S(2)}) collective-permute-start(bf16[256,2048]{1,0:T(8,128)(2,1)S(1)} %get-tuple-element.138), channel_id=1, source_target_pairs={{0,1},{1,0},{2,3},{3,2},{4,5},{5,4},{6,7},{7,6},{8,9},{9,8},{10,11... | collective-permute-start | bytes 3145736 | tf_op jit(solution)/shard_map/ppermute | solution.py:40
  192.9 8.4 %collective-permute-start.67 = (bf16[64,2048]{1,0:T(8,128)(2,1)S(1)}, bf16[64,2048]{1,0:T(8,128)(2,1)S(1)}, u32[]{:S(2)}, u32[]{:S(2)}) collective-permute-start(bf16[64,2048]{1,0:T(8,128)(2,1)S(1)} %get-tuple-element.140), channel_id=1, source_target_pairs={{0,4},{1,5},{2,6},{3,7},{4,0},{5,1},{6,2},{7,3},{8,12},{9,13},{10,... | collective-permute-start | bytes 786440 | tf_op jit(solution)/shard_map/ppermute | solution.py:40
  193.9 10.0 %collective-permute-start.73 = (bf16[16,2048]{1,0:T(8,128)(2,1)S(1)}, bf16[16,2048]{1,0:T(8,128)(2,1)S(1)}, u32[]{:S(2)}, u32[]{:S(2)}) collective-permute-start(bf16[16,2048]{1,0:T(8,128)(2,1)S(1)} %get-tuple-element.153), channel_id=1, source_target_pairs={{0,8},{1,9},{2,10},{3,11},{4,12},{5,13},{6,14},{7,15},{8,16},{9,17... | collective-permute-start | bytes 196616 | tf_op jit(solution)/shard_map/ppermute | solution.py:40
  195.0 10.8 %collective-permute-start.72 = (bf16[16,2048]{1,0:T(8,128)(2,1)S(1)}, bf16[16,2048]{1,0:T(8,128)(2,1)S(1)}, u32[]{:S(2)}, u32[]{:S(2)}) collective-permute-start(bf16[16,2048]{1,0:T(8,128)(2,1)S(1)} %get-tuple-element.154), channel_id=1, source_target_pairs={{0,16},{1,17},{2,18},{3,19},{4,20},{5,21},{6,22},{7,23},{8,24},{9,... | collective-permute-start | bytes 196616 | tf_op jit(solution)/shard_map/ppermute | solution.py:40
  197.1 8.7 %collective-permute-start.71 = (bf16[16,2048]{1,0:T(8,128)(2,1)S(1)}, bf16[16,2048]{1,0:T(8,128)(2,1)S(1)}, u32[]{:S(2)}, u32[]{:S(2)}) collective-permute-start(bf16[16,2048]{1,0:T(8,128)(2,1)S(1)} %get-tuple-element.152), channel_id=1, source_target_pairs={{0,24},{1,25},{2,26},{3,27},{4,28},{5,29},{6,30},{7,31},{8,0},{9,1... | collective-permute-start | bytes 196616 | tf_op jit(solution)/shard_map/ppermute | solution.py:40
  (31 other events, 266.9 us)

commit v10 on v9

--- a/solution.py
+++ b/solution.py
@@ -471,9 +471,8 @@
         told_near = lax.concatenate(
             list(gather_chips(gather_depth(told, EXPERT), EXPERT, Y, X)), 0
         )
-    latent, later_tokens, later_grads, told_near = tied(latent, tokens, out_grad, told_near)
+    latent, told_near = tied(latent, told_near)
     latent_own = gather_depth(latent, EXPERT)
-    next_tokens, next_grads = shifted(later_tokens, OWNERS, X), shifted(later_grads, OWNERS, Y)
     latent_own, mix_grad = tied(latent_own, mix_grad)
     near = (latent_own, shifted(latent_own, EXPERT, Y), shifted(latent_own, EXPERT, X))
     mix_own = gather_depth(mix_grad, EXPERT)
@@ -481,7 +480,7 @@
     plans, slot_count = expert_plans(
         lax.concatenate([told_near, told_far], 0), local_experts, row_count
     )
-    mix_own, near, next_tokens, next_grads = tied(mix_own, near, next_tokens, next_grads)
+    mix_own, near = tied(mix_own, near)
     near = gather_chips_by_turns(near, EXPERT, Y, X)
     far = tuple(shifted(part, EXPERT, CORE) for part in near[:3])
     near_grad = (mix_own, shifted(mix_own, EXPERT, Y), shifted(mix_own, EXPERT, X))
@@ -495,33 +494,19 @@
     forward = [first_sums] + [
         stage_sums(forward_kernel, plans, near, far, *shared, stage) for stage in STAGES[1:]
     ]
-    forward_near, forward_far = by_quarter(forward)
     far_grad = tuple(shifted(part, EXPERT, CORE) for part in near_grad)
+    last_sums, *along_grads = tied(forward[2], *near_grad[1:3])
+    forward_near, forward_far = by_quarter(forward[:2] + [last_sums])
     across, along_y, along_x, own = core_totals(forward_near, forward_far)
     forward_sums = [part.astype(jnp.bfloat16) for part in (across, along_y, along_x)] + [own]
-    mix_own, *forward_alongs = tied(near_grad[0], *forward_sums[1:])
-    near_grad = (mix_own,) + tuple(near_grad[1:])
+    near_grad = near_grad[:1] + tuple(along_grads) + near_grad[3:]
     backward = [
-        stage_sums(
-            backward_kernel, plans, near, far, *shared, STAGES[0], (near_grad, far_grad)
-        )
+        stage_sums(backward_kernel, plans, near, far, *shared, stage, (near_grad, far_grad))
+        for stage in STAGES
     ]
-    along_grads, forward_across = tied(near_grad[1:], forward_sums[0])
-    forward_sums = [forward_across] + forward_alongs
-    near_grad = near_grad[:1] + tuple(along_grads)
-    backward += [
-        stage_sums(backward_kernel, plans, near, far, *shared, stage, (near_grad, far_grad))
-        for stage in STAGES[1:]
-    ]
-    backward[0], next_tokens, next_grads, down_near, up_near = tied(
-        backward[0], next_tokens, next_grads, down_near, up_near
-    )
+    backward[0], down_near, up_near = tied(backward[0], down_near, up_near)
     backward_near, backward_far = by_quarter(backward)
-    last_tokens, last_grads, down_far, up_far = [
-        shifted(array, OWNERS, CORE) for array in (next_tokens, next_grads, down_near, up_near)
-    ]
-    quad_tokens = (tokens, other_tokens, next_tokens, last_tokens)
-    quad_grads = (out_grad, other_grads, next_grads, last_grads)
+    down_far, up_far = [shifted(array, OWNERS, CORE) for array in (down_near, up_near)]
 
     mixed_sums = chip_totals(*forward_sums)
     backward_across, *backward_sums = core_totals(backward_near, backward_far)
@@ -532,10 +517,17 @@
     mixed_rows = tensor_total(depth_total(mixed_sums, EXPERT)).astype(jnp.bfloat16)
     mixed_relative = matmul(mixed_rows, up_place, ((1,), (1,))).astype(jnp.bfloat16)
     latent_sums = chip_totals_by_turns(*backward_across, *backward_sums)
-    mixed_relative, latent_sums = tied(mixed_relative, latent_sums)
-    quad = quad_columns(mixed_relative, Y)
-    latent_grad = tensor_total(depth_total(latent_sums, EXPERT)).astype(jnp.bfloat16)
-    up_sent, up_kept = quad_grads_of(quad, quad_grads)
+    latent_sums, later_tokens, later_grads, *quad = tied(
+        latent_sums, tokens, out_grad, *quad_columns(mixed_relative, Y)
+    )
+    next_grads, next_tokens = shifted(later_grads, OWNERS, Y), shifted(later_tokens, OWNERS, X)
+    latent_grad, next_tokens, next_grads = tied(
+        depth_total(latent_sums, EXPERT), next_tokens, next_grads
+    )
+    quad_tokens = (tokens, other_tokens, next_tokens, shifted(next_tokens, OWNERS, CORE))
+    quad_grads = (out_grad, other_grads, next_grads, shifted(next_grads, OWNERS, CORE))
+    latent_grad = tensor_total(latent_grad).astype(jnp.bfloat16)
+    up_sent, up_kept = quad_grads_of(tuple(quad), quad_grads)
     up_sums = up_kept + shifted(up_sent, OWNERS, X).astype(jnp.float32)
     grad_relative = matmul(latent_grad, down_place, ((1,), (1,))).astype(jnp.bfloat16)
     quad = quad_columns(grad_relative, X)

time: 211 us -> 228 us (1.081)
  waiting for transfers between devices: 92.7 us -> 111 us
    ppermute x74, waiting for transfers between devices: 92.7 us -> 111 us  [shifted(): return lax.ppermute(block, axes, pairs)]
  transfers between devices with their start and end apart: 74 -> 74, of which waited for: 33 -> 31; matrix products, arithmetic and copies ran while one was open for 5% -> 5% of each run, Pallas kernels for 15% -> 14%
where the time goes in v10:
time: 228 us
  waiting for transfers between devices  111 us (49%)
  starting transfers between devices  65.9 us (29%)
  Pallas kernels  34.9 us (15%)
  other arithmetic  6.7 us (3%)
  matrix products  4.61 us (2%)
  local copies, waits for them, and re-layouts  3.28 us (1%)
    ppermute x74, waiting for transfers between devices, shifted(): return lax.ppermute(block, axes, pairs)  111 us
    ppermute x74, starting transfers between devices, shifted(): return lax.ppermute(block, axes, pairs)  65.9 us
    pallas_call x6, Pallas kernels, expert_call(): pl.pallas_call(kernel, out_shape=(jax.ShapeDtypeStruct((span, latent_widt...  30.6 us
  transfers between devices with their start and end apart: 74, of which 31 were waited for; matrix products, arithmetic and copies ran while one was open for 5% of the time, Pallas kernels for 14%

profile of v10, /device:TPU:0, one launch (start us, length us, event | category | flops | bytes accessed | tf_op | source)
XLA Modules:
  0.0 227.8 jit_solution(10160106888165304295)
XLA Ops:
  2.3 5.1 %collective-permute-start.2 = (bf16[16,4224]{1,0:T(8,128)(2,1)S(1)}, bf16[16,4224]{1,0:T(8,128)(2,1)S(1)}, u32[]{:S(2)}, u32[]{:S(2)}) collective-permute-start(bf16[16,4224]{1,0:T(8,128)(2,1)S(1)} %maximum_maximum_fusion), channel_id=1, source_target_pairs={{0,24},{1,25},{2,26},{3,27},{4,28},{5,29},{6,30},{7,31},{8,0},{9,1... | collective-permute-start | bytes 405512 | tf_op jit(solution)/shard_map/ppermute | solution.py:40
  8.6 2.9 %collective-permute-done.2 = bf16[16,4224]{1,0:T(8,128)(2,1)S(1)} collective-permute-done((bf16[16,4224]{1,0:T(8,128)(2,1)S(1)}, bf16[16,4224]{1,0:T(8,128)(2,1)S(1)}, u32[]{:S(2)}, u32[]{:S(2)}) %collective-permute-start.2) | collective-permute-done | bytes 135200 | tf_op jit(solution)/shard_map/ppermute | solution.py:40
  11.4 7.5 %collective-permute-done.1 = bf16[16,4224]{1,0:T(8,128)(2,1)S(1)} collective-permute-done((bf16[16,4224]{1,0:T(8,128)(2,1)S(1)}, bf16[16,4224]{1,0:T(8,128)(2,1)S(1)}, u32[]{:S(2)}, u32[]{:S(2)}) %collective-permute-start.1) | collective-permute-done | bytes 135200 | tf_op jit(solution)/shard_map/ppermute | solution.py:40
  19.9 1.6 collective-permute-start.5
  21.4 1.5 collective-permute-start.6
  23.7 9.9 %collective-permute-done.5.refs_5_ = bf16[64,4224]{1,0:T(8,128)(2,1)} collective-permute-done((bf16[64,4224]{1,0:T(8,128)(2,1)S(1)}, bf16[64,4224]{1,0:T(8,128)(2,1)}, u32[]{:S(2)}, u32[]{:S(2)}) %collective-permute-start.5) | collective-permute-done | bytes 540704 | tf_op jit(solution)/shard_map/ppermute | solution.py:40
  33.6 1.7 slice.258
  35.2 1.5 collective-permute-start.7
  37.5 1.5 collective-permute-start.8
  39.2 2.9 %collective-permute-done.7.refs_7_ = bf16[64,2048]{1,0:T(8,128)(2,1)} collective-permute-done((bf16[64,2048]{1,0:T(8,128)(2,1)}, bf16[64,2048]{1,0:T(8,128)(2,1)}, u32[]{:S(2)}, u32[]{:S(2)}) %collective-permute-start.7) | collective-permute-done | bytes 262176 | tf_op jit(solution)/shard_map/ppermute | solution.py:40
  42.2 2.2 collective-permute-done.8.refs_8_
  44.4 2.7 %shard_map.120 = (bf16[256,2048]{1,0:T(8,128)(2,1)S(1)}, bf16[256,2048]{1,0:T(8,128)(2,1)S(1)}, bf16[256,128]{1,0:T(8,128)(2,1)S(1)}, bf16[128,512]{1,0:T(8,128)(2,1)S(1)}, bf16[128,512]{1,0:T(8,128)(2,1)S(1)}) custom-call(bf16[128,2048]{1,0:T(8,128)(2,1)S(1)} %copy-done.4, bf16[128,2048]{1,0:T(8,128)(2,1)S(1)} %collective-permute-done.3.refs_1_.refs_5_, ...), custom_call_target="tpu_custom_call" | custom-call | flops 536870912 | bytes 4259840 | tf_op jit(solution)/shard_map/pallas_call | solution.py:138
  49.4 2.1 collective-permute-start.11
  51.5 1.9 collective-permute-start.10
  55.3 8.4 %collective-permute-done.11 = bf16[128,512]{1,0:T(8,128)(2,1)S(1)} collective-permute-done((bf16[128,512]{1,0:T(8,128)(2,1)S(1)}, bf16[128,512]{1,0:T(8,128)(2,1)S(1)}, u32[]{:S(2)}, u32[]{:S(2)}) %collective-permute-start.11) | collective-permute-done | bytes 131104 | tf_op jit(solution)/shard_map/ppermute | solution.py:40
  63.7 1.6 collective-permute-start.16
  66.4 2.0 collective-permute-start.13
  68.4 2.9 %collective-permute-done.15 = bf16[128,512]{1,0:T(8,128)(2,1)S(1)} collective-permute-done((bf16[128,512]{1,0:T(8,128)(2,1)S(1)}, bf16[128,512]{1,0:T(8,128)(2,1)S(1)}, u32[]{:S(2)}, u32[]{:S(2)}) %collective-permute-start.15) | collective-permute-done | bytes 131104 | tf_op jit(solution)/shard_map/ppermute | solution.py:40
  71.3 6.6 %collective-permute-done.14 = bf16[128,512]{1,0:T(8,128)(2,1)S(1)} collective-permute-done((bf16[128,512]{1,0:T(8,128)(2,1)S(1)}, bf16[128,512]{1,0:T(8,128)(2,1)S(1)}, u32[]{:S(2)}, u32[]{:S(2)}) %collective-permute-start.14) | collective-permute-done | bytes 131104 | tf_op jit(solution)/shard_map/ppermute | solution.py:40
  80.8 6.4 %collective-permute-done.18 = bf16[512,256]{1,0:T(8,128)(2,1)S(1)} collective-permute-done((bf16[512,256]{1,0:T(8,128)(2,1)S(1)}, bf16[512,256]{1,0:T(8,128)(2,1)S(1)}, u32[]{:S(2)}, u32[]{:S(2)}) %collective-permute-start.18) | collective-permute-done | bytes 262176 | tf_op jit(solution)/shard_map/ppermute | solution.py:40
  89.2 3.5 %shard_map.121 = (bf16[512,512]{1,0:T(8,128)(2,1)S(1)}, bf16[512,512]{1,0:T(8,128)(2,1)S(1)}) custom-call(s32[2,2,1,512]{3,2,1,0:T(1,128)S(1)} %pad_add_fusion.1.refs_0_, f32[2,2,1,512]{3,2,1,0:T(1,128)S(1)} %pad_maximum_fusion.7.refs_1_, bf16[512,512]{1,0:T(8,128)(2,1)S(1)} %pad_maximum_fusion.1.refs_2_, ...), custom_call_target="tpu_custom_call" | custom-call | flops 1207959552 | bytes 7348224 | tf_op jit(solution)/shard_map/pallas_call | solution.py:366
  92.7 8.1 %collective-permute-done.24.refs_6_ = bf16[512,512]{1,0:T(8,128)(2,1)S(1)} collective-permute-done((bf16[512,512]{1,0:T(8,128)(2,1)S(1)}, bf16[512,512]{1,0:T(8,128)(2,1)S(1)}, u32[]{:S(2)}, u32[]{:S(2)}) %collective-permute-start.24) | collective-permute-done | bytes 524320 | tf_op jit(solution)/shard_map/ppermute | solution.py:40
  102.0 5.3 %shard_map.123 = (bf16[512,512]{1,0:T(8,128)(2,1)S(1)}, bf16[512,512]{1,0:T(8,128)(2,1)S(1)}, bf16[512,512]{1,0:T(8,128)(2,1)S(1)}, bf16[512,512]{1,0:T(8,128)(2,1)S(1)}) custom-call(s32[4,2,1,512]{3,2,1,0:T(1,128)S(1)} %pad_add_fusion.refs_0_, f32[4,2,1,512]{3,2,1,0:T(1,128)S(1)} %pad_maximum_fusion.6.refs_1_, ...), custom_call_target="tpu_custom_call" | custom-call | flops 2415919104 | bytes 8404992 | tf_op jit(solution)/shard_map/pallas_call | solution.py:366
  108.2 5.2 %shard_map.126 = (bf16[512,512]{1,0:T(8,128)(2,1)S(1)}, bf16[512,512]{1,0:T(8,128)(2,1)S(1)}) custom-call(s32[2,2,1,512]{3,2,1,0:T(1,128)S(1)} %pad_add_fusion.1.refs_0_, f32[2,2,1,512]{3,2,1,0:T(1,128)S(1)} %pad_maximum_fusion.7.refs_1_, bf16[512,512]{1,0:T(8,128)(2,1)S(1)} %pad_maximum_fusion.1.refs_2_, ...), custom_call_target="tpu_custom_call" | custom-call | flops 2013265920 | bytes 8396800 | tf_op jit(solution)/shard_map/pallas_call | solution.py:366
  114.1 2.1 collective-permute-done.35
  116.8 3.5 %shard_map.122 = (bf16[512,512]{1,0:T(8,128)(2,1)S(1)}, bf16[512,512]{1,0:T(8,128)(2,1)S(1)}) custom-call(s32[2,2,1,512]{3,2,1,0:T(1,128)S(1)} %pad_add_fusion.2.refs_0_, f32[2,2,1,512]{3,2,1,0:T(1,128)S(1)} %pad_maximum_fusion.8.refs_1_, bf16[512,512]{1,0:T(8,128)(2,1)S(1)} %constant_dynamic-update-slice_fusion.refs_2_, ...), custom_call_target="tpu_custom_call" | custom-call | flops 1207959552 | bytes 7348224 | tf_op jit(solution)/shard_map/pallas_call | solution.py:366
  122.1 7.7 %shard_map.125 = (bf16[512,512]{1,0:T(8,128)(2,1)S(1)}, bf16[512,512]{1,0:T(8,128)(2,1)S(1)}, bf16[512,512]{1,0:T(8,128)(2,1)S(1)}, bf16[512,512]{1,0:T(8,128)(2,1)S(1)}) custom-call(s32[4,2,1,512]{3,2,1,0:T(1,128)S(1)} %pad_add_fusion.refs_0_, f32[4,2,1,512]{3,2,1,0:T(1,128)S(1)} %pad_maximum_fusion.6.refs_1_, ...), custom_call_target="tpu_custom_call" | custom-call | flops 4026531840 | bytes 10502144 | tf_op jit(solution)/shard_map/pallas_call | solution.py:366
  131.4 5.2 %shard_map.124 = (bf16[512,512]{1,0:T(8,128)(2,1)S(1)}, bf16[512,512]{1,0:T(8,128)(2,1)S(1)}) custom-call(s32[2,2,1,512]{3,2,1,0:T(1,128)S(1)} %pad_add_fusion.2.refs_0_, f32[2,2,1,512]{3,2,1,0:T(1,128)S(1)} %pad_maximum_fusion.8.refs_1_, bf16[512,512]{1,0:T(8,128)(2,1)S(1)} %constant_dynamic-update-slice_fusion.refs_2_, ...), custom_call_target="tpu_custom_call" | custom-call | flops 2013265920 | bytes 8396800 | tf_op jit(solution)/shard_map/pallas_call | solution.py:366
  138.6 2.1 collective-permute-start.27
  142.5 14.4 %collective-permute-done.31 = bf16[512,512]{1,0:T(8,128)(2,1)S(1)} collective-permute-done((bf16[512,512]{1,0:T(8,128)(2,1)S(1)}, bf16[512,512]{1,0:T(8,128)(2,1)S(1)}, u32[]{:S(2)}, u32[]{:S(2)}) %collective-permute-start.31) | collective-permute-done | bytes 524320 | tf_op jit(solution)/shard_map/ppermute | solution.py:40
  157.2 2.0 collective-permute-done.38
  159.2 2.4 %collective-permute-done.39 = bf16[512,256]{1,0:T(8,128)(2,1)S(1)} collective-permute-done((bf16[512,256]{1,0:T(8,128)(2,1)S(1)}, bf16[512,256]{1,0:T(8,128)(2,1)S(1)}, u32[]{:S(2)}, u32[]{:S(2)}) %collective-permute-start.39) | collective-permute-done | bytes 262176 | tf_op jit(solution)/shard_map/ppermute | solution.py:40
  163.2 2.0 collective-permute-start.49
  165.2 2.8 %collective-permute-start.48 = (bf16[128,512]{1,0:T(8,128)(2,1)S(1)}, bf16[128,512]{1,0:T(8,128)(2,1)S(1)}, u32[]{:S(2)}, u32[]{:S(2)}) collective-permute-start(bf16[128,512]{1,0:T(8,128)(2,1)S(1)} %get-tuple-element.143), channel_id=1, source_target_pairs={{0,24},{1,25},{2,26},{3,27},{4,28},{5,29},{6,30},{7,31},{8,0},{9,1... | collective-permute-start | bytes 393224 | tf_op jit(solution)/shard_map/ppermute | solution.py:40
  168.7 2.8 %collective-permute-done.50 = bf16[128,512]{1,0:T(8,128)(2,1)S(1)} collective-permute-done((bf16[128,512]{1,0:T(8,128)(2,1)S(1)}, bf16[128,512]{1,0:T(8,128)(2,1)S(1)}, u32[]{:S(2)}, u32[]{:S(2)}) %collective-permute-start.50) | collective-permute-done | bytes 131104 | tf_op jit(solution)/shard_map/ppermute | solution.py:40
  171.5 3.6 %collective-permute-done.49 = bf16[128,512]{1,0:T(8,128)(2,1)S(1)} collective-permute-done((bf16[128,512]{1,0:T(8,128)(2,1)S(1)}, bf16[128,512]{1,0:T(8,128)(2,1)S(1)}, u32[]{:S(2)}, u32[]{:S(2)}) %collective-permute-start.49) | collective-permute-done | bytes 131104 | tf_op jit(solution)/shard_map/ppermute | solution.py:40
  177.6 3.2 %collective-permute-done.46 = bf16[512,512]{1,0:T(8,128)(2,1)S(1)} collective-permute-done((bf16[512,512]{1,0:T(8,128)(2,1)S(1)}, bf16[512,512]{1,0:T(8,128)(2,1)S(1)}, u32[]{:S(2)}, u32[]{:S(2)}) %collective-permute-start.46) | collective-permute-done | bytes 524320 | tf_op jit(solution)/shard_map/ppermute | solution.py:40
  182.5 2.2 collective-permute-start.56
  184.7 1.4 collective-permute-start.55
  187.1 3.7 %collective-permute-done.56 = bf16[128,512]{1,0:T(8,128)(2,1)S(1)} collective-permute-done((bf16[128,512]{1,0:T(8,128)(2,1)S(1)}, bf16[128,512]{1,0:T(8,128)(2,1)S(1)}, u32[]{:S(2)}, u32[]{:S(2)}) %collective-permute-start.56) | collective-permute-done | bytes 131104 | tf_op jit(solution)/shard_map/ppermute | solution.py:40
  190.8 4.2 %collective-permute-done.55 = bf16[128,512]{1,0:T(8,128)(2,1)S(1)} collective-permute-done((bf16[128,512]{1,0:T(8,128)(2,1)S(1)}, bf16[128,512]{1,0:T(8,128)(2,1)S(1)}, u32[]{:S(2)}, u32[]{:S(2)}) %collective-permute-start.55) | collective-permute-done | bytes 131104 | tf_op jit(solution)/shard_map/ppermute | solution.py:40
  198.2 1.6 collective-permute-start.60
  202.1 5.6 %collective-permute-done.62.refs_2_ = bf16[128,128]{1,0:T(8,128)(2,1)S(1)} collective-permute-done((bf16[128,128]{1,0:T(8,128)(2,1)S(1)}, bf16[128,128]{1,0:T(8,128)(2,1)S(1)}, u32[]{:S(2)}, u32[]{:S(2)}) %collective-permute-start.62) | collective-permute-done | bytes 32800 | tf_op jit(solution)/shard_map/ppermute | solution.py:40
  209.8 3.3 %collective-permute-start.73 = (bf16[16,2048]{1,0:T(8,128)(2,1)S(1)}, bf16[16,2048]{1,0:T(8,128)(2,1)S(1)}, u32[]{:S(2)}, u32[]{:S(2)}) collective-permute-start(bf16[16,2048]{1,0:T(8,128)(2,1)S(1)} %get-tuple-element.149), channel_id=1, source_target_pairs={{0,8},{1,9},{2,10},{3,11},{4,12},{5,13},{6,14},{7,15},{8,16},{9,17... | collective-permute-start | bytes 196616 | tf_op jit(solution)/shard_map/ppermute | solution.py:40
  214.2 2.0 collective-permute-start.71
  218.5 1.9 collective-permute-start.70
  223.5 1.5 collective-permute-done.70
  225.0 2.0 collective-permute-done.69
  (200 shorter events, 48.0 us)
Async XLA Ops:
  2.3 9.1 %collective-permute-start.2 = (bf16[16,4224]{1,0:T(8,128)(2,1)S(1)}, bf16[16,4224]{1,0:T(8,128)(2,1)S(1)}, u32[]{:S(2)}, u32[]{:S(2)}) collective-permute-start(bf16[16,4224]{1,0:T(8,128)(2,1)S(1)} %maximum_maximum_fusion), channel_id=1, source_target_pairs={{0,24},{1,25},{2,26},{3,27},{4,28},{5,29},{6,30},{7,31},{8,0},{9,1... | collective-permute-start | bytes 405512 | tf_op jit(solution)/shard_map/ppermute | solution.py:40
  7.4 11.5 %collective-permute-start.1 = (bf16[16,4224]{1,0:T(8,128)(2,1)S(1)}, bf16[16,4224]{1,0:T(8,128)(2,1)S(1)}, u32[]{:S(2)}, u32[]{:S(2)}) collective-permute-start(bf16[16,4224]{1,0:T(8,128)(2,1)S(1)} %maximum_maximum_fusion), channel_id=1, source_target_pairs={{0,16},{1,17},{2,18},{3,19},{4,20},{5,21},{6,22},{7,23},{8,24},{9,... | collective-permute-start | bytes 405512 | tf_op jit(solution)/shard_map/ppermute | solution.py:40
  7.4 11.5 %collective-permute-start = (bf16[16,4224]{1,0:T(8,128)(2,1)S(1)}, bf16[16,4224]{1,0:T(8,128)(2,1)S(1)}, u32[]{:S(2)}, u32[]{:S(2)}) collective-permute-start(bf16[16,4224]{1,0:T(8,128)(2,1)S(1)} %maximum_maximum_fusion), channel_id=1, source_target_pairs={{0,8},{1,9},{2,10},{3,11},{4,12},{5,13},{6,14},{7,15},{8,16},{9,17... | collective-permute-start | bytes 405512 | tf_op jit(solution)/shard_map/ppermute | solution.py:40
  19.9 13.7 %collective-permute-start.5 = (bf16[64,4224]{1,0:T(8,128)(2,1)S(1)}, bf16[64,4224]{1,0:T(8,128)(2,1)}, u32[]{:S(2)}, u32[]{:S(2)}) collective-permute-start(bf16[64,4224]{1,0:T(8,128)(2,1)S(1)} %pad_maximum_fusion.refs_4_), channel_id=1, source_target_pairs={{0,4},{1,5},{2,6},{3,7},{4,0},{5,1},{6,2},{7,3},{8,12},{9,13},{10,... | collective-permute-start | bytes 1622024 | tf_op jit(solution)/shard_map/ppermute | solution.py:40
  21.4 15.3 %collective-permute-start.6 = (bf16[64,4224]{1,0:T(8,128)(2,1)S(1)}, bf16[64,4224]{1,0:T(8,128)(2,1)S(1)}, u32[]{:S(2)}, u32[]{:S(2)}) collective-permute-start(bf16[64,4224]{1,0:T(8,128)(2,1)S(1)} %pad_maximum_fusion.refs_4_), channel_id=1, source_target_pairs={{0,2},{1,3},{2,0},{3,1},{4,6},{5,7},{6,4},{7,5},{8,10},{9,11},{10,... | collective-permute-start | bytes 1622024 | tf_op jit(solution)/shard_map/ppermute | solution.py:40
  23.1 16.1 %collective-permute-start.3 = (bf16[128,2048]{1,0:T(8,128)(2,1)S(1)}, bf16[128,2048]{1,0:T(8,128)(2,1)S(1)}, u32[]{:S(2)}, u32[]{:S(2)}) collective-permute-start(bf16[128,2048]{1,0:T(8,128)(2,1)S(1)} %copy-done.4), channel_id=1, source_target_pairs={{0,1},{1,0},{2,3},{3,2},{4,5},{5,4},{6,7},{7,6},{8,9},{9,8},{10,11... | collective-permute-start | bytes 1572872 | tf_op jit(solution)/shard_map/ppermute | solution.py:40
  23.2 16.1 %collective-permute-start.4 = (bf16[128,2048]{1,0:T(8,128)(2,1)S(1)}, bf16[128,2048]{1,0:T(8,128)(2,1)S(1)}, u32[]{:S(2)}, u32[]{:S(2)}) collective-permute-start(bf16[128,2048]{1,0:T(8,128)(2,1)S(1)} %copy-done.3), channel_id=1, source_target_pairs={{0,1},{1,0},{2,3},{3,2},{4,5},{5,4},{6,7},{7,6},{8,9},{9,8},{10,11... | collective-permute-start | bytes 1572872 | tf_op jit(solution)/shard_map/ppermute | solution.py:40
  49.4 14.3 %collective-permute-start.11 = (bf16[128,512]{1,0:T(8,128)(2,1)S(1)}, bf16[128,512]{1,0:T(8,128)(2,1)S(1)}, u32[]{:S(2)}, u32[]{:S(2)}) collective-permute-start(bf16[128,512]{1,0:T(8,128)(2,1)S(1)} %convolution_convert_fusion.3), channel_id=1, source_target_pairs={{0,16},{1,17},{2,18},{3,19},{4,20},{5,21},{6,22},{7,23},{8,24},{9,... | collective-permute-start | bytes 393224 | tf_op jit(solution)/shard_map/ppermute | solution.py:40
  51.5 12.2 %collective-permute-start.10 = (bf16[128,512]{1,0:T(8,128)(2,1)S(1)}, bf16[128,512]{1,0:T(8,128)(2,1)S(1)}, u32[]{:S(2)}, u32[]{:S(2)}) collective-permute-start(bf16[128,512]{1,0:T(8,128)(2,1)S(1)} %convolution_convert_fusion.3), channel_id=1, source_target_pairs={{0,8},{1,9},{2,10},{3,11},{4,12},{5,13},{6,14},{7,15},{8,16},{9,17... | collective-permute-start | bytes 393224 | tf_op jit(solution)/shard_map/ppermute | solution.py:40
  63.7 14.3 %collective-permute-start.16 = (bf16[512,512]{1,0:T(8,128)(2,1)S(1)}, bf16[512,512]{1,0:T(8,128)(2,1)S(1)}, u32[]{:S(2)}, u32[]{:S(2)}) collective-permute-start(bf16[512,512]{1,0:T(8,128)(2,1)S(1)} %pad_maximum_fusion.1.refs_2_), channel_id=1, source_target_pairs={{0,4},{1,5},{2,6},{3,7},{4,0},{5,1},{6,2},{7,3},{8,12},{9,13},{10,... | collective-permute-start | bytes 1572872 | tf_op jit(solution)/shard_map/ppermute | solution.py:40
  65.3 13.2 %collective-permute-start.17 = (bf16[512,512]{1,0:T(8,128)(2,1)S(1)}, bf16[512,512]{1,0:T(8,128)(2,1)S(1)}, u32[]{:S(2)}, u32[]{:S(2)}) collective-permute-start(bf16[512,512]{1,0:T(8,128)(2,1)S(1)} %pad_maximum_fusion.1.refs_2_), channel_id=1, source_target_pairs={{0,2},{1,3},{2,0},{3,1},{4,6},{5,7},{6,4},{7,5},{8,10},{9,11},{10,... | collective-permute-start | bytes 1572872 | tf_op jit(solution)/shard_map/ppermute | solution.py:40
  65.8 12.1 %collective-permute-start.14 = (bf16[128,512]{1,0:T(8,128)(2,1)S(1)}, bf16[128,512]{1,0:T(8,128)(2,1)S(1)}, u32[]{:S(2)}, u32[]{:S(2)}) collective-permute-start(bf16[128,512]{1,0:T(8,128)(2,1)S(1)} %convolution_convert_fusion.2), channel_id=1, source_target_pairs={{0,16},{1,17},{2,18},{3,19},{4,20},{5,21},{6,22},{7,23},{8,24},{9,... | collective-permute-start | bytes 393224 | tf_op jit(solution)/shard_map/ppermute | solution.py:40
  66.4 11.5 %collective-permute-start.13 = (bf16[128,512]{1,0:T(8,128)(2,1)S(1)}, bf16[128,512]{1,0:T(8,128)(2,1)S(1)}, u32[]{:S(2)}, u32[]{:S(2)}) collective-permute-start(bf16[128,512]{1,0:T(8,128)(2,1)S(1)} %convolution_convert_fusion.2), channel_id=1, source_target_pairs={{0,8},{1,9},{2,10},{3,11},{4,12},{5,13},{6,14},{7,15},{8,16},{9,17... | collective-permute-start | bytes 393224 | tf_op jit(solution)/shard_map/ppermute | solution.py:40
  78.4 9.8 %collective-permute-start.21 = (bf16[512,512]{1,0:T(8,128)(2,1)S(1)}, bf16[512,512]{1,0:T(8,128)(2,1)S(1)}, u32[]{:S(2)}, u32[]{:S(2)}) collective-permute-start(bf16[512,512]{1,0:T(8,128)(2,1)S(1)} %pad_maximum_fusion.1.refs_2_), channel_id=1, source_target_pairs={{0,1},{1,0},{2,3},{3,2},{4,5},{5,4},{6,7},{7,6},{8,9},{9,8},{10,11... | collective-permute-start | bytes 1572872 | tf_op jit(solution)/shard_map/ppermute | solution.py:40
  78.5 8.8 %collective-permute-start.18 = (bf16[512,256]{1,0:T(8,128)(2,1)S(1)}, bf16[512,256]{1,0:T(8,128)(2,1)S(1)}, u32[]{:S(2)}, u32[]{:S(2)}) collective-permute-start(bf16[512,256]{1,0:T(8,128)(2,1)S(1)} %slice.210), channel_id=1, source_target_pairs={{0,2},{1,3},{2,0},{3,1},{4,6},{5,7},{6,4},{7,5},{8,10},{9,11},{10,... | collective-permute-start | bytes 786440 | tf_op jit(solution)/shard_map/ppermute | solution.py:40
  80.3 20.5 %collective-permute-start.28 = (bf16[512,512]{1,0:T(8,128)(2,1)S(1)}, bf16[512,512]{1,0:T(8,128)(2,1)S(1)}, u32[]{:S(2)}, u32[]{:S(2)}) collective-permute-start(bf16[512,512]{1,0:T(8,128)(2,1)S(1)} %collective-permute-done.16.refs_2_), channel_id=1, source_target_pairs={{0,1},{1,0},{2,3},{3,2},{4,5},{5,4},{6,7},{7,6},{8,9},{9,8},{10,11... | collective-permute-start | bytes 1572872 | tf_op jit(solution)/shard_map/ppermute | solution.py:40
  80.3 21.7 %collective-permute-start.29 = (bf16[512,512]{1,0:T(8,128)(2,1)S(1)}, bf16[512,512]{1,0:T(8,128)(2,1)S(1)}, u32[]{:S(2)}, u32[]{:S(2)}) collective-permute-start(bf16[512,512]{1,0:T(8,128)(2,1)S(1)} %collective-permute-done.17.refs_3_), channel_id=1, source_target_pairs={{0,1},{1,0},{2,3},{3,2},{4,5},{5,4},{6,7},{7,6},{8,9},{9,8},{10,11... | collective-permute-start | bytes 1572872 | tf_op jit(solution)/shard_map/ppermute | solution.py:40
  87.3 13.6 %collective-permute-start.24 = (bf16[512,512]{1,0:T(8,128)(2,1)S(1)}, bf16[512,512]{1,0:T(8,128)(2,1)S(1)}, u32[]{:S(2)}, u32[]{:S(2)}) collective-permute-start(bf16[512,512]{1,0:T(8,128)(2,1)S(1)} %pad_maximum_fusion.2.refs_4_), channel_id=1, source_target_pairs={{0,4},{1,5},{2,6},{3,7},{4,0},{5,1},{6,2},{7,3},{8,12},{9,13},{10,... | collective-permute-start | bytes 1572872 | tf_op jit(solution)/shard_map/ppermute | solution.py:40
  88.2 20.0 %collective-permute-start.44 = (bf16[512,512]{1,0:T(8,128)(2,1)S(1)}, bf16[512,512]{1,0:T(8,128)(2,1)S(1)}, u32[]{:S(2)}, u32[]{:S(2)}) collective-permute-start(bf16[512,512]{1,0:T(8,128)(2,1)S(1)} %pad_maximum_fusion.2.refs_4_), channel_id=1, source_target_pairs={{0,1},{1,0},{2,3},{3,2},{4,5},{5,4},{6,7},{7,6},{8,9},{9,8},{10,11... | collective-permute-start | bytes 1572872 | tf_op jit(solution)/shard_map/ppermute | solution.py:40
  88.2 19.4 %collective-permute-start.25 = (bf16[512,512]{1,0:T(8,128)(2,1)S(1)}, bf16[512,512]{1,0:T(8,128)(2,1)S(1)}, u32[]{:S(2)}, u32[]{:S(2)}) collective-permute-start(bf16[512,512]{1,0:T(8,128)(2,1)S(1)} %pad_maximum_fusion.2.refs_4_), channel_id=1, source_target_pairs={{0,2},{1,3},{2,0},{3,1},{4,6},{5,7},{6,4},{7,5},{8,10},{9,11},{10,... | collective-permute-start | bytes 1572872 | tf_op jit(solution)/shard_map/ppermute | solution.py:40
  100.8 15.4 %collective-permute-start.23 = (bf16[512,512]{1,0:T(8,128)(2,1)S(1)}, bf16[512,512]{1,0:T(8,128)(2,1)S(1)}, u32[]{:S(2)}, u32[]{:S(2)}) collective-permute-start(bf16[512,512]{1,0:T(8,128)(2,1)S(1)} %constant_dynamic-update-slice_fusion.refs_2_), channel_id=1, source_target_pairs={{0,1},{1,0},{2,3},{3,2},{4,5},{5,4},{6,7},{7,6},{8,9},{9,8},{10,11... | collective-permute-start | bytes 1572872 | tf_op jit(solution)/shard_map/ppermute | solution.py:40
  100.8 12.7 %collective-permute-start.34 = (bf16[512,256]{1,0:T(8,128)(2,1)S(1)}, bf16[512,256]{1,0:T(8,128)(2,1)S(1)}, u32[]{:S(2)}, u32[]{:S(2)}) collective-permute-start(bf16[512,256]{1,0:T(8,128)(2,1)S(1)} %slice.280), channel_id=1, source_target_pairs={{0,2},{1,3},{2,0},{3,1},{4,6},{5,7},{6,4},{7,5},{8,10},{9,11},{10,... | collective-permute-start | bytes 786440 | tf_op jit(solution)/shard_map/ppermute | solution.py:40
  107.3 13.0 %collective-permute-start.32 = (bf16[512,512]{1,0:T(8,128)(2,1)S(1)}, bf16[512,512]{1,0:T(8,128)(2,1)S(1)}, u32[]{:S(2)}, u32[]{:S(2)}) collective-permute-start(bf16[512,512]{1,0:T(8,128)(2,1)S(1)} %get-tuple-element.97), channel_id=1, source_target_pairs={{0,1},{1,0},{2,3},{3,2},{4,5},{5,4},{6,7},{7,6},{8,9},{9,8},{10,11... | collective-permute-start | bytes 1572872 | tf_op jit(solution)/shard_map/ppermute | solution.py:40
  116.2 13.9 %collective-permute-start.30 = (bf16[512,512]{1,0:T(8,128)(2,1)S(1)}, bf16[512,512]{1,0:T(8,128)(2,1)S(1)}, u32[]{:S(2)}, u32[]{:S(2)}) collective-permute-start(bf16[512,512]{1,0:T(8,128)(2,1)S(1)} %get-tuple-element.95), channel_id=1, source_target_pairs={{0,1},{1,0},{2,3},{3,2},{4,5},{5,4},{6,7},{7,6},{8,9},{9,8},{10,11... | collective-permute-start | bytes 1572872 | tf_op jit(solution)/shard_map/ppermute | solution.py:40
  116.3 25.7 %collective-permute-start.22 = (bf16[512,512]{1,0:T(8,128)(2,1)S(1)}, bf16[512,512]{1,0:T(8,128)(2,1)S(1)}, u32[]{:S(2)}, u32[]{:S(2)}) collective-permute-start(bf16[512,512]{1,0:T(8,128)(2,1)S(1)} %get-tuple-element.87), channel_id=1, source_target_pairs={{0,1},{1,0},{2,3},{3,2},{4,5},{5,4},{6,7},{7,6},{8,9},{9,8},{10,11... | collective-permute-start | bytes 1572872 | tf_op jit(solution)/shard_map/ppermute | solution.py:40
  120.4 9.5 %collective-permute-start.45 = (bf16[512,512]{1,0:T(8,128)(2,1)S(1)}, bf16[512,512]{1,0:T(8,128)(2,1)S(1)}, u32[]{:S(2)}, u32[]{:S(2)}) collective-permute-start(bf16[512,512]{1,0:T(8,128)(2,1)S(1)} %get-tuple-element.111), channel_id=1, source_target_pairs={{0,1},{1,0},{2,3},{3,2},{4,5},{5,4},{6,7},{7,6},{8,9},{9,8},{10,11... | collective-permute-start | bytes 1572872 | tf_op jit(solution)/shard_map/ppermute | solution.py:40
  120.6 10.2 %collective-permute-start.36 = (bf16[512,512]{1,0:T(8,128)(2,1)S(1)}, bf16[512,512]{1,0:T(8,128)(2,1)S(1)}, u32[]{:S(2)}, u32[]{:S(2)}) collective-permute-start(bf16[512,512]{1,0:T(8,128)(2,1)S(1)} %constant_dynamic-update-slice_fusion.2.refs_4_), channel_id=1, source_target_pairs={{0,1},{1,0},{2,3},{3,2},{4,5},{5,4},{6,7},{7,6},{8,9},{9,8},{10,11... | collective-permute-start | bytes 1572872 | tf_op jit(solution)/shard_map/ppermute | solution.py:40
  121.2 21.3 %collective-permute-start.33 = (bf16[512,512]{1,0:T(8,128)(2,1)S(1)}, bf16[512,512]{1,0:T(8,128)(2,1)S(1)}, u32[]{:S(2)}, u32[]{:S(2)}) collective-permute-start(bf16[512,512]{1,0:T(8,128)(2,1)S(1)} %add_convert_fusion.1), channel_id=1, source_target_pairs={{0,2},{1,3},{2,0},{3,1},{4,6},{5,7},{6,4},{7,5},{8,10},{9,11},{10,... | collective-permute-start | bytes 1572872 | tf_op jit(solution)/shard_map/ppermute | solution.py:40
  130.8 26.1 %collective-permute-start.31 = (bf16[512,512]{1,0:T(8,128)(2,1)S(1)}, bf16[512,512]{1,0:T(8,128)(2,1)S(1)}, u32[]{:S(2)}, u32[]{:S(2)}) collective-permute-start(bf16[512,512]{1,0:T(8,128)(2,1)S(1)} %add_convert_fusion.2), channel_id=1, source_target_pairs={{0,4},{1,5},{2,6},{3,7},{4,0},{5,1},{6,2},{7,3},{8,12},{9,13},{10,... | collective-permute-start | bytes 1572872 | tf_op jit(solution)/shard_map/ppermute | solution.py:40
  138.6 18.3 %collective-permute-start.27 = (bf16[512,512]{1,0:T(8,128)(2,1)S(1)}, bf16[512,512]{1,0:T(8,128)(2,1)S(1)}, u32[]{:S(2)}, u32[]{:S(2)}) collective-permute-start(bf16[512,512]{1,0:T(8,128)(2,1)S(1)} %add_convert_fusion.3), channel_id=1, source_target_pairs={{0,6},{1,7},{2,4},{3,5},{4,2},{5,3},{6,0},{7,1},{8,14},{9,15},{10,... | collective-permute-start | bytes 1572872 | tf_op jit(solution)/shard_map/ppermute | solution.py:40
  141.0 18.2 %collective-permute-start.38 = (bf16[512,256]{1,0:T(8,128)(2,1)S(1)}, bf16[512,256]{1,0:T(8,128)(2,1)S(1)}, u32[]{:S(2)}, u32[]{:S(2)}) collective-permute-start(bf16[512,256]{1,0:T(8,128)(2,1)S(1)} %get-tuple-element.147), channel_id=1, source_target_pairs={{0,2},{1,3},{2,0},{3,1},{4,6},{5,7},{6,4},{7,5},{8,10},{9,11},{10,... | collective-permute-start | bytes 786440 | tf_op jit(solution)/shard_map/ppermute | solution.py:40
  142.0 19.6 %collective-permute-start.39 = (bf16[512,256]{1,0:T(8,128)(2,1)S(1)}, bf16[512,256]{1,0:T(8,128)(2,1)S(1)}, u32[]{:S(2)}, u32[]{:S(2)}) collective-permute-start(bf16[512,256]{1,0:T(8,128)(2,1)S(1)} %get-tuple-element.146), channel_id=1, source_target_pairs={{0,4},{1,5},{2,6},{3,7},{4,0},{5,1},{6,2},{7,3},{8,12},{9,13},{10,... | collective-permute-start | bytes 786440 | tf_op jit(solution)/shard_map/ppermute | solution.py:40
  161.7 15.8 %collective-permute-start.47 = (bf16[512,512]{1,0:T(8,128)(2,1)S(1)}, bf16[512,512]{1,0:T(8,128)(2,1)S(1)}, u32[]{:S(2)}, u32[]{:S(2)}) collective-permute-start(bf16[512,512]{1,0:T(8,128)(2,1)S(1)} %pad_maximum_fusion.4), channel_id=1, source_target_pairs={{0,2},{1,3},{2,0},{3,1},{4,6},{5,7},{6,4},{7,5},{8,10},{9,11},{10,... | collective-permute-start | bytes 1572872 | tf_op jit(solution)/shard_map/ppermute | solution.py:40
  163.2 11.9 %collective-permute-start.49 = (bf16[128,512]{1,0:T(8,128)(2,1)S(1)}, bf16[128,512]{1,0:T(8,128)(2,1)S(1)}, u32[]{:S(2)}, u32[]{:S(2)}) collective-permute-start(bf16[128,512]{1,0:T(8,128)(2,1)S(1)} %get-tuple-element.145), channel_id=1, source_target_pairs={{0,16},{1,17},{2,18},{3,19},{4,20},{5,21},{6,22},{7,23},{8,24},{9,... | collective-permute-start | bytes 393224 | tf_op jit(solution)/shard_map/ppermute | solution.py:40
  165.2 9.9 %collective-permute-start.48 = (bf16[128,512]{1,0:T(8,128)(2,1)S(1)}, bf16[128,512]{1,0:T(8,128)(2,1)S(1)}, u32[]{:S(2)}, u32[]{:S(2)}) collective-permute-start(bf16[128,512]{1,0:T(8,128)(2,1)S(1)} %get-tuple-element.143), channel_id=1, source_target_pairs={{0,24},{1,25},{2,26},{3,27},{4,28},{5,29},{6,30},{7,31},{8,0},{9,1... | collective-permute-start | bytes 393224 | tf_op jit(solution)/shard_map/ppermute | solution.py:40
  168.1 12.6 %collective-permute-start.46 = (bf16[512,512]{1,0:T(8,128)(2,1)S(1)}, bf16[512,512]{1,0:T(8,128)(2,1)S(1)}, u32[]{:S(2)}, u32[]{:S(2)}) collective-permute-start(bf16[512,512]{1,0:T(8,128)(2,1)S(1)} %pad_maximum_fusion.3), channel_id=1, source_target_pairs={{0,4},{1,5},{2,6},{3,7},{4,0},{5,1},{6,2},{7,3},{8,12},{9,13},{10,... | collective-permute-start | bytes 1572872 | tf_op jit(solution)/shard_map/ppermute | solution.py:40
  181.2 14.1 %collective-permute-start.57 = (bf16[128,2048]{1,0:T(8,128)(2,1)S(1)}, bf16[128,2048]{1,0:T(8,128)(2,1)S(1)}, u32[]{:S(2)}, u32[]{:S(2)}) collective-permute-start(bf16[128,2048]{1,0:T(8,128)(2,1)S(1)} %copy-done.4), channel_id=1, source_target_pairs={{0,2},{1,3},{2,0},{3,1},{4,6},{5,7},{6,4},{7,5},{8,10},{9,11},{10,... | collective-permute-start | bytes 1572872 | tf_op jit(solution)/shard_map/ppermute | solution.py:40
  181.8 13.7 %collective-permute-start.58 = (bf16[128,2048]{1,0:T(8,128)(2,1)S(1)}, bf16[128,2048]{1,0:T(8,128)(2,1)S(1)}, u32[]{:S(2)}, u32[]{:S(2)}) collective-permute-start(bf16[128,2048]{1,0:T(8,128)(2,1)S(1)} %copy-done.3), channel_id=1, source_target_pairs={{0,4},{1,5},{2,6},{3,7},{4,0},{5,1},{6,2},{7,3},{8,12},{9,13},{10,... | collective-permute-start | bytes 1572872 | tf_op jit(solution)/shard_map/ppermute | solution.py:40
  184.7 10.3 %collective-permute-start.55 = (bf16[128,512]{1,0:T(8,128)(2,1)S(1)}, bf16[128,512]{1,0:T(8,128)(2,1)S(1)}, u32[]{:S(2)}, u32[]{:S(2)}) collective-permute-start(bf16[128,512]{1,0:T(8,128)(2,1)S(1)} %get-tuple-element.142), channel_id=1, source_target_pairs={{0,16},{1,17},{2,18},{3,19},{4,20},{5,21},{6,22},{7,23},{8,24},{9,... | collective-permute-start | bytes 393224 | tf_op jit(solution)/shard_map/ppermute | solution.py:40
  186.1 8.9 %collective-permute-start.54 = (bf16[128,512]{1,0:T(8,128)(2,1)S(1)}, bf16[128,512]{1,0:T(8,128)(2,1)S(1)}, u32[]{:S(2)}, u32[]{:S(2)}) collective-permute-start(bf16[128,512]{1,0:T(8,128)(2,1)S(1)} %get-tuple-element.140), channel_id=1, source_target_pairs={{0,24},{1,25},{2,26},{3,27},{4,28},{5,29},{6,30},{7,31},{8,0},{9,1... | collective-permute-start | bytes 393224 | tf_op jit(solution)/shard_map/ppermute | solution.py:40
  195.5 12.2 %collective-permute-start.64 = (bf16[128,2048]{1,0:T(8,128)(2,1)S(1)}, bf16[128,2048]{1,0:T(8,128)(2,1)S(1)}, u32[]{:S(2)}, u32[]{:S(2)}) collective-permute-start(bf16[128,2048]{1,0:T(8,128)(2,1)S(1)} %collective-permute-done.57.refs_6_), channel_id=1, source_target_pairs={{0,1},{1,0},{2,3},{3,2},{4,5},{5,4},{6,7},{7,6},{8,9},{9,8},{10,11... | collective-permute-start | bytes 1572872 | tf_op jit(solution)/shard_map/ppermute | solution.py:40
  198.2 10.3 %collective-permute-start.60 = (bf16[64,2048]{1,0:T(8,128)(2,1)S(1)}, bf16[64,2048]{1,0:T(8,128)(2,1)S(1)}, u32[]{:S(2)}, u32[]{:S(2)}) collective-permute-start(bf16[64,2048]{1,0:T(8,128)(2,1)S(1)} %get-tuple-element.127), channel_id=1, source_target_pairs={{0,2},{1,3},{2,0},{3,1},{4,6},{5,7},{6,4},{7,5},{8,10},{9,11},{10,... | collective-permute-start | bytes 786440 | tf_op jit(solution)/shard_map/ppermute | solution.py:40
  201.8 12.4 %collective-permute-start.65 = (bf16[256,2048]{1,0:T(8,128)(2,1)S(1)}, bf16[256,2048]{1,0:T(8,128)(2,1)S(1)}, u32[]{:S(2)}, u32[]{:S(2)}) collective-permute-start(bf16[256,2048]{1,0:T(8,128)(2,1)S(1)} %get-tuple-element.132), channel_id=1, source_target_pairs={{0,1},{1,0},{2,3},{3,2},{4,5},{5,4},{6,7},{7,6},{8,9},{9,8},{10,11... | collective-permute-start | bytes 3145736 | tf_op jit(solution)/shard_map/ppermute | solution.py:40
  207.7 9.6 %collective-permute-start.66 = (bf16[256,2048]{1,0:T(8,128)(2,1)S(1)}, bf16[256,2048]{1,0:T(8,128)(2,1)S(1)}, u32[]{:S(2)}, u32[]{:S(2)}) collective-permute-start(bf16[256,2048]{1,0:T(8,128)(2,1)S(1)} %get-tuple-element.134), channel_id=1, source_target_pairs={{0,1},{1,0},{2,3},{3,2},{4,5},{5,4},{6,7},{7,6},{8,9},{9,8},{10,11... | collective-permute-start | bytes 3145736 | tf_op jit(solution)/shard_map/ppermute | solution.py:40
  208.6 9.9 %collective-permute-start.67 = (bf16[64,2048]{1,0:T(8,128)(2,1)S(1)}, bf16[64,2048]{1,0:T(8,128)(2,1)S(1)}, u32[]{:S(2)}, u32[]{:S(2)}) collective-permute-start(bf16[64,2048]{1,0:T(8,128)(2,1)S(1)} %get-tuple-element.136), channel_id=1, source_target_pairs={{0,4},{1,5},{2,6},{3,7},{4,0},{5,1},{6,2},{7,3},{8,12},{9,13},{10,... | collective-permute-start | bytes 786440 | tf_op jit(solution)/shard_map/ppermute | solution.py:40
  209.8 11.7 %collective-permute-start.73 = (bf16[16,2048]{1,0:T(8,128)(2,1)S(1)}, bf16[16,2048]{1,0:T(8,128)(2,1)S(1)}, u32[]{:S(2)}, u32[]{:S(2)}) collective-permute-start(bf16[16,2048]{1,0:T(8,128)(2,1)S(1)} %get-tuple-element.149), channel_id=1, source_target_pairs={{0,8},{1,9},{2,10},{3,11},{4,12},{5,13},{6,14},{7,15},{8,16},{9,17... | collective-permute-start | bytes 196616 | tf_op jit(solution)/shard_map/ppermute | solution.py:40
  213.1 9.8 %collective-permute-start.72 = (bf16[16,2048]{1,0:T(8,128)(2,1)S(1)}, bf16[16,2048]{1,0:T(8,128)(2,1)S(1)}, u32[]{:S(2)}, u32[]{:S(2)}) collective-permute-start(bf16[16,2048]{1,0:T(8,128)(2,1)S(1)} %get-tuple-element.150), channel_id=1, source_target_pairs={{0,16},{1,17},{2,18},{3,19},{4,20},{5,21},{6,22},{7,23},{8,24},{9,... | collective-permute-start | bytes 196616 | tf_op jit(solution)/shard_map/ppermute | solution.py:40
  214.2 8.7 %collective-permute-start.71 = (bf16[16,2048]{1,0:T(8,128)(2,1)S(1)}, bf16[16,2048]{1,0:T(8,128)(2,1)S(1)}, u32[]{:S(2)}, u32[]{:S(2)}) collective-permute-start(bf16[16,2048]{1,0:T(8,128)(2,1)S(1)} %get-tuple-element.148), channel_id=1, source_target_pairs={{0,24},{1,25},{2,26},{3,27},{4,28},{5,29},{6,30},{7,31},{8,0},{9,1... | collective-permute-start | bytes 196616 | tf_op jit(solution)/shard_map/ppermute | solution.py:40
  (31 other events, 265.9 us)

commit v11 on v9

--- a/solution.py
+++ b/solution.py
@@ -101,14 +101,6 @@
         piece = shifted(pieces[step].astype(jnp.bfloat16), axes, Z, step=depth - step)
         total = total + piece.astype(jnp.float32)
     return total
-
-
-def chip_totals(across, along_y, along_x, own):
-    across = shifted(across.astype(jnp.bfloat16), EXPERT, X, Y)
-    along_y = shifted(along_y.astype(jnp.bfloat16), EXPERT, Y)
-    along_x = shifted(along_x.astype(jnp.bfloat16), EXPERT, X)
-    total = own + across.astype(jnp.float32)
-    return total + along_y.astype(jnp.float32) + along_x.astype(jnp.float32)
 
 
 def across_by_turns(across):
@@ -497,21 +489,13 @@
     ]
     forward_near, forward_far = by_quarter(forward)
     far_grad = tuple(shifted(part, EXPERT, CORE) for part in near_grad)
-    across, along_y, along_x, own = core_totals(forward_near, forward_far)
-    forward_sums = [part.astype(jnp.bfloat16) for part in (across, along_y, along_x)] + [own]
-    mix_own, *forward_alongs = tied(near_grad[0], *forward_sums[1:])
-    near_grad = (mix_own,) + tuple(near_grad[1:])
+    forward_across, *forward_sums = core_totals(forward_near, forward_far)
+    forward_across = across_by_turns(forward_across)
+    forward_across, along_grads = tied(forward_across, near_grad[1:])
+    near_grad = near_grad[:1] + tuple(along_grads)
     backward = [
-        stage_sums(
-            backward_kernel, plans, near, far, *shared, STAGES[0], (near_grad, far_grad)
-        )
-    ]
-    along_grads, forward_across = tied(near_grad[1:], forward_sums[0])
-    forward_sums = [forward_across] + forward_alongs
-    near_grad = near_grad[:1] + tuple(along_grads)
-    backward += [
         stage_sums(backward_kernel, plans, near, far, *shared, stage, (near_grad, far_grad))
-        for stage in STAGES[1:]
+        for stage in STAGES
     ]
     backward[0], next_tokens, next_grads, down_near, up_near = tied(
         backward[0], next_tokens, next_grads, down_near, up_near
@@ -523,7 +507,7 @@
     quad_tokens = (tokens, other_tokens, next_tokens, last_tokens)
     quad_grads = (out_grad, other_grads, next_grads, last_grads)
 
-    mixed_sums = chip_totals(*forward_sums)
+    mixed_sums = chip_totals_by_turns(*forward_across, *forward_sums)
     backward_across, *backward_sums = core_totals(backward_near, backward_far)
     backward_across = across_by_turns(backward_across)
     mixed_sums, backward_across, backward_sums = tied(
@@ -532,7 +516,6 @@
     mixed_rows = tensor_total(depth_total(mixed_sums, EXPERT)).astype(jnp.bfloat16)
     mixed_relative = matmul(mixed_rows, up_place, ((1,), (1,))).astype(jnp.bfloat16)
     latent_sums = chip_totals_by_turns(*backward_across, *backward_sums)
-    mixed_relative, latent_sums = tied(mixed_relative, latent_sums)
     quad = quad_columns(mixed_relative, Y)
     latent_grad = tensor_total(depth_total(latent_sums, EXPERT)).astype(jnp.bfloat16)
     up_sent, up_kept = quad_grads_of(quad, quad_grads)

time: 211 us -> 225 us (1.066)
  waiting for transfers between devices: 92.7 us -> 107 us
    ppermute x74 -> x75, waiting for transfers between devices: 92.7 us -> 107 us  [shifted(): return lax.ppermute(block, axes, pairs)]
    ppermute x74 -> x75, starting transfers between devices: 66.7 us -> 66.3 us  [shifted(): return lax.ppermute(block, axes, pairs)]
  transfers between devices with their start and end apart: 74 -> 75, of which waited for: 33 -> 30; matrix products, arithmetic and copies ran while one was open for 5% -> 5% of each run, Pallas kernels for 15% -> 14%
where the time goes in v11:
time: 225 us; the launch traced here: 224 us
  waiting for transfers between devices  107 us (48%)
  starting transfers between devices  66.3 us (29%)
  Pallas kernels  35.1 us (16%)
  other arithmetic  6.78 us (3%)
  matrix products  4.62 us (2%)
  local copies, waits for them, and re-layouts  3.39 us (2%)
    ppermute x75, waiting for transfers between devices, shifted(): return lax.ppermute(block, axes, pairs)  107 us
    ppermute x75, starting transfers between devices, shifted(): return lax.ppermute(block, axes, pairs)  66.3 us
    pallas_call x6, Pallas kernels, expert_call(): pl.pallas_call(kernel, out_shape=(jax.ShapeDtypeStruct((span, latent_widt...  30.8 us
    dot_general x8, matrix products, matmul(): lax.dot_general(left, right, (contract, ((), ())), preferred_element_type...  4.52 us
  transfers between devices with their start and end apart: 75, of which 30 were waited for; matrix products, arithmetic and copies ran while one was open for 5% of the time, Pallas kernels for 14%

profile of v11, /device:TPU:0, one launch (start us, length us, event | category | flops | bytes accessed | tf_op | source)
XLA Modules:
  0.0 224.4 jit_solution(6997454431216866718)
XLA Ops:
  2.3 5.1 %collective-permute-start.2 = (bf16[16,4224]{1,0:T(8,128)(2,1)S(1)}, bf16[16,4224]{1,0:T(8,128)(2,1)S(1)}, u32[]{:S(2)}, u32[]{:S(2)}) collective-permute-start(bf16[16,4224]{1,0:T(8,128)(2,1)S(1)} %maximum_maximum_fusion), channel_id=1, source_target_pairs={{0,24},{1,25},{2,26},{3,27},{4,28},{5,29},{6,30},{7,31},{8,0},{9,1... | collective-permute-start | bytes 405512 | tf_op jit(solution)/shard_map/ppermute | solution.py:40
  8.6 2.9 %collective-permute-done.2 = bf16[16,4224]{1,0:T(8,128)(2,1)S(1)} collective-permute-done((bf16[16,4224]{1,0:T(8,128)(2,1)S(1)}, bf16[16,4224]{1,0:T(8,128)(2,1)S(1)}, u32[]{:S(2)}, u32[]{:S(2)}) %collective-permute-start.2) | collective-permute-done | bytes 135200 | tf_op jit(solution)/shard_map/ppermute | solution.py:40
  11.4 7.5 %collective-permute-done.1 = bf16[16,4224]{1,0:T(8,128)(2,1)S(1)} collective-permute-done((bf16[16,4224]{1,0:T(8,128)(2,1)S(1)}, bf16[16,4224]{1,0:T(8,128)(2,1)S(1)}, u32[]{:S(2)}, u32[]{:S(2)}) %collective-permute-start.1) | collective-permute-done | bytes 135200 | tf_op jit(solution)/shard_map/ppermute | solution.py:40
  19.9 1.6 collective-permute-start.5
  23.7 9.9 %collective-permute-done.5.refs_5_ = bf16[64,4224]{1,0:T(8,128)(2,1)} collective-permute-done((bf16[64,4224]{1,0:T(8,128)(2,1)S(1)}, bf16[64,4224]{1,0:T(8,128)(2,1)}, u32[]{:S(2)}, u32[]{:S(2)}) %collective-permute-start.5) | collective-permute-done | bytes 540704 | tf_op jit(solution)/shard_map/ppermute | solution.py:40
  33.6 1.7 slice.284
  37.5 1.5 collective-permute-start.8
  39.2 2.9 %collective-permute-done.7.refs_7_ = bf16[64,2048]{1,0:T(8,128)(2,1)} collective-permute-done((bf16[64,2048]{1,0:T(8,128)(2,1)}, bf16[64,2048]{1,0:T(8,128)(2,1)}, u32[]{:S(2)}, u32[]{:S(2)}) %collective-permute-start.7) | collective-permute-done | bytes 262176 | tf_op jit(solution)/shard_map/ppermute | solution.py:40
  42.2 2.2 collective-permute-done.8.refs_8_
  44.4 2.7 %shard_map.120 = (bf16[256,2048]{1,0:T(8,128)(2,1)S(1)}, bf16[256,2048]{1,0:T(8,128)(2,1)S(1)}, bf16[256,128]{1,0:T(8,128)(2,1)S(1)}, bf16[128,512]{1,0:T(8,128)(2,1)S(1)}, bf16[128,512]{1,0:T(8,128)(2,1)S(1)}) custom-call(bf16[128,2048]{1,0:T(8,128)(2,1)S(1)} %copy-done.4, bf16[128,2048]{1,0:T(8,128)(2,1)S(1)} %collective-permute-done.3.refs_1_.refs_5_, ...), custom_call_target="tpu_custom_call" | custom-call | flops 536870912 | bytes 4259840 | tf_op jit(solution)/shard_map/pallas_call | solution.py:130
  49.4 2.1 collective-permute-start.11
  51.5 1.9 collective-permute-start.10
  54.7 1.5 collective-permute-start.19
  56.8 6.9 %collective-permute-done.11 = bf16[128,512]{1,0:T(8,128)(2,1)S(1)} collective-permute-done((bf16[128,512]{1,0:T(8,128)(2,1)S(1)}, bf16[128,512]{1,0:T(8,128)(2,1)S(1)}, u32[]{:S(2)}, u32[]{:S(2)}) %collective-permute-start.11) | collective-permute-done | bytes 131104 | tf_op jit(solution)/shard_map/ppermute | solution.py:40
  64.4 1.5 collective-permute-start.16
  65.9 3.8 %collective-permute-done.15 = bf16[128,512]{1,0:T(8,128)(2,1)S(1)} collective-permute-done((bf16[128,512]{1,0:T(8,128)(2,1)S(1)}, bf16[128,512]{1,0:T(8,128)(2,1)S(1)}, u32[]{:S(2)}, u32[]{:S(2)}) %collective-permute-start.15) | collective-permute-done | bytes 131104 | tf_op jit(solution)/shard_map/ppermute | solution.py:40
  70.3 3.3 %collective-permute-done.14 = bf16[128,512]{1,0:T(8,128)(2,1)S(1)} collective-permute-done((bf16[128,512]{1,0:T(8,128)(2,1)S(1)}, bf16[128,512]{1,0:T(8,128)(2,1)S(1)}, u32[]{:S(2)}, u32[]{:S(2)}) %collective-permute-start.14) | collective-permute-done | bytes 131104 | tf_op jit(solution)/shard_map/ppermute | solution.py:40
  73.7 6.7 %collective-permute-done.13 = bf16[128,512]{1,0:T(8,128)(2,1)S(1)} collective-permute-done((bf16[128,512]{1,0:T(8,128)(2,1)S(1)}, bf16[128,512]{1,0:T(8,128)(2,1)S(1)}, u32[]{:S(2)}, u32[]{:S(2)}) %collective-permute-start.13) | collective-permute-done | bytes 131104 | tf_op jit(solution)/shard_map/ppermute | solution.py:40
  82.0 1.6 collective-permute-start.21
  84.1 6.0 %collective-permute-done.20 = bf16[512,256]{1,0:T(8,128)(2,1)S(1)} collective-permute-done((bf16[512,256]{1,0:T(8,128)(2,1)S(1)}, bf16[512,256]{1,0:T(8,128)(2,1)S(1)}, u32[]{:S(2)}, u32[]{:S(2)}) %collective-permute-start.20) | collective-permute-done | bytes 262176 | tf_op jit(solution)/shard_map/ppermute | solution.py:40
  90.1 1.5 collective-permute-start.32
  92.5 3.7 %shard_map.121 = (bf16[512,512]{1,0:T(8,128)(2,1)S(1)}, bf16[512,512]{1,0:T(8,128)(2,1)S(1)}) custom-call(s32[2,2,1,512]{3,2,1,0:T(1,128)S(1)} %pad_add_fusion.1.refs_0_, f32[2,2,1,512]{3,2,1,0:T(1,128)S(1)} %pad_maximum_fusion.9.refs_1_, bf16[512,512]{1,0:T(8,128)(2,1)S(1)} %pad_maximum_fusion.1.refs_2_, ...), custom_call_target="tpu_custom_call" | custom-call | flops 1207959552 | bytes 7348224 | tf_op jit(solution)/shard_map/pallas_call | solution.py:358
  96.2 7.5 %collective-permute-done.32.refs_6_ = bf16[512,512]{1,0:T(8,128)(2,1)S(1)} collective-permute-done((bf16[512,512]{1,0:T(8,128)(2,1)S(1)}, bf16[512,512]{1,0:T(8,128)(2,1)S(1)}, u32[]{:S(2)}, u32[]{:S(2)}) %collective-permute-start.32) | collective-permute-done | bytes 524320 | tf_op jit(solution)/shard_map/ppermute | solution.py:40
  104.3 5.3 %shard_map.122 = (bf16[512,512]{1,0:T(8,128)(2,1)S(1)}, bf16[512,512]{1,0:T(8,128)(2,1)S(1)}, bf16[512,512]{1,0:T(8,128)(2,1)S(1)}, bf16[512,512]{1,0:T(8,128)(2,1)S(1)}) custom-call(s32[4,2,1,512]{3,2,1,0:T(1,128)S(1)} %pad_add_fusion.refs_0_, f32[4,2,1,512]{3,2,1,0:T(1,128)S(1)} %pad_maximum_fusion.8.refs_1_, ...), custom_call_target="tpu_custom_call" | custom-call | flops 2415919104 | bytes 8404992 | tf_op jit(solution)/shard_map/pallas_call | solution.py:358
  110.0 1.6 collective-permute-start.35
  111.6 5.2 %shard_map.126 = (bf16[512,512]{1,0:T(8,128)(2,1)S(1)}, bf16[512,512]{1,0:T(8,128)(2,1)S(1)}) custom-call(s32[2,2,1,512]{3,2,1,0:T(1,128)S(1)} %pad_add_fusion.1.refs_0_, f32[2,2,1,512]{3,2,1,0:T(1,128)S(1)} %pad_maximum_fusion.9.refs_1_, bf16[512,512]{1,0:T(8,128)(2,1)S(1)} %pad_maximum_fusion.1.refs_2_, ...), custom_call_target="tpu_custom_call" | custom-call | flops 2013265920 | bytes 8396800 | tf_op jit(solution)/shard_map/pallas_call | solution.py:358
  119.1 3.5 %shard_map.123 = (bf16[512,512]{1,0:T(8,128)(2,1)S(1)}, bf16[512,512]{1,0:T(8,128)(2,1)S(1)}) custom-call(s32[2,2,1,512]{3,2,1,0:T(1,128)S(1)} %pad_add_fusion.2.refs_0_, f32[2,2,1,512]{3,2,1,0:T(1,128)S(1)} %pad_maximum_fusion.10.refs_1_, bf16[512,512]{1,0:T(8,128)(2,1)S(1)} %constant_dynamic-update-slice_fusion.refs_2_, ...), custom_call_target="tpu_custom_call" | custom-call | flops 1207959552 | bytes 7348224 | tf_op jit(solution)/shard_map/pallas_call | solution.py:358
  124.8 1.6 collective-permute-start.30
  126.4 1.5 collective-permute-start.31
  128.1 5.2 %collective-permute-done.30 = bf16[512,256]{1,0:T(8,128)(2,1)S(1)} collective-permute-done((bf16[512,256]{1,0:T(8,128)(2,1)S(1)}, bf16[512,256]{1,0:T(8,128)(2,1)S(1)}, u32[]{:S(2)}, u32[]{:S(2)}) %collective-permute-start.30) | collective-permute-done | bytes 262176 | tf_op jit(solution)/shard_map/ppermute | solution.py:40
  135.2 5.2 %shard_map.124 = (bf16[512,512]{1,0:T(8,128)(2,1)S(1)}, bf16[512,512]{1,0:T(8,128)(2,1)S(1)}) custom-call(s32[2,2,1,512]{3,2,1,0:T(1,128)S(1)} %pad_add_fusion.2.refs_0_, f32[2,2,1,512]{3,2,1,0:T(1,128)S(1)} %pad_maximum_fusion.10.refs_1_, bf16[512,512]{1,0:T(8,128)(2,1)S(1)} %constant_dynamic-update-slice_fusion.refs_2_, ...), custom_call_target="tpu_custom_call" | custom-call | flops 2013265920 | bytes 8396800 | tf_op jit(solution)/shard_map/pallas_call | solution.py:358
  140.6 7.7 %shard_map.125 = (bf16[512,512]{1,0:T(8,128)(2,1)S(1)}, bf16[512,512]{1,0:T(8,128)(2,1)S(1)}, bf16[512,512]{1,0:T(8,128)(2,1)S(1)}, bf16[512,512]{1,0:T(8,128)(2,1)S(1)}) custom-call(s32[4,2,1,512]{3,2,1,0:T(1,128)S(1)} %pad_add_fusion.refs_0_, f32[4,2,1,512]{3,2,1,0:T(1,128)S(1)} %pad_maximum_fusion.8.refs_1_, ...), custom_call_target="tpu_custom_call" | custom-call | flops 4026531840 | bytes 10502144 | tf_op jit(solution)/shard_map/pallas_call | solution.py:358
  149.0 1.6 collective-permute-start.36
  150.8 1.6 collective-permute-start.41
  153.7 10.2 %collective-permute-done.36 = bf16[512,512]{1,0:T(8,128)(2,1)S(1)} collective-permute-done((bf16[512,512]{1,0:T(8,128)(2,1)S(1)}, bf16[512,512]{1,0:T(8,128)(2,1)S(1)}, u32[]{:S(2)}, u32[]{:S(2)}) %collective-permute-start.36) | collective-permute-done | bytes 524320 | tf_op jit(solution)/shard_map/ppermute | solution.py:40
  164.3 4.3 %collective-permute-done.42 = bf16[512,256]{1,0:T(8,128)(2,1)S(1)} collective-permute-done((bf16[512,256]{1,0:T(8,128)(2,1)S(1)}, bf16[512,256]{1,0:T(8,128)(2,1)S(1)}, u32[]{:S(2)}, u32[]{:S(2)}) %collective-permute-start.42) | collective-permute-done | bytes 262176 | tf_op jit(solution)/shard_map/ppermute | solution.py:40
  168.8 1.6 collective-permute-start.58
  170.5 1.6 collective-permute-start.57
  172.8 2.4 %collective-permute-start.50 = (bf16[128,512]{1,0:T(8,128)(2,1)S(1)}, bf16[128,512]{1,0:T(8,128)(2,1)S(1)}, u32[]{:S(2)}, u32[]{:S(2)}) collective-permute-start(bf16[128,512]{1,0:T(8,128)(2,1)S(1)} %get-tuple-element.141), channel_id=1, source_target_pairs={{0,16},{1,17},{2,18},{3,19},{4,20},{5,21},{6,22},{7,23},{8,24},{9,... | collective-permute-start | bytes 393224 | tf_op jit(solution)/shard_map/ppermute | solution.py:40
  176.5 4.0 %collective-permute-done.51 = bf16[128,512]{1,0:T(8,128)(2,1)S(1)} collective-permute-done((bf16[128,512]{1,0:T(8,128)(2,1)S(1)}, bf16[128,512]{1,0:T(8,128)(2,1)S(1)}, u32[]{:S(2)}, u32[]{:S(2)}) %collective-permute-start.51) | collective-permute-done | bytes 131104 | tf_op jit(solution)/shard_map/ppermute | solution.py:40
  180.5 3.3 %collective-permute-done.50 = bf16[128,512]{1,0:T(8,128)(2,1)S(1)} collective-permute-done((bf16[128,512]{1,0:T(8,128)(2,1)S(1)}, bf16[128,512]{1,0:T(8,128)(2,1)S(1)}, u32[]{:S(2)}, u32[]{:S(2)}) %collective-permute-start.50) | collective-permute-done | bytes 131104 | tf_op jit(solution)/shard_map/ppermute | solution.py:40
  184.6 2.6 %collective-permute-start.61 = (bf16[128,512]{1,0:T(8,128)(2,1)S(1)}, bf16[128,512]{1,0:T(8,128)(2,1)S(1)}, u32[]{:S(2)}, u32[]{:S(2)}) collective-permute-start(bf16[128,512]{1,0:T(8,128)(2,1)S(1)} %get-tuple-element.137), channel_id=1, source_target_pairs={{0,8},{1,9},{2,10},{3,11},{4,12},{5,13},{6,14},{7,15},{8,16},{9,17... | collective-permute-start | bytes 393224 | tf_op jit(solution)/shard_map/ppermute | solution.py:40
  187.2 1.9 collective-permute-start.60
  191.6 2.1 collective-permute-done.53.refs_2_
  198.3 5.9 %collective-permute-done.56 = bf16[64,2048]{1,0:T(8,128)(2,1)S(1)} collective-permute-done((bf16[64,2048]{1,0:T(8,128)(2,1)S(1)}, bf16[64,2048]{1,0:T(8,128)(2,1)S(1)}, u32[]{:S(2)}, u32[]{:S(2)}) %collective-permute-start.56) | collective-permute-done | bytes 262176 | tf_op jit(solution)/shard_map/ppermute | solution.py:40
  205.0 2.6 %collective-permute-done.64.refs_3_ = bf16[128,128]{1,0:T(8,128)(2,1)S(1)} collective-permute-done((bf16[128,128]{1,0:T(8,128)(2,1)S(1)}, bf16[128,128]{1,0:T(8,128)(2,1)S(1)}, u32[]{:S(2)}, u32[]{:S(2)}) %collective-permute-start.64) | collective-permute-done | bytes 32800 | tf_op jit(solution)/shard_map/ppermute | solution.py:40
  217.2 1.8 collective-permute-start.70
  218.9 2.4 %collective-permute-start.69 = (bf16[16,2048]{1,0:T(8,128)(2,1)S(1)}, bf16[16,2048]{1,0:T(8,128)(2,1)S(1)}, u32[]{:S(2)}, u32[]{:S(2)}) collective-permute-start(bf16[16,2048]{1,0:T(8,128)(2,1)S(1)} %get-tuple-element.149), channel_id=1, source_target_pairs={{0,24},{1,25},{2,26},{3,27},{4,28},{5,29},{6,30},{7,31},{8,0},{9,1... | collective-permute-start | bytes 196616 | tf_op jit(solution)/shard_map/ppermute | solution.py:40
  (207 shorter events, 50.1 us)
Async XLA Ops:
  2.3 9.1 %collective-permute-start.2 = (bf16[16,4224]{1,0:T(8,128)(2,1)S(1)}, bf16[16,4224]{1,0:T(8,128)(2,1)S(1)}, u32[]{:S(2)}, u32[]{:S(2)}) collective-permute-start(bf16[16,4224]{1,0:T(8,128)(2,1)S(1)} %maximum_maximum_fusion), channel_id=1, source_target_pairs={{0,24},{1,25},{2,26},{3,27},{4,28},{5,29},{6,30},{7,31},{8,0},{9,1... | collective-permute-start | bytes 405512 | tf_op jit(solution)/shard_map/ppermute | solution.py:40
  7.4 11.5 %collective-permute-start.1 = (bf16[16,4224]{1,0:T(8,128)(2,1)S(1)}, bf16[16,4224]{1,0:T(8,128)(2,1)S(1)}, u32[]{:S(2)}, u32[]{:S(2)}) collective-permute-start(bf16[16,4224]{1,0:T(8,128)(2,1)S(1)} %maximum_maximum_fusion), channel_id=1, source_target_pairs={{0,16},{1,17},{2,18},{3,19},{4,20},{5,21},{6,22},{7,23},{8,24},{9,... | collective-permute-start | bytes 405512 | tf_op jit(solution)/shard_map/ppermute | solution.py:40
  7.4 11.5 %collective-permute-start = (bf16[16,4224]{1,0:T(8,128)(2,1)S(1)}, bf16[16,4224]{1,0:T(8,128)(2,1)S(1)}, u32[]{:S(2)}, u32[]{:S(2)}) collective-permute-start(bf16[16,4224]{1,0:T(8,128)(2,1)S(1)} %maximum_maximum_fusion), channel_id=1, source_target_pairs={{0,8},{1,9},{2,10},{3,11},{4,12},{5,13},{6,14},{7,15},{8,16},{9,17... | collective-permute-start | bytes 405512 | tf_op jit(solution)/shard_map/ppermute | solution.py:40
  19.9 13.7 %collective-permute-start.5 = (bf16[64,4224]{1,0:T(8,128)(2,1)S(1)}, bf16[64,4224]{1,0:T(8,128)(2,1)}, u32[]{:S(2)}, u32[]{:S(2)}) collective-permute-start(bf16[64,4224]{1,0:T(8,128)(2,1)S(1)} %pad_maximum_fusion.refs_4_), channel_id=1, source_target_pairs={{0,4},{1,5},{2,6},{3,7},{4,0},{5,1},{6,2},{7,3},{8,12},{9,13},{10,... | collective-permute-start | bytes 1622024 | tf_op jit(solution)/shard_map/ppermute | solution.py:40
  21.4 15.3 %collective-permute-start.6 = (bf16[64,4224]{1,0:T(8,128)(2,1)S(1)}, bf16[64,4224]{1,0:T(8,128)(2,1)S(1)}, u32[]{:S(2)}, u32[]{:S(2)}) collective-permute-start(bf16[64,4224]{1,0:T(8,128)(2,1)S(1)} %pad_maximum_fusion.refs_4_), channel_id=1, source_target_pairs={{0,2},{1,3},{2,0},{3,1},{4,6},{5,7},{6,4},{7,5},{8,10},{9,11},{10,... | collective-permute-start | bytes 1622024 | tf_op jit(solution)/shard_map/ppermute | solution.py:40
  23.1 16.1 %collective-permute-start.3 = (bf16[128,2048]{1,0:T(8,128)(2,1)S(1)}, bf16[128,2048]{1,0:T(8,128)(2,1)S(1)}, u32[]{:S(2)}, u32[]{:S(2)}) collective-permute-start(bf16[128,2048]{1,0:T(8,128)(2,1)S(1)} %copy-done.4), channel_id=1, source_target_pairs={{0,1},{1,0},{2,3},{3,2},{4,5},{5,4},{6,7},{7,6},{8,9},{9,8},{10,11... | collective-permute-start | bytes 1572872 | tf_op jit(solution)/shard_map/ppermute | solution.py:40
  23.2 16.1 %collective-permute-start.4 = (bf16[128,2048]{1,0:T(8,128)(2,1)S(1)}, bf16[128,2048]{1,0:T(8,128)(2,1)S(1)}, u32[]{:S(2)}, u32[]{:S(2)}) collective-permute-start(bf16[128,2048]{1,0:T(8,128)(2,1)S(1)} %copy-done.3), channel_id=1, source_target_pairs={{0,1},{1,0},{2,3},{3,2},{4,5},{5,4},{6,7},{7,6},{8,9},{9,8},{10,11... | collective-permute-start | bytes 1572872 | tf_op jit(solution)/shard_map/ppermute | solution.py:40
  49.4 14.3 %collective-permute-start.11 = (bf16[128,512]{1,0:T(8,128)(2,1)S(1)}, bf16[128,512]{1,0:T(8,128)(2,1)S(1)}, u32[]{:S(2)}, u32[]{:S(2)}) collective-permute-start(bf16[128,512]{1,0:T(8,128)(2,1)S(1)} %convolution_convert_fusion.3), channel_id=1, source_target_pairs={{0,16},{1,17},{2,18},{3,19},{4,20},{5,21},{6,22},{7,23},{8,24},{9,... | collective-permute-start | bytes 393224 | tf_op jit(solution)/shard_map/ppermute | solution.py:40
  51.5 12.2 %collective-permute-start.10 = (bf16[128,512]{1,0:T(8,128)(2,1)S(1)}, bf16[128,512]{1,0:T(8,128)(2,1)S(1)}, u32[]{:S(2)}, u32[]{:S(2)}) collective-permute-start(bf16[128,512]{1,0:T(8,128)(2,1)S(1)} %convolution_convert_fusion.3), channel_id=1, source_target_pairs={{0,8},{1,9},{2,10},{3,11},{4,12},{5,13},{6,14},{7,15},{8,16},{9,17... | collective-permute-start | bytes 393224 | tf_op jit(solution)/shard_map/ppermute | solution.py:40
  53.4 27.0 %collective-permute-start.18 = (bf16[128,2048]{1,0:T(8,128)(2,1)S(1)}, bf16[128,2048]{1,0:T(8,128)(2,1)S(1)}, u32[]{:S(2)}, u32[]{:S(2)}) collective-permute-start(bf16[128,2048]{1,0:T(8,128)(2,1)S(1)} %copy-done.4), channel_id=1, source_target_pairs={{0,2},{1,3},{2,0},{3,1},{4,6},{5,7},{6,4},{7,5},{8,10},{9,11},{10,... | collective-permute-start | bytes 1572872 | tf_op jit(solution)/shard_map/ppermute | solution.py:40
  54.7 25.8 %collective-permute-start.19 = (bf16[128,2048]{1,0:T(8,128)(2,1)S(1)}, bf16[128,2048]{1,0:T(8,128)(2,1)S(1)}, u32[]{:S(2)}, u32[]{:S(2)}) collective-permute-start(bf16[128,2048]{1,0:T(8,128)(2,1)S(1)} %copy-done.3), channel_id=1, source_target_pairs={{0,4},{1,5},{2,6},{3,7},{4,0},{5,1},{6,2},{7,3},{8,12},{9,13},{10,... | collective-permute-start | bytes 1572872 | tf_op jit(solution)/shard_map/ppermute | solution.py:40
  63.8 9.9 %collective-permute-start.14 = (bf16[128,512]{1,0:T(8,128)(2,1)S(1)}, bf16[128,512]{1,0:T(8,128)(2,1)S(1)}, u32[]{:S(2)}, u32[]{:S(2)}) collective-permute-start(bf16[128,512]{1,0:T(8,128)(2,1)S(1)} %convolution_convert_fusion.2), channel_id=1, source_target_pairs={{0,16},{1,17},{2,18},{3,19},{4,20},{5,21},{6,22},{7,23},{8,24},{9,... | collective-permute-start | bytes 393224 | tf_op jit(solution)/shard_map/ppermute | solution.py:40
  64.4 16.0 %collective-permute-start.16 = (bf16[512,512]{1,0:T(8,128)(2,1)S(1)}, bf16[512,512]{1,0:T(8,128)(2,1)S(1)}, u32[]{:S(2)}, u32[]{:S(2)}) collective-permute-start(bf16[512,512]{1,0:T(8,128)(2,1)S(1)} %pad_maximum_fusion.1.refs_2_), channel_id=1, source_target_pairs={{0,4},{1,5},{2,6},{3,7},{4,0},{5,1},{6,2},{7,3},{8,12},{9,13},{10,... | collective-permute-start | bytes 1572872 | tf_op jit(solution)/shard_map/ppermute | solution.py:40
  69.8 11.6 %collective-permute-start.17 = (bf16[512,512]{1,0:T(8,128)(2,1)S(1)}, bf16[512,512]{1,0:T(8,128)(2,1)S(1)}, u32[]{:S(2)}, u32[]{:S(2)}) collective-permute-start(bf16[512,512]{1,0:T(8,128)(2,1)S(1)} %pad_maximum_fusion.1.refs_2_), channel_id=1, source_target_pairs={{0,2},{1,3},{2,0},{3,1},{4,6},{5,7},{6,4},{7,5},{8,10},{9,11},{10,... | collective-permute-start | bytes 1572872 | tf_op jit(solution)/shard_map/ppermute | solution.py:40
  81.3 10.5 %collective-permute-start.23 = (bf16[512,512]{1,0:T(8,128)(2,1)S(1)}, bf16[512,512]{1,0:T(8,128)(2,1)S(1)}, u32[]{:S(2)}, u32[]{:S(2)}) collective-permute-start(bf16[512,512]{1,0:T(8,128)(2,1)S(1)} %pad_maximum_fusion.1.refs_2_), channel_id=1, source_target_pairs={{0,1},{1,0},{2,3},{3,2},{4,5},{5,4},{6,7},{7,6},{8,9},{9,8},{10,11... | collective-permute-start | bytes 1572872 | tf_op jit(solution)/shard_map/ppermute | solution.py:40
  81.4 8.8 %collective-permute-start.20 = (bf16[512,256]{1,0:T(8,128)(2,1)S(1)}, bf16[512,256]{1,0:T(8,128)(2,1)S(1)}, u32[]{:S(2)}, u32[]{:S(2)}) collective-permute-start(bf16[512,256]{1,0:T(8,128)(2,1)S(1)} %slice.230), channel_id=1, source_target_pairs={{0,2},{1,3},{2,0},{3,1},{4,6},{5,7},{6,4},{7,5},{8,10},{9,11},{10,... | collective-permute-start | bytes 786440 | tf_op jit(solution)/shard_map/ppermute | solution.py:40
  82.0 9.7 %collective-permute-start.21 = (bf16[512,256]{1,0:T(8,128)(2,1)S(1)}, bf16[512,256]{1,0:T(8,128)(2,1)S(1)}, u32[]{:S(2)}, u32[]{:S(2)}) collective-permute-start(bf16[512,256]{1,0:T(8,128)(2,1)S(1)} %slice.231), channel_id=1, source_target_pairs={{0,4},{1,5},{2,6},{3,7},{4,0},{5,1},{6,2},{7,3},{8,12},{9,13},{10,... | collective-permute-start | bytes 786440 | tf_op jit(solution)/shard_map/ppermute | solution.py:40
  83.6 20.1 %collective-permute-start.25 = (bf16[512,512]{1,0:T(8,128)(2,1)S(1)}, bf16[512,512]{1,0:T(8,128)(2,1)S(1)}, u32[]{:S(2)}, u32[]{:S(2)}) collective-permute-start(bf16[512,512]{1,0:T(8,128)(2,1)S(1)} %collective-permute-done.16.refs_2_), channel_id=1, source_target_pairs={{0,1},{1,0},{2,3},{3,2},{4,5},{5,4},{6,7},{7,6},{8,9},{9,8},{10,11... | collective-permute-start | bytes 1572872 | tf_op jit(solution)/shard_map/ppermute | solution.py:40
  83.6 20.7 %collective-permute-start.26 = (bf16[512,512]{1,0:T(8,128)(2,1)S(1)}, bf16[512,512]{1,0:T(8,128)(2,1)S(1)}, u32[]{:S(2)}, u32[]{:S(2)}) collective-permute-start(bf16[512,512]{1,0:T(8,128)(2,1)S(1)} %collective-permute-done.17.refs_3_), channel_id=1, source_target_pairs={{0,1},{1,0},{2,3},{3,2},{4,5},{5,4},{6,7},{7,6},{8,9},{9,8},{10,11... | collective-permute-start | bytes 1572872 | tf_op jit(solution)/shard_map/ppermute | solution.py:40
  90.1 13.6 %collective-permute-start.32 = (bf16[512,512]{1,0:T(8,128)(2,1)S(1)}, bf16[512,512]{1,0:T(8,128)(2,1)S(1)}, u32[]{:S(2)}, u32[]{:S(2)}) collective-permute-start(bf16[512,512]{1,0:T(8,128)(2,1)S(1)} %pad_maximum_fusion.2.refs_4_), channel_id=1, source_target_pairs={{0,4},{1,5},{2,6},{3,7},{4,0},{5,1},{6,2},{7,3},{8,12},{9,13},{10,... | collective-permute-start | bytes 1572872 | tf_op jit(solution)/shard_map/ppermute | solution.py:40
  91.7 19.8 %collective-permute-start.47 = (bf16[512,512]{1,0:T(8,128)(2,1)S(1)}, bf16[512,512]{1,0:T(8,128)(2,1)S(1)}, u32[]{:S(2)}, u32[]{:S(2)}) collective-permute-start(bf16[512,512]{1,0:T(8,128)(2,1)S(1)} %pad_maximum_fusion.2.refs_4_), channel_id=1, source_target_pairs={{0,1},{1,0},{2,3},{3,2},{4,5},{5,4},{6,7},{7,6},{8,9},{9,8},{10,11... | collective-permute-start | bytes 1572872 | tf_op jit(solution)/shard_map/ppermute | solution.py:40
  91.8 18.1 %collective-permute-start.33 = (bf16[512,512]{1,0:T(8,128)(2,1)S(1)}, bf16[512,512]{1,0:T(8,128)(2,1)S(1)}, u32[]{:S(2)}, u32[]{:S(2)}) collective-permute-start(bf16[512,512]{1,0:T(8,128)(2,1)S(1)} %pad_maximum_fusion.2.refs_4_), channel_id=1, source_target_pairs={{0,2},{1,3},{2,0},{3,1},{4,6},{5,7},{6,4},{7,5},{8,10},{9,11},{10,... | collective-permute-start | bytes 1572872 | tf_op jit(solution)/shard_map/ppermute | solution.py:40
  103.7 14.9 %collective-permute-start.28 = (bf16[512,512]{1,0:T(8,128)(2,1)S(1)}, bf16[512,512]{1,0:T(8,128)(2,1)S(1)}, u32[]{:S(2)}, u32[]{:S(2)}) collective-permute-start(bf16[512,512]{1,0:T(8,128)(2,1)S(1)} %constant_dynamic-update-slice_fusion.refs_2_), channel_id=1, source_target_pairs={{0,1},{1,0},{2,3},{3,2},{4,5},{5,4},{6,7},{7,6},{8,9},{9,8},{10,11... | collective-permute-start | bytes 1572872 | tf_op jit(solution)/shard_map/ppermute | solution.py:40
  103.7 13.2 %collective-permute-start.34 = (bf16[512,256]{1,0:T(8,128)(2,1)S(1)}, bf16[512,256]{1,0:T(8,128)(2,1)S(1)}, u32[]{:S(2)}, u32[]{:S(2)}) collective-permute-start(bf16[512,256]{1,0:T(8,128)(2,1)S(1)} %slice.309), channel_id=1, source_target_pairs={{0,2},{1,3},{2,0},{3,1},{4,6},{5,7},{6,4},{7,5},{8,10},{9,11},{10,... | collective-permute-start | bytes 786440 | tf_op jit(solution)/shard_map/ppermute | solution.py:40
  109.7 13.0 %collective-permute-start.37 = (bf16[512,512]{1,0:T(8,128)(2,1)S(1)}, bf16[512,512]{1,0:T(8,128)(2,1)S(1)}, u32[]{:S(2)}, u32[]{:S(2)}) collective-permute-start(bf16[512,512]{1,0:T(8,128)(2,1)S(1)} %get-tuple-element.95), channel_id=1, source_target_pairs={{0,1},{1,0},{2,3},{3,2},{4,5},{5,4},{6,7},{7,6},{8,9},{9,8},{10,11... | collective-permute-start | bytes 1572872 | tf_op jit(solution)/shard_map/ppermute | solution.py:40
  116.9 35.6 %collective-permute-start.24 = (bf16[512,512]{1,0:T(8,128)(2,1)S(1)}, bf16[512,512]{1,0:T(8,128)(2,1)S(1)}, u32[]{:S(2)}, u32[]{:S(2)}) collective-permute-start(bf16[512,512]{1,0:T(8,128)(2,1)S(1)} %get-tuple-element.86), channel_id=1, source_target_pairs={{0,1},{1,0},{2,3},{3,2},{4,5},{5,4},{6,7},{7,6},{8,9},{9,8},{10,11... | collective-permute-start | bytes 1572872 | tf_op jit(solution)/shard_map/ppermute | solution.py:40
  118.6 22.0 %collective-permute-start.43 = (bf16[512,512]{1,0:T(8,128)(2,1)S(1)}, bf16[512,512]{1,0:T(8,128)(2,1)S(1)}, u32[]{:S(2)}, u32[]{:S(2)}) collective-permute-start(bf16[512,512]{1,0:T(8,128)(2,1)S(1)} %collective-permute-done.32.refs_6_), channel_id=1, source_target_pairs={{0,1},{1,0},{2,3},{3,2},{4,5},{5,4},{6,7},{7,6},{8,9},{9,8},{10,11... | collective-permute-start | bytes 1572872 | tf_op jit(solution)/shard_map/ppermute | solution.py:40
  122.9 12.3 %collective-permute-start.39 = (bf16[512,512]{1,0:T(8,128)(2,1)S(1)}, bf16[512,512]{1,0:T(8,128)(2,1)S(1)}, u32[]{:S(2)}, u32[]{:S(2)}) collective-permute-start(bf16[512,512]{1,0:T(8,128)(2,1)S(1)} %constant_dynamic-update-slice_fusion.2.refs_4_), channel_id=1, source_target_pairs={{0,1},{1,0},{2,3},{3,2},{4,5},{5,4},{6,7},{7,6},{8,9},{9,8},{10,11... | collective-permute-start | bytes 1572872 | tf_op jit(solution)/shard_map/ppermute | solution.py:40
  134.6 19.1 %collective-permute-start.38 = (bf16[512,512]{1,0:T(8,128)(2,1)S(1)}, bf16[512,512]{1,0:T(8,128)(2,1)S(1)}, u32[]{:S(2)}, u32[]{:S(2)}) collective-permute-start(bf16[512,512]{1,0:T(8,128)(2,1)S(1)} %pad_maximum_fusion.4), channel_id=1, source_target_pairs={{0,2},{1,3},{2,0},{3,1},{4,6},{5,7},{6,4},{7,5},{8,10},{9,11},{10,... | collective-permute-start | bytes 1572872 | tf_op jit(solution)/shard_map/ppermute | solution.py:40
  140.5 10.1 %collective-permute-start.40 = (bf16[512,512]{1,0:T(8,128)(2,1)S(1)}, bf16[512,512]{1,0:T(8,128)(2,1)S(1)}, u32[]{:S(2)}, u32[]{:S(2)}) collective-permute-start(bf16[512,512]{1,0:T(8,128)(2,1)S(1)} %get-tuple-element.99), channel_id=1, source_target_pairs={{0,1},{1,0},{2,3},{3,2},{4,5},{5,4},{6,7},{7,6},{8,9},{9,8},{10,11... | collective-permute-start | bytes 1572872 | tf_op jit(solution)/shard_map/ppermute | solution.py:40
  149.0 14.8 %collective-permute-start.36 = (bf16[512,512]{1,0:T(8,128)(2,1)S(1)}, bf16[512,512]{1,0:T(8,128)(2,1)S(1)}, u32[]{:S(2)}, u32[]{:S(2)}) collective-permute-start(bf16[512,512]{1,0:T(8,128)(2,1)S(1)} %pad_maximum_fusion.3), channel_id=1, source_target_pairs={{0,4},{1,5},{2,6},{3,7},{4,0},{5,1},{6,2},{7,3},{8,12},{9,13},{10,... | collective-permute-start | bytes 1572872 | tf_op jit(solution)/shard_map/ppermute | solution.py:40
  150.6 13.5 %collective-permute-start.46 = (bf16[512,512]{1,0:T(8,128)(2,1)S(1)}, bf16[512,512]{1,0:T(8,128)(2,1)S(1)}, u32[]{:S(2)}, u32[]{:S(2)}) collective-permute-start(bf16[512,512]{1,0:T(8,128)(2,1)S(1)} %get-tuple-element.105), channel_id=1, source_target_pairs={{0,1},{1,0},{2,3},{3,2},{4,5},{5,4},{6,7},{7,6},{8,9},{9,8},{10,11... | collective-permute-start | bytes 1572872 | tf_op jit(solution)/shard_map/ppermute | solution.py:40
  150.8 13.5 %collective-permute-start.41 = (bf16[512,256]{1,0:T(8,128)(2,1)S(1)}, bf16[512,256]{1,0:T(8,128)(2,1)S(1)}, u32[]{:S(2)}, u32[]{:S(2)}) collective-permute-start(bf16[512,256]{1,0:T(8,128)(2,1)S(1)} %get-tuple-element.143), channel_id=1, source_target_pairs={{0,2},{1,3},{2,0},{3,1},{4,6},{5,7},{6,4},{7,5},{8,10},{9,11},{10,... | collective-permute-start | bytes 786440 | tf_op jit(solution)/shard_map/ppermute | solution.py:40
  152.5 16.0 %collective-permute-start.42 = (bf16[512,256]{1,0:T(8,128)(2,1)S(1)}, bf16[512,256]{1,0:T(8,128)(2,1)S(1)}, u32[]{:S(2)}, u32[]{:S(2)}) collective-permute-start(bf16[512,256]{1,0:T(8,128)(2,1)S(1)} %get-tuple-element.142), channel_id=1, source_target_pairs={{0,4},{1,5},{2,6},{3,7},{4,0},{5,1},{6,2},{7,3},{8,12},{9,13},{10,... | collective-permute-start | bytes 786440 | tf_op jit(solution)/shard_map/ppermute | solution.py:40
  168.8 15.5 %collective-permute-start.58 = (bf16[512,512]{1,0:T(8,128)(2,1)S(1)}, bf16[512,512]{1,0:T(8,128)(2,1)S(1)}, u32[]{:S(2)}, u32[]{:S(2)}) collective-permute-start(bf16[512,512]{1,0:T(8,128)(2,1)S(1)} %pad_maximum_fusion.6), channel_id=1, source_target_pairs={{0,2},{1,3},{2,0},{3,1},{4,6},{5,7},{6,4},{7,5},{8,10},{9,11},{10,... | collective-permute-start | bytes 1572872 | tf_op jit(solution)/shard_map/ppermute | solution.py:40
  170.5 13.8 %collective-permute-start.57 = (bf16[512,512]{1,0:T(8,128)(2,1)S(1)}, bf16[512,512]{1,0:T(8,128)(2,1)S(1)}, u32[]{:S(2)}, u32[]{:S(2)}) collective-permute-start(bf16[512,512]{1,0:T(8,128)(2,1)S(1)} %pad_maximum_fusion.5), channel_id=1, source_target_pairs={{0,4},{1,5},{2,6},{3,7},{4,0},{5,1},{6,2},{7,3},{8,12},{9,13},{10,... | collective-permute-start | bytes 1572872 | tf_op jit(solution)/shard_map/ppermute | solution.py:40
  172.8 11.1 %collective-permute-start.50 = (bf16[128,512]{1,0:T(8,128)(2,1)S(1)}, bf16[128,512]{1,0:T(8,128)(2,1)S(1)}, u32[]{:S(2)}, u32[]{:S(2)}) collective-permute-start(bf16[128,512]{1,0:T(8,128)(2,1)S(1)} %get-tuple-element.141), channel_id=1, source_target_pairs={{0,16},{1,17},{2,18},{3,19},{4,20},{5,21},{6,22},{7,23},{8,24},{9,... | collective-permute-start | bytes 393224 | tf_op jit(solution)/shard_map/ppermute | solution.py:40
  175.2 8.7 %collective-permute-start.49 = (bf16[128,512]{1,0:T(8,128)(2,1)S(1)}, bf16[128,512]{1,0:T(8,128)(2,1)S(1)}, u32[]{:S(2)}, u32[]{:S(2)}) collective-permute-start(bf16[128,512]{1,0:T(8,128)(2,1)S(1)} %get-tuple-element.139), channel_id=1, source_target_pairs={{0,24},{1,25},{2,26},{3,27},{4,28},{5,29},{6,30},{7,31},{8,0},{9,1... | collective-permute-start | bytes 393224 | tf_op jit(solution)/shard_map/ppermute | solution.py:40
  180.5 9.2 %collective-permute-start.55 = (bf16[128,2048]{1,0:T(8,128)(2,1)S(1)}, bf16[128,2048]{1,0:T(8,128)(2,1)S(1)}, u32[]{:S(2)}, u32[]{:S(2)}) collective-permute-start(bf16[128,2048]{1,0:T(8,128)(2,1)S(1)} %collective-permute-done.19.refs_6_), channel_id=1, source_target_pairs={{0,1},{1,0},{2,3},{3,2},{4,5},{5,4},{6,7},{7,6},{8,9},{9,8},{10,11... | collective-permute-start | bytes 1572872 | tf_op jit(solution)/shard_map/ppermute | solution.py:40
  184.6 11.0 %collective-permute-start.61 = (bf16[128,512]{1,0:T(8,128)(2,1)S(1)}, bf16[128,512]{1,0:T(8,128)(2,1)S(1)}, u32[]{:S(2)}, u32[]{:S(2)}) collective-permute-start(bf16[128,512]{1,0:T(8,128)(2,1)S(1)} %get-tuple-element.137), channel_id=1, source_target_pairs={{0,8},{1,9},{2,10},{3,11},{4,12},{5,13},{6,14},{7,15},{8,16},{9,17... | collective-permute-start | bytes 393224 | tf_op jit(solution)/shard_map/ppermute | solution.py:40
  187.2 9.8 %collective-permute-start.60 = (bf16[128,512]{1,0:T(8,128)(2,1)S(1)}, bf16[128,512]{1,0:T(8,128)(2,1)S(1)}, u32[]{:S(2)}, u32[]{:S(2)}) collective-permute-start(bf16[128,512]{1,0:T(8,128)(2,1)S(1)} %get-tuple-element.138), channel_id=1, source_target_pairs={{0,16},{1,17},{2,18},{3,19},{4,20},{5,21},{6,22},{7,23},{8,24},{9,... | collective-permute-start | bytes 393224 | tf_op jit(solution)/shard_map/ppermute | solution.py:40
  193.7 10.6 %collective-permute-start.65 = (bf16[128,2048]{1,0:T(8,128)(2,1)S(1)}, bf16[128,2048]{1,0:T(8,128)(2,1)S(1)}, u32[]{:S(2)}, u32[]{:S(2)}) collective-permute-start(bf16[128,2048]{1,0:T(8,128)(2,1)S(1)} %collective-permute-done.18.refs_6_), channel_id=1, source_target_pairs={{0,1},{1,0},{2,3},{3,2},{4,5},{5,4},{6,7},{7,6},{8,9},{9,8},{10,11... | collective-permute-start | bytes 1572872 | tf_op jit(solution)/shard_map/ppermute | solution.py:40
  194.3 18.3 %collective-permute-start.66 = (bf16[256,2048]{1,0:T(8,128)(2,1)S(1)}, bf16[256,2048]{1,0:T(8,128)(2,1)S(1)}, u32[]{:S(2)}, u32[]{:S(2)}) collective-permute-start(bf16[256,2048]{1,0:T(8,128)(2,1)S(1)} %get-tuple-element.126), channel_id=1, source_target_pairs={{0,1},{1,0},{2,3},{3,2},{4,5},{5,4},{6,7},{7,6},{8,9},{9,8},{10,11... | collective-permute-start | bytes 3145736 | tf_op jit(solution)/shard_map/ppermute | solution.py:40
  195.6 8.7 %collective-permute-start.56 = (bf16[64,2048]{1,0:T(8,128)(2,1)S(1)}, bf16[64,2048]{1,0:T(8,128)(2,1)S(1)}, u32[]{:S(2)}, u32[]{:S(2)}) collective-permute-start(bf16[64,2048]{1,0:T(8,128)(2,1)S(1)} %get-tuple-element.117), channel_id=1, source_target_pairs={{0,2},{1,3},{2,0},{3,1},{4,6},{5,7},{6,4},{7,5},{8,10},{9,11},{10,... | collective-permute-start | bytes 786440 | tf_op jit(solution)/shard_map/ppermute | solution.py:40
  204.3 10.9 %collective-permute-start.67 = (bf16[256,2048]{1,0:T(8,128)(2,1)S(1)}, bf16[256,2048]{1,0:T(8,128)(2,1)S(1)}, u32[]{:S(2)}, u32[]{:S(2)}) collective-permute-start(bf16[256,2048]{1,0:T(8,128)(2,1)S(1)} %get-tuple-element.128), channel_id=1, source_target_pairs={{0,1},{1,0},{2,3},{3,2},{4,5},{5,4},{6,7},{7,6},{8,9},{9,8},{10,11... | collective-permute-start | bytes 3145736 | tf_op jit(solution)/shard_map/ppermute | solution.py:40
  209.4 9.5 %collective-permute-start.74 = (bf16[16,2048]{1,0:T(8,128)(2,1)S(1)}, bf16[16,2048]{1,0:T(8,128)(2,1)S(1)}, u32[]{:S(2)}, u32[]{:S(2)}) collective-permute-start(bf16[16,2048]{1,0:T(8,128)(2,1)S(1)} %get-tuple-element.147), channel_id=1, source_target_pairs={{0,8},{1,9},{2,10},{3,11},{4,12},{5,13},{6,14},{7,15},{8,16},{9,17... | collective-permute-start | bytes 196616 | tf_op jit(solution)/shard_map/ppermute | solution.py:40
  210.9 10.4 %collective-permute-start.73 = (bf16[16,2048]{1,0:T(8,128)(2,1)S(1)}, bf16[16,2048]{1,0:T(8,128)(2,1)S(1)}, u32[]{:S(2)}, u32[]{:S(2)}) collective-permute-start(bf16[16,2048]{1,0:T(8,128)(2,1)S(1)} %get-tuple-element.148), channel_id=1, source_target_pairs={{0,16},{1,17},{2,18},{3,19},{4,20},{5,21},{6,22},{7,23},{8,24},{9,... | collective-permute-start | bytes 196616 | tf_op jit(solution)/shard_map/ppermute | solution.py:40
  212.6 8.7 %collective-permute-start.72 = (bf16[16,2048]{1,0:T(8,128)(2,1)S(1)}, bf16[16,2048]{1,0:T(8,128)(2,1)S(1)}, u32[]{:S(2)}, u32[]{:S(2)}) collective-permute-start(bf16[16,2048]{1,0:T(8,128)(2,1)S(1)} %get-tuple-element.146), channel_id=1, source_target_pairs={{0,24},{1,25},{2,26},{3,27},{4,28},{5,29},{6,30},{7,31},{8,0},{9,1... | collective-permute-start | bytes 196616 | tf_op jit(solution)/shard_map/ppermute | solution.py:40
  (32 other events, 278.8 us)

commit v12 on v9

--- a/solution.py
+++ b/solution.py
@@ -485,16 +485,19 @@
     near = gather_chips_by_turns(near, EXPERT, Y, X)
     far = tuple(shifted(part, EXPERT, CORE) for part in near[:3])
     near_grad = (mix_own, shifted(mix_own, EXPERT, Y), shifted(mix_own, EXPERT, X))
-    near_grad = gather_chips_by_turns(near_grad, EXPERT, Y, X)
 
     weights = (expert_gate, expert_up, expert_down)
     shared = (weights, slot_count)
     first_sums = stage_sums(forward_kernel, plans, near, far, *shared, STAGES[0])
     last_near, first_sums = tied(near[3], first_sums)
     far = far + (shifted(last_near, EXPERT, CORE),)
-    forward = [first_sums] + [
-        stage_sums(forward_kernel, plans, near, far, *shared, stage) for stage in STAGES[1:]
-    ]
+    middle_sums, last_sums, near_grad = tied(
+        stage_sums(forward_kernel, plans, near, far, *shared, STAGES[1]),
+        stage_sums(forward_kernel, plans, near, far, *shared, STAGES[2]),
+        near_grad,
+    )
+    near_grad = gather_chips_by_turns(near_grad, EXPERT, Y, X)
+    forward = [first_sums, middle_sums, last_sums]
     forward_near, forward_far = by_quarter(forward)
     far_grad = tuple(shifted(part, EXPERT, CORE) for part in near_grad)
     across, along_y, along_x, own = core_totals(forward_near, forward_far)

time: 211 us -> 214 us (1.014)
  waiting for transfers between devices: 92.7 us -> 99.6 us
  starting transfers between devices: 66.7 us -> 63.5 us
    ppermute x74, waiting for transfers between devices: 92.7 us -> 99.6 us  [shifted(): return lax.ppermute(block, axes, pairs)]
    ppermute x74, starting transfers between devices: 66.7 us -> 63.5 us  [shifted(): return lax.ppermute(block, axes, pairs)]
  transfers between devices with their start and end apart: 74 -> 74, of which waited for: 33 -> 32; matrix products, arithmetic and copies ran while one was open for 5% -> 5% of each run, Pallas kernels for 15% -> 15%
where the time goes in v12:
time: 214 us
  waiting for transfers between devices  99.6 us (47%)
  starting transfers between devices  63.5 us (30%)
  Pallas kernels  34.9 us (16%)
  other arithmetic  6.72 us (3%)
  matrix products  4.61 us (2%)
  local copies, waits for them, and re-layouts  3.28 us (2%)
    ppermute x74, waiting for transfers between devices, shifted(): return lax.ppermute(block, axes, pairs)  99.6 us
    ppermute x74, starting transfers between devices, shifted(): return lax.ppermute(block, axes, pairs)  63.5 us
    pallas_call x6, Pallas kernels, expert_call(): pl.pallas_call(kernel, out_shape=(jax.ShapeDtypeStruct((span, latent_widt...  30.6 us
    dot_general x8, matrix products, matmul(): lax.dot_general(left, right, (contract, ((), ())), preferred_element_type...  4.52 us
    pallas_call x3, Pallas kernels, vmem_call(): pl.pallas_call(kernel, out_shape=out_shape, in_specs=[whole] * len(operan...  4.28 us
  transfers between devices with their start and end apart: 74, of which 32 were waited for; matrix products, arithmetic and copies ran while one was open for 5% of the time, Pallas kernels for 15%

profile of v12, /device:TPU:0, one launch (start us, length us, event | category | flops | bytes accessed | tf_op | source)
XLA Modules:
  0.0 214.1 jit_solution(10021387471076516735)
XLA Ops:
  2.3 5.1 %collective-permute-start.2 = (bf16[16,4224]{1,0:T(8,128)(2,1)S(1)}, bf16[16,4224]{1,0:T(8,128)(2,1)S(1)}, u32[]{:S(2)}, u32[]{:S(2)}) collective-permute-start(bf16[16,4224]{1,0:T(8,128)(2,1)S(1)} %maximum_maximum_fusion), channel_id=1, source_target_pairs={{0,24},{1,25},{2,26},{3,27},{4,28},{5,29},{6,30},{7,31},{8,0},{9,1... | collective-permute-start | bytes 405512 | tf_op jit(solution)/shard_map/ppermute | solution.py:40
  8.6 2.9 %collective-permute-done.2 = bf16[16,4224]{1,0:T(8,128)(2,1)S(1)} collective-permute-done((bf16[16,4224]{1,0:T(8,128)(2,1)S(1)}, bf16[16,4224]{1,0:T(8,128)(2,1)S(1)}, u32[]{:S(2)}, u32[]{:S(2)}) %collective-permute-start.2) | collective-permute-done | bytes 135200 | tf_op jit(solution)/shard_map/ppermute | solution.py:40
  11.4 7.5 %collective-permute-done.1 = bf16[16,4224]{1,0:T(8,128)(2,1)S(1)} collective-permute-done((bf16[16,4224]{1,0:T(8,128)(2,1)S(1)}, bf16[16,4224]{1,0:T(8,128)(2,1)S(1)}, u32[]{:S(2)}, u32[]{:S(2)}) %collective-permute-start.1) | collective-permute-done | bytes 135200 | tf_op jit(solution)/shard_map/ppermute | solution.py:40
  19.9 1.6 collective-permute-start.5
  21.4 1.5 collective-permute-start.6
  23.7 9.9 %collective-permute-done.5.refs_5_ = bf16[64,4224]{1,0:T(8,128)(2,1)} collective-permute-done((bf16[64,4224]{1,0:T(8,128)(2,1)S(1)}, bf16[64,4224]{1,0:T(8,128)(2,1)}, u32[]{:S(2)}, u32[]{:S(2)}) %collective-permute-start.5) | collective-permute-done | bytes 540704 | tf_op jit(solution)/shard_map/ppermute | solution.py:40
  33.6 1.7 slice.258
  35.2 1.5 collective-permute-start.7
  37.5 1.5 collective-permute-start.8
  39.2 2.9 %collective-permute-done.7.refs_7_ = bf16[64,2048]{1,0:T(8,128)(2,1)} collective-permute-done((bf16[64,2048]{1,0:T(8,128)(2,1)}, bf16[64,2048]{1,0:T(8,128)(2,1)}, u32[]{:S(2)}, u32[]{:S(2)}) %collective-permute-start.7) | collective-permute-done | bytes 262176 | tf_op jit(solution)/shard_map/ppermute | solution.py:40
  42.2 2.2 %collective-permute-done.8.refs_8_ = bf16[64,2176]{1,0:T(8,128)(2,1)S(1)} collective-permute-done((bf16[64,2176]{1,0:T(8,128)(2,1)}, bf16[64,2176]{1,0:T(8,128)(2,1)S(1)}, u32[]{:S(2)}, u32[]{:S(2)}) %collective-permute-start.8) | collective-permute-done | bytes 278560 | tf_op jit(solution)/shard_map/ppermute | solution.py:40
  44.4 2.7 %shard_map.120 = (bf16[256,2048]{1,0:T(8,128)(2,1)S(1)}, bf16[256,2048]{1,0:T(8,128)(2,1)S(1)}, bf16[256,128]{1,0:T(8,128)(2,1)S(1)}, bf16[128,512]{1,0:T(8,128)(2,1)S(1)}, bf16[128,512]{1,0:T(8,128)(2,1)S(1)}) custom-call(bf16[128,2048]{1,0:T(8,128)(2,1)S(1)} %copy-done.4, bf16[128,2048]{1,0:T(8,128)(2,1)S(1)} %collective-permute-done.3.refs_1_.refs_5_, ...), custom_call_target="tpu_custom_call" | custom-call | flops 536870912 | bytes 4259840 | tf_op jit(solution)/shard_map/pallas_call | solution.py:138
  49.4 2.1 collective-permute-start.12
  51.5 1.9 collective-permute-start.11
  54.7 1.5 collective-permute-start.20
  56.8 6.9 %collective-permute-done.12 = bf16[128,512]{1,0:T(8,128)(2,1)S(1)} collective-permute-done((bf16[128,512]{1,0:T(8,128)(2,1)S(1)}, bf16[128,512]{1,0:T(8,128)(2,1)S(1)}, u32[]{:S(2)}, u32[]{:S(2)}) %collective-permute-start.12) | collective-permute-done | bytes 131104 | tf_op jit(solution)/shard_map/ppermute | solution.py:40
  64.4 1.5 collective-permute-start.17
  65.9 3.8 %collective-permute-done.16 = bf16[128,512]{1,0:T(8,128)(2,1)S(1)} collective-permute-done((bf16[128,512]{1,0:T(8,128)(2,1)S(1)}, bf16[128,512]{1,0:T(8,128)(2,1)S(1)}, u32[]{:S(2)}, u32[]{:S(2)}) %collective-permute-start.16) | collective-permute-done | bytes 131104 | tf_op jit(solution)/shard_map/ppermute | solution.py:40
  70.3 3.3 %collective-permute-done.15 = bf16[128,512]{1,0:T(8,128)(2,1)S(1)} collective-permute-done((bf16[128,512]{1,0:T(8,128)(2,1)S(1)}, bf16[128,512]{1,0:T(8,128)(2,1)S(1)}, u32[]{:S(2)}, u32[]{:S(2)}) %collective-permute-start.15) | collective-permute-done | bytes 131104 | tf_op jit(solution)/shard_map/ppermute | solution.py:40
  73.7 6.7 %collective-permute-done.14 = bf16[128,512]{1,0:T(8,128)(2,1)S(1)} collective-permute-done((bf16[128,512]{1,0:T(8,128)(2,1)S(1)}, bf16[128,512]{1,0:T(8,128)(2,1)S(1)}, u32[]{:S(2)}, u32[]{:S(2)}) %collective-permute-start.14) | collective-permute-done | bytes 131104 | tf_op jit(solution)/shard_map/ppermute | solution.py:40
  82.0 1.6 collective-permute-start.24
  84.2 6.0 %collective-permute-done.23 = bf16[512,256]{1,0:T(8,128)(2,1)S(1)} collective-permute-done((bf16[512,256]{1,0:T(8,128)(2,1)S(1)}, bf16[512,256]{1,0:T(8,128)(2,1)S(1)}, u32[]{:S(2)}, u32[]{:S(2)}) %collective-permute-start.23) | collective-permute-done | bytes 262176 | tf_op jit(solution)/shard_map/ppermute | solution.py:40
  90.6 3.5 %shard_map.122 = (bf16[512,512]{1,0:T(8,128)(2,1)S(1)}, bf16[512,512]{1,0:T(8,128)(2,1)S(1)}) custom-call(s32[2,2,1,512]{3,2,1,0:T(1,128)S(1)} %pad_add_fusion.2.refs_0_, f32[2,2,1,512]{3,2,1,0:T(1,128)S(1)} %pad_maximum_fusion.8.refs_1_, bf16[512,512]{1,0:T(8,128)(2,1)S(1)} %pad_maximum_fusion.1.refs_2_, ...), custom_call_target="tpu_custom_call" | custom-call | flops 1207959552 | bytes 7348224 | tf_op jit(solution)/shard_map/pallas_call | solution.py:366
  94.2 1.6 collective-permute-start.27
  95.8 1.5 collective-permute-start.28
  97.3 5.3 %shard_map.121 = (bf16[512,512]{1,0:T(8,128)(2,1)S(1)}, bf16[512,512]{1,0:T(8,128)(2,1)S(1)}, bf16[512,512]{1,0:T(8,128)(2,1)S(1)}, bf16[512,512]{1,0:T(8,128)(2,1)S(1)}) custom-call(s32[4,2,1,512]{3,2,1,0:T(1,128)S(1)} %pad_add_fusion.refs_0_, f32[4,2,1,512]{3,2,1,0:T(1,128)S(1)} %pad_maximum_fusion.6.refs_1_, ...), custom_call_target="tpu_custom_call" | custom-call | flops 2415919104 | bytes 8404992 | tf_op jit(solution)/shard_map/pallas_call | solution.py:366
  102.7 3.5 %shard_map.123 = (bf16[512,512]{1,0:T(8,128)(2,1)S(1)}, bf16[512,512]{1,0:T(8,128)(2,1)S(1)}) custom-call(s32[2,2,1,512]{3,2,1,0:T(1,128)S(1)} %pad_add_fusion.1.refs_0_, f32[2,2,1,512]{3,2,1,0:T(1,128)S(1)} %pad_maximum_fusion.7.refs_1_, bf16[512,512]{1,0:T(8,128)(2,1)S(1)} %constant_dynamic-update-slice_fusion.refs_2_, ...), custom_call_target="tpu_custom_call" | custom-call | flops 1207959552 | bytes 7348224 | tf_op jit(solution)/shard_map/pallas_call | solution.py:366
  106.2 2.3 %collective-permute-done.27.refs_6_ = bf16[512,512]{1,0:T(8,128)(2,1)S(1)} collective-permute-done((bf16[512,512]{1,0:T(8,128)(2,1)S(1)}, bf16[512,512]{1,0:T(8,128)(2,1)S(1)}, u32[]{:S(2)}, u32[]{:S(2)}) %collective-permute-start.27) | collective-permute-done | bytes 524320 | tf_op jit(solution)/shard_map/ppermute | solution.py:40
  110.4 1.5 collective-permute-start.32
  112.7 6.4 %collective-permute-done.32 = bf16[512,256]{1,0:T(8,128)(2,1)S(1)} collective-permute-done((bf16[512,256]{1,0:T(8,128)(2,1)S(1)}, bf16[512,256]{1,0:T(8,128)(2,1)S(1)}, u32[]{:S(2)}, u32[]{:S(2)}) %collective-permute-start.32) | collective-permute-done | bytes 262176 | tf_op jit(solution)/shard_map/ppermute | solution.py:40
  121.4 1.7 collective-permute-done.34
  124.7 2.1 collective-permute-start.35
  126.8 7.5 %shard_map.125 = (bf16[512,512]{1,0:T(8,128)(2,1)S(1)}, bf16[512,512]{1,0:T(8,128)(2,1)S(1)}, bf16[512,512]{1,0:T(8,128)(2,1)S(1)}, bf16[512,512]{1,0:T(8,128)(2,1)S(1)}) custom-call(s32[4,2,1,512]{3,2,1,0:T(1,128)S(1)} %pad_add_fusion.refs_0_, f32[4,2,1,512]{3,2,1,0:T(1,128)S(1)} %pad_maximum_fusion.6.refs_1_, ...), custom_call_target="tpu_custom_call" | custom-call | flops 4026531840 | bytes 10502144 | tf_op jit(solution)/shard_map/pallas_call | solution.py:366
  134.4 5.5 %shard_map.126 = (bf16[512,512]{1,0:T(8,128)(2,1)S(1)}, bf16[512,512]{1,0:T(8,128)(2,1)S(1)}) custom-call(s32[2,2,1,512]{3,2,1,0:T(1,128)S(1)} %pad_add_fusion.2.refs_0_, f32[2,2,1,512]{3,2,1,0:T(1,128)S(1)} %pad_maximum_fusion.8.refs_1_, bf16[512,512]{1,0:T(8,128)(2,1)S(1)} %pad_maximum_fusion.1.refs_2_, ...), custom_call_target="tpu_custom_call" | custom-call | flops 2013265920 | bytes 8396800 | tf_op jit(solution)/shard_map/pallas_call | solution.py:366
  140.4 5.2 %shard_map.124 = (bf16[512,512]{1,0:T(8,128)(2,1)S(1)}, bf16[512,512]{1,0:T(8,128)(2,1)S(1)}) custom-call(s32[2,2,1,512]{3,2,1,0:T(1,128)S(1)} %pad_add_fusion.1.refs_0_, f32[2,2,1,512]{3,2,1,0:T(1,128)S(1)} %pad_maximum_fusion.7.refs_1_, bf16[512,512]{1,0:T(8,128)(2,1)S(1)} %constant_dynamic-update-slice_fusion.refs_2_, ...), custom_call_target="tpu_custom_call" | custom-call | flops 2013265920 | bytes 8396800 | tf_op jit(solution)/shard_map/pallas_call | solution.py:366
  145.8 3.3 %collective-permute-done.36 = bf16[512,512]{1,0:T(8,128)(2,1)S(1)} collective-permute-done((bf16[512,512]{1,0:T(8,128)(2,1)S(1)}, bf16[512,512]{1,0:T(8,128)(2,1)S(1)}, u32[]{:S(2)}, u32[]{:S(2)}) %collective-permute-start.36) | collective-permute-done | bytes 524320 | tf_op jit(solution)/shard_map/ppermute | solution.py:40
  152.5 7.1 %collective-permute-done.40 = bf16[512,256]{1,0:T(8,128)(2,1)S(1)} collective-permute-done((bf16[512,256]{1,0:T(8,128)(2,1)S(1)}, bf16[512,256]{1,0:T(8,128)(2,1)S(1)}, u32[]{:S(2)}, u32[]{:S(2)}) %collective-permute-start.40) | collective-permute-done | bytes 262176 | tf_op jit(solution)/shard_map/ppermute | solution.py:40
  162.8 2.4 %collective-permute-start.49 = (bf16[128,512]{1,0:T(8,128)(2,1)S(1)}, bf16[128,512]{1,0:T(8,128)(2,1)S(1)}, u32[]{:S(2)}, u32[]{:S(2)}) collective-permute-start(bf16[128,512]{1,0:T(8,128)(2,1)S(1)} %get-tuple-element.167), channel_id=1, source_target_pairs={{0,16},{1,17},{2,18},{3,19},{4,20},{5,21},{6,22},{7,23},{8,24},{9,... | collective-permute-start | bytes 393224 | tf_op jit(solution)/shard_map/ppermute | solution.py:40
  166.6 4.0 %collective-permute-done.50 = bf16[128,512]{1,0:T(8,128)(2,1)S(1)} collective-permute-done((bf16[128,512]{1,0:T(8,128)(2,1)S(1)}, bf16[128,512]{1,0:T(8,128)(2,1)S(1)}, u32[]{:S(2)}, u32[]{:S(2)}) %collective-permute-start.50) | collective-permute-done | bytes 131104 | tf_op jit(solution)/shard_map/ppermute | solution.py:40
  170.6 3.4 %collective-permute-done.49 = bf16[128,512]{1,0:T(8,128)(2,1)S(1)} collective-permute-done((bf16[128,512]{1,0:T(8,128)(2,1)S(1)}, bf16[128,512]{1,0:T(8,128)(2,1)S(1)}, u32[]{:S(2)}, u32[]{:S(2)}) %collective-permute-start.49) | collective-permute-done | bytes 131104 | tf_op jit(solution)/shard_map/ppermute | solution.py:40
  174.8 2.6 %collective-permute-start.60 = (bf16[128,512]{1,0:T(8,128)(2,1)S(1)}, bf16[128,512]{1,0:T(8,128)(2,1)S(1)}, u32[]{:S(2)}, u32[]{:S(2)}) collective-permute-start(bf16[128,512]{1,0:T(8,128)(2,1)S(1)} %get-tuple-element.163), channel_id=1, source_target_pairs={{0,8},{1,9},{2,10},{3,11},{4,12},{5,13},{6,14},{7,15},{8,16},{9,17... | collective-permute-start | bytes 393224 | tf_op jit(solution)/shard_map/ppermute | solution.py:40
  177.5 1.9 collective-permute-start.59
  180.0 1.5 collective-permute-start.54
  182.4 1.6 collective-permute-done.54.refs_2_
  190.3 5.2 %collective-permute-done.62.refs_2_ = bf16[128,128]{1,0:T(8,128)(2,1)S(1)} collective-permute-done((bf16[128,128]{1,0:T(8,128)(2,1)S(1)}, bf16[128,128]{1,0:T(8,128)(2,1)S(1)}, u32[]{:S(2)}, u32[]{:S(2)}) %collective-permute-start.62) | collective-permute-done | bytes 32800 | tf_op jit(solution)/shard_map/ppermute | solution.py:40
  200.5 1.7 collective-permute-start.71
  207.2 2.3 %collective-permute-start.68 = (bf16[16,2048]{1,0:T(8,128)(2,1)S(1)}, bf16[16,2048]{1,0:T(8,128)(2,1)S(1)}, u32[]{:S(2)}, u32[]{:S(2)}) collective-permute-start(bf16[16,2048]{1,0:T(8,128)(2,1)S(1)} %get-tuple-element.173), channel_id=1, source_target_pairs={{0,24},{1,25},{2,26},{3,27},{4,28},{5,29},{6,30},{7,31},{8,0},{9,1... | collective-permute-start | bytes 196616 | tf_op jit(solution)/shard_map/ppermute | solution.py:40
  211.5 1.8 collective-permute-done.69
  (200 shorter events, 49.8 us)
Async XLA Ops:
  2.3 9.1 %collective-permute-start.2 = (bf16[16,4224]{1,0:T(8,128)(2,1)S(1)}, bf16[16,4224]{1,0:T(8,128)(2,1)S(1)}, u32[]{:S(2)}, u32[]{:S(2)}) collective-permute-start(bf16[16,4224]{1,0:T(8,128)(2,1)S(1)} %maximum_maximum_fusion), channel_id=1, source_target_pairs={{0,24},{1,25},{2,26},{3,27},{4,28},{5,29},{6,30},{7,31},{8,0},{9,1... | collective-permute-start | bytes 405512 | tf_op jit(solution)/shard_map/ppermute | solution.py:40
  7.4 11.5 %collective-permute-start.1 = (bf16[16,4224]{1,0:T(8,128)(2,1)S(1)}, bf16[16,4224]{1,0:T(8,128)(2,1)S(1)}, u32[]{:S(2)}, u32[]{:S(2)}) collective-permute-start(bf16[16,4224]{1,0:T(8,128)(2,1)S(1)} %maximum_maximum_fusion), channel_id=1, source_target_pairs={{0,16},{1,17},{2,18},{3,19},{4,20},{5,21},{6,22},{7,23},{8,24},{9,... | collective-permute-start | bytes 405512 | tf_op jit(solution)/shard_map/ppermute | solution.py:40
  7.4 11.5 %collective-permute-start = (bf16[16,4224]{1,0:T(8,128)(2,1)S(1)}, bf16[16,4224]{1,0:T(8,128)(2,1)S(1)}, u32[]{:S(2)}, u32[]{:S(2)}) collective-permute-start(bf16[16,4224]{1,0:T(8,128)(2,1)S(1)} %maximum_maximum_fusion), channel_id=1, source_target_pairs={{0,8},{1,9},{2,10},{3,11},{4,12},{5,13},{6,14},{7,15},{8,16},{9,17... | collective-permute-start | bytes 405512 | tf_op jit(solution)/shard_map/ppermute | solution.py:40
  19.9 13.7 %collective-permute-start.5 = (bf16[64,4224]{1,0:T(8,128)(2,1)S(1)}, bf16[64,4224]{1,0:T(8,128)(2,1)}, u32[]{:S(2)}, u32[]{:S(2)}) collective-permute-start(bf16[64,4224]{1,0:T(8,128)(2,1)S(1)} %pad_maximum_fusion.refs_4_), channel_id=1, source_target_pairs={{0,4},{1,5},{2,6},{3,7},{4,0},{5,1},{6,2},{7,3},{8,12},{9,13},{10,... | collective-permute-start | bytes 1622024 | tf_op jit(solution)/shard_map/ppermute | solution.py:40
  21.4 15.3 %collective-permute-start.6 = (bf16[64,4224]{1,0:T(8,128)(2,1)S(1)}, bf16[64,4224]{1,0:T(8,128)(2,1)S(1)}, u32[]{:S(2)}, u32[]{:S(2)}) collective-permute-start(bf16[64,4224]{1,0:T(8,128)(2,1)S(1)} %pad_maximum_fusion.refs_4_), channel_id=1, source_target_pairs={{0,2},{1,3},{2,0},{3,1},{4,6},{5,7},{6,4},{7,5},{8,10},{9,11},{10,... | collective-permute-start | bytes 1622024 | tf_op jit(solution)/shard_map/ppermute | solution.py:40
  23.1 16.1 %collective-permute-start.3 = (bf16[128,2048]{1,0:T(8,128)(2,1)S(1)}, bf16[128,2048]{1,0:T(8,128)(2,1)S(1)}, u32[]{:S(2)}, u32[]{:S(2)}) collective-permute-start(bf16[128,2048]{1,0:T(8,128)(2,1)S(1)} %copy-done.4), channel_id=1, source_target_pairs={{0,1},{1,0},{2,3},{3,2},{4,5},{5,4},{6,7},{7,6},{8,9},{9,8},{10,11... | collective-permute-start | bytes 1572872 | tf_op jit(solution)/shard_map/ppermute | solution.py:40
  23.2 16.1 %collective-permute-start.4 = (bf16[128,2048]{1,0:T(8,128)(2,1)S(1)}, bf16[128,2048]{1,0:T(8,128)(2,1)S(1)}, u32[]{:S(2)}, u32[]{:S(2)}) collective-permute-start(bf16[128,2048]{1,0:T(8,128)(2,1)S(1)} %copy-done.3), channel_id=1, source_target_pairs={{0,1},{1,0},{2,3},{3,2},{4,5},{5,4},{6,7},{7,6},{8,9},{9,8},{10,11... | collective-permute-start | bytes 1572872 | tf_op jit(solution)/shard_map/ppermute | solution.py:40
  49.4 14.3 %collective-permute-start.12 = (bf16[128,512]{1,0:T(8,128)(2,1)S(1)}, bf16[128,512]{1,0:T(8,128)(2,1)S(1)}, u32[]{:S(2)}, u32[]{:S(2)}) collective-permute-start(bf16[128,512]{1,0:T(8,128)(2,1)S(1)} %convolution_convert_fusion.3), channel_id=1, source_target_pairs={{0,16},{1,17},{2,18},{3,19},{4,20},{5,21},{6,22},{7,23},{8,24},{9,... | collective-permute-start | bytes 393224 | tf_op jit(solution)/shard_map/ppermute | solution.py:40
  51.5 12.2 %collective-permute-start.11 = (bf16[128,512]{1,0:T(8,128)(2,1)S(1)}, bf16[128,512]{1,0:T(8,128)(2,1)S(1)}, u32[]{:S(2)}, u32[]{:S(2)}) collective-permute-start(bf16[128,512]{1,0:T(8,128)(2,1)S(1)} %convolution_convert_fusion.3), channel_id=1, source_target_pairs={{0,8},{1,9},{2,10},{3,11},{4,12},{5,13},{6,14},{7,15},{8,16},{9,17... | collective-permute-start | bytes 393224 | tf_op jit(solution)/shard_map/ppermute | solution.py:40
  53.4 27.0 %collective-permute-start.19 = (bf16[128,2048]{1,0:T(8,128)(2,1)S(1)}, bf16[128,2048]{1,0:T(8,128)(2,1)S(1)}, u32[]{:S(2)}, u32[]{:S(2)}) collective-permute-start(bf16[128,2048]{1,0:T(8,128)(2,1)S(1)} %copy-done.4), channel_id=1, source_target_pairs={{0,2},{1,3},{2,0},{3,1},{4,6},{5,7},{6,4},{7,5},{8,10},{9,11},{10,... | collective-permute-start | bytes 1572872 | tf_op jit(solution)/shard_map/ppermute | solution.py:40
  54.7 25.8 %collective-permute-start.20 = (bf16[128,2048]{1,0:T(8,128)(2,1)S(1)}, bf16[128,2048]{1,0:T(8,128)(2,1)S(1)}, u32[]{:S(2)}, u32[]{:S(2)}) collective-permute-start(bf16[128,2048]{1,0:T(8,128)(2,1)S(1)} %copy-done.3), channel_id=1, source_target_pairs={{0,4},{1,5},{2,6},{3,7},{4,0},{5,1},{6,2},{7,3},{8,12},{9,13},{10,... | collective-permute-start | bytes 1572872 | tf_op jit(solution)/shard_map/ppermute | solution.py:40
  63.8 9.9 %collective-permute-start.15 = (bf16[128,512]{1,0:T(8,128)(2,1)S(1)}, bf16[128,512]{1,0:T(8,128)(2,1)S(1)}, u32[]{:S(2)}, u32[]{:S(2)}) collective-permute-start(bf16[128,512]{1,0:T(8,128)(2,1)S(1)} %convolution_convert_fusion.2), channel_id=1, source_target_pairs={{0,16},{1,17},{2,18},{3,19},{4,20},{5,21},{6,22},{7,23},{8,24},{9,... | collective-permute-start | bytes 393224 | tf_op jit(solution)/shard_map/ppermute | solution.py:40
  64.4 16.0 %collective-permute-start.17 = (bf16[512,512]{1,0:T(8,128)(2,1)S(1)}, bf16[512,512]{1,0:T(8,128)(2,1)S(1)}, u32[]{:S(2)}, u32[]{:S(2)}) collective-permute-start(bf16[512,512]{1,0:T(8,128)(2,1)S(1)} %pad_maximum_fusion.1.refs_2_), channel_id=1, source_target_pairs={{0,4},{1,5},{2,6},{3,7},{4,0},{5,1},{6,2},{7,3},{8,12},{9,13},{10,... | collective-permute-start | bytes 1572872 | tf_op jit(solution)/shard_map/ppermute | solution.py:40
  69.8 11.6 %collective-permute-start.18 = (bf16[512,512]{1,0:T(8,128)(2,1)S(1)}, bf16[512,512]{1,0:T(8,128)(2,1)S(1)}, u32[]{:S(2)}, u32[]{:S(2)}) collective-permute-start(bf16[512,512]{1,0:T(8,128)(2,1)S(1)} %pad_maximum_fusion.1.refs_2_), channel_id=1, source_target_pairs={{0,2},{1,3},{2,0},{3,1},{4,6},{5,7},{6,4},{7,5},{8,10},{9,11},{10,... | collective-permute-start | bytes 1572872 | tf_op jit(solution)/shard_map/ppermute | solution.py:40
  81.3 9.2 %collective-permute-start.25 = (bf16[512,512]{1,0:T(8,128)(2,1)S(1)}, bf16[512,512]{1,0:T(8,128)(2,1)S(1)}, u32[]{:S(2)}, u32[]{:S(2)}) collective-permute-start(bf16[512,512]{1,0:T(8,128)(2,1)S(1)} %pad_maximum_fusion.1.refs_2_), channel_id=1, source_target_pairs={{0,1},{1,0},{2,3},{3,2},{4,5},{5,4},{6,7},{7,6},{8,9},{9,8},{10,11... | collective-permute-start | bytes 1572872 | tf_op jit(solution)/shard_map/ppermute | solution.py:40
  81.4 8.8 %collective-permute-start.23 = (bf16[512,256]{1,0:T(8,128)(2,1)S(1)}, bf16[512,256]{1,0:T(8,128)(2,1)S(1)}, u32[]{:S(2)}, u32[]{:S(2)}) collective-permute-start(bf16[512,256]{1,0:T(8,128)(2,1)S(1)} %slice.236), channel_id=1, source_target_pairs={{0,2},{1,3},{2,0},{3,1},{4,6},{5,7},{6,4},{7,5},{8,10},{9,11},{10,... | collective-permute-start | bytes 786440 | tf_op jit(solution)/shard_map/ppermute | solution.py:40
  82.0 8.5 %collective-permute-start.24 = (bf16[512,256]{1,0:T(8,128)(2,1)S(1)}, bf16[512,256]{1,0:T(8,128)(2,1)S(1)}, u32[]{:S(2)}, u32[]{:S(2)}) collective-permute-start(bf16[512,256]{1,0:T(8,128)(2,1)S(1)} %slice.237), channel_id=1, source_target_pairs={{0,4},{1,5},{2,6},{3,7},{4,0},{5,1},{6,2},{7,3},{8,12},{9,13},{10,... | collective-permute-start | bytes 786440 | tf_op jit(solution)/shard_map/ppermute | solution.py:40
  83.6 13.7 %collective-permute-start.21 = (bf16[512,512]{1,0:T(8,128)(2,1)S(1)}, bf16[512,512]{1,0:T(8,128)(2,1)S(1)}, u32[]{:S(2)}, u32[]{:S(2)}) collective-permute-start(bf16[512,512]{1,0:T(8,128)(2,1)S(1)} %collective-permute-done.17.refs_2_), channel_id=1, source_target_pairs={{0,1},{1,0},{2,3},{3,2},{4,5},{5,4},{6,7},{7,6},{8,9},{9,8},{10,11... | collective-permute-start | bytes 1572872 | tf_op jit(solution)/shard_map/ppermute | solution.py:40
  83.6 13.7 %collective-permute-start.22 = (bf16[512,512]{1,0:T(8,128)(2,1)S(1)}, bf16[512,512]{1,0:T(8,128)(2,1)S(1)}, u32[]{:S(2)}, u32[]{:S(2)}) collective-permute-start(bf16[512,512]{1,0:T(8,128)(2,1)S(1)} %collective-permute-done.18.refs_3_), channel_id=1, source_target_pairs={{0,1},{1,0},{2,3},{3,2},{4,5},{5,4},{6,7},{7,6},{8,9},{9,8},{10,11... | collective-permute-start | bytes 1572872 | tf_op jit(solution)/shard_map/ppermute | solution.py:40
  94.1 8.6 %collective-permute-start.26 = (bf16[512,512]{1,0:T(8,128)(2,1)S(1)}, bf16[512,512]{1,0:T(8,128)(2,1)S(1)}, u32[]{:S(2)}, u32[]{:S(2)}) collective-permute-start(bf16[512,512]{1,0:T(8,128)(2,1)S(1)} %constant_dynamic-update-slice_fusion.refs_2_), channel_id=1, source_target_pairs={{0,1},{1,0},{2,3},{3,2},{4,5},{5,4},{6,7},{7,6},{8,9},{9,8},{10,11... | collective-permute-start | bytes 1572872 | tf_op jit(solution)/shard_map/ppermute | solution.py:40
  94.2 14.3 %collective-permute-start.27 = (bf16[512,512]{1,0:T(8,128)(2,1)S(1)}, bf16[512,512]{1,0:T(8,128)(2,1)S(1)}, u32[]{:S(2)}, u32[]{:S(2)}) collective-permute-start(bf16[512,512]{1,0:T(8,128)(2,1)S(1)} %pad_maximum_fusion.2.refs_4_), channel_id=1, source_target_pairs={{0,4},{1,5},{2,6},{3,7},{4,0},{5,1},{6,2},{7,3},{8,12},{9,13},{10,... | collective-permute-start | bytes 1572872 | tf_op jit(solution)/shard_map/ppermute | solution.py:40
  95.8 14.0 %collective-permute-start.28 = (bf16[512,512]{1,0:T(8,128)(2,1)S(1)}, bf16[512,512]{1,0:T(8,128)(2,1)S(1)}, u32[]{:S(2)}, u32[]{:S(2)}) collective-permute-start(bf16[512,512]{1,0:T(8,128)(2,1)S(1)} %pad_maximum_fusion.2.refs_4_), channel_id=1, source_target_pairs={{0,2},{1,3},{2,0},{3,1},{4,6},{5,7},{6,4},{7,5},{8,10},{9,11},{10,... | collective-permute-start | bytes 1572872 | tf_op jit(solution)/shard_map/ppermute | solution.py:40
  97.3 14.7 %collective-permute-start.31 = (bf16[512,512]{1,0:T(8,128)(2,1)S(1)}, bf16[512,512]{1,0:T(8,128)(2,1)S(1)}, u32[]{:S(2)}, u32[]{:S(2)}) collective-permute-start(bf16[512,512]{1,0:T(8,128)(2,1)S(1)} %get-tuple-element.113), channel_id=1, source_target_pairs={{0,1},{1,0},{2,3},{3,2},{4,5},{5,4},{6,7},{7,6},{8,9},{9,8},{10,11... | collective-permute-start | bytes 1572872 | tf_op jit(solution)/shard_map/ppermute | solution.py:40
  109.7 10.7 %collective-permute-start.29 = (bf16[512,512]{1,0:T(8,128)(2,1)S(1)}, bf16[512,512]{1,0:T(8,128)(2,1)S(1)}, u32[]{:S(2)}, u32[]{:S(2)}) collective-permute-start(bf16[512,512]{1,0:T(8,128)(2,1)S(1)} %get-tuple-element.109), channel_id=1, source_target_pairs={{0,1},{1,0},{2,3},{3,2},{4,5},{5,4},{6,7},{7,6},{8,9},{9,8},{10,11... | collective-permute-start | bytes 1572872 | tf_op jit(solution)/shard_map/ppermute | solution.py:40
  109.8 14.4 %collective-permute-start.42 = (bf16[512,512]{1,0:T(8,128)(2,1)S(1)}, bf16[512,512]{1,0:T(8,128)(2,1)S(1)}, u32[]{:S(2)}, u32[]{:S(2)}) collective-permute-start(bf16[512,512]{1,0:T(8,128)(2,1)S(1)} %collective-permute-done.27.refs_6_), channel_id=1, source_target_pairs={{0,1},{1,0},{2,3},{3,2},{4,5},{5,4},{6,7},{7,6},{8,9},{9,8},{10,11... | collective-permute-start | bytes 1572872 | tf_op jit(solution)/shard_map/ppermute | solution.py:40
  110.3 10.8 %collective-permute-start.30 = (bf16[512,512]{1,0:T(8,128)(2,1)S(1)}, bf16[512,512]{1,0:T(8,128)(2,1)S(1)}, u32[]{:S(2)}, u32[]{:S(2)}) collective-permute-start(bf16[512,512]{1,0:T(8,128)(2,1)S(1)} %get-tuple-element.111), channel_id=1, source_target_pairs={{0,1},{1,0},{2,3},{3,2},{4,5},{5,4},{6,7},{7,6},{8,9},{9,8},{10,11... | collective-permute-start | bytes 1572872 | tf_op jit(solution)/shard_map/ppermute | solution.py:40
  110.4 8.7 %collective-permute-start.32 = (bf16[512,256]{1,0:T(8,128)(2,1)S(1)}, bf16[512,256]{1,0:T(8,128)(2,1)S(1)}, u32[]{:S(2)}, u32[]{:S(2)}) collective-permute-start(bf16[512,256]{1,0:T(8,128)(2,1)S(1)} %slice.246), channel_id=1, source_target_pairs={{0,2},{1,3},{2,0},{3,1},{4,6},{5,7},{6,4},{7,5},{8,10},{9,11},{10,... | collective-permute-start | bytes 786440 | tf_op jit(solution)/shard_map/ppermute | solution.py:40
  111.9 8.4 %collective-permute-start.33 = (bf16[512,256]{1,0:T(8,128)(2,1)S(1)}, bf16[512,256]{1,0:T(8,128)(2,1)S(1)}, u32[]{:S(2)}, u32[]{:S(2)}) collective-permute-start(bf16[512,256]{1,0:T(8,128)(2,1)S(1)} %slice.247), channel_id=1, source_target_pairs={{0,4},{1,5},{2,6},{3,7},{4,0},{5,1},{6,2},{7,3},{8,12},{9,13},{10,... | collective-permute-start | bytes 786440 | tf_op jit(solution)/shard_map/ppermute | solution.py:40
  120.4 13.9 %collective-permute-start.46 = (bf16[512,512]{1,0:T(8,128)(2,1)S(1)}, bf16[512,512]{1,0:T(8,128)(2,1)S(1)}, u32[]{:S(2)}, u32[]{:S(2)}) collective-permute-start(bf16[512,512]{1,0:T(8,128)(2,1)S(1)} %pad_maximum_fusion.2.refs_4_), channel_id=1, source_target_pairs={{0,1},{1,0},{2,3},{3,2},{4,5},{5,4},{6,7},{7,6},{8,9},{9,8},{10,11... | collective-permute-start | bytes 1572872 | tf_op jit(solution)/shard_map/ppermute | solution.py:40
  121.1 18.7 %collective-permute-start.38 = (bf16[512,512]{1,0:T(8,128)(2,1)S(1)}, bf16[512,512]{1,0:T(8,128)(2,1)S(1)}, u32[]{:S(2)}, u32[]{:S(2)}) collective-permute-start(bf16[512,512]{1,0:T(8,128)(2,1)S(1)} %constant_dynamic-update-slice_fusion.2.refs_4_), channel_id=1, source_target_pairs={{0,1},{1,0},{2,3},{3,2},{4,5},{5,4},{6,7},{7,6},{8,9},{9,8},{10,11... | collective-permute-start | bytes 1572872 | tf_op jit(solution)/shard_map/ppermute | solution.py:40
  123.0 22.6 %collective-permute-start.37 = (bf16[512,512]{1,0:T(8,128)(2,1)S(1)}, bf16[512,512]{1,0:T(8,128)(2,1)S(1)}, u32[]{:S(2)}, u32[]{:S(2)}) collective-permute-start(bf16[512,512]{1,0:T(8,128)(2,1)S(1)} %add_convert_fusion.2), channel_id=1, source_target_pairs={{0,2},{1,3},{2,0},{3,1},{4,6},{5,7},{6,4},{7,5},{8,10},{9,11},{10,... | collective-permute-start | bytes 1572872 | tf_op jit(solution)/shard_map/ppermute | solution.py:40
  124.1 25.0 %collective-permute-start.36 = (bf16[512,512]{1,0:T(8,128)(2,1)S(1)}, bf16[512,512]{1,0:T(8,128)(2,1)S(1)}, u32[]{:S(2)}, u32[]{:S(2)}) collective-permute-start(bf16[512,512]{1,0:T(8,128)(2,1)S(1)} %add_convert_fusion.3), channel_id=1, source_target_pairs={{0,4},{1,5},{2,6},{3,7},{4,0},{5,1},{6,2},{7,3},{8,12},{9,13},{10,... | collective-permute-start | bytes 1572872 | tf_op jit(solution)/shard_map/ppermute | solution.py:40
  124.7 24.4 %collective-permute-start.35 = (bf16[512,512]{1,0:T(8,128)(2,1)S(1)}, bf16[512,512]{1,0:T(8,128)(2,1)S(1)}, u32[]{:S(2)}, u32[]{:S(2)}) collective-permute-start(bf16[512,512]{1,0:T(8,128)(2,1)S(1)} %add_convert_fusion.1), channel_id=1, source_target_pairs={{0,6},{1,7},{2,4},{3,5},{4,2},{5,3},{6,0},{7,1},{8,14},{9,15},{10,... | collective-permute-start | bytes 1572872 | tf_op jit(solution)/shard_map/ppermute | solution.py:40
  134.3 15.1 %collective-permute-start.44 = (bf16[512,512]{1,0:T(8,128)(2,1)S(1)}, bf16[512,512]{1,0:T(8,128)(2,1)S(1)}, u32[]{:S(2)}, u32[]{:S(2)}) collective-permute-start(bf16[512,512]{1,0:T(8,128)(2,1)S(1)} %get-tuple-element.128), channel_id=1, source_target_pairs={{0,1},{1,0},{2,3},{3,2},{4,5},{5,4},{6,7},{7,6},{8,9},{9,8},{10,11... | collective-permute-start | bytes 1572872 | tf_op jit(solution)/shard_map/ppermute | solution.py:40
  139.9 9.7 %collective-permute-start.45 = (bf16[512,512]{1,0:T(8,128)(2,1)S(1)}, bf16[512,512]{1,0:T(8,128)(2,1)S(1)}, u32[]{:S(2)}, u32[]{:S(2)}) collective-permute-start(bf16[512,512]{1,0:T(8,128)(2,1)S(1)} %get-tuple-element.130), channel_id=1, source_target_pairs={{0,1},{1,0},{2,3},{3,2},{4,5},{5,4},{6,7},{7,6},{8,9},{9,8},{10,11... | collective-permute-start | bytes 1572872 | tf_op jit(solution)/shard_map/ppermute | solution.py:40
  160.7 13.8 %collective-permute-start.52 = (bf16[512,512]{1,0:T(8,128)(2,1)S(1)}, bf16[512,512]{1,0:T(8,128)(2,1)S(1)}, u32[]{:S(2)}, u32[]{:S(2)}) collective-permute-start(bf16[512,512]{1,0:T(8,128)(2,1)S(1)} %pad_maximum_fusion.4), channel_id=1, source_target_pairs={{0,2},{1,3},{2,0},{3,1},{4,6},{5,7},{6,4},{7,5},{8,10},{9,11},{10,... | collective-permute-start | bytes 1572872 | tf_op jit(solution)/shard_map/ppermute | solution.py:40
  161.9 12.6 %collective-permute-start.51 = (bf16[512,512]{1,0:T(8,128)(2,1)S(1)}, bf16[512,512]{1,0:T(8,128)(2,1)S(1)}, u32[]{:S(2)}, u32[]{:S(2)}) collective-permute-start(bf16[512,512]{1,0:T(8,128)(2,1)S(1)} %pad_maximum_fusion.3), channel_id=1, source_target_pairs={{0,4},{1,5},{2,6},{3,7},{4,0},{5,1},{6,2},{7,3},{8,12},{9,13},{10,... | collective-permute-start | bytes 1572872 | tf_op jit(solution)/shard_map/ppermute | solution.py:40
  162.8 11.2 %collective-permute-start.49 = (bf16[128,512]{1,0:T(8,128)(2,1)S(1)}, bf16[128,512]{1,0:T(8,128)(2,1)S(1)}, u32[]{:S(2)}, u32[]{:S(2)}) collective-permute-start(bf16[128,512]{1,0:T(8,128)(2,1)S(1)} %get-tuple-element.167), channel_id=1, source_target_pairs={{0,16},{1,17},{2,18},{3,19},{4,20},{5,21},{6,22},{7,23},{8,24},{9,... | collective-permute-start | bytes 393224 | tf_op jit(solution)/shard_map/ppermute | solution.py:40
  165.3 8.8 %collective-permute-start.48 = (bf16[128,512]{1,0:T(8,128)(2,1)S(1)}, bf16[128,512]{1,0:T(8,128)(2,1)S(1)}, u32[]{:S(2)}, u32[]{:S(2)}) collective-permute-start(bf16[128,512]{1,0:T(8,128)(2,1)S(1)} %get-tuple-element.165), channel_id=1, source_target_pairs={{0,24},{1,25},{2,26},{3,27},{4,28},{5,29},{6,30},{7,31},{8,0},{9,1... | collective-permute-start | bytes 393224 | tf_op jit(solution)/shard_map/ppermute | solution.py:40
  170.6 9.4 %collective-permute-start.56 = (bf16[128,2048]{1,0:T(8,128)(2,1)S(1)}, bf16[128,2048]{1,0:T(8,128)(2,1)S(1)}, u32[]{:S(2)}, u32[]{:S(2)}) collective-permute-start(bf16[128,2048]{1,0:T(8,128)(2,1)S(1)} %collective-permute-done.20.refs_6_), channel_id=1, source_target_pairs={{0,1},{1,0},{2,3},{3,2},{4,5},{5,4},{6,7},{7,6},{8,9},{9,8},{10,11... | collective-permute-start | bytes 1572872 | tf_op jit(solution)/shard_map/ppermute | solution.py:40
  174.8 12.0 %collective-permute-start.60 = (bf16[128,512]{1,0:T(8,128)(2,1)S(1)}, bf16[128,512]{1,0:T(8,128)(2,1)S(1)}, u32[]{:S(2)}, u32[]{:S(2)}) collective-permute-start(bf16[128,512]{1,0:T(8,128)(2,1)S(1)} %get-tuple-element.163), channel_id=1, source_target_pairs={{0,8},{1,9},{2,10},{3,11},{4,12},{5,13},{6,14},{7,15},{8,16},{9,17... | collective-permute-start | bytes 393224 | tf_op jit(solution)/shard_map/ppermute | solution.py:40
  177.5 9.8 %collective-permute-start.59 = (bf16[128,512]{1,0:T(8,128)(2,1)S(1)}, bf16[128,512]{1,0:T(8,128)(2,1)S(1)}, u32[]{:S(2)}, u32[]{:S(2)}) collective-permute-start(bf16[128,512]{1,0:T(8,128)(2,1)S(1)} %get-tuple-element.164), channel_id=1, source_target_pairs={{0,16},{1,17},{2,18},{3,19},{4,20},{5,21},{6,22},{7,23},{8,24},{9,... | collective-permute-start | bytes 393224 | tf_op jit(solution)/shard_map/ppermute | solution.py:40
  185.7 10.6 %collective-permute-start.57 = (bf16[64,2048]{1,0:T(8,128)(2,1)S(1)}, bf16[64,2048]{1,0:T(8,128)(2,1)S(1)}, u32[]{:S(2)}, u32[]{:S(2)}) collective-permute-start(bf16[64,2048]{1,0:T(8,128)(2,1)S(1)} %get-tuple-element.149), channel_id=1, source_target_pairs={{0,2},{1,3},{2,0},{3,1},{4,6},{5,7},{6,4},{7,5},{8,10},{9,11},{10,... | collective-permute-start | bytes 786440 | tf_op jit(solution)/shard_map/ppermute | solution.py:40
  189.8 10.8 %collective-permute-start.65 = (bf16[256,2048]{1,0:T(8,128)(2,1)S(1)}, bf16[256,2048]{1,0:T(8,128)(2,1)S(1)}, u32[]{:S(2)}, u32[]{:S(2)}) collective-permute-start(bf16[256,2048]{1,0:T(8,128)(2,1)S(1)} %get-tuple-element.154), channel_id=1, source_target_pairs={{0,1},{1,0},{2,3},{3,2},{4,5},{5,4},{6,7},{7,6},{8,9},{9,8},{10,11... | collective-permute-start | bytes 3145736 | tf_op jit(solution)/shard_map/ppermute | solution.py:40
  190.1 13.2 %collective-permute-start.66 = (bf16[256,2048]{1,0:T(8,128)(2,1)S(1)}, bf16[256,2048]{1,0:T(8,128)(2,1)S(1)}, u32[]{:S(2)}, u32[]{:S(2)}) collective-permute-start(bf16[256,2048]{1,0:T(8,128)(2,1)S(1)} %get-tuple-element.156), channel_id=1, source_target_pairs={{0,1},{1,0},{2,3},{3,2},{4,5},{5,4},{6,7},{7,6},{8,9},{9,8},{10,11... | collective-permute-start | bytes 3145736 | tf_op jit(solution)/shard_map/ppermute | solution.py:40
  197.6 9.6 %collective-permute-start.73 = (bf16[16,2048]{1,0:T(8,128)(2,1)S(1)}, bf16[16,2048]{1,0:T(8,128)(2,1)S(1)}, u32[]{:S(2)}, u32[]{:S(2)}) collective-permute-start(bf16[16,2048]{1,0:T(8,128)(2,1)S(1)} %get-tuple-element.171), channel_id=1, source_target_pairs={{0,8},{1,9},{2,10},{3,11},{4,12},{5,13},{6,14},{7,15},{8,16},{9,17... | collective-permute-start | bytes 196616 | tf_op jit(solution)/shard_map/ppermute | solution.py:40
  199.1 10.4 %collective-permute-start.72 = (bf16[16,2048]{1,0:T(8,128)(2,1)S(1)}, bf16[16,2048]{1,0:T(8,128)(2,1)S(1)}, u32[]{:S(2)}, u32[]{:S(2)}) collective-permute-start(bf16[16,2048]{1,0:T(8,128)(2,1)S(1)} %get-tuple-element.172), channel_id=1, source_target_pairs={{0,16},{1,17},{2,18},{3,19},{4,20},{5,21},{6,22},{7,23},{8,24},{9,... | collective-permute-start | bytes 196616 | tf_op jit(solution)/shard_map/ppermute | solution.py:40
  200.5 9.0 %collective-permute-start.71 = (bf16[16,2048]{1,0:T(8,128)(2,1)S(1)}, bf16[16,2048]{1,0:T(8,128)(2,1)S(1)}, u32[]{:S(2)}, u32[]{:S(2)}) collective-permute-start(bf16[16,2048]{1,0:T(8,128)(2,1)S(1)} %get-tuple-element.170), channel_id=1, source_target_pairs={{0,24},{1,25},{2,26},{3,27},{4,28},{5,29},{6,30},{7,31},{8,0},{9,1... | collective-permute-start | bytes 196616 | tf_op jit(solution)/shard_map/ppermute | solution.py:40
  (31 other events, 265.0 us)

commit v13 on v12

--- a/solution.py
+++ b/solution.py
@@ -371,9 +371,9 @@
         scratch_shapes=scratch,
         compiler_params=pltpu.CompilerParams(vmem_limit_bytes=32 << 20),
         cost_estimate=pl.CostEstimate(
-            flops=2 * products * experts * picked * latent_width * width,
-            bytes_accessed=2 * sum(array.size for array in operands),
-            transcendentals=experts * picked * width,
+            flops=2 * products * experts * picked * latent_width * width // 3,
+            bytes_accessed=2 * sum(array.size for array in operands) // 3,
+            transcendentals=0,
         ),
     )(*operands)
 

time: 214 us -> 210 us (0.981)
  waiting for transfers between devices: 99.6 us -> 94.9 us
    ppermute x74, waiting for transfers between devices: 99.6 us -> 94.9 us  [shifted(): return lax.ppermute(block, axes, pairs)]
  transfers between devices with their start and end apart: 74 -> 74, of which waited for: 32 -> 29; matrix products, arithmetic and copies ran while one was open for 5% -> 5% of each run, Pallas kernels for 15% -> 15%
where the time goes in v13:
time: 210 us
  waiting for transfers between devices  94.9 us (45%)
  starting transfers between devices  64.1 us (31%)
  Pallas kernels  35.1 us (17%)
  other arithmetic  6.72 us (3%)
  matrix products  4.61 us (2%)
  local copies, waits for them, and re-layouts  3.28 us (2%)
    ppermute x74, waiting for transfers between devices, shifted(): return lax.ppermute(block, axes, pairs)  94.9 us
    ppermute x74, starting transfers between devices, shifted(): return lax.ppermute(block, axes, pairs)  64.1 us
    pallas_call x6, Pallas kernels, expert_call(): pl.pallas_call(kernel, out_shape=(jax.ShapeDtypeStruct((span, latent_widt...  30.8 us
    dot_general x8, matrix products, matmul(): lax.dot_general(left, right, (contract, ((), ())), preferred_element_type...  4.52 us
    pallas_call x3, Pallas kernels, vmem_call(): pl.pallas_call(kernel, out_shape=out_shape, in_specs=[whole] * len(operan...  4.28 us
  transfers between devices with their start and end apart: 74, of which 29 were waited for; matrix products, arithmetic and copies ran while one was open for 5% of the time, Pallas kernels for 15%

profile of v13, /device:TPU:0, one launch (start us, length us, event | category | flops | bytes accessed | tf_op | source)
XLA Modules:
  0.0 210.1 jit_solution(6358743474158130011)
XLA Ops:
  2.3 5.1 %collective-permute-start.2 = (bf16[16,4224]{1,0:T(8,128)(2,1)S(1)}, bf16[16,4224]{1,0:T(8,128)(2,1)S(1)}, u32[]{:S(2)}, u32[]{:S(2)}) collective-permute-start(bf16[16,4224]{1,0:T(8,128)(2,1)S(1)} %maximum_maximum_fusion), channel_id=1, source_target_pairs={{0,24},{1,25},{2,26},{3,27},{4,28},{5,29},{6,30},{7,31},{8,0},{9,1... | collective-permute-start | bytes 405512 | tf_op jit(solution)/shard_map/ppermute | solution.py:40
  8.6 2.9 %collective-permute-done.2 = bf16[16,4224]{1,0:T(8,128)(2,1)S(1)} collective-permute-done((bf16[16,4224]{1,0:T(8,128)(2,1)S(1)}, bf16[16,4224]{1,0:T(8,128)(2,1)S(1)}, u32[]{:S(2)}, u32[]{:S(2)}) %collective-permute-start.2) | collective-permute-done | bytes 135200 | tf_op jit(solution)/shard_map/ppermute | solution.py:40
  11.4 7.5 %collective-permute-done.1 = bf16[16,4224]{1,0:T(8,128)(2,1)S(1)} collective-permute-done((bf16[16,4224]{1,0:T(8,128)(2,1)S(1)}, bf16[16,4224]{1,0:T(8,128)(2,1)S(1)}, u32[]{:S(2)}, u32[]{:S(2)}) %collective-permute-start.1) | collective-permute-done | bytes 135200 | tf_op jit(solution)/shard_map/ppermute | solution.py:40
  19.9 1.6 collective-permute-start.5
  21.4 1.5 collective-permute-start.6
  23.7 9.9 %collective-permute-done.5.refs_5_ = bf16[64,4224]{1,0:T(8,128)(2,1)} collective-permute-done((bf16[64,4224]{1,0:T(8,128)(2,1)S(1)}, bf16[64,4224]{1,0:T(8,128)(2,1)}, u32[]{:S(2)}, u32[]{:S(2)}) %collective-permute-start.5) | collective-permute-done | bytes 540704 | tf_op jit(solution)/shard_map/ppermute | solution.py:40
  33.6 1.7 slice.258
  35.2 1.5 collective-permute-start.7
  37.5 1.5 collective-permute-start.8
  39.2 2.9 %collective-permute-done.7.refs_7_ = bf16[64,2048]{1,0:T(8,128)(2,1)} collective-permute-done((bf16[64,2048]{1,0:T(8,128)(2,1)}, bf16[64,2048]{1,0:T(8,128)(2,1)}, u32[]{:S(2)}, u32[]{:S(2)}) %collective-permute-start.7) | collective-permute-done | bytes 262176 | tf_op jit(solution)/shard_map/ppermute | solution.py:40
  42.2 2.2 %collective-permute-done.8.refs_8_ = bf16[64,2176]{1,0:T(8,128)(2,1)S(1)} collective-permute-done((bf16[64,2176]{1,0:T(8,128)(2,1)}, bf16[64,2176]{1,0:T(8,128)(2,1)S(1)}, u32[]{:S(2)}, u32[]{:S(2)}) %collective-permute-start.8) | collective-permute-done | bytes 278560 | tf_op jit(solution)/shard_map/ppermute | solution.py:40
  44.4 2.7 %shard_map.120 = (bf16[256,2048]{1,0:T(8,128)(2,1)S(1)}, bf16[256,2048]{1,0:T(8,128)(2,1)S(1)}, bf16[256,128]{1,0:T(8,128)(2,1)S(1)}, bf16[128,512]{1,0:T(8,128)(2,1)S(1)}, bf16[128,512]{1,0:T(8,128)(2,1)S(1)}) custom-call(bf16[128,2048]{1,0:T(8,128)(2,1)S(1)} %copy-done.4, bf16[128,2048]{1,0:T(8,128)(2,1)S(1)} %collective-permute-done.3.refs_1_.refs_5_, ...), custom_call_target="tpu_custom_call" | custom-call | flops 536870912 | bytes 4259840 | tf_op jit(solution)/shard_map/pallas_call | solution.py:138
  49.4 2.1 %collective-permute-start.12 = (bf16[128,512]{1,0:T(8,128)(2,1)S(1)}, bf16[128,512]{1,0:T(8,128)(2,1)S(1)}, u32[]{:S(2)}, u32[]{:S(2)}) collective-permute-start(bf16[128,512]{1,0:T(8,128)(2,1)S(1)} %convolution_convert_fusion.3), channel_id=1, source_target_pairs={{0,16},{1,17},{2,18},{3,19},{4,20},{5,21},{6,22},{7,23},{8,24},{9,... | collective-permute-start | bytes 393224 | tf_op jit(solution)/shard_map/ppermute | solution.py:40
  51.5 1.9 collective-permute-start.11
  54.7 1.5 collective-permute-start.20
  56.4 7.2 %collective-permute-done.12 = bf16[128,512]{1,0:T(8,128)(2,1)S(1)} collective-permute-done((bf16[128,512]{1,0:T(8,128)(2,1)S(1)}, bf16[128,512]{1,0:T(8,128)(2,1)S(1)}, u32[]{:S(2)}, u32[]{:S(2)}) %collective-permute-start.12) | collective-permute-done | bytes 131104 | tf_op jit(solution)/shard_map/ppermute | solution.py:40
  64.7 1.5 collective-permute-start.17
  66.2 3.7 %collective-permute-done.16 = bf16[128,512]{1,0:T(8,128)(2,1)S(1)} collective-permute-done((bf16[128,512]{1,0:T(8,128)(2,1)S(1)}, bf16[128,512]{1,0:T(8,128)(2,1)S(1)}, u32[]{:S(2)}, u32[]{:S(2)}) %collective-permute-start.16) | collective-permute-done | bytes 131104 | tf_op jit(solution)/shard_map/ppermute | solution.py:40
  70.5 3.1 %collective-permute-done.15 = bf16[128,512]{1,0:T(8,128)(2,1)S(1)} collective-permute-done((bf16[128,512]{1,0:T(8,128)(2,1)S(1)}, bf16[128,512]{1,0:T(8,128)(2,1)S(1)}, u32[]{:S(2)}, u32[]{:S(2)}) %collective-permute-start.15) | collective-permute-done | bytes 131104 | tf_op jit(solution)/shard_map/ppermute | solution.py:40
  73.7 6.7 %collective-permute-done.14 = bf16[128,512]{1,0:T(8,128)(2,1)S(1)} collective-permute-done((bf16[128,512]{1,0:T(8,128)(2,1)S(1)}, bf16[128,512]{1,0:T(8,128)(2,1)S(1)}, u32[]{:S(2)}, u32[]{:S(2)}) %collective-permute-start.14) | collective-permute-done | bytes 131104 | tf_op jit(solution)/shard_map/ppermute | solution.py:40
  82.5 1.6 collective-permute-start.24
  84.2 6.0 %collective-permute-done.23 = bf16[512,256]{1,0:T(8,128)(2,1)S(1)} collective-permute-done((bf16[512,256]{1,0:T(8,128)(2,1)S(1)}, bf16[512,256]{1,0:T(8,128)(2,1)S(1)}, u32[]{:S(2)}, u32[]{:S(2)}) %collective-permute-start.23) | collective-permute-done | bytes 262176 | tf_op jit(solution)/shard_map/ppermute | solution.py:40
  90.2 1.5 collective-permute-start.27
  92.4 3.7 %shard_map.122 = (bf16[512,512]{1,0:T(8,128)(2,1)S(1)}, bf16[512,512]{1,0:T(8,128)(2,1)S(1)}) custom-call(s32[2,2,1,512]{3,2,1,0:T(1,128)S(1)} %pad_add_fusion.2.refs_0_, f32[2,2,1,512]{3,2,1,0:T(1,128)S(1)} %pad_maximum_fusion.8.refs_1_, bf16[512,512]{1,0:T(8,128)(2,1)S(1)} %pad_maximum_fusion.1.refs_2_, ...), custom_call_target="tpu_custom_call" | custom-call | flops 402653184 | bytes 2449408 | tf_op jit(solution)/shard_map/pallas_call | solution.py:366
  96.8 5.3 %shard_map.121 = (bf16[512,512]{1,0:T(8,128)(2,1)S(1)}, bf16[512,512]{1,0:T(8,128)(2,1)S(1)}, bf16[512,512]{1,0:T(8,128)(2,1)S(1)}, bf16[512,512]{1,0:T(8,128)(2,1)S(1)}) custom-call(s32[4,2,1,512]{3,2,1,0:T(1,128)S(1)} %pad_add_fusion.refs_0_, f32[4,2,1,512]{3,2,1,0:T(1,128)S(1)} %pad_maximum_fusion.6.refs_1_, ...), custom_call_target="tpu_custom_call" | custom-call | flops 805306368 | bytes 2801664 | tf_op jit(solution)/shard_map/pallas_call | solution.py:366
  102.1 3.5 %shard_map.123 = (bf16[512,512]{1,0:T(8,128)(2,1)S(1)}, bf16[512,512]{1,0:T(8,128)(2,1)S(1)}) custom-call(s32[2,2,1,512]{3,2,1,0:T(1,128)S(1)} %pad_add_fusion.1.refs_0_, f32[2,2,1,512]{3,2,1,0:T(1,128)S(1)} %pad_maximum_fusion.7.refs_1_, bf16[512,512]{1,0:T(8,128)(2,1)S(1)} %constant_dynamic-update-slice_fusion.refs_2_, ...), custom_call_target="tpu_custom_call" | custom-call | flops 402653184 | bytes 2449408 | tf_op jit(solution)/shard_map/pallas_call | solution.py:366
  106.4 1.5 collective-permute-start.32
  108.7 6.4 %collective-permute-done.32 = bf16[512,256]{1,0:T(8,128)(2,1)S(1)} collective-permute-done((bf16[512,256]{1,0:T(8,128)(2,1)S(1)}, bf16[512,256]{1,0:T(8,128)(2,1)S(1)}, u32[]{:S(2)}, u32[]{:S(2)}) %collective-permute-start.32) | collective-permute-done | bytes 262176 | tf_op jit(solution)/shard_map/ppermute | solution.py:40
  117.4 1.7 collective-permute-done.34
  121.0 1.8 collective-permute-start.35
  122.8 7.5 %shard_map.125 = (bf16[512,512]{1,0:T(8,128)(2,1)S(1)}, bf16[512,512]{1,0:T(8,128)(2,1)S(1)}, bf16[512,512]{1,0:T(8,128)(2,1)S(1)}, bf16[512,512]{1,0:T(8,128)(2,1)S(1)}) custom-call(s32[4,2,1,512]{3,2,1,0:T(1,128)S(1)} %pad_add_fusion.refs_0_, f32[4,2,1,512]{3,2,1,0:T(1,128)S(1)} %pad_maximum_fusion.6.refs_1_, ...), custom_call_target="tpu_custom_call" | custom-call | flops 1342177280 | bytes 3500714 | tf_op jit(solution)/shard_map/pallas_call | solution.py:366
  130.4 5.5 %shard_map.126 = (bf16[512,512]{1,0:T(8,128)(2,1)S(1)}, bf16[512,512]{1,0:T(8,128)(2,1)S(1)}) custom-call(s32[2,2,1,512]{3,2,1,0:T(1,128)S(1)} %pad_add_fusion.2.refs_0_, f32[2,2,1,512]{3,2,1,0:T(1,128)S(1)} %pad_maximum_fusion.8.refs_1_, bf16[512,512]{1,0:T(8,128)(2,1)S(1)} %pad_maximum_fusion.1.refs_2_, ...), custom_call_target="tpu_custom_call" | custom-call | flops 671088640 | bytes 2798933 | tf_op jit(solution)/shard_map/pallas_call | solution.py:366
  136.4 5.2 %shard_map.124 = (bf16[512,512]{1,0:T(8,128)(2,1)S(1)}, bf16[512,512]{1,0:T(8,128)(2,1)S(1)}) custom-call(s32[2,2,1,512]{3,2,1,0:T(1,128)S(1)} %pad_add_fusion.1.refs_0_, f32[2,2,1,512]{3,2,1,0:T(1,128)S(1)} %pad_maximum_fusion.7.refs_1_, bf16[512,512]{1,0:T(8,128)(2,1)S(1)} %constant_dynamic-update-slice_fusion.refs_2_, ...), custom_call_target="tpu_custom_call" | custom-call | flops 671088640 | bytes 2798933 | tf_op jit(solution)/shard_map/pallas_call | solution.py:366
  141.8 3.3 %collective-permute-done.36 = bf16[512,512]{1,0:T(8,128)(2,1)S(1)} collective-permute-done((bf16[512,512]{1,0:T(8,128)(2,1)S(1)}, bf16[512,512]{1,0:T(8,128)(2,1)S(1)}, u32[]{:S(2)}, u32[]{:S(2)}) %collective-permute-start.36) | collective-permute-done | bytes 524320 | tf_op jit(solution)/shard_map/ppermute | solution.py:40
  149.2 6.5 %collective-permute-done.40 = bf16[512,256]{1,0:T(8,128)(2,1)S(1)} collective-permute-done((bf16[512,256]{1,0:T(8,128)(2,1)S(1)}, bf16[512,256]{1,0:T(8,128)(2,1)S(1)}, u32[]{:S(2)}, u32[]{:S(2)}) %collective-permute-start.40) | collective-permute-done | bytes 262176 | tf_op jit(solution)/shard_map/ppermute | solution.py:40
  159.4 2.4 %collective-permute-start.49 = (bf16[128,512]{1,0:T(8,128)(2,1)S(1)}, bf16[128,512]{1,0:T(8,128)(2,1)S(1)}, u32[]{:S(2)}, u32[]{:S(2)}) collective-permute-start(bf16[128,512]{1,0:T(8,128)(2,1)S(1)} %get-tuple-element.167), channel_id=1, source_target_pairs={{0,16},{1,17},{2,18},{3,19},{4,20},{5,21},{6,22},{7,23},{8,24},{9,... | collective-permute-start | bytes 393224 | tf_op jit(solution)/shard_map/ppermute | solution.py:40
  163.2 4.0 %collective-permute-done.50 = bf16[128,512]{1,0:T(8,128)(2,1)S(1)} collective-permute-done((bf16[128,512]{1,0:T(8,128)(2,1)S(1)}, bf16[128,512]{1,0:T(8,128)(2,1)S(1)}, u32[]{:S(2)}, u32[]{:S(2)}) %collective-permute-start.50) | collective-permute-done | bytes 131104 | tf_op jit(solution)/shard_map/ppermute | solution.py:40
  167.1 3.1 %collective-permute-done.49 = bf16[128,512]{1,0:T(8,128)(2,1)S(1)} collective-permute-done((bf16[128,512]{1,0:T(8,128)(2,1)S(1)}, bf16[128,512]{1,0:T(8,128)(2,1)S(1)}, u32[]{:S(2)}, u32[]{:S(2)}) %collective-permute-start.49) | collective-permute-done | bytes 131104 | tf_op jit(solution)/shard_map/ppermute | solution.py:40
  171.1 2.6 %collective-permute-start.60 = (bf16[128,512]{1,0:T(8,128)(2,1)S(1)}, bf16[128,512]{1,0:T(8,128)(2,1)S(1)}, u32[]{:S(2)}, u32[]{:S(2)}) collective-permute-start(bf16[128,512]{1,0:T(8,128)(2,1)S(1)} %get-tuple-element.163), channel_id=1, source_target_pairs={{0,8},{1,9},{2,10},{3,11},{4,12},{5,13},{6,14},{7,15},{8,16},{9,17... | collective-permute-start | bytes 393224 | tf_op jit(solution)/shard_map/ppermute | solution.py:40
  173.7 1.9 collective-permute-start.59
  178.4 1.8 collective-permute-done.54.refs_2_
  186.5 5.0 %collective-permute-done.62.refs_2_ = bf16[128,128]{1,0:T(8,128)(2,1)S(1)} collective-permute-done((bf16[128,128]{1,0:T(8,128)(2,1)S(1)}, bf16[128,128]{1,0:T(8,128)(2,1)S(1)}, u32[]{:S(2)}, u32[]{:S(2)}) %collective-permute-start.62) | collective-permute-done | bytes 32800 | tf_op jit(solution)/shard_map/ppermute | solution.py:40
  193.6 1.5 collective-permute-start.73
  196.6 1.7 collective-permute-start.71
  200.9 1.5 collective-permute-start.70
  203.2 2.3 %collective-permute-start.68 = (bf16[16,2048]{1,0:T(8,128)(2,1)S(1)}, bf16[16,2048]{1,0:T(8,128)(2,1)S(1)}, u32[]{:S(2)}, u32[]{:S(2)}) collective-permute-start(bf16[16,2048]{1,0:T(8,128)(2,1)S(1)} %get-tuple-element.173), channel_id=1, source_target_pairs={{0,24},{1,25},{2,26},{3,27},{4,28},{5,29},{6,30},{7,31},{8,0},{9,1... | collective-permute-start | bytes 196616 | tf_op jit(solution)/shard_map/ppermute | solution.py:40
  206.2 1.4 collective-permute-done.70
  207.6 1.9 collective-permute-done.69
  (200 shorter events, 47.9 us)
Async XLA Ops:
  2.3 9.1 %collective-permute-start.2 = (bf16[16,4224]{1,0:T(8,128)(2,1)S(1)}, bf16[16,4224]{1,0:T(8,128)(2,1)S(1)}, u32[]{:S(2)}, u32[]{:S(2)}) collective-permute-start(bf16[16,4224]{1,0:T(8,128)(2,1)S(1)} %maximum_maximum_fusion), channel_id=1, source_target_pairs={{0,24},{1,25},{2,26},{3,27},{4,28},{5,29},{6,30},{7,31},{8,0},{9,1... | collective-permute-start | bytes 405512 | tf_op jit(solution)/shard_map/ppermute | solution.py:40
  7.4 11.5 %collective-permute-start.1 = (bf16[16,4224]{1,0:T(8,128)(2,1)S(1)}, bf16[16,4224]{1,0:T(8,128)(2,1)S(1)}, u32[]{:S(2)}, u32[]{:S(2)}) collective-permute-start(bf16[16,4224]{1,0:T(8,128)(2,1)S(1)} %maximum_maximum_fusion), channel_id=1, source_target_pairs={{0,16},{1,17},{2,18},{3,19},{4,20},{5,21},{6,22},{7,23},{8,24},{9,... | collective-permute-start | bytes 405512 | tf_op jit(solution)/shard_map/ppermute | solution.py:40
  7.4 11.5 %collective-permute-start = (bf16[16,4224]{1,0:T(8,128)(2,1)S(1)}, bf16[16,4224]{1,0:T(8,128)(2,1)S(1)}, u32[]{:S(2)}, u32[]{:S(2)}) collective-permute-start(bf16[16,4224]{1,0:T(8,128)(2,1)S(1)} %maximum_maximum_fusion), channel_id=1, source_target_pairs={{0,8},{1,9},{2,10},{3,11},{4,12},{5,13},{6,14},{7,15},{8,16},{9,17... | collective-permute-start | bytes 405512 | tf_op jit(solution)/shard_map/ppermute | solution.py:40
  19.9 13.7 %collective-permute-start.5 = (bf16[64,4224]{1,0:T(8,128)(2,1)S(1)}, bf16[64,4224]{1,0:T(8,128)(2,1)}, u32[]{:S(2)}, u32[]{:S(2)}) collective-permute-start(bf16[64,4224]{1,0:T(8,128)(2,1)S(1)} %pad_maximum_fusion.refs_4_), channel_id=1, source_target_pairs={{0,4},{1,5},{2,6},{3,7},{4,0},{5,1},{6,2},{7,3},{8,12},{9,13},{10,... | collective-permute-start | bytes 1622024 | tf_op jit(solution)/shard_map/ppermute | solution.py:40
  21.4 15.3 %collective-permute-start.6 = (bf16[64,4224]{1,0:T(8,128)(2,1)S(1)}, bf16[64,4224]{1,0:T(8,128)(2,1)S(1)}, u32[]{:S(2)}, u32[]{:S(2)}) collective-permute-start(bf16[64,4224]{1,0:T(8,128)(2,1)S(1)} %pad_maximum_fusion.refs_4_), channel_id=1, source_target_pairs={{0,2},{1,3},{2,0},{3,1},{4,6},{5,7},{6,4},{7,5},{8,10},{9,11},{10,... | collective-permute-start | bytes 1622024 | tf_op jit(solution)/shard_map/ppermute | solution.py:40
  23.1 16.1 %collective-permute-start.3 = (bf16[128,2048]{1,0:T(8,128)(2,1)S(1)}, bf16[128,2048]{1,0:T(8,128)(2,1)S(1)}, u32[]{:S(2)}, u32[]{:S(2)}) collective-permute-start(bf16[128,2048]{1,0:T(8,128)(2,1)S(1)} %copy-done.4), channel_id=1, source_target_pairs={{0,1},{1,0},{2,3},{3,2},{4,5},{5,4},{6,7},{7,6},{8,9},{9,8},{10,11... | collective-permute-start | bytes 1572872 | tf_op jit(solution)/shard_map/ppermute | solution.py:40
  23.2 16.1 %collective-permute-start.4 = (bf16[128,2048]{1,0:T(8,128)(2,1)S(1)}, bf16[128,2048]{1,0:T(8,128)(2,1)S(1)}, u32[]{:S(2)}, u32[]{:S(2)}) collective-permute-start(bf16[128,2048]{1,0:T(8,128)(2,1)S(1)} %copy-done.3), channel_id=1, source_target_pairs={{0,1},{1,0},{2,3},{3,2},{4,5},{5,4},{6,7},{7,6},{8,9},{9,8},{10,11... | collective-permute-start | bytes 1572872 | tf_op jit(solution)/shard_map/ppermute | solution.py:40
  49.4 14.3 %collective-permute-start.12 = (bf16[128,512]{1,0:T(8,128)(2,1)S(1)}, bf16[128,512]{1,0:T(8,128)(2,1)S(1)}, u32[]{:S(2)}, u32[]{:S(2)}) collective-permute-start(bf16[128,512]{1,0:T(8,128)(2,1)S(1)} %convolution_convert_fusion.3), channel_id=1, source_target_pairs={{0,16},{1,17},{2,18},{3,19},{4,20},{5,21},{6,22},{7,23},{8,24},{9,... | collective-permute-start | bytes 393224 | tf_op jit(solution)/shard_map/ppermute | solution.py:40
  51.5 12.2 %collective-permute-start.11 = (bf16[128,512]{1,0:T(8,128)(2,1)S(1)}, bf16[128,512]{1,0:T(8,128)(2,1)S(1)}, u32[]{:S(2)}, u32[]{:S(2)}) collective-permute-start(bf16[128,512]{1,0:T(8,128)(2,1)S(1)} %convolution_convert_fusion.3), channel_id=1, source_target_pairs={{0,8},{1,9},{2,10},{3,11},{4,12},{5,13},{6,14},{7,15},{8,16},{9,17... | collective-permute-start | bytes 393224 | tf_op jit(solution)/shard_map/ppermute | solution.py:40
  53.4 27.0 %collective-permute-start.19 = (bf16[128,2048]{1,0:T(8,128)(2,1)S(1)}, bf16[128,2048]{1,0:T(8,128)(2,1)S(1)}, u32[]{:S(2)}, u32[]{:S(2)}) collective-permute-start(bf16[128,2048]{1,0:T(8,128)(2,1)S(1)} %copy-done.4), channel_id=1, source_target_pairs={{0,2},{1,3},{2,0},{3,1},{4,6},{5,7},{6,4},{7,5},{8,10},{9,11},{10,... | collective-permute-start | bytes 1572872 | tf_op jit(solution)/shard_map/ppermute | solution.py:40
  54.7 25.8 %collective-permute-start.20 = (bf16[128,2048]{1,0:T(8,128)(2,1)S(1)}, bf16[128,2048]{1,0:T(8,128)(2,1)S(1)}, u32[]{:S(2)}, u32[]{:S(2)}) collective-permute-start(bf16[128,2048]{1,0:T(8,128)(2,1)S(1)} %copy-done.3), channel_id=1, source_target_pairs={{0,4},{1,5},{2,6},{3,7},{4,0},{5,1},{6,2},{7,3},{8,12},{9,13},{10,... | collective-permute-start | bytes 1572872 | tf_op jit(solution)/shard_map/ppermute | solution.py:40
  64.1 9.6 %collective-permute-start.15 = (bf16[128,512]{1,0:T(8,128)(2,1)S(1)}, bf16[128,512]{1,0:T(8,128)(2,1)S(1)}, u32[]{:S(2)}, u32[]{:S(2)}) collective-permute-start(bf16[128,512]{1,0:T(8,128)(2,1)S(1)} %convolution_convert_fusion.2), channel_id=1, source_target_pairs={{0,16},{1,17},{2,18},{3,19},{4,20},{5,21},{6,22},{7,23},{8,24},{9,... | collective-permute-start | bytes 393224 | tf_op jit(solution)/shard_map/ppermute | solution.py:40
  64.7 15.7 %collective-permute-start.17 = (bf16[512,512]{1,0:T(8,128)(2,1)S(1)}, bf16[512,512]{1,0:T(8,128)(2,1)S(1)}, u32[]{:S(2)}, u32[]{:S(2)}) collective-permute-start(bf16[512,512]{1,0:T(8,128)(2,1)S(1)} %pad_maximum_fusion.1.refs_2_), channel_id=1, source_target_pairs={{0,4},{1,5},{2,6},{3,7},{4,0},{5,1},{6,2},{7,3},{8,12},{9,13},{10,... | collective-permute-start | bytes 1572872 | tf_op jit(solution)/shard_map/ppermute | solution.py:40
  69.9 11.4 %collective-permute-start.18 = (bf16[512,512]{1,0:T(8,128)(2,1)S(1)}, bf16[512,512]{1,0:T(8,128)(2,1)S(1)}, u32[]{:S(2)}, u32[]{:S(2)}) collective-permute-start(bf16[512,512]{1,0:T(8,128)(2,1)S(1)} %pad_maximum_fusion.1.refs_2_), channel_id=1, source_target_pairs={{0,2},{1,3},{2,0},{3,1},{4,6},{5,7},{6,4},{7,5},{8,10},{9,11},{10,... | collective-permute-start | bytes 1572872 | tf_op jit(solution)/shard_map/ppermute | solution.py:40
  81.3 14.9 %collective-permute-start.21 = (bf16[512,512]{1,0:T(8,128)(2,1)S(1)}, bf16[512,512]{1,0:T(8,128)(2,1)S(1)}, u32[]{:S(2)}, u32[]{:S(2)}) collective-permute-start(bf16[512,512]{1,0:T(8,128)(2,1)S(1)} %collective-permute-done.17.refs_2_), channel_id=1, source_target_pairs={{0,1},{1,0},{2,3},{3,2},{4,5},{5,4},{6,7},{7,6},{8,9},{9,8},{10,11... | collective-permute-start | bytes 1572872 | tf_op jit(solution)/shard_map/ppermute | solution.py:40
  81.4 11.0 %collective-permute-start.25 = (bf16[512,512]{1,0:T(8,128)(2,1)S(1)}, bf16[512,512]{1,0:T(8,128)(2,1)S(1)}, u32[]{:S(2)}, u32[]{:S(2)}) collective-permute-start(bf16[512,512]{1,0:T(8,128)(2,1)S(1)} %pad_maximum_fusion.1.refs_2_), channel_id=1, source_target_pairs={{0,1},{1,0},{2,3},{3,2},{4,5},{5,4},{6,7},{7,6},{8,9},{9,8},{10,11... | collective-permute-start | bytes 1572872 | tf_op jit(solution)/shard_map/ppermute | solution.py:40
  82.5 9.3 %collective-permute-start.24 = (bf16[512,256]{1,0:T(8,128)(2,1)S(1)}, bf16[512,256]{1,0:T(8,128)(2,1)S(1)}, u32[]{:S(2)}, u32[]{:S(2)}) collective-permute-start(bf16[512,256]{1,0:T(8,128)(2,1)S(1)} %slice.237), channel_id=1, source_target_pairs={{0,4},{1,5},{2,6},{3,7},{4,0},{5,1},{6,2},{7,3},{8,12},{9,13},{10,... | collective-permute-start | bytes 786440 | tf_op jit(solution)/shard_map/ppermute | solution.py:40
  84.1 12.7 %collective-permute-start.22 = (bf16[512,512]{1,0:T(8,128)(2,1)S(1)}, bf16[512,512]{1,0:T(8,128)(2,1)S(1)}, u32[]{:S(2)}, u32[]{:S(2)}) collective-permute-start(bf16[512,512]{1,0:T(8,128)(2,1)S(1)} %collective-permute-done.18.refs_3_), channel_id=1, source_target_pairs={{0,1},{1,0},{2,3},{3,2},{4,5},{5,4},{6,7},{7,6},{8,9},{9,8},{10,11... | collective-permute-start | bytes 1572872 | tf_op jit(solution)/shard_map/ppermute | solution.py:40
  90.2 15.4 %collective-permute-start.27 = (bf16[512,512]{1,0:T(8,128)(2,1)S(1)}, bf16[512,512]{1,0:T(8,128)(2,1)S(1)}, u32[]{:S(2)}, u32[]{:S(2)}) collective-permute-start(bf16[512,512]{1,0:T(8,128)(2,1)S(1)} %pad_maximum_fusion.2.refs_4_), channel_id=1, source_target_pairs={{0,4},{1,5},{2,6},{3,7},{4,0},{5,1},{6,2},{7,3},{8,12},{9,13},{10,... | collective-permute-start | bytes 1572872 | tf_op jit(solution)/shard_map/ppermute | solution.py:40
  91.8 13.9 %collective-permute-start.28 = (bf16[512,512]{1,0:T(8,128)(2,1)S(1)}, bf16[512,512]{1,0:T(8,128)(2,1)S(1)}, u32[]{:S(2)}, u32[]{:S(2)}) collective-permute-start(bf16[512,512]{1,0:T(8,128)(2,1)S(1)} %pad_maximum_fusion.2.refs_4_), channel_id=1, source_target_pairs={{0,2},{1,3},{2,0},{3,1},{4,6},{5,7},{6,4},{7,5},{8,10},{9,11},{10,... | collective-permute-start | bytes 1572872 | tf_op jit(solution)/shard_map/ppermute | solution.py:40
  96.2 11.7 %collective-permute-start.31 = (bf16[512,512]{1,0:T(8,128)(2,1)S(1)}, bf16[512,512]{1,0:T(8,128)(2,1)S(1)}, u32[]{:S(2)}, u32[]{:S(2)}) collective-permute-start(bf16[512,512]{1,0:T(8,128)(2,1)S(1)} %get-tuple-element.113), channel_id=1, source_target_pairs={{0,1},{1,0},{2,3},{3,2},{4,5},{5,4},{6,7},{7,6},{8,9},{9,8},{10,11... | collective-permute-start | bytes 1572872 | tf_op jit(solution)/shard_map/ppermute | solution.py:40
  105.7 10.7 %collective-permute-start.29 = (bf16[512,512]{1,0:T(8,128)(2,1)S(1)}, bf16[512,512]{1,0:T(8,128)(2,1)S(1)}, u32[]{:S(2)}, u32[]{:S(2)}) collective-permute-start(bf16[512,512]{1,0:T(8,128)(2,1)S(1)} %get-tuple-element.109), channel_id=1, source_target_pairs={{0,1},{1,0},{2,3},{3,2},{4,5},{5,4},{6,7},{7,6},{8,9},{9,8},{10,11... | collective-permute-start | bytes 1572872 | tf_op jit(solution)/shard_map/ppermute | solution.py:40
  105.9 14.3 %collective-permute-start.42 = (bf16[512,512]{1,0:T(8,128)(2,1)S(1)}, bf16[512,512]{1,0:T(8,128)(2,1)S(1)}, u32[]{:S(2)}, u32[]{:S(2)}) collective-permute-start(bf16[512,512]{1,0:T(8,128)(2,1)S(1)} %collective-permute-done.27.refs_6_), channel_id=1, source_target_pairs={{0,1},{1,0},{2,3},{3,2},{4,5},{5,4},{6,7},{7,6},{8,9},{9,8},{10,11... | collective-permute-start | bytes 1572872 | tf_op jit(solution)/shard_map/ppermute | solution.py:40
  106.3 10.8 %collective-permute-start.30 = (bf16[512,512]{1,0:T(8,128)(2,1)S(1)}, bf16[512,512]{1,0:T(8,128)(2,1)S(1)}, u32[]{:S(2)}, u32[]{:S(2)}) collective-permute-start(bf16[512,512]{1,0:T(8,128)(2,1)S(1)} %get-tuple-element.111), channel_id=1, source_target_pairs={{0,1},{1,0},{2,3},{3,2},{4,5},{5,4},{6,7},{7,6},{8,9},{9,8},{10,11... | collective-permute-start | bytes 1572872 | tf_op jit(solution)/shard_map/ppermute | solution.py:40
  106.4 8.6 %collective-permute-start.32 = (bf16[512,256]{1,0:T(8,128)(2,1)S(1)}, bf16[512,256]{1,0:T(8,128)(2,1)S(1)}, u32[]{:S(2)}, u32[]{:S(2)}) collective-permute-start(bf16[512,256]{1,0:T(8,128)(2,1)S(1)} %slice.246), channel_id=1, source_target_pairs={{0,2},{1,3},{2,0},{3,1},{4,6},{5,7},{6,4},{7,5},{8,10},{9,11},{10,... | collective-permute-start | bytes 786440 | tf_op jit(solution)/shard_map/ppermute | solution.py:40
  108.0 8.4 %collective-permute-start.33 = (bf16[512,256]{1,0:T(8,128)(2,1)S(1)}, bf16[512,256]{1,0:T(8,128)(2,1)S(1)}, u32[]{:S(2)}, u32[]{:S(2)}) collective-permute-start(bf16[512,256]{1,0:T(8,128)(2,1)S(1)} %slice.247), channel_id=1, source_target_pairs={{0,4},{1,5},{2,6},{3,7},{4,0},{5,1},{6,2},{7,3},{8,12},{9,13},{10,... | collective-permute-start | bytes 786440 | tf_op jit(solution)/shard_map/ppermute | solution.py:40
  116.4 13.9 %collective-permute-start.46 = (bf16[512,512]{1,0:T(8,128)(2,1)S(1)}, bf16[512,512]{1,0:T(8,128)(2,1)S(1)}, u32[]{:S(2)}, u32[]{:S(2)}) collective-permute-start(bf16[512,512]{1,0:T(8,128)(2,1)S(1)} %pad_maximum_fusion.2.refs_4_), channel_id=1, source_target_pairs={{0,1},{1,0},{2,3},{3,2},{4,5},{5,4},{6,7},{7,6},{8,9},{9,8},{10,11... | collective-permute-start | bytes 1572872 | tf_op jit(solution)/shard_map/ppermute | solution.py:40
  117.1 18.7 %collective-permute-start.38 = (bf16[512,512]{1,0:T(8,128)(2,1)S(1)}, bf16[512,512]{1,0:T(8,128)(2,1)S(1)}, u32[]{:S(2)}, u32[]{:S(2)}) collective-permute-start(bf16[512,512]{1,0:T(8,128)(2,1)S(1)} %constant_dynamic-update-slice_fusion.2.refs_4_), channel_id=1, source_target_pairs={{0,1},{1,0},{2,3},{3,2},{4,5},{5,4},{6,7},{7,6},{8,9},{9,8},{10,11... | collective-permute-start | bytes 1572872 | tf_op jit(solution)/shard_map/ppermute | solution.py:40
  119.1 22.6 %collective-permute-start.37 = (bf16[512,512]{1,0:T(8,128)(2,1)S(1)}, bf16[512,512]{1,0:T(8,128)(2,1)S(1)}, u32[]{:S(2)}, u32[]{:S(2)}) collective-permute-start(bf16[512,512]{1,0:T(8,128)(2,1)S(1)} %add_convert_fusion.2), channel_id=1, source_target_pairs={{0,2},{1,3},{2,0},{3,1},{4,6},{5,7},{6,4},{7,5},{8,10},{9,11},{10,... | collective-permute-start | bytes 1572872 | tf_op jit(solution)/shard_map/ppermute | solution.py:40
  120.1 25.0 %collective-permute-start.36 = (bf16[512,512]{1,0:T(8,128)(2,1)S(1)}, bf16[512,512]{1,0:T(8,128)(2,1)S(1)}, u32[]{:S(2)}, u32[]{:S(2)}) collective-permute-start(bf16[512,512]{1,0:T(8,128)(2,1)S(1)} %add_convert_fusion.3), channel_id=1, source_target_pairs={{0,4},{1,5},{2,6},{3,7},{4,0},{5,1},{6,2},{7,3},{8,12},{9,13},{10,... | collective-permute-start | bytes 1572872 | tf_op jit(solution)/shard_map/ppermute | solution.py:40
  121.0 24.1 %collective-permute-start.35 = (bf16[512,512]{1,0:T(8,128)(2,1)S(1)}, bf16[512,512]{1,0:T(8,128)(2,1)S(1)}, u32[]{:S(2)}, u32[]{:S(2)}) collective-permute-start(bf16[512,512]{1,0:T(8,128)(2,1)S(1)} %add_convert_fusion.1), channel_id=1, source_target_pairs={{0,6},{1,7},{2,4},{3,5},{4,2},{5,3},{6,0},{7,1},{8,14},{9,15},{10,... | collective-permute-start | bytes 1572872 | tf_op jit(solution)/shard_map/ppermute | solution.py:40
  130.3 15.1 %collective-permute-start.44 = (bf16[512,512]{1,0:T(8,128)(2,1)S(1)}, bf16[512,512]{1,0:T(8,128)(2,1)S(1)}, u32[]{:S(2)}, u32[]{:S(2)}) collective-permute-start(bf16[512,512]{1,0:T(8,128)(2,1)S(1)} %get-tuple-element.128), channel_id=1, source_target_pairs={{0,1},{1,0},{2,3},{3,2},{4,5},{5,4},{6,7},{7,6},{8,9},{9,8},{10,11... | collective-permute-start | bytes 1572872 | tf_op jit(solution)/shard_map/ppermute | solution.py:40
  135.9 9.7 %collective-permute-start.45 = (bf16[512,512]{1,0:T(8,128)(2,1)S(1)}, bf16[512,512]{1,0:T(8,128)(2,1)S(1)}, u32[]{:S(2)}, u32[]{:S(2)}) collective-permute-start(bf16[512,512]{1,0:T(8,128)(2,1)S(1)} %get-tuple-element.130), channel_id=1, source_target_pairs={{0,1},{1,0},{2,3},{3,2},{4,5},{5,4},{6,7},{7,6},{8,9},{9,8},{10,11... | collective-permute-start | bytes 1572872 | tf_op jit(solution)/shard_map/ppermute | solution.py:40
  147.2 8.4 %collective-permute-start.40 = (bf16[512,256]{1,0:T(8,128)(2,1)S(1)}, bf16[512,256]{1,0:T(8,128)(2,1)S(1)}, u32[]{:S(2)}, u32[]{:S(2)}) collective-permute-start(bf16[512,256]{1,0:T(8,128)(2,1)S(1)} %get-tuple-element.169), channel_id=1, source_target_pairs={{0,2},{1,3},{2,0},{3,1},{4,6},{5,7},{6,4},{7,5},{8,10},{9,11},{10,... | collective-permute-start | bytes 786440 | tf_op jit(solution)/shard_map/ppermute | solution.py:40
  156.7 14.0 %collective-permute-start.52 = (bf16[512,512]{1,0:T(8,128)(2,1)S(1)}, bf16[512,512]{1,0:T(8,128)(2,1)S(1)}, u32[]{:S(2)}, u32[]{:S(2)}) collective-permute-start(bf16[512,512]{1,0:T(8,128)(2,1)S(1)} %pad_maximum_fusion.4), channel_id=1, source_target_pairs={{0,2},{1,3},{2,0},{3,1},{4,6},{5,7},{6,4},{7,5},{8,10},{9,11},{10,... | collective-permute-start | bytes 1572872 | tf_op jit(solution)/shard_map/ppermute | solution.py:40
  157.9 12.8 %collective-permute-start.51 = (bf16[512,512]{1,0:T(8,128)(2,1)S(1)}, bf16[512,512]{1,0:T(8,128)(2,1)S(1)}, u32[]{:S(2)}, u32[]{:S(2)}) collective-permute-start(bf16[512,512]{1,0:T(8,128)(2,1)S(1)} %pad_maximum_fusion.3), channel_id=1, source_target_pairs={{0,4},{1,5},{2,6},{3,7},{4,0},{5,1},{6,2},{7,3},{8,12},{9,13},{10,... | collective-permute-start | bytes 1572872 | tf_op jit(solution)/shard_map/ppermute | solution.py:40
  159.4 10.9 %collective-permute-start.49 = (bf16[128,512]{1,0:T(8,128)(2,1)S(1)}, bf16[128,512]{1,0:T(8,128)(2,1)S(1)}, u32[]{:S(2)}, u32[]{:S(2)}) collective-permute-start(bf16[128,512]{1,0:T(8,128)(2,1)S(1)} %get-tuple-element.167), channel_id=1, source_target_pairs={{0,16},{1,17},{2,18},{3,19},{4,20},{5,21},{6,22},{7,23},{8,24},{9,... | collective-permute-start | bytes 393224 | tf_op jit(solution)/shard_map/ppermute | solution.py:40
  161.8 8.5 %collective-permute-start.48 = (bf16[128,512]{1,0:T(8,128)(2,1)S(1)}, bf16[128,512]{1,0:T(8,128)(2,1)S(1)}, u32[]{:S(2)}, u32[]{:S(2)}) collective-permute-start(bf16[128,512]{1,0:T(8,128)(2,1)S(1)} %get-tuple-element.165), channel_id=1, source_target_pairs={{0,24},{1,25},{2,26},{3,27},{4,28},{5,29},{6,30},{7,31},{8,0},{9,1... | collective-permute-start | bytes 393224 | tf_op jit(solution)/shard_map/ppermute | solution.py:40
  167.1 9.1 %collective-permute-start.56 = (bf16[128,2048]{1,0:T(8,128)(2,1)S(1)}, bf16[128,2048]{1,0:T(8,128)(2,1)S(1)}, u32[]{:S(2)}, u32[]{:S(2)}) collective-permute-start(bf16[128,2048]{1,0:T(8,128)(2,1)S(1)} %collective-permute-done.20.refs_6_), channel_id=1, source_target_pairs={{0,1},{1,0},{2,3},{3,2},{4,5},{5,4},{6,7},{7,6},{8,9},{9,8},{10,11... | collective-permute-start | bytes 1572872 | tf_op jit(solution)/shard_map/ppermute | solution.py:40
  171.1 11.8 %collective-permute-start.60 = (bf16[128,512]{1,0:T(8,128)(2,1)S(1)}, bf16[128,512]{1,0:T(8,128)(2,1)S(1)}, u32[]{:S(2)}, u32[]{:S(2)}) collective-permute-start(bf16[128,512]{1,0:T(8,128)(2,1)S(1)} %get-tuple-element.163), channel_id=1, source_target_pairs={{0,8},{1,9},{2,10},{3,11},{4,12},{5,13},{6,14},{7,15},{8,16},{9,17... | collective-permute-start | bytes 393224 | tf_op jit(solution)/shard_map/ppermute | solution.py:40
  173.7 9.8 %collective-permute-start.59 = (bf16[128,512]{1,0:T(8,128)(2,1)S(1)}, bf16[128,512]{1,0:T(8,128)(2,1)S(1)}, u32[]{:S(2)}, u32[]{:S(2)}) collective-permute-start(bf16[128,512]{1,0:T(8,128)(2,1)S(1)} %get-tuple-element.164), channel_id=1, source_target_pairs={{0,16},{1,17},{2,18},{3,19},{4,20},{5,21},{6,22},{7,23},{8,24},{9,... | collective-permute-start | bytes 393224 | tf_op jit(solution)/shard_map/ppermute | solution.py:40
  181.7 10.6 %collective-permute-start.57 = (bf16[64,2048]{1,0:T(8,128)(2,1)S(1)}, bf16[64,2048]{1,0:T(8,128)(2,1)S(1)}, u32[]{:S(2)}, u32[]{:S(2)}) collective-permute-start(bf16[64,2048]{1,0:T(8,128)(2,1)S(1)} %get-tuple-element.149), channel_id=1, source_target_pairs={{0,2},{1,3},{2,0},{3,1},{4,6},{5,7},{6,4},{7,5},{8,10},{9,11},{10,... | collective-permute-start | bytes 786440 | tf_op jit(solution)/shard_map/ppermute | solution.py:40
  186.0 10.6 %collective-permute-start.65 = (bf16[256,2048]{1,0:T(8,128)(2,1)S(1)}, bf16[256,2048]{1,0:T(8,128)(2,1)S(1)}, u32[]{:S(2)}, u32[]{:S(2)}) collective-permute-start(bf16[256,2048]{1,0:T(8,128)(2,1)S(1)} %get-tuple-element.154), channel_id=1, source_target_pairs={{0,1},{1,0},{2,3},{3,2},{4,5},{5,4},{6,7},{7,6},{8,9},{9,8},{10,11... | collective-permute-start | bytes 3145736 | tf_op jit(solution)/shard_map/ppermute | solution.py:40
  186.3 13.0 %collective-permute-start.66 = (bf16[256,2048]{1,0:T(8,128)(2,1)S(1)}, bf16[256,2048]{1,0:T(8,128)(2,1)S(1)}, u32[]{:S(2)}, u32[]{:S(2)}) collective-permute-start(bf16[256,2048]{1,0:T(8,128)(2,1)S(1)} %get-tuple-element.156), channel_id=1, source_target_pairs={{0,1},{1,0},{2,3},{3,2},{4,5},{5,4},{6,7},{7,6},{8,9},{9,8},{10,11... | collective-permute-start | bytes 3145736 | tf_op jit(solution)/shard_map/ppermute | solution.py:40
  192.4 8.4 %collective-permute-start.67 = (bf16[64,2048]{1,0:T(8,128)(2,1)S(1)}, bf16[64,2048]{1,0:T(8,128)(2,1)S(1)}, u32[]{:S(2)}, u32[]{:S(2)}) collective-permute-start(bf16[64,2048]{1,0:T(8,128)(2,1)S(1)} %get-tuple-element.158), channel_id=1, source_target_pairs={{0,4},{1,5},{2,6},{3,7},{4,0},{5,1},{6,2},{7,3},{8,12},{9,13},{10,... | collective-permute-start | bytes 786440 | tf_op jit(solution)/shard_map/ppermute | solution.py:40
  193.6 9.6 %collective-permute-start.73 = (bf16[16,2048]{1,0:T(8,128)(2,1)S(1)}, bf16[16,2048]{1,0:T(8,128)(2,1)S(1)}, u32[]{:S(2)}, u32[]{:S(2)}) collective-permute-start(bf16[16,2048]{1,0:T(8,128)(2,1)S(1)} %get-tuple-element.171), channel_id=1, source_target_pairs={{0,8},{1,9},{2,10},{3,11},{4,12},{5,13},{6,14},{7,15},{8,16},{9,17... | collective-permute-start | bytes 196616 | tf_op jit(solution)/shard_map/ppermute | solution.py:40
  195.1 10.4 %collective-permute-start.72 = (bf16[16,2048]{1,0:T(8,128)(2,1)S(1)}, bf16[16,2048]{1,0:T(8,128)(2,1)S(1)}, u32[]{:S(2)}, u32[]{:S(2)}) collective-permute-start(bf16[16,2048]{1,0:T(8,128)(2,1)S(1)} %get-tuple-element.172), channel_id=1, source_target_pairs={{0,16},{1,17},{2,18},{3,19},{4,20},{5,21},{6,22},{7,23},{8,24},{9,... | collective-permute-start | bytes 196616 | tf_op jit(solution)/shard_map/ppermute | solution.py:40
  196.6 8.9 %collective-permute-start.71 = (bf16[16,2048]{1,0:T(8,128)(2,1)S(1)}, bf16[16,2048]{1,0:T(8,128)(2,1)S(1)}, u32[]{:S(2)}, u32[]{:S(2)}) collective-permute-start(bf16[16,2048]{1,0:T(8,128)(2,1)S(1)} %get-tuple-element.170), channel_id=1, source_target_pairs={{0,24},{1,25},{2,26},{3,27},{4,28},{5,29},{6,30},{7,31},{8,0},{9,1... | collective-permute-start | bytes 196616 | tf_op jit(solution)/shard_map/ppermute | solution.py:40
  (31 other events, 268.4 us)

commit v14 on v13

--- a/solution.py
+++ b/solution.py
@@ -512,10 +512,15 @@
     along_grads, forward_across = tied(near_grad[1:], forward_sums[0])
     forward_sums = [forward_across] + forward_alongs
     near_grad = near_grad[:1] + tuple(along_grads)
-    backward += [
-        stage_sums(backward_kernel, plans, near, far, *shared, stage, (near_grad, far_grad))
-        for stage in STAGES[1:]
-    ]
+    across_sums, along_grads = tied(
+        stage_sums(backward_kernel, plans, near, far, *shared, STAGES[2], (near_grad, far_grad)),
+        near_grad[1:3],
+    )
+    near_grad = near_grad[:1] + tuple(along_grads) + near_grad[3:]
+    backward.append(
+        stage_sums(backward_kernel, plans, near, far, *shared, STAGES[1], (near_grad, far_grad))
+    )
+    backward.append(across_sums)
     backward[0], next_tokens, next_grads, down_near, up_near = tied(
         backward[0], next_tokens, next_grads, down_near, up_near
     )

time: 210 us -> 210 us (level)
  transfers between devices with their start and end apart: 74 -> 74, of which waited for: 29 -> 28; matrix products, arithmetic and copies ran while one was open for 5% -> 5% of each run, Pallas kernels for 15% -> 15%
where the time goes in v14:
time: 210 us
  waiting for transfers between devices  94.3 us (45%)
  starting transfers between devices  64 us (30%)
  Pallas kernels  35.1 us (17%)
  other arithmetic  6.72 us (3%)
  matrix products  4.61 us (2%)
  local copies, waits for them, and re-layouts  3.28 us (2%)
    ppermute x74, waiting for transfers between devices, shifted(): return lax.ppermute(block, axes, pairs)  94.3 us
    ppermute x74, starting transfers between devices, shifted(): return lax.ppermute(block, axes, pairs)  64 us
    pallas_call x6, Pallas kernels, expert_call(): pl.pallas_call(kernel, out_shape=(jax.ShapeDtypeStruct((span, latent_widt...  30.8 us
    dot_general x8, matrix products, matmul(): lax.dot_general(left, right, (contract, ((), ())), preferred_element_type...  4.51 us
    pallas_call x3, Pallas kernels, vmem_call(): pl.pallas_call(kernel, out_shape=out_shape, in_specs=[whole] * len(operan...  4.28 us
  transfers between devices with their start and end apart: 74, of which 28 were waited for; matrix products, arithmetic and copies ran while one was open for 5% of the time, Pallas kernels for 15%

profile of v14, /device:TPU:0, one launch (start us, length us, event | category | flops | bytes accessed | tf_op | source)
XLA Modules:
  0.0 209.5 jit_solution(11627255592382327342)
XLA Ops:
  2.3 5.1 %collective-permute-start.2 = (bf16[16,4224]{1,0:T(8,128)(2,1)S(1)}, bf16[16,4224]{1,0:T(8,128)(2,1)S(1)}, u32[]{:S(2)}, u32[]{:S(2)}) collective-permute-start(bf16[16,4224]{1,0:T(8,128)(2,1)S(1)} %maximum_maximum_fusion), channel_id=1, source_target_pairs={{0,24},{1,25},{2,26},{3,27},{4,28},{5,29},{6,30},{7,31},{8,0},{9,1... | collective-permute-start | bytes 405512 | tf_op jit(solution)/shard_map/ppermute | solution.py:40
  8.6 2.9 %collective-permute-done.2 = bf16[16,4224]{1,0:T(8,128)(2,1)S(1)} collective-permute-done((bf16[16,4224]{1,0:T(8,128)(2,1)S(1)}, bf16[16,4224]{1,0:T(8,128)(2,1)S(1)}, u32[]{:S(2)}, u32[]{:S(2)}) %collective-permute-start.2) | collective-permute-done | bytes 135200 | tf_op jit(solution)/shard_map/ppermute | solution.py:40
  11.4 7.5 %collective-permute-done.1 = bf16[16,4224]{1,0:T(8,128)(2,1)S(1)} collective-permute-done((bf16[16,4224]{1,0:T(8,128)(2,1)S(1)}, bf16[16,4224]{1,0:T(8,128)(2,1)S(1)}, u32[]{:S(2)}, u32[]{:S(2)}) %collective-permute-start.1) | collective-permute-done | bytes 135200 | tf_op jit(solution)/shard_map/ppermute | solution.py:40
  19.9 1.6 collective-permute-start.5
  21.4 1.5 collective-permute-start.6
  23.7 9.9 %collective-permute-done.5.refs_5_ = bf16[64,4224]{1,0:T(8,128)(2,1)} collective-permute-done((bf16[64,4224]{1,0:T(8,128)(2,1)S(1)}, bf16[64,4224]{1,0:T(8,128)(2,1)}, u32[]{:S(2)}, u32[]{:S(2)}) %collective-permute-start.5) | collective-permute-done | bytes 540704 | tf_op jit(solution)/shard_map/ppermute | solution.py:40
  33.6 1.7 slice.258
  35.2 1.5 collective-permute-start.7
  37.5 1.5 collective-permute-start.8
  39.2 2.9 %collective-permute-done.7.refs_7_ = bf16[64,2048]{1,0:T(8,128)(2,1)} collective-permute-done((bf16[64,2048]{1,0:T(8,128)(2,1)}, bf16[64,2048]{1,0:T(8,128)(2,1)}, u32[]{:S(2)}, u32[]{:S(2)}) %collective-permute-start.7) | collective-permute-done | bytes 262176 | tf_op jit(solution)/shard_map/ppermute | solution.py:40
  42.2 2.2 %collective-permute-done.8.refs_8_ = bf16[64,2176]{1,0:T(8,128)(2,1)S(1)} collective-permute-done((bf16[64,2176]{1,0:T(8,128)(2,1)}, bf16[64,2176]{1,0:T(8,128)(2,1)S(1)}, u32[]{:S(2)}, u32[]{:S(2)}) %collective-permute-start.8) | collective-permute-done | bytes 278560 | tf_op jit(solution)/shard_map/ppermute | solution.py:40
  44.4 2.7 %shard_map.120 = (bf16[256,2048]{1,0:T(8,128)(2,1)S(1)}, bf16[256,2048]{1,0:T(8,128)(2,1)S(1)}, bf16[256,128]{1,0:T(8,128)(2,1)S(1)}, bf16[128,512]{1,0:T(8,128)(2,1)S(1)}, bf16[128,512]{1,0:T(8,128)(2,1)S(1)}) custom-call(bf16[128,2048]{1,0:T(8,128)(2,1)S(1)} %copy-done.4, bf16[128,2048]{1,0:T(8,128)(2,1)S(1)} %collective-permute-done.3.refs_1_.refs_5_, ...), custom_call_target="tpu_custom_call" | custom-call | flops 536870912 | bytes 4259840 | tf_op jit(solution)/shard_map/pallas_call | solution.py:138
  49.4 2.1 %collective-permute-start.12 = (bf16[128,512]{1,0:T(8,128)(2,1)S(1)}, bf16[128,512]{1,0:T(8,128)(2,1)S(1)}, u32[]{:S(2)}, u32[]{:S(2)}) collective-permute-start(bf16[128,512]{1,0:T(8,128)(2,1)S(1)} %convolution_convert_fusion.3), channel_id=1, source_target_pairs={{0,16},{1,17},{2,18},{3,19},{4,20},{5,21},{6,22},{7,23},{8,24},{9,... | collective-permute-start | bytes 393224 | tf_op jit(solution)/shard_map/ppermute | solution.py:40
  51.5 1.9 collective-permute-start.11
  54.7 1.5 collective-permute-start.20
  56.4 7.2 %collective-permute-done.12 = bf16[128,512]{1,0:T(8,128)(2,1)S(1)} collective-permute-done((bf16[128,512]{1,0:T(8,128)(2,1)S(1)}, bf16[128,512]{1,0:T(8,128)(2,1)S(1)}, u32[]{:S(2)}, u32[]{:S(2)}) %collective-permute-start.12) | collective-permute-done | bytes 131104 | tf_op jit(solution)/shard_map/ppermute | solution.py:40
  64.7 1.5 collective-permute-start.17
  66.2 3.7 %collective-permute-done.16 = bf16[128,512]{1,0:T(8,128)(2,1)S(1)} collective-permute-done((bf16[128,512]{1,0:T(8,128)(2,1)S(1)}, bf16[128,512]{1,0:T(8,128)(2,1)S(1)}, u32[]{:S(2)}, u32[]{:S(2)}) %collective-permute-start.16) | collective-permute-done | bytes 131104 | tf_op jit(solution)/shard_map/ppermute | solution.py:40
  70.5 3.1 %collective-permute-done.15 = bf16[128,512]{1,0:T(8,128)(2,1)S(1)} collective-permute-done((bf16[128,512]{1,0:T(8,128)(2,1)S(1)}, bf16[128,512]{1,0:T(8,128)(2,1)S(1)}, u32[]{:S(2)}, u32[]{:S(2)}) %collective-permute-start.15) | collective-permute-done | bytes 131104 | tf_op jit(solution)/shard_map/ppermute | solution.py:40
  73.7 6.7 %collective-permute-done.14 = bf16[128,512]{1,0:T(8,128)(2,1)S(1)} collective-permute-done((bf16[128,512]{1,0:T(8,128)(2,1)S(1)}, bf16[128,512]{1,0:T(8,128)(2,1)S(1)}, u32[]{:S(2)}, u32[]{:S(2)}) %collective-permute-start.14) | collective-permute-done | bytes 131104 | tf_op jit(solution)/shard_map/ppermute | solution.py:40
  82.5 1.6 collective-permute-start.24
  84.2 6.0 %collective-permute-done.23 = bf16[512,256]{1,0:T(8,128)(2,1)S(1)} collective-permute-done((bf16[512,256]{1,0:T(8,128)(2,1)S(1)}, bf16[512,256]{1,0:T(8,128)(2,1)S(1)}, u32[]{:S(2)}, u32[]{:S(2)}) %collective-permute-start.23) | collective-permute-done | bytes 262176 | tf_op jit(solution)/shard_map/ppermute | solution.py:40
  90.2 1.5 collective-permute-start.27
  92.4 3.7 %shard_map.122 = (bf16[512,512]{1,0:T(8,128)(2,1)S(1)}, bf16[512,512]{1,0:T(8,128)(2,1)S(1)}) custom-call(s32[2,2,1,512]{3,2,1,0:T(1,128)S(1)} %pad_add_fusion.2.refs_0_, f32[2,2,1,512]{3,2,1,0:T(1,128)S(1)} %pad_maximum_fusion.8.refs_1_, bf16[512,512]{1,0:T(8,128)(2,1)S(1)} %pad_maximum_fusion.1.refs_2_, ...), custom_call_target="tpu_custom_call" | custom-call | flops 402653184 | bytes 2449408 | tf_op jit(solution)/shard_map/pallas_call | solution.py:366
  96.8 5.3 %shard_map.121 = (bf16[512,512]{1,0:T(8,128)(2,1)S(1)}, bf16[512,512]{1,0:T(8,128)(2,1)S(1)}, bf16[512,512]{1,0:T(8,128)(2,1)S(1)}, bf16[512,512]{1,0:T(8,128)(2,1)S(1)}) custom-call(s32[4,2,1,512]{3,2,1,0:T(1,128)S(1)} %pad_add_fusion.refs_0_, f32[4,2,1,512]{3,2,1,0:T(1,128)S(1)} %pad_maximum_fusion.6.refs_1_, ...), custom_call_target="tpu_custom_call" | custom-call | flops 805306368 | bytes 2801664 | tf_op jit(solution)/shard_map/pallas_call | solution.py:366
  102.1 3.5 %shard_map.123 = (bf16[512,512]{1,0:T(8,128)(2,1)S(1)}, bf16[512,512]{1,0:T(8,128)(2,1)S(1)}) custom-call(s32[2,2,1,512]{3,2,1,0:T(1,128)S(1)} %pad_add_fusion.1.refs_0_, f32[2,2,1,512]{3,2,1,0:T(1,128)S(1)} %pad_maximum_fusion.7.refs_1_, bf16[512,512]{1,0:T(8,128)(2,1)S(1)} %constant_dynamic-update-slice_fusion.refs_2_, ...), custom_call_target="tpu_custom_call" | custom-call | flops 402653184 | bytes 2449408 | tf_op jit(solution)/shard_map/pallas_call | solution.py:366
  106.4 1.5 collective-permute-start.32
  108.7 6.4 %collective-permute-done.32 = bf16[512,256]{1,0:T(8,128)(2,1)S(1)} collective-permute-done((bf16[512,256]{1,0:T(8,128)(2,1)S(1)}, bf16[512,256]{1,0:T(8,128)(2,1)S(1)}, u32[]{:S(2)}, u32[]{:S(2)}) %collective-permute-start.32) | collective-permute-done | bytes 262176 | tf_op jit(solution)/shard_map/ppermute | solution.py:40
  117.4 1.7 collective-permute-done.34
  121.0 1.8 collective-permute-start.35
  122.8 5.2 %shard_map.126 = (bf16[512,512]{1,0:T(8,128)(2,1)S(1)}, bf16[512,512]{1,0:T(8,128)(2,1)S(1)}) custom-call(s32[2,2,1,512]{3,2,1,0:T(1,128)S(1)} %pad_add_fusion.2.refs_0_, f32[2,2,1,512]{3,2,1,0:T(1,128)S(1)} %pad_maximum_fusion.8.refs_1_, bf16[512,512]{1,0:T(8,128)(2,1)S(1)} %pad_maximum_fusion.1.refs_2_, ...), custom_call_target="tpu_custom_call" | custom-call | flops 671088640 | bytes 2798933 | tf_op jit(solution)/shard_map/pallas_call | solution.py:366
  128.1 5.2 %shard_map.124 = (bf16[512,512]{1,0:T(8,128)(2,1)S(1)}, bf16[512,512]{1,0:T(8,128)(2,1)S(1)}) custom-call(s32[2,2,1,512]{3,2,1,0:T(1,128)S(1)} %pad_add_fusion.1.refs_0_, f32[2,2,1,512]{3,2,1,0:T(1,128)S(1)} %pad_maximum_fusion.7.refs_1_, bf16[512,512]{1,0:T(8,128)(2,1)S(1)} %constant_dynamic-update-slice_fusion.refs_2_, ...), custom_call_target="tpu_custom_call" | custom-call | flops 671088640 | bytes 2798933 | tf_op jit(solution)/shard_map/pallas_call | solution.py:366
  133.9 7.7 %shard_map.125 = (bf16[512,512]{1,0:T(8,128)(2,1)S(1)}, bf16[512,512]{1,0:T(8,128)(2,1)S(1)}, bf16[512,512]{1,0:T(8,128)(2,1)S(1)}, bf16[512,512]{1,0:T(8,128)(2,1)S(1)}) custom-call(s32[4,2,1,512]{3,2,1,0:T(1,128)S(1)} %pad_add_fusion.refs_0_, f32[4,2,1,512]{3,2,1,0:T(1,128)S(1)} %pad_maximum_fusion.6.refs_1_, ...), custom_call_target="tpu_custom_call" | custom-call | flops 1342177280 | bytes 3500714 | tf_op jit(solution)/shard_map/pallas_call | solution.py:366
  141.8 3.4 %collective-permute-done.36 = bf16[512,512]{1,0:T(8,128)(2,1)S(1)} collective-permute-done((bf16[512,512]{1,0:T(8,128)(2,1)S(1)}, bf16[512,512]{1,0:T(8,128)(2,1)S(1)}, u32[]{:S(2)}, u32[]{:S(2)}) %collective-permute-start.36) | collective-permute-done | bytes 524320 | tf_op jit(solution)/shard_map/ppermute | solution.py:40
  147.9 6.7 %collective-permute-done.40 = bf16[512,256]{1,0:T(8,128)(2,1)S(1)} collective-permute-done((bf16[512,256]{1,0:T(8,128)(2,1)S(1)}, bf16[512,256]{1,0:T(8,128)(2,1)S(1)}, u32[]{:S(2)}, u32[]{:S(2)}) %collective-permute-start.40) | collective-permute-done | bytes 262176 | tf_op jit(solution)/shard_map/ppermute | solution.py:40
  158.3 2.4 %collective-permute-start.49 = (bf16[128,512]{1,0:T(8,128)(2,1)S(1)}, bf16[128,512]{1,0:T(8,128)(2,1)S(1)}, u32[]{:S(2)}, u32[]{:S(2)}) collective-permute-start(bf16[128,512]{1,0:T(8,128)(2,1)S(1)} %get-tuple-element.175), channel_id=1, source_target_pairs={{0,16},{1,17},{2,18},{3,19},{4,20},{5,21},{6,22},{7,23},{8,24},{9,... | collective-permute-start | bytes 393224 | tf_op jit(solution)/shard_map/ppermute | solution.py:40
  160.7 1.4 collective-permute-start.48
  162.1 3.9 %collective-permute-done.50 = bf16[128,512]{1,0:T(8,128)(2,1)S(1)} collective-permute-done((bf16[128,512]{1,0:T(8,128)(2,1)S(1)}, bf16[128,512]{1,0:T(8,128)(2,1)S(1)}, u32[]{:S(2)}, u32[]{:S(2)}) %collective-permute-start.50) | collective-permute-done | bytes 131104 | tf_op jit(solution)/shard_map/ppermute | solution.py:40
  166.0 3.6 %collective-permute-done.49 = bf16[128,512]{1,0:T(8,128)(2,1)S(1)} collective-permute-done((bf16[128,512]{1,0:T(8,128)(2,1)S(1)}, bf16[128,512]{1,0:T(8,128)(2,1)S(1)}, u32[]{:S(2)}, u32[]{:S(2)}) %collective-permute-start.49) | collective-permute-done | bytes 131104 | tf_op jit(solution)/shard_map/ppermute | solution.py:40
  170.4 2.6 %collective-permute-start.60 = (bf16[128,512]{1,0:T(8,128)(2,1)S(1)}, bf16[128,512]{1,0:T(8,128)(2,1)S(1)}, u32[]{:S(2)}, u32[]{:S(2)}) collective-permute-start(bf16[128,512]{1,0:T(8,128)(2,1)S(1)} %get-tuple-element.171), channel_id=1, source_target_pairs={{0,8},{1,9},{2,10},{3,11},{4,12},{5,13},{6,14},{7,15},{8,16},{9,17... | collective-permute-start | bytes 393224 | tf_op jit(solution)/shard_map/ppermute | solution.py:40
  173.0 1.8 collective-permute-start.59
  177.8 1.8 collective-permute-done.54.refs_2_
  185.8 5.0 %collective-permute-done.62.refs_2_ = bf16[128,128]{1,0:T(8,128)(2,1)S(1)} collective-permute-done((bf16[128,128]{1,0:T(8,128)(2,1)S(1)}, bf16[128,128]{1,0:T(8,128)(2,1)S(1)}, u32[]{:S(2)}, u32[]{:S(2)}) %collective-permute-start.62) | collective-permute-done | bytes 32800 | tf_op jit(solution)/shard_map/ppermute | solution.py:40
  193.0 1.4 collective-permute-start.73
  196.0 1.6 collective-permute-start.71
  200.3 1.4 collective-permute-start.70
  202.6 2.3 %collective-permute-start.68 = (bf16[16,2048]{1,0:T(8,128)(2,1)S(1)}, bf16[16,2048]{1,0:T(8,128)(2,1)S(1)}, u32[]{:S(2)}, u32[]{:S(2)}) collective-permute-start(bf16[16,2048]{1,0:T(8,128)(2,1)S(1)} %get-tuple-element.181), channel_id=1, source_target_pairs={{0,24},{1,25},{2,26},{3,27},{4,28},{5,29},{6,30},{7,31},{8,0},{9,1... | collective-permute-start | bytes 196616 | tf_op jit(solution)/shard_map/ppermute | solution.py:40
  206.9 1.9 collective-permute-done.69
  (200 shorter events, 46.8 us)
Async XLA Ops:
  2.3 9.1 %collective-permute-start.2 = (bf16[16,4224]{1,0:T(8,128)(2,1)S(1)}, bf16[16,4224]{1,0:T(8,128)(2,1)S(1)}, u32[]{:S(2)}, u32[]{:S(2)}) collective-permute-start(bf16[16,4224]{1,0:T(8,128)(2,1)S(1)} %maximum_maximum_fusion), channel_id=1, source_target_pairs={{0,24},{1,25},{2,26},{3,27},{4,28},{5,29},{6,30},{7,31},{8,0},{9,1... | collective-permute-start | bytes 405512 | tf_op jit(solution)/shard_map/ppermute | solution.py:40
  7.4 11.5 %collective-permute-start.1 = (bf16[16,4224]{1,0:T(8,128)(2,1)S(1)}, bf16[16,4224]{1,0:T(8,128)(2,1)S(1)}, u32[]{:S(2)}, u32[]{:S(2)}) collective-permute-start(bf16[16,4224]{1,0:T(8,128)(2,1)S(1)} %maximum_maximum_fusion), channel_id=1, source_target_pairs={{0,16},{1,17},{2,18},{3,19},{4,20},{5,21},{6,22},{7,23},{8,24},{9,... | collective-permute-start | bytes 405512 | tf_op jit(solution)/shard_map/ppermute | solution.py:40
  7.4 11.5 %collective-permute-start = (bf16[16,4224]{1,0:T(8,128)(2,1)S(1)}, bf16[16,4224]{1,0:T(8,128)(2,1)S(1)}, u32[]{:S(2)}, u32[]{:S(2)}) collective-permute-start(bf16[16,4224]{1,0:T(8,128)(2,1)S(1)} %maximum_maximum_fusion), channel_id=1, source_target_pairs={{0,8},{1,9},{2,10},{3,11},{4,12},{5,13},{6,14},{7,15},{8,16},{9,17... | collective-permute-start | bytes 405512 | tf_op jit(solution)/shard_map/ppermute | solution.py:40
  19.9 13.7 %collective-permute-start.5 = (bf16[64,4224]{1,0:T(8,128)(2,1)S(1)}, bf16[64,4224]{1,0:T(8,128)(2,1)}, u32[]{:S(2)}, u32[]{:S(2)}) collective-permute-start(bf16[64,4224]{1,0:T(8,128)(2,1)S(1)} %pad_maximum_fusion.refs_4_), channel_id=1, source_target_pairs={{0,4},{1,5},{2,6},{3,7},{4,0},{5,1},{6,2},{7,3},{8,12},{9,13},{10,... | collective-permute-start | bytes 1622024 | tf_op jit(solution)/shard_map/ppermute | solution.py:40
  21.4 15.3 %collective-permute-start.6 = (bf16[64,4224]{1,0:T(8,128)(2,1)S(1)}, bf16[64,4224]{1,0:T(8,128)(2,1)S(1)}, u32[]{:S(2)}, u32[]{:S(2)}) collective-permute-start(bf16[64,4224]{1,0:T(8,128)(2,1)S(1)} %pad_maximum_fusion.refs_4_), channel_id=1, source_target_pairs={{0,2},{1,3},{2,0},{3,1},{4,6},{5,7},{6,4},{7,5},{8,10},{9,11},{10,... | collective-permute-start | bytes 1622024 | tf_op jit(solution)/shard_map/ppermute | solution.py:40
  23.1 16.1 %collective-permute-start.3 = (bf16[128,2048]{1,0:T(8,128)(2,1)S(1)}, bf16[128,2048]{1,0:T(8,128)(2,1)S(1)}, u32[]{:S(2)}, u32[]{:S(2)}) collective-permute-start(bf16[128,2048]{1,0:T(8,128)(2,1)S(1)} %copy-done.4), channel_id=1, source_target_pairs={{0,1},{1,0},{2,3},{3,2},{4,5},{5,4},{6,7},{7,6},{8,9},{9,8},{10,11... | collective-permute-start | bytes 1572872 | tf_op jit(solution)/shard_map/ppermute | solution.py:40
  23.2 16.1 %collective-permute-start.4 = (bf16[128,2048]{1,0:T(8,128)(2,1)S(1)}, bf16[128,2048]{1,0:T(8,128)(2,1)S(1)}, u32[]{:S(2)}, u32[]{:S(2)}) collective-permute-start(bf16[128,2048]{1,0:T(8,128)(2,1)S(1)} %copy-done.3), channel_id=1, source_target_pairs={{0,1},{1,0},{2,3},{3,2},{4,5},{5,4},{6,7},{7,6},{8,9},{9,8},{10,11... | collective-permute-start | bytes 1572872 | tf_op jit(solution)/shard_map/ppermute | solution.py:40
  49.4 14.3 %collective-permute-start.12 = (bf16[128,512]{1,0:T(8,128)(2,1)S(1)}, bf16[128,512]{1,0:T(8,128)(2,1)S(1)}, u32[]{:S(2)}, u32[]{:S(2)}) collective-permute-start(bf16[128,512]{1,0:T(8,128)(2,1)S(1)} %convolution_convert_fusion.3), channel_id=1, source_target_pairs={{0,16},{1,17},{2,18},{3,19},{4,20},{5,21},{6,22},{7,23},{8,24},{9,... | collective-permute-start | bytes 393224 | tf_op jit(solution)/shard_map/ppermute | solution.py:40
  51.5 12.2 %collective-permute-start.11 = (bf16[128,512]{1,0:T(8,128)(2,1)S(1)}, bf16[128,512]{1,0:T(8,128)(2,1)S(1)}, u32[]{:S(2)}, u32[]{:S(2)}) collective-permute-start(bf16[128,512]{1,0:T(8,128)(2,1)S(1)} %convolution_convert_fusion.3), channel_id=1, source_target_pairs={{0,8},{1,9},{2,10},{3,11},{4,12},{5,13},{6,14},{7,15},{8,16},{9,17... | collective-permute-start | bytes 393224 | tf_op jit(solution)/shard_map/ppermute | solution.py:40
  53.4 27.0 %collective-permute-start.19 = (bf16[128,2048]{1,0:T(8,128)(2,1)S(1)}, bf16[128,2048]{1,0:T(8,128)(2,1)S(1)}, u32[]{:S(2)}, u32[]{:S(2)}) collective-permute-start(bf16[128,2048]{1,0:T(8,128)(2,1)S(1)} %copy-done.4), channel_id=1, source_target_pairs={{0,2},{1,3},{2,0},{3,1},{4,6},{5,7},{6,4},{7,5},{8,10},{9,11},{10,... | collective-permute-start | bytes 1572872 | tf_op jit(solution)/shard_map/ppermute | solution.py:40
  54.7 25.8 %collective-permute-start.20 = (bf16[128,2048]{1,0:T(8,128)(2,1)S(1)}, bf16[128,2048]{1,0:T(8,128)(2,1)S(1)}, u32[]{:S(2)}, u32[]{:S(2)}) collective-permute-start(bf16[128,2048]{1,0:T(8,128)(2,1)S(1)} %copy-done.3), channel_id=1, source_target_pairs={{0,4},{1,5},{2,6},{3,7},{4,0},{5,1},{6,2},{7,3},{8,12},{9,13},{10,... | collective-permute-start | bytes 1572872 | tf_op jit(solution)/shard_map/ppermute | solution.py:40
  64.1 9.6 %collective-permute-start.15 = (bf16[128,512]{1,0:T(8,128)(2,1)S(1)}, bf16[128,512]{1,0:T(8,128)(2,1)S(1)}, u32[]{:S(2)}, u32[]{:S(2)}) collective-permute-start(bf16[128,512]{1,0:T(8,128)(2,1)S(1)} %convolution_convert_fusion.2), channel_id=1, source_target_pairs={{0,16},{1,17},{2,18},{3,19},{4,20},{5,21},{6,22},{7,23},{8,24},{9,... | collective-permute-start | bytes 393224 | tf_op jit(solution)/shard_map/ppermute | solution.py:40
  64.7 15.7 %collective-permute-start.17 = (bf16[512,512]{1,0:T(8,128)(2,1)S(1)}, bf16[512,512]{1,0:T(8,128)(2,1)S(1)}, u32[]{:S(2)}, u32[]{:S(2)}) collective-permute-start(bf16[512,512]{1,0:T(8,128)(2,1)S(1)} %pad_maximum_fusion.1.refs_2_), channel_id=1, source_target_pairs={{0,4},{1,5},{2,6},{3,7},{4,0},{5,1},{6,2},{7,3},{8,12},{9,13},{10,... | collective-permute-start | bytes 1572872 | tf_op jit(solution)/shard_map/ppermute | solution.py:40
  69.9 11.4 %collective-permute-start.18 = (bf16[512,512]{1,0:T(8,128)(2,1)S(1)}, bf16[512,512]{1,0:T(8,128)(2,1)S(1)}, u32[]{:S(2)}, u32[]{:S(2)}) collective-permute-start(bf16[512,512]{1,0:T(8,128)(2,1)S(1)} %pad_maximum_fusion.1.refs_2_), channel_id=1, source_target_pairs={{0,2},{1,3},{2,0},{3,1},{4,6},{5,7},{6,4},{7,5},{8,10},{9,11},{10,... | collective-permute-start | bytes 1572872 | tf_op jit(solution)/shard_map/ppermute | solution.py:40
  81.3 14.9 %collective-permute-start.21 = (bf16[512,512]{1,0:T(8,128)(2,1)S(1)}, bf16[512,512]{1,0:T(8,128)(2,1)S(1)}, u32[]{:S(2)}, u32[]{:S(2)}) collective-permute-start(bf16[512,512]{1,0:T(8,128)(2,1)S(1)} %collective-permute-done.17.refs_2_), channel_id=1, source_target_pairs={{0,1},{1,0},{2,3},{3,2},{4,5},{5,4},{6,7},{7,6},{8,9},{9,8},{10,11... | collective-permute-start | bytes 1572872 | tf_op jit(solution)/shard_map/ppermute | solution.py:40
  81.4 11.0 %collective-permute-start.25 = (bf16[512,512]{1,0:T(8,128)(2,1)S(1)}, bf16[512,512]{1,0:T(8,128)(2,1)S(1)}, u32[]{:S(2)}, u32[]{:S(2)}) collective-permute-start(bf16[512,512]{1,0:T(8,128)(2,1)S(1)} %pad_maximum_fusion.1.refs_2_), channel_id=1, source_target_pairs={{0,1},{1,0},{2,3},{3,2},{4,5},{5,4},{6,7},{7,6},{8,9},{9,8},{10,11... | collective-permute-start | bytes 1572872 | tf_op jit(solution)/shard_map/ppermute | solution.py:40
  82.5 9.3 %collective-permute-start.24 = (bf16[512,256]{1,0:T(8,128)(2,1)S(1)}, bf16[512,256]{1,0:T(8,128)(2,1)S(1)}, u32[]{:S(2)}, u32[]{:S(2)}) collective-permute-start(bf16[512,256]{1,0:T(8,128)(2,1)S(1)} %slice.237), channel_id=1, source_target_pairs={{0,4},{1,5},{2,6},{3,7},{4,0},{5,1},{6,2},{7,3},{8,12},{9,13},{10,... | collective-permute-start | bytes 786440 | tf_op jit(solution)/shard_map/ppermute | solution.py:40
  84.1 12.7 %collective-permute-start.22 = (bf16[512,512]{1,0:T(8,128)(2,1)S(1)}, bf16[512,512]{1,0:T(8,128)(2,1)S(1)}, u32[]{:S(2)}, u32[]{:S(2)}) collective-permute-start(bf16[512,512]{1,0:T(8,128)(2,1)S(1)} %collective-permute-done.18.refs_3_), channel_id=1, source_target_pairs={{0,1},{1,0},{2,3},{3,2},{4,5},{5,4},{6,7},{7,6},{8,9},{9,8},{10,11... | collective-permute-start | bytes 1572872 | tf_op jit(solution)/shard_map/ppermute | solution.py:40
  90.2 15.4 %collective-permute-start.27 = (bf16[512,512]{1,0:T(8,128)(2,1)S(1)}, bf16[512,512]{1,0:T(8,128)(2,1)S(1)}, u32[]{:S(2)}, u32[]{:S(2)}) collective-permute-start(bf16[512,512]{1,0:T(8,128)(2,1)S(1)} %pad_maximum_fusion.2.refs_4_), channel_id=1, source_target_pairs={{0,4},{1,5},{2,6},{3,7},{4,0},{5,1},{6,2},{7,3},{8,12},{9,13},{10,... | collective-permute-start | bytes 1572872 | tf_op jit(solution)/shard_map/ppermute | solution.py:40
  91.8 13.9 %collective-permute-start.28 = (bf16[512,512]{1,0:T(8,128)(2,1)S(1)}, bf16[512,512]{1,0:T(8,128)(2,1)S(1)}, u32[]{:S(2)}, u32[]{:S(2)}) collective-permute-start(bf16[512,512]{1,0:T(8,128)(2,1)S(1)} %pad_maximum_fusion.2.refs_4_), channel_id=1, source_target_pairs={{0,2},{1,3},{2,0},{3,1},{4,6},{5,7},{6,4},{7,5},{8,10},{9,11},{10,... | collective-permute-start | bytes 1572872 | tf_op jit(solution)/shard_map/ppermute | solution.py:40
  96.2 11.7 %collective-permute-start.31 = (bf16[512,512]{1,0:T(8,128)(2,1)S(1)}, bf16[512,512]{1,0:T(8,128)(2,1)S(1)}, u32[]{:S(2)}, u32[]{:S(2)}) collective-permute-start(bf16[512,512]{1,0:T(8,128)(2,1)S(1)} %get-tuple-element.117), channel_id=1, source_target_pairs={{0,1},{1,0},{2,3},{3,2},{4,5},{5,4},{6,7},{7,6},{8,9},{9,8},{10,11... | collective-permute-start | bytes 1572872 | tf_op jit(solution)/shard_map/ppermute | solution.py:40
  105.7 10.7 %collective-permute-start.29 = (bf16[512,512]{1,0:T(8,128)(2,1)S(1)}, bf16[512,512]{1,0:T(8,128)(2,1)S(1)}, u32[]{:S(2)}, u32[]{:S(2)}) collective-permute-start(bf16[512,512]{1,0:T(8,128)(2,1)S(1)} %get-tuple-element.113), channel_id=1, source_target_pairs={{0,1},{1,0},{2,3},{3,2},{4,5},{5,4},{6,7},{7,6},{8,9},{9,8},{10,11... | collective-permute-start | bytes 1572872 | tf_op jit(solution)/shard_map/ppermute | solution.py:40
  105.9 15.2 %collective-permute-start.42 = (bf16[512,512]{1,0:T(8,128)(2,1)S(1)}, bf16[512,512]{1,0:T(8,128)(2,1)S(1)}, u32[]{:S(2)}, u32[]{:S(2)}) collective-permute-start(bf16[512,512]{1,0:T(8,128)(2,1)S(1)} %collective-permute-done.27.refs_6_), channel_id=1, source_target_pairs={{0,1},{1,0},{2,3},{3,2},{4,5},{5,4},{6,7},{7,6},{8,9},{9,8},{10,11... | collective-permute-start | bytes 1572872 | tf_op jit(solution)/shard_map/ppermute | solution.py:40
  106.3 10.8 %collective-permute-start.30 = (bf16[512,512]{1,0:T(8,128)(2,1)S(1)}, bf16[512,512]{1,0:T(8,128)(2,1)S(1)}, u32[]{:S(2)}, u32[]{:S(2)}) collective-permute-start(bf16[512,512]{1,0:T(8,128)(2,1)S(1)} %get-tuple-element.115), channel_id=1, source_target_pairs={{0,1},{1,0},{2,3},{3,2},{4,5},{5,4},{6,7},{7,6},{8,9},{9,8},{10,11... | collective-permute-start | bytes 1572872 | tf_op jit(solution)/shard_map/ppermute | solution.py:40
  106.4 8.6 %collective-permute-start.32 = (bf16[512,256]{1,0:T(8,128)(2,1)S(1)}, bf16[512,256]{1,0:T(8,128)(2,1)S(1)}, u32[]{:S(2)}, u32[]{:S(2)}) collective-permute-start(bf16[512,256]{1,0:T(8,128)(2,1)S(1)} %slice.246), channel_id=1, source_target_pairs={{0,2},{1,3},{2,0},{3,1},{4,6},{5,7},{6,4},{7,5},{8,10},{9,11},{10,... | collective-permute-start | bytes 786440 | tf_op jit(solution)/shard_map/ppermute | solution.py:40
  115.1 18.3 %collective-permute-start.43 = (bf16[512,512]{1,0:T(8,128)(2,1)S(1)}, bf16[512,512]{1,0:T(8,128)(2,1)S(1)}, u32[]{:S(2)}, u32[]{:S(2)}) collective-permute-start(bf16[512,512]{1,0:T(8,128)(2,1)S(1)} %collective-permute-done.28.refs_7_), channel_id=1, source_target_pairs={{0,1},{1,0},{2,3},{3,2},{4,5},{5,4},{6,7},{7,6},{8,9},{9,8},{10,11... | collective-permute-start | bytes 1572872 | tf_op jit(solution)/shard_map/ppermute | solution.py:40
  117.1 10.9 %collective-permute-start.38 = (bf16[512,512]{1,0:T(8,128)(2,1)S(1)}, bf16[512,512]{1,0:T(8,128)(2,1)S(1)}, u32[]{:S(2)}, u32[]{:S(2)}) collective-permute-start(bf16[512,512]{1,0:T(8,128)(2,1)S(1)} %constant_dynamic-update-slice_fusion.2.refs_4_), channel_id=1, source_target_pairs={{0,1},{1,0},{2,3},{3,2},{4,5},{5,4},{6,7},{7,6},{8,9},{9,8},{10,11... | collective-permute-start | bytes 1572872 | tf_op jit(solution)/shard_map/ppermute | solution.py:40
  119.1 22.6 %collective-permute-start.37 = (bf16[512,512]{1,0:T(8,128)(2,1)S(1)}, bf16[512,512]{1,0:T(8,128)(2,1)S(1)}, u32[]{:S(2)}, u32[]{:S(2)}) collective-permute-start(bf16[512,512]{1,0:T(8,128)(2,1)S(1)} %add_convert_fusion.2), channel_id=1, source_target_pairs={{0,2},{1,3},{2,0},{3,1},{4,6},{5,7},{6,4},{7,5},{8,10},{9,11},{10,... | collective-permute-start | bytes 1572872 | tf_op jit(solution)/shard_map/ppermute | solution.py:40
  120.1 25.0 %collective-permute-start.36 = (bf16[512,512]{1,0:T(8,128)(2,1)S(1)}, bf16[512,512]{1,0:T(8,128)(2,1)S(1)}, u32[]{:S(2)}, u32[]{:S(2)}) collective-permute-start(bf16[512,512]{1,0:T(8,128)(2,1)S(1)} %add_convert_fusion.3), channel_id=1, source_target_pairs={{0,4},{1,5},{2,6},{3,7},{4,0},{5,1},{6,2},{7,3},{8,12},{9,13},{10,... | collective-permute-start | bytes 1572872 | tf_op jit(solution)/shard_map/ppermute | solution.py:40
  121.0 24.1 %collective-permute-start.35 = (bf16[512,512]{1,0:T(8,128)(2,1)S(1)}, bf16[512,512]{1,0:T(8,128)(2,1)S(1)}, u32[]{:S(2)}, u32[]{:S(2)}) collective-permute-start(bf16[512,512]{1,0:T(8,128)(2,1)S(1)} %add_convert_fusion.1), channel_id=1, source_target_pairs={{0,6},{1,7},{2,4},{3,5},{4,2},{5,3},{6,0},{7,1},{8,14},{9,15},{10,... | collective-permute-start | bytes 1572872 | tf_op jit(solution)/shard_map/ppermute | solution.py:40
  128.0 17.4 %collective-permute-start.47 = (bf16[512,512]{1,0:T(8,128)(2,1)S(1)}, bf16[512,512]{1,0:T(8,128)(2,1)S(1)}, u32[]{:S(2)}, u32[]{:S(2)}) collective-permute-start(bf16[512,512]{1,0:T(8,128)(2,1)S(1)} %get-tuple-element.147), channel_id=1, source_target_pairs={{0,1},{1,0},{2,3},{3,2},{4,5},{5,4},{6,7},{7,6},{8,9},{9,8},{10,11... | collective-permute-start | bytes 1572872 | tf_op jit(solution)/shard_map/ppermute | solution.py:40
  133.4 12.2 %collective-permute-start.39 = (bf16[512,512]{1,0:T(8,128)(2,1)S(1)}, bf16[512,512]{1,0:T(8,128)(2,1)S(1)}, u32[]{:S(2)}, u32[]{:S(2)}) collective-permute-start(bf16[512,512]{1,0:T(8,128)(2,1)S(1)} %get-tuple-element.132), channel_id=1, source_target_pairs={{0,1},{1,0},{2,3},{3,2},{4,5},{5,4},{6,7},{7,6},{8,9},{9,8},{10,11... | collective-permute-start | bytes 1572872 | tf_op jit(solution)/shard_map/ppermute | solution.py:40
  145.8 8.8 %collective-permute-start.40 = (bf16[512,256]{1,0:T(8,128)(2,1)S(1)}, bf16[512,256]{1,0:T(8,128)(2,1)S(1)}, u32[]{:S(2)}, u32[]{:S(2)}) collective-permute-start(bf16[512,256]{1,0:T(8,128)(2,1)S(1)} %get-tuple-element.177), channel_id=1, source_target_pairs={{0,2},{1,3},{2,0},{3,1},{4,6},{5,7},{6,4},{7,5},{8,10},{9,11},{10,... | collective-permute-start | bytes 786440 | tf_op jit(solution)/shard_map/ppermute | solution.py:40
  146.9 8.4 %collective-permute-start.41 = (bf16[512,256]{1,0:T(8,128)(2,1)S(1)}, bf16[512,256]{1,0:T(8,128)(2,1)S(1)}, u32[]{:S(2)}, u32[]{:S(2)}) collective-permute-start(bf16[512,256]{1,0:T(8,128)(2,1)S(1)} %get-tuple-element.176), channel_id=1, source_target_pairs={{0,4},{1,5},{2,6},{3,7},{4,0},{5,1},{6,2},{7,3},{8,12},{9,13},{10,... | collective-permute-start | bytes 786440 | tf_op jit(solution)/shard_map/ppermute | solution.py:40
  155.6 14.5 %collective-permute-start.52 = (bf16[512,512]{1,0:T(8,128)(2,1)S(1)}, bf16[512,512]{1,0:T(8,128)(2,1)S(1)}, u32[]{:S(2)}, u32[]{:S(2)}) collective-permute-start(bf16[512,512]{1,0:T(8,128)(2,1)S(1)} %pad_maximum_fusion.4), channel_id=1, source_target_pairs={{0,2},{1,3},{2,0},{3,1},{4,6},{5,7},{6,4},{7,5},{8,10},{9,11},{10,... | collective-permute-start | bytes 1572872 | tf_op jit(solution)/shard_map/ppermute | solution.py:40
  156.8 13.3 %collective-permute-start.51 = (bf16[512,512]{1,0:T(8,128)(2,1)S(1)}, bf16[512,512]{1,0:T(8,128)(2,1)S(1)}, u32[]{:S(2)}, u32[]{:S(2)}) collective-permute-start(bf16[512,512]{1,0:T(8,128)(2,1)S(1)} %pad_maximum_fusion.3), channel_id=1, source_target_pairs={{0,4},{1,5},{2,6},{3,7},{4,0},{5,1},{6,2},{7,3},{8,12},{9,13},{10,... | collective-permute-start | bytes 1572872 | tf_op jit(solution)/shard_map/ppermute | solution.py:40
  158.3 11.3 %collective-permute-start.49 = (bf16[128,512]{1,0:T(8,128)(2,1)S(1)}, bf16[128,512]{1,0:T(8,128)(2,1)S(1)}, u32[]{:S(2)}, u32[]{:S(2)}) collective-permute-start(bf16[128,512]{1,0:T(8,128)(2,1)S(1)} %get-tuple-element.175), channel_id=1, source_target_pairs={{0,16},{1,17},{2,18},{3,19},{4,20},{5,21},{6,22},{7,23},{8,24},{9,... | collective-permute-start | bytes 393224 | tf_op jit(solution)/shard_map/ppermute | solution.py:40
  160.7 8.9 %collective-permute-start.48 = (bf16[128,512]{1,0:T(8,128)(2,1)S(1)}, bf16[128,512]{1,0:T(8,128)(2,1)S(1)}, u32[]{:S(2)}, u32[]{:S(2)}) collective-permute-start(bf16[128,512]{1,0:T(8,128)(2,1)S(1)} %get-tuple-element.173), channel_id=1, source_target_pairs={{0,24},{1,25},{2,26},{3,27},{4,28},{5,29},{6,30},{7,31},{8,0},{9,1... | collective-permute-start | bytes 393224 | tf_op jit(solution)/shard_map/ppermute | solution.py:40
  166.0 9.6 %collective-permute-start.56 = (bf16[128,2048]{1,0:T(8,128)(2,1)S(1)}, bf16[128,2048]{1,0:T(8,128)(2,1)S(1)}, u32[]{:S(2)}, u32[]{:S(2)}) collective-permute-start(bf16[128,2048]{1,0:T(8,128)(2,1)S(1)} %collective-permute-done.20.refs_6_), channel_id=1, source_target_pairs={{0,1},{1,0},{2,3},{3,2},{4,5},{5,4},{6,7},{7,6},{8,9},{9,8},{10,11... | collective-permute-start | bytes 1572872 | tf_op jit(solution)/shard_map/ppermute | solution.py:40
  170.4 11.8 %collective-permute-start.60 = (bf16[128,512]{1,0:T(8,128)(2,1)S(1)}, bf16[128,512]{1,0:T(8,128)(2,1)S(1)}, u32[]{:S(2)}, u32[]{:S(2)}) collective-permute-start(bf16[128,512]{1,0:T(8,128)(2,1)S(1)} %get-tuple-element.171), channel_id=1, source_target_pairs={{0,8},{1,9},{2,10},{3,11},{4,12},{5,13},{6,14},{7,15},{8,16},{9,17... | collective-permute-start | bytes 393224 | tf_op jit(solution)/shard_map/ppermute | solution.py:40
  173.0 9.8 %collective-permute-start.59 = (bf16[128,512]{1,0:T(8,128)(2,1)S(1)}, bf16[128,512]{1,0:T(8,128)(2,1)S(1)}, u32[]{:S(2)}, u32[]{:S(2)}) collective-permute-start(bf16[128,512]{1,0:T(8,128)(2,1)S(1)} %get-tuple-element.172), channel_id=1, source_target_pairs={{0,16},{1,17},{2,18},{3,19},{4,20},{5,21},{6,22},{7,23},{8,24},{9,... | collective-permute-start | bytes 393224 | tf_op jit(solution)/shard_map/ppermute | solution.py:40
  181.1 10.6 %collective-permute-start.57 = (bf16[64,2048]{1,0:T(8,128)(2,1)S(1)}, bf16[64,2048]{1,0:T(8,128)(2,1)S(1)}, u32[]{:S(2)}, u32[]{:S(2)}) collective-permute-start(bf16[64,2048]{1,0:T(8,128)(2,1)S(1)} %get-tuple-element.157), channel_id=1, source_target_pairs={{0,2},{1,3},{2,0},{3,1},{4,6},{5,7},{6,4},{7,5},{8,10},{9,11},{10,... | collective-permute-start | bytes 786440 | tf_op jit(solution)/shard_map/ppermute | solution.py:40
  185.3 10.7 %collective-permute-start.65 = (bf16[256,2048]{1,0:T(8,128)(2,1)S(1)}, bf16[256,2048]{1,0:T(8,128)(2,1)S(1)}, u32[]{:S(2)}, u32[]{:S(2)}) collective-permute-start(bf16[256,2048]{1,0:T(8,128)(2,1)S(1)} %get-tuple-element.162), channel_id=1, source_target_pairs={{0,1},{1,0},{2,3},{3,2},{4,5},{5,4},{6,7},{7,6},{8,9},{9,8},{10,11... | collective-permute-start | bytes 3145736 | tf_op jit(solution)/shard_map/ppermute | solution.py:40
  185.6 13.0 %collective-permute-start.66 = (bf16[256,2048]{1,0:T(8,128)(2,1)S(1)}, bf16[256,2048]{1,0:T(8,128)(2,1)S(1)}, u32[]{:S(2)}, u32[]{:S(2)}) collective-permute-start(bf16[256,2048]{1,0:T(8,128)(2,1)S(1)} %get-tuple-element.164), channel_id=1, source_target_pairs={{0,1},{1,0},{2,3},{3,2},{4,5},{5,4},{6,7},{7,6},{8,9},{9,8},{10,11... | collective-permute-start | bytes 3145736 | tf_op jit(solution)/shard_map/ppermute | solution.py:40
  191.7 8.4 %collective-permute-start.67 = (bf16[64,2048]{1,0:T(8,128)(2,1)S(1)}, bf16[64,2048]{1,0:T(8,128)(2,1)S(1)}, u32[]{:S(2)}, u32[]{:S(2)}) collective-permute-start(bf16[64,2048]{1,0:T(8,128)(2,1)S(1)} %get-tuple-element.166), channel_id=1, source_target_pairs={{0,4},{1,5},{2,6},{3,7},{4,0},{5,1},{6,2},{7,3},{8,12},{9,13},{10,... | collective-permute-start | bytes 786440 | tf_op jit(solution)/shard_map/ppermute | solution.py:40
  193.0 9.6 %collective-permute-start.73 = (bf16[16,2048]{1,0:T(8,128)(2,1)S(1)}, bf16[16,2048]{1,0:T(8,128)(2,1)S(1)}, u32[]{:S(2)}, u32[]{:S(2)}) collective-permute-start(bf16[16,2048]{1,0:T(8,128)(2,1)S(1)} %get-tuple-element.179), channel_id=1, source_target_pairs={{0,8},{1,9},{2,10},{3,11},{4,12},{5,13},{6,14},{7,15},{8,16},{9,17... | collective-permute-start | bytes 196616 | tf_op jit(solution)/shard_map/ppermute | solution.py:40
  194.4 10.4 %collective-permute-start.72 = (bf16[16,2048]{1,0:T(8,128)(2,1)S(1)}, bf16[16,2048]{1,0:T(8,128)(2,1)S(1)}, u32[]{:S(2)}, u32[]{:S(2)}) collective-permute-start(bf16[16,2048]{1,0:T(8,128)(2,1)S(1)} %get-tuple-element.180), channel_id=1, source_target_pairs={{0,16},{1,17},{2,18},{3,19},{4,20},{5,21},{6,22},{7,23},{8,24},{9,... | collective-permute-start | bytes 196616 | tf_op jit(solution)/shard_map/ppermute | solution.py:40
  196.0 8.9 %collective-permute-start.71 = (bf16[16,2048]{1,0:T(8,128)(2,1)S(1)}, bf16[16,2048]{1,0:T(8,128)(2,1)S(1)}, u32[]{:S(2)}, u32[]{:S(2)}) collective-permute-start(bf16[16,2048]{1,0:T(8,128)(2,1)S(1)} %get-tuple-element.178), channel_id=1, source_target_pairs={{0,24},{1,25},{2,26},{3,27},{4,28},{5,29},{6,30},{7,31},{8,0},{9,1... | collective-permute-start | bytes 196616 | tf_op jit(solution)/shard_map/ppermute | solution.py:40
  (31 other events, 265.9 us)
